TPU v7x, 32 devices: a whole 2x2x4 slice. The times are simulated.
32 devices in a mesh: wide: 8 (over z, y), narrow: 4 (over x, core).
Axes of the slice: x: 2, y: 2, z: 4, core: 2. Of those that a mesh axis runs over, the one named last changes fastest.
Arguments:
- level_rhs: float32 [8, 1024, 512], P('wide', 'narrow'), may hold values from -6 to 6
- galerkin_cols: int32 [3, 8, 16, 5], P(None, 'wide', 'narrow'), may hold values from 0 to 5, as said below
- galerkin_blocks: bfloat16 [3, 8, 16, 5, 64, 64], P(None, 'wide', 'narrow'), as said below
- restrict_cols: int32 [3, 8, 16, 3], P(None, 'wide', 'narrow'), may hold values from 0 to 7, as said below
- restrict_blocks: bfloat16 [3, 8, 16, 3, 64, 64], P(None, 'wide', 'narrow'), as said below
- prolong_cols: int32 [3, 8, 16, 2], P(None, 'wide', 'narrow'), may hold values from 0 to 3, as said below
- prolong_blocks: bfloat16 [3, 8, 16, 2, 64, 64], P(None, 'wide', 'narrow'), as said below
- coarse_inverse: bfloat16 [1024, 1024], P('narrow'), may hold values from -1.5 to 1.5
Outputs:
- correction: float32 [8, 1024, 512], P('wide', 'narrow')
Inputs may be any that keep to these rules, and one draw needn't show every extreme that they name: `galerkin_cols`: slot 0 of every block row names the row's own block; values below 4 name blocks of the same piece, 4 the last block of the piece before, 5 the first block of the piece after. At level k the entries of the 2**k subdomains of a group are equal. `galerkin_blocks`: at level k the blocks of the 2**k subdomains of a group are equal. The diagonal entries of every slot-0 block lie between 1 and 4. `restrict_cols`: values below 4 name blocks of the lower joined group, the others block value - 4 of the upper one; slots 0 and 1 of coarse block c name c and 4 + c. At level k the entries of the 2**(k+1) subdomains of a coarse group are equal. `restrict_blocks`: at level k the blocks of the 2**(k+1) subdomains of a coarse group are equal. `prolong_cols`: slot 0 names the fine block's own index. At level k the entries of the 2**k subdomains of a group are equal. `prolong_blocks`: at level k the blocks of the 2**k subdomains of a group are equal.
All inputs are finite; a program needn't handle non-finite values.
Results may differ from a plain program's by a relative error of at most 0.035.
Values may be sent and summed in bfloat16 or wider, within the bound.
No kernel may reach another device: no remote copies, remote signals or barrier semaphores. Data moves between devices by JAX's collectives and lax.ppermute only.
A program may use at most 64 MiB of HBM per device.

v0:
```python
import jax
import jax.numpy as jnp
from jax import lax
from jax.sharding import PartitionSpec as P

relax_down = 0.7
relax_up = 0.5


def extended(cells, sides, width):
    for axis, dim in sides:
        count = lax.axis_size(axis)
        ends = count - 1
        head = lax.slice_in_dim(cells, 0, width, axis=dim)
        tail = lax.slice_in_dim(cells, cells.shape[dim] - width, cells.shape[dim], axis=dim)
        cells = jnp.concatenate(
            [
                lax.ppermute(tail, axis, [(i, (i + 1) % count) for i in range(ends)]),
                cells,
                lax.ppermute(head, axis, [((i + 1) % count, i) for i in range(ends)]),
            ],
            axis=dim,
        )
    return cells


def from_partner(value, axis, stride):
    return lax.ppermute(value, axis, [(i, i ^ 1 << stride) for i in range(lax.axis_size(axis))])


def block_apply(blocks, picked):
    return jnp.einsum("bsrc,bscn->brn", blocks, picked, preferred_element_type=jnp.float32)


def on_device(
    level_rhs,
    galerkin_cols,
    galerkin_blocks,
    restrict_cols,
    restrict_blocks,
    prolong_cols,
    prolong_blocks,
    coarse_inverse,
):
    level_count = galerkin_cols.shape[0]
    blocks_dev = galerkin_cols.shape[2]
    block_size = galerkin_blocks.shape[-1]
    fields = level_rhs.shape[-1]
    current = level_rhs[0].reshape(blocks_dev, block_size, fields)
    wide_index = lax.axis_index("wide")
    stored = []
    for level_idx in range(level_count):
        col_ids = galerkin_cols[level_idx, 0]
        blocks = galerkin_blocks[level_idx, 0]
        diagonal = jnp.diagonal(blocks[:, 0], axis1=-2, axis2=-1).astype(jnp.float32)[:, :, None]
        smoothed = relax_down * current / diagonal
        rounded = smoothed.astype(jnp.bfloat16)
        padded = extended(rounded, (("narrow", 0),), 1)
        mapped = jnp.where(
            col_ids < blocks_dev, col_ids + 1, jnp.where(col_ids == blocks_dev, 0, blocks_dev + 1)
        )
        applied = block_apply(blocks, padded[mapped])
        residual = (current - applied).astype(jnp.bfloat16)
        upper_bit = wide_index >> level_idx & 1
        rest_ids = restrict_cols[level_idx, 0]
        own_half = (rest_ids >= blocks_dev).astype(jnp.int32) == upper_bit
        within = rest_ids % blocks_dev
        partner = from_partner(residual, "wide", level_idx)
        picked = jnp.where(own_half[:, :, None, None], residual[within], partner[within])
        coarse_rhs = block_apply(restrict_blocks[level_idx, 0], picked)
        stored.append((current, smoothed, diagonal))
        current = coarse_rhs
    flat_rhs = current.astype(jnp.bfloat16).reshape(blocks_dev * block_size, fields)
    solution = jnp.dot(
        coarse_inverse,
        lax.all_gather(flat_rhs, "narrow", axis=0, tiled=True),
        preferred_element_type=jnp.float32,
    )
    current_x = solution.reshape(blocks_dev, block_size, fields)
    for level_idx in reversed(range(level_count)):
        fine_rhs, smoothed, diagonal = stored[level_idx]
        coarse_bf = current_x.astype(jnp.bfloat16)
        prolonged = block_apply(prolong_blocks[level_idx, 0], coarse_bf[prolong_cols[level_idx, 0]])
        updated = smoothed + prolonged
        updated_bf = updated.astype(jnp.bfloat16)
        col_ids = galerkin_cols[level_idx, 0]
        inside = col_ids < blocks_dev
        picked = jnp.where(
            inside[:, :, None, None],
            updated_bf[jnp.minimum(col_ids, blocks_dev - 1)],
            jnp.zeros((), jnp.bfloat16),
        )
        applied = block_apply(galerkin_blocks[level_idx, 0], picked)
        current_x = updated + relax_up * (fine_rhs - applied) / diagonal
    return current_x.reshape(1, blocks_dev * block_size, fields)


def solution(mesh):
    in_specs = (
        P("wide", "narrow", None),
        P(None, "wide", "narrow", None),
        P(None, "wide", "narrow", None, None, None),
        P(None, "wide", "narrow", None),
        P(None, "wide", "narrow", None, None, None),
        P(None, "wide", "narrow", None),
        P(None, "wide", "narrow", None, None, None),
        P("narrow", None),
    )
    out_specs = P("wide", "narrow", None)
    return jax.shard_map(
        on_device, mesh=mesh, in_specs=in_specs, out_specs=out_specs, check_vma=False
    )
```

profile of v0, /device:TPU:0, one launch (start us, length us, event | category | flops | bytes accessed | tf_op | source)
XLA Modules:
  0.0 120.9 jit_solution(937389232059725203)
XLA Ops:
  6.6 1.3 %slice_bitcast_fusion = (bf16[4,5,64,64]{3,2,1,0:T(8,128)(2,1)S(1)}, bf16[4,5,64,64]{3,2,1,0:T(8,128)(2,1)S(1)}, bf16[4,5,64,64]{3,2,1,0:T(8,128)(2,1)S(1)}) fusion(bf16[3,1,4,5,64,64]{5,4,3,2,1,0:T(8,128)(2,1)} %param.10), kind=kLoop, calls=%fused_computation.83 | loop fusion | bytes 983040 | tf_op jit(solution)/shard_map/squeeze | solution.py:54
  8.5 0.8 gather_fusion
  9.6 2.4 %collective-permute-start = (bf16[1,64,512]{2,1,0:T(8,128)(2,1)S(1)}, bf16[1,64,512]{2,1,0:T(8,128)(2,1)S(1)}, u32[]{:S(2)}, u32[]{:S(2)}) collective-permute-start(bf16[1,64,512]{2,1,0:T(8,128)(2,1)S(1)} %get-tuple-element.18), channel_id=1, source_target_pairs={{0,1},{1,2},{2,3},{4,5},{5,6},{6,7},{8,9},{9,10},{10,11},{12,13},{... | collective-permute-start | bytes 196616 | tf_op jit(solution)/shard_map/ppermute | solution.py:18
  11.9 1.3 %collective-permute-start.1 = (bf16[1,64,512]{2,1,0:T(8,128)(2,1)S(1)}, bf16[1,64,512]{2,1,0:T(8,128)(2,1)S(1)}, u32[]{:S(2)}, u32[]{:S(2)}) collective-permute-start(bf16[1,64,512]{2,1,0:T(8,128)(2,1)S(1)} %get-tuple-element.19), channel_id=1, source_target_pairs={{1,0},{2,1},{3,2},{5,4},{6,5},{7,6},{9,8},{10,9},{11,10},{13,12},{... | collective-permute-start | bytes 196616 | tf_op jit(solution)/shard_map/ppermute | solution.py:20
  13.2 0.6 compare_select_fusion.9
  13.9 0.6 compare_select_fusion
  14.7 0.6 fusion.102
  16.0 0.8 gather_fusion.4
  17.2 0.6 gather_fusion.1
  17.9 1.4 %fusion.62 = bf16[4,64,512]{2,1,0:T(8,128)(2,1)S(1)} fusion(f32[4,64,512]{2,1,0:T(8,128)S(1)} %bitcast.254, bf16[4,5,64,512]{3,2,1,0:T(8,128)(2,1)S(1)} %bitcast.245, bf16[3,1,4,5,64,64]{5,4,3,2,1,0:T(8,128)(2,1)} %param.10), kind=kOutput, calls=%fused_computation.59 | convolution fusion | flops 84148224 | bytes 2424832 | tf_op jit(solution)/shard_map/bsrc,bscn->brn/dot_general | solution.py:32
  19.3 2.1 %collective-permute-start.2 = (bf16[4,64,512]{2,1,0:T(8,128)(2,1)S(1)}, bf16[4,64,512]{2,1,0:T(8,128)(2,1)S(1)}, u32[]{:S(2)}, u32[]{:S(2)}) collective-permute-start(bf16[4,64,512]{2,1,0:T(8,128)(2,1)S(1)} %fusion.62), channel_id=1, source_target_pairs={{0,4},{4,0},{8,12},{12,8},{16,20},{20,16},{24,28},{28,24},{1,5},{5... | collective-permute-start | bytes 786440 | tf_op jit(solution)/shard_map/ppermute | solution.py:28
  22.3 0.8 gather_fusion.8
  23.2 0.6 gather_fusion.2
  23.8 2.7 %collective-permute-done.2 = bf16[4,64,512]{2,1,0:T(8,128)(2,1)S(1)} collective-permute-done((bf16[4,64,512]{2,1,0:T(8,128)(2,1)S(1)}, bf16[4,64,512]{2,1,0:T(8,128)(2,1)S(1)}, u32[]{:S(2)}, u32[]{:S(2)}) %collective-permute-start.2) | collective-permute-done | bytes 262176 | tf_op jit(solution)/shard_map/ppermute | solution.py:28
  26.5 0.6 gather_fusion.3
  27.1 1.3 %convolution_bitcast_fusion.8 = f32[4,512,64]{1,2,0:T(8,128)S(1)} fusion(bf16[4,3,64,512]{3,2,1,0:T(8,128)(2,1)S(1)} %bitcast.248, bf16[4,3,64,512]{3,2,1,0:T(8,128)(2,1)S(1)} %bitcast.250, pred[4,3]{1,0:T(4,128)(4,1)S(1)} %bitcast.267, bf16[3,1,4,3,64,64]{5,4,3,2,1,0:T(8,128)(2,1)} %param.12), kind=kOutput, calls=%fused_computation.38 | convolution fusion | flops 50724864 | bytes 2293772 | tf_op jit(solution)/shard_map/bsrc,bscn->brn/dot_general | solution.py:32
  28.6 3.8 %collective-permute-start.3 = (bf16[1,64,512]{2,1,0:T(8,128)(2,1)S(1)}, bf16[1,64,512]{2,1,0:T(8,128)(2,1)S(1)}, u32[]{:S(2)}, u32[]{:S(2)}) collective-permute-start(bf16[1,64,512]{2,1,0:T(8,128)(2,1)S(1)} %get-tuple-element.16), channel_id=1, source_target_pairs={{0,1},{1,2},{2,3},{4,5},{5,6},{6,7},{8,9},{9,10},{10,11},{12,13},{... | collective-permute-start | bytes 196616 | tf_op jit(solution)/shard_map/ppermute | solution.py:18
  32.3 1.3 %collective-permute-start.4 = (bf16[1,64,512]{2,1,0:T(8,128)(2,1)S(1)}, bf16[1,64,512]{2,1,0:T(8,128)(2,1)S(1)}, u32[]{:S(2)}, u32[]{:S(2)}) collective-permute-start(bf16[1,64,512]{2,1,0:T(8,128)(2,1)S(1)} %get-tuple-element.17), channel_id=1, source_target_pairs={{1,0},{2,1},{3,2},{5,4},{6,5},{7,6},{9,8},{10,9},{11,10},{13,12},{... | collective-permute-start | bytes 196616 | tf_op jit(solution)/shard_map/ppermute | solution.py:20
  33.7 3.9 %collective-permute-done.4 = bf16[1,64,512]{2,1,0:T(8,128)(2,1)S(1)} collective-permute-done((bf16[1,64,512]{2,1,0:T(8,128)(2,1)S(1)}, bf16[1,64,512]{2,1,0:T(8,128)(2,1)S(1)}, u32[]{:S(2)}, u32[]{:S(2)}) %collective-permute-start.4) | collective-permute-done | bytes 65568 | tf_op jit(solution)/shard_map/ppermute | solution.py:20
  37.6 0.6 gather_fusion.5
  38.3 1.4 %fusion.76 = bf16[4,64,512]{2,1,0:T(8,128)(2,1)S(1)} fusion(f32[4,512,64]{1,2,0:T(8,128)S(1)} %convolution_bitcast_fusion.8, bf16[4,5,64,512]{3,2,1,0:T(8,128)(2,1)S(1)} %bitcast.246, bf16[3,1,4,5,64,64]{5,4,3,2,1,0:T(8,128)(2,1)} %param.10), kind=kOutput, calls=%fused_computation.66 | convolution fusion | flops 84148224 | bytes 2424832 | tf_op jit(solution)/shard_map/bsrc,bscn->brn/dot_general | solution.py:32
  39.7 1.6 %collective-permute-start.5 = (bf16[4,64,512]{2,1,0:T(8,128)(2,1)S(1)}, bf16[4,64,512]{2,1,0:T(8,128)(2,1)S(1)}, u32[]{:S(2)}, u32[]{:S(2)}) collective-permute-start(bf16[4,64,512]{2,1,0:T(8,128)(2,1)S(1)} %fusion.76), channel_id=1, source_target_pairs={{0,8},{4,12},{8,0},{12,4},{16,24},{20,28},{24,16},{28,20},{1,9},{5... | collective-permute-start | bytes 786440 | tf_op jit(solution)/shard_map/ppermute | solution.py:28
  41.5 0.6 gather_fusion.6
  42.1 4.8 %collective-permute-done.5 = bf16[4,64,512]{2,1,0:T(8,128)(2,1)S(1)} collective-permute-done((bf16[4,64,512]{2,1,0:T(8,128)(2,1)S(1)}, bf16[4,64,512]{2,1,0:T(8,128)(2,1)S(1)}, u32[]{:S(2)}, u32[]{:S(2)}) %collective-permute-start.5) | collective-permute-done | bytes 262176 | tf_op jit(solution)/shard_map/ppermute | solution.py:28
  46.9 0.6 gather_fusion.7
  47.5 1.3 %convolution_bitcast_fusion.7 = f32[4,512,64]{1,2,0:T(8,128)S(1)} fusion(bf16[4,3,64,512]{3,2,1,0:T(8,128)(2,1)S(1)} %bitcast.249, bf16[4,3,64,512]{3,2,1,0:T(8,128)(2,1)S(1)} %bitcast.251, pred[4,3]{1,0:T(4,128)(4,1)S(1)} %bitcast.266, bf16[3,1,4,3,64,64]{5,4,3,2,1,0:T(8,128)(2,1)} %param.12), kind=kOutput, calls=%fused_computation.37 | convolution fusion | flops 50724864 | bytes 2293772 | tf_op jit(solution)/shard_map/bsrc,bscn->brn/dot_general | solution.py:32
  49.0 3.8 %collective-permute-start.6 = (bf16[1,64,512]{2,1,0:T(8,128)(2,1)S(1)}, bf16[1,64,512]{2,1,0:T(8,128)(2,1)S(1)}, u32[]{:S(2)}, u32[]{:S(2)}) collective-permute-start(bf16[1,64,512]{2,1,0:T(8,128)(2,1)S(1)} %get-tuple-element.14), channel_id=1, source_target_pairs={{0,1},{1,2},{2,3},{4,5},{5,6},{6,7},{8,9},{9,10},{10,11},{12,13},{... | collective-permute-start | bytes 196616 | tf_op jit(solution)/shard_map/ppermute | solution.py:18
  52.7 1.3 %collective-permute-start.7 = (bf16[1,64,512]{2,1,0:T(8,128)(2,1)S(1)}, bf16[1,64,512]{2,1,0:T(8,128)(2,1)S(1)}, u32[]{:S(2)}, u32[]{:S(2)}) collective-permute-start(bf16[1,64,512]{2,1,0:T(8,128)(2,1)S(1)} %get-tuple-element.15), channel_id=1, source_target_pairs={{1,0},{2,1},{3,2},{5,4},{6,5},{7,6},{9,8},{10,9},{11,10},{13,12},{... | collective-permute-start | bytes 196616 | tf_op jit(solution)/shard_map/ppermute | solution.py:20
  54.0 1.8 %collective-permute-done.7 = bf16[1,64,512]{2,1,0:T(8,128)(2,1)S(1)} collective-permute-done((bf16[1,64,512]{2,1,0:T(8,128)(2,1)S(1)}, bf16[1,64,512]{2,1,0:T(8,128)(2,1)S(1)}, u32[]{:S(2)}, u32[]{:S(2)}) %collective-permute-start.7) | collective-permute-done | bytes 65568 | tf_op jit(solution)/shard_map/ppermute | solution.py:20
  55.9 0.6 gather_fusion.9
  56.6 1.4 %fusion.77 = bf16[4,64,512]{2,1,0:T(8,128)(2,1)S(1)} fusion(f32[4,512,64]{1,2,0:T(8,128)S(1)} %convolution_bitcast_fusion.7, bf16[4,5,64,512]{3,2,1,0:T(8,128)(2,1)S(1)} %bitcast.247, bf16[3,1,4,5,64,64]{5,4,3,2,1,0:T(8,128)(2,1)} %param.10), kind=kOutput, calls=%fused_computation.67 | convolution fusion | flops 84148224 | bytes 2424832 | tf_op jit(solution)/shard_map/bsrc,bscn->brn/dot_general | solution.py:32
  58.0 2.7 %collective-permute-start.8 = (bf16[4,64,512]{2,1,0:T(8,128)(2,1)S(1)}, bf16[4,64,512]{2,1,0:T(8,128)(2,1)S(1)}, u32[]{:S(2)}, u32[]{:S(2)}) collective-permute-start(bf16[4,64,512]{2,1,0:T(8,128)(2,1)S(1)} %fusion.77), channel_id=1, source_target_pairs={{0,16},{4,20},{8,24},{12,28},{16,0},{20,4},{24,8},{28,12},{1,17},{... | collective-permute-start | bytes 786440 | tf_op jit(solution)/shard_map/ppermute | solution.py:28
  60.9 0.6 gather_fusion.10
  61.5 11.0 %collective-permute-done.8 = bf16[4,64,512]{2,1,0:T(8,128)(2,1)S(1)} collective-permute-done((bf16[4,64,512]{2,1,0:T(8,128)(2,1)S(1)}, bf16[4,64,512]{2,1,0:T(8,128)(2,1)S(1)}, u32[]{:S(2)}, u32[]{:S(2)}) %collective-permute-start.8) | collective-permute-done | bytes 262176 | tf_op jit(solution)/shard_map/ppermute | solution.py:28
  72.6 1.5 %gather_fusion.11 = bf16[12,64,512]{2,1,0:T(8,128)(2,1)} fusion(bf16[4,64,512]{2,1,0:T(8,128)(2,1)S(1)} %collective-permute-done.8, s32[1024]{0:T(1024)S(1)} %pad_clamp_fusion.6), kind=kCustom, calls=%fused_computation.11 | custom fusion | bytes 1572912 | tf_op jit(solution)/shard_map/gather | solution.py:69
  74.1 2.4 %fusion.69 = bf16[4,512,64]{1,2,0:T(8,128)(2,1)} fusion(bf16[4,3,64,512]{3,2,1,0:T(8,128)(2,1)S(1)} %bitcast.260, bf16[4,3,64,512]{3,2,1,0:T(8,128)(2,1)} %bitcast.261, pred[4,3]{1,0:T(4,128)(4,1)S(1)} %bitcast.271, bf16[3,1,4,3,64,64]{5,4,3,2,1,0:T(8,128)(2,1)} %param.12), kind=kOutput, calls=%fused_computation.62 | convolution fusion | flops 50855936 | bytes 2031628 | tf_op jit(solution)/shard_map/bsrc,bscn->brn/dot_general | solution.py:32
  77.4 17.3 %all-gather.2.cloned.1.call-done = bf16[1024,512]{1,0:T(8,128)(2,1)} async-done(((bf16[256,512]{1,0:T(8,128)(2,1)}), bf16[1024,512]{1,0:T(8,128)(2,1)}) %all-gather.2.cloned.1.call-update) | async-done | bytes 1048592 | tf_op jit(solution)/shard_map/all_gather | solution.py:76
  94.6 1.7 %convolution_convert_fusion = bf16[512,256]{0,1:T(8,128)(2,1)S(1)} fusion(bf16[256,1024]{1,0:T(8,128)(2,1)S(1)} %copy-done, bf16[1024,512]{1,0:T(8,128)(2,1)} %all-gather.2.cloned.1.call-done), kind=kOutput, calls=%fused_computation.63 | convolution fusion | flops 268566528 | bytes 1835008 | tf_op jit(solution)/shard_map/dot_general | solution.py:74
  96.9 1.2 fusion.57
  98.1 1.8 %gather_fusion.13 = bf16[20,64,512]{2,1,0:T(8,128)(2,1)} fusion(bf16[4,64,512]{2,1,0:T(8,128)(2,1)S(1)} %convert_bitcast_fusion.1, s32[1024]{0:T(1024)S(1)} %pad_clamp_fusion.4), kind=kCustom, calls=%fused_computation.13 | custom fusion | bytes 2621520 | tf_op jit(solution)/shard_map/gather | solution.py:90
  99.9 1.8 %fusion.70 = bf16[4,64,512]{2,1,0:T(8,128)(2,1)S(1)} fusion(f32[4,512,64]{1,2,0:T(8,128)S(1)} %fusion.57, f32[4,512,64]{1,2,0:T(8,128)S(1)} %convolution_bitcast_fusion.7, bf16[4,5,64,512]{3,2,1,0:T(8,128)(2,1)} %bitcast.258, pred[4,5]{1,0:T(4,128)(4,1)S(1)} %bitcast.270, f32[4,64]{1,0:T(4,128)S(1)} %copy.33, bf16[3,1,4,5,64,64]{5,4,3,2,1,0:T(8,128)(2,1)S(1)} %copy-done.1), kind=kOutput, calls=%fused_computation.64 | convolution fusion | flops 85196800 | bytes 2951680 | tf_op jit(solution)/shard_map/bsrc,bscn->brn/dot_general | solution.py:32
  101.7 0.6 gather_fusion.14
  102.3 1.2 fusion.58
  103.5 1.8 %gather_fusion.15 = bf16[20,64,512]{2,1,0:T(8,128)(2,1)} fusion(bf16[4,64,512]{2,1,0:T(8,128)(2,1)S(1)} %convert_bitcast_fusion, s32[1024]{0:T(1024)S(1)} %pad_clamp_fusion.2), kind=kCustom, calls=%fused_computation.15 | custom fusion | bytes 2621520 | tf_op jit(solution)/shard_map/gather | solution.py:90
  105.3 1.8 %fusion.73 = bf16[4,64,512]{2,1,0:T(8,128)(2,1)S(1)} fusion(f32[4,512,64]{1,2,0:T(8,128)S(1)} %fusion.58, f32[4,512,64]{1,2,0:T(8,128)S(1)} %convolution_bitcast_fusion.8, bf16[4,5,64,512]{3,2,1,0:T(8,128)(2,1)} %bitcast.259, pred[4,5]{1,0:T(4,128)(4,1)S(1)} %bitcast.269, f32[4,64]{1,0:T(4,128)S(1)} %copy.29, bf16[3,1,4,5,64,64]{5,4,3,2,1,0:T(8,128)(2,1)S(1)} %copy-done.1), kind=kOutput, calls=%fused_computation.65 | convolution fusion | flops 85196800 | bytes 2951680 | tf_op jit(solution)/shard_map/bsrc,bscn->brn/dot_general | solution.py:32
  107.8 2.0 %fusion.112 = (bf16[4,64,512]{2,1,0:T(8,128)(2,1)S(1)}, f32[4,64,512]{2,1,0:T(8,128)}) fusion(bf16[4,2,64,512]{3,2,1,0:T(8,128)(2,1)S(1)} %bitcast.262, bf16[3,1,4,2,64,64]{5,4,3,2,1,0:T(8,128)(2,1)} %param.14, f32[4,64]{1,0:T(4,128)S(1)} %copy.25, f32[4,64,512]{2,1,0:T(8,128)S(1)} %bitcast.255), kind=kOutput, calls=%fused_computation.161 | convolution fusion | flops 34078720 | bytes 1967104 | tf_op jit(solution)/shard_map/bsrc,bscn->brn/dot_general | solution.py:32
  109.7 1.8 %gather_fusion.17 = bf16[20,64,512]{2,1,0:T(8,128)(2,1)} fusion(bf16[4,64,512]{2,1,0:T(8,128)(2,1)S(1)} %get-tuple-element.38, s32[1024]{0:T(1024)S(1)} %pad_clamp_fusion), kind=kCustom, calls=%fused_computation.17 | custom fusion | bytes 2621520 | tf_op jit(solution)/shard_map/gather | solution.py:90
  111.5 2.6 %fusion.51 = f32[4,64,512]{2,1,0:T(8,128)} fusion(f32[4,64,512]{2,1,0:T(8,128)S(1)} %copy-done.14, f32[4,64,512]{2,1,0:T(8,128)S(1)} %bitcast.256, bf16[4,5,64,512]{3,2,1,0:T(8,128)(2,1)} %bitcast.257, pred[4,5]{1,0:T(4,128)(4,1)S(1)} %bitcast.268, f32[4,64]{1,0:T(4,128)S(1)} %copy.25, bf16[3,1,4,5,64,64]{5,4,3,2,1,0:T(8,128)(2,1)S(1)} %copy-done.1), kind=kOutput, calls=%fused_computation.50 | convolution fusion | flops 85065728 | bytes 3213824 | tf_op jit(solution)/shard_map/bsrc,bscn->brn/dot_general | solution.py:32
  (95 shorter events, 6.1 us)
Async XLA Ops:
  6.5 88.1 %copy-start = (bf16[256,1024]{1,0:T(8,128)(2,1)S(1)}, bf16[256,1024]{1,0:T(8,128)(2,1)}, u32[]{:S(2)}) copy-start(bf16[256,1024]{1,0:T(8,128)(2,1)} %param.15) | copy-start | bytes 1572868
  6.5 88.1 %all-gather.2.cloned.1.call-start = ((), (), s32[]{:S(2)}) async-start(), calls=%async_computation | async-start | bytes 1310720 | tf_op jit(solution)/shard_map/all_gather | solution.py:76
  6.5 2.9 %copy-start.2 = (f32[1,256,512]{2,1,0:T(8,128)S(1)}, f32[1,256,512]{2,1,0:T(8,128)}, u32[]{:S(2)}) copy-start(f32[1,256,512]{2,1,0:T(8,128)} %param.8) | copy-start | bytes 1572868
  7.9 5.3 %copy-start.8 = (s32[3,1,4,5]{3,2,1,0:T(4,128)S(1)}, s32[3,1,4,5]{3,2,1,0:T(4,128)}, u32[]{:S(2)}) copy-start(s32[3,1,4,5]{3,2,1,0:T(4,128)} %param.9) | copy-start | bytes 724
  7.9 6.0 %copy-start.4 = (s32[3,1,4,3]{2,1,3,0:T(1,128)S(1)}, s32[3,1,4,3]{2,1,3,0:T(1,128)}, u32[]{:S(2)}) copy-start(s32[3,1,4,3]{2,1,3,0:T(1,128)} %param.11) | copy-start | bytes 436
  9.6 7.2 %collective-permute-start = (bf16[1,64,512]{2,1,0:T(8,128)(2,1)S(1)}, bf16[1,64,512]{2,1,0:T(8,128)(2,1)S(1)}, u32[]{:S(2)}, u32[]{:S(2)}) collective-permute-start(bf16[1,64,512]{2,1,0:T(8,128)(2,1)S(1)} %get-tuple-element.18), channel_id=1, source_target_pairs={{0,1},{1,2},{2,3},{4,5},{5,6},{6,7},{8,9},{9,10},{10,11},{12,13},{... | collective-permute-start | bytes 196616 | tf_op jit(solution)/shard_map/ppermute | solution.py:18
  11.9 5.3 %collective-permute-start.1 = (bf16[1,64,512]{2,1,0:T(8,128)(2,1)S(1)}, bf16[1,64,512]{2,1,0:T(8,128)(2,1)S(1)}, u32[]{:S(2)}, u32[]{:S(2)}) collective-permute-start(bf16[1,64,512]{2,1,0:T(8,128)(2,1)S(1)} %get-tuple-element.19), channel_id=1, source_target_pairs={{1,0},{2,1},{3,2},{5,4},{6,5},{7,6},{9,8},{10,9},{11,10},{13,12},{... | collective-permute-start | bytes 196616 | tf_op jit(solution)/shard_map/ppermute | solution.py:20
  19.3 7.2 %collective-permute-start.2 = (bf16[4,64,512]{2,1,0:T(8,128)(2,1)S(1)}, bf16[4,64,512]{2,1,0:T(8,128)(2,1)S(1)}, u32[]{:S(2)}, u32[]{:S(2)}) collective-permute-start(bf16[4,64,512]{2,1,0:T(8,128)(2,1)S(1)} %fusion.62), channel_id=1, source_target_pairs={{0,4},{4,0},{8,12},{12,8},{16,20},{20,16},{24,28},{28,24},{1,5},{5... | collective-permute-start | bytes 786440 | tf_op jit(solution)/shard_map/ppermute | solution.py:28
  28.6 5.1 %collective-permute-start.3 = (bf16[1,64,512]{2,1,0:T(8,128)(2,1)S(1)}, bf16[1,64,512]{2,1,0:T(8,128)(2,1)S(1)}, u32[]{:S(2)}, u32[]{:S(2)}) collective-permute-start(bf16[1,64,512]{2,1,0:T(8,128)(2,1)S(1)} %get-tuple-element.16), channel_id=1, source_target_pairs={{0,1},{1,2},{2,3},{4,5},{5,6},{6,7},{8,9},{9,10},{10,11},{12,13},{... | collective-permute-start | bytes 196616 | tf_op jit(solution)/shard_map/ppermute | solution.py:18
  32.3 5.2 %collective-permute-start.4 = (bf16[1,64,512]{2,1,0:T(8,128)(2,1)S(1)}, bf16[1,64,512]{2,1,0:T(8,128)(2,1)S(1)}, u32[]{:S(2)}, u32[]{:S(2)}) collective-permute-start(bf16[1,64,512]{2,1,0:T(8,128)(2,1)S(1)} %get-tuple-element.17), channel_id=1, source_target_pairs={{1,0},{2,1},{3,2},{5,4},{6,5},{7,6},{9,8},{10,9},{11,10},{13,12},{... | collective-permute-start | bytes 196616 | tf_op jit(solution)/shard_map/ppermute | solution.py:20
  39.7 7.2 %collective-permute-start.5 = (bf16[4,64,512]{2,1,0:T(8,128)(2,1)S(1)}, bf16[4,64,512]{2,1,0:T(8,128)(2,1)S(1)}, u32[]{:S(2)}, u32[]{:S(2)}) collective-permute-start(bf16[4,64,512]{2,1,0:T(8,128)(2,1)S(1)} %fusion.76), channel_id=1, source_target_pairs={{0,8},{4,12},{8,0},{12,4},{16,24},{20,28},{24,16},{28,20},{1,9},{5... | collective-permute-start | bytes 786440 | tf_op jit(solution)/shard_map/ppermute | solution.py:28
  49.0 5.1 %collective-permute-start.6 = (bf16[1,64,512]{2,1,0:T(8,128)(2,1)S(1)}, bf16[1,64,512]{2,1,0:T(8,128)(2,1)S(1)}, u32[]{:S(2)}, u32[]{:S(2)}) collective-permute-start(bf16[1,64,512]{2,1,0:T(8,128)(2,1)S(1)} %get-tuple-element.14), channel_id=1, source_target_pairs={{0,1},{1,2},{2,3},{4,5},{5,6},{6,7},{8,9},{9,10},{10,11},{12,13},{... | collective-permute-start | bytes 196616 | tf_op jit(solution)/shard_map/ppermute | solution.py:18
  52.7 3.1 %collective-permute-start.7 = (bf16[1,64,512]{2,1,0:T(8,128)(2,1)S(1)}, bf16[1,64,512]{2,1,0:T(8,128)(2,1)S(1)}, u32[]{:S(2)}, u32[]{:S(2)}) collective-permute-start(bf16[1,64,512]{2,1,0:T(8,128)(2,1)S(1)} %get-tuple-element.15), channel_id=1, source_target_pairs={{1,0},{2,1},{3,2},{5,4},{6,5},{7,6},{9,8},{10,9},{11,10},{13,12},{... | collective-permute-start | bytes 196616 | tf_op jit(solution)/shard_map/ppermute | solution.py:20
  56.6 4.1 %copy-start.7 = (s32[4,3,1]{0,2,1:T(1,128)S(1)}, s32[4,3,1]{0,2,1:T(1,128)}, u32[]{:S(2)}) copy-start(s32[4,3,1]{0,2,1:T(1,128)} %get-tuple-element.32) | copy-start | bytes 148
  56.6 4.2 %copy-start.9 = (pred[1,1,4,3]{2,1,3,0:T(4,128)(4,1)S(1)}, pred[1,1,4,3]{2,1,3,0:T(4,128)(4,1)}, u32[]{:S(2)}) copy-start(pred[1,1,4,3]{2,1,3,0:T(4,128)(4,1)} %get-tuple-element.29) | copy-start | bytes 40
  58.0 14.6 %collective-permute-start.8 = (bf16[4,64,512]{2,1,0:T(8,128)(2,1)S(1)}, bf16[4,64,512]{2,1,0:T(8,128)(2,1)S(1)}, u32[]{:S(2)}, u32[]{:S(2)}) collective-permute-start(bf16[4,64,512]{2,1,0:T(8,128)(2,1)S(1)} %fusion.77), channel_id=1, source_target_pairs={{0,16},{4,20},{8,24},{12,28},{16,0},{20,4},{24,8},{28,12},{1,17},{... | collective-permute-start | bytes 786440 | tf_op jit(solution)/shard_map/ppermute | solution.py:28
  74.1 2.4 %copy-start.10 = (s32[3,1,4,2]{2,3,1,0:T(2,128)S(1)}, s32[3,1,4,2]{2,3,1,0:T(2,128)}, u32[]{:S(2)}) copy-start(s32[3,1,4,2]{2,3,1,0:T(2,128)} %param.13) | copy-start | bytes 292
  74.1 2.6 %copy-start.6 = (s32[4,5,1]{1,0,2:T(4,128)S(1)}, s32[4,5,1]{1,0,2:T(4,128)}, u32[]{:S(2)}) copy-start(s32[4,5,1]{1,0,2:T(4,128)} %get-tuple-element.24) | copy-start | bytes 244
  74.1 2.9 %copy-start.5 = (s32[4,5,1]{1,0,2:T(4,128)S(1)}, s32[4,5,1]{1,0,2:T(4,128)}, u32[]{:S(2)}) copy-start(s32[4,5,1]{1,0,2:T(4,128)} %get-tuple-element.21) | copy-start | bytes 244
  98.1 1.8 %copy-start.1 = (bf16[3,1,4,5,64,64]{5,4,3,2,1,0:T(8,128)(2,1)S(1)}, bf16[3,1,4,5,64,64]{5,4,3,2,1,0:T(8,128)(2,1)}, u32[]{:S(2)}) copy-start(bf16[3,1,4,5,64,64]{5,4,3,2,1,0:T(8,128)(2,1)} %param.10) | copy-start | bytes 1474564
  98.1 1.8 %copy-start.13 = (pred[1,1,4,5]{3,2,1,0:T(4,128)(4,1)S(1)}, pred[1,1,4,5]{3,2,1,0:T(4,128)(4,1)}, u32[]{:S(2)}) copy-start(pred[1,1,4,5]{3,2,1,0:T(4,128)(4,1)} %get-tuple-element.23) | copy-start | bytes 64
  103.5 1.8 %copy-start.12 = (pred[1,1,4,5]{3,2,1,0:T(4,128)(4,1)S(1)}, pred[1,1,4,5]{3,2,1,0:T(4,128)(4,1)}, u32[]{:S(2)}) copy-start(pred[1,1,4,5]{3,2,1,0:T(4,128)(4,1)} %get-tuple-element.26) | copy-start | bytes 64
  105.3 2.4 %copy-start.3 = (f32[1,256,512]{2,1,0:T(8,128)S(1)}, f32[1,256,512]{2,1,0:T(8,128)}, u32[]{:S(2)}) copy-start(f32[1,256,512]{2,1,0:T(8,128)} %param.8) | copy-start | bytes 1572868
  109.7 1.8 %copy-start.11 = (pred[1,1,4,5]{3,2,1,0:T(4,128)(4,1)S(1)}, pred[1,1,4,5]{3,2,1,0:T(4,128)(4,1)}, u32[]{:S(2)}) copy-start(pred[1,1,4,5]{3,2,1,0:T(4,128)(4,1)} %get-tuple-element.28) | copy-start | bytes 64
  109.7 1.8 %copy-start.14 = (f32[4,64,512]{2,1,0:T(8,128)S(1)}, f32[4,64,512]{2,1,0:T(8,128)}, u32[]{:S(2)}) copy-start(f32[4,64,512]{2,1,0:T(8,128)} %get-tuple-element.39) | copy-start | bytes 1572868
Sparse Core Ops, SparseCore 0:
  76.6 17.9 all-gather.1
where the time goes:
time: 122 us; the launch traced here: 121 us
  waiting for transfers between devices  41.9 us (34%)
  matrix products  21.3 us (17%)
  local copies, waits for them, and re-layouts  21.2 us (17%)
  starting transfers between devices  20.1 us (16%)
  between operations  13.9 us (11%)
  other arithmetic  2.46 us (2%)
    dot_general x12, matrix products, block_apply(): jnp.einsum('bsrc,bscn->brn', blocks, picked, preferred_element_type=jnp.f...  19.7 us
    ppermute x3, waiting for transfers between devices, from_partner(): lax.ppermute(value, axis, [(i, i ^ 1 << stride) for i in range(lax.axis_s...  18.5 us
    all_gather x1, waiting for transfers between devices, on_device(): lax.all_gather(flat_rhs, 'narrow', axis=0, tiled=True)  17.3 us
    ppermute x3, starting transfers between devices, extended(): lax.ppermute(tail, axis, [(i, (i + 1) % count) for i in range(ends)])  9.88 us
    ppermute x3, starting transfers between devices, from_partner(): lax.ppermute(value, axis, [(i, i ^ 1 << stride) for i in range(lax.axis_s...  6.35 us
    ppermute x3, waiting for transfers between devices, extended(): lax.ppermute(head, axis, [((i + 1) % count, i) for i in range(ends)])  6.11 us
    gather x3, local copies, waits for them, and re-layouts, on_device(): updated_bf[jnp.minimum(col_ids, blocks_dev - 1)]  5.36 us
    ppermute x3, starting transfers between devices, extended(): lax.ppermute(head, axis, [((i + 1) % count, i) for i in range(ends)])  3.88 us
  transfers between devices with their start and end apart: 10, of which 7 were waited for; matrix products, arithmetic and copies ran while one was open for 7% of the time, Pallas kernels for 0%

commit v1 on v0

v1 whole, which is shorter than its diff:
```python
import functools

import jax
import jax.numpy as jnp
from jax import lax
from jax.experimental import pallas as pl
from jax.experimental.pallas import tpu as pltpu
from jax.sharding import PartitionSpec as P

relax_down = 0.7
relax_up = 0.5
f32 = jnp.float32
bf16 = jnp.bfloat16
grant = 12 * 1024 * 1024


def matmul(a, b):
    return jnp.dot(a, b, preferred_element_type=f32)


def array(shape, dtype):
    return jax.ShapeDtypeStruct(shape, dtype)


def whole():
    return pl.BlockSpec(memory_space=pltpu.VMEM)


def level_block(value, level_idx):
    shape = (1,) + value.shape[1:]
    return pl.BlockSpec(shape, lambda i: (level_idx,) + (0,) * (value.ndim - 1))


def scalars():
    return pl.BlockSpec(memory_space=pltpu.SMEM)


def run(body, name, outs, operands, flops=0):
    arrays = [o[0] if isinstance(o, tuple) else o for o in operands]
    specs = [o[1] if isinstance(o, tuple) else whole() for o in operands]
    windows = any(isinstance(o, tuple) and o[1].block_shape is not None for o in operands)
    moved = sum(a.size * a.dtype.itemsize for a in arrays)
    return pl.pallas_call(
        body,
        grid=(1,) if windows else (),
        out_shape=outs,
        in_specs=specs,
        out_specs=[pl.BlockSpec(memory_space=pltpu.VMEM)] * len(outs),
        compiler_params=pltpu.CompilerParams(vmem_limit_bytes=grant),
        cost_estimate=pl.CostEstimate(flops=flops, bytes_accessed=moved, transcendentals=0),
        name=name,
    )(*arrays)


def diagonal_of(block):
    size = block.shape[0]
    rows = lax.broadcasted_iota(jnp.int32, (size, size), 0)
    lanes = lax.broadcasted_iota(jnp.int32, (size, size), 1)
    return jnp.sum(jnp.where(rows == lanes, block, 0.0), axis=1, keepdims=True)


def placed(base, others, ids, target):
    total = base
    for block, ident in zip(others, ids):
        term = block * jnp.where(ident == target, 1.0, 0.0).astype(f32)
        total = term if total is None else total + term
    return total


def parity_of():
    return lax.rem(lax.axis_index("narrow"), 2)


def put_ends(first, last, even_ref, odd_ref):
    even = parity_of() == 0
    even_ref[...] = jnp.where(even, last, first)
    odd_ref[...] = jnp.where(even, first, last)


def assemble_galerkin(level_idx, cols, blocks, local_ref, rim_ref, scale_ref):
    count, slots, size = blocks.shape[2], blocks.shape[3], blocks.shape[4]
    parity = parity_of()
    for b in range(count):
        held = [blocks[0, 0, b, s].astype(f32) for s in range(slots)]
        ids = [cols[level_idx, 0, b, s] for s in range(1, slots)]
        rows = pl.ds(b * size, size)
        scale_ref[rows, :] = 1.0 / diagonal_of(held[0])
        line = [placed(held[0] if c == b else None, held[1:], ids, c) for c in range(count)]
        local_ref[rows, :] = jnp.concatenate(line, axis=1).astype(bf16)
        rims = [
            placed(None, held[1:], ids, count + 1 - parity),
            placed(None, held[1:], ids, count + parity),
        ]
        rim_ref[rows, :] = jnp.concatenate(rims, axis=1).astype(bf16)


def assemble_restrict(level_idx, cols, blocks, out_ref):
    count, slots, size = blocks.shape[2], blocks.shape[3], blocks.shape[4]
    for b in range(count):
        held = [blocks[0, 0, b, s].astype(f32) for s in range(slots)]
        ids = [cols[level_idx, 0, b, s] for s in range(2, slots)]
        fixed = {b: held[0], count + b: held[1]}
        line = [placed(fixed.get(c), held[2:], ids, c) for c in range(2 * count)]
        out_ref[pl.ds(b * size, size), :] = jnp.concatenate(line, axis=1).astype(bf16)


def assemble_prolong(level_idx, cols, blocks, out_ref):
    count, slots, size = blocks.shape[2], blocks.shape[3], blocks.shape[4]
    for b in range(count):
        held = [blocks[0, 0, b, s].astype(f32) for s in range(slots)]
        ids = [cols[level_idx, 0, b, s] for s in range(1, slots)]
        line = [placed(held[0] if c == b else None, held[1:], ids, c) for c in range(count)]
        out_ref[pl.ds(b * size, size), :] = jnp.concatenate(line, axis=1).astype(bf16)


def start_kernel(first_rhs, last_rhs, first_block, last_block, even_ref, odd_ref):
    first = first_rhs[0] * (relax_down / diagonal_of(first_block[0, 0, 0, 0].astype(f32)))
    last = last_rhs[0] * (relax_down / diagonal_of(last_block[0, 0, 0, 0].astype(f32)))
    put_ends(first.astype(bf16), last.astype(bf16), even_ref, odd_ref)


def first_local_kernel(rhs, _, cols, blocks, rcols, rblocks, rest, local, rim, scale, rmat):
    assemble_galerkin(0, cols, blocks, local, rim, scale)
    smoothed = (rhs[0] * (relax_down * scale[...])).astype(bf16)
    rest[...] = rhs[0] - matmul(local[...], smoothed)
    assemble_restrict(0, rcols, rblocks, rmat)


def split_residual_kernel(rest, rim, from_even, from_odd, sent, kept):
    half = sent.shape[1]
    upper = lax.rem(lax.axis_index("wide"), 2)
    for ref, side in ((sent, 1 - upper), (kept, upper)):
        lanes = pl.ds(pl.multiple_of(side * half, half), half)
        rims = jnp.concatenate([from_even[:, lanes], from_odd[:, lanes]], axis=0)
        ref[...] = (rest[:, lanes] - matmul(rim[...], rims)).astype(bf16)


def residual_kernel(rest, rim, from_even, from_odd, out):
    rims = jnp.concatenate([from_even[...], from_odd[...]], axis=0)
    out[...] = (rest[...] - matmul(rim[...], rims)).astype(bf16)


def side_of(rmat, level_idx, own):
    width = rmat.shape[1] // 2
    bit = lax.axis_index("wide") >> level_idx & 1
    side = bit if own else 1 - bit
    return rmat[:, pl.ds(pl.multiple_of(side * width, width), width)]


def own_part_kernel(level_idx, residual, rmat, *refs):
    if len(refs) > 1:
        cols, blocks, rcols, rblocks, part, local, rim, scale, next_rmat = refs
        part[...] = matmul(side_of(rmat, level_idx, True), residual[...])
        assemble_galerkin(level_idx + 1, cols, blocks, local, rim, scale)
        assemble_restrict(level_idx + 1, rcols, rblocks, next_rmat)
    else:
        (part,) = refs
        part[...] = matmul(side_of(rmat, level_idx, True), residual[...])


def join_kernel(level_idx, part, rmat, other, scale, rhs, smoothed, even_ref, odd_ref):
    size = even_ref.shape[0]
    current = part[...] + matmul(side_of(rmat, level_idx, False), other[...])
    rhs[...] = current
    rounded = (current * (relax_down * scale[...])).astype(bf16)
    smoothed[...] = rounded
    put_ends(rounded[:size], rounded[-size:], even_ref, odd_ref)


def last_join_kernel(level_idx, part, rmat, other, rounded):
    current = part[...] + matmul(side_of(rmat, level_idx, False), other[...])
    rounded[...] = current.astype(bf16)


def local_kernel(rhs, local, smoothed, rest):
    rest[...] = rhs[...] - matmul(local[...], smoothed[...])


def inverse_part(inverse, part, offset):
    depth = part.shape[0]
    piece = lax.axis_index("narrow") ^ offset
    return matmul(inverse[:, pl.ds(pl.multiple_of(piece * depth, depth), depth)], part[...])


def coarse_kernel(offsets, with_total, *refs):
    inverse, parts, refs = refs[0], refs[1 : 1 + len(offsets)], refs[1 + len(offsets) :]
    total = refs[0][...] if with_total else None
    for part, offset in zip(parts, offsets):
        term = inverse_part(inverse, part, offset)
        total = term if total is None else total + term
    refs[-1][...] = total


def prolong_kernel(levels, pcols, *refs):
    for level_idx, blocks, out in zip(levels, refs[: len(levels)], refs[len(levels) :]):
        assemble_prolong(level_idx, pcols, blocks, out)


def raise_level(coarse, rhs, scale, local, pmat):
    updated = rhs * (relax_down * scale) + matmul(pmat, coarse)
    applied = matmul(local, updated.astype(bf16))
    return updated + (relax_up * scale) * (rhs - applied)


def up_kernel(offset, depth, inverse, part, total, *refs):
    value = total[...] + inverse_part(inverse, part, offset)
    for step in range(depth):
        rhs, scale, local, pmat = refs[4 * step : 4 * step + 4]
        value = raise_level(value.astype(bf16), rhs[...], scale[...], local[...], pmat[...])
    refs[-1][...] = value.astype(bf16)


def final_own_kernel(coarse, rhs, scale, local, pmat, out):
    half = coarse.shape[1]
    side = lax.rem(lax.axis_index("wide"), 2)
    lanes = pl.ds(pl.multiple_of(side * half, half), half)
    out[...] = raise_level(coarse[...], rhs[0, :, lanes], scale[...], local[...], pmat[...])


def final_kernel(own, coarse, rhs, scale, local, pmat, out):
    half = coarse.shape[1]
    side = lax.rem(lax.axis_index("wide"), 2)
    lanes = pl.ds(pl.multiple_of(side * half, half), half)
    out[0, :, lanes] = own[...]
    lanes = pl.ds(pl.multiple_of((1 - side) * half, half), half)
    out[0, :, lanes] = raise_level(coarse[...], rhs[0, :, lanes], scale[...], local[...], pmat[...])


def exchange(value, axis, bit):
    count = lax.axis_size(axis)
    return lax.ppermute(value, axis, [(i, i ^ bit) for i in range(count)])


def swap_ends(even, odd):
    count = lax.axis_size("narrow")
    pairs = [(i, i ^ 1) for i in range(count) if i ^ 1 < count]
    gaps = [(i, i + 1) for i in range(1, count - 1, 2)]
    gaps = gaps + [(b, a) for a, b in gaps]
    return lax.ppermute(even, "narrow", pairs), lax.ppermute(odd, "narrow", gaps)


def on_device(
    level_rhs,
    galerkin_cols,
    galerkin_blocks,
    restrict_cols,
    restrict_blocks,
    prolong_cols,
    prolong_blocks,
    coarse_inverse,
):
    levels = galerkin_cols.shape[0]
    count = galerkin_cols.shape[2]
    size = galerkin_blocks.shape[-1]
    rows, fields = level_rhs.shape[1:]
    half = fields // 2
    gcols, rcols, pcols = ((c, scalars()) for c in (galerkin_cols, restrict_cols, prolong_cols))
    local_shape = array((rows, rows), bf16)
    rim_shape = array((rows, 2 * size), bf16)
    scale_shape = array((rows, 1), f32)
    rmat_shape = array((rows, 2 * rows), bf16)

    def ends(width):
        return array((size, width), bf16)

    def of_level(value, level_idx):
        return value, level_block(value, level_idx)

    def end_rows(which):
        return level_rhs, pl.BlockSpec((1, size, fields), lambda i: (0, which, 0))

    def end_block(which):
        return galerkin_blocks, pl.BlockSpec((1, 1, 1, 1, size, size), lambda i: (0, 0, which, 0, 0, 0))

    even, odd = run(
        start_kernel, "start", [ends(fields), ends(fields)],
        [end_rows(0), end_rows(count - 1), end_block(0), end_block(count - 1)],
    )
    from_even, from_odd = swap_ends(even, odd)
    rest, local, rim, scale, rmat = run(
        first_local_kernel, "first_local",
        [array((rows, fields), f32), local_shape, rim_shape, scale_shape, rmat_shape],
        [level_rhs, even, gcols, of_level(galerkin_blocks, 0), rcols, of_level(restrict_blocks, 0)],
        flops=2 * rows * rows * fields,
    )
    operators = [(local, scale)]
    sent, kept = run(
        split_residual_kernel, "split_residual", [array((rows, half), bf16)] * 2,
        [rest, rim, from_even, from_odd],
    )
    right_sides = [None]
    for level_idx in range(levels):
        other = exchange(sent, "wide", 1 << level_idx)
        square = 2 * rows * rows * half
        if level_idx + 1 < levels:
            part, local, rim, scale, next_rmat = run(
                functools.partial(own_part_kernel, level_idx), "own_part",
                [array((rows, half), f32), local_shape, rim_shape, scale_shape, rmat_shape],
                [kept, rmat, gcols, of_level(galerkin_blocks, level_idx + 1),
                 rcols, of_level(restrict_blocks, level_idx + 1)],
                flops=square,
            )
            operators.append((local, scale))
            rhs, smoothed, even, odd = run(
                functools.partial(join_kernel, level_idx), "join",
                [array((rows, half), f32), array((rows, half), bf16), ends(half), ends(half)],
                [part, rmat, other, scale],
                flops=square,
            )
            right_sides.append(rhs)
            rmat = next_rmat
            from_even, from_odd = swap_ends(even, odd)
            (rest,) = run(
                local_kernel, "local", [array((rows, half), f32)], [rhs, local, smoothed], flops=square
            )
            (sent,) = run(
                residual_kernel, "residual", [array((rows, half), bf16)], [rest, rim, from_even, from_odd]
            )
            kept = sent
        else:
            (part,) = run(
                functools.partial(own_part_kernel, level_idx), "own_part",
                [array((rows, half), f32)], [kept, rmat], flops=square,
            )
            (mine,) = run(
                functools.partial(last_join_kernel, level_idx), "last_join",
                [array((rows, half), bf16)], [part, rmat, other], flops=square,
            )
    pmats = run(
        functools.partial(prolong_kernel, tuple(range(levels))), "prolong_ops",
        [local_shape] * levels,
        [pcols] + [of_level(prolong_blocks, level_idx) for level_idx in range(levels)],
    )
    pieces = lax.axis_size("narrow")
    parts = {0: mine}
    order = sorted(range(1, pieces), key=lambda o: (bin(o).count("1"), -o))
    for offset in order:
        low = offset & -offset
        parts[offset] = exchange(parts[offset ^ low], "narrow", low)
    total_shape = [array((rows, half), f32)]
    square = 2 * rows * rows * half
    (total,) = run(
        functools.partial(coarse_kernel, (0,), False), "coarse_own", total_shape,
        [coarse_inverse, mine], flops=square,
    )
    middle = tuple(order[:-1])
    if middle:
        (total,) = run(
            functools.partial(coarse_kernel, middle, True), "coarse_middle", total_shape,
            [coarse_inverse] + [parts[o] for o in middle] + [total], flops=square * len(middle),
        )
    operands = []
    for level_idx in reversed(range(1, levels)):
        local, scale = operators[level_idx]
        operands += [right_sides[level_idx], scale, local, pmats[level_idx]]
    (coarse,) = run(
        functools.partial(up_kernel, order[-1], levels - 1), "up", [array((rows, half), bf16)],
        [coarse_inverse, parts[order[-1]], total] + operands, flops=square * (1 + 2 * (levels - 1)),
    )
    other = exchange(coarse, "wide", 1)
    local, scale = operators[0]
    (own,) = run(
        final_own_kernel, "final_own", [array((rows, half), f32)],
        [coarse, level_rhs, scale, local, pmats[0]], flops=2 * square,
    )
    (result,) = run(
        final_kernel, "final", [array((1, rows, fields), f32)],
        [own, other, level_rhs, scale, local, pmats[0]], flops=2 * square,
    )
    return result


def solution(mesh):
    in_specs = (
        P("wide", "narrow", None),
        P(None, "wide", "narrow", None),
        P(None, "wide", "narrow", None, None, None),
        P(None, "wide", "narrow", None),
        P(None, "wide", "narrow", None, None, None),
        P(None, "wide", "narrow", None),
        P(None, "wide", "narrow", None, None, None),
        P("narrow", None),
    )
    out_specs = P("wide", "narrow", None)
    return jax.shard_map(
        on_device, mesh=mesh, in_specs=in_specs, out_specs=out_specs, check_vma=False
    )
```

time: 122 us -> 53.4 us (0.44)
  waiting for transfers between devices: 41.9 us -> 15.1 us
  matrix products: 21.3 us -> 0 us
  local copies, waits for them, and re-layouts: 21.2 us -> 2.79 us
  between operations: 13.9 us -> 0.26 us
  Pallas kernels: 0 us -> 9.12 us
  starting transfers between devices: 20.1 us -> 25.8 us
  other arithmetic: 2.46 us -> 0 us
    dot_general x13 -> x0, matrix products: 21.3 us -> none  [the longest x12 19.7 us: block_apply(): jnp.einsum('bsrc,bscn->brn', blocks, picked, preferred_element_type=jnp.f...]
    all_gather x1 -> x0, waiting for transfers between devices: 17.3 us -> none  [on_device(): lax.all_gather(flat_rhs, 'narrow', axis=0, tiled=True)]
    gather x18 -> x0, local copies, waits for them, and re-layouts: 16 us -> none  [the longest x3 5.36 us: on_device(): updated_bf[jnp.minimum(col_ids, blocks_dev - 1)]]
    ppermute x9 -> x13, waiting for transfers between devices: 24.6 us -> 15.1 us  [the longest x7 15.1 us: exchange(): return lax.ppermute(value, axis, [(i, i ^ bit) for i in range(count)])]
    pallas_call x0 -> x19, Pallas kernels: none -> 9.12 us  [run(): pl.pallas_call(body, grid=(1,) if windows else (), out_shape=outs, in_spe...]
    ppermute x9 -> x13, starting transfers between devices: 20.1 us -> 25.8 us  [the longest x7 16.4 us: exchange(): return lax.ppermute(value, axis, [(i, i ^ bit) for i in range(count)])]
    squeeze x6 -> x0, local copies, waits for them, and re-layouts: 2.98 us -> none  [the longest x5 1.64 us: on_device(): blocks[:, 0]]
    unnamed x30 -> x22, local copies, waits for them, and re-layouts: 0.07 us -> 2.79 us
  transfers between devices with their start and end apart: 10 -> 13, of which waited for: 7 -> 5; matrix products, arithmetic and copies ran while one was open for 7% -> 0% of each run, Pallas kernels for 0% -> 11%
where the time goes in v1:
time: 53.4 us; the launch traced here: 53.1 us
  starting transfers between devices  25.8 us (48%)
  waiting for transfers between devices  15.1 us (28%)
  Pallas kernels  9.12 us (17%)
  local copies, waits for them, and re-layouts  2.79 us (5%)
    ppermute x7, starting transfers between devices, exchange(): return lax.ppermute(value, axis, [(i, i ^ bit) for i in range(count)])  16.4 us
    ppermute x7, waiting for transfers between devices, exchange(): return lax.ppermute(value, axis, [(i, i ^ bit) for i in range(count)])  15.1 us
    pallas_call x19, Pallas kernels, run(): pl.pallas_call(body, grid=(1,) if windows else (), out_shape=outs, in_spe...  9.12 us
    ppermute x3, starting transfers between devices, swap_ends(): lax.ppermute(even, 'narrow', pairs)  7.47 us
    unnamed x22, local copies, waits for them, and re-layouts  2.79 us
    ppermute x3, starting transfers between devices, swap_ends(): lax.ppermute(odd, 'narrow', gaps)  1.95 us
  transfers between devices with their start and end apart: 13, of which 5 were waited for; matrix products, arithmetic and copies ran while one was open for 0% of the time, Pallas kernels for 11%

profile of v1, /device:TPU:0, one launch (start us, length us, event | category | flops | bytes accessed | tf_op | source)
XLA Modules:
  0.0 53.1 jit_solution(8495946677092070134)
XLA Ops:
  0.0 1.2 %copy-done = bf16[3,1,4,5,64,64]{5,4,3,2,1,0:T(8,128)(2,1)S(1)} copy-done((bf16[3,1,4,5,64,64]{5,4,3,2,1,0:T(8,128)(2,1)S(1)}, bf16[3,1,4,5,64,64]{5,4,3,2,1,0:T(8,128)(2,1)}, u32[]{:S(2)}) %copy-start) | copy-done | bytes 491544
  1.2 1.0 %copy-done.2 = f32[1,256,512]{2,1,0:T(8,128)S(1)} copy-done((f32[1,256,512]{2,1,0:T(8,128)S(1)}, f32[1,256,512]{2,1,0:T(8,128)}, u32[]{:S(2)}) %copy-start.2) | copy-done | bytes 524312
  2.3 0.1 start.1
  2.4 0.0 copy-start.7
  2.4 0.5 collective-permute-start
  2.9 0.7 %collective-permute-start.1 = (bf16[64,512]{1,0:T(8,128)(2,1)S(1)}, bf16[64,512]{1,0:T(8,128)(2,1)S(1)}, u32[]{:S(2)}, u32[]{:S(2)}) collective-permute-start(bf16[64,512]{1,0:T(8,128)(2,1)S(1)} %get-tuple-element.38), channel_id=1, source_target_pairs={{1,2},{2,1},{5,6},{6,5},{9,10},{10,9},{13,14},{14,13},{17,18},{18,... | collective-permute-start | bytes 196616 | tf_op jit(solution)/shard_map/ppermute | solution.py:239
  3.6 0.1 copy.9.rcols.refs_2_
  3.7 0.1 copy-done.4
  3.8 1.3 %first_local.1 = (f32[256,512]{1,0:T(8,128)S(1)}, bf16[256,256]{1,0:T(8,128)(2,1)S(1)}, bf16[256,128]{1,0:T(8,128)(2,1)S(1)}, f32[256,1]{1,0:T(8,128)S(1)}, bf16[256,512]{1,0:T(8,128)(2,1)S(1)}) custom-call(f32[1,256,512]{2,1,0:T(8,128)S(1)} %copy-done.3, bf16[64,512]{1,0:T(8,128)(2,1)S(1)} %get-tuple-element.35._, s32[3,1,4,5]{3,2,1,0:T(4,128)S(1)} %copy-done.7, ...), custom_call_target="tpu_custom_call" | custom-call | flops 67108864 | bytes 1376640 | tf_op jit(solution)/shard_map/first_local/pallas_call | solution.py:43
  5.1 0.0 collective-permute-done.1.from_odd
  5.1 0.2 split_residual.1
  5.3 3.0 %collective-permute-start.2 = (bf16[256,256]{1,0:T(8,128)(2,1)S(1)}, bf16[256,256]{1,0:T(8,128)(2,1)S(1)}, u32[]{:S(2)}, u32[]{:S(2)}) collective-permute-start(bf16[256,256]{1,0:T(8,128)(2,1)S(1)} %get-tuple-element.42), channel_id=1, source_target_pairs={{0,4},{4,0},{8,12},{12,8},{16,20},{20,16},{24,28},{28,24},{1,5},{5... | collective-permute-start | bytes 393224 | tf_op jit(solution)/shard_map/ppermute | solution.py:231
  8.3 1.1 %own_part.3 = (f32[256,256]{1,0:T(8,128)S(1)}, bf16[256,256]{1,0:T(8,128)(2,1)S(1)}, bf16[256,128]{1,0:T(8,128)(2,1)S(1)}, f32[256,1]{1,0:T(8,128)S(1)}, bf16[256,512]{1,0:T(8,128)(2,1)S(1)}) custom-call(bf16[256,256]{1,0:T(8,128)(2,1)S(1)} %get-tuple-element.39.residual, bf16[256,512]{1,0:T(8,128)(2,1)S(1)} %get-tuple-element.40.rmat, ...), custom_call_target="tpu_custom_call" | custom-call | flops 33554432 | bytes 1180032 | tf_op jit(solution)/shard_map/own_part/pallas_call | solution.py:43
  9.5 1.8 %collective-permute-done.2.other = bf16[256,256]{1,0:T(8,128)(2,1)S(1)} collective-permute-done((bf16[256,256]{1,0:T(8,128)(2,1)S(1)}, bf16[256,256]{1,0:T(8,128)(2,1)S(1)}, u32[]{:S(2)}, u32[]{:S(2)}) %collective-permute-start.2) | collective-permute-done | bytes 131104 | tf_op jit(solution)/shard_map/ppermute | solution.py:231
  11.3 0.2 join.2
  11.5 2.7 %collective-permute-start.3 = (bf16[64,256]{1,0:T(8,128)(2,1)S(1)}, bf16[64,256]{1,0:T(8,128)(2,1)S(1)}, u32[]{:S(2)}, u32[]{:S(2)}) collective-permute-start(bf16[64,256]{1,0:T(8,128)(2,1)S(1)} %get-tuple-element.48), channel_id=1, source_target_pairs={{0,1},{1,0},{2,3},{3,2},{4,5},{5,4},{6,7},{7,6},{8,9},{9,8},{10,11... | collective-permute-start | bytes 98312 | tf_op jit(solution)/shard_map/ppermute | solution.py:239
  14.1 0.7 %collective-permute-start.4 = (bf16[64,256]{1,0:T(8,128)(2,1)S(1)}, bf16[64,256]{1,0:T(8,128)(2,1)S(1)}, u32[]{:S(2)}, u32[]{:S(2)}) collective-permute-start(bf16[64,256]{1,0:T(8,128)(2,1)S(1)} %get-tuple-element.49), channel_id=1, source_target_pairs={{1,2},{2,1},{5,6},{6,5},{9,10},{10,9},{13,14},{14,13},{17,18},{18,... | collective-permute-start | bytes 98312 | tf_op jit(solution)/shard_map/ppermute | solution.py:239
  14.8 0.2 local.2.rest
  15.0 0.0 collective-permute-done.3.from_even
  15.0 0.2 residual.2
  15.2 1.9 %collective-permute-start.5 = (bf16[256,256]{1,0:T(8,128)(2,1)S(1)}, bf16[256,256]{1,0:T(8,128)(2,1)S(1)}, u32[]{:S(2)}, u32[]{:S(2)}) collective-permute-start(bf16[256,256]{1,0:T(8,128)(2,1)S(1)} %residual.2), channel_id=1, source_target_pairs={{0,8},{4,12},{8,0},{12,4},{16,24},{20,28},{24,16},{28,20},{1,9},{5... | collective-permute-start | bytes 393224 | tf_op jit(solution)/shard_map/ppermute | solution.py:231
  17.1 1.1 %own_part.4 = (f32[256,256]{1,0:T(8,128)S(1)}, bf16[256,256]{1,0:T(8,128)(2,1)S(1)}, bf16[256,128]{1,0:T(8,128)(2,1)S(1)}, f32[256,1]{1,0:T(8,128)S(1)}, bf16[256,512]{1,0:T(8,128)(2,1)S(1)}) custom-call(bf16[256,256]{1,0:T(8,128)(2,1)S(1)} %residual.2, bf16[256,512]{1,0:T(8,128)(2,1)S(1)} %get-tuple-element.50.rmat, s32[3,1,4,5]{3,2,1,0:T(4,128)S(1)} %copy-done.7, ...), custom_call_target="tpu_custom_call" | custom-call | flops 33554432 | bytes 1180032 | tf_op jit(solution)/shard_map/own_part/pallas_call | solution.py:43
  18.2 2.0 %collective-permute-done.5.other = bf16[256,256]{1,0:T(8,128)(2,1)S(1)} collective-permute-done((bf16[256,256]{1,0:T(8,128)(2,1)S(1)}, bf16[256,256]{1,0:T(8,128)(2,1)S(1)}, u32[]{:S(2)}, u32[]{:S(2)}) %collective-permute-start.5) | collective-permute-done | bytes 131104 | tf_op jit(solution)/shard_map/ppermute | solution.py:231
  20.2 0.2 join.3
  20.4 4.3 %collective-permute-start.6 = (bf16[64,256]{1,0:T(8,128)(2,1)S(1)}, bf16[64,256]{1,0:T(8,128)(2,1)S(1)}, u32[]{:S(2)}, u32[]{:S(2)}) collective-permute-start(bf16[64,256]{1,0:T(8,128)(2,1)S(1)} %get-tuple-element.57), channel_id=1, source_target_pairs={{0,1},{1,0},{2,3},{3,2},{4,5},{5,4},{6,7},{7,6},{8,9},{9,8},{10,11... | collective-permute-start | bytes 98312 | tf_op jit(solution)/shard_map/ppermute | solution.py:239
  24.7 0.7 %collective-permute-start.7 = (bf16[64,256]{1,0:T(8,128)(2,1)S(1)}, bf16[64,256]{1,0:T(8,128)(2,1)S(1)}, u32[]{:S(2)}, u32[]{:S(2)}) collective-permute-start(bf16[64,256]{1,0:T(8,128)(2,1)S(1)} %get-tuple-element.58), channel_id=1, source_target_pairs={{1,2},{2,1},{5,6},{6,5},{9,10},{10,9},{13,14},{14,13},{17,18},{18,... | collective-permute-start | bytes 98312 | tf_op jit(solution)/shard_map/ppermute | solution.py:239
  25.4 0.2 local.3.rest
  25.6 0.0 collective-permute-done.6.from_even
  25.6 0.0 collective-permute-done.7.from_odd
  25.6 0.2 residual.3
  25.8 2.8 %collective-permute-start.8 = (bf16[256,256]{1,0:T(8,128)(2,1)S(1)}, bf16[256,256]{1,0:T(8,128)(2,1)S(1)}, u32[]{:S(2)}, u32[]{:S(2)}) collective-permute-start(bf16[256,256]{1,0:T(8,128)(2,1)S(1)} %residual.3), channel_id=1, source_target_pairs={{0,16},{4,20},{8,24},{12,28},{16,0},{20,4},{24,8},{28,12},{1,17},{... | collective-permute-start | bytes 393224 | tf_op jit(solution)/shard_map/ppermute | solution.py:231
  28.6 0.2 own_part.5.part
  28.8 0.0 copy-start.9
  28.8 0.0 copy-start.6
  28.8 4.3 %collective-permute-done.8.other = bf16[256,256]{1,0:T(8,128)(2,1)S(1)} collective-permute-done((bf16[256,256]{1,0:T(8,128)(2,1)S(1)}, bf16[256,256]{1,0:T(8,128)(2,1)S(1)}, u32[]{:S(2)}, u32[]{:S(2)}) %collective-permute-start.8) | collective-permute-done | bytes 131104 | tf_op jit(solution)/shard_map/ppermute | solution.py:231
  33.1 0.2 last_join.1.refs_1_
  33.3 7.1 %collective-permute-start.9 = (bf16[256,256]{1,0:T(8,128)(2,1)S(1)}, bf16[256,256]{1,0:T(8,128)(2,1)S(1)}, u32[]{:S(2)}, u32[]{:S(2)}) collective-permute-start(bf16[256,256]{1,0:T(8,128)(2,1)S(1)} %last_join.1.refs_1_), channel_id=1, source_target_pairs={{0,2},{1,3},{2,0},{3,1},{4,6},{5,7},{6,4},{7,5},{8,10},{9,11},{10,... | collective-permute-start | bytes 393224 | tf_op jit(solution)/shard_map/ppermute | solution.py:231
  40.4 2.9 %collective-permute-done.9.refs_1_ = bf16[256,256]{1,0:T(8,128)(2,1)S(1)} collective-permute-done((bf16[256,256]{1,0:T(8,128)(2,1)S(1)}, bf16[256,256]{1,0:T(8,128)(2,1)S(1)}, u32[]{:S(2)}, u32[]{:S(2)}) %collective-permute-start.9) | collective-permute-done | bytes 131104 | tf_op jit(solution)/shard_map/ppermute | solution.py:231
  43.4 0.1 copy.12.pcols
  43.5 0.8 %prolong_ops.1 = (bf16[256,256]{1,0:T(8,128)(2,1)S(1)}, bf16[256,256]{1,0:T(8,128)(2,1)S(1)}, bf16[256,256]{1,0:T(8,128)(2,1)S(1)}) custom-call(s32[3,1,4,2]{3,2,1,0:T(4,128)S(1)} %copy.12.pcols, bf16[3,1,4,2,64,64]{5,4,3,2,1,0:T(8,128)(2,1)S(1)} %copy-done.6, bf16[3,1,4,2,64,64]{5,4,3,2,1,0:T(8,128)(2,1)S(1)} %copy-done.6, ...), custom_call_target="tpu_custom_call" | custom-call | bytes 589920 | tf_op jit(solution)/shard_map/prolong_ops/pallas_call | solution.py:43
  44.3 0.2 copy-done.5
  44.5 0.2 coarse_own.1.refs_3_
  44.7 0.2 coarse_middle.1.total
  44.9 1.0 %up.1.coarse = bf16[256,256]{1,0:T(8,128)(2,1)S(1)} custom-call(bf16[256,1024]{1,0:T(8,128)(2,1)S(1)} %copy-done.5, bf16[256,256]{1,0:T(8,128)(2,1)S(1)} %collective-permute-done.10.part, f32[256,256]{1,0:T(8,128)S(1)} %coarse_middle.1.total, f32[256,256]{1,0:T(8,128)S(1)} %get-tuple-element.53.rhs.refs_0_, f32[256,1]{1,0:T(8,128)S(1)} %get-tuple-element.52.scale.refs_1_, ...), custom_call_target="tpu_custom_call" | custom-call | flops 167772160 | bytes 1968128 | tf_op jit(solution)/shard_map/up/pallas_call | solution.py:43
  45.9 1.6 %collective-permute-start.12 = (bf16[256,256]{1,0:T(8,128)(2,1)S(1)}, bf16[256,256]{1,0:T(8,128)(2,1)S(1)}, u32[]{:S(2)}, u32[]{:S(2)}) collective-permute-start(bf16[256,256]{1,0:T(8,128)(2,1)S(1)} %up.1.coarse), channel_id=1, source_target_pairs={{0,4},{4,0},{8,12},{12,8},{16,20},{20,16},{24,28},{28,24},{1,5},{5... | collective-permute-start | bytes 393224 | tf_op jit(solution)/shard_map/ppermute | solution.py:231
  47.5 0.4 final_own.1.own
  47.9 4.0 %collective-permute-done.12.coarse = bf16[256,256]{1,0:T(8,128)(2,1)S(1)} collective-permute-done((bf16[256,256]{1,0:T(8,128)(2,1)S(1)}, bf16[256,256]{1,0:T(8,128)(2,1)S(1)}, u32[]{:S(2)}, u32[]{:S(2)}) %collective-permute-start.12) | collective-permute-done | bytes 131104 | tf_op jit(solution)/shard_map/ppermute | solution.py:231
  51.9 1.2 %final.1 = f32[1,256,512]{2,1,0:T(8,128)} custom-call(f32[256,256]{1,0:T(8,128)S(1)} %final_own.1.own, bf16[256,256]{1,0:T(8,128)(2,1)S(1)} %collective-permute-done.12.coarse, f32[1,256,512]{2,1,0:T(8,128)S(1)} %copy-done.3, f32[256,1]{1,0:T(8,128)S(1)} %get-tuple-element.62.scale, bf16[256,256]{1,0:T(8,128)(2,1)S(1)} %get-tuple-element.63.local, ...), custom_call_target="tpu_custom_call" | custom-call | flops 67108864 | bytes 1180672 | tf_op jit(solution)/shard_map/final/pallas_call | solution.py:43
  (19 shorter events, 0.0 us)
Async XLA Ops:
  0.0 1.2 %copy-start = (bf16[3,1,4,5,64,64]{5,4,3,2,1,0:T(8,128)(2,1)S(1)}, bf16[3,1,4,5,64,64]{5,4,3,2,1,0:T(8,128)(2,1)}, u32[]{:S(2)}) copy-start(bf16[3,1,4,5,64,64]{5,4,3,2,1,0:T(8,128)(2,1)} %refs_1_.4) | copy-start | bytes 1474564
  1.2 1.0 %copy-start.2 = (f32[1,256,512]{2,1,0:T(8,128)S(1)}, f32[1,256,512]{2,1,0:T(8,128)}, u32[]{:S(2)}) copy-start(f32[1,256,512]{2,1,0:T(8,128)} %rhs.5) | copy-start | bytes 1572868
  2.2 1.3 %copy-start.8 = (s32[3,1,4,3]{2,1,3,0:T(1,128)S(1)}, s32[3,1,4,3]{2,1,3,0:T(1,128)}, u32[]{:S(2)}) copy-start(s32[3,1,4,3]{2,1,3,0:T(1,128)} %param.11) | copy-start | bytes 436
  2.2 1.4 %copy-start.1 = (bf16[3,1,4,5,64,64]{5,4,3,2,1,0:T(8,128)(2,1)S(1)}, bf16[3,1,4,5,64,64]{5,4,3,2,1,0:T(8,128)(2,1)}, u32[]{:S(2)}) copy-start(bf16[3,1,4,5,64,64]{5,4,3,2,1,0:T(8,128)(2,1)} %refs_1_.4) | copy-start | bytes 1474564
  2.2 1.4 %copy-start.3 = (f32[1,256,512]{2,1,0:T(8,128)S(1)}, f32[1,256,512]{2,1,0:T(8,128)}, u32[]{:S(2)}) copy-start(f32[1,256,512]{2,1,0:T(8,128)} %rhs.5) | copy-start | bytes 1572868
  2.3 1.5 %copy-start.4 = (bf16[3,1,4,3,64,64]{5,4,3,2,1,0:T(8,128)(2,1)S(1)}, bf16[3,1,4,3,64,64]{5,4,3,2,1,0:T(8,128)(2,1)}, u32[]{:S(2)}) copy-start(bf16[3,1,4,3,64,64]{5,4,3,2,1,0:T(8,128)(2,1)} %refs_3_.3) | copy-start | bytes 884740
  2.4 1.4 %copy-start.7 = (s32[3,1,4,5]{3,2,1,0:T(4,128)S(1)}, s32[3,1,4,5]{3,2,1,0:T(4,128)}, u32[]{:S(2)}) copy-start(s32[3,1,4,5]{3,2,1,0:T(4,128)} %refs_0_.6) | copy-start | bytes 724
  2.4 2.7 %collective-permute-start = (bf16[64,512]{1,0:T(8,128)(2,1)S(1)}, bf16[64,512]{1,0:T(8,128)(2,1)S(1)}, u32[]{:S(2)}, u32[]{:S(2)}) collective-permute-start(bf16[64,512]{1,0:T(8,128)(2,1)S(1)} %get-tuple-element.35._), channel_id=1, source_target_pairs={{0,1},{1,0},{2,3},{3,2},{4,5},{5,4},{6,7},{7,6},{8,9},{9,8},{10,11... | collective-permute-start | bytes 196616 | tf_op jit(solution)/shard_map/ppermute | solution.py:239
  2.9 2.2 %collective-permute-start.1 = (bf16[64,512]{1,0:T(8,128)(2,1)S(1)}, bf16[64,512]{1,0:T(8,128)(2,1)S(1)}, u32[]{:S(2)}, u32[]{:S(2)}) collective-permute-start(bf16[64,512]{1,0:T(8,128)(2,1)S(1)} %get-tuple-element.38), channel_id=1, source_target_pairs={{1,2},{2,1},{5,6},{6,5},{9,10},{10,9},{13,14},{14,13},{17,18},{18,... | collective-permute-start | bytes 196616 | tf_op jit(solution)/shard_map/ppermute | solution.py:239
  5.3 6.0 %collective-permute-start.2 = (bf16[256,256]{1,0:T(8,128)(2,1)S(1)}, bf16[256,256]{1,0:T(8,128)(2,1)S(1)}, u32[]{:S(2)}, u32[]{:S(2)}) collective-permute-start(bf16[256,256]{1,0:T(8,128)(2,1)S(1)} %get-tuple-element.42), channel_id=1, source_target_pairs={{0,4},{4,0},{8,12},{12,8},{16,20},{20,16},{24,28},{28,24},{1,5},{5... | collective-permute-start | bytes 393224 | tf_op jit(solution)/shard_map/ppermute | solution.py:231
  11.5 3.5 %collective-permute-start.3 = (bf16[64,256]{1,0:T(8,128)(2,1)S(1)}, bf16[64,256]{1,0:T(8,128)(2,1)S(1)}, u32[]{:S(2)}, u32[]{:S(2)}) collective-permute-start(bf16[64,256]{1,0:T(8,128)(2,1)S(1)} %get-tuple-element.48), channel_id=1, source_target_pairs={{0,1},{1,0},{2,3},{3,2},{4,5},{5,4},{6,7},{7,6},{8,9},{9,8},{10,11... | collective-permute-start | bytes 98312 | tf_op jit(solution)/shard_map/ppermute | solution.py:239
  14.1 0.9 %collective-permute-start.4 = (bf16[64,256]{1,0:T(8,128)(2,1)S(1)}, bf16[64,256]{1,0:T(8,128)(2,1)S(1)}, u32[]{:S(2)}, u32[]{:S(2)}) collective-permute-start(bf16[64,256]{1,0:T(8,128)(2,1)S(1)} %get-tuple-element.49), channel_id=1, source_target_pairs={{1,2},{2,1},{5,6},{6,5},{9,10},{10,9},{13,14},{14,13},{17,18},{18,... | collective-permute-start | bytes 98312 | tf_op jit(solution)/shard_map/ppermute | solution.py:239
  15.2 5.0 %collective-permute-start.5 = (bf16[256,256]{1,0:T(8,128)(2,1)S(1)}, bf16[256,256]{1,0:T(8,128)(2,1)S(1)}, u32[]{:S(2)}, u32[]{:S(2)}) collective-permute-start(bf16[256,256]{1,0:T(8,128)(2,1)S(1)} %residual.2), channel_id=1, source_target_pairs={{0,8},{4,12},{8,0},{12,4},{16,24},{20,28},{24,16},{28,20},{1,9},{5... | collective-permute-start | bytes 393224 | tf_op jit(solution)/shard_map/ppermute | solution.py:231
  20.4 5.2 %collective-permute-start.6 = (bf16[64,256]{1,0:T(8,128)(2,1)S(1)}, bf16[64,256]{1,0:T(8,128)(2,1)S(1)}, u32[]{:S(2)}, u32[]{:S(2)}) collective-permute-start(bf16[64,256]{1,0:T(8,128)(2,1)S(1)} %get-tuple-element.57), channel_id=1, source_target_pairs={{0,1},{1,0},{2,3},{3,2},{4,5},{5,4},{6,7},{7,6},{8,9},{9,8},{10,11... | collective-permute-start | bytes 98312 | tf_op jit(solution)/shard_map/ppermute | solution.py:239
  24.7 0.9 %collective-permute-start.7 = (bf16[64,256]{1,0:T(8,128)(2,1)S(1)}, bf16[64,256]{1,0:T(8,128)(2,1)S(1)}, u32[]{:S(2)}, u32[]{:S(2)}) collective-permute-start(bf16[64,256]{1,0:T(8,128)(2,1)S(1)} %get-tuple-element.58), channel_id=1, source_target_pairs={{1,2},{2,1},{5,6},{6,5},{9,10},{10,9},{13,14},{14,13},{17,18},{18,... | collective-permute-start | bytes 98312 | tf_op jit(solution)/shard_map/ppermute | solution.py:239
  25.8 7.3 %collective-permute-start.8 = (bf16[256,256]{1,0:T(8,128)(2,1)S(1)}, bf16[256,256]{1,0:T(8,128)(2,1)S(1)}, u32[]{:S(2)}, u32[]{:S(2)}) collective-permute-start(bf16[256,256]{1,0:T(8,128)(2,1)S(1)} %residual.3), channel_id=1, source_target_pairs={{0,16},{4,20},{8,24},{12,28},{16,0},{20,4},{24,8},{28,12},{1,17},{... | collective-permute-start | bytes 393224 | tf_op jit(solution)/shard_map/ppermute | solution.py:231
  28.8 14.6 %copy-start.9 = (s32[3,1,4,2]{2,3,1,0:T(2,128)S(1)}, s32[3,1,4,2]{2,3,1,0:T(2,128)}, u32[]{:S(2)}) copy-start(s32[3,1,4,2]{2,3,1,0:T(2,128)} %param.13) | copy-start | bytes 292
  28.8 14.7 %copy-start.6 = (bf16[3,1,4,2,64,64]{5,4,3,2,1,0:T(8,128)(2,1)S(1)}, bf16[3,1,4,2,64,64]{5,4,3,2,1,0:T(8,128)(2,1)}, u32[]{:S(2)}) copy-start(bf16[3,1,4,2,64,64]{5,4,3,2,1,0:T(8,128)(2,1)} %refs_2_.3) | copy-start | bytes 589828
  33.3 10.0 %collective-permute-start.9 = (bf16[256,256]{1,0:T(8,128)(2,1)S(1)}, bf16[256,256]{1,0:T(8,128)(2,1)S(1)}, u32[]{:S(2)}, u32[]{:S(2)}) collective-permute-start(bf16[256,256]{1,0:T(8,128)(2,1)S(1)} %last_join.1.refs_1_), channel_id=1, source_target_pairs={{0,2},{1,3},{2,0},{3,1},{4,6},{5,7},{6,4},{7,5},{8,10},{9,11},{10,... | collective-permute-start | bytes 393224 | tf_op jit(solution)/shard_map/ppermute | solution.py:231
  40.4 4.3 %collective-permute-start.11 = (bf16[256,256]{1,0:T(8,128)(2,1)S(1)}, bf16[256,256]{1,0:T(8,128)(2,1)S(1)}, u32[]{:S(2)}, u32[]{:S(2)}) collective-permute-start(bf16[256,256]{1,0:T(8,128)(2,1)S(1)} %last_join.1.refs_1_), channel_id=1, source_target_pairs={{0,1},{1,0},{2,3},{3,2},{4,5},{5,4},{6,7},{7,6},{8,9},{9,8},{10,11... | collective-permute-start | bytes 393224 | tf_op jit(solution)/shard_map/ppermute | solution.py:231
  43.3 1.6 %collective-permute-start.10 = (bf16[256,256]{1,0:T(8,128)(2,1)S(1)}, bf16[256,256]{1,0:T(8,128)(2,1)S(1)}, u32[]{:S(2)}, u32[]{:S(2)}) collective-permute-start(bf16[256,256]{1,0:T(8,128)(2,1)S(1)} %collective-permute-done.9.refs_1_), channel_id=1, source_target_pairs={{0,1},{1,0},{2,3},{3,2},{4,5},{5,4},{6,7},{7,6},{8,9},{9,8},{10,11... | collective-permute-start | bytes 393224 | tf_op jit(solution)/shard_map/ppermute | solution.py:231
  43.5 1.0 %copy-start.5 = (bf16[256,1024]{1,0:T(8,128)(2,1)S(1)}, bf16[256,1024]{1,0:T(8,128)(2,1)}, u32[]{:S(2)}) copy-start(bf16[256,1024]{1,0:T(8,128)(2,1)} %inverse.1) | copy-start | bytes 1572868
  45.9 6.0 %collective-permute-start.12 = (bf16[256,256]{1,0:T(8,128)(2,1)S(1)}, bf16[256,256]{1,0:T(8,128)(2,1)S(1)}, u32[]{:S(2)}, u32[]{:S(2)}) collective-permute-start(bf16[256,256]{1,0:T(8,128)(2,1)S(1)} %up.1.coarse), channel_id=1, source_target_pairs={{0,4},{4,0},{8,12},{12,8},{16,20},{20,16},{24,28},{28,24},{1,5},{5... | collective-permute-start | bytes 393224 | tf_op jit(solution)/shard_map/ppermute | solution.py:231

commit v2 on v1

v2 whole, which is shorter than its diff:
```python
import functools

import jax
import jax.numpy as jnp
from jax import lax
from jax.experimental import pallas as pl
from jax.experimental.pallas import tpu as pltpu
from jax.sharding import PartitionSpec as P

relax_down = 0.7
relax_up = 0.5
f32 = jnp.float32
bf16 = jnp.bfloat16
grant = 12 * 1024 * 1024


def matmul(a, b):
    return jnp.dot(a, b, preferred_element_type=f32)


def array(shape, dtype):
    return jax.ShapeDtypeStruct(shape, dtype)


def whole():
    return pl.BlockSpec(memory_space=pltpu.VMEM)


def level_block(value, level_idx):
    shape = (1,) + value.shape[1:]
    return pl.BlockSpec(shape, lambda i: (level_idx,) + (0,) * (value.ndim - 1))


def scalars():
    return pl.BlockSpec(memory_space=pltpu.SMEM)


def in_hbm(value):
    return pltpu.with_memory_space_constraint(value, pltpu.HBM), pl.BlockSpec(memory_space=pltpu.HBM)


def run(body, name, outs, operands, flops=0, scratch=()):
    arrays = [o[0] if isinstance(o, tuple) else o for o in operands]
    specs = [o[1] if isinstance(o, tuple) else whole() for o in operands]
    windows = any(isinstance(o, tuple) and o[1].block_shape is not None for o in operands)
    moved = sum(a.size * a.dtype.itemsize for a in arrays)
    return pl.pallas_call(
        body,
        grid=(1,) if windows else (),
        out_shape=outs,
        in_specs=specs,
        out_specs=[pl.BlockSpec(memory_space=pltpu.VMEM)] * len(outs),
        scratch_shapes=list(scratch),
        compiler_params=pltpu.CompilerParams(vmem_limit_bytes=grant),
        cost_estimate=pl.CostEstimate(flops=flops, bytes_accessed=moved, transcendentals=0),
        name=name,
    )(*arrays)


def diagonal_of(block):
    size = block.shape[0]
    rows = lax.broadcasted_iota(jnp.int32, (size, size), 0)
    lanes = lax.broadcasted_iota(jnp.int32, (size, size), 1)
    return jnp.sum(jnp.where(rows == lanes, block, 0.0), axis=1, keepdims=True)


def placed(base, others, ids, target):
    total = base
    for block, ident in zip(others, ids):
        term = block * jnp.where(ident == target, 1.0, 0.0).astype(f32)
        total = term if total is None else total + term
    return total


def parity_of():
    return lax.rem(lax.axis_index("narrow"), 2)


def put_ends(first, last, ends_ref):
    size = first.shape[0]
    even = parity_of() == 0
    ends_ref[:size, :] = jnp.where(even, last, first)
    ends_ref[size:, :] = jnp.where(even, first, last)


def assemble_galerkin(level_idx, cols, blocks, local_ref, rim_ref, scale_ref):
    count, slots, size = blocks.shape[2], blocks.shape[3], blocks.shape[4]
    parity = parity_of()
    for b in range(count):
        held = [blocks[0, 0, b, s].astype(f32) for s in range(slots)]
        ids = [cols[level_idx, 0, b, s] for s in range(1, slots)]
        rows = pl.ds(b * size, size)
        scale_ref[rows, :] = 1.0 / diagonal_of(held[0])
        line = [placed(held[0] if c == b else None, held[1:], ids, c) for c in range(count)]
        local_ref[rows, :] = jnp.concatenate(line, axis=1).astype(bf16)
        rims = [
            placed(None, held[1:], ids, count + 1 - parity),
            placed(None, held[1:], ids, count + parity),
        ]
        rim_ref[rows, :] = jnp.concatenate(rims, axis=1).astype(bf16)


def assemble_restrict(level_idx, cols, blocks, out_ref):
    count, slots, size = blocks.shape[2], blocks.shape[3], blocks.shape[4]
    for b in range(count):
        held = [blocks[0, 0, b, s].astype(f32) for s in range(slots)]
        ids = [cols[level_idx, 0, b, s] for s in range(2, slots)]
        fixed = {b: held[0], count + b: held[1]}
        line = [placed(fixed.get(c), held[2:], ids, c) for c in range(2 * count)]
        out_ref[pl.ds(b * size, size), :] = jnp.concatenate(line, axis=1).astype(bf16)


def assemble_prolong(level_idx, cols, blocks, out_ref):
    count, slots, size = blocks.shape[2], blocks.shape[3], blocks.shape[4]
    for b in range(count):
        held = [blocks[0, 0, b, s].astype(f32) for s in range(slots)]
        ids = [cols[level_idx, 0, b, s] for s in range(1, slots)]
        line = [placed(held[0] if c == b else None, held[1:], ids, c) for c in range(count)]
        out_ref[pl.ds(b * size, size), :] = jnp.concatenate(line, axis=1).astype(bf16)


def start_kernel(rhs, blocks, ends_ref, rows, pivots, sems):
    count, size = blocks.shape[2], blocks.shape[4]
    copies = []
    for slot, which in enumerate((0, count - 1)):
        source = rhs.at[0, pl.ds(which * size, size), :]
        copies.append(pltpu.make_async_copy(source, rows.at[slot], sems.at[slot]))
        source = blocks.at[0, 0, which, 0]
        copies.append(pltpu.make_async_copy(source, pivots.at[slot], sems.at[2 + slot]))
    for copy in copies:
        copy.start()
    for copy in copies:
        copy.wait()
    first, last = (
        (rows[slot] * (relax_down / diagonal_of(pivots[slot].astype(f32)))).astype(bf16)
        for slot in range(2)
    )
    put_ends(first, last, ends_ref)


def first_local_kernel(rhs, _, cols, blocks, rcols, rblocks, rest, local, rim, scale, rmat):
    assemble_galerkin(0, cols, blocks, local, rim, scale)
    smoothed = (rhs[0] * (relax_down * scale[...])).astype(bf16)
    rest[...] = rhs[0] - matmul(local[...], smoothed)
    assemble_restrict(0, rcols, rblocks, rmat)


def bit_of(level_idx):
    return lax.axis_index("wide") >> level_idx & 1


def residual_kernel(level_idx, rest, rim, inner, outer, *refs):
    size = outer.shape[0]
    if len(refs) == 1:
        rims = jnp.concatenate([inner[:size, :], outer[...]], axis=0)
        refs[0][...] = (rest[...] - matmul(rim[...], rims)).astype(bf16)
    else:
        half = refs[0].shape[1]
        bit = bit_of(level_idx)
        for ref, side in zip(refs, (1 - bit, bit)):
            lanes = pl.ds(pl.multiple_of(side * half, half), half)
            rims = jnp.concatenate([inner[:size, lanes], outer[:, lanes]], axis=0)
            ref[...] = (rest[:, lanes] - matmul(rim[...], rims)).astype(bf16)


def side_of(rmat, level_idx, own):
    width = rmat.shape[1] // 2
    bit = bit_of(level_idx)
    side = bit if own else 1 - bit
    return rmat[:, pl.ds(pl.multiple_of(side * width, width), width)]


def own_part_kernel(level_idx, residual, rmat, cols, blocks, rcols, rblocks, *refs):
    part, local, rim, scale, next_rmat = refs
    part[...] = matmul(side_of(rmat, level_idx, True), residual[...])
    assemble_galerkin(level_idx + 1, cols, blocks, local, rim, scale)
    assemble_restrict(level_idx + 1, rcols, rblocks, next_rmat)


def last_part_kernel(level_idx, levels, residual, rmat, pcols, *refs):
    refs[levels][...] = matmul(side_of(rmat, level_idx, True), residual[...])
    for idx, blocks, out in zip(range(levels), refs[:levels], refs[levels + 1 :]):
        assemble_prolong(idx, pcols, blocks, out)


def join_kernel(level_idx, part, rmat, other, scale, rhs, smoothed, ends_ref):
    size = ends_ref.shape[0] // 2
    current = part[...] + matmul(side_of(rmat, level_idx, False), other[...])
    rhs[...] = current
    rounded = (current * (relax_down * scale[...])).astype(bf16)
    smoothed[...] = rounded
    put_ends(rounded[:size], rounded[-size:], ends_ref)


def last_join_kernel(level_idx, part, rmat, other, rounded):
    current = part[...] + matmul(side_of(rmat, level_idx, False), other[...])
    rounded[...] = current.astype(bf16)


def local_kernel(rhs, local, smoothed, rest):
    rest[...] = rhs[...] - matmul(local[...], smoothed[...])


def inverse_part(inverse, part, offset):
    depth = part.shape[0]
    piece = lax.axis_index("narrow") ^ offset
    return matmul(inverse[:, pl.ds(pl.multiple_of(piece * depth, depth), depth)], part[...])


def coarse_kernel(offsets, with_total, *refs):
    inverse, parts, refs = refs[0], refs[1 : 1 + len(offsets)], refs[1 + len(offsets) :]
    total = refs[0][...] if with_total else None
    for part, offset in zip(parts, offsets):
        term = inverse_part(inverse, part, offset)
        total = term if total is None else total + term
    refs[-1][...] = total


def raise_level(coarse, rhs, scale, local, pmat):
    updated = rhs * (relax_down * scale) + matmul(pmat, coarse)
    applied = matmul(local, updated.astype(bf16))
    return updated + (relax_up * scale) * (rhs - applied)


def up_kernel(offset, depth, inverse, part, total, *refs):
    value = total[...] + inverse_part(inverse, part, offset)
    for step in range(depth):
        rhs, scale, local, pmat = refs[4 * step : 4 * step + 4]
        value = raise_level(value.astype(bf16), rhs[...], scale[...], local[...], pmat[...])
    refs[-1][...] = value.astype(bf16)


def lanes_of(place, width):
    start = 0
    for level_idx, flip, step in place:
        start = start + (bit_of(level_idx) ^ flip) * step
    return pl.ds(pl.multiple_of(start, width), width)


def raise_kernel(places, last, *refs):
    count = len(places)
    coarse, outs = refs[:count], refs[-count:]
    rhs, scale, local, pmat = refs[count : count + 4]
    for place, value, out in zip(places, coarse, outs):
        lanes = lanes_of(place, value.shape[1])
        held = rhs[0, :, lanes] if last else rhs[:, lanes]
        raised = raise_level(value[...], held, scale[...], local[...], pmat[...])
        out[...] = raised.astype(out.dtype)


def final_kernel(places, made, *refs):
    count = len(places)
    for place, value in zip(places[:made], refs[:made]):
        out = refs[-1]
        out[0, :, lanes_of(place, value.shape[1])] = value[...]
    rhs, scale, local, pmat, out = refs[count:]
    for place, value in zip(places[made:], refs[made:count]):
        lanes = lanes_of(place, value.shape[1])
        out[0, :, lanes] = raise_level(
            value[...], rhs[0, :, lanes], scale[...], local[...], pmat[...]
        )


def exchange(value, axis, bit):
    count = lax.axis_size(axis)
    return lax.ppermute(value, axis, [(i, i ^ bit) for i in range(count)])


def swap_ends(ends):
    count = lax.axis_size("narrow")
    size = ends.shape[0] // 2
    inner = exchange(ends, "narrow", 1)
    onward = [(i, i + 2) for i in range(0, count - 2, 2)]
    onward = onward + [(i, i - 2) for i in range(3, count, 2)]
    return inner, lax.ppermute(inner[size:], "narrow", onward)


def on_device(
    level_rhs,
    galerkin_cols,
    galerkin_blocks,
    restrict_cols,
    restrict_blocks,
    prolong_cols,
    prolong_blocks,
    coarse_inverse,
):
    levels = galerkin_cols.shape[0]
    count = galerkin_cols.shape[2]
    size = galerkin_blocks.shape[-1]
    rows, fields = level_rhs.shape[1:]
    splits = min(2, levels)
    widths = [fields >> min(level_idx, splits) for level_idx in range(levels + 1)]
    gcols, rcols, pcols = ((c, scalars()) for c in (galerkin_cols, restrict_cols, prolong_cols))
    operator_shapes = [
        array((rows, rows), bf16), array((rows, 2 * size), bf16),
        array((rows, 1), f32), array((rows, 2 * rows), bf16),
    ]

    def ends_shape(width):
        return array((2 * size, width), bf16)

    def of_level(value, level_idx):
        return value, level_block(value, level_idx)

    def flops(width, products=1):
        return 2 * products * rows * rows * width

    (ends,) = run(
        start_kernel, "start", [ends_shape(fields)],
        [in_hbm(level_rhs), in_hbm(galerkin_blocks)],
        scratch=[
            pltpu.VMEM((2, size, fields), f32), pltpu.VMEM((2, size, size), bf16),
            pltpu.SemaphoreType.DMA((4,)),
        ],
    )
    inner, outer = swap_ends(ends)
    rest, local, rim, scale, rmat = run(
        first_local_kernel, "first_local", [array((rows, fields), f32)] + operator_shapes,
        [level_rhs, inner, gcols, of_level(galerkin_blocks, 0), rcols, of_level(restrict_blocks, 0)],
        flops=flops(fields),
    )
    operators = [(scale, local)]
    right_sides = [level_rhs]
    for level_idx in range(levels):
        width = widths[level_idx + 1]
        outs = [array((rows, width), bf16)] * (2 if level_idx < splits else 1)
        outs = run(
            functools.partial(residual_kernel, level_idx), "residual", outs, [rest, rim, inner, outer]
        )
        kept = outs[-1]
        other = exchange(outs[0], "wide", 1 << level_idx)
        if level_idx + 1 < levels:
            part, local, rim, scale, next_rmat = run(
                functools.partial(own_part_kernel, level_idx), "own_part",
                [array((rows, width), f32)] + operator_shapes,
                [kept, rmat, gcols, of_level(galerkin_blocks, level_idx + 1),
                 rcols, of_level(restrict_blocks, level_idx + 1)],
                flops=flops(width),
            )
            operators.append((scale, local))
            rhs, smoothed, ends = run(
                functools.partial(join_kernel, level_idx), "join",
                [array((rows, width), f32), array((rows, width), bf16), ends_shape(width)],
                [part, rmat, other, scale],
                flops=flops(width),
            )
            right_sides.append(rhs)
            rmat = next_rmat
            inner, outer = swap_ends(ends)
            (rest,) = run(
                local_kernel, "local", [array((rows, width), f32)], [rhs, local, smoothed],
                flops=flops(width),
            )
        else:
            part, *pmats = run(
                functools.partial(last_part_kernel, level_idx, levels), "last_part",
                [array((rows, width), f32)] + operator_shapes[:1] * levels,
                [kept, rmat, pcols] + [of_level(prolong_blocks, idx) for idx in range(levels)],
                flops=flops(width),
            )
            (mine,) = run(
                functools.partial(last_join_kernel, level_idx), "last_join",
                [array((rows, width), bf16)], [part, rmat, other], flops=flops(width),
            )
    pieces = lax.axis_size("narrow")
    parts = {0: mine}
    order = sorted(range(1, pieces), key=lambda o: (bin(o).count("1"), -o))
    for offset in order:
        low = offset & -offset
        parts[offset] = exchange(parts[offset ^ low], "narrow", low)
    total_shape = [array((rows, width), f32)]
    (total,) = run(
        functools.partial(coarse_kernel, (0,), False), "coarse_own", total_shape,
        [coarse_inverse, mine], flops=flops(width),
    )
    middle = tuple(order[:-1])
    if middle:
        (total,) = run(
            functools.partial(coarse_kernel, middle, True), "coarse_middle", total_shape,
            [coarse_inverse] + [parts[o] for o in middle] + [total], flops=flops(width, len(middle)),
        )

    def raising(level_idx):
        return [right_sides[level_idx], *operators[level_idx], pmats[level_idx]]

    operands = []
    for level_idx in reversed(range(splits, levels)):
        operands += raising(level_idx)
    (coarse,) = run(
        functools.partial(up_kernel, order[-1], levels - splits), "up", [array((rows, width), bf16)],
        [coarse_inverse, parts[order[-1]], total] + operands,
        flops=flops(width, 1 + 2 * (levels - splits)),
    )
    chunks = [(coarse, ())]
    for level_idx in reversed(range(splits)):
        step = widths[level_idx + 1]
        own = [(value, place + ((level_idx, 0, step),)) for value, place in chunks]
        far = [
            (exchange(value, "wide", 1 << level_idx), place + ((level_idx, 1, step),))
            for value, place in chunks
        ]
        if level_idx > 0:
            raised = []
            for value, place in own + far:
                (result,) = run(
                    functools.partial(raise_kernel, (place,), False), "raise",
                    [array((rows, width), bf16)], [value] + raising(level_idx),
                    flops=flops(width, 2),
                )
                raised.append((result, place))
            chunks = raised
        else:
            places = tuple(place for _, place in own + far)
            early = run(
                functools.partial(raise_kernel, places[: len(own)], True), "raise_own",
                [array((rows, width), f32)] * len(own), [value for value, _ in own] + raising(0),
                flops=flops(width, 2 * len(own)),
            )
            (result,) = run(
                functools.partial(final_kernel, places, len(own)), "final",
                [array((1, rows, fields), f32)],
                list(early) + [value for value, _ in far] + raising(0),
                flops=flops(width, 2 * len(far)),
            )
    return result


def solution(mesh):
    in_specs = (
        P("wide", "narrow", None),
        P(None, "wide", "narrow", None),
        P(None, "wide", "narrow", None, None, None),
        P(None, "wide", "narrow", None),
        P(None, "wide", "narrow", None, None, None),
        P(None, "wide", "narrow", None),
        P(None, "wide", "narrow", None, None, None),
        P("narrow", None),
    )
    out_specs = P("wide", "narrow", None)
    return jax.shard_map(
        on_device, mesh=mesh, in_specs=in_specs, out_specs=out_specs, check_vma=False
    )
```

time: 53.4 us -> 56.3 us (1.054)
  waiting for transfers between devices: 15.1 us -> 17.6 us
  local copies, waits for them, and re-layouts: 2.79 us -> 1.32 us
  Pallas kernels: 9.12 us -> 10.5 us
    ppermute x6 -> x3, starting transfers between devices: 9.43 us -> 12.6 us  [swap_ends(): return (inner, lax.ppermute(inner[size:], 'narrow', onward))]
    ppermute x7 -> x12, starting transfers between devices: 16.4 us -> 13.7 us  [exchange(): return lax.ppermute(value, axis, [(i, i ^ bit) for i in range(count)])]
    ppermute x6 -> x3, waiting for transfers between devices: 0.02 us -> 2.62 us  [swap_ends(): return (inner, lax.ppermute(inner[size:], 'narrow', onward))]
    unnamed x22 -> x20, local copies, waits for them, and re-layouts: 2.79 us -> 1.31 us
    pallas_call x19 -> x20, Pallas kernels: 9.12 us -> 10.5 us  [run(): pl.pallas_call(body, grid=(1,) if windows else (), out_shape=outs, in_spe...]
    ppermute x7 -> x12, waiting for transfers between devices: 15.1 us -> 15 us  [exchange(): return lax.ppermute(value, axis, [(i, i ^ bit) for i in range(count)])]
  transfers between devices with their start and end apart: 13 -> 15, of which waited for: 5 -> 12; matrix products, arithmetic and copies ran while one was open for 0% -> 0% of each run, Pallas kernels for 11% -> 11%
where the time goes in v2:
time: 56.3 us; the launch traced here: 56 us
  starting transfers between devices  26.3 us (47%)
  waiting for transfers between devices  17.6 us (31%)
  Pallas kernels  10.5 us (19%)
  local copies, waits for them, and re-layouts  1.32 us (2%)
    ppermute x12, waiting for transfers between devices, exchange(): return lax.ppermute(value, axis, [(i, i ^ bit) for i in range(count)])  15 us
    ppermute x12, starting transfers between devices, exchange(): return lax.ppermute(value, axis, [(i, i ^ bit) for i in range(count)])  13.7 us
    ppermute x3, starting transfers between devices, swap_ends(): return (inner, lax.ppermute(inner[size:], 'narrow', onward))  12.6 us
    pallas_call x20, Pallas kernels, run(): pl.pallas_call(body, grid=(1,) if windows else (), out_shape=outs, in_spe...  10.5 us
    ppermute x3, waiting for transfers between devices, swap_ends(): return (inner, lax.ppermute(inner[size:], 'narrow', onward))  2.62 us
    unnamed x20, local copies, waits for them, and re-layouts  1.31 us
  transfers between devices with their start and end apart: 15, of which 12 were waited for; matrix products, arithmetic and copies ran while one was open for 0% of the time, Pallas kernels for 11%

profile of v2, /device:TPU:0, one launch (start us, length us, event | category | flops | bytes accessed | tf_op | source)
XLA Modules:
  0.0 56.0 jit_solution(14352363777132751545)
XLA Ops:
  0.0 1.2 %start.1 = bf16[128,512]{1,0:T(8,128)(2,1)S(1)} custom-call(f32[1,256,512]{2,1,0:T(8,128)} %refs_4_.1, bf16[3,1,4,5,64,64]{5,4,3,2,1,0:T(8,128)(2,1)} %blocks.7), custom_call_target="tpu_custom_call" | custom-call | bytes 1015808 | tf_op jit(solution)/shard_map/start/pallas_call | solution.py:47
  1.3 0.5 collective-permute-start
  1.8 1.0 %collective-permute-done._.inner = bf16[128,512]{1,0:T(8,128)(2,1)S(1)} collective-permute-done((bf16[128,512]{1,0:T(8,128)(2,1)S(1)}, bf16[128,512]{1,0:T(8,128)(2,1)S(1)}, u32[]{:S(2)}, u32[]{:S(2)}) %collective-permute-start) | collective-permute-done | bytes 131104 | tf_op jit(solution)/shard_map/ppermute | solution.py:266
  2.8 4.8 %collective-permute-start.1 = (bf16[64,512]{1,0:T(8,128)(2,1)S(1)}, bf16[64,512]{1,0:T(8,128)(2,1)S(1)}, u32[]{:S(2)}, u32[]{:S(2)}) collective-permute-start(bf16[64,512]{1,0:T(8,128)(2,1)S(1)} %slice.12), channel_id=1, source_target_pairs={{0,2},{3,1},{4,6},{7,5},{8,10},{11,9},{12,14},{15,13},{16,18},{19,... | collective-permute-start | bytes 196616 | tf_op jit(solution)/shard_map/ppermute | solution.py:275
  7.6 0.1 copy.9.rcols
  7.7 1.1 %copy-done.2 = bf16[3,1,4,3,64,64]{5,4,3,2,1,0:T(8,128)(2,1)S(1)} copy-done((bf16[3,1,4,3,64,64]{5,4,3,2,1,0:T(8,128)(2,1)S(1)}, bf16[3,1,4,3,64,64]{5,4,3,2,1,0:T(8,128)(2,1)}, u32[]{:S(2)}) %copy-start.2) | copy-done | bytes 294936
  8.7 1.3 %first_local.1 = (f32[256,512]{1,0:T(8,128)S(1)}, bf16[256,256]{1,0:T(8,128)(2,1)S(1)}, bf16[256,128]{1,0:T(8,128)(2,1)S(1)}, f32[256,1]{1,0:T(8,128)S(1)}, bf16[256,512]{1,0:T(8,128)(2,1)S(1)}) custom-call(f32[1,256,512]{2,1,0:T(8,128)S(1)} %copy-done.1, bf16[128,512]{1,0:T(8,128)(2,1)S(1)} %collective-permute-done._.inner, s32[3,1,4,5]{3,2,1,0:T(4,128)S(1)} %copy-done.6, ...), custom_call_target="tpu_custom_call" | custom-call | flops 67108864 | bytes 1442176 | tf_op jit(solution)/shard_map/first_local/pallas_call | solution.py:47
  10.0 0.2 residual.3
  10.3 1.6 %collective-permute-start.2 = (bf16[256,256]{1,0:T(8,128)(2,1)S(1)}, bf16[256,256]{1,0:T(8,128)(2,1)S(1)}, u32[]{:S(2)}, u32[]{:S(2)}) collective-permute-start(bf16[256,256]{1,0:T(8,128)(2,1)S(1)} %get-tuple-element.41), channel_id=1, source_target_pairs={{0,4},{4,0},{8,12},{12,8},{16,20},{20,16},{24,28},{28,24},{1,5},{5... | collective-permute-start | bytes 393224 | tf_op jit(solution)/shard_map/ppermute | solution.py:266
  11.9 1.1 %own_part.2 = (f32[256,256]{1,0:T(8,128)S(1)}, bf16[256,256]{1,0:T(8,128)(2,1)S(1)}, bf16[256,128]{1,0:T(8,128)(2,1)S(1)}, f32[256,1]{1,0:T(8,128)S(1)}, bf16[256,512]{1,0:T(8,128)(2,1)S(1)}) custom-call(bf16[256,256]{1,0:T(8,128)(2,1)S(1)} %get-tuple-element.38.residual, bf16[256,512]{1,0:T(8,128)(2,1)S(1)} %get-tuple-element.39.rmat, ...), custom_call_target="tpu_custom_call" | custom-call | flops 33554432 | bytes 1180032 | tf_op jit(solution)/shard_map/own_part/pallas_call | solution.py:47
  13.0 2.3 %collective-permute-done.2.other = bf16[256,256]{1,0:T(8,128)(2,1)S(1)} collective-permute-done((bf16[256,256]{1,0:T(8,128)(2,1)S(1)}, bf16[256,256]{1,0:T(8,128)(2,1)S(1)}, u32[]{:S(2)}, u32[]{:S(2)}) %collective-permute-start.2) | collective-permute-done | bytes 131104 | tf_op jit(solution)/shard_map/ppermute | solution.py:266
  15.3 0.2 join.2
  15.5 0.1 collective-permute-start.3
  15.6 1.2 %collective-permute-done.3.inner = bf16[128,256]{1,0:T(8,128)(2,1)S(1)} collective-permute-done((bf16[128,256]{1,0:T(8,128)(2,1)S(1)}, bf16[128,256]{1,0:T(8,128)(2,1)S(1)}, u32[]{:S(2)}, u32[]{:S(2)}) %collective-permute-start.3) | collective-permute-done | bytes 65568 | tf_op jit(solution)/shard_map/ppermute | solution.py:266
  16.8 3.6 %collective-permute-start.4 = (bf16[64,256]{1,0:T(8,128)(2,1)S(1)}, bf16[64,256]{1,0:T(8,128)(2,1)S(1)}, u32[]{:S(2)}, u32[]{:S(2)}) collective-permute-start(bf16[64,256]{1,0:T(8,128)(2,1)S(1)} %slice.13), channel_id=1, source_target_pairs={{0,2},{3,1},{4,6},{7,5},{8,10},{11,9},{12,14},{15,13},{16,18},{19,... | collective-permute-start | bytes 98312 | tf_op jit(solution)/shard_map/ppermute | solution.py:275
  20.5 0.2 local.2.rest
  20.7 1.4 %collective-permute-done.4.outer = bf16[64,256]{1,0:T(8,128)(2,1)S(1)} collective-permute-done((bf16[64,256]{1,0:T(8,128)(2,1)S(1)}, bf16[64,256]{1,0:T(8,128)(2,1)S(1)}, u32[]{:S(2)}, u32[]{:S(2)}) %collective-permute-start.4) | collective-permute-done | bytes 32800 | tf_op jit(solution)/shard_map/ppermute | solution.py:275
  22.1 0.2 residual.4
  22.2 1.6 %collective-permute-start.5 = (bf16[256,128]{1,0:T(8,128)(2,1)S(1)}, bf16[256,128]{1,0:T(8,128)(2,1)S(1)}, u32[]{:S(2)}, u32[]{:S(2)}) collective-permute-start(bf16[256,128]{1,0:T(8,128)(2,1)S(1)} %get-tuple-element.51), channel_id=1, source_target_pairs={{0,8},{4,12},{8,0},{12,4},{16,24},{20,28},{24,16},{28,20},{1,9},{5... | collective-permute-start | bytes 196616 | tf_op jit(solution)/shard_map/ppermute | solution.py:266
  23.9 1.1 %own_part.3 = (f32[256,128]{1,0:T(8,128)S(1)}, bf16[256,256]{1,0:T(8,128)(2,1)S(1)}, bf16[256,128]{1,0:T(8,128)(2,1)S(1)}, f32[256,1]{1,0:T(8,128)S(1)}, bf16[256,512]{1,0:T(8,128)(2,1)S(1)}) custom-call(bf16[256,128]{1,0:T(8,128)(2,1)S(1)} %get-tuple-element.48.residual, bf16[256,512]{1,0:T(8,128)(2,1)S(1)} %get-tuple-element.49.rmat, ...), custom_call_target="tpu_custom_call" | custom-call | flops 16777216 | bytes 1114496 | tf_op jit(solution)/shard_map/own_part/pallas_call | solution.py:47
  25.0 1.6 %collective-permute-done.5.other = bf16[256,128]{1,0:T(8,128)(2,1)S(1)} collective-permute-done((bf16[256,128]{1,0:T(8,128)(2,1)S(1)}, bf16[256,128]{1,0:T(8,128)(2,1)S(1)}, u32[]{:S(2)}, u32[]{:S(2)}) %collective-permute-start.5) | collective-permute-done | bytes 65568 | tf_op jit(solution)/shard_map/ppermute | solution.py:266
  26.6 0.2 join.3
  26.8 0.1 collective-permute-start.6
  26.8 1.2 %collective-permute-done.6.inner = bf16[128,128]{1,0:T(8,128)(2,1)S(1)} collective-permute-done((bf16[128,128]{1,0:T(8,128)(2,1)S(1)}, bf16[128,128]{1,0:T(8,128)(2,1)S(1)}, u32[]{:S(2)}, u32[]{:S(2)}) %collective-permute-start.6) | collective-permute-done | bytes 32800 | tf_op jit(solution)/shard_map/ppermute | solution.py:266
  28.0 4.2 %collective-permute-start.7 = (bf16[64,128]{1,0:T(8,128)(2,1)S(1)}, bf16[64,128]{1,0:T(8,128)(2,1)S(1)}, u32[]{:S(2)}, u32[]{:S(2)}) collective-permute-start(bf16[64,128]{1,0:T(8,128)(2,1)S(1)} %slice.14), channel_id=1, source_target_pairs={{0,2},{3,1},{4,6},{7,5},{8,10},{11,9},{12,14},{15,13},{16,18},{19,... | collective-permute-start | bytes 49160 | tf_op jit(solution)/shard_map/ppermute | solution.py:275
  32.3 0.2 local.3.rest
  32.4 1.2 %collective-permute-done.7.outer = bf16[64,128]{1,0:T(8,128)(2,1)S(1)} collective-permute-done((bf16[64,128]{1,0:T(8,128)(2,1)S(1)}, bf16[64,128]{1,0:T(8,128)(2,1)S(1)}, u32[]{:S(2)}, u32[]{:S(2)}) %collective-permute-start.7) | collective-permute-done | bytes 16416 | tf_op jit(solution)/shard_map/ppermute | solution.py:275
  33.7 0.1 residual.5
  33.8 2.7 %collective-permute-start.8 = (bf16[256,128]{1,0:T(8,128)(2,1)S(1)}, bf16[256,128]{1,0:T(8,128)(2,1)S(1)}, u32[]{:S(2)}, u32[]{:S(2)}) collective-permute-start(bf16[256,128]{1,0:T(8,128)(2,1)S(1)} %residual.5), channel_id=1, source_target_pairs={{0,16},{4,20},{8,24},{12,28},{16,0},{20,4},{24,8},{28,12},{1,17},{... | collective-permute-start | bytes 196616 | tf_op jit(solution)/shard_map/ppermute | solution.py:266
  36.5 0.1 copy.12.pcols
  36.6 0.8 %last_part.1 = (f32[256,128]{1,0:T(8,128)S(1)}, bf16[256,256]{1,0:T(8,128)(2,1)S(1)}, bf16[256,256]{1,0:T(8,128)(2,1)S(1)}, bf16[256,256]{1,0:T(8,128)(2,1)S(1)}) custom-call(bf16[256,128]{1,0:T(8,128)(2,1)S(1)} %residual.5, bf16[256,512]{1,0:T(8,128)(2,1)S(1)} %get-tuple-element.58.rmat, s32[3,1,4,2]{3,2,1,0:T(4,128)S(1)} %copy.12.pcols, ...), custom_call_target="tpu_custom_call" | custom-call | flops 16777216 | bytes 917600 | tf_op jit(solution)/shard_map/last_part/pallas_call | solution.py:47
  37.5 1.6 %collective-permute-done.8.other = bf16[256,128]{1,0:T(8,128)(2,1)S(1)} collective-permute-done((bf16[256,128]{1,0:T(8,128)(2,1)S(1)}, bf16[256,128]{1,0:T(8,128)(2,1)S(1)}, u32[]{:S(2)}, u32[]{:S(2)}) %collective-permute-start.8) | collective-permute-done | bytes 65568 | tf_op jit(solution)/shard_map/ppermute | solution.py:266
  39.1 0.2 last_join.1.refs_1_
  39.2 2.4 %collective-permute-start.9 = (bf16[256,128]{1,0:T(8,128)(2,1)S(1)}, bf16[256,128]{1,0:T(8,128)(2,1)S(1)}, u32[]{:S(2)}, u32[]{:S(2)}) collective-permute-start(bf16[256,128]{1,0:T(8,128)(2,1)S(1)} %last_join.1.refs_1_), channel_id=1, source_target_pairs={{0,2},{1,3},{2,0},{3,1},{4,6},{5,7},{6,4},{7,5},{8,10},{9,11},{10,... | collective-permute-start | bytes 196616 | tf_op jit(solution)/shard_map/ppermute | solution.py:266
  41.6 2.2 %collective-permute-done.9.refs_1_ = bf16[256,128]{1,0:T(8,128)(2,1)S(1)} collective-permute-done((bf16[256,128]{1,0:T(8,128)(2,1)S(1)}, bf16[256,128]{1,0:T(8,128)(2,1)S(1)}, u32[]{:S(2)}, u32[]{:S(2)}) %collective-permute-start.9) | collective-permute-done | bytes 65568 | tf_op jit(solution)/shard_map/ppermute | solution.py:266
  43.8 0.2 coarse_own.1.refs_3_
  44.0 0.2 coarse_middle.1.total
  44.3 0.8 %collective-permute-done.10.part = bf16[256,128]{1,0:T(8,128)(2,1)S(1)} collective-permute-done((bf16[256,128]{1,0:T(8,128)(2,1)S(1)}, bf16[256,128]{1,0:T(8,128)(2,1)S(1)}, u32[]{:S(2)}, u32[]{:S(2)}) %collective-permute-start.10) | collective-permute-done | bytes 65568 | tf_op jit(solution)/shard_map/ppermute | solution.py:266
  45.1 0.5 up.1.refs_0_
  45.6 1.6 %collective-permute-start.12 = (bf16[256,128]{1,0:T(8,128)(2,1)S(1)}, bf16[256,128]{1,0:T(8,128)(2,1)S(1)}, u32[]{:S(2)}, u32[]{:S(2)}) collective-permute-start(bf16[256,128]{1,0:T(8,128)(2,1)S(1)} %up.1.refs_0_), channel_id=1, source_target_pairs={{0,8},{4,12},{8,0},{12,4},{16,24},{20,28},{24,16},{28,20},{1,9},{5... | collective-permute-start | bytes 196616 | tf_op jit(solution)/shard_map/ppermute | solution.py:266
  47.3 0.4 raise.2.refs_0_
  47.7 1.6 %collective-permute-start.13 = (bf16[256,128]{1,0:T(8,128)(2,1)S(1)}, bf16[256,128]{1,0:T(8,128)(2,1)S(1)}, u32[]{:S(2)}, u32[]{:S(2)}) collective-permute-start(bf16[256,128]{1,0:T(8,128)(2,1)S(1)} %raise.2.refs_0_), channel_id=1, source_target_pairs={{0,4},{4,0},{8,12},{12,8},{16,20},{20,16},{24,28},{28,24},{1,5},{5... | collective-permute-start | bytes 196616 | tf_op jit(solution)/shard_map/ppermute | solution.py:266
  49.3 0.7 %collective-permute-done.12.refs_0_ = bf16[256,128]{1,0:T(8,128)(2,1)S(1)} collective-permute-done((bf16[256,128]{1,0:T(8,128)(2,1)S(1)}, bf16[256,128]{1,0:T(8,128)(2,1)S(1)}, u32[]{:S(2)}, u32[]{:S(2)}) %collective-permute-start.12) | collective-permute-done | bytes 65568 | tf_op jit(solution)/shard_map/ppermute | solution.py:266
  50.0 0.4 raise.3.refs_1_
  50.4 1.6 %collective-permute-start.14 = (bf16[256,128]{1,0:T(8,128)(2,1)S(1)}, bf16[256,128]{1,0:T(8,128)(2,1)S(1)}, u32[]{:S(2)}, u32[]{:S(2)}) collective-permute-start(bf16[256,128]{1,0:T(8,128)(2,1)S(1)} %raise.3.refs_1_), channel_id=1, source_target_pairs={{0,4},{4,0},{8,12},{12,8},{16,20},{20,16},{24,28},{28,24},{1,5},{5... | collective-permute-start | bytes 196616 | tf_op jit(solution)/shard_map/ppermute | solution.py:266
  52.0 0.5 raise_own.1
  52.4 2.3 %collective-permute-done.14.refs_3_ = bf16[256,128]{1,0:T(8,128)(2,1)S(1)} collective-permute-done((bf16[256,128]{1,0:T(8,128)(2,1)S(1)}, bf16[256,128]{1,0:T(8,128)(2,1)S(1)}, u32[]{:S(2)}, u32[]{:S(2)}) %collective-permute-start.14) | collective-permute-done | bytes 65568 | tf_op jit(solution)/shard_map/ppermute | solution.py:266
  54.7 1.3 %final.1 = f32[1,256,512]{2,1,0:T(8,128)} custom-call(f32[256,128]{1,0:T(8,128)S(1)} %get-tuple-element.65.refs_0_, f32[256,128]{1,0:T(8,128)S(1)} %get-tuple-element.66.refs_1_, bf16[256,128]{1,0:T(8,128)(2,1)S(1)} %collective-permute-done.13.refs_2_, bf16[256,128]{1,0:T(8,128)(2,1)S(1)} %collective-permute-done.14.refs_3_, f32[1,256,512]{2,1,0:T(8,128)S(1)} %copy-done.1, ...), custom_call_target="tpu_custom_call" | custom-call | flops 67108864 | bytes 1180672 | tf_op jit(solution)/shard_map/final/pallas_call | solution.py:47
  (25 shorter events, 0.1 us)
Async XLA Ops:
  0.0 7.7 %copy-start = (bf16[3,1,4,5,64,64]{5,4,3,2,1,0:T(8,128)(2,1)S(1)}, bf16[3,1,4,5,64,64]{5,4,3,2,1,0:T(8,128)(2,1)}, u32[]{:S(2)}) copy-start(bf16[3,1,4,5,64,64]{5,4,3,2,1,0:T(8,128)(2,1)} %blocks.7) | copy-start | bytes 1474564
  0.0 7.7 %copy-start.1 = (f32[1,256,512]{2,1,0:T(8,128)S(1)}, f32[1,256,512]{2,1,0:T(8,128)}, u32[]{:S(2)}) copy-start(f32[1,256,512]{2,1,0:T(8,128)} %refs_4_.1) | copy-start | bytes 1572868
  1.3 6.3 %copy-start.7 = (s32[3,1,4,3]{2,1,3,0:T(1,128)S(1)}, s32[3,1,4,3]{2,1,3,0:T(1,128)}, u32[]{:S(2)}) copy-start(s32[3,1,4,3]{2,1,3,0:T(1,128)} %param.11) | copy-start | bytes 436
  1.3 1.5 %collective-permute-start = (bf16[128,512]{1,0:T(8,128)(2,1)S(1)}, bf16[128,512]{1,0:T(8,128)(2,1)S(1)}, u32[]{:S(2)}, u32[]{:S(2)}) collective-permute-start(bf16[128,512]{1,0:T(8,128)(2,1)S(1)} %start.1), channel_id=1, source_target_pairs={{0,1},{1,0},{2,3},{3,2},{4,5},{5,4},{6,7},{7,6},{8,9},{9,8},{10,11... | collective-permute-start | bytes 393224 | tf_op jit(solution)/shard_map/ppermute | solution.py:266
  2.8 4.9 %copy-start.6 = (s32[3,1,4,5]{3,2,1,0:T(4,128)S(1)}, s32[3,1,4,5]{3,2,1,0:T(4,128)}, u32[]{:S(2)}) copy-start(s32[3,1,4,5]{3,2,1,0:T(4,128)} %cols.5) | copy-start | bytes 724
  2.8 7.2 %collective-permute-start.1 = (bf16[64,512]{1,0:T(8,128)(2,1)S(1)}, bf16[64,512]{1,0:T(8,128)(2,1)S(1)}, u32[]{:S(2)}, u32[]{:S(2)}) collective-permute-start(bf16[64,512]{1,0:T(8,128)(2,1)S(1)} %slice.12), channel_id=1, source_target_pairs={{0,2},{3,1},{4,6},{7,5},{8,10},{11,9},{12,14},{15,13},{16,18},{19,... | collective-permute-start | bytes 196616 | tf_op jit(solution)/shard_map/ppermute | solution.py:275
  7.7 1.1 %copy-start.2 = (bf16[3,1,4,3,64,64]{5,4,3,2,1,0:T(8,128)(2,1)S(1)}, bf16[3,1,4,3,64,64]{5,4,3,2,1,0:T(8,128)(2,1)}, u32[]{:S(2)}) copy-start(bf16[3,1,4,3,64,64]{5,4,3,2,1,0:T(8,128)(2,1)} %rblocks.5) | copy-start | bytes 884740
  10.0 1.8 %copy-start.3 = (bf16[3,1,4,3,64,64]{5,4,3,2,1,0:T(8,128)(2,1)S(1)}, bf16[3,1,4,3,64,64]{5,4,3,2,1,0:T(8,128)(2,1)}, u32[]{:S(2)}) copy-start(bf16[3,1,4,3,64,64]{5,4,3,2,1,0:T(8,128)(2,1)} %rblocks.5) | copy-start | bytes 884740
  10.3 5.0 %collective-permute-start.2 = (bf16[256,256]{1,0:T(8,128)(2,1)S(1)}, bf16[256,256]{1,0:T(8,128)(2,1)S(1)}, u32[]{:S(2)}, u32[]{:S(2)}) collective-permute-start(bf16[256,256]{1,0:T(8,128)(2,1)S(1)} %get-tuple-element.41), channel_id=1, source_target_pairs={{0,4},{4,0},{8,12},{12,8},{16,20},{20,16},{24,28},{28,24},{1,5},{5... | collective-permute-start | bytes 393224 | tf_op jit(solution)/shard_map/ppermute | solution.py:266
  15.5 1.3 %collective-permute-start.3 = (bf16[128,256]{1,0:T(8,128)(2,1)S(1)}, bf16[128,256]{1,0:T(8,128)(2,1)S(1)}, u32[]{:S(2)}, u32[]{:S(2)}) collective-permute-start(bf16[128,256]{1,0:T(8,128)(2,1)S(1)} %get-tuple-element.47), channel_id=1, source_target_pairs={{0,1},{1,0},{2,3},{3,2},{4,5},{5,4},{6,7},{7,6},{8,9},{9,8},{10,11... | collective-permute-start | bytes 196616 | tf_op jit(solution)/shard_map/ppermute | solution.py:266
  16.8 5.2 %collective-permute-start.4 = (bf16[64,256]{1,0:T(8,128)(2,1)S(1)}, bf16[64,256]{1,0:T(8,128)(2,1)S(1)}, u32[]{:S(2)}, u32[]{:S(2)}) collective-permute-start(bf16[64,256]{1,0:T(8,128)(2,1)S(1)} %slice.13), channel_id=1, source_target_pairs={{0,2},{3,1},{4,6},{7,5},{8,10},{11,9},{12,14},{15,13},{16,18},{19,... | collective-permute-start | bytes 98312 | tf_op jit(solution)/shard_map/ppermute | solution.py:275
  22.2 4.3 %collective-permute-start.5 = (bf16[256,128]{1,0:T(8,128)(2,1)S(1)}, bf16[256,128]{1,0:T(8,128)(2,1)S(1)}, u32[]{:S(2)}, u32[]{:S(2)}) collective-permute-start(bf16[256,128]{1,0:T(8,128)(2,1)S(1)} %get-tuple-element.51), channel_id=1, source_target_pairs={{0,8},{4,12},{8,0},{12,4},{16,24},{20,28},{24,16},{28,20},{1,9},{5... | collective-permute-start | bytes 196616 | tf_op jit(solution)/shard_map/ppermute | solution.py:266
  26.8 1.3 %collective-permute-start.6 = (bf16[128,128]{1,0:T(8,128)(2,1)S(1)}, bf16[128,128]{1,0:T(8,128)(2,1)S(1)}, u32[]{:S(2)}, u32[]{:S(2)}) collective-permute-start(bf16[128,128]{1,0:T(8,128)(2,1)S(1)} %get-tuple-element.57), channel_id=1, source_target_pairs={{0,1},{1,0},{2,3},{3,2},{4,5},{5,4},{6,7},{7,6},{8,9},{9,8},{10,11... | collective-permute-start | bytes 98312 | tf_op jit(solution)/shard_map/ppermute | solution.py:266
  28.0 5.6 %collective-permute-start.7 = (bf16[64,128]{1,0:T(8,128)(2,1)S(1)}, bf16[64,128]{1,0:T(8,128)(2,1)S(1)}, u32[]{:S(2)}, u32[]{:S(2)}) collective-permute-start(bf16[64,128]{1,0:T(8,128)(2,1)S(1)} %slice.14), channel_id=1, source_target_pairs={{0,2},{3,1},{4,6},{7,5},{8,10},{11,9},{12,14},{15,13},{16,18},{19,... | collective-permute-start | bytes 49160 | tf_op jit(solution)/shard_map/ppermute | solution.py:275
  32.2 4.4 %copy-start.5 = (bf16[3,1,4,2,64,64]{5,4,3,2,1,0:T(8,128)(2,1)S(1)}, bf16[3,1,4,2,64,64]{5,4,3,2,1,0:T(8,128)(2,1)}, u32[]{:S(2)}) copy-start(bf16[3,1,4,2,64,64]{5,4,3,2,1,0:T(8,128)(2,1)} %refs_2_.2) | copy-start | bytes 589828
  33.7 2.8 %copy-start.8 = (s32[3,1,4,2]{2,3,1,0:T(2,128)S(1)}, s32[3,1,4,2]{2,3,1,0:T(2,128)}, u32[]{:S(2)}) copy-start(s32[3,1,4,2]{2,3,1,0:T(2,128)} %param.13) | copy-start | bytes 292
  33.8 5.2 %collective-permute-start.8 = (bf16[256,128]{1,0:T(8,128)(2,1)S(1)}, bf16[256,128]{1,0:T(8,128)(2,1)S(1)}, u32[]{:S(2)}, u32[]{:S(2)}) collective-permute-start(bf16[256,128]{1,0:T(8,128)(2,1)S(1)} %residual.5), channel_id=1, source_target_pairs={{0,16},{4,20},{8,24},{12,28},{16,0},{20,4},{24,8},{28,12},{1,17},{... | collective-permute-start | bytes 196616 | tf_op jit(solution)/shard_map/ppermute | solution.py:266
  37.4 6.4 %copy-start.4 = (bf16[256,1024]{1,0:T(8,128)(2,1)S(1)}, bf16[256,1024]{1,0:T(8,128)(2,1)}, u32[]{:S(2)}) copy-start(bf16[256,1024]{1,0:T(8,128)(2,1)} %inverse.1) | copy-start | bytes 1572868
  39.2 4.6 %collective-permute-start.9 = (bf16[256,128]{1,0:T(8,128)(2,1)S(1)}, bf16[256,128]{1,0:T(8,128)(2,1)S(1)}, u32[]{:S(2)}, u32[]{:S(2)}) collective-permute-start(bf16[256,128]{1,0:T(8,128)(2,1)S(1)} %last_join.1.refs_1_), channel_id=1, source_target_pairs={{0,2},{1,3},{2,0},{3,1},{4,6},{5,7},{6,4},{7,5},{8,10},{9,11},{10,... | collective-permute-start | bytes 196616 | tf_op jit(solution)/shard_map/ppermute | solution.py:266
  41.6 2.4 %collective-permute-start.11 = (bf16[256,128]{1,0:T(8,128)(2,1)S(1)}, bf16[256,128]{1,0:T(8,128)(2,1)S(1)}, u32[]{:S(2)}, u32[]{:S(2)}) collective-permute-start(bf16[256,128]{1,0:T(8,128)(2,1)S(1)} %last_join.1.refs_1_), channel_id=1, source_target_pairs={{0,1},{1,0},{2,3},{3,2},{4,5},{5,4},{6,7},{7,6},{8,9},{9,8},{10,11... | collective-permute-start | bytes 196616 | tf_op jit(solution)/shard_map/ppermute | solution.py:266
  43.8 1.3 %collective-permute-start.10 = (bf16[256,128]{1,0:T(8,128)(2,1)S(1)}, bf16[256,128]{1,0:T(8,128)(2,1)S(1)}, u32[]{:S(2)}, u32[]{:S(2)}) collective-permute-start(bf16[256,128]{1,0:T(8,128)(2,1)S(1)} %collective-permute-done.9.refs_1_), channel_id=1, source_target_pairs={{0,1},{1,0},{2,3},{3,2},{4,5},{5,4},{6,7},{7,6},{8,9},{9,8},{10,11... | collective-permute-start | bytes 196616 | tf_op jit(solution)/shard_map/ppermute | solution.py:266
  45.6 4.3 %collective-permute-start.12 = (bf16[256,128]{1,0:T(8,128)(2,1)S(1)}, bf16[256,128]{1,0:T(8,128)(2,1)S(1)}, u32[]{:S(2)}, u32[]{:S(2)}) collective-permute-start(bf16[256,128]{1,0:T(8,128)(2,1)S(1)} %up.1.refs_0_), channel_id=1, source_target_pairs={{0,8},{4,12},{8,0},{12,4},{16,24},{20,28},{24,16},{28,20},{1,9},{5... | collective-permute-start | bytes 196616 | tf_op jit(solution)/shard_map/ppermute | solution.py:266
  47.7 4.7 %collective-permute-start.13 = (bf16[256,128]{1,0:T(8,128)(2,1)S(1)}, bf16[256,128]{1,0:T(8,128)(2,1)S(1)}, u32[]{:S(2)}, u32[]{:S(2)}) collective-permute-start(bf16[256,128]{1,0:T(8,128)(2,1)S(1)} %raise.2.refs_0_), channel_id=1, source_target_pairs={{0,4},{4,0},{8,12},{12,8},{16,20},{20,16},{24,28},{28,24},{1,5},{5... | collective-permute-start | bytes 196616 | tf_op jit(solution)/shard_map/ppermute | solution.py:266
  50.4 4.3 %collective-permute-start.14 = (bf16[256,128]{1,0:T(8,128)(2,1)S(1)}, bf16[256,128]{1,0:T(8,128)(2,1)S(1)}, u32[]{:S(2)}, u32[]{:S(2)}) collective-permute-start(bf16[256,128]{1,0:T(8,128)(2,1)S(1)} %raise.3.refs_1_), channel_id=1, source_target_pairs={{0,4},{4,0},{8,12},{12,8},{16,20},{20,16},{24,28},{28,24},{1,5},{5... | collective-permute-start | bytes 196616 | tf_op jit(solution)/shard_map/ppermute | solution.py:266

commit v3 on v2

--- a/solution.py
+++ b/solution.py
@@ -39,7 +39,7 @@
     return pltpu.with_memory_space_constraint(value, pltpu.HBM), pl.BlockSpec(memory_space=pltpu.HBM)
 
 
-def run(body, name, outs, operands, flops=0, scratch=()):
+def run(body, name, outs, operands, flops=0, scratch=(), out_space=pltpu.VMEM, aliases=None):
     arrays = [o[0] if isinstance(o, tuple) else o for o in operands]
     specs = [o[1] if isinstance(o, tuple) else whole() for o in operands]
     windows = any(isinstance(o, tuple) and o[1].block_shape is not None for o in operands)
@@ -49,7 +49,8 @@
         grid=(1,) if windows else (),
         out_shape=outs,
         in_specs=specs,
-        out_specs=[pl.BlockSpec(memory_space=pltpu.VMEM)] * len(outs),
+        out_specs=[pl.BlockSpec(memory_space=out_space)] * len(outs),
+        input_output_aliases=aliases or {},
         scratch_shapes=list(scratch),
         compiler_params=pltpu.CompilerParams(vmem_limit_bytes=grant),
         cost_estimate=pl.CostEstimate(flops=flops, bytes_accessed=moved, transcendentals=0),
@@ -76,16 +77,18 @@
     return lax.rem(lax.axis_index("narrow"), 2)
 
 
-def put_ends(first, last, ends_ref):
-    size = first.shape[0]
+def put_ends(first, last, inner_ref, outer_ref):
     even = parity_of() == 0
-    ends_ref[:size, :] = jnp.where(even, last, first)
-    ends_ref[size:, :] = jnp.where(even, first, last)
+    inner_ref[...] = jnp.where(even, last, first)
+    outer_ref[...] = jnp.where(even, first, last)
 
 
 def assemble_galerkin(level_idx, cols, blocks, local_ref, rim_ref, scale_ref):
     count, slots, size = blocks.shape[2], blocks.shape[3], blocks.shape[4]
     parity = parity_of()
+    piece = lax.axis_index("narrow")
+    last = lax.axis_size("narrow") - 1
+    inside = jnp.where((piece == 0) | (piece == last), 0.0, 1.0).astype(f32)
     for b in range(count):
         held = [blocks[0, 0, b, s].astype(f32) for s in range(slots)]
         ids = [cols[level_idx, 0, b, s] for s in range(1, slots)]
@@ -95,7 +98,7 @@
         local_ref[rows, :] = jnp.concatenate(line, axis=1).astype(bf16)
         rims = [
             placed(None, held[1:], ids, count + 1 - parity),
-            placed(None, held[1:], ids, count + parity),
+            placed(None, held[1:], ids, count + parity) * inside,
         ]
         rim_ref[rows, :] = jnp.concatenate(rims, axis=1).astype(bf16)
 
@@ -119,7 +122,7 @@
         out_ref[pl.ds(b * size, size), :] = jnp.concatenate(line, axis=1).astype(bf16)
 
 
-def start_kernel(rhs, blocks, ends_ref, rows, pivots, sems):
+def start_kernel(rhs, blocks, inner_ref, outer_ref, rows, pivots, sems):
     count, size = blocks.shape[2], blocks.shape[4]
     copies = []
     for slot, which in enumerate((0, count - 1)):
@@ -135,13 +138,18 @@
         (rows[slot] * (relax_down / diagonal_of(pivots[slot].astype(f32)))).astype(bf16)
         for slot in range(2)
     )
-    put_ends(first, last, ends_ref)
-
-
-def first_local_kernel(rhs, _, cols, blocks, rcols, rblocks, rest, local, rim, scale, rmat):
+    put_ends(first, last, inner_ref, outer_ref)
+
+
+def first_local_kernel(
+    rhs, _, cols, blocks, rcols, rsource, rest, local, rim, scale, rmat, rblocks, sem
+):
+    copy = pltpu.make_async_copy(rsource.at[pl.ds(0, 1)], rblocks, sem)
+    copy.start()
     assemble_galerkin(0, cols, blocks, local, rim, scale)
     smoothed = (rhs[0] * (relax_down * scale[...])).astype(bf16)
     rest[...] = rhs[0] - matmul(local[...], smoothed)
+    copy.wait()
     assemble_restrict(0, rcols, rblocks, rmat)
 
 
@@ -150,16 +158,15 @@
 
 
 def residual_kernel(level_idx, rest, rim, inner, outer, *refs):
-    size = outer.shape[0]
     if len(refs) == 1:
-        rims = jnp.concatenate([inner[:size, :], outer[...]], axis=0)
+        rims = jnp.concatenate([inner[...], outer[...]], axis=0)
         refs[0][...] = (rest[...] - matmul(rim[...], rims)).astype(bf16)
     else:
         half = refs[0].shape[1]
         bit = bit_of(level_idx)
         for ref, side in zip(refs, (1 - bit, bit)):
             lanes = pl.ds(pl.multiple_of(side * half, half), half)
-            rims = jnp.concatenate([inner[:size, lanes], outer[:, lanes]], axis=0)
+            rims = jnp.concatenate([inner[:, lanes], outer[:, lanes]], axis=0)
             ref[...] = (rest[:, lanes] - matmul(rim[...], rims)).astype(bf16)
 
 
@@ -183,13 +190,13 @@
         assemble_prolong(idx, pcols, blocks, out)
 
 
-def join_kernel(level_idx, part, rmat, other, scale, rhs, smoothed, ends_ref):
-    size = ends_ref.shape[0] // 2
+def join_kernel(level_idx, part, rmat, other, scale, rhs, smoothed, inner_ref, outer_ref):
+    size = inner_ref.shape[0]
     current = part[...] + matmul(side_of(rmat, level_idx, False), other[...])
     rhs[...] = current
     rounded = (current * (relax_down * scale[...])).astype(bf16)
     smoothed[...] = rounded
-    put_ends(rounded[:size], rounded[-size:], ends_ref)
+    put_ends(rounded[:size], rounded[-size:], inner_ref, outer_ref)
 
 
 def last_join_kernel(level_idx, part, rmat, other, rounded):
@@ -237,28 +244,25 @@
     return pl.ds(pl.multiple_of(start, width), width)
 
 
-def raise_kernel(places, last, *refs):
-    count = len(places)
-    coarse, outs = refs[:count], refs[-count:]
-    rhs, scale, local, pmat = refs[count : count + 4]
-    for place, value, out in zip(places, coarse, outs):
+def raise_kernel(place, coarse, rhs, scale, local, pmat, out):
+    lanes = lanes_of(place, coarse.shape[1])
+    raised = raise_level(coarse[...], rhs[:, lanes], scale[...], local[...], pmat[...])
+    out[...] = raised.astype(bf16)
+
+
+def last_raise_kernel(places, *refs):
+    coarse, refs = refs[: len(places)], refs[len(places) :]
+    rhs, scale, local, pmat = refs[:4]
+    out, sems = refs[-2 - len(places)], refs[-1]
+    copies = []
+    for slot, (place, value, made) in enumerate(zip(places, coarse, refs[-1 - len(places) : -1])):
         lanes = lanes_of(place, value.shape[1])
-        held = rhs[0, :, lanes] if last else rhs[:, lanes]
-        raised = raise_level(value[...], held, scale[...], local[...], pmat[...])
-        out[...] = raised.astype(out.dtype)
-
-
-def final_kernel(places, made, *refs):
-    count = len(places)
-    for place, value in zip(places[:made], refs[:made]):
-        out = refs[-1]
-        out[0, :, lanes_of(place, value.shape[1])] = value[...]
-    rhs, scale, local, pmat, out = refs[count:]
-    for place, value in zip(places[made:], refs[made:count]):
-        lanes = lanes_of(place, value.shape[1])
-        out[0, :, lanes] = raise_level(
-            value[...], rhs[0, :, lanes], scale[...], local[...], pmat[...]
-        )
+        made[...] = raise_level(value[...], rhs[0, :, lanes], scale[...], local[...], pmat[...])
+        copy = pltpu.make_async_copy(made, out.at[0, :, lanes], sems.at[slot])
+        copy.start()
+        copies.append(copy)
+    for copy in copies:
+        copy.wait()
 
 
 def exchange(value, axis, bit):
@@ -266,13 +270,10 @@
     return lax.ppermute(value, axis, [(i, i ^ bit) for i in range(count)])
 
 
-def swap_ends(ends):
+def swap_ends(inner, outer):
     count = lax.axis_size("narrow")
-    size = ends.shape[0] // 2
-    inner = exchange(ends, "narrow", 1)
-    onward = [(i, i + 2) for i in range(0, count - 2, 2)]
-    onward = onward + [(i, i - 2) for i in range(3, count, 2)]
-    return inner, lax.ppermute(inner[size:], "narrow", onward)
+    gaps = [(i, (i + 1 if i % 2 else i - 1) % count) for i in range(count)]
+    return exchange(inner, "narrow", 1), lax.ppermute(outer, "narrow", gaps)
 
 
 def on_device(
@@ -289,7 +290,7 @@
     count = galerkin_cols.shape[2]
     size = galerkin_blocks.shape[-1]
     rows, fields = level_rhs.shape[1:]
-    splits = min(2, levels)
+    splits = min(1, levels)
     widths = [fields >> min(level_idx, splits) for level_idx in range(levels + 1)]
     gcols, rcols, pcols = ((c, scalars()) for c in (galerkin_cols, restrict_cols, prolong_cols))
     operator_shapes = [
@@ -298,7 +299,7 @@
     ]
 
     def ends_shape(width):
-        return array((2 * size, width), bf16)
+        return array((size, width), bf16)
 
     def of_level(value, level_idx):
         return value, level_block(value, level_idx)
@@ -306,19 +307,20 @@
     def flops(width, products=1):
         return 2 * products * rows * rows * width
 
-    (ends,) = run(
-        start_kernel, "start", [ends_shape(fields)],
+    ends = run(
+        start_kernel, "start", [ends_shape(fields)] * 2,
         [in_hbm(level_rhs), in_hbm(galerkin_blocks)],
         scratch=[
             pltpu.VMEM((2, size, fields), f32), pltpu.VMEM((2, size, size), bf16),
             pltpu.SemaphoreType.DMA((4,)),
         ],
     )
-    inner, outer = swap_ends(ends)
+    inner, outer = swap_ends(*ends)
     rest, local, rim, scale, rmat = run(
         first_local_kernel, "first_local", [array((rows, fields), f32)] + operator_shapes,
-        [level_rhs, inner, gcols, of_level(galerkin_blocks, 0), rcols, of_level(restrict_blocks, 0)],
+        [level_rhs, ends[0], gcols, of_level(galerkin_blocks, 0), rcols, in_hbm(restrict_blocks)],
         flops=flops(fields),
+        scratch=[pltpu.VMEM((1,) + restrict_blocks.shape[1:], bf16), pltpu.SemaphoreType.DMA],
     )
     operators = [(scale, local)]
     right_sides = [level_rhs]
@@ -339,15 +341,15 @@
                 flops=flops(width),
             )
             operators.append((scale, local))
-            rhs, smoothed, ends = run(
+            rhs, smoothed, *ends = run(
                 functools.partial(join_kernel, level_idx), "join",
-                [array((rows, width), f32), array((rows, width), bf16), ends_shape(width)],
+                [array((rows, width), f32), array((rows, width), bf16)] + [ends_shape(width)] * 2,
                 [part, rmat, other, scale],
                 flops=flops(width),
             )
             right_sides.append(rhs)
             rmat = next_rmat
-            inner, outer = swap_ends(ends)
+            inner, outer = swap_ends(*ends)
             (rest,) = run(
                 local_kernel, "local", [array((rows, width), f32)], [rhs, local, smoothed],
                 flops=flops(width),
@@ -404,25 +406,28 @@
             raised = []
             for value, place in own + far:
                 (result,) = run(
-                    functools.partial(raise_kernel, (place,), False), "raise",
+                    functools.partial(raise_kernel, place), "raise",
                     [array((rows, width), bf16)], [value] + raising(level_idx),
                     flops=flops(width, 2),
                 )
                 raised.append((result, place))
             chunks = raised
         else:
-            places = tuple(place for _, place in own + far)
-            early = run(
-                functools.partial(raise_kernel, places[: len(own)], True), "raise_own",
-                [array((rows, width), f32)] * len(own), [value for value, _ in own] + raising(0),
-                flops=flops(width, 2 * len(own)),
-            )
-            (result,) = run(
-                functools.partial(final_kernel, places, len(own)), "final",
-                [array((1, rows, fields), f32)],
-                list(early) + [value for value, _ in far] + raising(0),
-                flops=flops(width, 2 * len(far)),
-            )
+            result = None
+            for group in (own, far):
+                operands = [value for value, _ in group] + raising(0)
+                aliases = {}
+                if result is not None:
+                    aliases[len(operands)] = 0
+                    operands.append(in_hbm(result))
+                (result,) = run(
+                    functools.partial(last_raise_kernel, tuple(place for _, place in group)),
+                    "last_raise", [array((1, rows, fields), f32)], operands,
+                    flops=flops(width, 2 * len(group)),
+                    scratch=[pltpu.VMEM((rows, width), f32)] * len(group)
+                    + [pltpu.SemaphoreType.DMA((len(group),))],
+                    out_space=pltpu.HBM, aliases=aliases,
+                )
     return result
 
 

time: 56.3 us -> 51 us (0.906)
  starting transfers between devices: 26.3 us -> 14.4 us
  waiting for transfers between devices: 17.6 us -> 23.7 us
  Pallas kernels: 10.5 us -> 11.6 us
    ppermute x3, starting transfers between devices: 12.6 us -> 5.07 us  [swap_ends(): return (exchange(inner, 'narrow', 1), lax.ppermute(outer, 'narrow', gaps))]
    ppermute x12 -> x10, waiting for transfers between devices: 15 us -> 19.7 us  [exchange(): return lax.ppermute(value, axis, [(i, i ^ bit) for i in range(count)])]
    ppermute x12 -> x10, starting transfers between devices: 13.7 us -> 9.29 us  [exchange(): return lax.ppermute(value, axis, [(i, i ^ bit) for i in range(count)])]
    ppermute x3, waiting for transfers between devices: 2.62 us -> 3.94 us  [swap_ends(): return (exchange(inner, 'narrow', 1), lax.ppermute(outer, 'narrow', gaps))]
    pallas_call x20 -> x18, Pallas kernels: 10.5 us -> 11.6 us  [run(): pl.pallas_call(body, grid=(1,) if windows else (), out_shape=outs, in_spe...]
    unnamed x20 -> x16, local copies, waits for them, and re-layouts: 1.31 us -> 0.93 us
  transfers between devices with their start and end apart: 15 -> 13, of which waited for: 12 -> 8; matrix products, arithmetic and copies ran while one was open for 0% -> 2% of each run, Pallas kernels for 11% -> 14%
where the time goes in v3:
time: 51 us; the launch traced here: 50.8 us
  waiting for transfers between devices  23.7 us (46%)
  starting transfers between devices  14.4 us (28%)
  Pallas kernels  11.6 us (23%)
  local copies, waits for them, and re-layouts  0.93 us (2%)
    ppermute x10, waiting for transfers between devices, exchange(): return lax.ppermute(value, axis, [(i, i ^ bit) for i in range(count)])  19.7 us
    pallas_call x18, Pallas kernels, run(): pl.pallas_call(body, grid=(1,) if windows else (), out_shape=outs, in_spe...  11.6 us
    ppermute x10, starting transfers between devices, exchange(): return lax.ppermute(value, axis, [(i, i ^ bit) for i in range(count)])  9.29 us
    ppermute x3, starting transfers between devices, swap_ends(): return (exchange(inner, 'narrow', 1), lax.ppermute(outer, 'narrow', gaps))  5.07 us
    ppermute x3, waiting for transfers between devices, swap_ends(): return (exchange(inner, 'narrow', 1), lax.ppermute(outer, 'narrow', gaps))  3.94 us
  transfers between devices with their start and end apart: 13, of which 8 were waited for; matrix products, arithmetic and copies ran while one was open for 2% of the time, Pallas kernels for 14%

profile of v3, /device:TPU:0, one launch (start us, length us, event | category | flops | bytes accessed | tf_op | source)
XLA Modules:
  0.0 50.8 jit_solution(875113205638761268)
XLA Ops:
  0.0 1.2 %start.1 = (bf16[64,512]{1,0:T(8,128)(2,1)S(1)}, bf16[64,512]{1,0:T(8,128)(2,1)S(1)}) custom-call(f32[1,256,512]{2,1,0:T(8,128)} %refs_1_.5, bf16[3,1,4,5,64,64]{5,4,3,2,1,0:T(8,128)(2,1)} %blocks.7), custom_call_target="tpu_custom_call" | custom-call | bytes 1015808 | tf_op jit(solution)/shard_map/start/pallas_call | solution.py:47
  1.3 0.0 copy-start.5
  1.3 0.5 %collective-permute-start = (bf16[64,512]{1,0:T(8,128)(2,1)S(1)}, bf16[64,512]{1,0:T(8,128)(2,1)S(1)}, u32[]{:S(2)}, u32[]{:S(2)}) collective-permute-start(bf16[64,512]{1,0:T(8,128)(2,1)S(1)} %get-tuple-element.36._), channel_id=1, source_target_pairs={{0,1},{1,0},{2,3},{3,2},{4,5},{5,4},{6,7},{7,6},{8,9},{9,8},{10,11... | collective-permute-start | bytes 196616 | tf_op jit(solution)/shard_map/ppermute | solution.py:270
  1.8 2.6 %collective-permute-start.1 = (bf16[64,512]{1,0:T(8,128)(2,1)S(1)}, bf16[64,512]{1,0:T(8,128)(2,1)S(1)}, u32[]{:S(2)}, u32[]{:S(2)}) collective-permute-start(bf16[64,512]{1,0:T(8,128)(2,1)S(1)} %get-tuple-element.39), channel_id=1, source_target_pairs={{0,3},{1,2},{2,1},{3,0},{4,7},{5,6},{6,5},{7,4},{8,11},{9,10},{10,... | collective-permute-start | bytes 196616 | tf_op jit(solution)/shard_map/ppermute | solution.py:276
  4.4 0.8 %copy.10.rcols = s32[3,1,4,3]{3,2,1,0:T(4,128)S(1)} copy(s32[3,1,4,3]{2,1,3,0:T(1,128)} %param.11) | data formatting | bytes 288 | tf_op args[3]
  5.2 2.1 %first_local.1 = (f32[256,512]{1,0:T(8,128)S(1)}, bf16[256,256]{1,0:T(8,128)(2,1)S(1)}, bf16[256,128]{1,0:T(8,128)(2,1)S(1)}, f32[256,1]{1,0:T(8,128)S(1)}, bf16[256,512]{1,0:T(8,128)(2,1)S(1)}) custom-call(f32[1,256,512]{2,1,0:T(8,128)S(1)} %copy-done.1, bf16[64,512]{1,0:T(8,128)(2,1)S(1)} %get-tuple-element.36._, s32[3,1,4,5]{3,2,1,0:T(4,128)S(1)} %copy-done.5, ...), custom_call_target="tpu_custom_call" | custom-call | flops 67108864 | bytes 1376640 | tf_op jit(solution)/shard_map/first_local/pallas_call | solution.py:47
  7.4 0.0 copy-start.2
  7.4 0.0 collective-permute-done.inner
  7.4 0.0 collective-permute-done.1.outer
  7.4 0.2 residual.3
  7.6 1.6 %collective-permute-start.2 = (bf16[256,256]{1,0:T(8,128)(2,1)S(1)}, bf16[256,256]{1,0:T(8,128)(2,1)S(1)}, u32[]{:S(2)}, u32[]{:S(2)}) collective-permute-start(bf16[256,256]{1,0:T(8,128)(2,1)S(1)} %get-tuple-element.43), channel_id=1, source_target_pairs={{0,4},{4,0},{8,12},{12,8},{16,20},{20,16},{24,28},{28,24},{1,5},{5... | collective-permute-start | bytes 393224 | tf_op jit(solution)/shard_map/ppermute | solution.py:270
  9.2 1.1 %own_part.2 = (f32[256,256]{1,0:T(8,128)S(1)}, bf16[256,256]{1,0:T(8,128)(2,1)S(1)}, bf16[256,128]{1,0:T(8,128)(2,1)S(1)}, f32[256,1]{1,0:T(8,128)S(1)}, bf16[256,512]{1,0:T(8,128)(2,1)S(1)}) custom-call(bf16[256,256]{1,0:T(8,128)(2,1)S(1)} %get-tuple-element.40.residual, bf16[256,512]{1,0:T(8,128)(2,1)S(1)} %get-tuple-element.41.rmat, ...), custom_call_target="tpu_custom_call" | custom-call | flops 33554432 | bytes 1180032 | tf_op jit(solution)/shard_map/own_part/pallas_call | solution.py:47
  10.3 2.8 %collective-permute-done.2.other = bf16[256,256]{1,0:T(8,128)(2,1)S(1)} collective-permute-done((bf16[256,256]{1,0:T(8,128)(2,1)S(1)}, bf16[256,256]{1,0:T(8,128)(2,1)S(1)}, u32[]{:S(2)}, u32[]{:S(2)}) %collective-permute-start.2) | collective-permute-done | bytes 131104 | tf_op jit(solution)/shard_map/ppermute | solution.py:270
  13.2 0.2 join.2
  13.4 0.1 collective-permute-start.3
  13.4 1.2 %collective-permute-start.4 = (bf16[64,256]{1,0:T(8,128)(2,1)S(1)}, bf16[64,256]{1,0:T(8,128)(2,1)S(1)}, u32[]{:S(2)}, u32[]{:S(2)}) collective-permute-start(bf16[64,256]{1,0:T(8,128)(2,1)S(1)} %get-tuple-element.50), channel_id=1, source_target_pairs={{0,3},{1,2},{2,1},{3,0},{4,7},{5,6},{6,5},{7,4},{8,11},{9,10},{10,... | collective-permute-start | bytes 98312 | tf_op jit(solution)/shard_map/ppermute | solution.py:276
  14.7 0.2 local.2.rest
  14.9 0.0 collective-permute-done.3.inner
  14.9 2.0 %collective-permute-done.4.outer = bf16[64,256]{1,0:T(8,128)(2,1)S(1)} collective-permute-done((bf16[64,256]{1,0:T(8,128)(2,1)S(1)}, bf16[64,256]{1,0:T(8,128)(2,1)S(1)}, u32[]{:S(2)}, u32[]{:S(2)}) %collective-permute-start.4) | collective-permute-done | bytes 32800 | tf_op jit(solution)/shard_map/ppermute | solution.py:276
  16.8 0.2 residual.4
  17.0 1.6 %collective-permute-start.5 = (bf16[256,256]{1,0:T(8,128)(2,1)S(1)}, bf16[256,256]{1,0:T(8,128)(2,1)S(1)}, u32[]{:S(2)}, u32[]{:S(2)}) collective-permute-start(bf16[256,256]{1,0:T(8,128)(2,1)S(1)} %residual.4), channel_id=1, source_target_pairs={{0,8},{4,12},{8,0},{12,4},{16,24},{20,28},{24,16},{28,20},{1,9},{5... | collective-permute-start | bytes 393224 | tf_op jit(solution)/shard_map/ppermute | solution.py:270
  18.7 1.1 %own_part.3 = (f32[256,256]{1,0:T(8,128)S(1)}, bf16[256,256]{1,0:T(8,128)(2,1)S(1)}, bf16[256,128]{1,0:T(8,128)(2,1)S(1)}, f32[256,1]{1,0:T(8,128)S(1)}, bf16[256,512]{1,0:T(8,128)(2,1)S(1)}) custom-call(bf16[256,256]{1,0:T(8,128)(2,1)S(1)} %residual.4, bf16[256,512]{1,0:T(8,128)(2,1)S(1)} %get-tuple-element.51.rmat, s32[3,1,4,5]{3,2,1,0:T(4,128)S(1)} %copy-done.5, ...), custom_call_target="tpu_custom_call" | custom-call | flops 33554432 | bytes 1180032 | tf_op jit(solution)/shard_map/own_part/pallas_call | solution.py:47
  19.8 3.1 %collective-permute-done.5.other = bf16[256,256]{1,0:T(8,128)(2,1)S(1)} collective-permute-done((bf16[256,256]{1,0:T(8,128)(2,1)S(1)}, bf16[256,256]{1,0:T(8,128)(2,1)S(1)}, u32[]{:S(2)}, u32[]{:S(2)}) %collective-permute-start.5) | collective-permute-done | bytes 131104 | tf_op jit(solution)/shard_map/ppermute | solution.py:270
  22.9 0.2 join.3
  23.1 0.1 collective-permute-start.6
  23.2 1.2 %collective-permute-start.7 = (bf16[64,256]{1,0:T(8,128)(2,1)S(1)}, bf16[64,256]{1,0:T(8,128)(2,1)S(1)}, u32[]{:S(2)}, u32[]{:S(2)}) collective-permute-start(bf16[64,256]{1,0:T(8,128)(2,1)S(1)} %get-tuple-element.59), channel_id=1, source_target_pairs={{0,3},{1,2},{2,1},{3,0},{4,7},{5,6},{6,5},{7,4},{8,11},{9,10},{10,... | collective-permute-start | bytes 98312 | tf_op jit(solution)/shard_map/ppermute | solution.py:276
  24.4 0.2 local.3.rest
  24.6 0.0 copy-start.4
  24.7 2.0 %collective-permute-done.7.outer = bf16[64,256]{1,0:T(8,128)(2,1)S(1)} collective-permute-done((bf16[64,256]{1,0:T(8,128)(2,1)S(1)}, bf16[64,256]{1,0:T(8,128)(2,1)S(1)}, u32[]{:S(2)}, u32[]{:S(2)}) %collective-permute-start.7) | collective-permute-done | bytes 32800 | tf_op jit(solution)/shard_map/ppermute | solution.py:276
  26.6 0.2 residual.5
  26.8 2.7 %collective-permute-start.8 = (bf16[256,256]{1,0:T(8,128)(2,1)S(1)}, bf16[256,256]{1,0:T(8,128)(2,1)S(1)}, u32[]{:S(2)}, u32[]{:S(2)}) collective-permute-start(bf16[256,256]{1,0:T(8,128)(2,1)S(1)} %residual.5), channel_id=1, source_target_pairs={{0,16},{4,20},{8,24},{12,28},{16,0},{20,4},{24,8},{28,12},{1,17},{... | collective-permute-start | bytes 393224 | tf_op jit(solution)/shard_map/ppermute | solution.py:270
  29.5 0.1 copy.13.pcols
  29.6 0.8 %last_part.1 = (f32[256,256]{1,0:T(8,128)S(1)}, bf16[256,256]{1,0:T(8,128)(2,1)S(1)}, bf16[256,256]{1,0:T(8,128)(2,1)S(1)}, bf16[256,256]{1,0:T(8,128)(2,1)S(1)}) custom-call(bf16[256,256]{1,0:T(8,128)(2,1)S(1)} %residual.5, bf16[256,512]{1,0:T(8,128)(2,1)S(1)} %get-tuple-element.60.rmat, s32[3,1,4,2]{3,2,1,0:T(4,128)S(1)} %copy.13.pcols, ...), custom_call_target="tpu_custom_call" | custom-call | flops 33554432 | bytes 983136 | tf_op jit(solution)/shard_map/last_part/pallas_call | solution.py:47
  30.4 0.0 copy-start.3
  30.4 6.0 %collective-permute-done.8.other = bf16[256,256]{1,0:T(8,128)(2,1)S(1)} collective-permute-done((bf16[256,256]{1,0:T(8,128)(2,1)S(1)}, bf16[256,256]{1,0:T(8,128)(2,1)S(1)}, u32[]{:S(2)}, u32[]{:S(2)}) %collective-permute-start.8) | collective-permute-done | bytes 131104 | tf_op jit(solution)/shard_map/ppermute | solution.py:270
  36.4 0.2 last_join.1.refs_1_
  36.6 1.2 %collective-permute-start.9 = (bf16[256,256]{1,0:T(8,128)(2,1)S(1)}, bf16[256,256]{1,0:T(8,128)(2,1)S(1)}, u32[]{:S(2)}, u32[]{:S(2)}) collective-permute-start(bf16[256,256]{1,0:T(8,128)(2,1)S(1)} %last_join.1.refs_1_), channel_id=1, source_target_pairs={{0,2},{1,3},{2,0},{3,1},{4,6},{5,7},{6,4},{7,5},{8,10},{9,11},{10,... | collective-permute-start | bytes 393224 | tf_op jit(solution)/shard_map/ppermute | solution.py:270
  37.8 0.0 collective-permute-start.11
  37.8 4.0 %collective-permute-done.9.refs_1_ = bf16[256,256]{1,0:T(8,128)(2,1)S(1)} collective-permute-done((bf16[256,256]{1,0:T(8,128)(2,1)S(1)}, bf16[256,256]{1,0:T(8,128)(2,1)S(1)}, u32[]{:S(2)}, u32[]{:S(2)}) %collective-permute-start.9) | collective-permute-done | bytes 131104 | tf_op jit(solution)/shard_map/ppermute | solution.py:270
  41.8 0.2 coarse_own.1.refs_3_
  41.9 0.0 collective-permute-done.11.refs_2_
  42.0 0.2 coarse_middle.1.total
  42.2 0.9 %collective-permute-done.10.part = bf16[256,256]{1,0:T(8,128)(2,1)S(1)} collective-permute-done((bf16[256,256]{1,0:T(8,128)(2,1)S(1)}, bf16[256,256]{1,0:T(8,128)(2,1)S(1)}, u32[]{:S(2)}, u32[]{:S(2)}) %collective-permute-start.10) | collective-permute-done | bytes 131104 | tf_op jit(solution)/shard_map/ppermute | solution.py:270
  43.1 1.0 %up.1.refs_0_ = bf16[256,256]{1,0:T(8,128)(2,1)S(1)} custom-call(bf16[256,1024]{1,0:T(8,128)(2,1)S(1)} %copy-done.3, bf16[256,256]{1,0:T(8,128)(2,1)S(1)} %collective-permute-done.10.part, f32[256,256]{1,0:T(8,128)S(1)} %coarse_middle.1.total, f32[256,256]{1,0:T(8,128)S(1)} %get-tuple-element.54.rhs.refs_0_, f32[256,1]{1,0:T(8,128)S(1)} %get-tuple-element.53.scale.refs_1_, ...), custom_call_target="tpu_custom_call" | custom-call | flops 167772160 | bytes 1968128 | tf_op jit(solution)/shard_map/up/pallas_call | solution.py:47
  44.1 1.6 %collective-permute-start.12 = (bf16[256,256]{1,0:T(8,128)(2,1)S(1)}, bf16[256,256]{1,0:T(8,128)(2,1)S(1)}, u32[]{:S(2)}, u32[]{:S(2)}) collective-permute-start(bf16[256,256]{1,0:T(8,128)(2,1)S(1)} %up.1.refs_0_), channel_id=1, source_target_pairs={{0,4},{4,0},{8,12},{12,8},{16,20},{20,16},{24,28},{28,24},{1,5},{5... | collective-permute-start | bytes 393224 | tf_op jit(solution)/shard_map/ppermute | solution.py:270
  45.6 1.1 %last_raise.2.refs_5_ = f32[1,256,512]{2,1,0:T(8,128)} custom-call(bf16[256,256]{1,0:T(8,128)(2,1)S(1)} %up.1.refs_0_, f32[1,256,512]{2,1,0:T(8,128)S(1)} %copy-done.1, f32[256,1]{1,0:T(8,128)S(1)} %get-tuple-element.64.refs_2_, bf16[256,256]{1,0:T(8,128)(2,1)S(1)} %get-tuple-element.65.refs_3_, bf16[256,256]{1,0:T(8,128)(2,1)S(1)} %get-tuple-element.66.refs_4_), custom_call_target="tpu_custom_call" | custom-call | flops 67108864 | bytes 918528 | tf_op jit(solution)/shard_map/last_raise/pallas_call | solution.py:47
  46.8 2.9 %collective-permute-done.12.refs_0_ = bf16[256,256]{1,0:T(8,128)(2,1)S(1)} collective-permute-done((bf16[256,256]{1,0:T(8,128)(2,1)S(1)}, bf16[256,256]{1,0:T(8,128)(2,1)S(1)}, u32[]{:S(2)}, u32[]{:S(2)}) %collective-permute-start.12) | collective-permute-done | bytes 131104 | tf_op jit(solution)/shard_map/ppermute | solution.py:270
  49.7 1.1 %last_raise.3 = f32[1,256,512]{2,1,0:T(8,128)} custom-call(bf16[256,256]{1,0:T(8,128)(2,1)S(1)} %collective-permute-done.12.refs_0_, f32[1,256,512]{2,1,0:T(8,128)S(1)} %copy-done.1, f32[256,1]{1,0:T(8,128)S(1)} %get-tuple-element.64.refs_2_, bf16[256,256]{1,0:T(8,128)(2,1)S(1)} %get-tuple-element.65.refs_3_, ...), custom_call_target="tpu_custom_call", output_to_operand_aliasing={{}: (5, {})} | custom-call | flops 67108864 | bytes 1442816 | tf_op jit(solution)/shard_map/last_raise/pallas_call | solution.py:47
  (12 shorter events, 0.0 us)
Async XLA Ops:
  0.0 5.2 %copy-start = (bf16[3,1,4,5,64,64]{5,4,3,2,1,0:T(8,128)(2,1)S(1)}, bf16[3,1,4,5,64,64]{5,4,3,2,1,0:T(8,128)(2,1)}, u32[]{:S(2)}) copy-start(bf16[3,1,4,5,64,64]{5,4,3,2,1,0:T(8,128)(2,1)} %blocks.7) | copy-start | bytes 1474564
  0.0 5.2 %copy-start.1 = (f32[1,256,512]{2,1,0:T(8,128)S(1)}, f32[1,256,512]{2,1,0:T(8,128)}, u32[]{:S(2)}) copy-start(f32[1,256,512]{2,1,0:T(8,128)} %refs_1_.5) | copy-start | bytes 1572868
  1.3 3.9 %copy-start.5 = (s32[3,1,4,5]{3,2,1,0:T(4,128)S(1)}, s32[3,1,4,5]{3,2,1,0:T(4,128)}, u32[]{:S(2)}) copy-start(s32[3,1,4,5]{3,2,1,0:T(4,128)} %cols.5) | copy-start | bytes 724
  1.3 6.1 %collective-permute-start = (bf16[64,512]{1,0:T(8,128)(2,1)S(1)}, bf16[64,512]{1,0:T(8,128)(2,1)S(1)}, u32[]{:S(2)}, u32[]{:S(2)}) collective-permute-start(bf16[64,512]{1,0:T(8,128)(2,1)S(1)} %get-tuple-element.36._), channel_id=1, source_target_pairs={{0,1},{1,0},{2,3},{3,2},{4,5},{5,4},{6,7},{7,6},{8,9},{9,8},{10,11... | collective-permute-start | bytes 196616 | tf_op jit(solution)/shard_map/ppermute | solution.py:270
  1.8 5.6 %collective-permute-start.1 = (bf16[64,512]{1,0:T(8,128)(2,1)S(1)}, bf16[64,512]{1,0:T(8,128)(2,1)S(1)}, u32[]{:S(2)}, u32[]{:S(2)}) collective-permute-start(bf16[64,512]{1,0:T(8,128)(2,1)S(1)} %get-tuple-element.39), channel_id=1, source_target_pairs={{0,3},{1,2},{2,1},{3,0},{4,7},{5,6},{6,5},{7,4},{8,11},{9,10},{10,... | collective-permute-start | bytes 196616 | tf_op jit(solution)/shard_map/ppermute | solution.py:276
  7.4 1.8 %copy-start.2 = (bf16[3,1,4,3,64,64]{5,4,3,2,1,0:T(8,128)(2,1)S(1)}, bf16[3,1,4,3,64,64]{5,4,3,2,1,0:T(8,128)(2,1)}, u32[]{:S(2)}) copy-start(bf16[3,1,4,3,64,64]{5,4,3,2,1,0:T(8,128)(2,1)} %rblocks.3) | copy-start | bytes 884740
  7.6 5.5 %collective-permute-start.2 = (bf16[256,256]{1,0:T(8,128)(2,1)S(1)}, bf16[256,256]{1,0:T(8,128)(2,1)S(1)}, u32[]{:S(2)}, u32[]{:S(2)}) collective-permute-start(bf16[256,256]{1,0:T(8,128)(2,1)S(1)} %get-tuple-element.43), channel_id=1, source_target_pairs={{0,4},{4,0},{8,12},{12,8},{16,20},{20,16},{24,28},{28,24},{1,5},{5... | collective-permute-start | bytes 393224 | tf_op jit(solution)/shard_map/ppermute | solution.py:270
  13.4 1.5 %collective-permute-start.3 = (bf16[64,256]{1,0:T(8,128)(2,1)S(1)}, bf16[64,256]{1,0:T(8,128)(2,1)S(1)}, u32[]{:S(2)}, u32[]{:S(2)}) collective-permute-start(bf16[64,256]{1,0:T(8,128)(2,1)S(1)} %get-tuple-element.49), channel_id=1, source_target_pairs={{0,1},{1,0},{2,3},{3,2},{4,5},{5,4},{6,7},{7,6},{8,9},{9,8},{10,11... | collective-permute-start | bytes 98312 | tf_op jit(solution)/shard_map/ppermute | solution.py:270
  13.4 3.4 %collective-permute-start.4 = (bf16[64,256]{1,0:T(8,128)(2,1)S(1)}, bf16[64,256]{1,0:T(8,128)(2,1)S(1)}, u32[]{:S(2)}, u32[]{:S(2)}) collective-permute-start(bf16[64,256]{1,0:T(8,128)(2,1)S(1)} %get-tuple-element.50), channel_id=1, source_target_pairs={{0,3},{1,2},{2,1},{3,0},{4,7},{5,6},{6,5},{7,4},{8,11},{9,10},{10,... | collective-permute-start | bytes 98312 | tf_op jit(solution)/shard_map/ppermute | solution.py:276
  17.0 5.9 %collective-permute-start.5 = (bf16[256,256]{1,0:T(8,128)(2,1)S(1)}, bf16[256,256]{1,0:T(8,128)(2,1)S(1)}, u32[]{:S(2)}, u32[]{:S(2)}) collective-permute-start(bf16[256,256]{1,0:T(8,128)(2,1)S(1)} %residual.4), channel_id=1, source_target_pairs={{0,8},{4,12},{8,0},{12,4},{16,24},{20,28},{24,16},{28,20},{1,9},{5... | collective-permute-start | bytes 393224 | tf_op jit(solution)/shard_map/ppermute | solution.py:270
  23.1 1.5 %collective-permute-start.6 = (bf16[64,256]{1,0:T(8,128)(2,1)S(1)}, bf16[64,256]{1,0:T(8,128)(2,1)S(1)}, u32[]{:S(2)}, u32[]{:S(2)}) collective-permute-start(bf16[64,256]{1,0:T(8,128)(2,1)S(1)} %get-tuple-element.58), channel_id=1, source_target_pairs={{0,1},{1,0},{2,3},{3,2},{4,5},{5,4},{6,7},{7,6},{8,9},{9,8},{10,11... | collective-permute-start | bytes 98312 | tf_op jit(solution)/shard_map/ppermute | solution.py:270
  23.2 3.4 %collective-permute-start.7 = (bf16[64,256]{1,0:T(8,128)(2,1)S(1)}, bf16[64,256]{1,0:T(8,128)(2,1)S(1)}, u32[]{:S(2)}, u32[]{:S(2)}) collective-permute-start(bf16[64,256]{1,0:T(8,128)(2,1)S(1)} %get-tuple-element.59), channel_id=1, source_target_pairs={{0,3},{1,2},{2,1},{3,0},{4,7},{5,6},{6,5},{7,4},{8,11},{9,10},{10,... | collective-permute-start | bytes 98312 | tf_op jit(solution)/shard_map/ppermute | solution.py:276
  24.6 4.9 %copy-start.4 = (bf16[3,1,4,2,64,64]{5,4,3,2,1,0:T(8,128)(2,1)S(1)}, bf16[3,1,4,2,64,64]{5,4,3,2,1,0:T(8,128)(2,1)}, u32[]{:S(2)}) copy-start(bf16[3,1,4,2,64,64]{5,4,3,2,1,0:T(8,128)(2,1)} %refs_2_.1) | copy-start | bytes 589828
  26.6 2.8 %copy-start.6 = (s32[3,1,4,2]{2,3,1,0:T(2,128)S(1)}, s32[3,1,4,2]{2,3,1,0:T(2,128)}, u32[]{:S(2)}) copy-start(s32[3,1,4,2]{2,3,1,0:T(2,128)} %param.13) | copy-start | bytes 292
  26.8 9.6 %collective-permute-start.8 = (bf16[256,256]{1,0:T(8,128)(2,1)S(1)}, bf16[256,256]{1,0:T(8,128)(2,1)S(1)}, u32[]{:S(2)}, u32[]{:S(2)}) collective-permute-start(bf16[256,256]{1,0:T(8,128)(2,1)S(1)} %residual.5), channel_id=1, source_target_pairs={{0,16},{4,20},{8,24},{12,28},{16,0},{20,4},{24,8},{28,12},{1,17},{... | collective-permute-start | bytes 393224 | tf_op jit(solution)/shard_map/ppermute | solution.py:270
  30.4 11.3 %copy-start.3 = (bf16[256,1024]{1,0:T(8,128)(2,1)S(1)}, bf16[256,1024]{1,0:T(8,128)(2,1)}, u32[]{:S(2)}) copy-start(bf16[256,1024]{1,0:T(8,128)(2,1)} %inverse.1) | copy-start | bytes 1572868
  36.6 5.1 %collective-permute-start.9 = (bf16[256,256]{1,0:T(8,128)(2,1)S(1)}, bf16[256,256]{1,0:T(8,128)(2,1)S(1)}, u32[]{:S(2)}, u32[]{:S(2)}) collective-permute-start(bf16[256,256]{1,0:T(8,128)(2,1)S(1)} %last_join.1.refs_1_), channel_id=1, source_target_pairs={{0,2},{1,3},{2,0},{3,1},{4,6},{5,7},{6,4},{7,5},{8,10},{9,11},{10,... | collective-permute-start | bytes 393224 | tf_op jit(solution)/shard_map/ppermute | solution.py:270
  37.8 4.2 %collective-permute-start.11 = (bf16[256,256]{1,0:T(8,128)(2,1)S(1)}, bf16[256,256]{1,0:T(8,128)(2,1)S(1)}, u32[]{:S(2)}, u32[]{:S(2)}) collective-permute-start(bf16[256,256]{1,0:T(8,128)(2,1)S(1)} %last_join.1.refs_1_), channel_id=1, source_target_pairs={{0,1},{1,0},{2,3},{3,2},{4,5},{5,4},{6,7},{7,6},{8,9},{9,8},{10,11... | collective-permute-start | bytes 393224 | tf_op jit(solution)/shard_map/ppermute | solution.py:270
  41.7 1.3 %collective-permute-start.10 = (bf16[256,256]{1,0:T(8,128)(2,1)S(1)}, bf16[256,256]{1,0:T(8,128)(2,1)S(1)}, u32[]{:S(2)}, u32[]{:S(2)}) collective-permute-start(bf16[256,256]{1,0:T(8,128)(2,1)S(1)} %collective-permute-done.9.refs_1_), channel_id=1, source_target_pairs={{0,1},{1,0},{2,3},{3,2},{4,5},{5,4},{6,7},{7,6},{8,9},{9,8},{10,11... | collective-permute-start | bytes 393224 | tf_op jit(solution)/shard_map/ppermute | solution.py:270
  44.1 5.6 %collective-permute-start.12 = (bf16[256,256]{1,0:T(8,128)(2,1)S(1)}, bf16[256,256]{1,0:T(8,128)(2,1)S(1)}, u32[]{:S(2)}, u32[]{:S(2)}) collective-permute-start(bf16[256,256]{1,0:T(8,128)(2,1)S(1)} %up.1.refs_0_), channel_id=1, source_target_pairs={{0,4},{4,0},{8,12},{12,8},{16,20},{20,16},{24,28},{28,24},{1,5},{5... | collective-permute-start | bytes 393224 | tf_op jit(solution)/shard_map/ppermute | solution.py:270

commit v4 on v3

v4 whole, which is shorter than its diff:
```python
import functools

import jax
import jax.numpy as jnp
from jax import lax
from jax.experimental import pallas as pl
from jax.experimental.pallas import tpu as pltpu
from jax.sharding import PartitionSpec as P

relax_down = 0.7
relax_up = 0.5
f32 = jnp.float32
bf16 = jnp.bfloat16
grant = 12 * 1024 * 1024
chunk_width = 128


def matmul(a, b):
    return jnp.dot(a, b, preferred_element_type=f32)


def array(shape, dtype):
    return jax.ShapeDtypeStruct(shape, dtype)


def whole():
    return pl.BlockSpec(memory_space=pltpu.VMEM)


def level_block(value, level_idx):
    shape = (1,) + value.shape[1:]
    return pl.BlockSpec(shape, lambda i: (level_idx,) + (0,) * (value.ndim - 1))


def scalars():
    return pl.BlockSpec(memory_space=pltpu.SMEM)


def in_hbm(value):
    return pltpu.with_memory_space_constraint(value, pltpu.HBM), pl.BlockSpec(memory_space=pltpu.HBM)


def run(body, name, outs, operands, flops=0, scratch=(), out_space=pltpu.VMEM, aliases=None):
    arrays = [o[0] if isinstance(o, tuple) else o for o in operands]
    specs = [o[1] if isinstance(o, tuple) else whole() for o in operands]
    windows = any(isinstance(o, tuple) and o[1].block_shape is not None for o in operands)
    moved = sum(a.size * a.dtype.itemsize for a in arrays)
    return pl.pallas_call(
        body,
        grid=(1,) if windows else (),
        out_shape=outs,
        in_specs=specs,
        out_specs=[pl.BlockSpec(memory_space=out_space)] * len(outs),
        input_output_aliases=aliases or {},
        scratch_shapes=list(scratch),
        compiler_params=pltpu.CompilerParams(vmem_limit_bytes=grant),
        cost_estimate=pl.CostEstimate(flops=flops, bytes_accessed=moved, transcendentals=0),
        name=name,
    )(*arrays)


def diagonal_of(block):
    size = block.shape[0]
    rows = lax.broadcasted_iota(jnp.int32, (size, size), 0)
    lanes = lax.broadcasted_iota(jnp.int32, (size, size), 1)
    return jnp.sum(jnp.where(rows == lanes, block, 0.0), axis=1, keepdims=True)


def placed(base, others, ids, target):
    total = base
    for block, ident in zip(others, ids):
        term = block * jnp.where(ident == target, 1.0, 0.0).astype(f32)
        total = term if total is None else total + term
    return total


def parity_of():
    return lax.rem(lax.axis_index("narrow"), 2)


def put_ends(first, last, inner_ref, outer_ref):
    even = parity_of() == 0
    inner_ref[...] = jnp.where(even, last, first)
    outer_ref[...] = jnp.where(even, first, last)


def assemble_galerkin(level_idx, cols, blocks, local_ref, rim_ref, scale_ref):
    count, slots, size = blocks.shape[2], blocks.shape[3], blocks.shape[4]
    parity = parity_of()
    piece = lax.axis_index("narrow")
    last = lax.axis_size("narrow") - 1
    inside = jnp.where((piece == 0) | (piece == last), 0.0, 1.0).astype(f32)
    for b in range(count):
        held = [blocks[0, 0, b, s].astype(f32) for s in range(slots)]
        ids = [cols[level_idx, 0, b, s] for s in range(1, slots)]
        rows = pl.ds(b * size, size)
        scale_ref[rows, :] = 1.0 / diagonal_of(held[0])
        line = [placed(held[0] if c == b else None, held[1:], ids, c) for c in range(count)]
        local_ref[rows, :] = jnp.concatenate(line, axis=1).astype(bf16)
        rims = [
            placed(None, held[1:], ids, count + 1 - parity),
            placed(None, held[1:], ids, count + parity) * inside,
        ]
        rim_ref[rows, :] = jnp.concatenate(rims, axis=1).astype(bf16)


def assemble_restrict(level_idx, cols, blocks, out_ref):
    count, slots, size = blocks.shape[2], blocks.shape[3], blocks.shape[4]
    for b in range(count):
        held = [blocks[0, 0, b, s].astype(f32) for s in range(slots)]
        ids = [cols[level_idx, 0, b, s] for s in range(2, slots)]
        fixed = {b: held[0], count + b: held[1]}
        line = [placed(fixed.get(c), held[2:], ids, c) for c in range(2 * count)]
        out_ref[pl.ds(b * size, size), :] = jnp.concatenate(line, axis=1).astype(bf16)


def assemble_prolong(level_idx, cols, blocks, out_ref):
    count, slots, size = blocks.shape[2], blocks.shape[3], blocks.shape[4]
    for b in range(count):
        held = [blocks[0, 0, b, s].astype(f32) for s in range(slots)]
        ids = [cols[level_idx, 0, b, s] for s in range(1, slots)]
        line = [placed(held[0] if c == b else None, held[1:], ids, c) for c in range(count)]
        out_ref[pl.ds(b * size, size), :] = jnp.concatenate(line, axis=1).astype(bf16)


def start_kernel(rhs, blocks, inner_ref, outer_ref, rows, pivots, sems):
    count, size = blocks.shape[2], blocks.shape[4]
    copies = []
    for slot, which in enumerate((0, count - 1)):
        source = rhs.at[0, pl.ds(which * size, size), :]
        copies.append(pltpu.make_async_copy(source, rows.at[slot], sems.at[slot]))
        source = blocks.at[0, 0, which, 0]
        copies.append(pltpu.make_async_copy(source, pivots.at[slot], sems.at[2 + slot]))
    for copy in copies:
        copy.start()
    for copy in copies:
        copy.wait()
    first, last = (
        (rows[slot] * (relax_down / diagonal_of(pivots[slot].astype(f32)))).astype(bf16)
        for slot in range(2)
    )
    put_ends(first, last, inner_ref, outer_ref)


def first_local_kernel(rhs, _, cols, blocks, rest, local, rim, scale):
    assemble_galerkin(0, cols, blocks, local, rim, scale)
    smoothed = (rhs[0] * (relax_down * scale[...])).astype(bf16)
    rest[...] = rhs[0] - matmul(local[...], smoothed)


def bit_of(level_idx):
    return lax.axis_index("wide") >> level_idx & 1


def lanes_of(place, width):
    start = 0
    for level_idx, flip, step in place:
        start = start + (bit_of(level_idx) ^ flip if level_idx >= 0 else flip) * step
    return pl.ds(pl.multiple_of(start, width), width)


def first_residual_kernel(places, rest, rim, inner, outer, *refs):
    for ref, place in zip(refs, places):
        lanes = lanes_of(place, ref.shape[1])
        rims = jnp.concatenate([inner[:, lanes], outer[:, lanes]], axis=0)
        ref[...] = (rest[:, lanes] - matmul(rim[...], rims)).astype(bf16)


def residual_kernel(rhs, local, smoothed, rim, inner, outer, out):
    rims = jnp.concatenate([inner[...], outer[...]], axis=0)
    applied = matmul(local[...], smoothed[...]) + matmul(rim[...], rims)
    out[...] = (rhs[...] - applied).astype(bf16)


def operators_kernel(level_idx, _, rcols, rblocks, cols, blocks, rmat, local, rim, scale):
    assemble_restrict(level_idx, rcols, rblocks, rmat)
    assemble_galerkin(level_idx + 1, cols, blocks, local, rim, scale)


def last_operators_kernel(level_idx, levels, _, rcols, rblocks, pcols, *refs):
    assemble_restrict(level_idx, rcols, rblocks, refs[levels])
    for idx, blocks, out in zip(range(levels), refs[:levels], refs[levels + 1 :]):
        assemble_prolong(idx, pcols, blocks, out)


def restricted(level_idx, rmat, kept, other):
    width = rmat.shape[1] // 2
    own = pl.multiple_of(bit_of(level_idx) * width, width)
    far = pl.multiple_of((1 - bit_of(level_idx)) * width, width)
    total = matmul(rmat[:, pl.ds(own, width)], kept[...])
    return total + matmul(rmat[:, pl.ds(far, width)], other[...])


def join_kernel(level_idx, rmat, kept, other, scale, rhs, smoothed, inner_ref, outer_ref):
    size = inner_ref.shape[0]
    current = restricted(level_idx, rmat, kept, other)
    rhs[...] = current
    rounded = (current * (relax_down * scale[...])).astype(bf16)
    smoothed[...] = rounded
    put_ends(rounded[:size], rounded[-size:], inner_ref, outer_ref)


def last_join_kernel(level_idx, rmat, kept, other, rounded):
    rounded[...] = restricted(level_idx, rmat, kept, other).astype(bf16)


def inverse_part(inverse, part, offset):
    depth = part.shape[0]
    piece = lax.axis_index("narrow") ^ offset
    return matmul(inverse[:, pl.ds(pl.multiple_of(piece * depth, depth), depth)], part[...])


def raise_level(coarse, rhs, scale, local, pmat):
    updated = rhs * (relax_down * scale) + matmul(pmat, coarse)
    applied = matmul(local, updated.astype(bf16))
    return updated + (relax_up * scale) * (rhs - applied)


def up_kernel(offsets, depth, inverse, *refs):
    value = None
    for part, offset in zip(refs, offsets):
        term = inverse_part(inverse, part, offset)
        value = term if value is None else value + term
    refs = refs[len(offsets) :]
    for step in range(depth):
        rhs, scale, local, pmat = refs[4 * step : 4 * step + 4]
        value = raise_level(value.astype(bf16), rhs[...], scale[...], local[...], pmat[...])
    refs[-1][...] = value.astype(bf16)


def last_raise_kernel(places, *refs):
    coarse, refs = refs[: len(places)], refs[len(places) :]
    rhs, scale, local, pmat = refs[:4]
    out, sems = refs[-2 - len(places)], refs[-1]
    copies = []
    for slot, (place, value, made) in enumerate(zip(places, coarse, refs[-1 - len(places) : -1])):
        lanes = lanes_of(place, value.shape[1])
        made[...] = raise_level(value[...], rhs[0, :, lanes], scale[...], local[...], pmat[...])
        copy = pltpu.make_async_copy(made, out.at[0, :, lanes], sems.at[slot])
        copy.start()
        copies.append(copy)
    for copy in copies:
        copy.wait()


def exchange(value, axis, bit):
    count = lax.axis_size(axis)
    return lax.ppermute(value, axis, [(i, i ^ bit) for i in range(count)])


def swap_ends(inner, outer):
    count = lax.axis_size("narrow")
    gaps = [(i, (i + 1 if i % 2 else i - 1) % count) for i in range(count)]
    outer = lax.ppermute(outer, "narrow", gaps)
    return exchange(inner, "narrow", 1), outer


def on_device(
    level_rhs,
    galerkin_cols,
    galerkin_blocks,
    restrict_cols,
    restrict_blocks,
    prolong_cols,
    prolong_blocks,
    coarse_inverse,
):
    levels = galerkin_cols.shape[0]
    count = galerkin_cols.shape[2]
    size = galerkin_blocks.shape[-1]
    rows, fields = level_rhs.shape[1:]
    half = fields // 2
    chunks = range(half // chunk_width)
    width = half // len(chunks)
    gcols, rcols, pcols = ((c, scalars()) for c in (galerkin_cols, restrict_cols, prolong_cols))
    operator_shapes = [
        array((rows, rows), bf16), array((rows, 2 * size), bf16), array((rows, 1), f32)
    ]
    rmat_shape = array((rows, 2 * rows), bf16)
    chunk_shape = array((rows, width), bf16)

    def ends_shape(columns):
        return array((size, columns), bf16)

    def of_level(value, level_idx):
        return value, level_block(value, level_idx)

    def flops(columns, products=1):
        return 2 * products * rows * rows * columns

    def place_of(chunk, flip):
        return (0, flip, half), (-1, chunk, width)

    ends = run(
        start_kernel, "start", [ends_shape(fields)] * 2,
        [in_hbm(level_rhs), in_hbm(galerkin_blocks)],
        scratch=[
            pltpu.VMEM((2, size, fields), f32), pltpu.VMEM((2, size, size), bf16),
            pltpu.SemaphoreType.DMA((4,)),
        ],
    )
    inner, outer = swap_ends(*ends)
    rest, local, rim, scale = run(
        first_local_kernel, "first_local", [array((rows, fields), f32)] + operator_shapes,
        [level_rhs, ends[0], gcols, of_level(galerkin_blocks, 0)], flops=flops(fields),
    )
    operators = [(scale, local)]
    sent, kept = [], []
    for chunk in chunks:
        places = place_of(chunk, 1), place_of(chunk, 0)
        far, near = run(
            functools.partial(first_residual_kernel, places), "first_residual", [chunk_shape] * 2,
            [rest, rim, inner, outer],
        )
        sent.append(far)
        kept.append(near)
    right_sides = [level_rhs]
    for level_idx in range(levels):
        other = [exchange(value, "wide", 1 << level_idx) for value in sent]
        if level_idx + 1 < levels:
            rmat, local, rim, scale = run(
                functools.partial(operators_kernel, level_idx), "operators",
                [rmat_shape] + operator_shapes,
                [kept[0], rcols, of_level(restrict_blocks, level_idx),
                 gcols, of_level(galerkin_blocks, level_idx + 1)],
            )
            operators.append((scale, local))
            sent = []
            sides = []
            for chunk in chunks:
                rhs, smoothed, *ends = run(
                    functools.partial(join_kernel, level_idx), "join",
                    [array((rows, width), f32), chunk_shape] + [ends_shape(width)] * 2,
                    [rmat, kept[chunk], other[chunk], scale], flops=flops(width, 2),
                )
                inner, outer = swap_ends(*ends)
                (value,) = run(
                    residual_kernel, "residual", [chunk_shape],
                    [rhs, local, smoothed, rim, inner, outer], flops=flops(width, 2),
                )
                sides.append(rhs)
                sent.append(value)
            kept = sent
            right_sides.append(sides)
        else:
            rmat, *pmats = run(
                functools.partial(last_operators_kernel, level_idx, levels), "last_operators",
                [rmat_shape] + operator_shapes[:1] * levels,
                [kept[0], rcols, of_level(restrict_blocks, level_idx), pcols]
                + [of_level(prolong_blocks, idx) for idx in range(levels)],
            )
            mine = [
                run(
                    functools.partial(last_join_kernel, level_idx), "last_join", [chunk_shape],
                    [rmat, kept[chunk], other[chunk]], flops=flops(width, 2),
                )[0]
                for chunk in chunks
            ]
    pieces = lax.axis_size("narrow")
    order = sorted(range(1, pieces), key=lambda o: (bin(o).count("1"), -o))
    own, far = [], []
    for chunk in chunks:
        parts = {0: mine[chunk]}
        for offset in order:
            low = offset & -offset
            parts[offset] = exchange(parts[offset ^ low], "narrow", low)
        offsets = tuple(parts)
        operands = [coarse_inverse] + [parts[o] for o in offsets]
        for level_idx in reversed(range(1, levels)):
            operands += [right_sides[level_idx][chunk], *operators[level_idx], pmats[level_idx]]
        (coarse,) = run(
            functools.partial(up_kernel, offsets, levels - 1), "up", [chunk_shape], operands,
            flops=flops(width, len(offsets) + 2 * (levels - 1)),
        )
        own.append((coarse, place_of(chunk, 0)))
        far.append((exchange(coarse, "wide", 1), place_of(chunk, 1)))
    result = None
    for group in [own] + [[value] for value in far]:
        operands = [value for value, _ in group] + [level_rhs, *operators[0], pmats[0]]
        aliases = {}
        if result is not None:
            aliases[len(operands)] = 0
            operands.append(in_hbm(result))
        (result,) = run(
            functools.partial(last_raise_kernel, tuple(place for _, place in group)),
            "last_raise", [array((1, rows, fields), f32)], operands,
            flops=flops(width, 2 * len(group)),
            scratch=[pltpu.VMEM((rows, width), f32)] * len(group)
            + [pltpu.SemaphoreType.DMA((len(group),))],
            out_space=pltpu.HBM, aliases=aliases,
        )
    return result


def solution(mesh):
    in_specs = (
        P("wide", "narrow", None),
        P(None, "wide", "narrow", None),
        P(None, "wide", "narrow", None, None, None),
        P(None, "wide", "narrow", None),
        P(None, "wide", "narrow", None, None, None),
        P(None, "wide", "narrow", None),
        P(None, "wide", "narrow", None, None, None),
        P("narrow", None),
    )
    out_specs = P("wide", "narrow", None)
    return jax.shard_map(
        on_device, mesh=mesh, in_specs=in_specs, out_specs=out_specs, check_vma=False
    )
```

time: 51 us -> 47.9 us (0.939)
  waiting for transfers between devices: 23.7 us -> 7.44 us
  starting transfers between devices: 14.4 us -> 25.2 us
  Pallas kernels: 11.6 us -> 13.4 us
    ppermute x10 -> x19, waiting for transfers between devices: 19.7 us -> 7.21 us  [exchange(): return lax.ppermute(value, axis, [(i, i ^ bit) for i in range(count)])]
    ppermute x10 -> x19, starting transfers between devices: 9.29 us -> 16.8 us  [exchange(): return lax.ppermute(value, axis, [(i, i ^ bit) for i in range(count)])]
    ppermute x3 -> x5, waiting for transfers between devices: 3.94 us -> 0.23 us  [swap_ends(): outer = lax.ppermute(outer, 'narrow', gaps)]
    ppermute x3 -> x5, starting transfers between devices: 5.07 us -> 8.37 us  [swap_ends(): outer = lax.ppermute(outer, 'narrow', gaps)]
    pallas_call x18 -> x22, Pallas kernels: 11.6 us -> 13.4 us  [run(): pl.pallas_call(body, grid=(1,) if windows else (), out_shape=outs, in_spe...]
    unnamed x16 -> x20, local copies, waits for them, and re-layouts: 0.93 us -> 1.41 us
  transfers between devices with their start and end apart: 13 -> 24, of which waited for: 8 -> 8; matrix products, arithmetic and copies ran while one was open for 2% -> 0% of each run, Pallas kernels for 14% -> 23%
where the time goes in v4:
time: 47.9 us; the launch traced here: 47.6 us
  starting transfers between devices  25.2 us (53%)
  Pallas kernels  13.4 us (28%)
  waiting for transfers between devices  7.44 us (16%)
  local copies, waits for them, and re-layouts  1.41 us (3%)
    ppermute x19, starting transfers between devices, exchange(): return lax.ppermute(value, axis, [(i, i ^ bit) for i in range(count)])  16.8 us
    pallas_call x22, Pallas kernels, run(): pl.pallas_call(body, grid=(1,) if windows else (), out_shape=outs, in_spe...  13.4 us
    ppermute x5, starting transfers between devices, swap_ends(): outer = lax.ppermute(outer, 'narrow', gaps)  8.37 us
    ppermute x19, waiting for transfers between devices, exchange(): return lax.ppermute(value, axis, [(i, i ^ bit) for i in range(count)])  7.21 us
    unnamed x20, local copies, waits for them, and re-layouts  1.41 us
  transfers between devices with their start and end apart: 24, of which 8 were waited for; matrix products, arithmetic and copies ran while one was open for 0% of the time, Pallas kernels for 23%

profile of v4, /device:TPU:0, one launch (start us, length us, event | category | flops | bytes accessed | tf_op | source)
XLA Modules:
  0.0 47.6 jit_solution(2884437332472769322)
XLA Ops:
  0.0 1.2 %start.1 = (bf16[64,512]{1,0:T(8,128)(2,1)S(1)}, bf16[64,512]{1,0:T(8,128)(2,1)S(1)}) custom-call(f32[1,256,512]{2,1,0:T(8,128)} %refs_1_.5, bf16[3,1,4,5,64,64]{5,4,3,2,1,0:T(8,128)(2,1)} %blocks.7), custom_call_target="tpu_custom_call" | custom-call | bytes 1015808 | tf_op jit(solution)/shard_map/start/pallas_call | solution.py:48
  1.3 2.4 %collective-permute-start.1 = (bf16[64,512]{1,0:T(8,128)(2,1)S(1)}, bf16[64,512]{1,0:T(8,128)(2,1)S(1)}, u32[]{:S(2)}, u32[]{:S(2)}) collective-permute-start(bf16[64,512]{1,0:T(8,128)(2,1)S(1)} %get-tuple-element.46), channel_id=1, source_target_pairs={{0,3},{1,2},{2,1},{3,0},{4,7},{5,6},{6,5},{7,4},{8,11},{9,10},{10,... | collective-permute-start | bytes 196616 | tf_op jit(solution)/shard_map/ppermute | solution.py:254
  3.7 0.7 %collective-permute-start = (bf16[64,512]{1,0:T(8,128)(2,1)S(1)}, bf16[64,512]{1,0:T(8,128)(2,1)S(1)}, u32[]{:S(2)}, u32[]{:S(2)}) collective-permute-start(bf16[64,512]{1,0:T(8,128)(2,1)S(1)} %get-tuple-element.43._), channel_id=1, source_target_pairs={{0,1},{1,0},{2,3},{3,2},{4,5},{5,4},{6,7},{7,6},{8,9},{9,8},{10,11... | collective-permute-start | bytes 196616 | tf_op jit(solution)/shard_map/ppermute | solution.py:248
  4.4 0.7 %copy-done.5 = s32[3,1,4,5]{3,2,1,0:T(4,128)S(1)} copy-done((s32[3,1,4,5]{3,2,1,0:T(4,128)S(1)}, s32[3,1,4,5]{3,2,1,0:T(4,128)}, u32[]{:S(2)}) %copy-start.5) | copy-done | bytes 264
  5.1 1.1 %first_local.1 = (f32[256,512]{1,0:T(8,128)S(1)}, bf16[256,256]{1,0:T(8,128)(2,1)S(1)}, bf16[256,128]{1,0:T(8,128)(2,1)S(1)}, f32[256,1]{1,0:T(8,128)S(1)}) custom-call(f32[1,256,512]{2,1,0:T(8,128)S(1)} %copy-done.1, bf16[64,512]{1,0:T(8,128)(2,1)S(1)} %get-tuple-element.43._, s32[3,1,4,5]{3,2,1,0:T(4,128)S(1)} %copy-done.5, ...), custom_call_target="tpu_custom_call" | custom-call | flops 67108864 | bytes 1081584 | tf_op jit(solution)/shard_map/first_local/pallas_call | solution.py:48
  6.2 0.2 first_residual.2
  6.4 2.5 %collective-permute-start.2 = (bf16[256,128]{1,0:T(8,128)(2,1)S(1)}, bf16[256,128]{1,0:T(8,128)(2,1)S(1)}, u32[]{:S(2)}, u32[]{:S(2)}) collective-permute-start(bf16[256,128]{1,0:T(8,128)(2,1)S(1)} %get-tuple-element.49), channel_id=1, source_target_pairs={{0,4},{4,0},{8,12},{12,8},{16,20},{20,16},{24,28},{28,24},{1,5},{5... | collective-permute-start | bytes 196616 | tf_op jit(solution)/shard_map/ppermute | solution.py:248
  9.2 0.4 copy-done.7
  9.8 1.1 %operators.2 = (bf16[256,512]{1,0:T(8,128)(2,1)S(1)}, bf16[256,256]{1,0:T(8,128)(2,1)S(1)}, bf16[256,128]{1,0:T(8,128)(2,1)S(1)}, f32[256,1]{1,0:T(8,128)S(1)}) custom-call(bf16[256,128]{1,0:T(8,128)(2,1)S(1)} %get-tuple-element.47._.kept, s32[3,1,4,3]{3,2,1,0:T(4,128)S(1)} %copy.11.rcols, bf16[3,1,4,3,64,64]{5,4,3,2,1,0:T(8,128)(2,1)S(1)} %copy-done.2, ...), custom_call_target="tpu_custom_call" | custom-call | bytes 852352 | tf_op jit(solution)/shard_map/operators/pallas_call | solution.py:48
  10.9 0.4 collective-permute-done.2.other
  11.3 0.2 join.4
  11.6 2.1 %collective-permute-start.4 = (bf16[64,128]{1,0:T(8,128)(2,1)S(1)}, bf16[64,128]{1,0:T(8,128)(2,1)S(1)}, u32[]{:S(2)}, u32[]{:S(2)}) collective-permute-start(bf16[64,128]{1,0:T(8,128)(2,1)S(1)} %get-tuple-element.56), channel_id=1, source_target_pairs={{0,3},{1,2},{2,1},{3,0},{4,7},{5,6},{6,5},{7,4},{8,11},{9,10},{10,... | collective-permute-start | bytes 49160 | tf_op jit(solution)/shard_map/ppermute | solution.py:254
  13.7 0.2 join.6
  14.1 1.3 %collective-permute-start.10 = (bf16[64,128]{1,0:T(8,128)(2,1)S(1)}, bf16[64,128]{1,0:T(8,128)(2,1)S(1)}, u32[]{:S(2)}, u32[]{:S(2)}) collective-permute-start(bf16[64,128]{1,0:T(8,128)(2,1)S(1)} %get-tuple-element.71), channel_id=1, source_target_pairs={{0,3},{1,2},{2,1},{3,0},{4,7},{5,6},{6,5},{7,4},{8,11},{9,10},{10,... | collective-permute-start | bytes 49160 | tf_op jit(solution)/shard_map/ppermute | solution.py:254
  15.4 0.2 residual.4._.kept
  15.6 1.6 %collective-permute-start.5 = (bf16[256,128]{1,0:T(8,128)(2,1)S(1)}, bf16[256,128]{1,0:T(8,128)(2,1)S(1)}, u32[]{:S(2)}, u32[]{:S(2)}) collective-permute-start(bf16[256,128]{1,0:T(8,128)(2,1)S(1)} %residual.4._.kept), channel_id=1, source_target_pairs={{0,8},{4,12},{8,0},{12,4},{16,24},{20,28},{24,16},{28,20},{1,9},{5... | collective-permute-start | bytes 196616 | tf_op jit(solution)/shard_map/ppermute | solution.py:248
  17.2 0.2 residual.6.kept
  17.4 1.6 %collective-permute-start.11 = (bf16[256,128]{1,0:T(8,128)(2,1)S(1)}, bf16[256,128]{1,0:T(8,128)(2,1)S(1)}, u32[]{:S(2)}, u32[]{:S(2)}) collective-permute-start(bf16[256,128]{1,0:T(8,128)(2,1)S(1)} %residual.6.kept), channel_id=1, source_target_pairs={{0,8},{4,12},{8,0},{12,4},{16,24},{20,28},{24,16},{28,20},{1,9},{5... | collective-permute-start | bytes 196616 | tf_op jit(solution)/shard_map/ppermute | solution.py:248
  19.1 1.1 %operators.3 = (bf16[256,512]{1,0:T(8,128)(2,1)S(1)}, bf16[256,256]{1,0:T(8,128)(2,1)S(1)}, bf16[256,128]{1,0:T(8,128)(2,1)S(1)}, f32[256,1]{1,0:T(8,128)S(1)}) custom-call(bf16[256,128]{1,0:T(8,128)(2,1)S(1)} %residual.4._.kept, s32[3,1,4,3]{3,2,1,0:T(4,128)S(1)} %copy.11.rcols, bf16[3,1,4,3,64,64]{5,4,3,2,1,0:T(8,128)(2,1)S(1)} %copy-done.2, ...), custom_call_target="tpu_custom_call" | custom-call | bytes 852352 | tf_op jit(solution)/shard_map/operators/pallas_call | solution.py:48
  20.2 0.2 join.5
  20.4 0.2 collective-permute-start.6
  20.7 1.2 %collective-permute-start.7 = (bf16[64,128]{1,0:T(8,128)(2,1)S(1)}, bf16[64,128]{1,0:T(8,128)(2,1)S(1)}, u32[]{:S(2)}, u32[]{:S(2)}) collective-permute-start(bf16[64,128]{1,0:T(8,128)(2,1)S(1)} %get-tuple-element.64), channel_id=1, source_target_pairs={{0,3},{1,2},{2,1},{3,0},{4,7},{5,6},{6,5},{7,4},{8,11},{9,10},{10,... | collective-permute-start | bytes 49160 | tf_op jit(solution)/shard_map/ppermute | solution.py:254
  21.9 0.2 join.7
  22.2 0.2 collective-permute-start.12
  22.4 1.3 %collective-permute-start.13 = (bf16[64,128]{1,0:T(8,128)(2,1)S(1)}, bf16[64,128]{1,0:T(8,128)(2,1)S(1)}, u32[]{:S(2)}, u32[]{:S(2)}) collective-permute-start(bf16[64,128]{1,0:T(8,128)(2,1)S(1)} %get-tuple-element.75), channel_id=1, source_target_pairs={{0,3},{1,2},{2,1},{3,0},{4,7},{5,6},{6,5},{7,4},{8,11},{9,10},{10,... | collective-permute-start | bytes 49160 | tf_op jit(solution)/shard_map/ppermute | solution.py:254
  23.6 0.2 collective-permute-done.7.outer
  23.8 0.2 residual.5._.kept
  24.1 2.7 %collective-permute-start.19 = (bf16[256,128]{1,0:T(8,128)(2,1)S(1)}, bf16[256,128]{1,0:T(8,128)(2,1)S(1)}, u32[]{:S(2)}, u32[]{:S(2)}) collective-permute-start(bf16[256,128]{1,0:T(8,128)(2,1)S(1)} %residual.5._.kept), channel_id=1, source_target_pairs={{0,16},{4,20},{8,24},{12,28},{16,0},{20,4},{24,8},{28,12},{1,17},{... | collective-permute-start | bytes 196616 | tf_op jit(solution)/shard_map/ppermute | solution.py:248
  26.7 0.2 residual.7.kept
  26.9 1.5 %collective-permute-start.14 = (bf16[256,128]{1,0:T(8,128)(2,1)S(1)}, bf16[256,128]{1,0:T(8,128)(2,1)S(1)}, u32[]{:S(2)}, u32[]{:S(2)}) collective-permute-start(bf16[256,128]{1,0:T(8,128)(2,1)S(1)} %residual.7.kept), channel_id=1, source_target_pairs={{0,16},{4,20},{8,24},{12,28},{16,0},{20,4},{24,8},{28,12},{1,17},{... | collective-permute-start | bytes 196616 | tf_op jit(solution)/shard_map/ppermute | solution.py:248
  28.6 1.0 %last_operators.1 = (bf16[256,512]{1,0:T(8,128)(2,1)S(1)}, bf16[256,256]{1,0:T(8,128)(2,1)S(1)}, bf16[256,256]{1,0:T(8,128)(2,1)S(1)}, bf16[256,256]{1,0:T(8,128)(2,1)S(1)}) custom-call(bf16[256,128]{1,0:T(8,128)(2,1)S(1)} %residual.5._.kept, s32[3,1,4,3]{3,2,1,0:T(4,128)S(1)} %copy.11.rcols, bf16[3,1,4,3,64,64]{5,4,3,2,1,0:T(8,128)(2,1)S(1)} %copy-done.2, ...), custom_call_target="tpu_custom_call" | custom-call | bytes 950512 | tf_op jit(solution)/shard_map/last_operators/pallas_call | solution.py:48
  29.6 1.3 %collective-permute-done.19.other = bf16[256,128]{1,0:T(8,128)(2,1)S(1)} collective-permute-done((bf16[256,128]{1,0:T(8,128)(2,1)S(1)}, bf16[256,128]{1,0:T(8,128)(2,1)S(1)}, u32[]{:S(2)}, u32[]{:S(2)}) %collective-permute-start.19) | collective-permute-done | bytes 65568 | tf_op jit(solution)/shard_map/ppermute | solution.py:248
  30.9 0.2 last_join.3.refs_0_
  31.1 1.4 %collective-permute-start.20 = (bf16[256,128]{1,0:T(8,128)(2,1)S(1)}, bf16[256,128]{1,0:T(8,128)(2,1)S(1)}, u32[]{:S(2)}, u32[]{:S(2)}) collective-permute-start(bf16[256,128]{1,0:T(8,128)(2,1)S(1)} %last_join.3.refs_0_), channel_id=1, source_target_pairs={{0,2},{1,3},{2,0},{3,1},{4,6},{5,7},{6,4},{7,5},{8,10},{9,11},{10,... | collective-permute-start | bytes 196616 | tf_op jit(solution)/shard_map/ppermute | solution.py:248
  32.5 1.1 %collective-permute-done.14.other = bf16[256,128]{1,0:T(8,128)(2,1)S(1)} collective-permute-done((bf16[256,128]{1,0:T(8,128)(2,1)S(1)}, bf16[256,128]{1,0:T(8,128)(2,1)S(1)}, u32[]{:S(2)}, u32[]{:S(2)}) %collective-permute-start.14) | collective-permute-done | bytes 65568 | tf_op jit(solution)/shard_map/ppermute | solution.py:248
  33.6 0.2 last_join.2.refs_0_
  33.8 1.4 %collective-permute-start.15 = (bf16[256,128]{1,0:T(8,128)(2,1)S(1)}, bf16[256,128]{1,0:T(8,128)(2,1)S(1)}, u32[]{:S(2)}, u32[]{:S(2)}) collective-permute-start(bf16[256,128]{1,0:T(8,128)(2,1)S(1)} %last_join.2.refs_0_), channel_id=1, source_target_pairs={{0,2},{1,3},{2,0},{3,1},{4,6},{5,7},{6,4},{7,5},{8,10},{9,11},{10,... | collective-permute-start | bytes 196616 | tf_op jit(solution)/shard_map/ppermute | solution.py:248
  35.2 0.6 %collective-permute-done.20.refs_1_ = bf16[256,128]{1,0:T(8,128)(2,1)S(1)} collective-permute-done((bf16[256,128]{1,0:T(8,128)(2,1)S(1)}, bf16[256,128]{1,0:T(8,128)(2,1)S(1)}, u32[]{:S(2)}, u32[]{:S(2)}) %collective-permute-start.20) | collective-permute-done | bytes 65568 | tf_op jit(solution)/shard_map/ppermute | solution.py:248
  35.8 0.5 %collective-permute-start.16 = (bf16[256,128]{1,0:T(8,128)(2,1)S(1)}, bf16[256,128]{1,0:T(8,128)(2,1)S(1)}, u32[]{:S(2)}, u32[]{:S(2)}) collective-permute-start(bf16[256,128]{1,0:T(8,128)(2,1)S(1)} %last_join.2.refs_0_), channel_id=1, source_target_pairs={{0,1},{1,0},{2,3},{3,2},{4,5},{5,4},{6,7},{7,6},{8,9},{9,8},{10,11... | collective-permute-start | bytes 196616 | tf_op jit(solution)/shard_map/ppermute | solution.py:248
  36.3 1.8 %collective-permute-done.15.refs_1_ = bf16[256,128]{1,0:T(8,128)(2,1)S(1)} collective-permute-done((bf16[256,128]{1,0:T(8,128)(2,1)S(1)}, bf16[256,128]{1,0:T(8,128)(2,1)S(1)}, u32[]{:S(2)}, u32[]{:S(2)}) %collective-permute-start.15) | collective-permute-done | bytes 65568 | tf_op jit(solution)/shard_map/ppermute | solution.py:248
  38.1 1.0 %up.3.refs_0_ = bf16[256,128]{1,0:T(8,128)(2,1)S(1)} custom-call(bf16[256,1024]{1,0:T(8,128)(2,1)S(1)} %copy-done.4, bf16[256,128]{1,0:T(8,128)(2,1)S(1)} %last_join.3.refs_0_, bf16[256,128]{1,0:T(8,128)(2,1)S(1)} %collective-permute-done.20.refs_1_, bf16[256,128]{1,0:T(8,128)(2,1)S(1)} %collective-permute-done.21.refs_2_, ...), custom_call_target="tpu_custom_call" | custom-call | flops 134217728 | bytes 1574912 | tf_op jit(solution)/shard_map/up/pallas_call | solution.py:48
  39.2 2.0 %collective-permute-start.23 = (bf16[256,128]{1,0:T(8,128)(2,1)S(1)}, bf16[256,128]{1,0:T(8,128)(2,1)S(1)}, u32[]{:S(2)}, u32[]{:S(2)}) collective-permute-start(bf16[256,128]{1,0:T(8,128)(2,1)S(1)} %up.3.refs_0_), channel_id=1, source_target_pairs={{0,4},{4,0},{8,12},{12,8},{16,20},{20,16},{24,28},{28,24},{1,5},{5... | collective-permute-start | bytes 196616 | tf_op jit(solution)/shard_map/ppermute | solution.py:248
  41.2 1.0 %up.2.refs_1_ = bf16[256,128]{1,0:T(8,128)(2,1)S(1)} custom-call(bf16[256,1024]{1,0:T(8,128)(2,1)S(1)} %copy-done.4, bf16[256,128]{1,0:T(8,128)(2,1)S(1)} %last_join.2.refs_0_, bf16[256,128]{1,0:T(8,128)(2,1)S(1)} %collective-permute-done.15.refs_1_, bf16[256,128]{1,0:T(8,128)(2,1)S(1)} %collective-permute-done.16.refs_2_, ...), custom_call_target="tpu_custom_call" | custom-call | flops 134217728 | bytes 1574912 | tf_op jit(solution)/shard_map/up/pallas_call | solution.py:48
  42.4 1.1 %last_raise.3.refs_5_ = f32[1,256,512]{2,1,0:T(8,128)} custom-call(bf16[256,128]{1,0:T(8,128)(2,1)S(1)} %up.3.refs_0_, bf16[256,128]{1,0:T(8,128)(2,1)S(1)} %up.2.refs_1_, f32[1,256,512]{2,1,0:T(8,128)S(1)} %copy-done.1, f32[256,1]{1,0:T(8,128)S(1)} %get-tuple-element.78.refs_3_.refs_2_, bf16[256,256]{1,0:T(8,128)(2,1)S(1)} %get-tuple-element.79.refs_4_.refs_3_, ...), custom_call_target="tpu_custom_call" | custom-call | flops 67108864 | bytes 918528 | tf_op jit(solution)/shard_map/last_raise/pallas_call | solution.py:48
  43.6 0.4 collective-permute-done.23.refs_0_
  44.0 1.1 %last_raise.4.refs_5_ = f32[1,256,512]{2,1,0:T(8,128)} custom-call(bf16[256,128]{1,0:T(8,128)(2,1)S(1)} %collective-permute-done.23.refs_0_, f32[1,256,512]{2,1,0:T(8,128)S(1)} %copy-done.1, f32[256,1]{1,0:T(8,128)S(1)} %get-tuple-element.78.refs_3_.refs_2_, bf16[256,256]{1,0:T(8,128)(2,1)S(1)} %get-tuple-element.79.refs_4_.refs_3_, ...), custom_call_target="tpu_custom_call", output_to_operand_aliasing={{}: (5, {})} | custom-call | flops 33554432 | bytes 1377280 | tf_op jit(solution)/shard_map/last_raise/pallas_call | solution.py:48
  45.0 1.6 %collective-permute-done.18.refs_0_ = bf16[256,128]{1,0:T(8,128)(2,1)S(1)} collective-permute-done((bf16[256,128]{1,0:T(8,128)(2,1)S(1)}, bf16[256,128]{1,0:T(8,128)(2,1)S(1)}, u32[]{:S(2)}, u32[]{:S(2)}) %collective-permute-start.18) | collective-permute-done | bytes 65568 | tf_op jit(solution)/shard_map/ppermute | solution.py:248
  46.6 1.1 %last_raise.5 = f32[1,256,512]{2,1,0:T(8,128)} custom-call(bf16[256,128]{1,0:T(8,128)(2,1)S(1)} %collective-permute-done.18.refs_0_, f32[1,256,512]{2,1,0:T(8,128)S(1)} %copy-done.1, f32[256,1]{1,0:T(8,128)S(1)} %get-tuple-element.78.refs_3_.refs_2_, bf16[256,256]{1,0:T(8,128)(2,1)S(1)} %get-tuple-element.79.refs_4_.refs_3_, ...), custom_call_target="tpu_custom_call", output_to_operand_aliasing={{}: (5, {})} | custom-call | flops 33554432 | bytes 1377280 | tf_op jit(solution)/shard_map/last_raise/pallas_call | solution.py:48
  (42 shorter events, 1.1 us)
Async XLA Ops:
  0.0 4.4 %copy-start.1 = (f32[1,256,512]{2,1,0:T(8,128)S(1)}, f32[1,256,512]{2,1,0:T(8,128)}, u32[]{:S(2)}) copy-start(f32[1,256,512]{2,1,0:T(8,128)} %refs_1_.5) | copy-start | bytes 1572868
  0.0 4.4 %copy-start = (bf16[3,1,4,5,64,64]{5,4,3,2,1,0:T(8,128)(2,1)S(1)}, bf16[3,1,4,5,64,64]{5,4,3,2,1,0:T(8,128)(2,1)}, u32[]{:S(2)}) copy-start(bf16[3,1,4,5,64,64]{5,4,3,2,1,0:T(8,128)(2,1)} %blocks.7) | copy-start | bytes 1474564
  1.3 4.9 %collective-permute-start.1 = (bf16[64,512]{1,0:T(8,128)(2,1)S(1)}, bf16[64,512]{1,0:T(8,128)(2,1)S(1)}, u32[]{:S(2)}, u32[]{:S(2)}) collective-permute-start(bf16[64,512]{1,0:T(8,128)(2,1)S(1)} %get-tuple-element.46), channel_id=1, source_target_pairs={{0,3},{1,2},{2,1},{3,0},{4,7},{5,6},{6,5},{7,4},{8,11},{9,10},{10,... | collective-permute-start | bytes 196616 | tf_op jit(solution)/shard_map/ppermute | solution.py:254
  3.7 2.5 %collective-permute-start = (bf16[64,512]{1,0:T(8,128)(2,1)S(1)}, bf16[64,512]{1,0:T(8,128)(2,1)S(1)}, u32[]{:S(2)}, u32[]{:S(2)}) collective-permute-start(bf16[64,512]{1,0:T(8,128)(2,1)S(1)} %get-tuple-element.43._), channel_id=1, source_target_pairs={{0,1},{1,0},{2,3},{3,2},{4,5},{5,4},{6,7},{7,6},{8,9},{9,8},{10,11... | collective-permute-start | bytes 196616 | tf_op jit(solution)/shard_map/ppermute | solution.py:248
  4.4 0.7 %copy-start.5 = (s32[3,1,4,5]{3,2,1,0:T(4,128)S(1)}, s32[3,1,4,5]{3,2,1,0:T(4,128)}, u32[]{:S(2)}) copy-start(s32[3,1,4,5]{3,2,1,0:T(4,128)} %cols.5) | copy-start | bytes 724
  6.2 3.5 %copy-start.2 = (bf16[3,1,4,3,64,64]{5,4,3,2,1,0:T(8,128)(2,1)S(1)}, bf16[3,1,4,3,64,64]{5,4,3,2,1,0:T(8,128)(2,1)}, u32[]{:S(2)}) copy-start(bf16[3,1,4,3,64,64]{5,4,3,2,1,0:T(8,128)(2,1)} %rblocks.5) | copy-start | bytes 884740
  6.4 4.9 %collective-permute-start.2 = (bf16[256,128]{1,0:T(8,128)(2,1)S(1)}, bf16[256,128]{1,0:T(8,128)(2,1)S(1)}, u32[]{:S(2)}, u32[]{:S(2)}) collective-permute-start(bf16[256,128]{1,0:T(8,128)(2,1)S(1)} %get-tuple-element.49), channel_id=1, source_target_pairs={{0,4},{4,0},{8,12},{12,8},{16,20},{20,16},{24,28},{28,24},{1,5},{5... | collective-permute-start | bytes 196616 | tf_op jit(solution)/shard_map/ppermute | solution.py:248
  8.9 0.7 %copy-start.7 = (s32[3,1,4,3]{2,1,3,0:T(1,128)S(1)}, s32[3,1,4,3]{2,1,3,0:T(1,128)}, u32[]{:S(2)}) copy-start(s32[3,1,4,3]{2,1,3,0:T(1,128)} %param.11) | copy-start | bytes 436
  9.1 0.7 %copy-start.6 = (s32[3,1,4,5]{3,2,1,0:T(4,128)S(1)}, s32[3,1,4,5]{3,2,1,0:T(4,128)}, u32[]{:S(2)}) copy-start(s32[3,1,4,5]{3,2,1,0:T(4,128)} %cols.5) | copy-start | bytes 724
  9.1 4.6 %collective-permute-start.8 = (bf16[256,128]{1,0:T(8,128)(2,1)S(1)}, bf16[256,128]{1,0:T(8,128)(2,1)S(1)}, u32[]{:S(2)}, u32[]{:S(2)}) collective-permute-start(bf16[256,128]{1,0:T(8,128)(2,1)S(1)} %get-tuple-element.67), channel_id=1, source_target_pairs={{0,4},{4,0},{8,12},{12,8},{16,20},{20,16},{24,28},{28,24},{1,5},{5... | collective-permute-start | bytes 196616 | tf_op jit(solution)/shard_map/ppermute | solution.py:248
  11.5 3.9 %collective-permute-start.3 = (bf16[64,128]{1,0:T(8,128)(2,1)S(1)}, bf16[64,128]{1,0:T(8,128)(2,1)S(1)}, u32[]{:S(2)}, u32[]{:S(2)}) collective-permute-start(bf16[64,128]{1,0:T(8,128)(2,1)S(1)} %get-tuple-element.55), channel_id=1, source_target_pairs={{0,1},{1,0},{2,3},{3,2},{4,5},{5,4},{6,7},{7,6},{8,9},{9,8},{10,11... | collective-permute-start | bytes 49160 | tf_op jit(solution)/shard_map/ppermute | solution.py:248
  11.6 3.8 %collective-permute-start.4 = (bf16[64,128]{1,0:T(8,128)(2,1)S(1)}, bf16[64,128]{1,0:T(8,128)(2,1)S(1)}, u32[]{:S(2)}, u32[]{:S(2)}) collective-permute-start(bf16[64,128]{1,0:T(8,128)(2,1)S(1)} %get-tuple-element.56), channel_id=1, source_target_pairs={{0,3},{1,2},{2,1},{3,0},{4,7},{5,6},{6,5},{7,4},{8,11},{9,10},{10,... | collective-permute-start | bytes 49160 | tf_op jit(solution)/shard_map/ppermute | solution.py:254
  13.9 3.3 %collective-permute-start.9 = (bf16[64,128]{1,0:T(8,128)(2,1)S(1)}, bf16[64,128]{1,0:T(8,128)(2,1)S(1)}, u32[]{:S(2)}, u32[]{:S(2)}) collective-permute-start(bf16[64,128]{1,0:T(8,128)(2,1)S(1)} %get-tuple-element.70), channel_id=1, source_target_pairs={{0,1},{1,0},{2,3},{3,2},{4,5},{5,4},{6,7},{7,6},{8,9},{9,8},{10,11... | collective-permute-start | bytes 49160 | tf_op jit(solution)/shard_map/ppermute | solution.py:248
  14.1 3.2 %collective-permute-start.10 = (bf16[64,128]{1,0:T(8,128)(2,1)S(1)}, bf16[64,128]{1,0:T(8,128)(2,1)S(1)}, u32[]{:S(2)}, u32[]{:S(2)}) collective-permute-start(bf16[64,128]{1,0:T(8,128)(2,1)S(1)} %get-tuple-element.71), channel_id=1, source_target_pairs={{0,3},{1,2},{2,1},{3,0},{4,7},{5,6},{6,5},{7,4},{8,11},{9,10},{10,... | collective-permute-start | bytes 49160 | tf_op jit(solution)/shard_map/ppermute | solution.py:254
  15.6 4.6 %collective-permute-start.5 = (bf16[256,128]{1,0:T(8,128)(2,1)S(1)}, bf16[256,128]{1,0:T(8,128)(2,1)S(1)}, u32[]{:S(2)}, u32[]{:S(2)}) collective-permute-start(bf16[256,128]{1,0:T(8,128)(2,1)S(1)} %residual.4._.kept), channel_id=1, source_target_pairs={{0,8},{4,12},{8,0},{12,4},{16,24},{20,28},{24,16},{28,20},{1,9},{5... | collective-permute-start | bytes 196616 | tf_op jit(solution)/shard_map/ppermute | solution.py:248
  17.4 4.5 %collective-permute-start.11 = (bf16[256,128]{1,0:T(8,128)(2,1)S(1)}, bf16[256,128]{1,0:T(8,128)(2,1)S(1)}, u32[]{:S(2)}, u32[]{:S(2)}) collective-permute-start(bf16[256,128]{1,0:T(8,128)(2,1)S(1)} %residual.6.kept), channel_id=1, source_target_pairs={{0,8},{4,12},{8,0},{12,4},{16,24},{20,28},{24,16},{28,20},{1,9},{5... | collective-permute-start | bytes 196616 | tf_op jit(solution)/shard_map/ppermute | solution.py:248
  20.4 3.2 %collective-permute-start.6 = (bf16[64,128]{1,0:T(8,128)(2,1)S(1)}, bf16[64,128]{1,0:T(8,128)(2,1)S(1)}, u32[]{:S(2)}, u32[]{:S(2)}) collective-permute-start(bf16[64,128]{1,0:T(8,128)(2,1)S(1)} %get-tuple-element.63), channel_id=1, source_target_pairs={{0,1},{1,0},{2,3},{3,2},{4,5},{5,4},{6,7},{7,6},{8,9},{9,8},{10,11... | collective-permute-start | bytes 49160 | tf_op jit(solution)/shard_map/ppermute | solution.py:248
  20.7 3.2 %collective-permute-start.7 = (bf16[64,128]{1,0:T(8,128)(2,1)S(1)}, bf16[64,128]{1,0:T(8,128)(2,1)S(1)}, u32[]{:S(2)}, u32[]{:S(2)}) collective-permute-start(bf16[64,128]{1,0:T(8,128)(2,1)S(1)} %get-tuple-element.64), channel_id=1, source_target_pairs={{0,3},{1,2},{2,1},{3,0},{4,7},{5,6},{6,5},{7,4},{8,11},{9,10},{10,... | collective-permute-start | bytes 49160 | tf_op jit(solution)/shard_map/ppermute | solution.py:254
  22.2 4.5 %collective-permute-start.12 = (bf16[64,128]{1,0:T(8,128)(2,1)S(1)}, bf16[64,128]{1,0:T(8,128)(2,1)S(1)}, u32[]{:S(2)}, u32[]{:S(2)}) collective-permute-start(bf16[64,128]{1,0:T(8,128)(2,1)S(1)} %get-tuple-element.74), channel_id=1, source_target_pairs={{0,1},{1,0},{2,3},{3,2},{4,5},{5,4},{6,7},{7,6},{8,9},{9,8},{10,11... | collective-permute-start | bytes 49160 | tf_op jit(solution)/shard_map/ppermute | solution.py:248
  22.4 4.3 %collective-permute-start.13 = (bf16[64,128]{1,0:T(8,128)(2,1)S(1)}, bf16[64,128]{1,0:T(8,128)(2,1)S(1)}, u32[]{:S(2)}, u32[]{:S(2)}) collective-permute-start(bf16[64,128]{1,0:T(8,128)(2,1)S(1)} %get-tuple-element.75), channel_id=1, source_target_pairs={{0,3},{1,2},{2,1},{3,0},{4,7},{5,6},{6,5},{7,4},{8,11},{9,10},{10,... | collective-permute-start | bytes 49160 | tf_op jit(solution)/shard_map/ppermute | solution.py:254
  23.8 4.7 %copy-start.3 = (bf16[3,1,4,2,64,64]{5,4,3,2,1,0:T(8,128)(2,1)S(1)}, bf16[3,1,4,2,64,64]{5,4,3,2,1,0:T(8,128)(2,1)}, u32[]{:S(2)}) copy-start(bf16[3,1,4,2,64,64]{5,4,3,2,1,0:T(8,128)(2,1)} %refs_2_.2) | copy-start | bytes 589828
  24.1 6.9 %collective-permute-start.19 = (bf16[256,128]{1,0:T(8,128)(2,1)S(1)}, bf16[256,128]{1,0:T(8,128)(2,1)S(1)}, u32[]{:S(2)}, u32[]{:S(2)}) collective-permute-start(bf16[256,128]{1,0:T(8,128)(2,1)S(1)} %residual.5._.kept), channel_id=1, source_target_pairs={{0,16},{4,20},{8,24},{12,28},{16,0},{20,4},{24,8},{28,12},{1,17},{... | collective-permute-start | bytes 196616 | tf_op jit(solution)/shard_map/ppermute | solution.py:248
  26.7 1.7 %copy-start.8 = (s32[3,1,4,2]{2,3,1,0:T(2,128)S(1)}, s32[3,1,4,2]{2,3,1,0:T(2,128)}, u32[]{:S(2)}) copy-start(s32[3,1,4,2]{2,3,1,0:T(2,128)} %param.13) | copy-start | bytes 292
  26.9 6.6 %collective-permute-start.14 = (bf16[256,128]{1,0:T(8,128)(2,1)S(1)}, bf16[256,128]{1,0:T(8,128)(2,1)S(1)}, u32[]{:S(2)}, u32[]{:S(2)}) collective-permute-start(bf16[256,128]{1,0:T(8,128)(2,1)S(1)} %residual.7.kept), channel_id=1, source_target_pairs={{0,16},{4,20},{8,24},{12,28},{16,0},{20,4},{24,8},{28,12},{1,17},{... | collective-permute-start | bytes 196616 | tf_op jit(solution)/shard_map/ppermute | solution.py:248
  29.6 8.6 %copy-start.4 = (bf16[256,1024]{1,0:T(8,128)(2,1)S(1)}, bf16[256,1024]{1,0:T(8,128)(2,1)}, u32[]{:S(2)}) copy-start(bf16[256,1024]{1,0:T(8,128)(2,1)} %inverse.3) | copy-start | bytes 1572868
  31.1 4.7 %collective-permute-start.20 = (bf16[256,128]{1,0:T(8,128)(2,1)S(1)}, bf16[256,128]{1,0:T(8,128)(2,1)S(1)}, u32[]{:S(2)}, u32[]{:S(2)}) collective-permute-start(bf16[256,128]{1,0:T(8,128)(2,1)S(1)} %last_join.3.refs_0_), channel_id=1, source_target_pairs={{0,2},{1,3},{2,0},{3,1},{4,6},{5,7},{6,4},{7,5},{8,10},{9,11},{10,... | collective-permute-start | bytes 196616 | tf_op jit(solution)/shard_map/ppermute | solution.py:248
  33.8 4.3 %collective-permute-start.15 = (bf16[256,128]{1,0:T(8,128)(2,1)S(1)}, bf16[256,128]{1,0:T(8,128)(2,1)S(1)}, u32[]{:S(2)}, u32[]{:S(2)}) collective-permute-start(bf16[256,128]{1,0:T(8,128)(2,1)S(1)} %last_join.2.refs_0_), channel_id=1, source_target_pairs={{0,2},{1,3},{2,0},{3,1},{4,6},{5,7},{6,4},{7,5},{8,10},{9,11},{10,... | collective-permute-start | bytes 196616 | tf_op jit(solution)/shard_map/ppermute | solution.py:248
  35.2 3.0 %collective-permute-start.21 = (bf16[256,128]{1,0:T(8,128)(2,1)S(1)}, bf16[256,128]{1,0:T(8,128)(2,1)S(1)}, u32[]{:S(2)}, u32[]{:S(2)}) collective-permute-start(bf16[256,128]{1,0:T(8,128)(2,1)S(1)} %last_join.3.refs_0_), channel_id=1, source_target_pairs={{0,1},{1,0},{2,3},{3,2},{4,5},{5,4},{6,7},{7,6},{8,9},{9,8},{10,11... | collective-permute-start | bytes 196616 | tf_op jit(solution)/shard_map/ppermute | solution.py:248
  35.8 2.3 %collective-permute-start.22 = (bf16[256,128]{1,0:T(8,128)(2,1)S(1)}, bf16[256,128]{1,0:T(8,128)(2,1)S(1)}, u32[]{:S(2)}, u32[]{:S(2)}) collective-permute-start(bf16[256,128]{1,0:T(8,128)(2,1)S(1)} %collective-permute-done.20.refs_1_), channel_id=1, source_target_pairs={{0,1},{1,0},{2,3},{3,2},{4,5},{5,4},{6,7},{7,6},{8,9},{9,8},{10,11... | collective-permute-start | bytes 196616 | tf_op jit(solution)/shard_map/ppermute | solution.py:248
  35.8 5.4 %collective-permute-start.16 = (bf16[256,128]{1,0:T(8,128)(2,1)S(1)}, bf16[256,128]{1,0:T(8,128)(2,1)S(1)}, u32[]{:S(2)}, u32[]{:S(2)}) collective-permute-start(bf16[256,128]{1,0:T(8,128)(2,1)S(1)} %last_join.2.refs_0_), channel_id=1, source_target_pairs={{0,1},{1,0},{2,3},{3,2},{4,5},{5,4},{6,7},{7,6},{8,9},{9,8},{10,11... | collective-permute-start | bytes 196616 | tf_op jit(solution)/shard_map/ppermute | solution.py:248
  38.1 3.1 %collective-permute-start.17 = (bf16[256,128]{1,0:T(8,128)(2,1)S(1)}, bf16[256,128]{1,0:T(8,128)(2,1)S(1)}, u32[]{:S(2)}, u32[]{:S(2)}) collective-permute-start(bf16[256,128]{1,0:T(8,128)(2,1)S(1)} %collective-permute-done.15.refs_1_), channel_id=1, source_target_pairs={{0,1},{1,0},{2,3},{3,2},{4,5},{5,4},{6,7},{7,6},{8,9},{9,8},{10,11... | collective-permute-start | bytes 196616 | tf_op jit(solution)/shard_map/ppermute | solution.py:248
  39.2 4.8 %collective-permute-start.23 = (bf16[256,128]{1,0:T(8,128)(2,1)S(1)}, bf16[256,128]{1,0:T(8,128)(2,1)S(1)}, u32[]{:S(2)}, u32[]{:S(2)}) collective-permute-start(bf16[256,128]{1,0:T(8,128)(2,1)S(1)} %up.3.refs_0_), channel_id=1, source_target_pairs={{0,4},{4,0},{8,12},{12,8},{16,20},{20,16},{24,28},{28,24},{1,5},{5... | collective-permute-start | bytes 196616 | tf_op jit(solution)/shard_map/ppermute | solution.py:248
  42.3 4.3 %collective-permute-start.18 = (bf16[256,128]{1,0:T(8,128)(2,1)S(1)}, bf16[256,128]{1,0:T(8,128)(2,1)S(1)}, u32[]{:S(2)}, u32[]{:S(2)}) collective-permute-start(bf16[256,128]{1,0:T(8,128)(2,1)S(1)} %up.2.refs_1_), channel_id=1, source_target_pairs={{0,4},{4,0},{8,12},{12,8},{16,20},{20,16},{24,28},{28,24},{1,5},{5... | collective-permute-start | bytes 196616 | tf_op jit(solution)/shard_map/ppermute | solution.py:248

commit v5 on v4

--- a/solution.py
+++ b/solution.py
@@ -12,7 +12,6 @@
 f32 = jnp.float32
 bf16 = jnp.bfloat16
 grant = 12 * 1024 * 1024
-chunk_width = 128
 
 
 def matmul(a, b):
@@ -142,10 +141,12 @@
     put_ends(first, last, inner_ref, outer_ref)
 
 
-def first_local_kernel(rhs, _, cols, blocks, rest, local, rim, scale):
+def first_local_kernel(rhs, _, cols, blocks, rest, base, local, rim, scale):
     assemble_galerkin(0, cols, blocks, local, rim, scale)
-    smoothed = (rhs[0] * (relax_down * scale[...])).astype(bf16)
-    rest[...] = rhs[0] - matmul(local[...], smoothed)
+    smoothed = rhs[0] * (relax_down * scale[...])
+    left = rhs[0] - matmul(local[...], smoothed.astype(bf16))
+    rest[...] = left
+    base[...] = smoothed + (relax_up * scale[...]) * left
 
 
 def bit_of(level_idx):
@@ -155,21 +156,23 @@
 def lanes_of(place, width):
     start = 0
     for level_idx, flip, step in place:
-        start = start + (bit_of(level_idx) ^ flip if level_idx >= 0 else flip) * step
+        start = start + (bit_of(level_idx) ^ flip) * step
     return pl.ds(pl.multiple_of(start, width), width)
 
 
-def first_residual_kernel(places, rest, rim, inner, outer, *refs):
+def first_residual_kernel(places, rest, rim, outer, inner, *refs):
     for ref, place in zip(refs, places):
         lanes = lanes_of(place, ref.shape[1])
         rims = jnp.concatenate([inner[:, lanes], outer[:, lanes]], axis=0)
         ref[...] = (rest[:, lanes] - matmul(rim[...], rims)).astype(bf16)
 
 
-def residual_kernel(rhs, local, smoothed, rim, inner, outer, out):
+def residual_kernel(rhs, smoothed, scale, local, rim, outer, inner, _, out, base):
     rims = jnp.concatenate([inner[...], outer[...]], axis=0)
-    applied = matmul(local[...], smoothed[...]) + matmul(rim[...], rims)
-    out[...] = (rhs[...] - applied).astype(bf16)
+    left = rhs[...] - matmul(local[...], smoothed[...])
+    out[...] = (left - matmul(rim[...], rims)).astype(bf16)
+    made = rhs[...] * (relax_down * scale[...]) + (relax_up * scale[...]) * left
+    base[...] = made.astype(base.dtype)
 
 
 def operators_kernel(level_idx, _, rcols, rblocks, cols, blocks, rmat, local, rim, scale):
@@ -177,10 +180,44 @@
     assemble_galerkin(level_idx + 1, cols, blocks, local, rim, scale)
 
 
-def last_operators_kernel(level_idx, levels, _, rcols, rblocks, pcols, *refs):
-    assemble_restrict(level_idx, rcols, rblocks, refs[levels])
-    for idx, blocks, out in zip(range(levels), refs[:levels], refs[levels + 1 :]):
-        assemble_prolong(idx, pcols, blocks, out)
+def raising(level_idx, pcols, blocks, local, scale, held):
+    assemble_prolong(level_idx, pcols, blocks, held)
+    applied = matmul(local[...], held[...])
+    return (held[...].astype(f32) - (relax_up * scale[...]) * applied).astype(bf16)
+
+
+def coarse_operators_kernel(level_idx, first, levels, *refs):
+    _, rcols, rblocks, pcols, inverse, one, two, *refs = refs
+    places = range(first, levels)
+    blocks, refs = refs[: len(places)], refs[len(places) :]
+    pairs, refs = refs[: 2 * len(places)], refs[2 * len(places) :]
+    rmat, coarse, bases, *up, held = refs
+    width = one.shape[1]
+    bases[:, :width] = one[...]
+    bases[:, width:] = two[...]
+    assemble_restrict(level_idx, rcols, rblocks, rmat)
+    for idx in places:
+        slot = idx - first
+        made = raising(idx, pcols, blocks[slot], pairs[2 * slot + 1], pairs[2 * slot], held)
+        if idx == levels - 1:
+            coarse[...] = matmul(made, inverse[...]).astype(bf16)
+        else:
+            up[slot][...] = made
+
+
+def fine_operators_kernel(
+    places, _, pcols, blocks_0, blocks_1, scale_0, local_0, scale_1, local_1,
+    base, near, far, both, total, held,
+):
+    lower = raising(0, pcols, blocks_0, local_0, scale_0, held)
+    upper = raising(1, pcols, blocks_1, local_1, scale_1, held)
+    both[...] = matmul(lower, upper).astype(bf16)
+    width = near.shape[1] // 2
+    for slot, place in enumerate(places):
+        source = near if slot < 2 else far
+        lanes = lanes_of(place, width)
+        columns = pl.ds(slot % 2 * width, width)
+        total[:, lanes] = base[:, lanes] + matmul(lower, source[:, columns])
 
 
 def restricted(level_idx, rmat, kept, other):
@@ -210,32 +247,25 @@
     return matmul(inverse[:, pl.ds(pl.multiple_of(piece * depth, depth), depth)], part[...])
 
 
-def raise_level(coarse, rhs, scale, local, pmat):
-    updated = rhs * (relax_down * scale) + matmul(pmat, coarse)
-    applied = matmul(local, updated.astype(bf16))
-    return updated + (relax_up * scale) * (rhs - applied)
-
-
-def up_kernel(offsets, depth, inverse, *refs):
-    value = None
-    for part, offset in zip(refs, offsets):
-        term = inverse_part(inverse, part, offset)
-        value = term if value is None else value + term
-    refs = refs[len(offsets) :]
-    for step in range(depth):
-        rhs, scale, local, pmat = refs[4 * step : 4 * step + 4]
-        value = raise_level(value.astype(bf16), rhs[...], scale[...], local[...], pmat[...])
+def up_kernel(offsets, inverse, *refs):
+    parts, refs = refs[: len(offsets)], refs[len(offsets) :]
+    value = refs[0][...]
+    for part, offset in zip(parts, offsets):
+        value = value + inverse_part(inverse, part, offset)
+    for step in range((len(refs) - 2) // 2):
+        base, up = refs[1 + 2 * step : 3 + 2 * step]
+        value = base[...] + matmul(up[...], value.astype(bf16))
     refs[-1][...] = value.astype(bf16)
 
 
-def last_raise_kernel(places, *refs):
+def output_kernel(places, *refs):
     coarse, refs = refs[: len(places)], refs[len(places) :]
-    rhs, scale, local, pmat = refs[:4]
+    total, both = refs[:2]
     out, sems = refs[-2 - len(places)], refs[-1]
     copies = []
     for slot, (place, value, made) in enumerate(zip(places, coarse, refs[-1 - len(places) : -1])):
         lanes = lanes_of(place, value.shape[1])
-        made[...] = raise_level(value[...], rhs[0, :, lanes], scale[...], local[...], pmat[...])
+        made[...] = total[:, lanes] + matmul(both[...], value[...])
         copy = pltpu.make_async_copy(made, out.at[0, :, lanes], sems.at[slot])
         copy.start()
         copies.append(copy)
@@ -270,14 +300,14 @@
     size = galerkin_blocks.shape[-1]
     rows, fields = level_rhs.shape[1:]
     half = fields // 2
-    chunks = range(half // chunk_width)
-    width = half // len(chunks)
+    width = half // 2
     gcols, rcols, pcols = ((c, scalars()) for c in (galerkin_cols, restrict_cols, prolong_cols))
-    operator_shapes = [
-        array((rows, rows), bf16), array((rows, 2 * size), bf16), array((rows, 1), f32)
-    ]
+    square_shape = array((rows, rows), bf16)
+    operator_shapes = [square_shape, array((rows, 2 * size), bf16), array((rows, 1), f32)]
     rmat_shape = array((rows, 2 * rows), bf16)
     chunk_shape = array((rows, width), bf16)
+    real_shape = array((rows, width), f32)
+    held = [pltpu.VMEM((rows, rows), bf16)]
 
     def ends_shape(columns):
         return array((size, columns), bf16)
@@ -288,8 +318,8 @@
     def flops(columns, products=1):
         return 2 * products * rows * rows * columns
 
-    def place_of(chunk, flip):
-        return (0, flip, half), (-1, chunk, width)
+    def place_of(far, given):
+        return (0, far, half), (1, given, width)
 
     ends = run(
         start_kernel, "start", [ends_shape(fields)] * 2,
@@ -300,91 +330,101 @@
         ],
     )
     inner, outer = swap_ends(*ends)
-    rest, local, rim, scale = run(
-        first_local_kernel, "first_local", [array((rows, fields), f32)] + operator_shapes,
+    rest, base, local, rim, scale = run(
+        first_local_kernel, "first_local", [array((rows, fields), f32)] * 2 + operator_shapes,
         [level_rhs, ends[0], gcols, of_level(galerkin_blocks, 0)], flops=flops(fields),
     )
     operators = [(scale, local)]
     sent, kept = [], []
-    for chunk in chunks:
-        places = place_of(chunk, 1), place_of(chunk, 0)
+    for given in (1, 0):
+        places = place_of(1, given), place_of(0, given)
         far, near = run(
             functools.partial(first_residual_kernel, places), "first_residual", [chunk_shape] * 2,
-            [rest, rim, inner, outer],
+            [rest, rim, outer, inner],
         )
         sent.append(far)
         kept.append(near)
-    right_sides = [level_rhs]
-    for level_idx in range(levels):
+    bases = []
+    pieces = lax.axis_size("narrow")
+    for level_idx in range(levels - 1):
         other = [exchange(value, "wide", 1 << level_idx) for value in sent]
-        if level_idx + 1 < levels:
-            rmat, local, rim, scale = run(
-                functools.partial(operators_kernel, level_idx), "operators",
-                [rmat_shape] + operator_shapes,
-                [kept[0], rcols, of_level(restrict_blocks, level_idx),
-                 gcols, of_level(galerkin_blocks, level_idx + 1)],
+        rmat, local, rim, scale = run(
+            functools.partial(operators_kernel, level_idx), "operators",
+            [rmat_shape] + operator_shapes,
+            [sent[0], rcols, of_level(restrict_blocks, level_idx),
+             gcols, of_level(galerkin_blocks, level_idx + 1)],
+        )
+        operators.append((scale, local))
+        joined = []
+        for near, far in zip(kept, other):
+            rhs, smoothed, *ends = run(
+                functools.partial(join_kernel, level_idx), "join",
+                [real_shape, chunk_shape] + [ends_shape(width)] * 2,
+                [rmat, near, far, scale], flops=flops(width, 2),
             )
-            operators.append((scale, local))
-            sent = []
-            sides = []
-            for chunk in chunks:
-                rhs, smoothed, *ends = run(
-                    functools.partial(join_kernel, level_idx), "join",
-                    [array((rows, width), f32), chunk_shape] + [ends_shape(width)] * 2,
-                    [rmat, kept[chunk], other[chunk], scale], flops=flops(width, 2),
-                )
-                inner, outer = swap_ends(*ends)
-                (value,) = run(
-                    residual_kernel, "residual", [chunk_shape],
-                    [rhs, local, smoothed, rim, inner, outer], flops=flops(width, 2),
-                )
-                sides.append(rhs)
-                sent.append(value)
-            kept = sent
-            right_sides.append(sides)
-        else:
-            rmat, *pmats = run(
-                functools.partial(last_operators_kernel, level_idx, levels), "last_operators",
-                [rmat_shape] + operator_shapes[:1] * levels,
-                [kept[0], rcols, of_level(restrict_blocks, level_idx), pcols]
-                + [of_level(prolong_blocks, idx) for idx in range(levels)],
+            inner, outer = swap_ends(*ends)
+            joined.append((rhs, smoothed, scale, local, rim, outer, inner))
+        made = []
+        for operands in joined:
+            value, made_base = run(
+                residual_kernel, "residual",
+                [chunk_shape, chunk_shape if level_idx == 0 else real_shape],
+                [*operands, joined[-1][1]], flops=flops(width, 2),
             )
-            mine = [
-                run(
-                    functools.partial(last_join_kernel, level_idx), "last_join", [chunk_shape],
-                    [rmat, kept[chunk], other[chunk]], flops=flops(width, 2),
-                )[0]
-                for chunk in chunks
-            ]
-    pieces = lax.axis_size("narrow")
+            made.append(value)
+            bases.append(made_base)
+        sent, kept = made[:1], made[-1:]
+    last = levels - 1
+    (other,) = (exchange(value, "wide", 1 << last) for value in sent)
+    rmat, coarse_mat, near_bases, *ups = run(
+        functools.partial(coarse_operators_kernel, last, 2, levels), "coarse_operators",
+        [rmat_shape, array((rows, pieces * rows), bf16), array((rows, half), bf16)]
+        + [square_shape] * (levels - 3),
+        [kept[0], rcols, of_level(restrict_blocks, last), pcols, coarse_inverse, *bases[:2]]
+        + [of_level(prolong_blocks, idx) for idx in range(2, levels)]
+        + [value for pair in operators[2:] for value in pair],
+        flops=flops(rows, 2 * (levels - 2) + pieces), scratch=held,
+    )
+    far_bases = exchange(near_bases, "wide", 1)
+    (mine,) = run(
+        functools.partial(last_join_kernel, last), "last_join", [chunk_shape],
+        [rmat, kept[0], other], flops=flops(width, 2),
+    )
     order = sorted(range(1, pieces), key=lambda o: (bin(o).count("1"), -o))
-    own, far = [], []
-    for chunk in chunks:
-        parts = {0: mine[chunk]}
-        for offset in order:
-            low = offset & -offset
-            parts[offset] = exchange(parts[offset ^ low], "narrow", low)
-        offsets = tuple(parts)
-        operands = [coarse_inverse] + [parts[o] for o in offsets]
-        for level_idx in reversed(range(1, levels)):
-            operands += [right_sides[level_idx][chunk], *operators[level_idx], pmats[level_idx]]
-        (coarse,) = run(
-            functools.partial(up_kernel, offsets, levels - 1), "up", [chunk_shape], operands,
-            flops=flops(width, len(offsets) + 2 * (levels - 1)),
-        )
-        own.append((coarse, place_of(chunk, 0)))
-        far.append((exchange(coarse, "wide", 1), place_of(chunk, 1)))
+    parts = {0: mine}
+    for offset in order:
+        low = offset & -offset
+        parts[offset] = exchange(parts[offset ^ low], "narrow", low)
+    places = [place_of(far, given) for far in (0, 1) for given in (1, 0)]
+    both, total = run(
+        functools.partial(fine_operators_kernel, places), "fine_operators",
+        [square_shape, array((rows, fields), f32)],
+        [mine, pcols, of_level(prolong_blocks, 0), of_level(prolong_blocks, 1),
+         *operators[0], *operators[1], base, near_bases, far_bases],
+        flops=flops(rows, 5), scratch=held,
+    )
+    offsets = tuple(parts)
+    operands = [coarse_mat] + [parts[o] for o in offsets] + [bases[-1]]
+    for idx in reversed(range(2, last)):
+        operands += [bases[idx], ups[idx - 2]]
+    (value,) = run(
+        functools.partial(up_kernel, offsets), "up", [chunk_shape], operands,
+        flops=flops(width, len(offsets) + levels - 3),
+    )
+    gathered = [(value, place_of(0, 0))]
+    for bits in (2, 1, 3):
+        gathered.append((exchange(value, "wide", bits), place_of(bits & 1, bits >> 1)))
     result = None
-    for group in [own] + [[value] for value in far]:
-        operands = [value for value, _ in group] + [level_rhs, *operators[0], pmats[0]]
+    for group in (gathered[:1], gathered[1:3], gathered[3:]):
+        operands = [value for value, _ in group] + [total, both]
         aliases = {}
         if result is not None:
             aliases[len(operands)] = 0
             operands.append(in_hbm(result))
         (result,) = run(
-            functools.partial(last_raise_kernel, tuple(place for _, place in group)),
-            "last_raise", [array((1, rows, fields), f32)], operands,
-            flops=flops(width, 2 * len(group)),
+            functools.partial(output_kernel, tuple(place for _, place in group)),
+            "output", [array((1, rows, fields), f32)], operands,
+            flops=flops(width, len(group)),
             scratch=[pltpu.VMEM((rows, width), f32)] * len(group)
             + [pltpu.SemaphoreType.DMA((len(group),))],
             out_space=pltpu.HBM, aliases=aliases,

time: 47.9 us -> 45.3 us (0.946)
  starting transfers between devices: 25.2 us -> 22 us
  waiting for transfers between devices: 7.44 us -> 9.5 us
  Pallas kernels: 13.4 us -> 11.9 us
    ppermute x5 -> x4, starting transfers between devices: 8.37 us -> 3.33 us  [swap_ends(): outer = lax.ppermute(outer, 'narrow', gaps)]
    ppermute x5 -> x4, waiting for transfers between devices: 0.23 us -> 3.25 us  [swap_ends(): outer = lax.ppermute(outer, 'narrow', gaps)]
    ppermute x19 -> x15, starting transfers between devices: 16.8 us -> 18.7 us  [exchange(): return lax.ppermute(value, axis, [(i, i ^ bit) for i in range(count)])]
    pallas_call x22 -> x19, Pallas kernels: 13.4 us -> 11.9 us  [run(): pl.pallas_call(body, grid=(1,) if windows else (), out_shape=outs, in_spe...]
    ppermute x19 -> x15, waiting for transfers between devices: 7.21 us -> 6.25 us  [exchange(): return lax.ppermute(value, axis, [(i, i ^ bit) for i in range(count)])]
  transfers between devices with their start and end apart: 24 -> 19, of which waited for: 8 -> 8; matrix products, arithmetic and copies ran while one was open for 0% -> 0% of each run, Pallas kernels for 23% -> 20%
where the time goes in v5:
time: 45.3 us; the launch traced here: 45.1 us
  starting transfers between devices  22 us (49%)
  Pallas kernels  11.9 us (26%)
  waiting for transfers between devices  9.5 us (21%)
  local copies, waits for them, and re-layouts  1.41 us (3%)
    ppermute x15, starting transfers between devices, exchange(): return lax.ppermute(value, axis, [(i, i ^ bit) for i in range(count)])  18.7 us
    pallas_call x19, Pallas kernels, run(): pl.pallas_call(body, grid=(1,) if windows else (), out_shape=outs, in_spe...  11.9 us
    ppermute x15, waiting for transfers between devices, exchange(): return lax.ppermute(value, axis, [(i, i ^ bit) for i in range(count)])  6.25 us
    ppermute x4, starting transfers between devices, swap_ends(): outer = lax.ppermute(outer, 'narrow', gaps)  3.33 us
    ppermute x4, waiting for transfers between devices, swap_ends(): outer = lax.ppermute(outer, 'narrow', gaps)  3.25 us
    unnamed x20, local copies, waits for them, and re-layouts  1.41 us
  transfers between devices with their start and end apart: 19, of which 8 were waited for; matrix products, arithmetic and copies ran while one was open for 0% of the time, Pallas kernels for 20%

profile of v5, /device:TPU:0, one launch (start us, length us, event | category | flops | bytes accessed | tf_op | source)
XLA Modules:
  0.0 45.1 jit_solution(2631693453375782470)
XLA Ops:
  0.0 1.2 %start.1 = (bf16[64,512]{1,0:T(8,128)(2,1)S(1)}, bf16[64,512]{1,0:T(8,128)(2,1)S(1)}) custom-call(f32[1,256,512]{2,1,0:T(8,128)} %rhs.3, bf16[3,1,4,5,64,64]{5,4,3,2,1,0:T(8,128)(2,1)} %blocks.7), custom_call_target="tpu_custom_call" | custom-call | bytes 1015808 | tf_op jit(solution)/shard_map/start/pallas_call | solution.py:47
  1.3 2.4 %collective-permute-start = (bf16[64,512]{1,0:T(8,128)(2,1)S(1)}, bf16[64,512]{1,0:T(8,128)(2,1)S(1)}, u32[]{:S(2)}, u32[]{:S(2)}) collective-permute-start(bf16[64,512]{1,0:T(8,128)(2,1)S(1)} %get-tuple-element.50), channel_id=1, source_target_pairs={{0,3},{1,2},{2,1},{3,0},{4,7},{5,6},{6,5},{7,4},{8,11},{9,10},{10,... | collective-permute-start | bytes 196616 | tf_op jit(solution)/shard_map/ppermute | solution.py:284
  3.7 0.7 %collective-permute-start.1 = (bf16[64,512]{1,0:T(8,128)(2,1)S(1)}, bf16[64,512]{1,0:T(8,128)(2,1)S(1)}, u32[]{:S(2)}, u32[]{:S(2)}) collective-permute-start(bf16[64,512]{1,0:T(8,128)(2,1)S(1)} %get-tuple-element.47._), channel_id=1, source_target_pairs={{0,1},{1,0},{2,3},{3,2},{4,5},{5,4},{6,7},{7,6},{8,9},{9,8},{10,11... | collective-permute-start | bytes 196616 | tf_op jit(solution)/shard_map/ppermute | solution.py:278
  4.4 0.7 %copy-done.5 = s32[3,1,4,5]{3,2,1,0:T(4,128)S(1)} copy-done((s32[3,1,4,5]{3,2,1,0:T(4,128)S(1)}, s32[3,1,4,5]{3,2,1,0:T(4,128)}, u32[]{:S(2)}) %copy-start.5) | copy-done | bytes 264
  5.1 1.1 %first_local.1 = (f32[256,512]{1,0:T(8,128)S(1)}, f32[256,512]{1,0:T(8,128)S(1)}, bf16[256,256]{1,0:T(8,128)(2,1)S(1)}, bf16[256,128]{1,0:T(8,128)(2,1)S(1)}, f32[256,1]{1,0:T(8,128)S(1)}) custom-call(f32[1,256,512]{2,1,0:T(8,128)S(1)} %copy-done.3, bf16[64,512]{1,0:T(8,128)(2,1)S(1)} %get-tuple-element.47._, s32[3,1,4,5]{3,2,1,0:T(4,128)S(1)} %copy-done.5, ...), custom_call_target="tpu_custom_call" | custom-call | flops 67108864 | bytes 1081584 | tf_op jit(solution)/shard_map/first_local/pallas_call | solution.py:47
  6.3 0.2 first_residual.2
  6.4 2.5 %collective-permute-start.2 = (bf16[256,128]{1,0:T(8,128)(2,1)S(1)}, bf16[256,128]{1,0:T(8,128)(2,1)S(1)}, u32[]{:S(2)}, u32[]{:S(2)}) collective-permute-start(bf16[256,128]{1,0:T(8,128)(2,1)S(1)} %get-tuple-element.51._), channel_id=1, source_target_pairs={{0,4},{4,0},{8,12},{12,8},{16,20},{20,16},{24,28},{28,24},{1,5},{5... | collective-permute-start | bytes 196616 | tf_op jit(solution)/shard_map/ppermute | solution.py:278
  8.9 0.2 first_residual.3
  9.1 0.1 collective-permute-start.5
  9.2 0.4 copy-done.7
  9.6 0.1 copy.11.rcols.refs_1_
  9.7 0.1 copy-done.6
  9.8 1.1 %operators.2 = (bf16[256,512]{1,0:T(8,128)(2,1)S(1)}, bf16[256,256]{1,0:T(8,128)(2,1)S(1)}, bf16[256,128]{1,0:T(8,128)(2,1)S(1)}, f32[256,1]{1,0:T(8,128)S(1)}) custom-call(bf16[256,128]{1,0:T(8,128)(2,1)S(1)} %get-tuple-element.51._, s32[3,1,4,3]{3,2,1,0:T(4,128)S(1)} %copy.11.rcols.refs_1_, bf16[3,1,4,3,64,64]{5,4,3,2,1,0:T(8,128)(2,1)S(1)} %copy-done.1, ...), custom_call_target="tpu_custom_call" | custom-call | bytes 852352 | tf_op jit(solution)/shard_map/operators/pallas_call | solution.py:47
  10.9 0.4 collective-permute-done.2.other
  11.3 0.2 join.3
  11.5 0.7 %collective-permute-start.3 = (bf16[64,128]{1,0:T(8,128)(2,1)S(1)}, bf16[64,128]{1,0:T(8,128)(2,1)S(1)}, u32[]{:S(2)}, u32[]{:S(2)}) collective-permute-start(bf16[64,128]{1,0:T(8,128)(2,1)S(1)} %get-tuple-element.59), channel_id=1, source_target_pairs={{0,3},{1,2},{2,1},{3,0},{4,7},{5,6},{6,5},{7,4},{8,11},{9,10},{10,... | collective-permute-start | bytes 49160 | tf_op jit(solution)/shard_map/ppermute | solution.py:284
  12.2 1.5 %collective-permute-start.4 = (bf16[64,128]{1,0:T(8,128)(2,1)S(1)}, bf16[64,128]{1,0:T(8,128)(2,1)S(1)}, u32[]{:S(2)}, u32[]{:S(2)}) collective-permute-start(bf16[64,128]{1,0:T(8,128)(2,1)S(1)} %get-tuple-element.60), channel_id=1, source_target_pairs={{0,1},{1,0},{2,3},{3,2},{4,5},{5,4},{6,7},{7,6},{8,9},{9,8},{10,11... | collective-permute-start | bytes 49160 | tf_op jit(solution)/shard_map/ppermute | solution.py:278
  13.7 0.2 join.4
  13.9 0.8 %collective-permute-done.3.outer = bf16[64,128]{1,0:T(8,128)(2,1)S(1)} collective-permute-done((bf16[64,128]{1,0:T(8,128)(2,1)S(1)}, bf16[64,128]{1,0:T(8,128)(2,1)S(1)}, u32[]{:S(2)}, u32[]{:S(2)}) %collective-permute-start.3) | collective-permute-done | bytes 16416 | tf_op jit(solution)/shard_map/ppermute | solution.py:284
  14.7 0.2 residual.3
  14.9 2.2 %collective-permute-start.8 = (bf16[256,128]{1,0:T(8,128)(2,1)S(1)}, bf16[256,128]{1,0:T(8,128)(2,1)S(1)}, u32[]{:S(2)}, u32[]{:S(2)}) collective-permute-start(bf16[256,128]{1,0:T(8,128)(2,1)S(1)} %get-tuple-element.64._), channel_id=1, source_target_pairs={{0,8},{4,12},{8,0},{12,4},{16,24},{20,28},{24,16},{28,20},{1,9},{5... | collective-permute-start | bytes 196616 | tf_op jit(solution)/shard_map/ppermute | solution.py:278
  17.2 1.5 %collective-permute-start.7 = (bf16[64,128]{1,0:T(8,128)(2,1)S(1)}, bf16[64,128]{1,0:T(8,128)(2,1)S(1)}, u32[]{:S(2)}, u32[]{:S(2)}) collective-permute-start(bf16[64,128]{1,0:T(8,128)(2,1)S(1)} %get-tuple-element.68), channel_id=1, source_target_pairs={{0,1},{1,0},{2,3},{3,2},{4,5},{5,4},{6,7},{7,6},{8,9},{9,8},{10,11... | collective-permute-start | bytes 49160 | tf_op jit(solution)/shard_map/ppermute | solution.py:278
  18.7 1.1 %operators.3 = (bf16[256,512]{1,0:T(8,128)(2,1)S(1)}, bf16[256,256]{1,0:T(8,128)(2,1)S(1)}, bf16[256,128]{1,0:T(8,128)(2,1)S(1)}, f32[256,1]{1,0:T(8,128)S(1)}) custom-call(bf16[256,128]{1,0:T(8,128)(2,1)S(1)} %get-tuple-element.64._, s32[3,1,4,3]{3,2,1,0:T(4,128)S(1)} %copy.11.rcols.refs_1_, bf16[3,1,4,3,64,64]{5,4,3,2,1,0:T(8,128)(2,1)S(1)} %copy-done.1, ...), custom_call_target="tpu_custom_call" | custom-call | bytes 852352 | tf_op jit(solution)/shard_map/operators/pallas_call | solution.py:47
  19.8 0.6 %collective-permute-done.6.outer = bf16[64,128]{1,0:T(8,128)(2,1)S(1)} collective-permute-done((bf16[64,128]{1,0:T(8,128)(2,1)S(1)}, bf16[64,128]{1,0:T(8,128)(2,1)S(1)}, u32[]{:S(2)}, u32[]{:S(2)}) %collective-permute-start.6) | collective-permute-done | bytes 16416 | tf_op jit(solution)/shard_map/ppermute | solution.py:284
  20.5 0.2 residual.4
  20.7 0.2 join.5
  20.9 0.2 collective-permute-start.9
  21.2 1.2 %collective-permute-start.10 = (bf16[64,128]{1,0:T(8,128)(2,1)S(1)}, bf16[64,128]{1,0:T(8,128)(2,1)S(1)}, u32[]{:S(2)}, u32[]{:S(2)}) collective-permute-start(bf16[64,128]{1,0:T(8,128)(2,1)S(1)} %get-tuple-element.76), channel_id=1, source_target_pairs={{0,1},{1,0},{2,3},{3,2},{4,5},{5,4},{6,7},{7,6},{8,9},{9,8},{10,11... | collective-permute-start | bytes 49160 | tf_op jit(solution)/shard_map/ppermute | solution.py:278
  22.4 1.8 %collective-permute-done.9.outer = bf16[64,128]{1,0:T(8,128)(2,1)S(1)} collective-permute-done((bf16[64,128]{1,0:T(8,128)(2,1)S(1)}, bf16[64,128]{1,0:T(8,128)(2,1)S(1)}, u32[]{:S(2)}, u32[]{:S(2)}) %collective-permute-start.9) | collective-permute-done | bytes 16416 | tf_op jit(solution)/shard_map/ppermute | solution.py:284
  24.2 0.2 residual.5
  24.4 2.6 %collective-permute-start.11 = (bf16[256,128]{1,0:T(8,128)(2,1)S(1)}, bf16[256,128]{1,0:T(8,128)(2,1)S(1)}, u32[]{:S(2)}, u32[]{:S(2)}) collective-permute-start(bf16[256,128]{1,0:T(8,128)(2,1)S(1)} %get-tuple-element.77.refs_0_.kept), channel_id=1, source_target_pairs={{0,16},{4,20},{8,24},{12,28},{16,0},{20,4},{24,8},{28,12},{1,17},{... | collective-permute-start | bytes 196616 | tf_op jit(solution)/shard_map/ppermute | solution.py:278
  27.0 0.1 copy.14.refs_3_.pcols
  27.2 1.3 %coarse_operators.1 = (bf16[256,512]{1,0:T(8,128)(2,1)S(1)}, bf16[256,1024]{1,0:T(8,128)(2,1)S(1)}, bf16[256,256]{1,0:T(8,128)(2,1)S(1)}) custom-call(bf16[256,128]{1,0:T(8,128)(2,1)S(1)} %get-tuple-element.77.refs_0_.kept, s32[3,1,4,3]{3,2,1,0:T(4,128)S(1)} %copy.11.rcols.refs_1_, bf16[3,1,4,3,64,64]{5,4,3,2,1,0:T(8,128)(2,1)S(1)} %copy-done.1, ...), custom_call_target="tpu_custom_call" | custom-call | flops 201326592 | bytes 1344752 | tf_op jit(solution)/shard_map/coarse_operators/pallas_call | solution.py:47
  28.4 2.5 %collective-permute-done.11.other = bf16[256,128]{1,0:T(8,128)(2,1)S(1)} collective-permute-done((bf16[256,128]{1,0:T(8,128)(2,1)S(1)}, bf16[256,128]{1,0:T(8,128)(2,1)S(1)}, u32[]{:S(2)}, u32[]{:S(2)}) %collective-permute-start.11) | collective-permute-done | bytes 65568 | tf_op jit(solution)/shard_map/ppermute | solution.py:278
  30.9 0.2 last_join.1.refs_0_._
  31.1 0.8 %collective-permute-start.12 = (bf16[256,128]{1,0:T(8,128)(2,1)S(1)}, bf16[256,128]{1,0:T(8,128)(2,1)S(1)}, u32[]{:S(2)}, u32[]{:S(2)}) collective-permute-start(bf16[256,128]{1,0:T(8,128)(2,1)S(1)} %last_join.1.refs_0_._), channel_id=1, source_target_pairs={{0,2},{1,3},{2,0},{3,1},{4,6},{5,7},{6,4},{7,5},{8,10},{9,11},{10,... | collective-permute-start | bytes 196616 | tf_op jit(solution)/shard_map/ppermute | solution.py:278
  31.9 2.0 %collective-permute-start.16 = (bf16[256,256]{1,0:T(8,128)(2,1)S(1)}, bf16[256,256]{1,0:T(8,128)(2,1)S(1)}, u32[]{:S(2)}, u32[]{:S(2)}) collective-permute-start(bf16[256,256]{1,0:T(8,128)(2,1)S(1)} %get-tuple-element.86.near), channel_id=1, source_target_pairs={{0,4},{4,0},{8,12},{12,8},{16,20},{20,16},{24,28},{28,24},{1,5},{5... | collective-permute-start | bytes 393224 | tf_op jit(solution)/shard_map/ppermute | solution.py:278
  33.8 1.6 %collective-permute-done.12.refs_1_ = bf16[256,128]{1,0:T(8,128)(2,1)S(1)} collective-permute-done((bf16[256,128]{1,0:T(8,128)(2,1)S(1)}, bf16[256,128]{1,0:T(8,128)(2,1)S(1)}, u32[]{:S(2)}, u32[]{:S(2)}) %collective-permute-start.12) | collective-permute-done | bytes 65568 | tf_op jit(solution)/shard_map/ppermute | solution.py:278
  35.4 1.2 %collective-permute-done.14.refs_3_ = bf16[256,128]{1,0:T(8,128)(2,1)S(1)} collective-permute-done((bf16[256,128]{1,0:T(8,128)(2,1)S(1)}, bf16[256,128]{1,0:T(8,128)(2,1)S(1)}, u32[]{:S(2)}, u32[]{:S(2)}) %collective-permute-start.14) | collective-permute-done | bytes 65568 | tf_op jit(solution)/shard_map/ppermute | solution.py:278
  36.7 0.3 up.1.refs_0_
  37.0 0.1 collective-permute-start.17
  37.1 2.0 %collective-permute-start.18 = (bf16[256,128]{1,0:T(8,128)(2,1)S(1)}, bf16[256,128]{1,0:T(8,128)(2,1)S(1)}, u32[]{:S(2)}, u32[]{:S(2)}) collective-permute-start(bf16[256,128]{1,0:T(8,128)(2,1)S(1)} %up.1.refs_0_), channel_id=1, source_target_pairs={{0,4},{4,0},{8,12},{12,8},{16,20},{20,16},{24,28},{28,24},{1,5},{5... | collective-permute-start | bytes 196616 | tf_op jit(solution)/shard_map/ppermute | solution.py:278
  39.1 1.4 %collective-permute-start.15 = (bf16[256,128]{1,0:T(8,128)(2,1)S(1)}, bf16[256,128]{1,0:T(8,128)(2,1)S(1)}, u32[]{:S(2)}, u32[]{:S(2)}) collective-permute-start(bf16[256,128]{1,0:T(8,128)(2,1)S(1)} %up.1.refs_0_), channel_id=1, source_target_pairs={{0,12},{4,8},{8,4},{12,0},{16,28},{20,24},{24,20},{28,16},{1,13},{... | collective-permute-start | bytes 196616 | tf_op jit(solution)/shard_map/ppermute | solution.py:278
  40.5 1.3 %fine_operators.1 = (bf16[256,256]{1,0:T(8,128)(2,1)S(1)}, f32[256,512]{1,0:T(8,128)S(1)}) custom-call(bf16[256,128]{1,0:T(8,128)(2,1)S(1)} %last_join.1.refs_0_._, s32[3,1,4,2]{3,2,1,0:T(4,128)S(1)} %copy.14.refs_3_.pcols, bf16[3,1,4,2,64,64]{5,4,3,2,1,0:T(8,128)(2,1)S(1)} %copy-done.2, bf16[3,1,4,2,64,64]{5,4,3,2,1,0:T(8,128)(2,1)S(1)} %copy-done.2, ...), custom_call_target="tpu_custom_call" | custom-call | flops 167772160 | bytes 1509472 | tf_op jit(solution)/shard_map/fine_operators/pallas_call | solution.py:47
  41.8 0.8 %output.3.refs_4_ = f32[1,256,512]{2,1,0:T(8,128)} custom-call(bf16[256,128]{1,0:T(8,128)(2,1)S(1)} %up.1.refs_0_, f32[256,512]{1,0:T(8,128)S(1)} %get-tuple-element.87.refs_1_.refs_2_, bf16[256,256]{1,0:T(8,128)(2,1)S(1)} %get-tuple-element.88.refs_2_.refs_3_), custom_call_target="tpu_custom_call" | custom-call | flops 16777216 | bytes 720896 | tf_op jit(solution)/shard_map/output/pallas_call | solution.py:47
  42.7 0.9 %output.4.refs_3_ = f32[1,256,512]{2,1,0:T(8,128)} custom-call(bf16[256,128]{1,0:T(8,128)(2,1)S(1)} %collective-permute-done.17.refs_0_, bf16[256,128]{1,0:T(8,128)(2,1)S(1)} %collective-permute-done.18.refs_1_, f32[256,512]{1,0:T(8,128)S(1)} %get-tuple-element.87.refs_1_.refs_2_, ...), custom_call_target="tpu_custom_call", output_to_operand_aliasing={{}: (4, {})} | custom-call | flops 33554432 | bytes 1310720 | tf_op jit(solution)/shard_map/output/pallas_call | solution.py:47
  43.7 0.6 %collective-permute-done.15.refs_0_ = bf16[256,128]{1,0:T(8,128)(2,1)S(1)} collective-permute-done((bf16[256,128]{1,0:T(8,128)(2,1)S(1)}, bf16[256,128]{1,0:T(8,128)(2,1)S(1)}, u32[]{:S(2)}, u32[]{:S(2)}) %collective-permute-start.15) | collective-permute-done | bytes 65568 | tf_op jit(solution)/shard_map/ppermute | solution.py:278
  44.2 0.8 %output.5 = f32[1,256,512]{2,1,0:T(8,128)} custom-call(bf16[256,128]{1,0:T(8,128)(2,1)S(1)} %collective-permute-done.15.refs_0_, f32[256,512]{1,0:T(8,128)S(1)} %get-tuple-element.87.refs_1_.refs_2_, bf16[256,256]{1,0:T(8,128)(2,1)S(1)} %get-tuple-element.88.refs_2_.refs_3_, f32[1,256,512]{2,1,0:T(8,128)} %output.4.refs_3_), custom_call_target="tpu_custom_call", output_to_operand_aliasing={{}: (3, {})} | custom-call | flops 16777216 | bytes 1245184 | tf_op jit(solution)/shard_map/output/pallas_call | solution.py:47
  (29 shorter events, 0.1 us)
Async XLA Ops:
  0.0 4.4 %copy-start.3 = (f32[1,256,512]{2,1,0:T(8,128)S(1)}, f32[1,256,512]{2,1,0:T(8,128)}, u32[]{:S(2)}) copy-start(f32[1,256,512]{2,1,0:T(8,128)} %rhs.3) | copy-start | bytes 1572868
  0.0 4.4 %copy-start = (bf16[3,1,4,5,64,64]{5,4,3,2,1,0:T(8,128)(2,1)S(1)}, bf16[3,1,4,5,64,64]{5,4,3,2,1,0:T(8,128)(2,1)}, u32[]{:S(2)}) copy-start(bf16[3,1,4,5,64,64]{5,4,3,2,1,0:T(8,128)(2,1)} %blocks.7) | copy-start | bytes 1474564
  1.3 5.0 %collective-permute-start = (bf16[64,512]{1,0:T(8,128)(2,1)S(1)}, bf16[64,512]{1,0:T(8,128)(2,1)S(1)}, u32[]{:S(2)}, u32[]{:S(2)}) collective-permute-start(bf16[64,512]{1,0:T(8,128)(2,1)S(1)} %get-tuple-element.50), channel_id=1, source_target_pairs={{0,3},{1,2},{2,1},{3,0},{4,7},{5,6},{6,5},{7,4},{8,11},{9,10},{10,... | collective-permute-start | bytes 196616 | tf_op jit(solution)/shard_map/ppermute | solution.py:284
  3.7 2.5 %collective-permute-start.1 = (bf16[64,512]{1,0:T(8,128)(2,1)S(1)}, bf16[64,512]{1,0:T(8,128)(2,1)S(1)}, u32[]{:S(2)}, u32[]{:S(2)}) collective-permute-start(bf16[64,512]{1,0:T(8,128)(2,1)S(1)} %get-tuple-element.47._), channel_id=1, source_target_pairs={{0,1},{1,0},{2,3},{3,2},{4,5},{5,4},{6,7},{7,6},{8,9},{9,8},{10,11... | collective-permute-start | bytes 196616 | tf_op jit(solution)/shard_map/ppermute | solution.py:278
  4.4 0.7 %copy-start.5 = (s32[3,1,4,5]{3,2,1,0:T(4,128)S(1)}, s32[3,1,4,5]{3,2,1,0:T(4,128)}, u32[]{:S(2)}) copy-start(s32[3,1,4,5]{3,2,1,0:T(4,128)} %cols.5) | copy-start | bytes 724
  6.2 3.5 %copy-start.1 = (bf16[3,1,4,3,64,64]{5,4,3,2,1,0:T(8,128)(2,1)S(1)}, bf16[3,1,4,3,64,64]{5,4,3,2,1,0:T(8,128)(2,1)}, u32[]{:S(2)}) copy-start(bf16[3,1,4,3,64,64]{5,4,3,2,1,0:T(8,128)(2,1)} %refs_2_.1) | copy-start | bytes 884740
  6.4 4.8 %collective-permute-start.2 = (bf16[256,128]{1,0:T(8,128)(2,1)S(1)}, bf16[256,128]{1,0:T(8,128)(2,1)S(1)}, u32[]{:S(2)}, u32[]{:S(2)}) collective-permute-start(bf16[256,128]{1,0:T(8,128)(2,1)S(1)} %get-tuple-element.51._), channel_id=1, source_target_pairs={{0,4},{4,0},{8,12},{12,8},{16,20},{20,16},{24,28},{28,24},{1,5},{5... | collective-permute-start | bytes 196616 | tf_op jit(solution)/shard_map/ppermute | solution.py:278
  8.9 0.7 %copy-start.7 = (s32[3,1,4,3]{2,1,3,0:T(1,128)S(1)}, s32[3,1,4,3]{2,1,3,0:T(1,128)}, u32[]{:S(2)}) copy-start(s32[3,1,4,3]{2,1,3,0:T(1,128)} %param.11) | copy-start | bytes 436
  9.1 0.7 %copy-start.6 = (s32[3,1,4,5]{3,2,1,0:T(4,128)S(1)}, s32[3,1,4,5]{3,2,1,0:T(4,128)}, u32[]{:S(2)}) copy-start(s32[3,1,4,5]{3,2,1,0:T(4,128)} %cols.5) | copy-start | bytes 724
  9.1 4.6 %collective-permute-start.5 = (bf16[256,128]{1,0:T(8,128)(2,1)S(1)}, bf16[256,128]{1,0:T(8,128)(2,1)S(1)}, u32[]{:S(2)}, u32[]{:S(2)}) collective-permute-start(bf16[256,128]{1,0:T(8,128)(2,1)S(1)} %get-tuple-element.62), channel_id=1, source_target_pairs={{0,4},{4,0},{8,12},{12,8},{16,20},{20,16},{24,28},{28,24},{1,5},{5... | collective-permute-start | bytes 196616 | tf_op jit(solution)/shard_map/ppermute | solution.py:278
  11.5 3.2 %collective-permute-start.3 = (bf16[64,128]{1,0:T(8,128)(2,1)S(1)}, bf16[64,128]{1,0:T(8,128)(2,1)S(1)}, u32[]{:S(2)}, u32[]{:S(2)}) collective-permute-start(bf16[64,128]{1,0:T(8,128)(2,1)S(1)} %get-tuple-element.59), channel_id=1, source_target_pairs={{0,3},{1,2},{2,1},{3,0},{4,7},{5,6},{6,5},{7,4},{8,11},{9,10},{10,... | collective-permute-start | bytes 49160 | tf_op jit(solution)/shard_map/ppermute | solution.py:284
  12.2 2.5 %collective-permute-start.4 = (bf16[64,128]{1,0:T(8,128)(2,1)S(1)}, bf16[64,128]{1,0:T(8,128)(2,1)S(1)}, u32[]{:S(2)}, u32[]{:S(2)}) collective-permute-start(bf16[64,128]{1,0:T(8,128)(2,1)S(1)} %get-tuple-element.60), channel_id=1, source_target_pairs={{0,1},{1,0},{2,3},{3,2},{4,5},{5,4},{6,7},{7,6},{8,9},{9,8},{10,11... | collective-permute-start | bytes 49160 | tf_op jit(solution)/shard_map/ppermute | solution.py:278
  14.9 5.7 %collective-permute-start.8 = (bf16[256,128]{1,0:T(8,128)(2,1)S(1)}, bf16[256,128]{1,0:T(8,128)(2,1)S(1)}, u32[]{:S(2)}, u32[]{:S(2)}) collective-permute-start(bf16[256,128]{1,0:T(8,128)(2,1)S(1)} %get-tuple-element.64._), channel_id=1, source_target_pairs={{0,8},{4,12},{8,0},{12,4},{16,24},{20,28},{24,16},{28,20},{1,9},{5... | collective-permute-start | bytes 196616 | tf_op jit(solution)/shard_map/ppermute | solution.py:278
  17.1 3.3 %collective-permute-start.6 = (bf16[64,128]{1,0:T(8,128)(2,1)S(1)}, bf16[64,128]{1,0:T(8,128)(2,1)S(1)}, u32[]{:S(2)}, u32[]{:S(2)}) collective-permute-start(bf16[64,128]{1,0:T(8,128)(2,1)S(1)} %get-tuple-element.67), channel_id=1, source_target_pairs={{0,3},{1,2},{2,1},{3,0},{4,7},{5,6},{6,5},{7,4},{8,11},{9,10},{10,... | collective-permute-start | bytes 49160 | tf_op jit(solution)/shard_map/ppermute | solution.py:284
  17.2 3.3 %collective-permute-start.7 = (bf16[64,128]{1,0:T(8,128)(2,1)S(1)}, bf16[64,128]{1,0:T(8,128)(2,1)S(1)}, u32[]{:S(2)}, u32[]{:S(2)}) collective-permute-start(bf16[64,128]{1,0:T(8,128)(2,1)S(1)} %get-tuple-element.68), channel_id=1, source_target_pairs={{0,1},{1,0},{2,3},{3,2},{4,5},{5,4},{6,7},{7,6},{8,9},{9,8},{10,11... | collective-permute-start | bytes 49160 | tf_op jit(solution)/shard_map/ppermute | solution.py:278
  20.7 6.5 %copy-start.4 = (bf16[256,1024]{1,0:T(8,128)(2,1)S(1)}, bf16[256,1024]{1,0:T(8,128)(2,1)}, u32[]{:S(2)}) copy-start(bf16[256,1024]{1,0:T(8,128)(2,1)} %refs_4_.1) | copy-start | bytes 1572868
  20.9 6.2 %copy-start.2 = (bf16[3,1,4,2,64,64]{5,4,3,2,1,0:T(8,128)(2,1)S(1)}, bf16[3,1,4,2,64,64]{5,4,3,2,1,0:T(8,128)(2,1)}, u32[]{:S(2)}) copy-start(bf16[3,1,4,2,64,64]{5,4,3,2,1,0:T(8,128)(2,1)} %blocks_1.1) | copy-start | bytes 589828
  20.9 3.2 %collective-permute-start.9 = (bf16[64,128]{1,0:T(8,128)(2,1)S(1)}, bf16[64,128]{1,0:T(8,128)(2,1)S(1)}, u32[]{:S(2)}, u32[]{:S(2)}) collective-permute-start(bf16[64,128]{1,0:T(8,128)(2,1)S(1)} %get-tuple-element.75), channel_id=1, source_target_pairs={{0,3},{1,2},{2,1},{3,0},{4,7},{5,6},{6,5},{7,4},{8,11},{9,10},{10,... | collective-permute-start | bytes 49160 | tf_op jit(solution)/shard_map/ppermute | solution.py:284
  21.2 3.0 %collective-permute-start.10 = (bf16[64,128]{1,0:T(8,128)(2,1)S(1)}, bf16[64,128]{1,0:T(8,128)(2,1)S(1)}, u32[]{:S(2)}, u32[]{:S(2)}) collective-permute-start(bf16[64,128]{1,0:T(8,128)(2,1)S(1)} %get-tuple-element.76), channel_id=1, source_target_pairs={{0,1},{1,0},{2,3},{3,2},{4,5},{5,4},{6,7},{7,6},{8,9},{9,8},{10,11... | collective-permute-start | bytes 49160 | tf_op jit(solution)/shard_map/ppermute | solution.py:278
  24.2 2.9 %copy-start.8 = (s32[3,1,4,2]{2,3,1,0:T(2,128)S(1)}, s32[3,1,4,2]{2,3,1,0:T(2,128)}, u32[]{:S(2)}) copy-start(s32[3,1,4,2]{2,3,1,0:T(2,128)} %param.13) | copy-start | bytes 292
  24.4 6.5 %collective-permute-start.11 = (bf16[256,128]{1,0:T(8,128)(2,1)S(1)}, bf16[256,128]{1,0:T(8,128)(2,1)S(1)}, u32[]{:S(2)}, u32[]{:S(2)}) collective-permute-start(bf16[256,128]{1,0:T(8,128)(2,1)S(1)} %get-tuple-element.77.refs_0_.kept), channel_id=1, source_target_pairs={{0,16},{4,20},{8,24},{12,28},{16,0},{20,4},{24,8},{28,12},{1,17},{... | collective-permute-start | bytes 196616 | tf_op jit(solution)/shard_map/ppermute | solution.py:278
  31.1 4.3 %collective-permute-start.12 = (bf16[256,128]{1,0:T(8,128)(2,1)S(1)}, bf16[256,128]{1,0:T(8,128)(2,1)S(1)}, u32[]{:S(2)}, u32[]{:S(2)}) collective-permute-start(bf16[256,128]{1,0:T(8,128)(2,1)S(1)} %last_join.1.refs_0_._), channel_id=1, source_target_pairs={{0,2},{1,3},{2,0},{3,1},{4,6},{5,7},{6,4},{7,5},{8,10},{9,11},{10,... | collective-permute-start | bytes 196616 | tf_op jit(solution)/shard_map/ppermute | solution.py:278
  31.9 8.7 %collective-permute-start.16 = (bf16[256,256]{1,0:T(8,128)(2,1)S(1)}, bf16[256,256]{1,0:T(8,128)(2,1)S(1)}, u32[]{:S(2)}, u32[]{:S(2)}) collective-permute-start(bf16[256,256]{1,0:T(8,128)(2,1)S(1)} %get-tuple-element.86.near), channel_id=1, source_target_pairs={{0,4},{4,0},{8,12},{12,8},{16,20},{20,16},{24,28},{28,24},{1,5},{5... | collective-permute-start | bytes 393224 | tf_op jit(solution)/shard_map/ppermute | solution.py:278
  33.8 1.6 %collective-permute-start.13 = (bf16[256,128]{1,0:T(8,128)(2,1)S(1)}, bf16[256,128]{1,0:T(8,128)(2,1)S(1)}, u32[]{:S(2)}, u32[]{:S(2)}) collective-permute-start(bf16[256,128]{1,0:T(8,128)(2,1)S(1)} %last_join.1.refs_0_._), channel_id=1, source_target_pairs={{0,1},{1,0},{2,3},{3,2},{4,5},{5,4},{6,7},{7,6},{8,9},{9,8},{10,11... | collective-permute-start | bytes 196616 | tf_op jit(solution)/shard_map/ppermute | solution.py:278
  35.4 1.3 %collective-permute-start.14 = (bf16[256,128]{1,0:T(8,128)(2,1)S(1)}, bf16[256,128]{1,0:T(8,128)(2,1)S(1)}, u32[]{:S(2)}, u32[]{:S(2)}) collective-permute-start(bf16[256,128]{1,0:T(8,128)(2,1)S(1)} %collective-permute-done.12.refs_1_), channel_id=1, source_target_pairs={{0,1},{1,0},{2,3},{3,2},{4,5},{5,4},{6,7},{7,6},{8,9},{9,8},{10,11... | collective-permute-start | bytes 196616 | tf_op jit(solution)/shard_map/ppermute | solution.py:278
  37.0 5.7 %collective-permute-start.17 = (bf16[256,128]{1,0:T(8,128)(2,1)S(1)}, bf16[256,128]{1,0:T(8,128)(2,1)S(1)}, u32[]{:S(2)}, u32[]{:S(2)}) collective-permute-start(bf16[256,128]{1,0:T(8,128)(2,1)S(1)} %up.1.refs_0_), channel_id=1, source_target_pairs={{0,8},{4,12},{8,0},{12,4},{16,24},{20,28},{24,16},{28,20},{1,9},{5... | collective-permute-start | bytes 196616 | tf_op jit(solution)/shard_map/ppermute | solution.py:278
  37.1 5.6 %collective-permute-start.18 = (bf16[256,128]{1,0:T(8,128)(2,1)S(1)}, bf16[256,128]{1,0:T(8,128)(2,1)S(1)}, u32[]{:S(2)}, u32[]{:S(2)}) collective-permute-start(bf16[256,128]{1,0:T(8,128)(2,1)S(1)} %up.1.refs_0_), channel_id=1, source_target_pairs={{0,4},{4,0},{8,12},{12,8},{16,20},{20,16},{24,28},{28,24},{1,5},{5... | collective-permute-start | bytes 196616 | tf_op jit(solution)/shard_map/ppermute | solution.py:278
  39.1 5.2 %collective-permute-start.15 = (bf16[256,128]{1,0:T(8,128)(2,1)S(1)}, bf16[256,128]{1,0:T(8,128)(2,1)S(1)}, u32[]{:S(2)}, u32[]{:S(2)}) collective-permute-start(bf16[256,128]{1,0:T(8,128)(2,1)S(1)} %up.1.refs_0_), channel_id=1, source_target_pairs={{0,12},{4,8},{8,4},{12,0},{16,28},{20,24},{24,20},{28,16},{1,13},{... | collective-permute-start | bytes 196616 | tf_op jit(solution)/shard_map/ppermute | solution.py:278

commit v6 on v5

--- a/solution.py
+++ b/solution.py
@@ -122,7 +122,8 @@
         out_ref[pl.ds(b * size, size), :] = jnp.concatenate(line, axis=1).astype(bf16)
 
 
-def start_kernel(rhs, blocks, inner_ref, outer_ref, rows, pivots, sems):
+def start_kernel(places, rhs, blocks, inner_ref, *refs):
+    *outers, rows, outer, pivots, sems = refs
     count, size = blocks.shape[2], blocks.shape[4]
     copies = []
     for slot, which in enumerate((0, count - 1)):
@@ -138,7 +139,11 @@
         (rows[slot] * (relax_down / diagonal_of(pivots[slot].astype(f32)))).astype(bf16)
         for slot in range(2)
     )
-    put_ends(first, last, inner_ref, outer_ref)
+    put_ends(first, last, inner_ref, outer)
+    for ref, pair in zip(outers, places):
+        width = ref.shape[1] // 2
+        for slot, place in enumerate(pair):
+            ref[:, slot * width : (slot + 1) * width] = outer[:, lanes_of(place, width)]
 
 
 def first_local_kernel(rhs, _, cols, blocks, rest, base, local, rim, scale):
@@ -161,9 +166,11 @@
 
 
 def first_residual_kernel(places, rest, rim, outer, inner, *refs):
-    for ref, place in zip(refs, places):
-        lanes = lanes_of(place, ref.shape[1])
-        rims = jnp.concatenate([inner[:, lanes], outer[:, lanes]], axis=0)
+    width = refs[0].shape[1]
+    for slot, (ref, place) in enumerate(zip(refs, places)):
+        lanes = lanes_of(place, width)
+        columns = pl.ds(slot * width, width)
+        rims = jnp.concatenate([inner[:, lanes], outer[:, columns]], axis=0)
         ref[...] = (rest[:, lanes] - matmul(rim[...], rims)).astype(bf16)
 
 
@@ -252,8 +259,8 @@
     value = refs[0][...]
     for part, offset in zip(parts, offsets):
         value = value + inverse_part(inverse, part, offset)
-    for step in range((len(refs) - 2) // 2):
-        base, up = refs[1 + 2 * step : 3 + 2 * step]
+    for step in range((len(refs) - 3) // 2):
+        base, up = refs[2 + 2 * step : 4 + 2 * step]
         value = base[...] + matmul(up[...], value.astype(bf16))
     refs[-1][...] = value.astype(bf16)
 
@@ -278,11 +285,10 @@
     return lax.ppermute(value, axis, [(i, i ^ bit) for i in range(count)])
 
 
-def swap_ends(inner, outer):
+def swap_outer(outer):
     count = lax.axis_size("narrow")
     gaps = [(i, (i + 1 if i % 2 else i - 1) % count) for i in range(count)]
-    outer = lax.ppermute(outer, "narrow", gaps)
-    return exchange(inner, "narrow", 1), outer
+    return lax.ppermute(outer, "narrow", gaps)
 
 
 def on_device(
@@ -321,23 +327,26 @@
     def place_of(far, given):
         return (0, far, half), (1, given, width)
 
-    ends = run(
-        start_kernel, "start", [ends_shape(fields)] * 2,
+    pairs = [(place_of(1, given), place_of(0, given)) for given in (1, 0)]
+    inner, *outers = run(
+        functools.partial(start_kernel, pairs), "start",
+        [ends_shape(fields)] + [ends_shape(half)] * 2,
         [in_hbm(level_rhs), in_hbm(galerkin_blocks)],
         scratch=[
-            pltpu.VMEM((2, size, fields), f32), pltpu.VMEM((2, size, size), bf16),
-            pltpu.SemaphoreType.DMA((4,)),
+            pltpu.VMEM((2, size, fields), f32), pltpu.VMEM((size, fields), bf16),
+            pltpu.VMEM((2, size, size), bf16), pltpu.SemaphoreType.DMA((4,)),
         ],
     )
-    inner, outer = swap_ends(*ends)
+    first = outers[0]
+    outers = [swap_outer(outer) for outer in outers]
+    inner = exchange(inner, "narrow", 1)
     rest, base, local, rim, scale = run(
         first_local_kernel, "first_local", [array((rows, fields), f32)] * 2 + operator_shapes,
-        [level_rhs, ends[0], gcols, of_level(galerkin_blocks, 0)], flops=flops(fields),
+        [level_rhs, first, gcols, of_level(galerkin_blocks, 0)], flops=flops(fields),
     )
     operators = [(scale, local)]
     sent, kept = [], []
-    for given in (1, 0):
-        places = place_of(1, given), place_of(0, given)
+    for places, outer in zip(pairs, outers):
         far, near = run(
             functools.partial(first_residual_kernel, places), "first_residual", [chunk_shape] * 2,
             [rest, rim, outer, inner],
@@ -345,13 +354,14 @@
         sent.append(far)
         kept.append(near)
     bases = []
+    anchor = sent[0]
     pieces = lax.axis_size("narrow")
     for level_idx in range(levels - 1):
         other = [exchange(value, "wide", 1 << level_idx) for value in sent]
         rmat, local, rim, scale = run(
             functools.partial(operators_kernel, level_idx), "operators",
             [rmat_shape] + operator_shapes,
-            [sent[0], rcols, of_level(restrict_blocks, level_idx),
+            [anchor, rcols, of_level(restrict_blocks, level_idx),
              gcols, of_level(galerkin_blocks, level_idx + 1)],
         )
         operators.append((scale, local))
@@ -362,14 +372,15 @@
                 [real_shape, chunk_shape] + [ends_shape(width)] * 2,
                 [rmat, near, far, scale], flops=flops(width, 2),
             )
-            inner, outer = swap_ends(*ends)
+            inner, outer = exchange(ends[0], "narrow", 1), swap_outer(ends[1])
             joined.append((rhs, smoothed, scale, local, rim, outer, inner))
+        anchor = joined[-1][1]
         made = []
         for operands in joined:
             value, made_base = run(
                 residual_kernel, "residual",
                 [chunk_shape, chunk_shape if level_idx == 0 else real_shape],
-                [*operands, joined[-1][1]], flops=flops(width, 2),
+                [*operands, joined[-1][-1]], flops=flops(width, 2),
             )
             made.append(value)
             bases.append(made_base)
@@ -404,7 +415,7 @@
         flops=flops(rows, 5), scratch=held,
     )
     offsets = tuple(parts)
-    operands = [coarse_mat] + [parts[o] for o in offsets] + [bases[-1]]
+    operands = [coarse_mat] + [parts[o] for o in offsets] + [bases[-1], both]
     for idx in reversed(range(2, last)):
         operands += [bases[idx], ups[idx - 2]]
     (value,) = run(
@@ -412,7 +423,7 @@
         flops=flops(width, len(offsets) + levels - 3),
     )
     gathered = [(value, place_of(0, 0))]
-    for bits in (2, 1, 3):
+    for bits in (3, 1, 2):
         gathered.append((exchange(value, "wide", bits), place_of(bits & 1, bits >> 1)))
     result = None
     for group in (gathered[:1], gathered[1:3], gathered[3:]):

time: 45.3 us -> 46.9 us (1.035)
  waiting for transfers between devices: 9.5 us -> 7.74 us
  local copies, waits for them, and re-layouts: 1.41 us -> 2.98 us
  Pallas kernels: 11.9 us -> 12.8 us
  starting transfers between devices: 22 us -> 22.7 us
    ppermute x4 -> x5, starting transfers between devices: 3.33 us -> 6.52 us  [swap_outer(): return lax.ppermute(outer, 'narrow', gaps)]
    ppermute x15, starting transfers between devices: 18.7 us -> 16.2 us  [exchange(): return lax.ppermute(value, axis, [(i, i ^ bit) for i in range(count)])]
    unnamed x20 -> x28, local copies, waits for them, and re-layouts: 1.41 us -> 2.98 us
    ppermute x15, waiting for transfers between devices: 6.25 us -> 4.69 us  [exchange(): return lax.ppermute(value, axis, [(i, i ^ bit) for i in range(count)])]
    pallas_call x19, Pallas kernels: 11.9 us -> 12.8 us  [run(): pl.pallas_call(body, grid=(1,) if windows else (), out_shape=outs, in_spe...]
    ppermute x4 -> x5, waiting for transfers between devices: 3.25 us -> 3.05 us  [swap_outer(): return lax.ppermute(outer, 'narrow', gaps)]
  transfers between devices with their start and end apart: 19 -> 20, of which waited for: 8 -> 8; matrix products, arithmetic and copies ran while one was open for 0% -> 0% of each run, Pallas kernels for 20% -> 21%
where the time goes in v6:
time: 46.9 us; the launch traced here: 46.5 us
  starting transfers between devices  22.7 us (48%)
  Pallas kernels  12.8 us (27%)
  waiting for transfers between devices  7.74 us (17%)
  local copies, waits for them, and re-layouts  2.98 us (6%)
    ppermute x15, starting transfers between devices, exchange(): return lax.ppermute(value, axis, [(i, i ^ bit) for i in range(count)])  16.2 us
    pallas_call x19, Pallas kernels, run(): pl.pallas_call(body, grid=(1,) if windows else (), out_shape=outs, in_spe...  12.8 us
    ppermute x5, starting transfers between devices, swap_outer(): return lax.ppermute(outer, 'narrow', gaps)  6.52 us
    ppermute x15, waiting for transfers between devices, exchange(): return lax.ppermute(value, axis, [(i, i ^ bit) for i in range(count)])  4.69 us
    ppermute x5, waiting for transfers between devices, swap_outer(): return lax.ppermute(outer, 'narrow', gaps)  3.05 us
    unnamed x28, local copies, waits for them, and re-layouts  2.98 us
  transfers between devices with their start and end apart: 20, of which 8 were waited for; matrix products, arithmetic and copies ran while one was open for 0% of the time, Pallas kernels for 21%

profile of v6, /device:TPU:0, one launch (start us, length us, event | category | flops | bytes accessed | tf_op | source)
XLA Modules:
  0.0 46.5 jit_solution(5769371241271590147)
XLA Ops:
  0.0 1.3 %start.1 = (bf16[64,512]{1,0:T(8,128)(2,1)S(1)}, bf16[64,256]{1,0:T(8,128)(2,1)S(1)}, bf16[64,256]{1,0:T(8,128)(2,1)S(1)}) custom-call(f32[1,256,512]{2,1,0:T(8,128)} %rhs.3, bf16[3,1,4,5,64,64]{5,4,3,2,1,0:T(8,128)(2,1)} %blocks.7), custom_call_target="tpu_custom_call" | custom-call | bytes 1015808 | tf_op jit(solution)/shard_map/start/pallas_call | solution.py:47
  1.3 0.5 %collective-permute-start.1 = (bf16[64,512]{1,0:T(8,128)(2,1)S(1)}, bf16[64,512]{1,0:T(8,128)(2,1)S(1)}, u32[]{:S(2)}, u32[]{:S(2)}) collective-permute-start(bf16[64,512]{1,0:T(8,128)(2,1)S(1)} %get-tuple-element.51), channel_id=1, source_target_pairs={{0,1},{1,0},{2,3},{3,2},{4,5},{5,4},{6,7},{7,6},{8,9},{9,8},{10,11... | collective-permute-start | bytes 196616 | tf_op jit(solution)/shard_map/ppermute | solution.py:285
  1.8 2.6 %collective-permute-start = (bf16[64,256]{1,0:T(8,128)(2,1)S(1)}, bf16[64,256]{1,0:T(8,128)(2,1)S(1)}, u32[]{:S(2)}, u32[]{:S(2)}) collective-permute-start(bf16[64,256]{1,0:T(8,128)(2,1)S(1)} %get-tuple-element.48._), channel_id=1, source_target_pairs={{0,3},{1,2},{2,1},{3,0},{4,7},{5,6},{6,5},{7,4},{8,11},{9,10},{10,... | collective-permute-start | bytes 98312 | tf_op jit(solution)/shard_map/ppermute | solution.py:291
  4.4 0.7 %copy-done.9 = s32[3,1,4,5]{3,2,1,0:T(4,128)S(1)} copy-done((s32[3,1,4,5]{3,2,1,0:T(4,128)S(1)}, s32[3,1,4,5]{3,2,1,0:T(4,128)}, u32[]{:S(2)}) %copy-start.9) | copy-done | bytes 264
  5.1 1.1 %first_local.1 = (f32[256,512]{1,0:T(8,128)S(1)}, f32[256,512]{1,0:T(8,128)S(1)}, bf16[256,256]{1,0:T(8,128)(2,1)S(1)}, bf16[256,128]{1,0:T(8,128)(2,1)S(1)}, f32[256,1]{1,0:T(8,128)S(1)}) custom-call(f32[1,256,512]{2,1,0:T(8,128)S(1)} %copy-done.3, bf16[64,256]{1,0:T(8,128)(2,1)S(1)} %get-tuple-element.48._, s32[3,1,4,5]{3,2,1,0:T(4,128)S(1)} %copy-done.9, ...), custom_call_target="tpu_custom_call" | custom-call | flops 67108864 | bytes 1048816 | tf_op jit(solution)/shard_map/first_local/pallas_call | solution.py:47
  6.3 0.2 first_residual.2
  6.5 1.8 %collective-permute-start.6 = (bf16[256,128]{1,0:T(8,128)(2,1)S(1)}, bf16[256,128]{1,0:T(8,128)(2,1)S(1)}, u32[]{:S(2)}, u32[]{:S(2)}) collective-permute-start(bf16[256,128]{1,0:T(8,128)(2,1)S(1)} %get-tuple-element.52._), channel_id=1, source_target_pairs={{0,4},{4,0},{8,12},{12,8},{16,20},{20,16},{24,28},{28,24},{1,5},{5... | collective-permute-start | bytes 196616 | tf_op jit(solution)/shard_map/ppermute | solution.py:285
  8.3 0.2 first_residual.3
  8.5 1.2 %collective-permute-start.3 = (bf16[256,128]{1,0:T(8,128)(2,1)S(1)}, bf16[256,128]{1,0:T(8,128)(2,1)S(1)}, u32[]{:S(2)}, u32[]{:S(2)}) collective-permute-start(bf16[256,128]{1,0:T(8,128)(2,1)S(1)} %get-tuple-element.56), channel_id=1, source_target_pairs={{0,4},{4,0},{8,12},{12,8},{16,20},{20,16},{24,28},{28,24},{1,5},{5... | collective-permute-start | bytes 196616 | tf_op jit(solution)/shard_map/ppermute | solution.py:285
  9.6 0.1 copy.11.rcols.refs_1_
  9.8 1.1 %operators.2 = (bf16[256,512]{1,0:T(8,128)(2,1)S(1)}, bf16[256,256]{1,0:T(8,128)(2,1)S(1)}, bf16[256,128]{1,0:T(8,128)(2,1)S(1)}, f32[256,1]{1,0:T(8,128)S(1)}) custom-call(bf16[256,128]{1,0:T(8,128)(2,1)S(1)} %get-tuple-element.52._, s32[3,1,4,3]{3,2,1,0:T(4,128)S(1)} %copy.11.rcols.refs_1_, bf16[3,1,4,3,64,64]{5,4,3,2,1,0:T(8,128)(2,1)S(1)} %copy-done.1, ...), custom_call_target="tpu_custom_call" | custom-call | bytes 852352 | tf_op jit(solution)/shard_map/operators/pallas_call | solution.py:47
  11.0 0.2 join.4
  11.2 1.2 %collective-permute-start.7 = (bf16[64,128]{1,0:T(8,128)(2,1)S(1)}, bf16[64,128]{1,0:T(8,128)(2,1)S(1)}, u32[]{:S(2)}, u32[]{:S(2)}) collective-permute-start(bf16[64,128]{1,0:T(8,128)(2,1)S(1)} %get-tuple-element.69), channel_id=1, source_target_pairs={{0,3},{1,2},{2,1},{3,0},{4,7},{5,6},{6,5},{7,4},{8,11},{9,10},{10,... | collective-permute-start | bytes 49160 | tf_op jit(solution)/shard_map/ppermute | solution.py:291
  12.4 0.8 %collective-permute-start.8 = (bf16[64,128]{1,0:T(8,128)(2,1)S(1)}, bf16[64,128]{1,0:T(8,128)(2,1)S(1)}, u32[]{:S(2)}, u32[]{:S(2)}) collective-permute-start(bf16[64,128]{1,0:T(8,128)(2,1)S(1)} %get-tuple-element.70), channel_id=1, source_target_pairs={{0,1},{1,0},{2,3},{3,2},{4,5},{5,4},{6,7},{7,6},{8,9},{9,8},{10,11... | collective-permute-start | bytes 49160 | tf_op jit(solution)/shard_map/ppermute | solution.py:285
  13.2 0.2 join.3
  13.5 1.0 %collective-permute-done.7.outer = bf16[64,128]{1,0:T(8,128)(2,1)S(1)} collective-permute-done((bf16[64,128]{1,0:T(8,128)(2,1)S(1)}, bf16[64,128]{1,0:T(8,128)(2,1)S(1)}, u32[]{:S(2)}, u32[]{:S(2)}) %collective-permute-start.7) | collective-permute-done | bytes 16416 | tf_op jit(solution)/shard_map/ppermute | solution.py:291
  14.4 0.2 collective-permute-done.5.inner._
  14.6 0.2 residual.4
  14.9 1.9 %collective-permute-start.9 = (bf16[256,128]{1,0:T(8,128)(2,1)S(1)}, bf16[256,128]{1,0:T(8,128)(2,1)S(1)}, u32[]{:S(2)}, u32[]{:S(2)}) collective-permute-start(bf16[256,128]{1,0:T(8,128)(2,1)S(1)} %get-tuple-element.71), channel_id=1, source_target_pairs={{0,8},{4,12},{8,0},{12,4},{16,24},{20,28},{24,16},{28,20},{1,9},{5... | collective-permute-start | bytes 196616 | tf_op jit(solution)/shard_map/ppermute | solution.py:285
  16.7 1.1 %collective-permute-start.4 = (bf16[64,128]{1,0:T(8,128)(2,1)S(1)}, bf16[64,128]{1,0:T(8,128)(2,1)S(1)}, u32[]{:S(2)}, u32[]{:S(2)}) collective-permute-start(bf16[64,128]{1,0:T(8,128)(2,1)S(1)} %get-tuple-element.63), channel_id=1, source_target_pairs={{0,3},{1,2},{2,1},{3,0},{4,7},{5,6},{6,5},{7,4},{8,11},{9,10},{10,... | collective-permute-start | bytes 49160 | tf_op jit(solution)/shard_map/ppermute | solution.py:291
  17.9 1.1 %operators.3 = (bf16[256,512]{1,0:T(8,128)(2,1)S(1)}, bf16[256,256]{1,0:T(8,128)(2,1)S(1)}, bf16[256,128]{1,0:T(8,128)(2,1)S(1)}, f32[256,1]{1,0:T(8,128)S(1)}) custom-call(bf16[256,128]{1,0:T(8,128)(2,1)S(1)} %get-tuple-element.58._.smoothed, s32[3,1,4,3]{3,2,1,0:T(4,128)S(1)} %copy.11.rcols.refs_1_, bf16[3,1,4,3,64,64]{5,4,3,2,1,0:T(8,128)(2,1)S(1)} %copy-done.1, ...), custom_call_target="tpu_custom_call" | custom-call | bytes 852352 | tf_op jit(solution)/shard_map/operators/pallas_call | solution.py:47
  19.0 0.9 %collective-permute-done.4.outer = bf16[64,128]{1,0:T(8,128)(2,1)S(1)} collective-permute-done((bf16[64,128]{1,0:T(8,128)(2,1)S(1)}, bf16[64,128]{1,0:T(8,128)(2,1)S(1)}, u32[]{:S(2)}, u32[]{:S(2)}) %collective-permute-start.4) | collective-permute-done | bytes 16416 | tf_op jit(solution)/shard_map/ppermute | solution.py:291
  19.9 0.2 residual.3
  20.1 0.2 join.5
  20.4 0.4 copy-done.7
  20.7 1.6 %collective-permute-start.10 = (bf16[64,128]{1,0:T(8,128)(2,1)S(1)}, bf16[64,128]{1,0:T(8,128)(2,1)S(1)}, u32[]{:S(2)}, u32[]{:S(2)}) collective-permute-start(bf16[64,128]{1,0:T(8,128)(2,1)S(1)} %get-tuple-element.77), channel_id=1, source_target_pairs={{0,3},{1,2},{2,1},{3,0},{4,7},{5,6},{6,5},{7,4},{8,11},{9,10},{10,... | collective-permute-start | bytes 49160 | tf_op jit(solution)/shard_map/ppermute | solution.py:291
  22.3 0.4 collective-permute-start.11
  22.7 1.2 %collective-permute-done.10.outer = bf16[64,128]{1,0:T(8,128)(2,1)S(1)} collective-permute-done((bf16[64,128]{1,0:T(8,128)(2,1)S(1)}, bf16[64,128]{1,0:T(8,128)(2,1)S(1)}, u32[]{:S(2)}, u32[]{:S(2)}) %collective-permute-start.10) | collective-permute-done | bytes 16416 | tf_op jit(solution)/shard_map/ppermute | solution.py:291
  23.9 0.2 residual.5
  24.1 2.7 %collective-permute-start.12 = (bf16[256,128]{1,0:T(8,128)(2,1)S(1)}, bf16[256,128]{1,0:T(8,128)(2,1)}, u32[]{:S(2)}, u32[]{:S(2)}) collective-permute-start(bf16[256,128]{1,0:T(8,128)(2,1)S(1)} %get-tuple-element.79.refs_0_.kept), channel_id=1, source_target_pairs={{0,16},{4,20},{8,24},{12,28},{16,0},{20,4},{24,8},{28,12},{1,17},{... | collective-permute-start | bytes 196616 | tf_op jit(solution)/shard_map/ppermute | solution.py:285
  26.8 0.1 copy.14.refs_3_.pcols
  26.9 0.8 %copy-done.6 = bf16[256,128]{1,0:T(8,128)(2,1)S(1)} copy-done((bf16[256,128]{1,0:T(8,128)(2,1)S(1)}, bf16[256,128]{1,0:T(8,128)(2,1)}, u32[]{:S(2)}) %copy-start.6) | copy-done | bytes 65560
  27.7 0.8 %copy-done.8 = bf16[256,128]{1,0:T(8,128)(2,1)S(1)} copy-done((bf16[256,128]{1,0:T(8,128)(2,1)S(1)}, bf16[256,128]{1,0:T(8,128)(2,1)}, u32[]{:S(2)}) %copy-start.8) | copy-done | bytes 65560
  28.5 1.3 %coarse_operators.1 = (bf16[256,512]{1,0:T(8,128)(2,1)S(1)}, bf16[256,1024]{1,0:T(8,128)(2,1)S(1)}, bf16[256,256]{1,0:T(8,128)(2,1)S(1)}) custom-call(bf16[256,128]{1,0:T(8,128)(2,1)S(1)} %get-tuple-element.79.refs_0_.kept, s32[3,1,4,3]{3,2,1,0:T(4,128)S(1)} %copy.11.rcols.refs_1_, bf16[3,1,4,3,64,64]{5,4,3,2,1,0:T(8,128)(2,1)S(1)} %copy-done.1, ...), custom_call_target="tpu_custom_call" | custom-call | flops 201326592 | bytes 1344752 | tf_op jit(solution)/shard_map/coarse_operators/pallas_call | solution.py:47
  29.8 1.9 %collective-permute-start.16 = (bf16[256,256]{1,0:T(8,128)(2,1)S(1)}, bf16[256,256]{1,0:T(8,128)(2,1)S(1)}, u32[]{:S(2)}, u32[]{:S(2)}) collective-permute-start(bf16[256,256]{1,0:T(8,128)(2,1)S(1)} %get-tuple-element.88.near), channel_id=1, source_target_pairs={{0,4},{4,0},{8,12},{12,8},{16,20},{20,16},{24,28},{28,24},{1,5},{5... | collective-permute-start | bytes 393224 | tf_op jit(solution)/shard_map/ppermute | solution.py:285
  31.7 1.1 %last_join.1._.refs_0_ = bf16[256,128]{1,0:T(8,128)(2,1)S(1)} custom-call(bf16[256,512]{1,0:T(8,128)(2,1)S(1)} %get-tuple-element.83.rmat, bf16[256,128]{1,0:T(8,128)(2,1)S(1)} %get-tuple-element.79.refs_0_.kept, bf16[256,128]{1,0:T(8,128)(2,1)} %collective-permute-done.12.other), custom_call_target="tpu_custom_call" | custom-call | flops 33554432 | bytes 393216 | tf_op jit(solution)/shard_map/last_join/pallas_call | solution.py:47
  32.7 1.6 %collective-permute-start.13 = (bf16[256,128]{1,0:T(8,128)(2,1)S(1)}, bf16[256,128]{1,0:T(8,128)(2,1)S(1)}, u32[]{:S(2)}, u32[]{:S(2)}) collective-permute-start(bf16[256,128]{1,0:T(8,128)(2,1)S(1)} %last_join.1._.refs_0_), channel_id=1, source_target_pairs={{0,2},{1,3},{2,0},{3,1},{4,6},{5,7},{6,4},{7,5},{8,10},{9,11},{10,... | collective-permute-start | bytes 196616 | tf_op jit(solution)/shard_map/ppermute | solution.py:285
  34.3 2.7 %collective-permute-done.13.refs_1_ = bf16[256,128]{1,0:T(8,128)(2,1)S(1)} collective-permute-done((bf16[256,128]{1,0:T(8,128)(2,1)S(1)}, bf16[256,128]{1,0:T(8,128)(2,1)S(1)}, u32[]{:S(2)}, u32[]{:S(2)}) %collective-permute-start.13) | collective-permute-done | bytes 65568 | tf_op jit(solution)/shard_map/ppermute | solution.py:285
  37.1 1.3 %fine_operators.1 = (bf16[256,256]{1,0:T(8,128)(2,1)S(1)}, f32[256,512]{1,0:T(8,128)S(1)}) custom-call(bf16[256,128]{1,0:T(8,128)(2,1)S(1)} %last_join.1._.refs_0_, s32[3,1,4,2]{3,2,1,0:T(4,128)S(1)} %copy.14.refs_3_.pcols, bf16[3,1,4,2,64,64]{5,4,3,2,1,0:T(8,128)(2,1)S(1)} %copy-done.2, bf16[3,1,4,2,64,64]{5,4,3,2,1,0:T(8,128)(2,1)S(1)} %copy-done.2, ...), custom_call_target="tpu_custom_call" | custom-call | flops 167772160 | bytes 1509472 | tf_op jit(solution)/shard_map/fine_operators/pallas_call | solution.py:47
  38.4 0.3 up.1.refs_0_
  38.7 0.3 collective-permute-start.18
  39.0 1.7 %collective-permute-start.19 = (bf16[256,128]{1,0:T(8,128)(2,1)S(1)}, bf16[256,128]{1,0:T(8,128)(2,1)S(1)}, u32[]{:S(2)}, u32[]{:S(2)}) collective-permute-start(bf16[256,128]{1,0:T(8,128)(2,1)S(1)} %up.1.refs_0_), channel_id=1, source_target_pairs={{0,4},{4,0},{8,12},{12,8},{16,20},{20,16},{24,28},{28,24},{1,5},{5... | collective-permute-start | bytes 196616 | tf_op jit(solution)/shard_map/ppermute | solution.py:285
  40.8 1.5 %collective-permute-start.17 = (bf16[256,128]{1,0:T(8,128)(2,1)S(1)}, bf16[256,128]{1,0:T(8,128)(2,1)S(1)}, u32[]{:S(2)}, u32[]{:S(2)}) collective-permute-start(bf16[256,128]{1,0:T(8,128)(2,1)S(1)} %up.1.refs_0_), channel_id=1, source_target_pairs={{0,8},{4,12},{8,0},{12,4},{16,24},{20,28},{24,16},{28,20},{1,9},{5... | collective-permute-start | bytes 196616 | tf_op jit(solution)/shard_map/ppermute | solution.py:285
  42.2 0.8 %output.3.refs_4_ = f32[1,256,512]{2,1,0:T(8,128)} custom-call(bf16[256,128]{1,0:T(8,128)(2,1)S(1)} %up.1.refs_0_, f32[256,512]{1,0:T(8,128)S(1)} %get-tuple-element.90.refs_1_.refs_2_, bf16[256,256]{1,0:T(8,128)(2,1)S(1)} %get-tuple-element.89.refs_5_.refs_2_.refs_3_), custom_call_target="tpu_custom_call" | custom-call | flops 16777216 | bytes 720896 | tf_op jit(solution)/shard_map/output/pallas_call | solution.py:47
  43.1 1.5 %collective-permute-done.18.refs_0_ = bf16[256,128]{1,0:T(8,128)(2,1)S(1)} collective-permute-done((bf16[256,128]{1,0:T(8,128)(2,1)S(1)}, bf16[256,128]{1,0:T(8,128)(2,1)S(1)}, u32[]{:S(2)}, u32[]{:S(2)}) %collective-permute-start.18) | collective-permute-done | bytes 65568 | tf_op jit(solution)/shard_map/ppermute | solution.py:285
  44.6 0.2 collective-permute-done.19.refs_1_
  44.7 0.9 %output.4.refs_3_ = f32[1,256,512]{2,1,0:T(8,128)} custom-call(bf16[256,128]{1,0:T(8,128)(2,1)S(1)} %collective-permute-done.18.refs_0_, bf16[256,128]{1,0:T(8,128)(2,1)S(1)} %collective-permute-done.19.refs_1_, f32[256,512]{1,0:T(8,128)S(1)} %get-tuple-element.90.refs_1_.refs_2_, ...), custom_call_target="tpu_custom_call", output_to_operand_aliasing={{}: (4, {})} | custom-call | flops 33554432 | bytes 1310720 | tf_op jit(solution)/shard_map/output/pallas_call | solution.py:47
  45.7 0.8 %output.5 = f32[1,256,512]{2,1,0:T(8,128)} custom-call(bf16[256,128]{1,0:T(8,128)(2,1)S(1)} %collective-permute-done.17.refs_0_, f32[256,512]{1,0:T(8,128)S(1)} %get-tuple-element.90.refs_1_.refs_2_, bf16[256,256]{1,0:T(8,128)(2,1)S(1)} %get-tuple-element.89.refs_5_.refs_2_.refs_3_, f32[1,256,512]{2,1,0:T(8,128)} %output.4.refs_3_), custom_call_target="tpu_custom_call", output_to_operand_aliasing={{}: (3, {})} | custom-call | flops 16777216 | bytes 1245184 | tf_op jit(solution)/shard_map/output/pallas_call | solution.py:47
  (39 shorter events, 0.3 us)
Async XLA Ops:
  0.0 4.4 %copy-start = (bf16[3,1,4,5,64,64]{5,4,3,2,1,0:T(8,128)(2,1)S(1)}, bf16[3,1,4,5,64,64]{5,4,3,2,1,0:T(8,128)(2,1)}, u32[]{:S(2)}) copy-start(bf16[3,1,4,5,64,64]{5,4,3,2,1,0:T(8,128)(2,1)} %blocks.7) | copy-start | bytes 1474564
  0.0 4.4 %copy-start.3 = (f32[1,256,512]{2,1,0:T(8,128)S(1)}, f32[1,256,512]{2,1,0:T(8,128)}, u32[]{:S(2)}) copy-start(f32[1,256,512]{2,1,0:T(8,128)} %rhs.3) | copy-start | bytes 1572868
  1.3 5.0 %collective-permute-start.1 = (bf16[64,512]{1,0:T(8,128)(2,1)S(1)}, bf16[64,512]{1,0:T(8,128)(2,1)S(1)}, u32[]{:S(2)}, u32[]{:S(2)}) collective-permute-start(bf16[64,512]{1,0:T(8,128)(2,1)S(1)} %get-tuple-element.51), channel_id=1, source_target_pairs={{0,1},{1,0},{2,3},{3,2},{4,5},{5,4},{6,7},{7,6},{8,9},{9,8},{10,11... | collective-permute-start | bytes 196616 | tf_op jit(solution)/shard_map/ppermute | solution.py:285
  1.8 4.5 %collective-permute-start = (bf16[64,256]{1,0:T(8,128)(2,1)S(1)}, bf16[64,256]{1,0:T(8,128)(2,1)S(1)}, u32[]{:S(2)}, u32[]{:S(2)}) collective-permute-start(bf16[64,256]{1,0:T(8,128)(2,1)S(1)} %get-tuple-element.48._), channel_id=1, source_target_pairs={{0,3},{1,2},{2,1},{3,0},{4,7},{5,6},{6,5},{7,4},{8,11},{9,10},{10,... | collective-permute-start | bytes 98312 | tf_op jit(solution)/shard_map/ppermute | solution.py:291
  4.4 3.9 %collective-permute-start.2 = (bf16[64,256]{1,0:T(8,128)(2,1)S(1)}, bf16[64,256]{1,0:T(8,128)(2,1)S(1)}, u32[]{:S(2)}, u32[]{:S(2)}) collective-permute-start(bf16[64,256]{1,0:T(8,128)(2,1)S(1)} %get-tuple-element.54), channel_id=1, source_target_pairs={{0,3},{1,2},{2,1},{3,0},{4,7},{5,6},{6,5},{7,4},{8,11},{9,10},{10,... | collective-permute-start | bytes 98312 | tf_op jit(solution)/shard_map/ppermute | solution.py:291
  4.4 0.7 %copy-start.9 = (s32[3,1,4,5]{3,2,1,0:T(4,128)S(1)}, s32[3,1,4,5]{3,2,1,0:T(4,128)}, u32[]{:S(2)}) copy-start(s32[3,1,4,5]{3,2,1,0:T(4,128)} %cols.5) | copy-start | bytes 724
  6.3 3.5 %copy-start.1 = (bf16[3,1,4,3,64,64]{5,4,3,2,1,0:T(8,128)(2,1)S(1)}, bf16[3,1,4,3,64,64]{5,4,3,2,1,0:T(8,128)(2,1)}, u32[]{:S(2)}) copy-start(bf16[3,1,4,3,64,64]{5,4,3,2,1,0:T(8,128)(2,1)} %refs_2_.1) | copy-start | bytes 884740
  6.5 4.5 %collective-permute-start.6 = (bf16[256,128]{1,0:T(8,128)(2,1)S(1)}, bf16[256,128]{1,0:T(8,128)(2,1)S(1)}, u32[]{:S(2)}, u32[]{:S(2)}) collective-permute-start(bf16[256,128]{1,0:T(8,128)(2,1)S(1)} %get-tuple-element.52._), channel_id=1, source_target_pairs={{0,4},{4,0},{8,12},{12,8},{16,20},{20,16},{24,28},{28,24},{1,5},{5... | collective-permute-start | bytes 196616 | tf_op jit(solution)/shard_map/ppermute | solution.py:285
  8.3 1.4 %copy-start.11 = (s32[3,1,4,3]{2,1,3,0:T(1,128)S(1)}, s32[3,1,4,3]{2,1,3,0:T(1,128)}, u32[]{:S(2)}) copy-start(s32[3,1,4,3]{2,1,3,0:T(1,128)} %param.11) | copy-start | bytes 436
  8.5 1.3 %copy-start.10 = (s32[3,1,4,5]{3,2,1,0:T(4,128)S(1)}, s32[3,1,4,5]{3,2,1,0:T(4,128)}, u32[]{:S(2)}) copy-start(s32[3,1,4,5]{3,2,1,0:T(4,128)} %cols.5) | copy-start | bytes 724
  8.5 4.7 %collective-permute-start.3 = (bf16[256,128]{1,0:T(8,128)(2,1)S(1)}, bf16[256,128]{1,0:T(8,128)(2,1)S(1)}, u32[]{:S(2)}, u32[]{:S(2)}) collective-permute-start(bf16[256,128]{1,0:T(8,128)(2,1)S(1)} %get-tuple-element.56), channel_id=1, source_target_pairs={{0,4},{4,0},{8,12},{12,8},{16,20},{20,16},{24,28},{28,24},{1,5},{5... | collective-permute-start | bytes 196616 | tf_op jit(solution)/shard_map/ppermute | solution.py:285
  11.2 3.2 %collective-permute-start.7 = (bf16[64,128]{1,0:T(8,128)(2,1)S(1)}, bf16[64,128]{1,0:T(8,128)(2,1)S(1)}, u32[]{:S(2)}, u32[]{:S(2)}) collective-permute-start(bf16[64,128]{1,0:T(8,128)(2,1)S(1)} %get-tuple-element.69), channel_id=1, source_target_pairs={{0,3},{1,2},{2,1},{3,0},{4,7},{5,6},{6,5},{7,4},{8,11},{9,10},{10,... | collective-permute-start | bytes 49160 | tf_op jit(solution)/shard_map/ppermute | solution.py:291
  12.4 2.1 %collective-permute-start.8 = (bf16[64,128]{1,0:T(8,128)(2,1)S(1)}, bf16[64,128]{1,0:T(8,128)(2,1)S(1)}, u32[]{:S(2)}, u32[]{:S(2)}) collective-permute-start(bf16[64,128]{1,0:T(8,128)(2,1)S(1)} %get-tuple-element.70), channel_id=1, source_target_pairs={{0,1},{1,0},{2,3},{3,2},{4,5},{5,4},{6,7},{7,6},{8,9},{9,8},{10,11... | collective-permute-start | bytes 49160 | tf_op jit(solution)/shard_map/ppermute | solution.py:285
  13.4 1.2 %collective-permute-start.5 = (bf16[64,128]{1,0:T(8,128)(2,1)S(1)}, bf16[64,128]{1,0:T(8,128)(2,1)S(1)}, u32[]{:S(2)}, u32[]{:S(2)}) collective-permute-start(bf16[64,128]{1,0:T(8,128)(2,1)S(1)} %get-tuple-element.64), channel_id=1, source_target_pairs={{0,1},{1,0},{2,3},{3,2},{4,5},{5,4},{6,7},{7,6},{8,9},{9,8},{10,11... | collective-permute-start | bytes 49160 | tf_op jit(solution)/shard_map/ppermute | solution.py:285
  14.8 4.1 %copy-start.5 = (bf16[256,128]{1,0:T(8,128)(2,1)}, bf16[256,128]{1,0:T(8,128)(2,1)S(1)}, u32[]{:S(2)}) copy-start(bf16[256,128]{1,0:T(8,128)(2,1)S(1)} %get-tuple-element.80.refs_5_) | copy-start | bytes 196612
  14.9 5.2 %collective-permute-start.9 = (bf16[256,128]{1,0:T(8,128)(2,1)S(1)}, bf16[256,128]{1,0:T(8,128)(2,1)S(1)}, u32[]{:S(2)}, u32[]{:S(2)}) collective-permute-start(bf16[256,128]{1,0:T(8,128)(2,1)S(1)} %get-tuple-element.71), channel_id=1, source_target_pairs={{0,8},{4,12},{8,0},{12,4},{16,24},{20,28},{24,16},{28,20},{1,9},{5... | collective-permute-start | bytes 196616 | tf_op jit(solution)/shard_map/ppermute | solution.py:285
  16.7 3.2 %collective-permute-start.4 = (bf16[64,128]{1,0:T(8,128)(2,1)S(1)}, bf16[64,128]{1,0:T(8,128)(2,1)S(1)}, u32[]{:S(2)}, u32[]{:S(2)}) collective-permute-start(bf16[64,128]{1,0:T(8,128)(2,1)S(1)} %get-tuple-element.63), channel_id=1, source_target_pairs={{0,3},{1,2},{2,1},{3,0},{4,7},{5,6},{6,5},{7,4},{8,11},{9,10},{10,... | collective-permute-start | bytes 49160 | tf_op jit(solution)/shard_map/ppermute | solution.py:291
  20.1 0.6 %copy-start.7 = (bf16[256,128]{1,0:T(8,128)(2,1)}, bf16[256,128]{1,0:T(8,128)(2,1)S(1)}, u32[]{:S(2)}) copy-start(bf16[256,128]{1,0:T(8,128)(2,1)S(1)} %get-tuple-element.81.refs_6_) | copy-start | bytes 196612
  20.1 6.7 %copy-start.4 = (bf16[256,1024]{1,0:T(8,128)(2,1)S(1)}, bf16[256,1024]{1,0:T(8,128)(2,1)}, u32[]{:S(2)}) copy-start(bf16[256,1024]{1,0:T(8,128)(2,1)} %refs_4_.1) | copy-start | bytes 1572868
  20.7 6.1 %copy-start.2 = (bf16[3,1,4,2,64,64]{5,4,3,2,1,0:T(8,128)(2,1)S(1)}, bf16[3,1,4,2,64,64]{5,4,3,2,1,0:T(8,128)(2,1)}, u32[]{:S(2)}) copy-start(bf16[3,1,4,2,64,64]{5,4,3,2,1,0:T(8,128)(2,1)} %blocks_1.1) | copy-start | bytes 589828
  20.7 3.2 %collective-permute-start.10 = (bf16[64,128]{1,0:T(8,128)(2,1)S(1)}, bf16[64,128]{1,0:T(8,128)(2,1)S(1)}, u32[]{:S(2)}, u32[]{:S(2)}) collective-permute-start(bf16[64,128]{1,0:T(8,128)(2,1)S(1)} %get-tuple-element.77), channel_id=1, source_target_pairs={{0,3},{1,2},{2,1},{3,0},{4,7},{5,6},{6,5},{7,4},{8,11},{9,10},{10,... | collective-permute-start | bytes 49160 | tf_op jit(solution)/shard_map/ppermute | solution.py:291
  22.3 1.6 %collective-permute-start.11 = (bf16[64,128]{1,0:T(8,128)(2,1)S(1)}, bf16[64,128]{1,0:T(8,128)(2,1)S(1)}, u32[]{:S(2)}, u32[]{:S(2)}) collective-permute-start(bf16[64,128]{1,0:T(8,128)(2,1)S(1)} %get-tuple-element.78), channel_id=1, source_target_pairs={{0,1},{1,0},{2,3},{3,2},{4,5},{5,4},{6,7},{7,6},{8,9},{9,8},{10,11... | collective-permute-start | bytes 49160 | tf_op jit(solution)/shard_map/ppermute | solution.py:285
  23.9 2.9 %copy-start.12 = (s32[3,1,4,2]{2,3,1,0:T(2,128)S(1)}, s32[3,1,4,2]{2,3,1,0:T(2,128)}, u32[]{:S(2)}) copy-start(s32[3,1,4,2]{2,3,1,0:T(2,128)} %param.13) | copy-start | bytes 292
  24.1 7.6 %collective-permute-start.12 = (bf16[256,128]{1,0:T(8,128)(2,1)S(1)}, bf16[256,128]{1,0:T(8,128)(2,1)}, u32[]{:S(2)}, u32[]{:S(2)}) collective-permute-start(bf16[256,128]{1,0:T(8,128)(2,1)S(1)} %get-tuple-element.79.refs_0_.kept), channel_id=1, source_target_pairs={{0,16},{4,20},{8,24},{12,28},{16,0},{20,4},{24,8},{28,12},{1,17},{... | collective-permute-start | bytes 196616 | tf_op jit(solution)/shard_map/ppermute | solution.py:285
  26.9 0.8 %copy-start.6 = (bf16[256,128]{1,0:T(8,128)(2,1)S(1)}, bf16[256,128]{1,0:T(8,128)(2,1)}, u32[]{:S(2)}) copy-start(bf16[256,128]{1,0:T(8,128)(2,1)} %copy-done.5) | copy-start | bytes 196612
  27.7 0.8 %copy-start.8 = (bf16[256,128]{1,0:T(8,128)(2,1)S(1)}, bf16[256,128]{1,0:T(8,128)(2,1)}, u32[]{:S(2)}) copy-start(bf16[256,128]{1,0:T(8,128)(2,1)} %copy-done.7) | copy-start | bytes 196612
  29.8 7.2 %collective-permute-start.16 = (bf16[256,256]{1,0:T(8,128)(2,1)S(1)}, bf16[256,256]{1,0:T(8,128)(2,1)S(1)}, u32[]{:S(2)}, u32[]{:S(2)}) collective-permute-start(bf16[256,256]{1,0:T(8,128)(2,1)S(1)} %get-tuple-element.88.near), channel_id=1, source_target_pairs={{0,4},{4,0},{8,12},{12,8},{16,20},{20,16},{24,28},{28,24},{1,5},{5... | collective-permute-start | bytes 393224 | tf_op jit(solution)/shard_map/ppermute | solution.py:285
  32.7 4.3 %collective-permute-start.13 = (bf16[256,128]{1,0:T(8,128)(2,1)S(1)}, bf16[256,128]{1,0:T(8,128)(2,1)S(1)}, u32[]{:S(2)}, u32[]{:S(2)}) collective-permute-start(bf16[256,128]{1,0:T(8,128)(2,1)S(1)} %last_join.1._.refs_0_), channel_id=1, source_target_pairs={{0,2},{1,3},{2,0},{3,1},{4,6},{5,7},{6,4},{7,5},{8,10},{9,11},{10,... | collective-permute-start | bytes 196616 | tf_op jit(solution)/shard_map/ppermute | solution.py:285
  34.3 4.1 %collective-permute-start.14 = (bf16[256,128]{1,0:T(8,128)(2,1)S(1)}, bf16[256,128]{1,0:T(8,128)(2,1)S(1)}, u32[]{:S(2)}, u32[]{:S(2)}) collective-permute-start(bf16[256,128]{1,0:T(8,128)(2,1)S(1)} %last_join.1._.refs_0_), channel_id=1, source_target_pairs={{0,1},{1,0},{2,3},{3,2},{4,5},{5,4},{6,7},{7,6},{8,9},{9,8},{10,11... | collective-permute-start | bytes 196616 | tf_op jit(solution)/shard_map/ppermute | solution.py:285
  37.1 1.3 %collective-permute-start.15 = (bf16[256,128]{1,0:T(8,128)(2,1)S(1)}, bf16[256,128]{1,0:T(8,128)(2,1)S(1)}, u32[]{:S(2)}, u32[]{:S(2)}) collective-permute-start(bf16[256,128]{1,0:T(8,128)(2,1)S(1)} %collective-permute-done.13.refs_1_), channel_id=1, source_target_pairs={{0,1},{1,0},{2,3},{3,2},{4,5},{5,4},{6,7},{7,6},{8,9},{9,8},{10,11... | collective-permute-start | bytes 196616 | tf_op jit(solution)/shard_map/ppermute | solution.py:285
  38.7 5.9 %collective-permute-start.18 = (bf16[256,128]{1,0:T(8,128)(2,1)S(1)}, bf16[256,128]{1,0:T(8,128)(2,1)S(1)}, u32[]{:S(2)}, u32[]{:S(2)}) collective-permute-start(bf16[256,128]{1,0:T(8,128)(2,1)S(1)} %up.1.refs_0_), channel_id=1, source_target_pairs={{0,12},{4,8},{8,4},{12,0},{16,28},{20,24},{24,20},{28,16},{1,13},{... | collective-permute-start | bytes 196616 | tf_op jit(solution)/shard_map/ppermute | solution.py:285
  39.0 5.7 %collective-permute-start.19 = (bf16[256,128]{1,0:T(8,128)(2,1)S(1)}, bf16[256,128]{1,0:T(8,128)(2,1)S(1)}, u32[]{:S(2)}, u32[]{:S(2)}) collective-permute-start(bf16[256,128]{1,0:T(8,128)(2,1)S(1)} %up.1.refs_0_), channel_id=1, source_target_pairs={{0,4},{4,0},{8,12},{12,8},{16,20},{20,16},{24,28},{28,24},{1,5},{5... | collective-permute-start | bytes 196616 | tf_op jit(solution)/shard_map/ppermute | solution.py:285
  40.8 4.9 %collective-permute-start.17 = (bf16[256,128]{1,0:T(8,128)(2,1)S(1)}, bf16[256,128]{1,0:T(8,128)(2,1)S(1)}, u32[]{:S(2)}, u32[]{:S(2)}) collective-permute-start(bf16[256,128]{1,0:T(8,128)(2,1)S(1)} %up.1.refs_0_), channel_id=1, source_target_pairs={{0,8},{4,12},{8,0},{12,4},{16,24},{20,28},{24,16},{28,20},{1,9},{5... | collective-permute-start | bytes 196616 | tf_op jit(solution)/shard_map/ppermute | solution.py:285

commit v7 on v6

--- a/solution.py
+++ b/solution.py
@@ -12,6 +12,7 @@
 f32 = jnp.float32
 bf16 = jnp.bfloat16
 grant = 12 * 1024 * 1024
+late_cost = 4 * 10**9
 
 
 def matmul(a, b):
@@ -39,15 +40,19 @@
     return pltpu.with_memory_space_constraint(value, pltpu.HBM), pl.BlockSpec(memory_space=pltpu.HBM)
 
 
+def in_vmem(value):
+    return pltpu.with_memory_space_constraint(value, pltpu.VMEM)
+
+
 def run(body, name, outs, operands, flops=0, scratch=(), out_space=pltpu.VMEM, aliases=None):
-    arrays = [o[0] if isinstance(o, tuple) else o for o in operands]
+    arrays = [o[0] if isinstance(o, tuple) else in_vmem(o) for o in operands]
     specs = [o[1] if isinstance(o, tuple) else whole() for o in operands]
     windows = any(isinstance(o, tuple) and o[1].block_shape is not None for o in operands)
     moved = sum(a.size * a.dtype.itemsize for a in arrays)
     return pl.pallas_call(
         body,
         grid=(1,) if windows else (),
-        out_shape=outs,
+        out_shape=[out_space(o.shape, o.dtype) for o in outs],
         in_specs=specs,
         out_specs=[pl.BlockSpec(memory_space=out_space)] * len(outs),
         input_output_aliases=aliases or {},
@@ -122,8 +127,8 @@
         out_ref[pl.ds(b * size, size), :] = jnp.concatenate(line, axis=1).astype(bf16)
 
 
-def start_kernel(places, rhs, blocks, inner_ref, *refs):
-    *outers, rows, outer, pivots, sems = refs
+def start_kernel(places, rhs, blocks, *refs):
+    table, held, inner_ref, *outers, rows, outer, pivots, sems = refs
     count, size = blocks.shape[2], blocks.shape[4]
     copies = []
     for slot, which in enumerate((0, count - 1)):
@@ -131,6 +136,7 @@
         copies.append(pltpu.make_async_copy(source, rows.at[slot], sems.at[slot]))
         source = blocks.at[0, 0, which, 0]
         copies.append(pltpu.make_async_copy(source, pivots.at[slot], sems.at[2 + slot]))
+    copies.append(pltpu.make_async_copy(table, held, sems.at[4]))
     for copy in copies:
         copy.start()
     for copy in copies:
@@ -262,18 +268,18 @@
     for step in range((len(refs) - 3) // 2):
         base, up = refs[2 + 2 * step : 4 + 2 * step]
         value = base[...] + matmul(up[...], value.astype(bf16))
-    refs[-1][...] = value.astype(bf16)
-
-
-def output_kernel(places, *refs):
-    coarse, refs = refs[: len(places)], refs[len(places) :]
-    total, both = refs[:2]
-    out, sems = refs[-2 - len(places)], refs[-1]
+    for peer in range(refs[-1].shape[0]):
+        refs[-1][peer] = value.astype(bf16)
+
+
+def output_kernel(gathered, total, both, out, made, sems):
+    peers, _, width = gathered.shape
+    half = peers * width // 2
     copies = []
-    for slot, (place, value, made) in enumerate(zip(places, coarse, refs[-1 - len(places) : -1])):
-        lanes = lanes_of(place, value.shape[1])
-        made[...] = total[:, lanes] + matmul(both[...], value[...])
-        copy = pltpu.make_async_copy(made, out.at[0, :, lanes], sems.at[slot])
+    for peer in range(peers):
+        lanes = pl.ds(peer % 2 * half + peer // 2 * width, width)
+        made[peer] = total[:, lanes] + matmul(both[...], gathered[peer])
+        copy = pltpu.make_async_copy(made.at[peer], out.at[0, :, lanes], sems.at[peer])
         copy.start()
         copies.append(copy)
     for copy in copies:
@@ -307,7 +313,7 @@
     rows, fields = level_rhs.shape[1:]
     half = fields // 2
     width = half // 2
-    gcols, rcols, pcols = ((c, scalars()) for c in (galerkin_cols, restrict_cols, prolong_cols))
+    rcols, pcols = ((c, scalars()) for c in (restrict_cols, prolong_cols))
     square_shape = array((rows, rows), bf16)
     operator_shapes = [square_shape, array((rows, 2 * size), bf16), array((rows, 1), f32)]
     rmat_shape = array((rows, 2 * rows), bf16)
@@ -328,15 +334,16 @@
         return (0, far, half), (1, given, width)
 
     pairs = [(place_of(1, given), place_of(0, given)) for given in (1, 0)]
-    inner, *outers = run(
+    gcols, inner, *outers = run(
         functools.partial(start_kernel, pairs), "start",
-        [ends_shape(fields)] + [ends_shape(half)] * 2,
-        [in_hbm(level_rhs), in_hbm(galerkin_blocks)],
+        [array(galerkin_cols.shape, jnp.int32), ends_shape(fields)] + [ends_shape(half)] * 2,
+        [in_hbm(level_rhs), in_hbm(galerkin_blocks), in_hbm(galerkin_cols)],
         scratch=[
             pltpu.VMEM((2, size, fields), f32), pltpu.VMEM((size, fields), bf16),
-            pltpu.VMEM((2, size, size), bf16), pltpu.SemaphoreType.DMA((4,)),
+            pltpu.VMEM((2, size, size), bf16), pltpu.SemaphoreType.DMA((5,)),
         ],
     )
+    gcols = in_vmem(gcols), scalars()
     first = outers[0]
     outers = [swap_outer(outer) for outer in outers]
     inner = exchange(inner, "narrow", 1)
@@ -374,17 +381,17 @@
             )
             inner, outer = exchange(ends[0], "narrow", 1), swap_outer(ends[1])
             joined.append((rhs, smoothed, scale, local, rim, outer, inner))
-        anchor = joined[-1][1]
         made = []
         for operands in joined:
             value, made_base = run(
                 residual_kernel, "residual",
                 [chunk_shape, chunk_shape if level_idx == 0 else real_shape],
-                [*operands, joined[-1][-1]], flops=flops(width, 2),
+                [*operands, joined[-1][1]], flops=flops(width, 2) if not made else late_cost,
             )
             made.append(value)
             bases.append(made_base)
         sent, kept = made[:1], made[-1:]
+        anchor = made[0]
     last = levels - 1
     (other,) = (exchange(value, "wide", 1 << last) for value in sent)
     rmat, coarse_mat, near_bases, *ups = run(
@@ -419,27 +426,17 @@
     for idx in reversed(range(2, last)):
         operands += [bases[idx], ups[idx - 2]]
     (value,) = run(
-        functools.partial(up_kernel, offsets), "up", [chunk_shape], operands,
+        functools.partial(up_kernel, offsets), "up", [array((4, rows, width), bf16)], operands,
         flops=flops(width, len(offsets) + levels - 3),
     )
-    gathered = [(value, place_of(0, 0))]
-    for bits in (3, 1, 2):
-        gathered.append((exchange(value, "wide", bits), place_of(bits & 1, bits >> 1)))
-    result = None
-    for group in (gathered[:1], gathered[1:3], gathered[3:]):
-        operands = [value for value, _ in group] + [total, both]
-        aliases = {}
-        if result is not None:
-            aliases[len(operands)] = 0
-            operands.append(in_hbm(result))
-        (result,) = run(
-            functools.partial(output_kernel, tuple(place for _, place in group)),
-            "output", [array((1, rows, fields), f32)], operands,
-            flops=flops(width, len(group)),
-            scratch=[pltpu.VMEM((rows, width), f32)] * len(group)
-            + [pltpu.SemaphoreType.DMA((len(group),))],
-            out_space=pltpu.HBM, aliases=aliases,
-        )
+    peers = 4
+    groups = [list(range(i, i + peers)) for i in range(0, lax.axis_size("wide"), peers)]
+    gathered = lax.all_to_all(value, "wide", 0, 0, axis_index_groups=groups)
+    (result,) = run(
+        output_kernel, "output", [array((1, rows, fields), f32)], [gathered, total, both],
+        flops=flops(fields), out_space=pltpu.HBM,
+        scratch=[pltpu.VMEM((peers, rows, width), f32), pltpu.SemaphoreType.DMA((peers,))],
+    )
     return result
 
 

time: 46.9 us -> 48.5 us (1.034)
  blocking collectives: 0 us -> 9.3 us
  starting transfers between devices: 22.7 us -> 18.6 us
  waiting for transfers between devices: 7.74 us -> 5.65 us
  Pallas kernels: 12.8 us -> 11.2 us
    all_to_all x0 -> x1, blocking collectives: none -> 9.3 us  [on_device(): gathered = lax.all_to_all(value, 'wide', 0, 0, axis_index_groups=groups)]
    ppermute x15 -> x12, starting transfers between devices: 16.2 us -> 13.4 us  [exchange(): return lax.ppermute(value, axis, [(i, i ^ bit) for i in range(count)])]
    pallas_call x19 -> x17, Pallas kernels: 12.8 us -> 11.2 us  [run(): pl.pallas_call(body, grid=(1,) if windows else (), out_shape=[out_space(o...]
    ppermute x15 -> x12, waiting for transfers between devices: 4.69 us -> 3.37 us  [exchange(): return lax.ppermute(value, axis, [(i, i ^ bit) for i in range(count)])]
    ppermute x5, starting transfers between devices: 6.52 us -> 5.22 us  [swap_outer(): return lax.ppermute(outer, 'narrow', gaps)]
    ppermute x5, waiting for transfers between devices: 3.05 us -> 2.28 us  [swap_outer(): return lax.ppermute(outer, 'narrow', gaps)]
    unnamed x28 -> x24, local copies, waits for them, and re-layouts: 2.98 us -> 3.15 us
  transfers between devices with their start and end apart: 20 -> 17, of which waited for: 8 -> 4; matrix products, arithmetic and copies ran while one was open for 0% -> 0% of each run, Pallas kernels for 21% -> 17%
where the time goes in v7:
time: 48.5 us; the launch traced here: 48.2 us
  starting transfers between devices  18.6 us (38%)
  Pallas kernels  11.2 us (23%)
  blocking collectives  9.3 us (19%)
  waiting for transfers between devices  5.65 us (12%)
  local copies, waits for them, and re-layouts  3.15 us (6%)
    ppermute x12, starting transfers between devices, exchange(): return lax.ppermute(value, axis, [(i, i ^ bit) for i in range(count)])  13.4 us
    pallas_call x17, Pallas kernels, run(): pl.pallas_call(body, grid=(1,) if windows else (), out_shape=[out_space(o...  11.2 us
    all_to_all x1, blocking collectives, on_device(): gathered = lax.all_to_all(value, 'wide', 0, 0, axis_index_groups=groups)  9.3 us
    ppermute x5, starting transfers between devices, swap_outer(): return lax.ppermute(outer, 'narrow', gaps)  5.22 us
    ppermute x12, waiting for transfers between devices, exchange(): return lax.ppermute(value, axis, [(i, i ^ bit) for i in range(count)])  3.37 us
    unnamed x24, local copies, waits for them, and re-layouts  3.15 us
    ppermute x5, waiting for transfers between devices, swap_outer(): return lax.ppermute(outer, 'narrow', gaps)  2.28 us
  transfers between devices with their start and end apart: 17, of which 4 were waited for; matrix products, arithmetic and copies ran while one was open for 0% of the time, Pallas kernels for 17%

profile of v7, /device:TPU:0, one launch (start us, length us, event | category | flops | bytes accessed | tf_op | source)
XLA Modules:
  0.0 48.2 jit_solution(7304634539960747325)
XLA Ops:
  0.0 1.3 %start.1 = (s32[3,1,4,5]{3,2,1,0:T(4,128)S(1)}, bf16[64,512]{1,0:T(8,128)(2,1)S(1)}, bf16[64,256]{1,0:T(8,128)(2,1)S(1)}, bf16[64,256]{1,0:T(8,128)(2,1)S(1)}) custom-call(f32[1,256,512]{2,1,0:T(8,128)} %rhs.3, bf16[3,1,4,5,64,64]{5,4,3,2,1,0:T(8,128)(2,1)} %blocks.7, s32[3,1,4,5]{3,2,1,0:T(4,128)} %refs_0_.1), custom_call_target="tpu_custom_call" | custom-call | bytes 1016048 | tf_op jit(solution)/shard_map/start/pallas_call | solution.py:52
  1.3 0.5 %collective-permute-start.1 = (bf16[64,512]{1,0:T(8,128)(2,1)S(1)}, bf16[64,512]{1,0:T(8,128)(2,1)S(1)}, u32[]{:S(2)}, u32[]{:S(2)}) collective-permute-start(bf16[64,512]{1,0:T(8,128)(2,1)S(1)} %get-tuple-element.53), channel_id=1, source_target_pairs={{0,1},{1,0},{2,3},{3,2},{4,5},{5,4},{6,7},{7,6},{8,9},{9,8},{10,11... | collective-permute-start | bytes 196616 | tf_op jit(solution)/shard_map/ppermute | solution.py:291
  1.8 2.6 %collective-permute-start = (bf16[64,256]{1,0:T(8,128)(2,1)S(1)}, bf16[64,256]{1,0:T(8,128)(2,1)S(1)}, u32[]{:S(2)}, u32[]{:S(2)}) collective-permute-start(bf16[64,256]{1,0:T(8,128)(2,1)S(1)} %get-tuple-element.49._), channel_id=1, source_target_pairs={{0,3},{1,2},{2,1},{3,0},{4,7},{5,6},{6,5},{7,4},{8,11},{9,10},{10,... | collective-permute-start | bytes 98312 | tf_op jit(solution)/shard_map/ppermute | solution.py:297
  4.4 0.0 collective-permute-start.5
  4.5 1.1 %first_local.1 = (f32[256,512]{1,0:T(8,128)S(1)}, f32[256,512]{1,0:T(8,128)S(1)}, bf16[256,256]{1,0:T(8,128)(2,1)S(1)}, bf16[256,128]{1,0:T(8,128)(2,1)S(1)}, f32[256,1]{1,0:T(8,128)S(1)}) custom-call(f32[1,256,512]{2,1,0:T(8,128)S(1)} %copy-done.3, bf16[64,256]{1,0:T(8,128)(2,1)S(1)} %get-tuple-element.49._, s32[3,1,4,5]{3,2,1,0:T(4,128)S(1)} %get-tuple-element.50.cols, ...), custom_call_target="tpu_custom_call" | custom-call | flops 67108864 | bytes 1048816 | tf_op jit(solution)/shard_map/first_local/pallas_call | solution.py:52
  5.6 0.5 %collective-permute-done.outer = bf16[64,256]{1,0:T(8,128)(2,1)S(1)} collective-permute-done((bf16[64,256]{1,0:T(8,128)(2,1)S(1)}, bf16[64,256]{1,0:T(8,128)(2,1)S(1)}, u32[]{:S(2)}, u32[]{:S(2)}) %collective-permute-start) | collective-permute-done | bytes 32800 | tf_op jit(solution)/shard_map/ppermute | solution.py:297
  6.1 0.2 first_residual.2
  6.3 1.7 %collective-permute-start.2 = (bf16[256,128]{1,0:T(8,128)(2,1)S(1)}, bf16[256,128]{1,0:T(8,128)(2,1)S(1)}, u32[]{:S(2)}, u32[]{:S(2)}) collective-permute-start(bf16[256,128]{1,0:T(8,128)(2,1)S(1)} %get-tuple-element.54._), channel_id=1, source_target_pairs={{0,4},{4,0},{8,12},{12,8},{16,20},{20,16},{24,28},{28,24},{1,5},{5... | collective-permute-start | bytes 196616 | tf_op jit(solution)/shard_map/ppermute | solution.py:291
  8.0 0.2 first_residual.3
  8.2 1.4 %collective-permute-start.6 = (bf16[256,128]{1,0:T(8,128)(2,1)S(1)}, bf16[256,128]{1,0:T(8,128)(2,1)S(1)}, u32[]{:S(2)}, u32[]{:S(2)}) collective-permute-start(bf16[256,128]{1,0:T(8,128)(2,1)S(1)} %get-tuple-element.66), channel_id=1, source_target_pairs={{0,4},{4,0},{8,12},{12,8},{16,20},{20,16},{24,28},{28,24},{1,5},{5... | collective-permute-start | bytes 196616 | tf_op jit(solution)/shard_map/ppermute | solution.py:291
  9.6 0.1 copy.9.rcols.refs_1_
  9.8 1.1 %operators.2 = (bf16[256,512]{1,0:T(8,128)(2,1)S(1)}, bf16[256,256]{1,0:T(8,128)(2,1)S(1)}, bf16[256,128]{1,0:T(8,128)(2,1)S(1)}, f32[256,1]{1,0:T(8,128)S(1)}) custom-call(bf16[256,128]{1,0:T(8,128)(2,1)S(1)} %get-tuple-element.54._, s32[3,1,4,3]{3,2,1,0:T(4,128)S(1)} %copy.9.rcols.refs_1_, bf16[3,1,4,3,64,64]{5,4,3,2,1,0:T(8,128)(2,1)S(1)} %copy-done.1, ...), custom_call_target="tpu_custom_call" | custom-call | bytes 852352 | tf_op jit(solution)/shard_map/operators/pallas_call | solution.py:52
  10.9 0.0 collective-permute-done.2.other
  10.9 0.2 join.3
  11.1 1.5 %collective-permute-start.3 = (bf16[64,128]{1,0:T(8,128)(2,1)S(1)}, bf16[64,128]{1,0:T(8,128)(2,1)S(1)}, u32[]{:S(2)}, u32[]{:S(2)}) collective-permute-start(bf16[64,128]{1,0:T(8,128)(2,1)S(1)} %get-tuple-element.62), channel_id=1, source_target_pairs={{0,3},{1,2},{2,1},{3,0},{4,7},{5,6},{6,5},{7,4},{8,11},{9,10},{10,... | collective-permute-start | bytes 49160 | tf_op jit(solution)/shard_map/ppermute | solution.py:297
  12.6 0.6 %collective-permute-start.4 = (bf16[64,128]{1,0:T(8,128)(2,1)S(1)}, bf16[64,128]{1,0:T(8,128)(2,1)S(1)}, u32[]{:S(2)}, u32[]{:S(2)}) collective-permute-start(bf16[64,128]{1,0:T(8,128)(2,1)S(1)} %get-tuple-element.63), channel_id=1, source_target_pairs={{0,1},{1,0},{2,3},{3,2},{4,5},{5,4},{6,7},{7,6},{8,9},{9,8},{10,11... | collective-permute-start | bytes 49160 | tf_op jit(solution)/shard_map/ppermute | solution.py:291
  13.2 0.0 collective-permute-done.6.other
  13.2 0.2 join.4
  13.4 0.8 %collective-permute-start.7 = (bf16[64,128]{1,0:T(8,128)(2,1)S(1)}, bf16[64,128]{1,0:T(8,128)(2,1)S(1)}, u32[]{:S(2)}, u32[]{:S(2)}) collective-permute-start(bf16[64,128]{1,0:T(8,128)(2,1)S(1)} %get-tuple-element.71), channel_id=1, source_target_pairs={{0,3},{1,2},{2,1},{3,0},{4,7},{5,6},{6,5},{7,4},{8,11},{9,10},{10,... | collective-permute-start | bytes 49160 | tf_op jit(solution)/shard_map/ppermute | solution.py:297
  14.2 0.6 %collective-permute-start.8 = (bf16[64,128]{1,0:T(8,128)(2,1)S(1)}, bf16[64,128]{1,0:T(8,128)(2,1)S(1)}, u32[]{:S(2)}, u32[]{:S(2)}) collective-permute-start(bf16[64,128]{1,0:T(8,128)(2,1)S(1)} %get-tuple-element.72), channel_id=1, source_target_pairs={{0,1},{1,0},{2,3},{3,2},{4,5},{5,4},{6,7},{7,6},{8,9},{9,8},{10,11... | collective-permute-start | bytes 49160 | tf_op jit(solution)/shard_map/ppermute | solution.py:291
  14.9 0.2 residual.3
  15.1 0.0 copy-start.5
  15.1 0.6 %copy-done.5 = bf16[256,128]{1,0:T(8,128)(2,1)} copy-done((bf16[256,128]{1,0:T(8,128)(2,1)}, bf16[256,128]{1,0:T(8,128)(2,1)S(1)}, u32[]{:S(2)}) %copy-start.5) | copy-done | bytes 65560
  15.7 1.6 %collective-permute-start.9 = (bf16[256,128]{1,0:T(8,128)(2,1)S(1)}, bf16[256,128]{1,0:T(8,128)(2,1)S(1)}, u32[]{:S(2)}, u32[]{:S(2)}) collective-permute-start(bf16[256,128]{1,0:T(8,128)(2,1)S(1)} %get-tuple-element.68._), channel_id=1, source_target_pairs={{0,8},{4,12},{8,0},{12,4},{16,24},{20,28},{24,16},{28,20},{1,9},{5... | collective-permute-start | bytes 196616 | tf_op jit(solution)/shard_map/ppermute | solution.py:291
  17.3 0.2 residual.4
  17.5 0.6 %copy-done.7 = bf16[256,128]{1,0:T(8,128)(2,1)} copy-done((bf16[256,128]{1,0:T(8,128)(2,1)}, bf16[256,128]{1,0:T(8,128)(2,1)S(1)}, u32[]{:S(2)}) %copy-start.7) | copy-done | bytes 65560
  18.2 1.1 %operators.3 = (bf16[256,512]{1,0:T(8,128)(2,1)S(1)}, bf16[256,256]{1,0:T(8,128)(2,1)S(1)}, bf16[256,128]{1,0:T(8,128)(2,1)S(1)}, f32[256,1]{1,0:T(8,128)S(1)}) custom-call(bf16[256,128]{1,0:T(8,128)(2,1)S(1)} %get-tuple-element.68._, s32[3,1,4,3]{3,2,1,0:T(4,128)S(1)} %copy.9.rcols.refs_1_, bf16[3,1,4,3,64,64]{5,4,3,2,1,0:T(8,128)(2,1)S(1)} %copy-done.1, ...), custom_call_target="tpu_custom_call" | custom-call | bytes 852352 | tf_op jit(solution)/shard_map/operators/pallas_call | solution.py:52
  19.3 0.7 %collective-permute-done.9.other = bf16[256,128]{1,0:T(8,128)(2,1)S(1)} collective-permute-done((bf16[256,128]{1,0:T(8,128)(2,1)S(1)}, bf16[256,128]{1,0:T(8,128)(2,1)S(1)}, u32[]{:S(2)}, u32[]{:S(2)}) %collective-permute-start.9) | collective-permute-done | bytes 65568 | tf_op jit(solution)/shard_map/ppermute | solution.py:291
  20.0 0.2 join.5
  20.2 0.0 copy-start.2
  20.2 0.3 collective-permute-start.10
  20.5 1.3 %collective-permute-start.11 = (bf16[64,128]{1,0:T(8,128)(2,1)S(1)}, bf16[64,128]{1,0:T(8,128)(2,1)S(1)}, u32[]{:S(2)}, u32[]{:S(2)}) collective-permute-start(bf16[64,128]{1,0:T(8,128)(2,1)S(1)} %get-tuple-element.80), channel_id=1, source_target_pairs={{0,1},{1,0},{2,3},{3,2},{4,5},{5,4},{6,7},{7,6},{8,9},{9,8},{10,11... | collective-permute-start | bytes 49160 | tf_op jit(solution)/shard_map/ppermute | solution.py:291
  21.8 1.8 %collective-permute-done.10.outer = bf16[64,128]{1,0:T(8,128)(2,1)S(1)} collective-permute-done((bf16[64,128]{1,0:T(8,128)(2,1)S(1)}, bf16[64,128]{1,0:T(8,128)(2,1)S(1)}, u32[]{:S(2)}, u32[]{:S(2)}) %collective-permute-start.10) | collective-permute-done | bytes 16416 | tf_op jit(solution)/shard_map/ppermute | solution.py:297
  23.6 0.2 residual.5
  23.8 2.7 %collective-permute-start.12 = (bf16[256,128]{1,0:T(8,128)(2,1)S(1)}, bf16[256,128]{1,0:T(8,128)(2,1)}, u32[]{:S(2)}, u32[]{:S(2)}) collective-permute-start(bf16[256,128]{1,0:T(8,128)(2,1)S(1)} %get-tuple-element.81.refs_0_.kept), channel_id=1, source_target_pairs={{0,16},{4,20},{8,24},{12,28},{16,0},{20,4},{24,8},{28,12},{1,17},{... | collective-permute-start | bytes 196616 | tf_op jit(solution)/shard_map/ppermute | solution.py:291
  26.5 0.1 copy.12.refs_3_.pcols
  26.6 0.8 %copy-done.6 = bf16[256,128]{1,0:T(8,128)(2,1)S(1)} copy-done((bf16[256,128]{1,0:T(8,128)(2,1)S(1)}, bf16[256,128]{1,0:T(8,128)(2,1)}, u32[]{:S(2)}) %copy-start.6) | copy-done | bytes 65560
  27.4 0.8 %copy-done.8 = bf16[256,128]{1,0:T(8,128)(2,1)S(1)} copy-done((bf16[256,128]{1,0:T(8,128)(2,1)S(1)}, bf16[256,128]{1,0:T(8,128)(2,1)}, u32[]{:S(2)}) %copy-start.8) | copy-done | bytes 65560
  28.3 1.3 %coarse_operators.1 = (bf16[256,512]{1,0:T(8,128)(2,1)S(1)}, bf16[256,1024]{1,0:T(8,128)(2,1)S(1)}, bf16[256,256]{1,0:T(8,128)(2,1)S(1)}) custom-call(bf16[256,128]{1,0:T(8,128)(2,1)S(1)} %get-tuple-element.81.refs_0_.kept, s32[3,1,4,3]{3,2,1,0:T(4,128)S(1)} %copy.9.rcols.refs_1_, bf16[3,1,4,3,64,64]{5,4,3,2,1,0:T(8,128)(2,1)S(1)} %copy-done.1, ...), custom_call_target="tpu_custom_call" | custom-call | flops 201326592 | bytes 1344752 | tf_op jit(solution)/shard_map/coarse_operators/pallas_call | solution.py:52
  29.5 1.3 %collective-permute-start.16 = (bf16[256,256]{1,0:T(8,128)(2,1)S(1)}, bf16[256,256]{1,0:T(8,128)(2,1)S(1)}, u32[]{:S(2)}, u32[]{:S(2)}) collective-permute-start(bf16[256,256]{1,0:T(8,128)(2,1)S(1)} %get-tuple-element.90.near), channel_id=1, source_target_pairs={{0,4},{4,0},{8,12},{12,8},{16,20},{20,16},{24,28},{28,24},{1,5},{5... | collective-permute-start | bytes 393224 | tf_op jit(solution)/shard_map/ppermute | solution.py:291
  30.8 1.0 %last_join.1._.refs_0_ = bf16[256,128]{1,0:T(8,128)(2,1)S(1)} custom-call(bf16[256,512]{1,0:T(8,128)(2,1)S(1)} %get-tuple-element.85.rmat, bf16[256,128]{1,0:T(8,128)(2,1)S(1)} %get-tuple-element.81.refs_0_.kept, bf16[256,128]{1,0:T(8,128)(2,1)} %collective-permute-done.12.other), custom_call_target="tpu_custom_call" | custom-call | flops 33554432 | bytes 393216 | tf_op jit(solution)/shard_map/last_join/pallas_call | solution.py:52
  31.9 1.7 %collective-permute-start.13 = (bf16[256,128]{1,0:T(8,128)(2,1)S(1)}, bf16[256,128]{1,0:T(8,128)(2,1)S(1)}, u32[]{:S(2)}, u32[]{:S(2)}) collective-permute-start(bf16[256,128]{1,0:T(8,128)(2,1)S(1)} %last_join.1._.refs_0_), channel_id=1, source_target_pairs={{0,2},{1,3},{2,0},{3,1},{4,6},{5,7},{6,4},{7,5},{8,10},{9,11},{10,... | collective-permute-start | bytes 196616 | tf_op jit(solution)/shard_map/ppermute | solution.py:291
  33.6 0.0 collective-permute-start.14
  33.6 2.6 %collective-permute-done.13.refs_1_ = bf16[256,128]{1,0:T(8,128)(2,1)S(1)} collective-permute-done((bf16[256,128]{1,0:T(8,128)(2,1)S(1)}, bf16[256,128]{1,0:T(8,128)(2,1)S(1)}, u32[]{:S(2)}, u32[]{:S(2)}) %collective-permute-start.13) | collective-permute-done | bytes 65568 | tf_op jit(solution)/shard_map/ppermute | solution.py:291
  36.2 1.3 %fine_operators.1 = (bf16[256,256]{1,0:T(8,128)(2,1)S(1)}, f32[256,512]{1,0:T(8,128)S(1)}) custom-call(bf16[256,128]{1,0:T(8,128)(2,1)S(1)} %last_join.1._.refs_0_, s32[3,1,4,2]{3,2,1,0:T(4,128)S(1)} %copy.12.refs_3_.pcols, bf16[3,1,4,2,64,64]{5,4,3,2,1,0:T(8,128)(2,1)S(1)} %copy-done.2, bf16[3,1,4,2,64,64]{5,4,3,2,1,0:T(8,128)(2,1)S(1)} %copy-done.2, ...), custom_call_target="tpu_custom_call" | custom-call | flops 167772160 | bytes 1509472 | tf_op jit(solution)/shard_map/fine_operators/pallas_call | solution.py:52
  37.5 0.3 up.1
  37.8 9.3 %all_to_all.5.gathered = bf16[4,256,128]{2,1,0:T(8,128)(2,1)S(1)} all-to-all(bf16[4,256,128]{2,1,0:T(8,128)(2,1)S(1)} %up.1), channel_id=1, replica_groups={{0,4,8,12},{16,20,24,28},{1,5,9,13},{17,21,25,29},{2,6,10,14},{18,22,26..., dimensions={0} | all-to-all | bytes 524288 | tf_op jit(solution)/shard_map/all_to_all | solution.py:434
  47.1 1.0 %output.1 = f32[1,256,512]{2,1,0:T(8,128)} custom-call(bf16[4,256,128]{2,1,0:T(8,128)(2,1)S(1)} %all_to_all.5.gathered, f32[256,512]{1,0:T(8,128)S(1)} %get-tuple-element.92.total, bf16[256,256]{1,0:T(8,128)(2,1)S(1)} %get-tuple-element.91.refs_5_.both), custom_call_target="tpu_custom_call" | custom-call | flops 67108864 | bytes 917504 | tf_op jit(solution)/shard_map/output/pallas_call | solution.py:52
  (28 shorter events, 0.1 us)
Async XLA Ops:
  0.0 4.4 %copy-start = (bf16[3,1,4,5,64,64]{5,4,3,2,1,0:T(8,128)(2,1)S(1)}, bf16[3,1,4,5,64,64]{5,4,3,2,1,0:T(8,128)(2,1)}, u32[]{:S(2)}) copy-start(bf16[3,1,4,5,64,64]{5,4,3,2,1,0:T(8,128)(2,1)} %blocks.7) | copy-start | bytes 1474564
  0.0 4.4 %copy-start.3 = (f32[1,256,512]{2,1,0:T(8,128)S(1)}, f32[1,256,512]{2,1,0:T(8,128)}, u32[]{:S(2)}) copy-start(f32[1,256,512]{2,1,0:T(8,128)} %rhs.3) | copy-start | bytes 1572868
  1.3 4.8 %collective-permute-start.1 = (bf16[64,512]{1,0:T(8,128)(2,1)S(1)}, bf16[64,512]{1,0:T(8,128)(2,1)S(1)}, u32[]{:S(2)}, u32[]{:S(2)}) collective-permute-start(bf16[64,512]{1,0:T(8,128)(2,1)S(1)} %get-tuple-element.53), channel_id=1, source_target_pairs={{0,1},{1,0},{2,3},{3,2},{4,5},{5,4},{6,7},{7,6},{8,9},{9,8},{10,11... | collective-permute-start | bytes 196616 | tf_op jit(solution)/shard_map/ppermute | solution.py:291
  1.8 4.3 %collective-permute-start = (bf16[64,256]{1,0:T(8,128)(2,1)S(1)}, bf16[64,256]{1,0:T(8,128)(2,1)S(1)}, u32[]{:S(2)}, u32[]{:S(2)}) collective-permute-start(bf16[64,256]{1,0:T(8,128)(2,1)S(1)} %get-tuple-element.49._), channel_id=1, source_target_pairs={{0,3},{1,2},{2,1},{3,0},{4,7},{5,6},{6,5},{7,4},{8,11},{9,10},{10,... | collective-permute-start | bytes 98312 | tf_op jit(solution)/shard_map/ppermute | solution.py:297
  4.4 3.6 %collective-permute-start.5 = (bf16[64,256]{1,0:T(8,128)(2,1)S(1)}, bf16[64,256]{1,0:T(8,128)(2,1)S(1)}, u32[]{:S(2)}, u32[]{:S(2)}) collective-permute-start(bf16[64,256]{1,0:T(8,128)(2,1)S(1)} %get-tuple-element.64), channel_id=1, source_target_pairs={{0,3},{1,2},{2,1},{3,0},{4,7},{5,6},{6,5},{7,4},{8,11},{9,10},{10,... | collective-permute-start | bytes 98312 | tf_op jit(solution)/shard_map/ppermute | solution.py:297
  6.1 3.7 %copy-start.1 = (bf16[3,1,4,3,64,64]{5,4,3,2,1,0:T(8,128)(2,1)S(1)}, bf16[3,1,4,3,64,64]{5,4,3,2,1,0:T(8,128)(2,1)}, u32[]{:S(2)}) copy-start(bf16[3,1,4,3,64,64]{5,4,3,2,1,0:T(8,128)(2,1)} %refs_2_.1) | copy-start | bytes 884740
  6.3 4.6 %collective-permute-start.2 = (bf16[256,128]{1,0:T(8,128)(2,1)S(1)}, bf16[256,128]{1,0:T(8,128)(2,1)S(1)}, u32[]{:S(2)}, u32[]{:S(2)}) collective-permute-start(bf16[256,128]{1,0:T(8,128)(2,1)S(1)} %get-tuple-element.54._), channel_id=1, source_target_pairs={{0,4},{4,0},{8,12},{12,8},{16,20},{20,16},{24,28},{28,24},{1,5},{5... | collective-permute-start | bytes 196616 | tf_op jit(solution)/shard_map/ppermute | solution.py:291
  8.0 1.6 %copy-start.9 = (s32[3,1,4,3]{2,1,3,0:T(1,128)S(1)}, s32[3,1,4,3]{2,1,3,0:T(1,128)}, u32[]{:S(2)}) copy-start(s32[3,1,4,3]{2,1,3,0:T(1,128)} %param.11) | copy-start | bytes 436
  8.2 5.0 %collective-permute-start.6 = (bf16[256,128]{1,0:T(8,128)(2,1)S(1)}, bf16[256,128]{1,0:T(8,128)(2,1)S(1)}, u32[]{:S(2)}, u32[]{:S(2)}) collective-permute-start(bf16[256,128]{1,0:T(8,128)(2,1)S(1)} %get-tuple-element.66), channel_id=1, source_target_pairs={{0,4},{4,0},{8,12},{12,8},{16,20},{20,16},{24,28},{28,24},{1,5},{5... | collective-permute-start | bytes 196616 | tf_op jit(solution)/shard_map/ppermute | solution.py:291
  11.1 3.8 %collective-permute-start.3 = (bf16[64,128]{1,0:T(8,128)(2,1)S(1)}, bf16[64,128]{1,0:T(8,128)(2,1)S(1)}, u32[]{:S(2)}, u32[]{:S(2)}) collective-permute-start(bf16[64,128]{1,0:T(8,128)(2,1)S(1)} %get-tuple-element.62), channel_id=1, source_target_pairs={{0,3},{1,2},{2,1},{3,0},{4,7},{5,6},{6,5},{7,4},{8,11},{9,10},{10,... | collective-permute-start | bytes 49160 | tf_op jit(solution)/shard_map/ppermute | solution.py:297
  12.6 2.3 %collective-permute-start.4 = (bf16[64,128]{1,0:T(8,128)(2,1)S(1)}, bf16[64,128]{1,0:T(8,128)(2,1)S(1)}, u32[]{:S(2)}, u32[]{:S(2)}) collective-permute-start(bf16[64,128]{1,0:T(8,128)(2,1)S(1)} %get-tuple-element.63), channel_id=1, source_target_pairs={{0,1},{1,0},{2,3},{3,2},{4,5},{5,4},{6,7},{7,6},{8,9},{9,8},{10,11... | collective-permute-start | bytes 49160 | tf_op jit(solution)/shard_map/ppermute | solution.py:291
  13.4 3.9 %collective-permute-start.7 = (bf16[64,128]{1,0:T(8,128)(2,1)S(1)}, bf16[64,128]{1,0:T(8,128)(2,1)S(1)}, u32[]{:S(2)}, u32[]{:S(2)}) collective-permute-start(bf16[64,128]{1,0:T(8,128)(2,1)S(1)} %get-tuple-element.71), channel_id=1, source_target_pairs={{0,3},{1,2},{2,1},{3,0},{4,7},{5,6},{6,5},{7,4},{8,11},{9,10},{10,... | collective-permute-start | bytes 49160 | tf_op jit(solution)/shard_map/ppermute | solution.py:297
  14.2 3.1 %collective-permute-start.8 = (bf16[64,128]{1,0:T(8,128)(2,1)S(1)}, bf16[64,128]{1,0:T(8,128)(2,1)S(1)}, u32[]{:S(2)}, u32[]{:S(2)}) collective-permute-start(bf16[64,128]{1,0:T(8,128)(2,1)S(1)} %get-tuple-element.72), channel_id=1, source_target_pairs={{0,1},{1,0},{2,3},{3,2},{4,5},{5,4},{6,7},{7,6},{8,9},{9,8},{10,11... | collective-permute-start | bytes 49160 | tf_op jit(solution)/shard_map/ppermute | solution.py:291
  15.1 0.6 %copy-start.5 = (bf16[256,128]{1,0:T(8,128)(2,1)}, bf16[256,128]{1,0:T(8,128)(2,1)S(1)}, u32[]{:S(2)}) copy-start(bf16[256,128]{1,0:T(8,128)(2,1)S(1)} %get-tuple-element.82.refs_5_) | copy-start | bytes 196612
  15.7 4.3 %collective-permute-start.9 = (bf16[256,128]{1,0:T(8,128)(2,1)S(1)}, bf16[256,128]{1,0:T(8,128)(2,1)S(1)}, u32[]{:S(2)}, u32[]{:S(2)}) collective-permute-start(bf16[256,128]{1,0:T(8,128)(2,1)S(1)} %get-tuple-element.68._), channel_id=1, source_target_pairs={{0,8},{4,12},{8,0},{12,4},{16,24},{20,28},{24,16},{28,20},{1,9},{5... | collective-permute-start | bytes 196616 | tf_op jit(solution)/shard_map/ppermute | solution.py:291
  17.5 0.6 %copy-start.7 = (bf16[256,128]{1,0:T(8,128)(2,1)}, bf16[256,128]{1,0:T(8,128)(2,1)S(1)}, u32[]{:S(2)}) copy-start(bf16[256,128]{1,0:T(8,128)(2,1)S(1)} %get-tuple-element.83.refs_6_) | copy-start | bytes 196612
  20.0 6.6 %copy-start.4 = (bf16[256,1024]{1,0:T(8,128)(2,1)S(1)}, bf16[256,1024]{1,0:T(8,128)(2,1)}, u32[]{:S(2)}) copy-start(bf16[256,1024]{1,0:T(8,128)(2,1)} %refs_4_.1) | copy-start | bytes 1572868
  20.2 6.4 %copy-start.2 = (bf16[3,1,4,2,64,64]{5,4,3,2,1,0:T(8,128)(2,1)S(1)}, bf16[3,1,4,2,64,64]{5,4,3,2,1,0:T(8,128)(2,1)}, u32[]{:S(2)}) copy-start(bf16[3,1,4,2,64,64]{5,4,3,2,1,0:T(8,128)(2,1)} %blocks_1.1) | copy-start | bytes 589828
  20.2 3.3 %collective-permute-start.10 = (bf16[64,128]{1,0:T(8,128)(2,1)S(1)}, bf16[64,128]{1,0:T(8,128)(2,1)S(1)}, u32[]{:S(2)}, u32[]{:S(2)}) collective-permute-start(bf16[64,128]{1,0:T(8,128)(2,1)S(1)} %get-tuple-element.79), channel_id=1, source_target_pairs={{0,3},{1,2},{2,1},{3,0},{4,7},{5,6},{6,5},{7,4},{8,11},{9,10},{10,... | collective-permute-start | bytes 49160 | tf_op jit(solution)/shard_map/ppermute | solution.py:297
  20.5 3.1 %collective-permute-start.11 = (bf16[64,128]{1,0:T(8,128)(2,1)S(1)}, bf16[64,128]{1,0:T(8,128)(2,1)S(1)}, u32[]{:S(2)}, u32[]{:S(2)}) collective-permute-start(bf16[64,128]{1,0:T(8,128)(2,1)S(1)} %get-tuple-element.80), channel_id=1, source_target_pairs={{0,1},{1,0},{2,3},{3,2},{4,5},{5,4},{6,7},{7,6},{8,9},{9,8},{10,11... | collective-permute-start | bytes 49160 | tf_op jit(solution)/shard_map/ppermute | solution.py:291
  23.6 2.9 %copy-start.10 = (s32[3,1,4,2]{2,3,1,0:T(2,128)S(1)}, s32[3,1,4,2]{2,3,1,0:T(2,128)}, u32[]{:S(2)}) copy-start(s32[3,1,4,2]{2,3,1,0:T(2,128)} %param.13) | copy-start | bytes 292
  23.8 7.0 %collective-permute-start.12 = (bf16[256,128]{1,0:T(8,128)(2,1)S(1)}, bf16[256,128]{1,0:T(8,128)(2,1)}, u32[]{:S(2)}, u32[]{:S(2)}) collective-permute-start(bf16[256,128]{1,0:T(8,128)(2,1)S(1)} %get-tuple-element.81.refs_0_.kept), channel_id=1, source_target_pairs={{0,16},{4,20},{8,24},{12,28},{16,0},{20,4},{24,8},{28,12},{1,17},{... | collective-permute-start | bytes 196616 | tf_op jit(solution)/shard_map/ppermute | solution.py:291
  26.6 0.8 %copy-start.6 = (bf16[256,128]{1,0:T(8,128)(2,1)S(1)}, bf16[256,128]{1,0:T(8,128)(2,1)}, u32[]{:S(2)}) copy-start(bf16[256,128]{1,0:T(8,128)(2,1)} %copy-done.5) | copy-start | bytes 196612
  27.4 0.8 %copy-start.8 = (bf16[256,128]{1,0:T(8,128)(2,1)S(1)}, bf16[256,128]{1,0:T(8,128)(2,1)}, u32[]{:S(2)}) copy-start(bf16[256,128]{1,0:T(8,128)(2,1)} %copy-done.7) | copy-start | bytes 196612
  29.5 6.7 %collective-permute-start.16 = (bf16[256,256]{1,0:T(8,128)(2,1)S(1)}, bf16[256,256]{1,0:T(8,128)(2,1)S(1)}, u32[]{:S(2)}, u32[]{:S(2)}) collective-permute-start(bf16[256,256]{1,0:T(8,128)(2,1)S(1)} %get-tuple-element.90.near), channel_id=1, source_target_pairs={{0,4},{4,0},{8,12},{12,8},{16,20},{20,16},{24,28},{28,24},{1,5},{5... | collective-permute-start | bytes 393224 | tf_op jit(solution)/shard_map/ppermute | solution.py:291
  31.9 4.3 %collective-permute-start.13 = (bf16[256,128]{1,0:T(8,128)(2,1)S(1)}, bf16[256,128]{1,0:T(8,128)(2,1)S(1)}, u32[]{:S(2)}, u32[]{:S(2)}) collective-permute-start(bf16[256,128]{1,0:T(8,128)(2,1)S(1)} %last_join.1._.refs_0_), channel_id=1, source_target_pairs={{0,2},{1,3},{2,0},{3,1},{4,6},{5,7},{6,4},{7,5},{8,10},{9,11},{10,... | collective-permute-start | bytes 196616 | tf_op jit(solution)/shard_map/ppermute | solution.py:291
  33.6 4.0 %collective-permute-start.14 = (bf16[256,128]{1,0:T(8,128)(2,1)S(1)}, bf16[256,128]{1,0:T(8,128)(2,1)S(1)}, u32[]{:S(2)}, u32[]{:S(2)}) collective-permute-start(bf16[256,128]{1,0:T(8,128)(2,1)S(1)} %last_join.1._.refs_0_), channel_id=1, source_target_pairs={{0,1},{1,0},{2,3},{3,2},{4,5},{5,4},{6,7},{7,6},{8,9},{9,8},{10,11... | collective-permute-start | bytes 196616 | tf_op jit(solution)/shard_map/ppermute | solution.py:291
  36.2 1.3 %collective-permute-start.15 = (bf16[256,128]{1,0:T(8,128)(2,1)S(1)}, bf16[256,128]{1,0:T(8,128)(2,1)S(1)}, u32[]{:S(2)}, u32[]{:S(2)}) collective-permute-start(bf16[256,128]{1,0:T(8,128)(2,1)S(1)} %collective-permute-done.13.refs_1_), channel_id=1, source_target_pairs={{0,1},{1,0},{2,3},{3,2},{4,5},{5,4},{6,7},{7,6},{8,9},{9,8},{10,11... | collective-permute-start | bytes 196616 | tf_op jit(solution)/shard_map/ppermute | solution.py:291

commit v8 on v7

--- a/solution.py
+++ b/solution.py
@@ -112,7 +112,7 @@
     count, slots, size = blocks.shape[2], blocks.shape[3], blocks.shape[4]
     for b in range(count):
         held = [blocks[0, 0, b, s].astype(f32) for s in range(slots)]
-        ids = [cols[level_idx, 0, b, s] for s in range(2, slots)]
+        ids = [cols[level_idx, s, 0, b] for s in range(2, slots)]
         fixed = {b: held[0], count + b: held[1]}
         line = [placed(fixed.get(c), held[2:], ids, c) for c in range(2 * count)]
         out_ref[pl.ds(b * size, size), :] = jnp.concatenate(line, axis=1).astype(bf16)
@@ -122,7 +122,7 @@
     count, slots, size = blocks.shape[2], blocks.shape[3], blocks.shape[4]
     for b in range(count):
         held = [blocks[0, 0, b, s].astype(f32) for s in range(slots)]
-        ids = [cols[level_idx, 0, b, s] for s in range(1, slots)]
+        ids = [cols[level_idx, 0, s, b] for s in range(1, slots)]
         line = [placed(held[0] if c == b else None, held[1:], ids, c) for c in range(count)]
         out_ref[pl.ds(b * size, size), :] = jnp.concatenate(line, axis=1).astype(bf16)
 
@@ -184,8 +184,7 @@
     rims = jnp.concatenate([inner[...], outer[...]], axis=0)
     left = rhs[...] - matmul(local[...], smoothed[...])
     out[...] = (left - matmul(rim[...], rims)).astype(bf16)
-    made = rhs[...] * (relax_down * scale[...]) + (relax_up * scale[...]) * left
-    base[...] = made.astype(base.dtype)
+    base[...] = rhs[...] * (relax_down * scale[...]) + (relax_up * scale[...]) * left
 
 
 def operators_kernel(level_idx, _, rcols, rblocks, cols, blocks, rmat, local, rim, scale):
@@ -200,14 +199,11 @@
 
 
 def coarse_operators_kernel(level_idx, first, levels, *refs):
-    _, rcols, rblocks, pcols, inverse, one, two, *refs = refs
+    _, rcols, rblocks, pcols, inverse, *refs = refs
     places = range(first, levels)
     blocks, refs = refs[: len(places)], refs[len(places) :]
     pairs, refs = refs[: 2 * len(places)], refs[2 * len(places) :]
-    rmat, coarse, bases, *up, held = refs
-    width = one.shape[1]
-    bases[:, :width] = one[...]
-    bases[:, width:] = two[...]
+    rmat, coarse, *up, held = refs
     assemble_restrict(level_idx, rcols, rblocks, rmat)
     for idx in places:
         slot = idx - first
@@ -219,18 +215,10 @@
 
 
 def fine_operators_kernel(
-    places, _, pcols, blocks_0, blocks_1, scale_0, local_0, scale_1, local_1,
-    base, near, far, both, total, held,
+    _, pcols, blocks_0, blocks_1, scale_0, local_0, scale_1, local_1, lower, upper, held
 ):
-    lower = raising(0, pcols, blocks_0, local_0, scale_0, held)
-    upper = raising(1, pcols, blocks_1, local_1, scale_1, held)
-    both[...] = matmul(lower, upper).astype(bf16)
-    width = near.shape[1] // 2
-    for slot, place in enumerate(places):
-        source = near if slot < 2 else far
-        lanes = lanes_of(place, width)
-        columns = pl.ds(slot % 2 * width, width)
-        total[:, lanes] = base[:, lanes] + matmul(lower, source[:, columns])
+    upper[...] = raising(1, pcols, blocks_1, local_1, scale_1, held)
+    lower[...] = raising(0, pcols, blocks_0, local_0, scale_0, held)
 
 
 def restricted(level_idx, rmat, kept, other):
@@ -265,21 +253,26 @@
     value = refs[0][...]
     for part, offset in zip(parts, offsets):
         value = value + inverse_part(inverse, part, offset)
-    for step in range((len(refs) - 3) // 2):
-        base, up = refs[2 + 2 * step : 4 + 2 * step]
-        value = base[...] + matmul(up[...], value.astype(bf16))
-    for peer in range(refs[-1].shape[0]):
-        refs[-1][peer] = value.astype(bf16)
-
-
-def output_kernel(gathered, total, both, out, made, sems):
-    peers, _, width = gathered.shape
-    half = peers * width // 2
+    refs, (base, up, coarse, raised) = refs[1:-4], refs[-4:]
+    for step in range(len(refs) // 2):
+        value = refs[2 * step][...] + matmul(refs[2 * step + 1][...], value.astype(bf16))
+    value = value.astype(bf16)
+    coarse[...] = value
+    raised[...] = (base[...] + matmul(up[...], value)).astype(bf16)
+
+
+def raise_kernel(coarse, base, up, out):
+    out[...] = (base[...] + matmul(up[...], coarse[...])).astype(bf16)
+
+
+def output_kernel(places, *refs):
+    coarse, (base, lower), refs = refs[: len(places)], refs[len(places) :][:2], refs[len(places) + 2 :]
+    out, made, sems = refs[-3:]
     copies = []
-    for peer in range(peers):
-        lanes = pl.ds(peer % 2 * half + peer // 2 * width, width)
-        made[peer] = total[:, lanes] + matmul(both[...], gathered[peer])
-        copy = pltpu.make_async_copy(made.at[peer], out.at[0, :, lanes], sems.at[peer])
+    for slot, (place, value) in enumerate(zip(places, coarse)):
+        lanes = lanes_of(place, value.shape[1])
+        made[slot] = base[:, lanes] + matmul(lower[...], value[...])
+        copy = pltpu.make_async_copy(made.at[slot], out.at[0, :, lanes], sems.at[slot])
         copy.start()
         copies.append(copy)
     for copy in copies:
@@ -313,7 +306,8 @@
     rows, fields = level_rhs.shape[1:]
     half = fields // 2
     width = half // 2
-    rcols, pcols = ((c, scalars()) for c in (restrict_cols, prolong_cols))
+    rcols = restrict_cols.transpose(0, 3, 1, 2), scalars()
+    pcols = prolong_cols.transpose(0, 1, 3, 2), scalars()
     square_shape = array((rows, rows), bf16)
     operator_shapes = [square_shape, array((rows, 2 * size), bf16), array((rows, 1), f32)]
     rmat_shape = array((rows, 2 * rows), bf16)
@@ -385,7 +379,7 @@
         for operands in joined:
             value, made_base = run(
                 residual_kernel, "residual",
-                [chunk_shape, chunk_shape if level_idx == 0 else real_shape],
+                [chunk_shape, real_shape],
                 [*operands, joined[-1][1]], flops=flops(width, 2) if not made else late_cost,
             )
             made.append(value)
@@ -394,16 +388,15 @@
         anchor = made[0]
     last = levels - 1
     (other,) = (exchange(value, "wide", 1 << last) for value in sent)
-    rmat, coarse_mat, near_bases, *ups = run(
+    rmat, coarse_mat, *ups = run(
         functools.partial(coarse_operators_kernel, last, 2, levels), "coarse_operators",
-        [rmat_shape, array((rows, pieces * rows), bf16), array((rows, half), bf16)]
+        [rmat_shape, array((rows, pieces * rows), bf16)]
         + [square_shape] * (levels - 3),
-        [kept[0], rcols, of_level(restrict_blocks, last), pcols, coarse_inverse, *bases[:2]]
+        [kept[0], rcols, of_level(restrict_blocks, last), pcols, coarse_inverse]
         + [of_level(prolong_blocks, idx) for idx in range(2, levels)]
         + [value for pair in operators[2:] for value in pair],
         flops=flops(rows, 2 * (levels - 2) + pieces), scratch=held,
     )
-    far_bases = exchange(near_bases, "wide", 1)
     (mine,) = run(
         functools.partial(last_join_kernel, last), "last_join", [chunk_shape],
         [rmat, kept[0], other], flops=flops(width, 2),
@@ -413,30 +406,45 @@
     for offset in order:
         low = offset & -offset
         parts[offset] = exchange(parts[offset ^ low], "narrow", low)
-    places = [place_of(far, given) for far in (0, 1) for given in (1, 0)]
-    both, total = run(
-        functools.partial(fine_operators_kernel, places), "fine_operators",
-        [square_shape, array((rows, fields), f32)],
+    lower, upper = run(
+        fine_operators_kernel, "fine_operators", [square_shape] * 2,
         [mine, pcols, of_level(prolong_blocks, 0), of_level(prolong_blocks, 1),
-         *operators[0], *operators[1], base, near_bases, far_bases],
-        flops=flops(rows, 5), scratch=held,
+         *operators[0], *operators[1]],
+        flops=flops(rows, 2), scratch=held,
     )
     offsets = tuple(parts)
-    operands = [coarse_mat] + [parts[o] for o in offsets] + [bases[-1], both]
+    operands = [coarse_mat] + [parts[o] for o in offsets] + [bases[-1]]
     for idx in reversed(range(2, last)):
         operands += [bases[idx], ups[idx - 2]]
-    (value,) = run(
-        functools.partial(up_kernel, offsets), "up", [array((4, rows, width), bf16)], operands,
-        flops=flops(width, len(offsets) + levels - 3),
-    )
-    peers = 4
-    groups = [list(range(i, i + peers)) for i in range(0, lax.axis_size("wide"), peers)]
-    gathered = lax.all_to_all(value, "wide", 0, 0, axis_index_groups=groups)
-    (result,) = run(
-        output_kernel, "output", [array((1, rows, fields), f32)], [gathered, total, both],
-        flops=flops(fields), out_space=pltpu.HBM,
-        scratch=[pltpu.VMEM((peers, rows, width), f32), pltpu.SemaphoreType.DMA((peers,))],
-    )
+    coarse, near = run(
+        functools.partial(up_kernel, offsets), "up", [chunk_shape] * 2,
+        operands + [bases[1], upper], flops=flops(width, len(offsets) + levels - 2),
+    )
+    other = exchange(coarse, "wide", 2)
+    far = exchange(near, "wide", 1)
+    (near_other,) = run(
+        raise_kernel, "raise", [chunk_shape], [other, bases[0], upper], flops=flops(width)
+    )
+    far_other = exchange(near_other, "wide", 1)
+    result = None
+    for group in (
+        [(near, place_of(0, 0))],
+        [(near_other, place_of(0, 1)), (far, place_of(1, 0))],
+        [(far_other, place_of(1, 1))],
+    ):
+        operands = [value for value, _ in group] + [base, lower]
+        aliases = {}
+        if result is not None:
+            aliases[len(operands)] = 0
+            operands.append(in_hbm(result))
+        (result,) = run(
+            functools.partial(output_kernel, tuple(place for _, place in group)),
+            "output", [array((1, rows, fields), f32)], operands,
+            flops=flops(width, len(group)), out_space=pltpu.HBM, aliases=aliases,
+            scratch=[
+                pltpu.VMEM((len(group), rows, width), f32), pltpu.SemaphoreType.DMA((len(group),))
+            ],
+        )
     return result
 
 

time: 48.5 us -> 46 us (0.948)
  blocking collectives: 9.3 us -> 0 us
  waiting for transfers between devices: 5.65 us -> 14.7 us
  local copies, waits for them, and re-layouts: 3.15 us -> 0.03 us
  Pallas kernels: 11.2 us -> 11.9 us
  starting transfers between devices: 18.6 us -> 19.1 us
    all_to_all x1 -> x0, blocking collectives: 9.3 us -> none  [on_device(): gathered = lax.all_to_all(value, 'wide', 0, 0, axis_index_groups=groups)]
    ppermute x12 -> x14, waiting for transfers between devices: 3.37 us -> 12.4 us  [exchange(): return lax.ppermute(value, axis, [(i, i ^ bit) for i in range(count)])]
    unnamed x24 -> x14, local copies, waits for them, and re-layouts: 3.15 us -> 0.03 us
    pallas_call x17 -> x20, Pallas kernels: 11.2 us -> 11.9 us  [run(): pl.pallas_call(body, grid=(1,) if windows else (), out_shape=[out_space(o...]
    ppermute x12 -> x14, starting transfers between devices: 13.4 us -> 14 us  [exchange(): return lax.ppermute(value, axis, [(i, i ^ bit) for i in range(count)])]
  transfers between devices with their start and end apart: 17 -> 19, of which waited for: 4 -> 8; matrix products, arithmetic and copies ran while one was open for 0% -> 0% of each run, Pallas kernels for 17% -> 19%
where the time goes in v8:
time: 46 us; the launch traced here: 45.9 us
  starting transfers between devices  19.1 us (42%)
  waiting for transfers between devices  14.7 us (32%)
  Pallas kernels  11.9 us (26%)
    ppermute x14, starting transfers between devices, exchange(): return lax.ppermute(value, axis, [(i, i ^ bit) for i in range(count)])  14 us
    ppermute x14, waiting for transfers between devices, exchange(): return lax.ppermute(value, axis, [(i, i ^ bit) for i in range(count)])  12.4 us
    pallas_call x20, Pallas kernels, run(): pl.pallas_call(body, grid=(1,) if windows else (), out_shape=[out_space(o...  11.9 us
    ppermute x5, starting transfers between devices, swap_outer(): return lax.ppermute(outer, 'narrow', gaps)  5.14 us
    ppermute x5, waiting for transfers between devices, swap_outer(): return lax.ppermute(outer, 'narrow', gaps)  2.28 us
  transfers between devices with their start and end apart: 19, of which 8 were waited for; matrix products, arithmetic and copies ran while one was open for 0% of the time, Pallas kernels for 19%

profile of v8, /device:TPU:0, one launch (start us, length us, event | category | flops | bytes accessed | tf_op | source)
XLA Modules:
  0.0 45.9 jit_solution(7321110953147239700)
XLA Ops:
  0.0 1.3 %start.1 = (s32[3,1,4,5]{3,2,1,0:T(4,128)S(1)}, bf16[64,512]{1,0:T(8,128)(2,1)S(1)}, bf16[64,256]{1,0:T(8,128)(2,1)S(1)}, bf16[64,256]{1,0:T(8,128)(2,1)S(1)}) custom-call(f32[1,256,512]{2,1,0:T(8,128)} %rhs.3, bf16[3,1,4,5,64,64]{5,4,3,2,1,0:T(8,128)(2,1)} %blocks.7, s32[3,1,4,5]{3,2,1,0:T(4,128)} %refs_0_.1), custom_call_target="tpu_custom_call" | custom-call | bytes 1016048 | tf_op jit(solution)/shard_map/start/pallas_call | solution.py:52
  1.3 0.5 %collective-permute-start.1 = (bf16[64,512]{1,0:T(8,128)(2,1)S(1)}, bf16[64,512]{1,0:T(8,128)(2,1)S(1)}, u32[]{:S(2)}, u32[]{:S(2)}) collective-permute-start(bf16[64,512]{1,0:T(8,128)(2,1)S(1)} %get-tuple-element.54), channel_id=1, source_target_pairs={{0,1},{1,0},{2,3},{3,2},{4,5},{5,4},{6,7},{7,6},{8,9},{9,8},{10,11... | collective-permute-start | bytes 196616 | tf_op jit(solution)/shard_map/ppermute | solution.py:284
  1.8 2.6 %collective-permute-start = (bf16[64,256]{1,0:T(8,128)(2,1)S(1)}, bf16[64,256]{1,0:T(8,128)(2,1)S(1)}, u32[]{:S(2)}, u32[]{:S(2)}) collective-permute-start(bf16[64,256]{1,0:T(8,128)(2,1)S(1)} %get-tuple-element.50._), channel_id=1, source_target_pairs={{0,3},{1,2},{2,1},{3,0},{4,7},{5,6},{6,5},{7,4},{8,11},{9,10},{10,... | collective-permute-start | bytes 98312 | tf_op jit(solution)/shard_map/ppermute | solution.py:290
  4.4 0.0 collective-permute-start.5
  4.5 1.1 %first_local.1 = (f32[256,512]{1,0:T(8,128)S(1)}, f32[256,512]{1,0:T(8,128)S(1)}, bf16[256,256]{1,0:T(8,128)(2,1)S(1)}, bf16[256,128]{1,0:T(8,128)(2,1)S(1)}, f32[256,1]{1,0:T(8,128)S(1)}) custom-call(f32[1,256,512]{2,1,0:T(8,128)S(1)} %copy-done.3, bf16[64,256]{1,0:T(8,128)(2,1)S(1)} %get-tuple-element.50._, s32[3,1,4,5]{3,2,1,0:T(4,128)S(1)} %get-tuple-element.51.cols, ...), custom_call_target="tpu_custom_call" | custom-call | flops 67108864 | bytes 1048816 | tf_op jit(solution)/shard_map/first_local/pallas_call | solution.py:52
  5.6 0.5 %collective-permute-done.outer = bf16[64,256]{1,0:T(8,128)(2,1)S(1)} collective-permute-done((bf16[64,256]{1,0:T(8,128)(2,1)S(1)}, bf16[64,256]{1,0:T(8,128)(2,1)S(1)}, u32[]{:S(2)}, u32[]{:S(2)}) %collective-permute-start) | collective-permute-done | bytes 32800 | tf_op jit(solution)/shard_map/ppermute | solution.py:290
  6.1 0.2 first_residual.2
  6.3 1.7 %collective-permute-start.2 = (bf16[256,128]{1,0:T(8,128)(2,1)S(1)}, bf16[256,128]{1,0:T(8,128)(2,1)S(1)}, u32[]{:S(2)}, u32[]{:S(2)}) collective-permute-start(bf16[256,128]{1,0:T(8,128)(2,1)S(1)} %get-tuple-element.55._), channel_id=1, source_target_pairs={{0,4},{4,0},{8,12},{12,8},{16,20},{20,16},{24,28},{28,24},{1,5},{5... | collective-permute-start | bytes 196616 | tf_op jit(solution)/shard_map/ppermute | solution.py:284
  8.0 0.2 first_residual.3
  8.2 1.4 %collective-permute-start.6 = (bf16[256,128]{1,0:T(8,128)(2,1)S(1)}, bf16[256,128]{1,0:T(8,128)(2,1)S(1)}, u32[]{:S(2)}, u32[]{:S(2)}) collective-permute-start(bf16[256,128]{1,0:T(8,128)(2,1)S(1)} %get-tuple-element.67), channel_id=1, source_target_pairs={{0,4},{4,0},{8,12},{12,8},{16,20},{20,16},{24,28},{28,24},{1,5},{5... | collective-permute-start | bytes 196616 | tf_op jit(solution)/shard_map/ppermute | solution.py:284
  9.6 1.1 %operators.2 = (bf16[256,512]{1,0:T(8,128)(2,1)S(1)}, bf16[256,256]{1,0:T(8,128)(2,1)S(1)}, bf16[256,128]{1,0:T(8,128)(2,1)S(1)}, f32[256,1]{1,0:T(8,128)S(1)}) custom-call(bf16[256,128]{1,0:T(8,128)(2,1)S(1)} %get-tuple-element.55._, s32[3,3,1,4]{3,2,1,0:T(1,128)S(1)} %bitcast.2, bf16[3,1,4,3,64,64]{5,4,3,2,1,0:T(8,128)(2,1)S(1)} %copy-done.1, ...), custom_call_target="tpu_custom_call" | custom-call | bytes 852352 | tf_op jit(solution)/shard_map/operators/pallas_call | solution.py:52
  10.8 0.2 join.3
  11.0 1.6 %collective-permute-start.3 = (bf16[64,128]{1,0:T(8,128)(2,1)S(1)}, bf16[64,128]{1,0:T(8,128)(2,1)S(1)}, u32[]{:S(2)}, u32[]{:S(2)}) collective-permute-start(bf16[64,128]{1,0:T(8,128)(2,1)S(1)} %get-tuple-element.63), channel_id=1, source_target_pairs={{0,3},{1,2},{2,1},{3,0},{4,7},{5,6},{6,5},{7,4},{8,11},{9,10},{10,... | collective-permute-start | bytes 49160 | tf_op jit(solution)/shard_map/ppermute | solution.py:290
  12.6 0.6 %collective-permute-start.4 = (bf16[64,128]{1,0:T(8,128)(2,1)S(1)}, bf16[64,128]{1,0:T(8,128)(2,1)S(1)}, u32[]{:S(2)}, u32[]{:S(2)}) collective-permute-start(bf16[64,128]{1,0:T(8,128)(2,1)S(1)} %get-tuple-element.64), channel_id=1, source_target_pairs={{0,1},{1,0},{2,3},{3,2},{4,5},{5,4},{6,7},{7,6},{8,9},{9,8},{10,11... | collective-permute-start | bytes 49160 | tf_op jit(solution)/shard_map/ppermute | solution.py:284
  13.2 0.2 join.4
  13.4 0.8 %collective-permute-start.7 = (bf16[64,128]{1,0:T(8,128)(2,1)S(1)}, bf16[64,128]{1,0:T(8,128)(2,1)S(1)}, u32[]{:S(2)}, u32[]{:S(2)}) collective-permute-start(bf16[64,128]{1,0:T(8,128)(2,1)S(1)} %get-tuple-element.72), channel_id=1, source_target_pairs={{0,3},{1,2},{2,1},{3,0},{4,7},{5,6},{6,5},{7,4},{8,11},{9,10},{10,... | collective-permute-start | bytes 49160 | tf_op jit(solution)/shard_map/ppermute | solution.py:290
  14.2 0.6 %collective-permute-start.8 = (bf16[64,128]{1,0:T(8,128)(2,1)S(1)}, bf16[64,128]{1,0:T(8,128)(2,1)S(1)}, u32[]{:S(2)}, u32[]{:S(2)}) collective-permute-start(bf16[64,128]{1,0:T(8,128)(2,1)S(1)} %get-tuple-element.73), channel_id=1, source_target_pairs={{0,1},{1,0},{2,3},{3,2},{4,5},{5,4},{6,7},{7,6},{8,9},{9,8},{10,11... | collective-permute-start | bytes 49160 | tf_op jit(solution)/shard_map/ppermute | solution.py:284
  14.9 0.2 residual.3
  15.1 1.6 %collective-permute-start.9 = (bf16[256,128]{1,0:T(8,128)(2,1)S(1)}, bf16[256,128]{1,0:T(8,128)(2,1)S(1)}, u32[]{:S(2)}, u32[]{:S(2)}) collective-permute-start(bf16[256,128]{1,0:T(8,128)(2,1)S(1)} %get-tuple-element.69._), channel_id=1, source_target_pairs={{0,8},{4,12},{8,0},{12,4},{16,24},{20,28},{24,16},{28,20},{1,9},{5... | collective-permute-start | bytes 196616 | tf_op jit(solution)/shard_map/ppermute | solution.py:284
  16.8 0.2 residual.4
  17.0 1.1 %operators.3 = (bf16[256,512]{1,0:T(8,128)(2,1)S(1)}, bf16[256,256]{1,0:T(8,128)(2,1)S(1)}, bf16[256,128]{1,0:T(8,128)(2,1)S(1)}, f32[256,1]{1,0:T(8,128)S(1)}) custom-call(bf16[256,128]{1,0:T(8,128)(2,1)S(1)} %get-tuple-element.69._, s32[3,3,1,4]{3,2,1,0:T(1,128)S(1)} %bitcast.3, bf16[3,1,4,3,64,64]{5,4,3,2,1,0:T(8,128)(2,1)S(1)} %copy-done.1, ...), custom_call_target="tpu_custom_call" | custom-call | bytes 852352 | tf_op jit(solution)/shard_map/operators/pallas_call | solution.py:52
  18.1 1.4 %collective-permute-done.9.other = bf16[256,128]{1,0:T(8,128)(2,1)S(1)} collective-permute-done((bf16[256,128]{1,0:T(8,128)(2,1)S(1)}, bf16[256,128]{1,0:T(8,128)(2,1)S(1)}, u32[]{:S(2)}, u32[]{:S(2)}) %collective-permute-start.9) | collective-permute-done | bytes 65568 | tf_op jit(solution)/shard_map/ppermute | solution.py:284
  19.4 0.2 join.5
  19.7 0.0 copy-start.2
  19.7 0.1 collective-permute-start.10
  19.8 1.5 %collective-permute-start.11 = (bf16[64,128]{1,0:T(8,128)(2,1)S(1)}, bf16[64,128]{1,0:T(8,128)(2,1)S(1)}, u32[]{:S(2)}, u32[]{:S(2)}) collective-permute-start(bf16[64,128]{1,0:T(8,128)(2,1)S(1)} %get-tuple-element.81), channel_id=1, source_target_pairs={{0,1},{1,0},{2,3},{3,2},{4,5},{5,4},{6,7},{7,6},{8,9},{9,8},{10,11... | collective-permute-start | bytes 49160 | tf_op jit(solution)/shard_map/ppermute | solution.py:284
  21.3 1.8 %collective-permute-done.10.outer = bf16[64,128]{1,0:T(8,128)(2,1)S(1)} collective-permute-done((bf16[64,128]{1,0:T(8,128)(2,1)S(1)}, bf16[64,128]{1,0:T(8,128)(2,1)S(1)}, u32[]{:S(2)}, u32[]{:S(2)}) %collective-permute-start.10) | collective-permute-done | bytes 16416 | tf_op jit(solution)/shard_map/ppermute | solution.py:290
  23.0 0.2 residual.5
  23.2 0.0 copy-start.6
  23.3 2.7 %collective-permute-start.12 = (bf16[256,128]{1,0:T(8,128)(2,1)S(1)}, bf16[256,128]{1,0:T(8,128)(2,1)S(1)}, u32[]{:S(2)}, u32[]{:S(2)}) collective-permute-start(bf16[256,128]{1,0:T(8,128)(2,1)S(1)} %get-tuple-element.82.refs_0_.kept), channel_id=1, source_target_pairs={{0,16},{4,20},{8,24},{12,28},{16,0},{20,4},{24,8},{28,12},{1,17},{... | collective-permute-start | bytes 196616 | tf_op jit(solution)/shard_map/ppermute | solution.py:284
  26.0 1.2 %coarse_operators.1 = (bf16[256,512]{1,0:T(8,128)(2,1)S(1)}, bf16[256,1024]{1,0:T(8,128)(2,1)S(1)}) custom-call(bf16[256,128]{1,0:T(8,128)(2,1)S(1)} %get-tuple-element.82.refs_0_.kept, s32[3,3,1,4]{3,2,1,0:T(1,128)S(1)} %bitcast.4, bf16[3,1,4,3,64,64]{5,4,3,2,1,0:T(8,128)(2,1)S(1)} %copy-done.1, s32[3,1,2,4]{3,2,1,0:T(2,128)S(1)} %bitcast.5, ...), custom_call_target="tpu_custom_call" | custom-call | flops 201326592 | bytes 1213680 | tf_op jit(solution)/shard_map/coarse_operators/pallas_call | solution.py:52
  27.1 2.8 %collective-permute-done.12.other = bf16[256,128]{1,0:T(8,128)(2,1)S(1)} collective-permute-done((bf16[256,128]{1,0:T(8,128)(2,1)S(1)}, bf16[256,128]{1,0:T(8,128)(2,1)S(1)}, u32[]{:S(2)}, u32[]{:S(2)}) %collective-permute-start.12) | collective-permute-done | bytes 65568 | tf_op jit(solution)/shard_map/ppermute | solution.py:284
  29.9 0.2 last_join.1._.refs_0_
  30.1 0.1 collective-permute-start.13
  30.2 0.1 collective-permute-start.14
  30.3 4.2 %collective-permute-done.13.refs_1_ = bf16[256,128]{1,0:T(8,128)(2,1)S(1)} collective-permute-done((bf16[256,128]{1,0:T(8,128)(2,1)S(1)}, bf16[256,128]{1,0:T(8,128)(2,1)S(1)}, u32[]{:S(2)}, u32[]{:S(2)}) %collective-permute-start.13) | collective-permute-done | bytes 65568 | tf_op jit(solution)/shard_map/ppermute | solution.py:284
  34.4 0.9 %fine_operators.1 = (bf16[256,256]{1,0:T(8,128)(2,1)S(1)}, bf16[256,256]{1,0:T(8,128)(2,1)S(1)}) custom-call(bf16[256,128]{1,0:T(8,128)(2,1)S(1)} %last_join.1._.refs_0_, s32[3,1,2,4]{3,2,1,0:T(2,128)S(1)} %bitcast.6, bf16[3,1,4,2,64,64]{5,4,3,2,1,0:T(8,128)(2,1)S(1)} %copy-done.2, bf16[3,1,4,2,64,64]{5,4,3,2,1,0:T(8,128)(2,1)S(1)} %copy-done.2, ...), custom_call_target="tpu_custom_call" | custom-call | flops 67108864 | bytes 723040 | tf_op jit(solution)/shard_map/fine_operators/pallas_call | solution.py:52
  35.4 0.3 collective-permute-done.15.refs_3_
  35.7 0.5 %up.1 = (bf16[256,128]{1,0:T(8,128)(2,1)S(1)}, bf16[256,128]{1,0:T(8,128)(2,1)S(1)}) custom-call(bf16[256,1024]{1,0:T(8,128)(2,1)S(1)} %get-tuple-element.83.inverse, bf16[256,128]{1,0:T(8,128)(2,1)S(1)} %last_join.1._.refs_0_, bf16[256,128]{1,0:T(8,128)(2,1)S(1)} %collective-permute-done.13.refs_1_, bf16[256,128]{1,0:T(8,128)(2,1)S(1)} %collective-permute-done.14.refs_2_, ...), custom_call_target="tpu_custom_call" | custom-call | flops 83886080 | bytes 1179648 | tf_op jit(solution)/shard_map/up/pallas_call | solution.py:52
  36.2 0.6 %collective-permute-start.16 = (bf16[256,128]{1,0:T(8,128)(2,1)S(1)}, bf16[256,128]{1,0:T(8,128)(2,1)S(1)}, u32[]{:S(2)}, u32[]{:S(2)}) collective-permute-start(bf16[256,128]{1,0:T(8,128)(2,1)S(1)} %get-tuple-element.90), channel_id=1, source_target_pairs={{0,8},{4,12},{8,0},{12,4},{16,24},{20,28},{24,16},{28,20},{1,9},{5... | collective-permute-start | bytes 196616 | tf_op jit(solution)/shard_map/ppermute | solution.py:284
  36.8 1.2 %collective-permute-start.18 = (bf16[256,128]{1,0:T(8,128)(2,1)S(1)}, bf16[256,128]{1,0:T(8,128)(2,1)S(1)}, u32[]{:S(2)}, u32[]{:S(2)}) collective-permute-start(bf16[256,128]{1,0:T(8,128)(2,1)S(1)} %get-tuple-element.94.refs_0_), channel_id=1, source_target_pairs={{0,4},{4,0},{8,12},{12,8},{16,20},{20,16},{24,28},{28,24},{1,5},{5... | collective-permute-start | bytes 196616 | tf_op jit(solution)/shard_map/ppermute | solution.py:284
  38.0 2.5 %collective-permute-done.16.coarse = bf16[256,128]{1,0:T(8,128)(2,1)S(1)} collective-permute-done((bf16[256,128]{1,0:T(8,128)(2,1)S(1)}, bf16[256,128]{1,0:T(8,128)(2,1)S(1)}, u32[]{:S(2)}, u32[]{:S(2)}) %collective-permute-start.16) | collective-permute-done | bytes 65568 | tf_op jit(solution)/shard_map/ppermute | solution.py:284
  40.6 0.2 raise.1.refs_0_
  40.7 1.3 %collective-permute-start.17 = (bf16[256,128]{1,0:T(8,128)(2,1)S(1)}, bf16[256,128]{1,0:T(8,128)(2,1)S(1)}, u32[]{:S(2)}, u32[]{:S(2)}) collective-permute-start(bf16[256,128]{1,0:T(8,128)(2,1)S(1)} %raise.1.refs_0_), channel_id=1, source_target_pairs={{0,4},{4,0},{8,12},{12,8},{16,20},{20,16},{24,28},{28,24},{1,5},{5... | collective-permute-start | bytes 196616 | tf_op jit(solution)/shard_map/ppermute | solution.py:284
  42.0 0.8 %output.3.refs_4_ = f32[1,256,512]{2,1,0:T(8,128)} custom-call(bf16[256,128]{1,0:T(8,128)(2,1)S(1)} %get-tuple-element.94.refs_0_, f32[256,512]{1,0:T(8,128)S(1)} %get-tuple-element.92.refs_1_.refs_2_, bf16[256,256]{1,0:T(8,128)(2,1)S(1)} %get-tuple-element.93.refs_2_.refs_3_), custom_call_target="tpu_custom_call" | custom-call | flops 16777216 | bytes 720896 | tf_op jit(solution)/shard_map/output/pallas_call | solution.py:52
  42.9 0.9 %output.4.refs_3_ = f32[1,256,512]{2,1,0:T(8,128)} custom-call(bf16[256,128]{1,0:T(8,128)(2,1)S(1)} %raise.1.refs_0_, bf16[256,128]{1,0:T(8,128)(2,1)S(1)} %collective-permute-done.18.refs_1_, f32[256,512]{1,0:T(8,128)S(1)} %get-tuple-element.92.refs_1_.refs_2_, ...), custom_call_target="tpu_custom_call", output_to_operand_aliasing={{}: (4, {})} | custom-call | flops 33554432 | bytes 1310720 | tf_op jit(solution)/shard_map/output/pallas_call | solution.py:52
  43.8 1.3 %collective-permute-done.17.refs_0_ = bf16[256,128]{1,0:T(8,128)(2,1)S(1)} collective-permute-done((bf16[256,128]{1,0:T(8,128)(2,1)S(1)}, bf16[256,128]{1,0:T(8,128)(2,1)S(1)}, u32[]{:S(2)}, u32[]{:S(2)}) %collective-permute-start.17) | collective-permute-done | bytes 65568 | tf_op jit(solution)/shard_map/ppermute | solution.py:284
  45.1 0.8 %output.5 = f32[1,256,512]{2,1,0:T(8,128)} custom-call(bf16[256,128]{1,0:T(8,128)(2,1)S(1)} %collective-permute-done.17.refs_0_, f32[256,512]{1,0:T(8,128)S(1)} %get-tuple-element.92.refs_1_.refs_2_, bf16[256,256]{1,0:T(8,128)(2,1)S(1)} %get-tuple-element.93.refs_2_.refs_3_, f32[1,256,512]{2,1,0:T(8,128)} %output.4.refs_3_), custom_call_target="tpu_custom_call", output_to_operand_aliasing={{}: (3, {})} | custom-call | flops 16777216 | bytes 1245184 | tf_op jit(solution)/shard_map/output/pallas_call | solution.py:52
  (24 shorter events, 0.1 us)
Async XLA Ops:
  0.0 4.4 %copy-start = (bf16[3,1,4,5,64,64]{5,4,3,2,1,0:T(8,128)(2,1)S(1)}, bf16[3,1,4,5,64,64]{5,4,3,2,1,0:T(8,128)(2,1)}, u32[]{:S(2)}) copy-start(bf16[3,1,4,5,64,64]{5,4,3,2,1,0:T(8,128)(2,1)} %blocks.7) | copy-start | bytes 1474564
  0.0 4.4 %copy-start.3 = (f32[1,256,512]{2,1,0:T(8,128)S(1)}, f32[1,256,512]{2,1,0:T(8,128)}, u32[]{:S(2)}) copy-start(f32[1,256,512]{2,1,0:T(8,128)} %rhs.3) | copy-start | bytes 1572868
  1.3 4.8 %collective-permute-start.1 = (bf16[64,512]{1,0:T(8,128)(2,1)S(1)}, bf16[64,512]{1,0:T(8,128)(2,1)S(1)}, u32[]{:S(2)}, u32[]{:S(2)}) collective-permute-start(bf16[64,512]{1,0:T(8,128)(2,1)S(1)} %get-tuple-element.54), channel_id=1, source_target_pairs={{0,1},{1,0},{2,3},{3,2},{4,5},{5,4},{6,7},{7,6},{8,9},{9,8},{10,11... | collective-permute-start | bytes 196616 | tf_op jit(solution)/shard_map/ppermute | solution.py:284
  1.8 4.3 %collective-permute-start = (bf16[64,256]{1,0:T(8,128)(2,1)S(1)}, bf16[64,256]{1,0:T(8,128)(2,1)S(1)}, u32[]{:S(2)}, u32[]{:S(2)}) collective-permute-start(bf16[64,256]{1,0:T(8,128)(2,1)S(1)} %get-tuple-element.50._), channel_id=1, source_target_pairs={{0,3},{1,2},{2,1},{3,0},{4,7},{5,6},{6,5},{7,4},{8,11},{9,10},{10,... | collective-permute-start | bytes 98312 | tf_op jit(solution)/shard_map/ppermute | solution.py:290
  4.4 3.6 %collective-permute-start.5 = (bf16[64,256]{1,0:T(8,128)(2,1)S(1)}, bf16[64,256]{1,0:T(8,128)(2,1)S(1)}, u32[]{:S(2)}, u32[]{:S(2)}) collective-permute-start(bf16[64,256]{1,0:T(8,128)(2,1)S(1)} %get-tuple-element.65), channel_id=1, source_target_pairs={{0,3},{1,2},{2,1},{3,0},{4,7},{5,6},{6,5},{7,4},{8,11},{9,10},{10,... | collective-permute-start | bytes 98312 | tf_op jit(solution)/shard_map/ppermute | solution.py:290
  6.1 3.5 %copy-start.1 = (bf16[3,1,4,3,64,64]{5,4,3,2,1,0:T(8,128)(2,1)S(1)}, bf16[3,1,4,3,64,64]{5,4,3,2,1,0:T(8,128)(2,1)}, u32[]{:S(2)}) copy-start(bf16[3,1,4,3,64,64]{5,4,3,2,1,0:T(8,128)(2,1)} %refs_2_.1) | copy-start | bytes 884740
  6.3 4.5 %collective-permute-start.2 = (bf16[256,128]{1,0:T(8,128)(2,1)S(1)}, bf16[256,128]{1,0:T(8,128)(2,1)S(1)}, u32[]{:S(2)}, u32[]{:S(2)}) collective-permute-start(bf16[256,128]{1,0:T(8,128)(2,1)S(1)} %get-tuple-element.55._), channel_id=1, source_target_pairs={{0,4},{4,0},{8,12},{12,8},{16,20},{20,16},{24,28},{28,24},{1,5},{5... | collective-permute-start | bytes 196616 | tf_op jit(solution)/shard_map/ppermute | solution.py:284
  8.0 1.6 %copy-start.5 = (s32[3,1,4,3]{2,1,3,0:T(1,128)S(1)}, s32[3,1,4,3]{2,1,3,0:T(1,128)}, u32[]{:S(2)}) copy-start(s32[3,1,4,3]{2,1,3,0:T(1,128)} %param.11) | copy-start | bytes 436
  8.2 5.0 %collective-permute-start.6 = (bf16[256,128]{1,0:T(8,128)(2,1)S(1)}, bf16[256,128]{1,0:T(8,128)(2,1)S(1)}, u32[]{:S(2)}, u32[]{:S(2)}) collective-permute-start(bf16[256,128]{1,0:T(8,128)(2,1)S(1)} %get-tuple-element.67), channel_id=1, source_target_pairs={{0,4},{4,0},{8,12},{12,8},{16,20},{20,16},{24,28},{28,24},{1,5},{5... | collective-permute-start | bytes 196616 | tf_op jit(solution)/shard_map/ppermute | solution.py:284
  11.0 3.9 %collective-permute-start.3 = (bf16[64,128]{1,0:T(8,128)(2,1)S(1)}, bf16[64,128]{1,0:T(8,128)(2,1)S(1)}, u32[]{:S(2)}, u32[]{:S(2)}) collective-permute-start(bf16[64,128]{1,0:T(8,128)(2,1)S(1)} %get-tuple-element.63), channel_id=1, source_target_pairs={{0,3},{1,2},{2,1},{3,0},{4,7},{5,6},{6,5},{7,4},{8,11},{9,10},{10,... | collective-permute-start | bytes 49160 | tf_op jit(solution)/shard_map/ppermute | solution.py:290
  12.6 2.3 %collective-permute-start.4 = (bf16[64,128]{1,0:T(8,128)(2,1)S(1)}, bf16[64,128]{1,0:T(8,128)(2,1)S(1)}, u32[]{:S(2)}, u32[]{:S(2)}) collective-permute-start(bf16[64,128]{1,0:T(8,128)(2,1)S(1)} %get-tuple-element.64), channel_id=1, source_target_pairs={{0,1},{1,0},{2,3},{3,2},{4,5},{5,4},{6,7},{7,6},{8,9},{9,8},{10,11... | collective-permute-start | bytes 49160 | tf_op jit(solution)/shard_map/ppermute | solution.py:284
  13.4 3.4 %collective-permute-start.7 = (bf16[64,128]{1,0:T(8,128)(2,1)S(1)}, bf16[64,128]{1,0:T(8,128)(2,1)S(1)}, u32[]{:S(2)}, u32[]{:S(2)}) collective-permute-start(bf16[64,128]{1,0:T(8,128)(2,1)S(1)} %get-tuple-element.72), channel_id=1, source_target_pairs={{0,3},{1,2},{2,1},{3,0},{4,7},{5,6},{6,5},{7,4},{8,11},{9,10},{10,... | collective-permute-start | bytes 49160 | tf_op jit(solution)/shard_map/ppermute | solution.py:290
  14.2 2.5 %collective-permute-start.8 = (bf16[64,128]{1,0:T(8,128)(2,1)S(1)}, bf16[64,128]{1,0:T(8,128)(2,1)S(1)}, u32[]{:S(2)}, u32[]{:S(2)}) collective-permute-start(bf16[64,128]{1,0:T(8,128)(2,1)S(1)} %get-tuple-element.73), channel_id=1, source_target_pairs={{0,1},{1,0},{2,3},{3,2},{4,5},{5,4},{6,7},{7,6},{8,9},{9,8},{10,11... | collective-permute-start | bytes 49160 | tf_op jit(solution)/shard_map/ppermute | solution.py:284
  15.1 4.3 %collective-permute-start.9 = (bf16[256,128]{1,0:T(8,128)(2,1)S(1)}, bf16[256,128]{1,0:T(8,128)(2,1)S(1)}, u32[]{:S(2)}, u32[]{:S(2)}) collective-permute-start(bf16[256,128]{1,0:T(8,128)(2,1)S(1)} %get-tuple-element.69._), channel_id=1, source_target_pairs={{0,8},{4,12},{8,0},{12,4},{16,24},{20,28},{24,16},{28,20},{1,9},{5... | collective-permute-start | bytes 196616 | tf_op jit(solution)/shard_map/ppermute | solution.py:284
  19.4 6.5 %copy-start.4 = (bf16[256,1024]{1,0:T(8,128)(2,1)S(1)}, bf16[256,1024]{1,0:T(8,128)(2,1)}, u32[]{:S(2)}) copy-start(bf16[256,1024]{1,0:T(8,128)(2,1)} %refs_4_.1) | copy-start | bytes 1572868
  19.7 6.3 %copy-start.2 = (bf16[3,1,4,2,64,64]{5,4,3,2,1,0:T(8,128)(2,1)S(1)}, bf16[3,1,4,2,64,64]{5,4,3,2,1,0:T(8,128)(2,1)}, u32[]{:S(2)}) copy-start(bf16[3,1,4,2,64,64]{5,4,3,2,1,0:T(8,128)(2,1)} %blocks_1.1) | copy-start | bytes 589828
  19.7 3.4 %collective-permute-start.10 = (bf16[64,128]{1,0:T(8,128)(2,1)S(1)}, bf16[64,128]{1,0:T(8,128)(2,1)S(1)}, u32[]{:S(2)}, u32[]{:S(2)}) collective-permute-start(bf16[64,128]{1,0:T(8,128)(2,1)S(1)} %get-tuple-element.80), channel_id=1, source_target_pairs={{0,3},{1,2},{2,1},{3,0},{4,7},{5,6},{6,5},{7,4},{8,11},{9,10},{10,... | collective-permute-start | bytes 49160 | tf_op jit(solution)/shard_map/ppermute | solution.py:290
  19.8 3.3 %collective-permute-start.11 = (bf16[64,128]{1,0:T(8,128)(2,1)S(1)}, bf16[64,128]{1,0:T(8,128)(2,1)S(1)}, u32[]{:S(2)}, u32[]{:S(2)}) collective-permute-start(bf16[64,128]{1,0:T(8,128)(2,1)S(1)} %get-tuple-element.81), channel_id=1, source_target_pairs={{0,1},{1,0},{2,3},{3,2},{4,5},{5,4},{6,7},{7,6},{8,9},{9,8},{10,11... | collective-permute-start | bytes 49160 | tf_op jit(solution)/shard_map/ppermute | solution.py:284
  23.2 2.7 %copy-start.6 = (s32[3,1,4,2]{2,3,1,0:T(2,128)S(1)}, s32[3,1,4,2]{2,3,1,0:T(2,128)}, u32[]{:S(2)}) copy-start(s32[3,1,4,2]{2,3,1,0:T(2,128)} %param.13) | copy-start | bytes 292
  23.3 6.6 %collective-permute-start.12 = (bf16[256,128]{1,0:T(8,128)(2,1)S(1)}, bf16[256,128]{1,0:T(8,128)(2,1)S(1)}, u32[]{:S(2)}, u32[]{:S(2)}) collective-permute-start(bf16[256,128]{1,0:T(8,128)(2,1)S(1)} %get-tuple-element.82.refs_0_.kept), channel_id=1, source_target_pairs={{0,16},{4,20},{8,24},{12,28},{16,0},{20,4},{24,8},{28,12},{1,17},{... | collective-permute-start | bytes 196616 | tf_op jit(solution)/shard_map/ppermute | solution.py:284
  30.1 4.3 %collective-permute-start.13 = (bf16[256,128]{1,0:T(8,128)(2,1)S(1)}, bf16[256,128]{1,0:T(8,128)(2,1)S(1)}, u32[]{:S(2)}, u32[]{:S(2)}) collective-permute-start(bf16[256,128]{1,0:T(8,128)(2,1)S(1)} %last_join.1._.refs_0_), channel_id=1, source_target_pairs={{0,2},{1,3},{2,0},{3,1},{4,6},{5,7},{6,4},{7,5},{8,10},{9,11},{10,... | collective-permute-start | bytes 196616 | tf_op jit(solution)/shard_map/ppermute | solution.py:284
  30.2 5.2 %collective-permute-start.14 = (bf16[256,128]{1,0:T(8,128)(2,1)S(1)}, bf16[256,128]{1,0:T(8,128)(2,1)S(1)}, u32[]{:S(2)}, u32[]{:S(2)}) collective-permute-start(bf16[256,128]{1,0:T(8,128)(2,1)S(1)} %last_join.1._.refs_0_), channel_id=1, source_target_pairs={{0,1},{1,0},{2,3},{3,2},{4,5},{5,4},{6,7},{7,6},{8,9},{9,8},{10,11... | collective-permute-start | bytes 196616 | tf_op jit(solution)/shard_map/ppermute | solution.py:284
  34.4 1.3 %collective-permute-start.15 = (bf16[256,128]{1,0:T(8,128)(2,1)S(1)}, bf16[256,128]{1,0:T(8,128)(2,1)S(1)}, u32[]{:S(2)}, u32[]{:S(2)}) collective-permute-start(bf16[256,128]{1,0:T(8,128)(2,1)S(1)} %collective-permute-done.13.refs_1_), channel_id=1, source_target_pairs={{0,1},{1,0},{2,3},{3,2},{4,5},{5,4},{6,7},{7,6},{8,9},{9,8},{10,11... | collective-permute-start | bytes 196616 | tf_op jit(solution)/shard_map/ppermute | solution.py:284
  36.2 4.3 %collective-permute-start.16 = (bf16[256,128]{1,0:T(8,128)(2,1)S(1)}, bf16[256,128]{1,0:T(8,128)(2,1)S(1)}, u32[]{:S(2)}, u32[]{:S(2)}) collective-permute-start(bf16[256,128]{1,0:T(8,128)(2,1)S(1)} %get-tuple-element.90), channel_id=1, source_target_pairs={{0,8},{4,12},{8,0},{12,4},{16,24},{20,28},{24,16},{28,20},{1,9},{5... | collective-permute-start | bytes 196616 | tf_op jit(solution)/shard_map/ppermute | solution.py:284
  36.8 6.0 %collective-permute-start.18 = (bf16[256,128]{1,0:T(8,128)(2,1)S(1)}, bf16[256,128]{1,0:T(8,128)(2,1)S(1)}, u32[]{:S(2)}, u32[]{:S(2)}) collective-permute-start(bf16[256,128]{1,0:T(8,128)(2,1)S(1)} %get-tuple-element.94.refs_0_), channel_id=1, source_target_pairs={{0,4},{4,0},{8,12},{12,8},{16,20},{20,16},{24,28},{28,24},{1,5},{5... | collective-permute-start | bytes 196616 | tf_op jit(solution)/shard_map/ppermute | solution.py:284
  40.7 4.3 %collective-permute-start.17 = (bf16[256,128]{1,0:T(8,128)(2,1)S(1)}, bf16[256,128]{1,0:T(8,128)(2,1)S(1)}, u32[]{:S(2)}, u32[]{:S(2)}) collective-permute-start(bf16[256,128]{1,0:T(8,128)(2,1)S(1)} %raise.1.refs_0_), channel_id=1, source_target_pairs={{0,4},{4,0},{8,12},{12,8},{16,20},{20,16},{24,28},{28,24},{1,5},{5... | collective-permute-start | bytes 196616 | tf_op jit(solution)/shard_map/ppermute | solution.py:284

commit v9 on v8

--- a/solution.py
+++ b/solution.py
@@ -184,7 +184,8 @@
     rims = jnp.concatenate([inner[...], outer[...]], axis=0)
     left = rhs[...] - matmul(local[...], smoothed[...])
     out[...] = (left - matmul(rim[...], rims)).astype(bf16)
-    base[...] = rhs[...] * (relax_down * scale[...]) + (relax_up * scale[...]) * left
+    made = rhs[...] * (relax_down * scale[...]) + (relax_up * scale[...]) * left
+    base[...] = made.astype(base.dtype)
 
 
 def operators_kernel(level_idx, _, rcols, rblocks, cols, blocks, rmat, local, rim, scale):
@@ -199,7 +200,7 @@
 
 
 def coarse_operators_kernel(level_idx, first, levels, *refs):
-    _, rcols, rblocks, pcols, inverse, *refs = refs
+    _, _, rcols, rblocks, pcols, inverse, *refs = refs
     places = range(first, levels)
     blocks, refs = refs[: len(places)], refs[len(places) :]
     pairs, refs = refs[: 2 * len(places)], refs[2 * len(places) :]
@@ -261,17 +262,19 @@
     raised[...] = (base[...] + matmul(up[...], value)).astype(bf16)
 
 
-def raise_kernel(coarse, base, up, out):
-    out[...] = (base[...] + matmul(up[...], coarse[...])).astype(bf16)
-
-
-def output_kernel(places, *refs):
-    coarse, (base, lower), refs = refs[: len(places)], refs[len(places) :][:2], refs[len(places) + 2 :]
+def output_kernel(places, raised, *refs):
+    count = len(places)
+    coarse, refs = refs[:count], refs[count:]
+    bases, refs = refs[: sum(raised)], refs[sum(raised) :]
+    base, lower, upper = refs[:3]
     out, made, sems = refs[-3:]
     copies = []
     for slot, (place, value) in enumerate(zip(places, coarse)):
+        value = value[...]
+        if raised[slot]:
+            value = (bases[sum(raised[:slot])][...] + matmul(upper[...], value)).astype(bf16)
         lanes = lanes_of(place, value.shape[1])
-        made[slot] = base[:, lanes] + matmul(lower[...], value[...])
+        made[slot] = base[:, lanes] + matmul(lower[...], value)
         copy = pltpu.make_async_copy(made.at[slot], out.at[0, :, lanes], sems.at[slot])
         copy.start()
         copies.append(copy)
@@ -379,7 +382,7 @@
         for operands in joined:
             value, made_base = run(
                 residual_kernel, "residual",
-                [chunk_shape, real_shape],
+                [chunk_shape, real_shape if made or level_idx else chunk_shape],
                 [*operands, joined[-1][1]], flops=flops(width, 2) if not made else late_cost,
             )
             made.append(value)
@@ -388,11 +391,12 @@
         anchor = made[0]
     last = levels - 1
     (other,) = (exchange(value, "wide", 1 << last) for value in sent)
+    far_base = exchange(bases[0], "wide", 1)
     rmat, coarse_mat, *ups = run(
         functools.partial(coarse_operators_kernel, last, 2, levels), "coarse_operators",
         [rmat_shape, array((rows, pieces * rows), bf16)]
         + [square_shape] * (levels - 3),
-        [kept[0], rcols, of_level(restrict_blocks, last), pcols, coarse_inverse]
+        [kept[0], far_base, rcols, of_level(restrict_blocks, last), pcols, coarse_inverse]
         + [of_level(prolong_blocks, idx) for idx in range(2, levels)]
         + [value for pair in operators[2:] for value in pair],
         flops=flops(rows, 2 * (levels - 2) + pieces), scratch=held,
@@ -420,25 +424,26 @@
         functools.partial(up_kernel, offsets), "up", [chunk_shape] * 2,
         operands + [bases[1], upper], flops=flops(width, len(offsets) + levels - 2),
     )
+    diagonal = exchange(coarse, "wide", 3)
+    far = exchange(near, "wide", 1)
     other = exchange(coarse, "wide", 2)
-    far = exchange(near, "wide", 1)
-    (near_other,) = run(
-        raise_kernel, "raise", [chunk_shape], [other, bases[0], upper], flops=flops(width)
-    )
-    far_other = exchange(near_other, "wide", 1)
     result = None
     for group in (
-        [(near, place_of(0, 0))],
-        [(near_other, place_of(0, 1)), (far, place_of(1, 0))],
-        [(far_other, place_of(1, 1))],
+        [(near, place_of(0, 0), None)],
+        [(diagonal, place_of(1, 1), far_base),
+         (far, place_of(1, 0), None),
+         (other, place_of(0, 1), bases[0])],
     ):
-        operands = [value for value, _ in group] + [base, lower]
+        values, places, raising_bases = zip(*group)
+        raised = tuple(value is not None for value in raising_bases)
+        operands = list(values) + [value for value in raising_bases if value is not None]
+        operands += [base, lower, upper]
         aliases = {}
         if result is not None:
             aliases[len(operands)] = 0
             operands.append(in_hbm(result))
         (result,) = run(
-            functools.partial(output_kernel, tuple(place for _, place in group)),
+            functools.partial(output_kernel, places, raised),
             "output", [array((1, rows, fields), f32)], operands,
             flops=flops(width, len(group)), out_space=pltpu.HBM, aliases=aliases,
             scratch=[

time: 46 us -> 44.3 us (0.963)
  waiting for transfers between devices: 14.7 us -> 11.5 us
  starting transfers between devices: 19.1 us -> 21.2 us
  Pallas kernels: 11.9 us -> 11.3 us
    ppermute x14 -> x15, starting transfers between devices: 14 us -> 16 us  [exchange(): return lax.ppermute(value, axis, [(i, i ^ bit) for i in range(count)])]
    ppermute x14 -> x15, waiting for transfers between devices: 12.4 us -> 10.8 us  [exchange(): return lax.ppermute(value, axis, [(i, i ^ bit) for i in range(count)])]
    ppermute x5, waiting for transfers between devices: 2.28 us -> 0.68 us  [swap_outer(): return lax.ppermute(outer, 'narrow', gaps)]
    pallas_call x20 -> x18, Pallas kernels: 11.9 us -> 11.3 us  [run(): pl.pallas_call(body, grid=(1,) if windows else (), out_shape=[out_space(o...]
  transfers between devices with their start and end apart: 19 -> 20, of which waited for: 8 -> 8; matrix products, arithmetic and copies ran while one was open for 0% -> 0% of each run, Pallas kernels for 19% -> 18%
where the time goes in v9:
time: 44.3 us; the launch traced here: 44.1 us
  starting transfers between devices  21.2 us (48%)
  waiting for transfers between devices  11.5 us (26%)
  Pallas kernels  11.3 us (26%)
    ppermute x15, starting transfers between devices, exchange(): return lax.ppermute(value, axis, [(i, i ^ bit) for i in range(count)])  16 us
    pallas_call x18, Pallas kernels, run(): pl.pallas_call(body, grid=(1,) if windows else (), out_shape=[out_space(o...  11.3 us
    ppermute x15, waiting for transfers between devices, exchange(): return lax.ppermute(value, axis, [(i, i ^ bit) for i in range(count)])  10.8 us
    ppermute x5, starting transfers between devices, swap_outer(): return lax.ppermute(outer, 'narrow', gaps)  5.14 us
  transfers between devices with their start and end apart: 20, of which 8 were waited for; matrix products, arithmetic and copies ran while one was open for 0% of the time, Pallas kernels for 18%

profile of v9, /device:TPU:0, one launch (start us, length us, event | category | flops | bytes accessed | tf_op | source)
XLA Modules:
  0.0 44.1 jit_solution(2826633835774340937)
XLA Ops:
  0.0 1.3 %start.1 = (s32[3,1,4,5]{3,2,1,0:T(4,128)S(1)}, bf16[64,512]{1,0:T(8,128)(2,1)S(1)}, bf16[64,256]{1,0:T(8,128)(2,1)S(1)}, bf16[64,256]{1,0:T(8,128)(2,1)S(1)}) custom-call(f32[1,256,512]{2,1,0:T(8,128)} %rhs.3, bf16[3,1,4,5,64,64]{5,4,3,2,1,0:T(8,128)(2,1)} %blocks.7, s32[3,1,4,5]{3,2,1,0:T(4,128)} %refs_0_.1), custom_call_target="tpu_custom_call" | custom-call | bytes 1016048 | tf_op jit(solution)/shard_map/start/pallas_call | solution.py:52
  1.3 0.5 %collective-permute-start.1 = (bf16[64,512]{1,0:T(8,128)(2,1)S(1)}, bf16[64,512]{1,0:T(8,128)(2,1)S(1)}, u32[]{:S(2)}, u32[]{:S(2)}) collective-permute-start(bf16[64,512]{1,0:T(8,128)(2,1)S(1)} %get-tuple-element.54), channel_id=1, source_target_pairs={{0,1},{1,0},{2,3},{3,2},{4,5},{5,4},{6,7},{7,6},{8,9},{9,8},{10,11... | collective-permute-start | bytes 196616 | tf_op jit(solution)/shard_map/ppermute | solution.py:287
  1.8 2.6 %collective-permute-start = (bf16[64,256]{1,0:T(8,128)(2,1)S(1)}, bf16[64,256]{1,0:T(8,128)(2,1)S(1)}, u32[]{:S(2)}, u32[]{:S(2)}) collective-permute-start(bf16[64,256]{1,0:T(8,128)(2,1)S(1)} %get-tuple-element.50._), channel_id=1, source_target_pairs={{0,3},{1,2},{2,1},{3,0},{4,7},{5,6},{6,5},{7,4},{8,11},{9,10},{10,... | collective-permute-start | bytes 98312 | tf_op jit(solution)/shard_map/ppermute | solution.py:293
  4.4 0.0 collective-permute-start.5
  4.5 1.1 %first_local.1 = (f32[256,512]{1,0:T(8,128)S(1)}, f32[256,512]{1,0:T(8,128)S(1)}, bf16[256,256]{1,0:T(8,128)(2,1)S(1)}, bf16[256,128]{1,0:T(8,128)(2,1)S(1)}, f32[256,1]{1,0:T(8,128)S(1)}) custom-call(f32[1,256,512]{2,1,0:T(8,128)S(1)} %copy-done.3, bf16[64,256]{1,0:T(8,128)(2,1)S(1)} %get-tuple-element.50._, s32[3,1,4,5]{3,2,1,0:T(4,128)S(1)} %get-tuple-element.51.cols, ...), custom_call_target="tpu_custom_call" | custom-call | flops 67108864 | bytes 1048816 | tf_op jit(solution)/shard_map/first_local/pallas_call | solution.py:52
  5.6 0.5 %collective-permute-done.outer = bf16[64,256]{1,0:T(8,128)(2,1)S(1)} collective-permute-done((bf16[64,256]{1,0:T(8,128)(2,1)S(1)}, bf16[64,256]{1,0:T(8,128)(2,1)S(1)}, u32[]{:S(2)}, u32[]{:S(2)}) %collective-permute-start) | collective-permute-done | bytes 32800 | tf_op jit(solution)/shard_map/ppermute | solution.py:293
  6.1 0.2 first_residual.2
  6.3 1.7 %collective-permute-start.2 = (bf16[256,128]{1,0:T(8,128)(2,1)S(1)}, bf16[256,128]{1,0:T(8,128)(2,1)S(1)}, u32[]{:S(2)}, u32[]{:S(2)}) collective-permute-start(bf16[256,128]{1,0:T(8,128)(2,1)S(1)} %get-tuple-element.55._), channel_id=1, source_target_pairs={{0,4},{4,0},{8,12},{12,8},{16,20},{20,16},{24,28},{28,24},{1,5},{5... | collective-permute-start | bytes 196616 | tf_op jit(solution)/shard_map/ppermute | solution.py:287
  8.0 0.2 first_residual.3
  8.2 1.4 %collective-permute-start.6 = (bf16[256,128]{1,0:T(8,128)(2,1)S(1)}, bf16[256,128]{1,0:T(8,128)(2,1)S(1)}, u32[]{:S(2)}, u32[]{:S(2)}) collective-permute-start(bf16[256,128]{1,0:T(8,128)(2,1)S(1)} %get-tuple-element.67), channel_id=1, source_target_pairs={{0,4},{4,0},{8,12},{12,8},{16,20},{20,16},{24,28},{28,24},{1,5},{5... | collective-permute-start | bytes 196616 | tf_op jit(solution)/shard_map/ppermute | solution.py:287
  9.6 1.1 %operators.2 = (bf16[256,512]{1,0:T(8,128)(2,1)S(1)}, bf16[256,256]{1,0:T(8,128)(2,1)S(1)}, bf16[256,128]{1,0:T(8,128)(2,1)S(1)}, f32[256,1]{1,0:T(8,128)S(1)}) custom-call(bf16[256,128]{1,0:T(8,128)(2,1)S(1)} %get-tuple-element.55._, s32[3,3,1,4]{3,2,1,0:T(1,128)S(1)} %bitcast.2, bf16[3,1,4,3,64,64]{5,4,3,2,1,0:T(8,128)(2,1)S(1)} %copy-done.1, ...), custom_call_target="tpu_custom_call" | custom-call | bytes 852352 | tf_op jit(solution)/shard_map/operators/pallas_call | solution.py:52
  10.8 0.0 collective-permute-done.2.other
  10.8 0.2 join.3
  11.0 1.6 %collective-permute-start.3 = (bf16[64,128]{1,0:T(8,128)(2,1)S(1)}, bf16[64,128]{1,0:T(8,128)(2,1)S(1)}, u32[]{:S(2)}, u32[]{:S(2)}) collective-permute-start(bf16[64,128]{1,0:T(8,128)(2,1)S(1)} %get-tuple-element.63), channel_id=1, source_target_pairs={{0,3},{1,2},{2,1},{3,0},{4,7},{5,6},{6,5},{7,4},{8,11},{9,10},{10,... | collective-permute-start | bytes 49160 | tf_op jit(solution)/shard_map/ppermute | solution.py:293
  12.6 0.6 %collective-permute-start.4 = (bf16[64,128]{1,0:T(8,128)(2,1)S(1)}, bf16[64,128]{1,0:T(8,128)(2,1)S(1)}, u32[]{:S(2)}, u32[]{:S(2)}) collective-permute-start(bf16[64,128]{1,0:T(8,128)(2,1)S(1)} %get-tuple-element.64), channel_id=1, source_target_pairs={{0,1},{1,0},{2,3},{3,2},{4,5},{5,4},{6,7},{7,6},{8,9},{9,8},{10,11... | collective-permute-start | bytes 49160 | tf_op jit(solution)/shard_map/ppermute | solution.py:287
  13.2 0.2 join.4
  13.4 0.8 %collective-permute-start.7 = (bf16[64,128]{1,0:T(8,128)(2,1)S(1)}, bf16[64,128]{1,0:T(8,128)(2,1)S(1)}, u32[]{:S(2)}, u32[]{:S(2)}) collective-permute-start(bf16[64,128]{1,0:T(8,128)(2,1)S(1)} %get-tuple-element.72), channel_id=1, source_target_pairs={{0,3},{1,2},{2,1},{3,0},{4,7},{5,6},{6,5},{7,4},{8,11},{9,10},{10,... | collective-permute-start | bytes 49160 | tf_op jit(solution)/shard_map/ppermute | solution.py:293
  14.2 0.6 %collective-permute-start.8 = (bf16[64,128]{1,0:T(8,128)(2,1)S(1)}, bf16[64,128]{1,0:T(8,128)(2,1)S(1)}, u32[]{:S(2)}, u32[]{:S(2)}) collective-permute-start(bf16[64,128]{1,0:T(8,128)(2,1)S(1)} %get-tuple-element.73), channel_id=1, source_target_pairs={{0,1},{1,0},{2,3},{3,2},{4,5},{5,4},{6,7},{7,6},{8,9},{9,8},{10,11... | collective-permute-start | bytes 49160 | tf_op jit(solution)/shard_map/ppermute | solution.py:287
  14.9 0.2 residual.3
  15.1 1.6 %collective-permute-start.9 = (bf16[256,128]{1,0:T(8,128)(2,1)S(1)}, bf16[256,128]{1,0:T(8,128)(2,1)S(1)}, u32[]{:S(2)}, u32[]{:S(2)}) collective-permute-start(bf16[256,128]{1,0:T(8,128)(2,1)S(1)} %get-tuple-element.69._), channel_id=1, source_target_pairs={{0,8},{4,12},{8,0},{12,4},{16,24},{20,28},{24,16},{28,20},{1,9},{5... | collective-permute-start | bytes 196616 | tf_op jit(solution)/shard_map/ppermute | solution.py:287
  16.8 0.2 residual.4
  17.0 1.1 %operators.3 = (bf16[256,512]{1,0:T(8,128)(2,1)S(1)}, bf16[256,256]{1,0:T(8,128)(2,1)S(1)}, bf16[256,128]{1,0:T(8,128)(2,1)S(1)}, f32[256,1]{1,0:T(8,128)S(1)}) custom-call(bf16[256,128]{1,0:T(8,128)(2,1)S(1)} %get-tuple-element.69._, s32[3,3,1,4]{3,2,1,0:T(1,128)S(1)} %bitcast.3, bf16[3,1,4,3,64,64]{5,4,3,2,1,0:T(8,128)(2,1)S(1)} %copy-done.1, ...), custom_call_target="tpu_custom_call" | custom-call | bytes 852352 | tf_op jit(solution)/shard_map/operators/pallas_call | solution.py:52
  18.1 1.4 %collective-permute-done.9.other = bf16[256,128]{1,0:T(8,128)(2,1)S(1)} collective-permute-done((bf16[256,128]{1,0:T(8,128)(2,1)S(1)}, bf16[256,128]{1,0:T(8,128)(2,1)S(1)}, u32[]{:S(2)}, u32[]{:S(2)}) %collective-permute-start.9) | collective-permute-done | bytes 65568 | tf_op jit(solution)/shard_map/ppermute | solution.py:287
  19.4 0.2 join.5
  19.7 0.0 copy-start.2
  19.7 0.1 collective-permute-start.10
  19.8 1.5 %collective-permute-start.11 = (bf16[64,128]{1,0:T(8,128)(2,1)S(1)}, bf16[64,128]{1,0:T(8,128)(2,1)S(1)}, u32[]{:S(2)}, u32[]{:S(2)}) collective-permute-start(bf16[64,128]{1,0:T(8,128)(2,1)S(1)} %get-tuple-element.81), channel_id=1, source_target_pairs={{0,1},{1,0},{2,3},{3,2},{4,5},{5,4},{6,7},{7,6},{8,9},{9,8},{10,11... | collective-permute-start | bytes 49160 | tf_op jit(solution)/shard_map/ppermute | solution.py:287
  21.3 1.6 %collective-permute-start.12 = (bf16[256,128]{1,0:T(8,128)(2,1)S(1)}, bf16[256,128]{1,0:T(8,128)(2,1)S(1)}, u32[]{:S(2)}, u32[]{:S(2)}) collective-permute-start(bf16[256,128]{1,0:T(8,128)(2,1)S(1)} %get-tuple-element.83.refs_4_), channel_id=1, source_target_pairs={{0,4},{4,0},{8,12},{12,8},{16,20},{20,16},{24,28},{28,24},{1,5},{5... | collective-permute-start | bytes 196616 | tf_op jit(solution)/shard_map/ppermute | solution.py:287
  22.9 0.2 collective-permute-done.10.outer
  23.0 0.2 residual.5
  23.2 0.0 copy-start.6
  23.3 2.7 %collective-permute-start.13 = (bf16[256,128]{1,0:T(8,128)(2,1)S(1)}, bf16[256,128]{1,0:T(8,128)(2,1)S(1)}, u32[]{:S(2)}, u32[]{:S(2)}) collective-permute-start(bf16[256,128]{1,0:T(8,128)(2,1)S(1)} %get-tuple-element.82.refs_0_.kept), channel_id=1, source_target_pairs={{0,16},{4,20},{8,24},{12,28},{16,0},{20,4},{24,8},{28,12},{1,17},{... | collective-permute-start | bytes 196616 | tf_op jit(solution)/shard_map/ppermute | solution.py:287
  26.0 1.2 %coarse_operators.1 = (bf16[256,512]{1,0:T(8,128)(2,1)S(1)}, bf16[256,1024]{1,0:T(8,128)(2,1)S(1)}) custom-call(bf16[256,128]{1,0:T(8,128)(2,1)S(1)} %get-tuple-element.82.refs_0_.kept, bf16[256,128]{1,0:T(8,128)(2,1)S(1)} %collective-permute-done.12.refs_1_.refs_3_, s32[3,3,1,4]{3,2,1,0:T(1,128)S(1)} %bitcast.4, ...), custom_call_target="tpu_custom_call" | custom-call | flops 201326592 | bytes 1279216 | tf_op jit(solution)/shard_map/coarse_operators/pallas_call | solution.py:52
  27.2 2.7 %collective-permute-done.13.other = bf16[256,128]{1,0:T(8,128)(2,1)S(1)} collective-permute-done((bf16[256,128]{1,0:T(8,128)(2,1)S(1)}, bf16[256,128]{1,0:T(8,128)(2,1)S(1)}, u32[]{:S(2)}, u32[]{:S(2)}) %collective-permute-start.13) | collective-permute-done | bytes 65568 | tf_op jit(solution)/shard_map/ppermute | solution.py:287
  29.9 0.2 last_join.1._.refs_0_
  30.1 0.1 collective-permute-start.14
  30.2 0.1 collective-permute-start.15
  30.3 4.2 %collective-permute-done.14.refs_1_ = bf16[256,128]{1,0:T(8,128)(2,1)S(1)} collective-permute-done((bf16[256,128]{1,0:T(8,128)(2,1)S(1)}, bf16[256,128]{1,0:T(8,128)(2,1)S(1)}, u32[]{:S(2)}, u32[]{:S(2)}) %collective-permute-start.14) | collective-permute-done | bytes 65568 | tf_op jit(solution)/shard_map/ppermute | solution.py:287
  34.4 0.9 %fine_operators.1 = (bf16[256,256]{1,0:T(8,128)(2,1)S(1)}, bf16[256,256]{1,0:T(8,128)(2,1)S(1)}) custom-call(bf16[256,128]{1,0:T(8,128)(2,1)S(1)} %last_join.1._.refs_0_, s32[3,1,2,4]{3,2,1,0:T(2,128)S(1)} %bitcast.6, bf16[3,1,4,2,64,64]{5,4,3,2,1,0:T(8,128)(2,1)S(1)} %copy-done.2, bf16[3,1,4,2,64,64]{5,4,3,2,1,0:T(8,128)(2,1)S(1)} %copy-done.2, ...), custom_call_target="tpu_custom_call" | custom-call | flops 67108864 | bytes 723040 | tf_op jit(solution)/shard_map/fine_operators/pallas_call | solution.py:52
  35.4 0.3 collective-permute-done.16.refs_3_
  35.7 0.5 %up.1 = (bf16[256,128]{1,0:T(8,128)(2,1)S(1)}, bf16[256,128]{1,0:T(8,128)(2,1)S(1)}) custom-call(bf16[256,1024]{1,0:T(8,128)(2,1)S(1)} %get-tuple-element.84.inverse, bf16[256,128]{1,0:T(8,128)(2,1)S(1)} %last_join.1._.refs_0_, bf16[256,128]{1,0:T(8,128)(2,1)S(1)} %collective-permute-done.14.refs_1_, bf16[256,128]{1,0:T(8,128)(2,1)S(1)} %collective-permute-done.15.refs_2_, ...), custom_call_target="tpu_custom_call" | custom-call | flops 83886080 | bytes 1179648 | tf_op jit(solution)/shard_map/up/pallas_call | solution.py:52
  36.2 1.2 %collective-permute-start.17 = (bf16[256,128]{1,0:T(8,128)(2,1)S(1)}, bf16[256,128]{1,0:T(8,128)(2,1)S(1)}, u32[]{:S(2)}, u32[]{:S(2)}) collective-permute-start(bf16[256,128]{1,0:T(8,128)(2,1)S(1)} %get-tuple-element.91), channel_id=1, source_target_pairs={{0,12},{4,8},{8,4},{12,0},{16,28},{20,24},{24,20},{28,16},{1,13},{... | collective-permute-start | bytes 196616 | tf_op jit(solution)/shard_map/ppermute | solution.py:287
  37.5 0.8 %collective-permute-start.18 = (bf16[256,128]{1,0:T(8,128)(2,1)S(1)}, bf16[256,128]{1,0:T(8,128)(2,1)S(1)}, u32[]{:S(2)}, u32[]{:S(2)}) collective-permute-start(bf16[256,128]{1,0:T(8,128)(2,1)S(1)} %get-tuple-element.92.refs_0_), channel_id=1, source_target_pairs={{0,4},{4,0},{8,12},{12,8},{16,20},{20,16},{24,28},{28,24},{1,5},{5... | collective-permute-start | bytes 196616 | tf_op jit(solution)/shard_map/ppermute | solution.py:287
  38.3 1.5 %collective-permute-start.19 = (bf16[256,128]{1,0:T(8,128)(2,1)S(1)}, bf16[256,128]{1,0:T(8,128)(2,1)S(1)}, u32[]{:S(2)}, u32[]{:S(2)}) collective-permute-start(bf16[256,128]{1,0:T(8,128)(2,1)S(1)} %get-tuple-element.91), channel_id=1, source_target_pairs={{0,8},{4,12},{8,0},{12,4},{16,24},{20,28},{24,16},{28,20},{1,9},{5... | collective-permute-start | bytes 196616 | tf_op jit(solution)/shard_map/ppermute | solution.py:287
  39.8 0.8 %output.2.refs_8_ = f32[1,256,512]{2,1,0:T(8,128)} custom-call(bf16[256,128]{1,0:T(8,128)(2,1)S(1)} %get-tuple-element.92.refs_0_, f32[256,512]{1,0:T(8,128)S(1)} %get-tuple-element.93.refs_1_.refs_5_, bf16[256,256]{1,0:T(8,128)(2,1)S(1)} %get-tuple-element.94.refs_2_.refs_6_, bf16[256,256]{1,0:T(8,128)(2,1)S(1)} %get-tuple-element.90.refs_6_.refs_3_.refs_7_), custom_call_target="tpu_custom_call" | custom-call | flops 16777216 | bytes 851968 | tf_op jit(solution)/shard_map/output/pallas_call | solution.py:52
  40.6 1.2 %collective-permute-done.17.refs_0_ = bf16[256,128]{1,0:T(8,128)(2,1)S(1)} collective-permute-done((bf16[256,128]{1,0:T(8,128)(2,1)S(1)}, bf16[256,128]{1,0:T(8,128)(2,1)S(1)}, u32[]{:S(2)}, u32[]{:S(2)}) %collective-permute-start.17) | collective-permute-done | bytes 65568 | tf_op jit(solution)/shard_map/ppermute | solution.py:287
  41.8 1.0 %collective-permute-done.18.refs_1_ = bf16[256,128]{1,0:T(8,128)(2,1)S(1)} collective-permute-done((bf16[256,128]{1,0:T(8,128)(2,1)S(1)}, bf16[256,128]{1,0:T(8,128)(2,1)S(1)}, u32[]{:S(2)}, u32[]{:S(2)}) %collective-permute-start.18) | collective-permute-done | bytes 65568 | tf_op jit(solution)/shard_map/ppermute | solution.py:287
  42.8 1.3 %output.3 = f32[1,256,512]{2,1,0:T(8,128)} custom-call(bf16[256,128]{1,0:T(8,128)(2,1)S(1)} %collective-permute-done.17.refs_0_, bf16[256,128]{1,0:T(8,128)(2,1)S(1)} %collective-permute-done.18.refs_1_, bf16[256,128]{1,0:T(8,128)(2,1)S(1)} %collective-permute-done.19.refs_2_, ...), custom_call_target="tpu_custom_call", output_to_operand_aliasing={{}: (8, {})} | custom-call | flops 50331648 | bytes 1638400 | tf_op jit(solution)/shard_map/output/pallas_call | solution.py:52
  (24 shorter events, 0.1 us)
Async XLA Ops:
  0.0 4.4 %copy-start = (bf16[3,1,4,5,64,64]{5,4,3,2,1,0:T(8,128)(2,1)S(1)}, bf16[3,1,4,5,64,64]{5,4,3,2,1,0:T(8,128)(2,1)}, u32[]{:S(2)}) copy-start(bf16[3,1,4,5,64,64]{5,4,3,2,1,0:T(8,128)(2,1)} %blocks.7) | copy-start | bytes 1474564
  0.0 4.4 %copy-start.3 = (f32[1,256,512]{2,1,0:T(8,128)S(1)}, f32[1,256,512]{2,1,0:T(8,128)}, u32[]{:S(2)}) copy-start(f32[1,256,512]{2,1,0:T(8,128)} %rhs.3) | copy-start | bytes 1572868
  1.3 4.8 %collective-permute-start.1 = (bf16[64,512]{1,0:T(8,128)(2,1)S(1)}, bf16[64,512]{1,0:T(8,128)(2,1)S(1)}, u32[]{:S(2)}, u32[]{:S(2)}) collective-permute-start(bf16[64,512]{1,0:T(8,128)(2,1)S(1)} %get-tuple-element.54), channel_id=1, source_target_pairs={{0,1},{1,0},{2,3},{3,2},{4,5},{5,4},{6,7},{7,6},{8,9},{9,8},{10,11... | collective-permute-start | bytes 196616 | tf_op jit(solution)/shard_map/ppermute | solution.py:287
  1.8 4.3 %collective-permute-start = (bf16[64,256]{1,0:T(8,128)(2,1)S(1)}, bf16[64,256]{1,0:T(8,128)(2,1)S(1)}, u32[]{:S(2)}, u32[]{:S(2)}) collective-permute-start(bf16[64,256]{1,0:T(8,128)(2,1)S(1)} %get-tuple-element.50._), channel_id=1, source_target_pairs={{0,3},{1,2},{2,1},{3,0},{4,7},{5,6},{6,5},{7,4},{8,11},{9,10},{10,... | collective-permute-start | bytes 98312 | tf_op jit(solution)/shard_map/ppermute | solution.py:293
  4.4 3.6 %collective-permute-start.5 = (bf16[64,256]{1,0:T(8,128)(2,1)S(1)}, bf16[64,256]{1,0:T(8,128)(2,1)S(1)}, u32[]{:S(2)}, u32[]{:S(2)}) collective-permute-start(bf16[64,256]{1,0:T(8,128)(2,1)S(1)} %get-tuple-element.65), channel_id=1, source_target_pairs={{0,3},{1,2},{2,1},{3,0},{4,7},{5,6},{6,5},{7,4},{8,11},{9,10},{10,... | collective-permute-start | bytes 98312 | tf_op jit(solution)/shard_map/ppermute | solution.py:293
  6.1 3.5 %copy-start.1 = (bf16[3,1,4,3,64,64]{5,4,3,2,1,0:T(8,128)(2,1)S(1)}, bf16[3,1,4,3,64,64]{5,4,3,2,1,0:T(8,128)(2,1)}, u32[]{:S(2)}) copy-start(bf16[3,1,4,3,64,64]{5,4,3,2,1,0:T(8,128)(2,1)} %refs_3_.1) | copy-start | bytes 884740
  6.3 4.5 %collective-permute-start.2 = (bf16[256,128]{1,0:T(8,128)(2,1)S(1)}, bf16[256,128]{1,0:T(8,128)(2,1)S(1)}, u32[]{:S(2)}, u32[]{:S(2)}) collective-permute-start(bf16[256,128]{1,0:T(8,128)(2,1)S(1)} %get-tuple-element.55._), channel_id=1, source_target_pairs={{0,4},{4,0},{8,12},{12,8},{16,20},{20,16},{24,28},{28,24},{1,5},{5... | collective-permute-start | bytes 196616 | tf_op jit(solution)/shard_map/ppermute | solution.py:287
  8.0 1.6 %copy-start.5 = (s32[3,1,4,3]{2,1,3,0:T(1,128)S(1)}, s32[3,1,4,3]{2,1,3,0:T(1,128)}, u32[]{:S(2)}) copy-start(s32[3,1,4,3]{2,1,3,0:T(1,128)} %param.11) | copy-start | bytes 436
  8.2 5.0 %collective-permute-start.6 = (bf16[256,128]{1,0:T(8,128)(2,1)S(1)}, bf16[256,128]{1,0:T(8,128)(2,1)S(1)}, u32[]{:S(2)}, u32[]{:S(2)}) collective-permute-start(bf16[256,128]{1,0:T(8,128)(2,1)S(1)} %get-tuple-element.67), channel_id=1, source_target_pairs={{0,4},{4,0},{8,12},{12,8},{16,20},{20,16},{24,28},{28,24},{1,5},{5... | collective-permute-start | bytes 196616 | tf_op jit(solution)/shard_map/ppermute | solution.py:287
  11.0 3.9 %collective-permute-start.3 = (bf16[64,128]{1,0:T(8,128)(2,1)S(1)}, bf16[64,128]{1,0:T(8,128)(2,1)S(1)}, u32[]{:S(2)}, u32[]{:S(2)}) collective-permute-start(bf16[64,128]{1,0:T(8,128)(2,1)S(1)} %get-tuple-element.63), channel_id=1, source_target_pairs={{0,3},{1,2},{2,1},{3,0},{4,7},{5,6},{6,5},{7,4},{8,11},{9,10},{10,... | collective-permute-start | bytes 49160 | tf_op jit(solution)/shard_map/ppermute | solution.py:293
  12.6 2.3 %collective-permute-start.4 = (bf16[64,128]{1,0:T(8,128)(2,1)S(1)}, bf16[64,128]{1,0:T(8,128)(2,1)S(1)}, u32[]{:S(2)}, u32[]{:S(2)}) collective-permute-start(bf16[64,128]{1,0:T(8,128)(2,1)S(1)} %get-tuple-element.64), channel_id=1, source_target_pairs={{0,1},{1,0},{2,3},{3,2},{4,5},{5,4},{6,7},{7,6},{8,9},{9,8},{10,11... | collective-permute-start | bytes 49160 | tf_op jit(solution)/shard_map/ppermute | solution.py:287
  13.4 3.4 %collective-permute-start.7 = (bf16[64,128]{1,0:T(8,128)(2,1)S(1)}, bf16[64,128]{1,0:T(8,128)(2,1)S(1)}, u32[]{:S(2)}, u32[]{:S(2)}) collective-permute-start(bf16[64,128]{1,0:T(8,128)(2,1)S(1)} %get-tuple-element.72), channel_id=1, source_target_pairs={{0,3},{1,2},{2,1},{3,0},{4,7},{5,6},{6,5},{7,4},{8,11},{9,10},{10,... | collective-permute-start | bytes 49160 | tf_op jit(solution)/shard_map/ppermute | solution.py:293
  14.2 2.5 %collective-permute-start.8 = (bf16[64,128]{1,0:T(8,128)(2,1)S(1)}, bf16[64,128]{1,0:T(8,128)(2,1)S(1)}, u32[]{:S(2)}, u32[]{:S(2)}) collective-permute-start(bf16[64,128]{1,0:T(8,128)(2,1)S(1)} %get-tuple-element.73), channel_id=1, source_target_pairs={{0,1},{1,0},{2,3},{3,2},{4,5},{5,4},{6,7},{7,6},{8,9},{9,8},{10,11... | collective-permute-start | bytes 49160 | tf_op jit(solution)/shard_map/ppermute | solution.py:287
  15.1 4.3 %collective-permute-start.9 = (bf16[256,128]{1,0:T(8,128)(2,1)S(1)}, bf16[256,128]{1,0:T(8,128)(2,1)S(1)}, u32[]{:S(2)}, u32[]{:S(2)}) collective-permute-start(bf16[256,128]{1,0:T(8,128)(2,1)S(1)} %get-tuple-element.69._), channel_id=1, source_target_pairs={{0,8},{4,12},{8,0},{12,4},{16,24},{20,28},{24,16},{28,20},{1,9},{5... | collective-permute-start | bytes 196616 | tf_op jit(solution)/shard_map/ppermute | solution.py:287
  19.4 6.5 %copy-start.4 = (bf16[256,1024]{1,0:T(8,128)(2,1)S(1)}, bf16[256,1024]{1,0:T(8,128)(2,1)}, u32[]{:S(2)}) copy-start(bf16[256,1024]{1,0:T(8,128)(2,1)} %refs_5_.1) | copy-start | bytes 1572868
  19.7 6.3 %copy-start.2 = (bf16[3,1,4,2,64,64]{5,4,3,2,1,0:T(8,128)(2,1)S(1)}, bf16[3,1,4,2,64,64]{5,4,3,2,1,0:T(8,128)(2,1)}, u32[]{:S(2)}) copy-start(bf16[3,1,4,2,64,64]{5,4,3,2,1,0:T(8,128)(2,1)} %blocks_1.1) | copy-start | bytes 589828
  19.7 3.4 %collective-permute-start.10 = (bf16[64,128]{1,0:T(8,128)(2,1)S(1)}, bf16[64,128]{1,0:T(8,128)(2,1)S(1)}, u32[]{:S(2)}, u32[]{:S(2)}) collective-permute-start(bf16[64,128]{1,0:T(8,128)(2,1)S(1)} %get-tuple-element.80), channel_id=1, source_target_pairs={{0,3},{1,2},{2,1},{3,0},{4,7},{5,6},{6,5},{7,4},{8,11},{9,10},{10,... | collective-permute-start | bytes 49160 | tf_op jit(solution)/shard_map/ppermute | solution.py:293
  19.8 3.3 %collective-permute-start.11 = (bf16[64,128]{1,0:T(8,128)(2,1)S(1)}, bf16[64,128]{1,0:T(8,128)(2,1)S(1)}, u32[]{:S(2)}, u32[]{:S(2)}) collective-permute-start(bf16[64,128]{1,0:T(8,128)(2,1)S(1)} %get-tuple-element.81), channel_id=1, source_target_pairs={{0,1},{1,0},{2,3},{3,2},{4,5},{5,4},{6,7},{7,6},{8,9},{9,8},{10,11... | collective-permute-start | bytes 49160 | tf_op jit(solution)/shard_map/ppermute | solution.py:287
  21.3 4.7 %collective-permute-start.12 = (bf16[256,128]{1,0:T(8,128)(2,1)S(1)}, bf16[256,128]{1,0:T(8,128)(2,1)S(1)}, u32[]{:S(2)}, u32[]{:S(2)}) collective-permute-start(bf16[256,128]{1,0:T(8,128)(2,1)S(1)} %get-tuple-element.83.refs_4_), channel_id=1, source_target_pairs={{0,4},{4,0},{8,12},{12,8},{16,20},{20,16},{24,28},{28,24},{1,5},{5... | collective-permute-start | bytes 196616 | tf_op jit(solution)/shard_map/ppermute | solution.py:287
  23.2 2.7 %copy-start.6 = (s32[3,1,4,2]{2,3,1,0:T(2,128)S(1)}, s32[3,1,4,2]{2,3,1,0:T(2,128)}, u32[]{:S(2)}) copy-start(s32[3,1,4,2]{2,3,1,0:T(2,128)} %param.13) | copy-start | bytes 292
  23.3 6.6 %collective-permute-start.13 = (bf16[256,128]{1,0:T(8,128)(2,1)S(1)}, bf16[256,128]{1,0:T(8,128)(2,1)S(1)}, u32[]{:S(2)}, u32[]{:S(2)}) collective-permute-start(bf16[256,128]{1,0:T(8,128)(2,1)S(1)} %get-tuple-element.82.refs_0_.kept), channel_id=1, source_target_pairs={{0,16},{4,20},{8,24},{12,28},{16,0},{20,4},{24,8},{28,12},{1,17},{... | collective-permute-start | bytes 196616 | tf_op jit(solution)/shard_map/ppermute | solution.py:287
  30.1 4.3 %collective-permute-start.14 = (bf16[256,128]{1,0:T(8,128)(2,1)S(1)}, bf16[256,128]{1,0:T(8,128)(2,1)S(1)}, u32[]{:S(2)}, u32[]{:S(2)}) collective-permute-start(bf16[256,128]{1,0:T(8,128)(2,1)S(1)} %last_join.1._.refs_0_), channel_id=1, source_target_pairs={{0,2},{1,3},{2,0},{3,1},{4,6},{5,7},{6,4},{7,5},{8,10},{9,11},{10,... | collective-permute-start | bytes 196616 | tf_op jit(solution)/shard_map/ppermute | solution.py:287
  30.2 5.2 %collective-permute-start.15 = (bf16[256,128]{1,0:T(8,128)(2,1)S(1)}, bf16[256,128]{1,0:T(8,128)(2,1)S(1)}, u32[]{:S(2)}, u32[]{:S(2)}) collective-permute-start(bf16[256,128]{1,0:T(8,128)(2,1)S(1)} %last_join.1._.refs_0_), channel_id=1, source_target_pairs={{0,1},{1,0},{2,3},{3,2},{4,5},{5,4},{6,7},{7,6},{8,9},{9,8},{10,11... | collective-permute-start | bytes 196616 | tf_op jit(solution)/shard_map/ppermute | solution.py:287
  34.4 1.3 %collective-permute-start.16 = (bf16[256,128]{1,0:T(8,128)(2,1)S(1)}, bf16[256,128]{1,0:T(8,128)(2,1)S(1)}, u32[]{:S(2)}, u32[]{:S(2)}) collective-permute-start(bf16[256,128]{1,0:T(8,128)(2,1)S(1)} %collective-permute-done.14.refs_1_), channel_id=1, source_target_pairs={{0,1},{1,0},{2,3},{3,2},{4,5},{5,4},{6,7},{7,6},{8,9},{9,8},{10,11... | collective-permute-start | bytes 196616 | tf_op jit(solution)/shard_map/ppermute | solution.py:287
  36.2 5.6 %collective-permute-start.17 = (bf16[256,128]{1,0:T(8,128)(2,1)S(1)}, bf16[256,128]{1,0:T(8,128)(2,1)S(1)}, u32[]{:S(2)}, u32[]{:S(2)}) collective-permute-start(bf16[256,128]{1,0:T(8,128)(2,1)S(1)} %get-tuple-element.91), channel_id=1, source_target_pairs={{0,12},{4,8},{8,4},{12,0},{16,28},{20,24},{24,20},{28,16},{1,13},{... | collective-permute-start | bytes 196616 | tf_op jit(solution)/shard_map/ppermute | solution.py:287
  37.5 5.3 %collective-permute-start.18 = (bf16[256,128]{1,0:T(8,128)(2,1)S(1)}, bf16[256,128]{1,0:T(8,128)(2,1)S(1)}, u32[]{:S(2)}, u32[]{:S(2)}) collective-permute-start(bf16[256,128]{1,0:T(8,128)(2,1)S(1)} %get-tuple-element.92.refs_0_), channel_id=1, source_target_pairs={{0,4},{4,0},{8,12},{12,8},{16,20},{20,16},{24,28},{28,24},{1,5},{5... | collective-permute-start | bytes 196616 | tf_op jit(solution)/shard_map/ppermute | solution.py:287
  38.3 4.5 %collective-permute-start.19 = (bf16[256,128]{1,0:T(8,128)(2,1)S(1)}, bf16[256,128]{1,0:T(8,128)(2,1)S(1)}, u32[]{:S(2)}, u32[]{:S(2)}) collective-permute-start(bf16[256,128]{1,0:T(8,128)(2,1)S(1)} %get-tuple-element.91), channel_id=1, source_target_pairs={{0,8},{4,12},{8,0},{12,4},{16,24},{20,28},{24,16},{28,20},{1,9},{5... | collective-permute-start | bytes 196616 | tf_op jit(solution)/shard_map/ppermute | solution.py:287

commit v10 on v9

--- a/solution.py
+++ b/solution.py
@@ -118,6 +118,18 @@
         out_ref[pl.ds(b * size, size), :] = jnp.concatenate(line, axis=1).astype(bf16)
 
 
+def assemble_share(level_idx, cols, blocks, out_ref):
+    count, slots, size = blocks.shape[2], blocks.shape[3], blocks.shape[4]
+    bit = bit_of(level_idx)
+    for b in range(count):
+        held = [blocks[0, 0, b, s].astype(f32) for s in range(slots)]
+        ids = [cols[level_idx, s, 0, b] for s in range(2, slots)]
+        own = jnp.where(bit == 0, held[0], held[1])
+        first = bit * count
+        line = [placed(own if c == b else None, held[2:], ids, first + c) for c in range(count)]
+        out_ref[pl.ds(b * size, size), :] = jnp.concatenate(line, axis=1).astype(bf16)
+
+
 def assemble_prolong(level_idx, cols, blocks, out_ref):
     count, slots, size = blocks.shape[2], blocks.shape[3], blocks.shape[4]
     for b in range(count):
@@ -188,7 +200,19 @@
     base[...] = made.astype(base.dtype)
 
 
-def operators_kernel(level_idx, _, rcols, rblocks, cols, blocks, rmat, local, rim, scale):
+def last_residual_kernel(rhs, smoothed, scale, local, rim, outer, inner, share, out, base):
+    rims = jnp.concatenate([inner[...], outer[...]], axis=0)
+    left = rhs[...] - matmul(local[...], smoothed[...])
+    residual = (left - matmul(rim[...], rims)).astype(bf16)
+    out[...] = matmul(share[...], residual).astype(bf16)
+    base[...] = rhs[...] * (relax_down * scale[...]) + (relax_up * scale[...]) * left
+
+
+def operators_kernel(level_idx, _, rcols, rblocks, cols, blocks, *refs):
+    if len(refs) > 4:
+        last_blocks, *refs = refs
+        assemble_share(level_idx + 1, rcols, last_blocks, refs.pop())
+    rmat, local, rim, scale = refs
     assemble_restrict(level_idx, rcols, rblocks, rmat)
     assemble_galerkin(level_idx + 1, cols, blocks, local, rim, scale)
 
@@ -199,13 +223,12 @@
     return (held[...].astype(f32) - (relax_up * scale[...]) * applied).astype(bf16)
 
 
-def coarse_operators_kernel(level_idx, first, levels, *refs):
-    _, _, rcols, rblocks, pcols, inverse, *refs = refs
+def coarse_operators_kernel(first, levels, *refs):
+    _, _, pcols, inverse, *refs = refs
     places = range(first, levels)
     blocks, refs = refs[: len(places)], refs[len(places) :]
     pairs, refs = refs[: 2 * len(places)], refs[2 * len(places) :]
-    rmat, coarse, *up, held = refs
-    assemble_restrict(level_idx, rcols, rblocks, rmat)
+    coarse, *up, held = refs
     for idx in places:
         slot = idx - first
         made = raising(idx, pcols, blocks[slot], pairs[2 * slot + 1], pairs[2 * slot], held)
@@ -239,22 +262,22 @@
     put_ends(rounded[:size], rounded[-size:], inner_ref, outer_ref)
 
 
-def last_join_kernel(level_idx, rmat, kept, other, rounded):
-    rounded[...] = restricted(level_idx, rmat, kept, other).astype(bf16)
-
-
 def inverse_part(inverse, part, offset):
     depth = part.shape[0]
     piece = lax.axis_index("narrow") ^ offset
     return matmul(inverse[:, pl.ds(pl.multiple_of(piece * depth, depth), depth)], part[...])
 
 
+def share_sum_kernel(far, own, *refs):
+    refs[-1][...] = (far[...].astype(f32) + own[...].astype(f32)).astype(bf16)
+
+
 def up_kernel(offsets, inverse, *refs):
-    parts, refs = refs[: len(offsets)], refs[len(offsets) :]
-    value = refs[0][...]
-    for part, offset in zip(parts, offsets):
+    value = refs[len(offsets)][...]
+    for part, offset in zip(refs, offsets):
         value = value + inverse_part(inverse, part, offset)
-    refs, (base, up, coarse, raised) = refs[1:-4], refs[-4:]
+    refs = refs[len(offsets) + 1 :]
+    refs, (base, up, coarse, raised) = refs[:-4], refs[-4:]
     for step in range(len(refs) // 2):
         value = refs[2 * step][...] + matmul(refs[2 * step + 1][...], value.astype(bf16))
     value = value.astype(bf16)
@@ -285,6 +308,15 @@
 def exchange(value, axis, bit):
     count = lax.axis_size(axis)
     return lax.ppermute(value, axis, [(i, i ^ bit) for i in range(count)])
+
+
+def exchange_both(value, bit, offset):
+    wide, narrow = lax.axis_size("wide"), lax.axis_size("narrow")
+    pairs = [
+        (w * narrow + j, (w ^ bit) * narrow + (j ^ offset))
+        for w in range(wide) for j in range(narrow)
+    ]
+    return lax.ppermute(value, ("wide", "narrow"), pairs)
 
 
 def swap_outer(outer):
@@ -357,16 +389,20 @@
         )
         sent.append(far)
         kept.append(near)
+    last = levels - 1
     bases = []
     anchor = sent[0]
     pieces = lax.axis_size("narrow")
     for level_idx in range(levels - 1):
         other = [exchange(value, "wide", 1 << level_idx) for value in sent]
-        rmat, local, rim, scale = run(
-            functools.partial(operators_kernel, level_idx), "operators",
-            [rmat_shape] + operator_shapes,
-            [anchor, rcols, of_level(restrict_blocks, level_idx),
-             gcols, of_level(galerkin_blocks, level_idx + 1)],
+        shapes = [rmat_shape] + operator_shapes
+        operands = [anchor, rcols, of_level(restrict_blocks, level_idx),
+                    gcols, of_level(galerkin_blocks, level_idx + 1)]
+        if level_idx + 1 == last:
+            shapes.append(square_shape)
+            operands.append(of_level(restrict_blocks, last))
+        rmat, local, rim, scale, *share = run(
+            functools.partial(operators_kernel, level_idx), "operators", shapes, operands
         )
         operators.append((scale, local))
         joined = []
@@ -381,41 +417,40 @@
         made = []
         for operands in joined:
             value, made_base = run(
-                residual_kernel, "residual",
+                last_residual_kernel if share else residual_kernel, "residual",
                 [chunk_shape, real_shape if made or level_idx else chunk_shape],
-                [*operands, joined[-1][1]], flops=flops(width, 2) if not made else late_cost,
+                [*operands, *(share or [joined[-1][1]])],
+                flops=flops(width, 2) if not made else late_cost,
             )
             made.append(value)
             bases.append(made_base)
         sent, kept = made[:1], made[-1:]
         anchor = made[0]
-    last = levels - 1
-    (other,) = (exchange(value, "wide", 1 << last) for value in sent)
+    (mine,) = kept
+    far_parts = {o: exchange_both(mine, 1 << last, o) for o in range(0, pieces, 2)}
     far_base = exchange(bases[0], "wide", 1)
-    rmat, coarse_mat, *ups = run(
-        functools.partial(coarse_operators_kernel, last, 2, levels), "coarse_operators",
-        [rmat_shape, array((rows, pieces * rows), bf16)]
-        + [square_shape] * (levels - 3),
-        [kept[0], far_base, rcols, of_level(restrict_blocks, last), pcols, coarse_inverse]
+    own_parts = {o: exchange(mine, "narrow", o) if o else mine for o in range(0, pieces, 2)}
+    coarse_mat, *ups = run(
+        functools.partial(coarse_operators_kernel, 2, levels), "coarse_operators",
+        [array((rows, pieces * rows), bf16)] + [square_shape] * (levels - 3),
+        [mine, far_base, pcols, coarse_inverse]
         + [of_level(prolong_blocks, idx) for idx in range(2, levels)]
         + [value for pair in operators[2:] for value in pair],
         flops=flops(rows, 2 * (levels - 2) + pieces), scratch=held,
     )
-    (mine,) = run(
-        functools.partial(last_join_kernel, last), "last_join", [chunk_shape],
-        [rmat, kept[0], other], flops=flops(width, 2),
-    )
-    order = sorted(range(1, pieces), key=lambda o: (bin(o).count("1"), -o))
-    parts = {0: mine}
-    for offset in order:
-        low = offset & -offset
-        parts[offset] = exchange(parts[offset ^ low], "narrow", low)
     lower, upper = run(
         fine_operators_kernel, "fine_operators", [square_shape] * 2,
         [mine, pcols, of_level(prolong_blocks, 0), of_level(prolong_blocks, 1),
          *operators[0], *operators[1]],
         flops=flops(rows, 2), scratch=held,
     )
+    parts = {}
+    for offset in range(0, pieces, 2):
+        (parts[offset],) = run(
+            share_sum_kernel, "share_sum", [chunk_shape],
+            [far_parts[offset], own_parts[offset], coarse_mat, upper],
+        )
+        parts[offset + 1] = exchange(parts[offset], "narrow", 1)
     offsets = tuple(parts)
     operands = [coarse_mat] + [parts[o] for o in offsets] + [bases[-1]]
     for idx in reversed(range(2, last)):

time: 44.3 us -> 43.5 us (0.982)
  waiting for transfers between devices: 11.5 us -> 8.8 us
  starting transfers between devices: 21.2 us -> 22.9 us
    ppermute x15 -> x14, waiting for transfers between devices: 10.8 us -> 5.45 us  [exchange(): return lax.ppermute(value, axis, [(i, i ^ bit) for i in range(count)])]
    ppermute x0 -> x2, starting transfers between devices: none -> 3.74 us  [exchange_both(): return lax.ppermute(value, ('wide', 'narrow'), pairs)]
    ppermute x0 -> x2, waiting for transfers between devices: none -> 2.67 us  [exchange_both(): return lax.ppermute(value, ('wide', 'narrow'), pairs)]
    ppermute x15 -> x14, starting transfers between devices: 16 us -> 14 us  [exchange(): return lax.ppermute(value, axis, [(i, i ^ bit) for i in range(count)])]
    pallas_call x18 -> x19, Pallas kernels: 11.3 us -> 11.3 us  [run(): pl.pallas_call(body, grid=(1,) if windows else (), out_shape=[out_space(o...]
  transfers between devices with their start and end apart: 20 -> 21, of which waited for: 8 -> 10; matrix products, arithmetic and copies ran while one was open for 0% -> 0% of each run, Pallas kernels for 18% -> 18%
where the time goes in v10:
time: 43.5 us; the launch traced here: 43.3 us
  starting transfers between devices  22.9 us (53%)
  Pallas kernels  11.3 us (26%)
  waiting for transfers between devices  8.8 us (20%)
    ppermute x14, starting transfers between devices, exchange(): return lax.ppermute(value, axis, [(i, i ^ bit) for i in range(count)])  14 us
    pallas_call x19, Pallas kernels, run(): pl.pallas_call(body, grid=(1,) if windows else (), out_shape=[out_space(o...  11.3 us
    ppermute x14, waiting for transfers between devices, exchange(): return lax.ppermute(value, axis, [(i, i ^ bit) for i in range(count)])  5.45 us
    ppermute x5, starting transfers between devices, swap_outer(): return lax.ppermute(outer, 'narrow', gaps)  5.14 us
    ppermute x2, starting transfers between devices, exchange_both(): return lax.ppermute(value, ('wide', 'narrow'), pairs)  3.74 us
    ppermute x2, waiting for transfers between devices, exchange_both(): return lax.ppermute(value, ('wide', 'narrow'), pairs)  2.67 us
  transfers between devices with their start and end apart: 21, of which 10 were waited for; matrix products, arithmetic and copies ran while one was open for 0% of the time, Pallas kernels for 18%

profile of v10, /device:TPU:0, one launch (start us, length us, event | category | flops | bytes accessed | tf_op | source)
XLA Modules:
  0.0 43.3 jit_solution(7680495460846966226)
XLA Ops:
  0.0 1.3 %start.1 = (s32[3,1,4,5]{3,2,1,0:T(4,128)S(1)}, bf16[64,512]{1,0:T(8,128)(2,1)S(1)}, bf16[64,256]{1,0:T(8,128)(2,1)S(1)}, bf16[64,256]{1,0:T(8,128)(2,1)S(1)}) custom-call(f32[1,256,512]{2,1,0:T(8,128)} %rhs.3, bf16[3,1,4,5,64,64]{5,4,3,2,1,0:T(8,128)(2,1)} %blocks.7, s32[3,1,4,5]{3,2,1,0:T(4,128)} %refs_0_.2), custom_call_target="tpu_custom_call" | custom-call | bytes 1016048 | tf_op jit(solution)/shard_map/start/pallas_call | solution.py:52
  1.3 0.5 %collective-permute-start.1 = (bf16[64,512]{1,0:T(8,128)(2,1)S(1)}, bf16[64,512]{1,0:T(8,128)(2,1)S(1)}, u32[]{:S(2)}, u32[]{:S(2)}) collective-permute-start(bf16[64,512]{1,0:T(8,128)(2,1)S(1)} %get-tuple-element.53), channel_id=1, source_target_pairs={{0,1},{1,0},{2,3},{3,2},{4,5},{5,4},{6,7},{7,6},{8,9},{9,8},{10,11... | collective-permute-start | bytes 196616 | tf_op jit(solution)/shard_map/ppermute | solution.py:310
  1.8 2.6 %collective-permute-start = (bf16[64,256]{1,0:T(8,128)(2,1)S(1)}, bf16[64,256]{1,0:T(8,128)(2,1)S(1)}, u32[]{:S(2)}, u32[]{:S(2)}) collective-permute-start(bf16[64,256]{1,0:T(8,128)(2,1)S(1)} %get-tuple-element.49._), channel_id=1, source_target_pairs={{0,3},{1,2},{2,1},{3,0},{4,7},{5,6},{6,5},{7,4},{8,11},{9,10},{10,... | collective-permute-start | bytes 98312 | tf_op jit(solution)/shard_map/ppermute | solution.py:325
  4.5 1.1 %first_local.1 = (f32[256,512]{1,0:T(8,128)S(1)}, f32[256,512]{1,0:T(8,128)S(1)}, bf16[256,256]{1,0:T(8,128)(2,1)S(1)}, bf16[256,128]{1,0:T(8,128)(2,1)S(1)}, f32[256,1]{1,0:T(8,128)S(1)}) custom-call(f32[1,256,512]{2,1,0:T(8,128)S(1)} %copy-done.3, bf16[64,256]{1,0:T(8,128)(2,1)S(1)} %get-tuple-element.49._, s32[3,1,4,5]{3,2,1,0:T(4,128)S(1)} %get-tuple-element.50.cols, ...), custom_call_target="tpu_custom_call" | custom-call | flops 67108864 | bytes 1048816 | tf_op jit(solution)/shard_map/first_local/pallas_call | solution.py:52
  5.6 0.5 %collective-permute-done.outer = bf16[64,256]{1,0:T(8,128)(2,1)S(1)} collective-permute-done((bf16[64,256]{1,0:T(8,128)(2,1)S(1)}, bf16[64,256]{1,0:T(8,128)(2,1)S(1)}, u32[]{:S(2)}, u32[]{:S(2)}) %collective-permute-start) | collective-permute-done | bytes 32800 | tf_op jit(solution)/shard_map/ppermute | solution.py:325
  6.1 0.2 first_residual.2
  6.3 1.7 %collective-permute-start.2 = (bf16[256,128]{1,0:T(8,128)(2,1)S(1)}, bf16[256,128]{1,0:T(8,128)(2,1)S(1)}, u32[]{:S(2)}, u32[]{:S(2)}) collective-permute-start(bf16[256,128]{1,0:T(8,128)(2,1)S(1)} %get-tuple-element.54._), channel_id=1, source_target_pairs={{0,4},{4,0},{8,12},{12,8},{16,20},{20,16},{24,28},{28,24},{1,5},{5... | collective-permute-start | bytes 196616 | tf_op jit(solution)/shard_map/ppermute | solution.py:310
  8.0 0.2 first_residual.3
  8.2 1.4 %collective-permute-start.6 = (bf16[256,128]{1,0:T(8,128)(2,1)S(1)}, bf16[256,128]{1,0:T(8,128)(2,1)S(1)}, u32[]{:S(2)}, u32[]{:S(2)}) collective-permute-start(bf16[256,128]{1,0:T(8,128)(2,1)S(1)} %get-tuple-element.66), channel_id=1, source_target_pairs={{0,4},{4,0},{8,12},{12,8},{16,20},{20,16},{24,28},{28,24},{1,5},{5... | collective-permute-start | bytes 196616 | tf_op jit(solution)/shard_map/ppermute | solution.py:310
  9.6 1.1 %operators.2 = (bf16[256,512]{1,0:T(8,128)(2,1)S(1)}, bf16[256,256]{1,0:T(8,128)(2,1)S(1)}, bf16[256,128]{1,0:T(8,128)(2,1)S(1)}, f32[256,1]{1,0:T(8,128)S(1)}) custom-call(bf16[256,128]{1,0:T(8,128)(2,1)S(1)} %get-tuple-element.54._, s32[3,3,1,4]{3,2,1,0:T(1,128)S(1)} %bitcast.2, bf16[3,1,4,3,64,64]{5,4,3,2,1,0:T(8,128)(2,1)S(1)} %copy-done.1, ...), custom_call_target="tpu_custom_call" | custom-call | bytes 852352 | tf_op jit(solution)/shard_map/operators/pallas_call | solution.py:52
  10.8 0.2 join.3
  11.0 1.6 %collective-permute-start.3 = (bf16[64,128]{1,0:T(8,128)(2,1)S(1)}, bf16[64,128]{1,0:T(8,128)(2,1)S(1)}, u32[]{:S(2)}, u32[]{:S(2)}) collective-permute-start(bf16[64,128]{1,0:T(8,128)(2,1)S(1)} %get-tuple-element.62), channel_id=1, source_target_pairs={{0,3},{1,2},{2,1},{3,0},{4,7},{5,6},{6,5},{7,4},{8,11},{9,10},{10,... | collective-permute-start | bytes 49160 | tf_op jit(solution)/shard_map/ppermute | solution.py:325
  12.6 0.6 %collective-permute-start.4 = (bf16[64,128]{1,0:T(8,128)(2,1)S(1)}, bf16[64,128]{1,0:T(8,128)(2,1)S(1)}, u32[]{:S(2)}, u32[]{:S(2)}) collective-permute-start(bf16[64,128]{1,0:T(8,128)(2,1)S(1)} %get-tuple-element.63), channel_id=1, source_target_pairs={{0,1},{1,0},{2,3},{3,2},{4,5},{5,4},{6,7},{7,6},{8,9},{9,8},{10,11... | collective-permute-start | bytes 49160 | tf_op jit(solution)/shard_map/ppermute | solution.py:310
  13.2 0.2 join.4
  13.4 0.8 %collective-permute-start.7 = (bf16[64,128]{1,0:T(8,128)(2,1)S(1)}, bf16[64,128]{1,0:T(8,128)(2,1)S(1)}, u32[]{:S(2)}, u32[]{:S(2)}) collective-permute-start(bf16[64,128]{1,0:T(8,128)(2,1)S(1)} %get-tuple-element.71), channel_id=1, source_target_pairs={{0,3},{1,2},{2,1},{3,0},{4,7},{5,6},{6,5},{7,4},{8,11},{9,10},{10,... | collective-permute-start | bytes 49160 | tf_op jit(solution)/shard_map/ppermute | solution.py:325
  14.2 0.6 %collective-permute-start.8 = (bf16[64,128]{1,0:T(8,128)(2,1)S(1)}, bf16[64,128]{1,0:T(8,128)(2,1)S(1)}, u32[]{:S(2)}, u32[]{:S(2)}) collective-permute-start(bf16[64,128]{1,0:T(8,128)(2,1)S(1)} %get-tuple-element.72), channel_id=1, source_target_pairs={{0,1},{1,0},{2,3},{3,2},{4,5},{5,4},{6,7},{7,6},{8,9},{9,8},{10,11... | collective-permute-start | bytes 49160 | tf_op jit(solution)/shard_map/ppermute | solution.py:310
  14.9 0.2 residual.3
  15.1 1.6 %collective-permute-start.9 = (bf16[256,128]{1,0:T(8,128)(2,1)S(1)}, bf16[256,128]{1,0:T(8,128)(2,1)S(1)}, u32[]{:S(2)}, u32[]{:S(2)}) collective-permute-start(bf16[256,128]{1,0:T(8,128)(2,1)S(1)} %get-tuple-element.68._), channel_id=1, source_target_pairs={{0,8},{4,12},{8,0},{12,4},{16,24},{20,28},{24,16},{28,20},{1,9},{5... | collective-permute-start | bytes 196616 | tf_op jit(solution)/shard_map/ppermute | solution.py:310
  16.8 0.2 residual.4
  17.0 1.2 %operators.3 = (bf16[256,512]{1,0:T(8,128)(2,1)S(1)}, bf16[256,256]{1,0:T(8,128)(2,1)S(1)}, bf16[256,128]{1,0:T(8,128)(2,1)S(1)}, f32[256,1]{1,0:T(8,128)S(1)}, bf16[256,256]{1,0:T(8,128)(2,1)S(1)}) custom-call(bf16[256,128]{1,0:T(8,128)(2,1)S(1)} %get-tuple-element.68._, s32[3,3,1,4]{3,2,1,0:T(1,128)S(1)} %bitcast.3, ...), custom_call_target="tpu_custom_call" | custom-call | bytes 1147264 | tf_op jit(solution)/shard_map/operators/pallas_call | solution.py:52
  18.2 1.3 %collective-permute-done.9.other = bf16[256,128]{1,0:T(8,128)(2,1)S(1)} collective-permute-done((bf16[256,128]{1,0:T(8,128)(2,1)S(1)}, bf16[256,128]{1,0:T(8,128)(2,1)S(1)}, u32[]{:S(2)}, u32[]{:S(2)}) %collective-permute-start.9) | collective-permute-done | bytes 65568 | tf_op jit(solution)/shard_map/ppermute | solution.py:310
  19.4 0.2 join.5
  19.7 0.1 collective-permute-start.10
  19.8 1.5 %collective-permute-start.11 = (bf16[64,128]{1,0:T(8,128)(2,1)S(1)}, bf16[64,128]{1,0:T(8,128)(2,1)S(1)}, u32[]{:S(2)}, u32[]{:S(2)}) collective-permute-start(bf16[64,128]{1,0:T(8,128)(2,1)S(1)} %get-tuple-element.80), channel_id=1, source_target_pairs={{0,1},{1,0},{2,3},{3,2},{4,5},{5,4},{6,7},{7,6},{8,9},{9,8},{10,11... | collective-permute-start | bytes 49160 | tf_op jit(solution)/shard_map/ppermute | solution.py:310
  21.2 1.6 %collective-permute-start.12 = (bf16[256,128]{1,0:T(8,128)(2,1)S(1)}, bf16[256,128]{1,0:T(8,128)(2,1)S(1)}, u32[]{:S(2)}, u32[]{:S(2)}) collective-permute-start(bf16[256,128]{1,0:T(8,128)(2,1)S(1)} %get-tuple-element.83.refs_4_), channel_id=1, source_target_pairs={{0,4},{4,0},{8,12},{12,8},{16,20},{20,16},{24,28},{28,24},{1,5},{5... | collective-permute-start | bytes 196616 | tf_op jit(solution)/shard_map/ppermute | solution.py:310
  22.8 0.2 collective-permute-done.10.outer
  23.0 0.4 residual.5
  23.5 3.4 %collective-permute-start.15 = (bf16[256,128]{1,0:T(8,128)(2,1)S(1)}, bf16[256,128]{1,0:T(8,128)(2,1)S(1)}, u32[]{:S(2)}, u32[]{:S(2)}) collective-permute-start(bf16[256,128]{1,0:T(8,128)(2,1)S(1)} %get-tuple-element.82.refs_0_._.own), channel_id=1, source_target_pairs={{0,18},{1,19},{2,16},{3,17},{4,22},{5,23},{6,20},{7,21},{8,26},{9,... | collective-permute-start | bytes 196616 | tf_op jit(solution)/shard_map/ppermute | solution.py:319
  26.9 0.7 %collective-permute-start.16 = (bf16[256,128]{1,0:T(8,128)(2,1)S(1)}, bf16[256,128]{1,0:T(8,128)(2,1)S(1)}, u32[]{:S(2)}, u32[]{:S(2)}) collective-permute-start(bf16[256,128]{1,0:T(8,128)(2,1)S(1)} %get-tuple-element.82.refs_0_._.own), channel_id=1, source_target_pairs={{0,2},{1,3},{2,0},{3,1},{4,6},{5,7},{6,4},{7,5},{8,10},{9,11},{10,... | collective-permute-start | bytes 196616 | tf_op jit(solution)/shard_map/ppermute | solution.py:310
  27.6 0.3 collective-permute-start.13
  27.9 0.9 %fine_operators.1 = (bf16[256,256]{1,0:T(8,128)(2,1)S(1)}, bf16[256,256]{1,0:T(8,128)(2,1)S(1)}) custom-call(bf16[256,128]{1,0:T(8,128)(2,1)S(1)} %get-tuple-element.82.refs_0_._.own, s32[3,1,2,4]{3,2,1,0:T(2,128)S(1)} %bitcast.4, bf16[3,1,4,2,64,64]{5,4,3,2,1,0:T(8,128)(2,1)S(1)} %copy-done.2, bf16[3,1,4,2,64,64]{5,4,3,2,1,0:T(8,128)(2,1)S(1)} %copy-done.2, ...), custom_call_target="tpu_custom_call" | custom-call | flops 67108864 | bytes 723040 | tf_op jit(solution)/shard_map/fine_operators/pallas_call | solution.py:52
  28.9 0.1 copy-done.4
  29.0 1.1 %coarse_operators.1.refs_0_.inverse = bf16[256,1024]{1,0:T(8,128)(2,1)S(1)} custom-call(bf16[256,128]{1,0:T(8,128)(2,1)S(1)} %get-tuple-element.82.refs_0_._.own, bf16[256,128]{1,0:T(8,128)(2,1)S(1)} %collective-permute-done.12.refs_1_.refs_3_, s32[3,1,2,4]{3,2,1,0:T(2,128)S(1)} %bitcast.5, bf16[256,1024]{1,0:T(8,128)(2,1)S(1)} %copy-done.4, ...), custom_call_target="tpu_custom_call" | custom-call | flops 201326592 | bytes 984160 | tf_op jit(solution)/shard_map/coarse_operators/pallas_call | solution.py:52
  30.1 1.2 %collective-permute-done.15.far = bf16[256,128]{1,0:T(8,128)(2,1)S(1)} collective-permute-done((bf16[256,128]{1,0:T(8,128)(2,1)S(1)}, bf16[256,128]{1,0:T(8,128)(2,1)S(1)}, u32[]{:S(2)}, u32[]{:S(2)}) %collective-permute-start.15) | collective-permute-done | bytes 65568 | tf_op jit(solution)/shard_map/ppermute | solution.py:319
  31.3 0.2 collective-permute-done.16.own
  31.5 0.1 collective-permute-start.17
  31.6 1.5 %collective-permute-done.13.far = bf16[256,128]{1,0:T(8,128)(2,1)S(1)} collective-permute-done((bf16[256,128]{1,0:T(8,128)(2,1)S(1)}, bf16[256,128]{1,0:T(8,128)(2,1)S(1)}, u32[]{:S(2)}, u32[]{:S(2)}) %collective-permute-start.13) | collective-permute-done | bytes 65568 | tf_op jit(solution)/shard_map/ppermute | solution.py:319
  33.1 0.1 collective-permute-start.14
  33.2 1.2 %collective-permute-done.14.refs_1_ = bf16[256,128]{1,0:T(8,128)(2,1)S(1)} collective-permute-done((bf16[256,128]{1,0:T(8,128)(2,1)S(1)}, bf16[256,128]{1,0:T(8,128)(2,1)S(1)}, u32[]{:S(2)}, u32[]{:S(2)}) %collective-permute-start.14) | collective-permute-done | bytes 65568 | tf_op jit(solution)/shard_map/ppermute | solution.py:310
  34.4 0.5 %up.1 = (bf16[256,128]{1,0:T(8,128)(2,1)S(1)}, bf16[256,128]{1,0:T(8,128)(2,1)S(1)}) custom-call(bf16[256,1024]{1,0:T(8,128)(2,1)S(1)} %coarse_operators.1.refs_0_.inverse, bf16[256,128]{1,0:T(8,128)(2,1)S(1)} %share_sum.2.refs_0_, bf16[256,128]{1,0:T(8,128)(2,1)S(1)} %collective-permute-done.14.refs_1_, bf16[256,128]{1,0:T(8,128)(2,1)S(1)} %share_sum.3.refs_2_, ...), custom_call_target="tpu_custom_call" | custom-call | flops 83886080 | bytes 1179648 | tf_op jit(solution)/shard_map/up/pallas_call | solution.py:52
  34.9 2.0 %collective-permute-start.18 = (bf16[256,128]{1,0:T(8,128)(2,1)S(1)}, bf16[256,128]{1,0:T(8,128)(2,1)S(1)}, u32[]{:S(2)}, u32[]{:S(2)}) collective-permute-start(bf16[256,128]{1,0:T(8,128)(2,1)S(1)} %get-tuple-element.89), channel_id=1, source_target_pairs={{0,12},{4,8},{8,4},{12,0},{16,28},{20,24},{24,20},{28,16},{1,13},{... | collective-permute-start | bytes 196616 | tf_op jit(solution)/shard_map/ppermute | solution.py:310
  36.9 0.8 %collective-permute-start.19 = (bf16[256,128]{1,0:T(8,128)(2,1)S(1)}, bf16[256,128]{1,0:T(8,128)(2,1)S(1)}, u32[]{:S(2)}, u32[]{:S(2)}) collective-permute-start(bf16[256,128]{1,0:T(8,128)(2,1)S(1)} %get-tuple-element.90.refs_0_), channel_id=1, source_target_pairs={{0,4},{4,0},{8,12},{12,8},{16,20},{20,16},{24,28},{28,24},{1,5},{5... | collective-permute-start | bytes 196616 | tf_op jit(solution)/shard_map/ppermute | solution.py:310
  37.7 0.7 %collective-permute-start.20 = (bf16[256,128]{1,0:T(8,128)(2,1)S(1)}, bf16[256,128]{1,0:T(8,128)(2,1)S(1)}, u32[]{:S(2)}, u32[]{:S(2)}) collective-permute-start(bf16[256,128]{1,0:T(8,128)(2,1)S(1)} %get-tuple-element.89), channel_id=1, source_target_pairs={{0,8},{4,12},{8,0},{12,4},{16,24},{20,28},{24,16},{28,20},{1,9},{5... | collective-permute-start | bytes 196616 | tf_op jit(solution)/shard_map/ppermute | solution.py:310
  38.5 0.8 %output.2.refs_8_ = f32[1,256,512]{2,1,0:T(8,128)} custom-call(bf16[256,128]{1,0:T(8,128)(2,1)S(1)} %get-tuple-element.90.refs_0_, f32[256,512]{1,0:T(8,128)S(1)} %get-tuple-element.91.refs_1_.refs_5_, bf16[256,256]{1,0:T(8,128)(2,1)S(1)} %get-tuple-element.92.refs_2_.refs_6_, bf16[256,256]{1,0:T(8,128)(2,1)S(1)} %get-tuple-element.86.refs_1_.refs_6_.refs_3_.refs_7_), custom_call_target="tpu_custom_call" | custom-call | flops 16777216 | bytes 851968 | tf_op jit(solution)/shard_map/output/pallas_call | solution.py:52
  39.3 0.9 %collective-permute-done.18.refs_0_ = bf16[256,128]{1,0:T(8,128)(2,1)S(1)} collective-permute-done((bf16[256,128]{1,0:T(8,128)(2,1)S(1)}, bf16[256,128]{1,0:T(8,128)(2,1)S(1)}, u32[]{:S(2)}, u32[]{:S(2)}) %collective-permute-start.18) | collective-permute-done | bytes 65568 | tf_op jit(solution)/shard_map/ppermute | solution.py:310
  40.3 1.2 %collective-permute-done.19.refs_1_ = bf16[256,128]{1,0:T(8,128)(2,1)S(1)} collective-permute-done((bf16[256,128]{1,0:T(8,128)(2,1)S(1)}, bf16[256,128]{1,0:T(8,128)(2,1)S(1)}, u32[]{:S(2)}, u32[]{:S(2)}) %collective-permute-start.19) | collective-permute-done | bytes 65568 | tf_op jit(solution)/shard_map/ppermute | solution.py:310
  41.5 0.5 %collective-permute-done.20.refs_2_ = bf16[256,128]{1,0:T(8,128)(2,1)S(1)} collective-permute-done((bf16[256,128]{1,0:T(8,128)(2,1)S(1)}, bf16[256,128]{1,0:T(8,128)(2,1)S(1)}, u32[]{:S(2)}, u32[]{:S(2)}) %collective-permute-start.20) | collective-permute-done | bytes 65568 | tf_op jit(solution)/shard_map/ppermute | solution.py:310
  42.0 1.3 %output.3 = f32[1,256,512]{2,1,0:T(8,128)} custom-call(bf16[256,128]{1,0:T(8,128)(2,1)S(1)} %collective-permute-done.18.refs_0_, bf16[256,128]{1,0:T(8,128)(2,1)S(1)} %collective-permute-done.19.refs_1_, bf16[256,128]{1,0:T(8,128)(2,1)S(1)} %collective-permute-done.20.refs_2_, ...), custom_call_target="tpu_custom_call", output_to_operand_aliasing={{}: (8, {})} | custom-call | flops 50331648 | bytes 1638400 | tf_op jit(solution)/shard_map/output/pallas_call | solution.py:52
  (27 shorter events, 0.1 us)
Async XLA Ops:
  0.0 4.4 %copy-start = (bf16[3,1,4,5,64,64]{5,4,3,2,1,0:T(8,128)(2,1)S(1)}, bf16[3,1,4,5,64,64]{5,4,3,2,1,0:T(8,128)(2,1)}, u32[]{:S(2)}) copy-start(bf16[3,1,4,5,64,64]{5,4,3,2,1,0:T(8,128)(2,1)} %blocks.7) | copy-start | bytes 1474564
  0.0 4.4 %copy-start.3 = (f32[1,256,512]{2,1,0:T(8,128)S(1)}, f32[1,256,512]{2,1,0:T(8,128)}, u32[]{:S(2)}) copy-start(f32[1,256,512]{2,1,0:T(8,128)} %rhs.3) | copy-start | bytes 1572868
  1.3 4.8 %collective-permute-start.1 = (bf16[64,512]{1,0:T(8,128)(2,1)S(1)}, bf16[64,512]{1,0:T(8,128)(2,1)S(1)}, u32[]{:S(2)}, u32[]{:S(2)}) collective-permute-start(bf16[64,512]{1,0:T(8,128)(2,1)S(1)} %get-tuple-element.53), channel_id=1, source_target_pairs={{0,1},{1,0},{2,3},{3,2},{4,5},{5,4},{6,7},{7,6},{8,9},{9,8},{10,11... | collective-permute-start | bytes 196616 | tf_op jit(solution)/shard_map/ppermute | solution.py:310
  1.8 4.3 %collective-permute-start = (bf16[64,256]{1,0:T(8,128)(2,1)S(1)}, bf16[64,256]{1,0:T(8,128)(2,1)S(1)}, u32[]{:S(2)}, u32[]{:S(2)}) collective-permute-start(bf16[64,256]{1,0:T(8,128)(2,1)S(1)} %get-tuple-element.49._), channel_id=1, source_target_pairs={{0,3},{1,2},{2,1},{3,0},{4,7},{5,6},{6,5},{7,4},{8,11},{9,10},{10,... | collective-permute-start | bytes 98312 | tf_op jit(solution)/shard_map/ppermute | solution.py:325
  4.4 3.6 %collective-permute-start.5 = (bf16[64,256]{1,0:T(8,128)(2,1)S(1)}, bf16[64,256]{1,0:T(8,128)(2,1)S(1)}, u32[]{:S(2)}, u32[]{:S(2)}) collective-permute-start(bf16[64,256]{1,0:T(8,128)(2,1)S(1)} %get-tuple-element.64), channel_id=1, source_target_pairs={{0,3},{1,2},{2,1},{3,0},{4,7},{5,6},{6,5},{7,4},{8,11},{9,10},{10,... | collective-permute-start | bytes 98312 | tf_op jit(solution)/shard_map/ppermute | solution.py:325
  6.1 3.5 %copy-start.1 = (bf16[3,1,4,3,64,64]{5,4,3,2,1,0:T(8,128)(2,1)S(1)}, bf16[3,1,4,3,64,64]{5,4,3,2,1,0:T(8,128)(2,1)}, u32[]{:S(2)}) copy-start(bf16[3,1,4,3,64,64]{5,4,3,2,1,0:T(8,128)(2,1)} %refs_0_.3) | copy-start | bytes 884740
  6.3 4.5 %collective-permute-start.2 = (bf16[256,128]{1,0:T(8,128)(2,1)S(1)}, bf16[256,128]{1,0:T(8,128)(2,1)S(1)}, u32[]{:S(2)}, u32[]{:S(2)}) collective-permute-start(bf16[256,128]{1,0:T(8,128)(2,1)S(1)} %get-tuple-element.54._), channel_id=1, source_target_pairs={{0,4},{4,0},{8,12},{12,8},{16,20},{20,16},{24,28},{28,24},{1,5},{5... | collective-permute-start | bytes 196616 | tf_op jit(solution)/shard_map/ppermute | solution.py:310
  8.0 1.6 %copy-start.5 = (s32[3,1,4,3]{2,1,3,0:T(1,128)S(1)}, s32[3,1,4,3]{2,1,3,0:T(1,128)}, u32[]{:S(2)}) copy-start(s32[3,1,4,3]{2,1,3,0:T(1,128)} %param.11) | copy-start | bytes 436
  8.2 5.0 %collective-permute-start.6 = (bf16[256,128]{1,0:T(8,128)(2,1)S(1)}, bf16[256,128]{1,0:T(8,128)(2,1)S(1)}, u32[]{:S(2)}, u32[]{:S(2)}) collective-permute-start(bf16[256,128]{1,0:T(8,128)(2,1)S(1)} %get-tuple-element.66), channel_id=1, source_target_pairs={{0,4},{4,0},{8,12},{12,8},{16,20},{20,16},{24,28},{28,24},{1,5},{5... | collective-permute-start | bytes 196616 | tf_op jit(solution)/shard_map/ppermute | solution.py:310
  11.0 3.9 %collective-permute-start.3 = (bf16[64,128]{1,0:T(8,128)(2,1)S(1)}, bf16[64,128]{1,0:T(8,128)(2,1)S(1)}, u32[]{:S(2)}, u32[]{:S(2)}) collective-permute-start(bf16[64,128]{1,0:T(8,128)(2,1)S(1)} %get-tuple-element.62), channel_id=1, source_target_pairs={{0,3},{1,2},{2,1},{3,0},{4,7},{5,6},{6,5},{7,4},{8,11},{9,10},{10,... | collective-permute-start | bytes 49160 | tf_op jit(solution)/shard_map/ppermute | solution.py:325
  12.6 2.3 %collective-permute-start.4 = (bf16[64,128]{1,0:T(8,128)(2,1)S(1)}, bf16[64,128]{1,0:T(8,128)(2,1)S(1)}, u32[]{:S(2)}, u32[]{:S(2)}) collective-permute-start(bf16[64,128]{1,0:T(8,128)(2,1)S(1)} %get-tuple-element.63), channel_id=1, source_target_pairs={{0,1},{1,0},{2,3},{3,2},{4,5},{5,4},{6,7},{7,6},{8,9},{9,8},{10,11... | collective-permute-start | bytes 49160 | tf_op jit(solution)/shard_map/ppermute | solution.py:310
  13.4 3.4 %collective-permute-start.7 = (bf16[64,128]{1,0:T(8,128)(2,1)S(1)}, bf16[64,128]{1,0:T(8,128)(2,1)S(1)}, u32[]{:S(2)}, u32[]{:S(2)}) collective-permute-start(bf16[64,128]{1,0:T(8,128)(2,1)S(1)} %get-tuple-element.71), channel_id=1, source_target_pairs={{0,3},{1,2},{2,1},{3,0},{4,7},{5,6},{6,5},{7,4},{8,11},{9,10},{10,... | collective-permute-start | bytes 49160 | tf_op jit(solution)/shard_map/ppermute | solution.py:325
  14.2 2.5 %collective-permute-start.8 = (bf16[64,128]{1,0:T(8,128)(2,1)S(1)}, bf16[64,128]{1,0:T(8,128)(2,1)S(1)}, u32[]{:S(2)}, u32[]{:S(2)}) collective-permute-start(bf16[64,128]{1,0:T(8,128)(2,1)S(1)} %get-tuple-element.72), channel_id=1, source_target_pairs={{0,1},{1,0},{2,3},{3,2},{4,5},{5,4},{6,7},{7,6},{8,9},{9,8},{10,11... | collective-permute-start | bytes 49160 | tf_op jit(solution)/shard_map/ppermute | solution.py:310
  15.1 4.3 %collective-permute-start.9 = (bf16[256,128]{1,0:T(8,128)(2,1)S(1)}, bf16[256,128]{1,0:T(8,128)(2,1)S(1)}, u32[]{:S(2)}, u32[]{:S(2)}) collective-permute-start(bf16[256,128]{1,0:T(8,128)(2,1)S(1)} %get-tuple-element.68._), channel_id=1, source_target_pairs={{0,8},{4,12},{8,0},{12,4},{16,24},{20,28},{24,16},{28,20},{1,9},{5... | collective-permute-start | bytes 196616 | tf_op jit(solution)/shard_map/ppermute | solution.py:310
  19.7 8.2 %copy-start.2 = (bf16[3,1,4,2,64,64]{5,4,3,2,1,0:T(8,128)(2,1)S(1)}, bf16[3,1,4,2,64,64]{5,4,3,2,1,0:T(8,128)(2,1)}, u32[]{:S(2)}) copy-start(bf16[3,1,4,2,64,64]{5,4,3,2,1,0:T(8,128)(2,1)} %blocks_1.1) | copy-start | bytes 589828
  19.7 3.3 %collective-permute-start.10 = (bf16[64,128]{1,0:T(8,128)(2,1)S(1)}, bf16[64,128]{1,0:T(8,128)(2,1)S(1)}, u32[]{:S(2)}, u32[]{:S(2)}) collective-permute-start(bf16[64,128]{1,0:T(8,128)(2,1)S(1)} %get-tuple-element.79), channel_id=1, source_target_pairs={{0,3},{1,2},{2,1},{3,0},{4,7},{5,6},{6,5},{7,4},{8,11},{9,10},{10,... | collective-permute-start | bytes 49160 | tf_op jit(solution)/shard_map/ppermute | solution.py:325
  19.8 3.3 %collective-permute-start.11 = (bf16[64,128]{1,0:T(8,128)(2,1)S(1)}, bf16[64,128]{1,0:T(8,128)(2,1)S(1)}, u32[]{:S(2)}, u32[]{:S(2)}) collective-permute-start(bf16[64,128]{1,0:T(8,128)(2,1)S(1)} %get-tuple-element.80), channel_id=1, source_target_pairs={{0,1},{1,0},{2,3},{3,2},{4,5},{5,4},{6,7},{7,6},{8,9},{9,8},{10,11... | collective-permute-start | bytes 49160 | tf_op jit(solution)/shard_map/ppermute | solution.py:310
  21.2 7.6 %collective-permute-start.12 = (bf16[256,128]{1,0:T(8,128)(2,1)S(1)}, bf16[256,128]{1,0:T(8,128)(2,1)S(1)}, u32[]{:S(2)}, u32[]{:S(2)}) collective-permute-start(bf16[256,128]{1,0:T(8,128)(2,1)S(1)} %get-tuple-element.83.refs_4_), channel_id=1, source_target_pairs={{0,4},{4,0},{8,12},{12,8},{16,20},{20,16},{24,28},{28,24},{1,5},{5... | collective-permute-start | bytes 196616 | tf_op jit(solution)/shard_map/ppermute | solution.py:310
  23.5 4.5 %copy-start.6 = (s32[3,1,4,2]{2,3,1,0:T(2,128)S(1)}, s32[3,1,4,2]{2,3,1,0:T(2,128)}, u32[]{:S(2)}) copy-start(s32[3,1,4,2]{2,3,1,0:T(2,128)} %param.13) | copy-start | bytes 292
  23.5 7.8 %collective-permute-start.15 = (bf16[256,128]{1,0:T(8,128)(2,1)S(1)}, bf16[256,128]{1,0:T(8,128)(2,1)S(1)}, u32[]{:S(2)}, u32[]{:S(2)}) collective-permute-start(bf16[256,128]{1,0:T(8,128)(2,1)S(1)} %get-tuple-element.82.refs_0_._.own), channel_id=1, source_target_pairs={{0,18},{1,19},{2,16},{3,17},{4,22},{5,23},{6,20},{7,21},{8,26},{9,... | collective-permute-start | bytes 196616 | tf_op jit(solution)/shard_map/ppermute | solution.py:319
  26.9 4.6 %collective-permute-start.16 = (bf16[256,128]{1,0:T(8,128)(2,1)S(1)}, bf16[256,128]{1,0:T(8,128)(2,1)S(1)}, u32[]{:S(2)}, u32[]{:S(2)}) collective-permute-start(bf16[256,128]{1,0:T(8,128)(2,1)S(1)} %get-tuple-element.82.refs_0_._.own), channel_id=1, source_target_pairs={{0,2},{1,3},{2,0},{3,1},{4,6},{5,7},{6,4},{7,5},{8,10},{9,11},{10,... | collective-permute-start | bytes 196616 | tf_op jit(solution)/shard_map/ppermute | solution.py:310
  27.6 5.5 %collective-permute-start.13 = (bf16[256,128]{1,0:T(8,128)(2,1)S(1)}, bf16[256,128]{1,0:T(8,128)(2,1)S(1)}, u32[]{:S(2)}, u32[]{:S(2)}) collective-permute-start(bf16[256,128]{1,0:T(8,128)(2,1)S(1)} %get-tuple-element.82.refs_0_._.own), channel_id=1, source_target_pairs={{0,16},{1,17},{2,18},{3,19},{4,20},{5,21},{6,22},{7,23},{8,24},{9,... | collective-permute-start | bytes 196616 | tf_op jit(solution)/shard_map/ppermute | solution.py:319
  27.9 1.0 %copy-start.4 = (bf16[256,1024]{1,0:T(8,128)(2,1)S(1)}, bf16[256,1024]{1,0:T(8,128)(2,1)}, u32[]{:S(2)}) copy-start(bf16[256,1024]{1,0:T(8,128)(2,1)} %refs_3_.1) | copy-start | bytes 1572868
  31.5 1.6 %collective-permute-start.17 = (bf16[256,128]{1,0:T(8,128)(2,1)S(1)}, bf16[256,128]{1,0:T(8,128)(2,1)S(1)}, u32[]{:S(2)}, u32[]{:S(2)}) collective-permute-start(bf16[256,128]{1,0:T(8,128)(2,1)S(1)} %share_sum.3.refs_2_), channel_id=1, source_target_pairs={{0,1},{1,0},{2,3},{3,2},{4,5},{5,4},{6,7},{7,6},{8,9},{9,8},{10,11... | collective-permute-start | bytes 196616 | tf_op jit(solution)/shard_map/ppermute | solution.py:310
  33.1 1.3 %collective-permute-start.14 = (bf16[256,128]{1,0:T(8,128)(2,1)S(1)}, bf16[256,128]{1,0:T(8,128)(2,1)S(1)}, u32[]{:S(2)}, u32[]{:S(2)}) collective-permute-start(bf16[256,128]{1,0:T(8,128)(2,1)S(1)} %share_sum.2.refs_0_), channel_id=1, source_target_pairs={{0,1},{1,0},{2,3},{3,2},{4,5},{5,4},{6,7},{7,6},{8,9},{9,8},{10,11... | collective-permute-start | bytes 196616 | tf_op jit(solution)/shard_map/ppermute | solution.py:310
  34.9 5.3 %collective-permute-start.18 = (bf16[256,128]{1,0:T(8,128)(2,1)S(1)}, bf16[256,128]{1,0:T(8,128)(2,1)S(1)}, u32[]{:S(2)}, u32[]{:S(2)}) collective-permute-start(bf16[256,128]{1,0:T(8,128)(2,1)S(1)} %get-tuple-element.89), channel_id=1, source_target_pairs={{0,12},{4,8},{8,4},{12,0},{16,28},{20,24},{24,20},{28,16},{1,13},{... | collective-permute-start | bytes 196616 | tf_op jit(solution)/shard_map/ppermute | solution.py:310
  36.9 4.6 %collective-permute-start.19 = (bf16[256,128]{1,0:T(8,128)(2,1)S(1)}, bf16[256,128]{1,0:T(8,128)(2,1)S(1)}, u32[]{:S(2)}, u32[]{:S(2)}) collective-permute-start(bf16[256,128]{1,0:T(8,128)(2,1)S(1)} %get-tuple-element.90.refs_0_), channel_id=1, source_target_pairs={{0,4},{4,0},{8,12},{12,8},{16,20},{20,16},{24,28},{28,24},{1,5},{5... | collective-permute-start | bytes 196616 | tf_op jit(solution)/shard_map/ppermute | solution.py:310
  37.7 4.3 %collective-permute-start.20 = (bf16[256,128]{1,0:T(8,128)(2,1)S(1)}, bf16[256,128]{1,0:T(8,128)(2,1)S(1)}, u32[]{:S(2)}, u32[]{:S(2)}) collective-permute-start(bf16[256,128]{1,0:T(8,128)(2,1)S(1)} %get-tuple-element.89), channel_id=1, source_target_pairs={{0,8},{4,12},{8,0},{12,4},{16,24},{20,28},{24,16},{28,20},{1,9},{5... | collective-permute-start | bytes 196616 | tf_op jit(solution)/shard_map/ppermute | solution.py:310

commit v11 on v10

v11 whole, which is shorter than its diff:
```python
import functools

import jax
import jax.numpy as jnp
from jax import lax
from jax.experimental import pallas as pl
from jax.experimental.pallas import tpu as pltpu
from jax.sharding import PartitionSpec as P

relax_down = 0.7
relax_up = 0.5
f32 = jnp.float32
bf16 = jnp.bfloat16
grant = 12 * 1024 * 1024


def matmul(a, b):
    return jnp.dot(a, b, preferred_element_type=f32)


def array(shape, dtype):
    return jax.ShapeDtypeStruct(shape, dtype)


def whole():
    return pl.BlockSpec(memory_space=pltpu.VMEM)


def level_block(value, level_idx):
    shape = (1,) + value.shape[1:]
    return pl.BlockSpec(shape, lambda i: (level_idx,) + (0,) * (value.ndim - 1))


def scalars():
    return pl.BlockSpec(memory_space=pltpu.SMEM)


def in_hbm(value):
    return pltpu.with_memory_space_constraint(value, pltpu.HBM), pl.BlockSpec(memory_space=pltpu.HBM)


def in_vmem(value):
    return pltpu.with_memory_space_constraint(value, pltpu.VMEM)


def run(body, name, outs, operands, flops=0, scratch=(), out_space=pltpu.VMEM, aliases=None):
    arrays = [o[0] if isinstance(o, tuple) else in_vmem(o) for o in operands]
    specs = [o[1] if isinstance(o, tuple) else whole() for o in operands]
    windows = any(isinstance(o, tuple) and o[1].block_shape is not None for o in operands)
    moved = sum(a.size * a.dtype.itemsize for a in arrays)
    return pl.pallas_call(
        body,
        grid=(1,) if windows else (),
        out_shape=[out_space(o.shape, o.dtype) for o in outs],
        in_specs=specs,
        out_specs=[pl.BlockSpec(memory_space=out_space)] * len(outs),
        input_output_aliases=aliases or {},
        scratch_shapes=list(scratch),
        compiler_params=pltpu.CompilerParams(vmem_limit_bytes=grant),
        cost_estimate=pl.CostEstimate(flops=flops, bytes_accessed=moved, transcendentals=0),
        name=name,
    )(*arrays)


def diagonal_of(block):
    size = block.shape[0]
    rows = lax.broadcasted_iota(jnp.int32, (size, size), 0)
    lanes = lax.broadcasted_iota(jnp.int32, (size, size), 1)
    return jnp.sum(jnp.where(rows == lanes, block, 0.0), axis=1, keepdims=True)


def placed(base, others, ids, target):
    total = base
    for block, ident in zip(others, ids):
        term = block * jnp.where(ident == target, 1.0, 0.0).astype(f32)
        total = term if total is None else total + term
    return total


def parity_of():
    return lax.rem(lax.axis_index("narrow"), 2)


def put_ends(first, last, inner_ref, outer_ref):
    even = parity_of() == 0
    inner_ref[...] = jnp.where(even, last, first)
    outer_ref[...] = jnp.where(even, first, last)


def assemble_galerkin(level_idx, cols, blocks, local_ref, rim_ref, scale_ref):
    count, slots, size = blocks.shape[2], blocks.shape[3], blocks.shape[4]
    parity = parity_of()
    piece = lax.axis_index("narrow")
    last = lax.axis_size("narrow") - 1
    inside = jnp.where((piece == 0) | (piece == last), 0.0, 1.0).astype(f32)
    for b in range(count):
        held = [blocks[0, 0, b, s].astype(f32) for s in range(slots)]
        ids = [cols[level_idx, 0, b, s] for s in range(1, slots)]
        rows = pl.ds(b * size, size)
        scale_ref[rows, :] = 1.0 / diagonal_of(held[0])
        line = [placed(held[0] if c == b else None, held[1:], ids, c) for c in range(count)]
        local_ref[rows, :] = jnp.concatenate(line, axis=1).astype(bf16)
        rims = [
            placed(None, held[1:], ids, count + 1 - parity),
            placed(None, held[1:], ids, count + parity) * inside,
        ]
        rim_ref[rows, :] = jnp.concatenate(rims, axis=1).astype(bf16)


def assemble_share(level_idx, cols, blocks, out_ref):
    count, slots, size = blocks.shape[2], blocks.shape[3], blocks.shape[4]
    bit = bit_of(level_idx)
    for b in range(count):
        held = [blocks[0, 0, b, s].astype(f32) for s in range(slots)]
        ids = [cols[level_idx, s, 0, b] for s in range(2, slots)]
        own = jnp.where(bit == 0, held[0], held[1])
        first = bit * count
        line = [placed(own if c == b else None, held[2:], ids, first + c) for c in range(count)]
        out_ref[pl.ds(b * size, size), :] = jnp.concatenate(line, axis=1).astype(bf16)


def assemble_prolong(level_idx, cols, blocks, out_ref):
    count, slots, size = blocks.shape[2], blocks.shape[3], blocks.shape[4]
    for b in range(count):
        held = [blocks[0, 0, b, s].astype(f32) for s in range(slots)]
        ids = [cols[level_idx, 0, s, b] for s in range(1, slots)]
        line = [placed(held[0] if c == b else None, held[1:], ids, c) for c in range(count)]
        out_ref[pl.ds(b * size, size), :] = jnp.concatenate(line, axis=1).astype(bf16)


def start_kernel(places, rhs, blocks, gtable, rtable, rblocks, *refs):
    gheld, rheld, rheld_blocks, held, inner_ref, *outers, rows, outer, pivots, sems = refs
    count, size = blocks.shape[2], blocks.shape[4]
    copies = []
    for slot, which in enumerate((0, count - 1)):
        source = rhs.at[0, pl.ds(which * size, size), :]
        copies.append(pltpu.make_async_copy(source, rows.at[slot], sems.at[slot]))
        source = blocks.at[0, 0, which, 0]
        copies.append(pltpu.make_async_copy(source, pivots.at[slot], sems.at[2 + slot]))
    copies.append(pltpu.make_async_copy(gtable, gheld, sems.at[4]))
    copies.append(pltpu.make_async_copy(rtable, rheld, sems.at[5]))
    copies.append(pltpu.make_async_copy(rblocks.at[pl.ds(0, 1)], rheld_blocks, sems.at[6]))
    for which in range(count):
        source = blocks.at[1, 0, which, 0]
        copies.append(pltpu.make_async_copy(source, held.at[which], sems.at[7 + which]))
    for copy in copies:
        copy.start()
    for copy in copies:
        copy.wait()
    first, last = (
        (rows[slot] * (relax_down / diagonal_of(pivots[slot].astype(f32)))).astype(bf16)
        for slot in range(2)
    )
    put_ends(first, last, inner_ref, outer)
    for ref, pair in zip(outers, places):
        width = ref.shape[1] // 2
        for slot, place in enumerate(pair):
            ref[:, slot * width : (slot + 1) * width] = outer[:, lanes_of(place, width)]


def first_local_kernel(
    rhs, _, cols, blocks, rcols, rblocks, pivots, rest, base, local, rim, scale, share, next_scale
):
    assemble_galerkin(0, cols, blocks, local, rim, scale)
    smoothed = rhs[0] * (relax_down * scale[...])
    left = rhs[0] - matmul(local[...], smoothed.astype(bf16))
    rest[...] = left
    base[...] = smoothed + (relax_up * scale[...]) * left
    assemble_share(0, rcols, rblocks, share)
    size = pivots.shape[1]
    for b in range(pivots.shape[0]):
        next_scale[pl.ds(b * size, size), :] = relax_down / diagonal_of(pivots[b].astype(f32))


def bit_of(level_idx):
    return lax.axis_index("wide") >> level_idx & 1


def lanes_of(place, width):
    start = 0
    for level_idx, flip, step in place:
        start = start + (bit_of(level_idx) ^ flip) * step
    return pl.ds(pl.multiple_of(start, width), width)


def ends_of(part, next_scale):
    size = part.shape[0] // 4
    first = (part[:size] * next_scale[:size, :]).astype(bf16)
    last = (part[-size:] * next_scale[-size:, :]).astype(bf16)
    even = parity_of() == 0
    return jnp.where(even, last, first), jnp.where(even, first, last)


def first_residual_kernel(places, rest, rim, outer, inner, share, next_scale, *refs):
    held, refs = refs[:-6], refs[-6:]
    kept, joined = refs[0], refs[1:]
    ends = joined[1:]
    width = kept.shape[1]
    for slot, place in enumerate(places):
        lanes = lanes_of(place, width)
        columns = pl.ds(slot * width, width)
        rims = jnp.concatenate([inner[:, lanes], outer[:, columns]], axis=0)
        residual = (rest[:, lanes] - matmul(rim[...], rims)).astype(bf16)
        part = matmul(share[...], residual)
        if slot:
            kept[...] = part
        else:
            joined[0][:, joined[0].shape[1] - width :] = part.astype(bf16)
        for ref, made in zip(ends[2 * slot : 2 * slot + 2], ends_of(part, next_scale)):
            ref[:, ref.shape[1] - width :] = made
    for ref, value in zip(joined, held):
        ref[:, :width] = value[...]


def level_kernel(slot, kinds, rhs_own, rhs_far, scale, local, rim, *refs):
    far_inner, far_outer, near_inner, near_outer, share, *refs = refs
    width = rhs_own.shape[1]
    columns = pl.ds(slot * width, width)
    halo = [
        (far[:, columns].astype(f32) + near[:, columns].astype(f32)).astype(bf16)
        for far, near in ((far_inner, near_inner), (far_outer, near_outer))
    ]
    rhs = rhs_own[...] + rhs_far[:, columns].astype(f32)
    smoothed = rhs * (relax_down * scale[...])
    left = rhs - matmul(local[...], smoothed.astype(bf16))
    rims = jnp.concatenate(halo, axis=0)
    residual = (left - matmul(rim[...], rims)).astype(bf16)
    part = matmul(share[...], residual)
    if "ends" in kinds:
        next_scale, *refs = refs
    base, *refs = refs
    made = smoothed + (relax_up * scale[...]) * left
    base[...] = made.astype(base.dtype)
    if "sent" in kinds:
        refs[0][...] = part.astype(bf16)
        refs = refs[1:]
    if "kept" in kinds:
        refs[0][...] = part
        refs = refs[1:]
    if "ends" in kinds:
        refs[0][...], refs[1][...] = ends_of(part, next_scale)


def operators_kernel(level_idx, _, cols, blocks, rcols, rblocks, *refs):
    if len(refs) > 4:
        pivots, *refs, next_scale = refs
        size = pivots.shape[-1]
        for b in range(pivots.shape[2]):
            made = relax_down / diagonal_of(pivots[0, 0, b, 0].astype(f32))
            next_scale[pl.ds(b * size, size), :] = made
    local, rim, scale, share = refs
    assemble_galerkin(level_idx, cols, blocks, local, rim, scale)
    assemble_share(level_idx, rcols, rblocks, share)


def raising(level_idx, pcols, blocks, local, scale, held):
    assemble_prolong(level_idx, pcols, blocks, held)
    applied = matmul(local[...], held[...])
    return (held[...].astype(f32) - (relax_up * scale[...]) * applied).astype(bf16)


def coarse_operators_kernel(first, levels, *refs):
    _, one, two, pcols, inverse, *refs = refs
    places = range(first, levels)
    blocks, refs = refs[: len(places)], refs[len(places) :]
    pairs, refs = refs[: 2 * len(places)], refs[2 * len(places) :]
    pair, coarse, *up, held = refs
    width = one.shape[1]
    pair[:, :width] = one[...]
    pair[:, width:] = two[...]
    for idx in places:
        slot = idx - first
        made = raising(idx, pcols, blocks[slot], pairs[2 * slot + 1], pairs[2 * slot], held)
        if idx == levels - 1:
            coarse[...] = matmul(made, inverse[...]).astype(bf16)
        else:
            up[slot][...] = made


def fine_operators_kernel(
    places, _, pcols, blocks_0, blocks_1, scale_0, local_0, scale_1, local_1,
    base, bases, lower, both, total, held,
):
    lower[...] = raising(0, pcols, blocks_0, local_0, scale_0, held)
    upper = raising(1, pcols, blocks_1, local_1, scale_1, held)
    both[...] = matmul(lower[...], upper).astype(bf16)
    total_kernel(places, base, bases, lower, total)


def total_kernel(places, base, bases, lower, total):
    width = bases.shape[1] // len(places)
    for slot, place in enumerate(places):
        columns = pl.ds(slot * width, width)
        lanes = lanes_of(place, width)
        total[:, columns] = base[:, lanes] + matmul(lower[...], bases[:, columns])


def inverse_part(inverse, part, offset):
    depth = part.shape[0]
    piece = lax.axis_index("narrow") ^ offset
    return matmul(inverse[:, pl.ds(pl.multiple_of(piece * depth, depth), depth)], part[...])


def share_sum_kernel(far, own, *refs):
    refs[-1][...] = (far[...].astype(f32) + own[...].astype(f32)).astype(bf16)


def up_kernel(offsets, inverse, *refs):
    value = refs[len(offsets)][...]
    for part, offset in zip(refs, offsets):
        value = value + inverse_part(inverse, part, offset)
    refs, out = refs[len(offsets) + 1 : -1], refs[-1]
    for step in range(len(refs) // 2):
        value = refs[2 * step][...] + matmul(refs[2 * step + 1][...], value.astype(bf16))
    out[...] = value.astype(bf16)


def output_kernel(places, slots, *refs):
    coarse, totals = refs[: len(places)], refs[len(places) : 2 * len(places)]
    both, refs = refs[2 * len(places)], refs[2 * len(places) :]
    out, made, sems = refs[-3:]
    copies = []
    for item, (place, value) in enumerate(zip(places, coarse)):
        width = value.shape[1]
        held = totals[item][:, slots[item] * width : (slots[item] + 1) * width]
        made[item] = held + matmul(both[...], value[...])
        target = out.at[0, :, lanes_of(place, width)]
        copy = pltpu.make_async_copy(made.at[item], target, sems.at[item])
        copy.start()
        copies.append(copy)
    for copy in copies:
        copy.wait()


def exchange(value, axis, bit):
    count = lax.axis_size(axis)
    return lax.ppermute(value, axis, [(i, i ^ bit) for i in range(count)])


def exchange_both(value, bit, beside):
    wide, narrow = lax.axis_size("wide"), lax.axis_size("narrow")
    pairs = [
        (w * narrow + j, (w ^ bit) * narrow + beside(j)) for w in range(wide) for j in range(narrow)
    ]
    return lax.ppermute(value, ("wide", "narrow"), pairs)


def swap_ends(inner, outer, bit):
    count = lax.axis_size("narrow")
    outer = exchange_both(outer, bit, lambda j: (j + 1 if j % 2 else j - 1) % count)
    return exchange_both(inner, bit, lambda j: j ^ 1), outer


def swap_outer(outer):
    count = lax.axis_size("narrow")
    gaps = [(i, (i + 1 if i % 2 else i - 1) % count) for i in range(count)]
    return lax.ppermute(outer, "narrow", gaps)


def on_device(
    level_rhs,
    galerkin_cols,
    galerkin_blocks,
    restrict_cols,
    restrict_blocks,
    prolong_cols,
    prolong_blocks,
    coarse_inverse,
):
    levels = galerkin_cols.shape[0]
    count = galerkin_cols.shape[2]
    size = galerkin_blocks.shape[-1]
    rows, fields = level_rhs.shape[1:]
    half = fields // 2
    width = half // 2
    last = levels - 1
    pieces = lax.axis_size("narrow")
    pcols = prolong_cols.transpose(0, 1, 3, 2), scalars()
    rtable = restrict_cols.transpose(0, 3, 1, 2)
    square_shape = array((rows, rows), bf16)
    scale_shape = array((rows, 1), f32)
    operator_shapes = [square_shape, array((rows, 2 * size), bf16), scale_shape]
    chunk_shape = array((rows, width), bf16)
    real_shape = array((rows, width), f32)
    held = [pltpu.VMEM((rows, rows), bf16)]

    def ends_shape(columns):
        return array((size, columns), bf16)

    def of_level(value, level_idx):
        return value, level_block(value, level_idx)

    def pivots_of(level_idx):
        shape = (1, 1, count, 1, size, size)
        return galerkin_blocks, pl.BlockSpec(shape, lambda i: (level_idx, 0, 0, 0, 0, 0))

    def flops(columns, products=1):
        return 2 * products * rows * rows * columns

    def place_of(far, given):
        return (0, far, half), (1, given, width)

    pairs = [(place_of(1, given), place_of(0, given)) for given in (1, 0)]
    first_restrict = (1,) + restrict_blocks.shape[1:]
    gcols, rcols, rfirst, pivots, inner, *outers = run(
        functools.partial(start_kernel, pairs), "start",
        [array(galerkin_cols.shape, jnp.int32), array(rtable.shape, jnp.int32),
         array(first_restrict, bf16), array((count, size, size), bf16), ends_shape(fields)]
        + [ends_shape(half)] * 2,
        [in_hbm(value) for value in
         (level_rhs, galerkin_blocks, galerkin_cols, rtable, restrict_blocks)],
        scratch=[
            pltpu.VMEM((2, size, fields), f32), pltpu.VMEM((size, fields), bf16),
            pltpu.VMEM((2, size, size), bf16), pltpu.SemaphoreType.DMA((7 + count,)),
        ],
    )
    gcols, rcols = ((in_vmem(value), scalars()) for value in (gcols, rcols))
    first = outers[0]
    outers = [swap_outer(outer) for outer in outers]
    inner = exchange(inner, "narrow", 1)
    rest, base, local, rim, scale, share, next_scale = run(
        first_local_kernel, "first_local",
        [array((rows, fields), f32)] * 2 + operator_shapes + [square_shape, scale_shape],
        [level_rhs, first, gcols, of_level(galerkin_blocks, 0), rcols, rfirst, pivots],
        flops=flops(fields),
    )
    operators = [(scale, local)]
    kept, joined = [], []
    for places, outer in zip(pairs, outers):
        columns = half if kept else width
        near, *joined = run(
            functools.partial(first_residual_kernel, places), "first_residual",
            [real_shape, array((rows, columns), bf16)] + [ends_shape(columns)] * 4,
            [rest, rim, outer, inner, share, next_scale, *joined],
            flops=flops(width, 3),
        )
        kept.append(near)
    sent, far_ends, near_ends = joined[0], joined[1:3], joined[3:]
    bases = []
    for level_idx in range(1, levels):
        bit = 1 << level_idx - 1
        far_ends = swap_ends(*far_ends, bit)
        other = exchange(sent, "wide", bit)
        near_ends = swap_ends(*near_ends, 0)
        shapes = operator_shapes + [square_shape]
        operands = [sent, gcols, of_level(galerkin_blocks, level_idx),
                    rcols, of_level(restrict_blocks, level_idx)]
        if level_idx < last:
            shapes = shapes + [scale_shape]
            operands.append(pivots_of(level_idx + 1))
        local, rim, scale, share, *next_scale = run(
            functools.partial(operators_kernel, level_idx), "operators", shapes, operands
        )
        operators.append((scale, local))
        for slot, mine in enumerate(kept):
            kinds = ["base", "sent", "kept", "ends"]
            if level_idx == 1:
                kinds = ["base", "kept", "ends"] if slot else ["base", "sent", "ends"]
            elif level_idx == last:
                kinds = ["base", "sent"]
            shapes = [real_shape]
            operands = [mine, other, scale, local, rim, *far_ends, *near_ends, share, *next_scale]
            if level_idx == 1:
                shapes = [chunk_shape]
            if "sent" in kinds:
                shapes.append(chunk_shape)
            if "kept" in kinds:
                shapes.append(real_shape)
            if "ends" in kinds:
                shapes += [ends_shape(width)] * 2
            made_base, *made = run(
                functools.partial(level_kernel, slot, kinds), "level", shapes, operands,
                flops=flops(width, 3),
            )
            bases.append(made_base)
            if "sent" in kinds:
                next_sent = made.pop(0)
            if "kept" in kinds:
                own = [made.pop(0)]
            if "ends" in kinds:
                if "sent" in kinds:
                    sent_ends = made
                kept_ends = made
        sent = next_sent
        if level_idx < last:
            kept, far_ends, near_ends = own, sent_ends, kept_ends
    mine = sent
    far_parts = {
        o: exchange_both(mine, 1 << last, functools.partial(lambda o, j: j ^ o, o))
        for o in range(0, pieces, 2)
    }
    own_parts = {o: exchange(mine, "narrow", o) if o else mine for o in range(0, pieces, 2)}
    near_bases, coarse_mat, *ups = run(
        functools.partial(coarse_operators_kernel, 2, levels), "coarse_operators",
        [array((rows, half), bf16), array((rows, pieces * rows), bf16)]
        + [square_shape] * (levels - 3),
        [mine, *bases[:2], pcols, coarse_inverse]
        + [of_level(prolong_blocks, idx) for idx in range(2, levels)]
        + [value for pair in operators[2:] for value in pair],
        flops=flops(rows, 2 * (levels - 2) + pieces), scratch=held,
    )
    near_places, far_places = ([place_of(far, given) for given in (1, 0)] for far in (0, 1))
    total_shape = array((rows, half), f32)
    lower, both, near_total = run(
        functools.partial(fine_operators_kernel, near_places), "fine_operators",
        [square_shape] * 2 + [total_shape],
        [mine, pcols, of_level(prolong_blocks, 0), of_level(prolong_blocks, 1),
         *operators[0], *operators[1], base, near_bases],
        flops=flops(rows, 4), scratch=held,
    )
    far_bases = exchange(near_bases, "wide", 1)
    (far_total,) = run(
        functools.partial(total_kernel, far_places), "far_total", [total_shape],
        [base, far_bases, lower], flops=flops(half),
    )
    parts = {}
    for offset in range(0, pieces, 2):
        (parts[offset],) = run(
            share_sum_kernel, "share_sum", [chunk_shape],
            [far_parts[offset], own_parts[offset], coarse_mat, both],
        )
        parts[offset + 1] = exchange(parts[offset], "narrow", 1)
    offsets = tuple(parts)
    operands = [coarse_mat] + [parts[o] for o in offsets] + [bases[-1]]
    for idx in reversed(range(2, last)):
        operands += [bases[idx], ups[idx - 2]]
    (coarse,) = run(
        functools.partial(up_kernel, offsets), "up", [chunk_shape], operands,
        flops=flops(width, len(offsets) + levels - 3),
    )
    diagonal, far, other = (exchange(coarse, "wide", bits) for bits in (3, 1, 2))
    result = None
    for group in (
        [(coarse, near_total, place_of(0, 0), 1)],
        [(diagonal, far_total, place_of(1, 1), 0)],
        [(far, far_total, place_of(1, 0), 1), (other, near_total, place_of(0, 1), 0)],
    ):
        values, totals, places, slots = zip(*group)
        operands = [*values, *totals, both]
        aliases = {}
        if result is not None:
            aliases[len(operands)] = 0
            operands.append(in_hbm(result))
        (result,) = run(
            functools.partial(output_kernel, places, slots), "output",
            [array((1, rows, fields), f32)], operands,
            flops=flops(width, len(group)), out_space=pltpu.HBM, aliases=aliases,
            scratch=[
                pltpu.VMEM((len(group), rows, width), f32), pltpu.SemaphoreType.DMA((len(group),))
            ],
        )
    return result


def solution(mesh):
    in_specs = (
        P("wide", "narrow", None),
        P(None, "wide", "narrow", None),
        P(None, "wide", "narrow", None, None, None),
        P(None, "wide", "narrow", None),
        P(None, "wide", "narrow", None, None, None),
        P(None, "wide", "narrow", None),
        P(None, "wide", "narrow", None, None, None),
        P("narrow", None),
    )
    out_specs = P("wide", "narrow", None)
    return jax.shard_map(
        on_device, mesh=mesh, in_specs=in_specs, out_specs=out_specs, check_vma=False
    )
```

time: 43.5 us -> 45.1 us (1.037)
  Pallas kernels: 11.3 us -> 12.5 us
  waiting for transfers between devices: 8.8 us -> 9.62 us
    ppermute x2 -> x10, starting transfers between devices: 3.74 us -> 10 us  [exchange_both(): return lax.ppermute(value, ('wide', 'narrow'), pairs)]
    ppermute x14 -> x10, starting transfers between devices: 14 us -> 9.86 us  [exchange(): return lax.ppermute(value, axis, [(i, i ^ bit) for i in range(count)])]
    ppermute x14 -> x10, waiting for transfers between devices: 5.45 us -> 2.69 us  [exchange(): return lax.ppermute(value, axis, [(i, i ^ bit) for i in range(count)])]
    ppermute x2 -> x10, waiting for transfers between devices: 2.67 us -> 5.21 us  [exchange_both(): return lax.ppermute(value, ('wide', 'narrow'), pairs)]
    ppermute x5 -> x2, starting transfers between devices: 5.14 us -> 2.63 us  [swap_outer(): return lax.ppermute(outer, 'narrow', gaps)]
    pallas_call x19 -> x18, Pallas kernels: 11.3 us -> 12.5 us  [run(): pl.pallas_call(body, grid=(1,) if windows else (), out_shape=[out_space(o...]
    ppermute x5 -> x2, waiting for transfers between devices: 0.68 us -> 1.73 us  [swap_outer(): return lax.ppermute(outer, 'narrow', gaps)]
  transfers between devices with their start and end apart: 21 -> 22, of which waited for: 10 -> 7; matrix products, arithmetic and copies ran while one was open for 0% -> 0% of each run, Pallas kernels for 18% -> 20%
where the time goes in v11:
time: 45.1 us; the launch traced here: 44.9 us
  starting transfers between devices  22.5 us (50%)
  Pallas kernels  12.5 us (28%)
  waiting for transfers between devices  9.62 us (21%)
    pallas_call x18, Pallas kernels, run(): pl.pallas_call(body, grid=(1,) if windows else (), out_shape=[out_space(o...  12.5 us
    ppermute x10, starting transfers between devices, exchange_both(): return lax.ppermute(value, ('wide', 'narrow'), pairs)  10 us
    ppermute x10, starting transfers between devices, exchange(): return lax.ppermute(value, axis, [(i, i ^ bit) for i in range(count)])  9.86 us
    ppermute x10, waiting for transfers between devices, exchange_both(): return lax.ppermute(value, ('wide', 'narrow'), pairs)  5.21 us
    ppermute x10, waiting for transfers between devices, exchange(): return lax.ppermute(value, axis, [(i, i ^ bit) for i in range(count)])  2.69 us
    ppermute x2, starting transfers between devices, swap_outer(): return lax.ppermute(outer, 'narrow', gaps)  2.63 us
    ppermute x2, waiting for transfers between devices, swap_outer(): return lax.ppermute(outer, 'narrow', gaps)  1.73 us
  transfers between devices with their start and end apart: 22, of which 7 were waited for; matrix products, arithmetic and copies ran while one was open for 0% of the time, Pallas kernels for 20%

profile of v11, /device:TPU:0, one launch (start us, length us, event | category | flops | bytes accessed | tf_op | source)
XLA Modules:
  0.0 44.9 jit_solution(2010621376943014001)
XLA Ops:
  0.0 1.5 %start.1 = (s32[3,1,4,5]{3,2,1,0:T(4,128)S(1)}, s32[3,3,1,4]{3,2,1,0:T(1,128)S(1)}, bf16[1,1,4,3,64,64]{5,4,3,2,1,0:T(8,128)(2,1)S(1)}, bf16[4,64,64]{2,1,0:T(8,...) custom-call(f32[1,256,512]{2,1,0:T(8,128)} %rhs.3, ...), custom_call_target="tpu_custom_call" | custom-call | bytes 1311104 | tf_op jit(solution)/shard_map/start/pallas_call | solution.py:51
  1.5 0.5 %collective-permute-start.1 = (bf16[64,512]{1,0:T(8,128)(2,1)S(1)}, bf16[64,512]{1,0:T(8,128)(2,1)S(1)}, u32[]{:S(2)}, u32[]{:S(2)}) collective-permute-start(bf16[64,512]{1,0:T(8,128)(2,1)S(1)} %get-tuple-element.63), channel_id=1, source_target_pairs={{0,1},{1,0},{2,3},{3,2},{4,5},{5,4},{6,7},{7,6},{8,9},{9,8},{10,11... | collective-permute-start | bytes 196616 | tf_op jit(solution)/shard_map/ppermute | solution.py:337
  2.0 2.6 %collective-permute-start.2 = (bf16[64,256]{1,0:T(8,128)(2,1)S(1)}, bf16[64,256]{1,0:T(8,128)(2,1)S(1)}, u32[]{:S(2)}, u32[]{:S(2)}) collective-permute-start(bf16[64,256]{1,0:T(8,128)(2,1)S(1)} %get-tuple-element.55._), channel_id=1, source_target_pairs={{0,3},{1,2},{2,1},{3,0},{4,7},{5,6},{6,5},{7,4},{8,11},{9,10},{10,... | collective-permute-start | bytes 98312 | tf_op jit(solution)/shard_map/ppermute | solution.py:357
  4.6 0.0 collective-permute-start
  4.6 1.3 %first_local.1 = (f32[256,512]{1,0:T(8,128)S(1)}, f32[256,512]{1,0:T(8,128)S(1)}, bf16[256,256]{1,0:T(8,128)(2,1)S(1)}, bf16[256,128]{1,0:T(8,128)(2,1)S(1)}, f3...) custom-call(f32[1,256,512]{2,1,0:T(8,128)S(1)} %copy-done.3, ...), custom_call_target="tpu_custom_call" | custom-call | flops 67108864 | bytes 1180032 | tf_op jit(solution)/shard_map/first_local/pallas_call | solution.py:51
  5.9 0.4 collective-permute-done.2.outer
  6.3 0.4 first_residual.2
  6.7 0.0 copy-start.1
  6.7 1.4 %collective-permute-done.outer = bf16[64,256]{1,0:T(8,128)(2,1)S(1)} collective-permute-done((bf16[64,256]{1,0:T(8,128)(2,1)S(1)}, bf16[64,256]{1,0:T(8,128)(2,1)S(1)}, u32[]{:S(2)}, u32[]{:S(2)}) %collective-permute-start) | collective-permute-done | bytes 32800 | tf_op jit(solution)/shard_map/ppermute | solution.py:357
  8.1 0.4 first_residual.3
  8.5 1.6 %collective-permute-start.3 = (bf16[256,256]{1,0:T(8,128)(2,1)S(1)}, bf16[256,256]{1,0:T(8,128)(2,1)S(1)}, u32[]{:S(2)}, u32[]{:S(2)}) collective-permute-start(bf16[256,256]{1,0:T(8,128)(2,1)S(1)} %get-tuple-element.72._), channel_id=1, source_target_pairs={{0,4},{4,0},{8,12},{12,8},{16,20},{20,16},{24,28},{28,24},{1,5},{5... | collective-permute-start | bytes 393224 | tf_op jit(solution)/shard_map/ppermute | solution.py:337
  10.0 0.0 collective-permute-start.4
  10.0 1.9 %collective-permute-start.5 = (bf16[64,256]{1,0:T(8,128)(2,1)S(1)}, bf16[64,256]{1,0:T(8,128)(2,1)S(1)}, u32[]{:S(2)}, u32[]{:S(2)}) collective-permute-start(bf16[64,256]{1,0:T(8,128)(2,1)S(1)} %get-tuple-element.77), channel_id=1, source_target_pairs={{0,7},{1,6},{2,5},{3,4},{4,3},{5,2},{6,1},{7,0},{8,15},{9,14},{10,... | collective-permute-start | bytes 98312 | tf_op jit(solution)/shard_map/ppermute | solution.py:345
  12.0 0.3 collective-permute-start.6
  12.2 1.1 %collective-permute-start.7 = (bf16[64,256]{1,0:T(8,128)(2,1)S(1)}, bf16[64,256]{1,0:T(8,128)(2,1)S(1)}, u32[]{:S(2)}, u32[]{:S(2)}) collective-permute-start(bf16[64,256]{1,0:T(8,128)(2,1)S(1)} %get-tuple-element.79), channel_id=1, source_target_pairs={{0,3},{1,2},{2,1},{3,0},{4,7},{5,6},{6,5},{7,4},{8,11},{9,10},{10,... | collective-permute-start | bytes 98312 | tf_op jit(solution)/shard_map/ppermute | solution.py:345
  13.4 1.1 %operators.2 = (bf16[256,256]{1,0:T(8,128)(2,1)S(1)}, bf16[256,128]{1,0:T(8,128)(2,1)S(1)}, f32[256,1]{1,0:T(8,128)S(1)}, bf16[256,256]{1,0:T(8,128)(2,1)S(1)}, f32[256,1]{1,0:T(8,128)S(1)}) custom-call(bf16[256,256]{1,0:T(8,128)(2,1)S(1)} %get-tuple-element.72._, s32[3,1,4,5]{3,2,1,0:T(4,128)S(1)} %get-tuple-element.56.cols, ...), custom_call_target="tpu_custom_call" | custom-call | bytes 1409408 | tf_op jit(solution)/shard_map/operators/pallas_call | solution.py:51
  14.4 0.1 collective-permute-done.4.refs_0_
  14.5 1.1 %collective-permute-done.7.refs_3_ = bf16[64,256]{1,0:T(8,128)(2,1)S(1)} collective-permute-done((bf16[64,256]{1,0:T(8,128)(2,1)S(1)}, bf16[64,256]{1,0:T(8,128)(2,1)S(1)}, u32[]{:S(2)}, u32[]{:S(2)}) %collective-permute-start.7) | collective-permute-done | bytes 32800 | tf_op jit(solution)/shard_map/ppermute | solution.py:345
  15.6 0.5 %level.4 = (bf16[256,128]{1,0:T(8,128)(2,1)S(1)}, bf16[256,128]{1,0:T(8,128)(2,1)S(1)}, bf16[64,128]{1,0:T(8,128)(2,1)S(1)}, bf16[64,128]{1,0:T(8,128)(2,1)S(1)}) custom-call(f32[256,128]{1,0:T(8,128)S(1)} %get-tuple-element.83.rhs_own, bf16[256,256]{1,0:T(8,128)(2,1)S(1)} %collective-permute-done.3.rhs_far, f32[256,1]{1,0:T(8,128)S(1)} %get-tuple-element.73.scale.scale_1, ...), custom_call_target="tpu_custom_call" | custom-call | flops 50331648 | bytes 722944 | tf_op jit(solution)/shard_map/level/pallas_call | solution.py:51
  16.1 1.6 %collective-permute-start.8 = (bf16[256,128]{1,0:T(8,128)(2,1)S(1)}, bf16[256,128]{1,0:T(8,128)(2,1)S(1)}, u32[]{:S(2)}, u32[]{:S(2)}) collective-permute-start(bf16[256,128]{1,0:T(8,128)(2,1)S(1)} %get-tuple-element.84._), channel_id=1, source_target_pairs={{0,8},{4,12},{8,0},{12,4},{16,24},{20,28},{24,16},{28,20},{1,9},{5... | collective-permute-start | bytes 196616 | tf_op jit(solution)/shard_map/ppermute | solution.py:337
  17.7 0.0 collective-permute-start.9
  17.7 2.2 %collective-permute-start.10 = (bf16[64,128]{1,0:T(8,128)(2,1)S(1)}, bf16[64,128]{1,0:T(8,128)(2,1)S(1)}, u32[]{:S(2)}, u32[]{:S(2)}) collective-permute-start(bf16[64,128]{1,0:T(8,128)(2,1)S(1)} %get-tuple-element.89), channel_id=1, source_target_pairs={{0,11},{1,10},{2,9},{3,8},{4,15},{5,14},{6,13},{7,12},{8,3},{9,2},... | collective-permute-start | bytes 49160 | tf_op jit(solution)/shard_map/ppermute | solution.py:345
  19.9 0.5 %level.3 = (bf16[256,128]{1,0:T(8,128)(2,1)S(1)}, f32[256,128]{1,0:T(8,128)S(1)}, bf16[64,128]{1,0:T(8,128)(2,1)S(1)}, bf16[64,128]{1,0:T(8,128)(2,1)S(1)}) custom-call(f32[256,128]{1,0:T(8,128)S(1)} %get-tuple-element.71.rhs_own, bf16[256,256]{1,0:T(8,128)(2,1)S(1)} %collective-permute-done.3.rhs_far, f32[256,1]{1,0:T(8,128)S(1)} %get-tuple-element.73.scale.scale_1, ...), custom_call_target="tpu_custom_call" | custom-call | flops 50331648 | bytes 722944 | tf_op jit(solution)/shard_map/level/pallas_call | solution.py:51
  20.4 0.3 collective-permute-start.11
  20.7 0.9 %collective-permute-start.12 = (bf16[64,128]{1,0:T(8,128)(2,1)S(1)}, bf16[64,128]{1,0:T(8,128)(2,1)S(1)}, u32[]{:S(2)}, u32[]{:S(2)}) collective-permute-start(bf16[64,128]{1,0:T(8,128)(2,1)S(1)} %get-tuple-element.91), channel_id=1, source_target_pairs={{0,3},{1,2},{2,1},{3,0},{4,7},{5,6},{6,5},{7,4},{8,11},{9,10},{10,... | collective-permute-start | bytes 49160 | tf_op jit(solution)/shard_map/ppermute | solution.py:345
  21.6 1.0 %operators.3 = (bf16[256,256]{1,0:T(8,128)(2,1)S(1)}, bf16[256,128]{1,0:T(8,128)(2,1)S(1)}, f32[256,1]{1,0:T(8,128)S(1)}, bf16[256,256]{1,0:T(8,128)(2,1)S(1)}) custom-call(bf16[256,128]{1,0:T(8,128)(2,1)S(1)} %get-tuple-element.84._, s32[3,1,4,5]{3,2,1,0:T(4,128)S(1)} %get-tuple-element.56.cols, bf16[3,1,4,5,64,64]{5,4,3,2,1,0:T(8,128)(2,1)S(1)} %copy-done, ...), custom_call_target="tpu_custom_call" | custom-call | bytes 852352 | tf_op jit(solution)/shard_map/operators/pallas_call | solution.py:51
  22.7 0.0 copy-start.2
  22.7 1.2 %collective-permute-done.12.refs_3_ = bf16[64,128]{1,0:T(8,128)(2,1)S(1)} collective-permute-done((bf16[64,128]{1,0:T(8,128)(2,1)S(1)}, bf16[64,128]{1,0:T(8,128)(2,1)S(1)}, u32[]{:S(2)}, u32[]{:S(2)}) %collective-permute-start.12) | collective-permute-done | bytes 16416 | tf_op jit(solution)/shard_map/ppermute | solution.py:345
  23.9 0.5 %level.5 = (f32[256,128]{1,0:T(8,128)S(1)}, bf16[256,128]{1,0:T(8,128)(2,1)S(1)}) custom-call(f32[256,128]{1,0:T(8,128)S(1)} %get-tuple-element.82.rhs_own, bf16[256,128]{1,0:T(8,128)(2,1)S(1)} %collective-permute-done.8.rhs_far, f32[256,1]{1,0:T(8,128)S(1)} %get-tuple-element.85.scale.refs_6_, bf16[256,256]{1,0:T(8,128)(2,1)S(1)} %get-tuple-element.86.local.refs_7_, ...), custom_call_target="tpu_custom_call" | custom-call | flops 50331648 | bytes 590848 | tf_op jit(solution)/shard_map/level/pallas_call | solution.py:51
  24.4 0.0 copy-start.5
  24.4 2.7 %collective-permute-start.13 = (bf16[256,128]{1,0:T(8,128)(2,1)S(1)}, bf16[256,128]{1,0:T(8,128)(2,1)S(1)}, u32[]{:S(2)}, u32[]{:S(2)}) collective-permute-start(bf16[256,128]{1,0:T(8,128)(2,1)S(1)} %get-tuple-element.93.refs_0_._.own), channel_id=1, source_target_pairs={{0,16},{1,17},{2,18},{3,19},{4,20},{5,21},{6,22},{7,23},{8,24},{9,... | collective-permute-start | bytes 196616 | tf_op jit(solution)/shard_map/ppermute | solution.py:345
  27.0 0.6 %collective-permute-start.15 = (bf16[256,128]{1,0:T(8,128)(2,1)S(1)}, bf16[256,128]{1,0:T(8,128)(2,1)S(1)}, u32[]{:S(2)}, u32[]{:S(2)}) collective-permute-start(bf16[256,128]{1,0:T(8,128)(2,1)S(1)} %get-tuple-element.93.refs_0_._.own), channel_id=1, source_target_pairs={{0,18},{1,19},{2,16},{3,17},{4,22},{5,23},{6,20},{7,21},{8,26},{9,... | collective-permute-start | bytes 196616 | tf_op jit(solution)/shard_map/ppermute | solution.py:345
  27.7 1.2 %collective-permute-start.16 = (bf16[256,128]{1,0:T(8,128)(2,1)S(1)}, bf16[256,128]{1,0:T(8,128)(2,1)S(1)}, u32[]{:S(2)}, u32[]{:S(2)}) collective-permute-start(bf16[256,128]{1,0:T(8,128)(2,1)S(1)} %get-tuple-element.93.refs_0_._.own), channel_id=1, source_target_pairs={{0,2},{1,3},{2,0},{3,1},{4,6},{5,7},{6,4},{7,5},{8,10},{9,11},{10,... | collective-permute-start | bytes 196616 | tf_op jit(solution)/shard_map/ppermute | solution.py:337
  28.8 1.1 %coarse_operators.1 = (bf16[256,256]{1,0:T(8,128)(2,1)S(1)}, bf16[256,1024]{1,0:T(8,128)(2,1)S(1)}) custom-call(bf16[256,128]{1,0:T(8,128)(2,1)S(1)} %get-tuple-element.93.refs_0_._.own, bf16[256,128]{1,0:T(8,128)(2,1)S(1)} %get-tuple-element.94.refs_1_, bf16[256,128]{1,0:T(8,128)(2,1)S(1)} %get-tuple-element.95.refs_2_, s32[3,1,2,4]{3,2,1,0:T(2,128)S(1)} %bitcast.2, ...), custom_call_target="tpu_custom_call" | custom-call | flops 201326592 | bytes 1049696 | tf_op jit(solution)/shard_map/coarse_operators/pallas_call | solution.py:51
  30.0 1.2 %fine_operators.1 = (bf16[256,256]{1,0:T(8,128)(2,1)S(1)}, bf16[256,256]{1,0:T(8,128)(2,1)S(1)}, f32[256,256]{1,0:T(8,128)S(1)}) custom-call(bf16[256,128]{1,0:T(8,128)(2,1)S(1)} %get-tuple-element.93.refs_0_._.own, s32[3,1,2,4]{3,2,1,0:T(2,128)S(1)} %bitcast.3, bf16[3,1,4,2,64,64]{5,4,3,2,1,0:T(8,128)(2,1)S(1)} %copy-done.2, ...), custom_call_target="tpu_custom_call" | custom-call | flops 134217728 | bytes 1378400 | tf_op jit(solution)/shard_map/fine_operators/pallas_call | solution.py:51
  31.2 0.1 collective-permute-start.14
  31.3 2.9 %collective-permute-done.15.far = bf16[256,128]{1,0:T(8,128)(2,1)S(1)} collective-permute-done((bf16[256,128]{1,0:T(8,128)(2,1)S(1)}, bf16[256,128]{1,0:T(8,128)(2,1)S(1)}, u32[]{:S(2)}, u32[]{:S(2)}) %collective-permute-start.15) | collective-permute-done | bytes 65568 | tf_op jit(solution)/shard_map/ppermute | solution.py:345
  34.2 0.1 collective-permute-start.17
  34.3 1.2 %collective-permute-start.20 = (bf16[256,256]{1,0:T(8,128)(2,1)S(1)}, bf16[256,256]{1,0:T(8,128)(2,1)S(1)}, u32[]{:S(2)}, u32[]{:S(2)}) collective-permute-start(bf16[256,256]{1,0:T(8,128)(2,1)S(1)} %get-tuple-element.100.bases), channel_id=1, source_target_pairs={{0,4},{4,0},{8,12},{12,8},{16,20},{20,16},{24,28},{28,24},{1,5},{5... | collective-permute-start | bytes 393224 | tf_op jit(solution)/shard_map/ppermute | solution.py:337
  35.5 0.3 up.1.refs_0_
  35.8 0.1 collective-permute-start.21
  35.9 1.2 %collective-permute-start.18 = (bf16[256,128]{1,0:T(8,128)(2,1)S(1)}, bf16[256,128]{1,0:T(8,128)(2,1)S(1)}, u32[]{:S(2)}, u32[]{:S(2)}) collective-permute-start(bf16[256,128]{1,0:T(8,128)(2,1)S(1)} %up.1.refs_0_), channel_id=1, source_target_pairs={{0,4},{4,0},{8,12},{12,8},{16,20},{20,16},{24,28},{28,24},{1,5},{5... | collective-permute-start | bytes 196616 | tf_op jit(solution)/shard_map/ppermute | solution.py:337
  37.1 2.2 %collective-permute-start.19 = (bf16[256,128]{1,0:T(8,128)(2,1)S(1)}, bf16[256,128]{1,0:T(8,128)(2,1)S(1)}, u32[]{:S(2)}, u32[]{:S(2)}) collective-permute-start(bf16[256,128]{1,0:T(8,128)(2,1)S(1)} %up.1.refs_0_), channel_id=1, source_target_pairs={{0,8},{4,12},{8,0},{12,4},{16,24},{20,28},{24,16},{28,20},{1,9},{5... | collective-permute-start | bytes 196616 | tf_op jit(solution)/shard_map/ppermute | solution.py:337
  39.4 2.7 %collective-permute-done.20.bases = bf16[256,256]{1,0:T(8,128)(2,1)S(1)} collective-permute-done((bf16[256,256]{1,0:T(8,128)(2,1)S(1)}, bf16[256,256]{1,0:T(8,128)(2,1)S(1)}, u32[]{:S(2)}, u32[]{:S(2)}) %collective-permute-start.20) | collective-permute-done | bytes 131104 | tf_op jit(solution)/shard_map/ppermute | solution.py:337
  42.1 0.2 far_total.1.refs_1_.refs_2_
  42.3 0.8 %output.3.refs_3_ = f32[1,256,512]{2,1,0:T(8,128)} custom-call(bf16[256,128]{1,0:T(8,128)(2,1)S(1)} %up.1.refs_0_, f32[256,256]{1,0:T(8,128)S(1)} %get-tuple-element.104.refs_1_.refs_3_, bf16[256,256]{1,0:T(8,128)(2,1)S(1)} %get-tuple-element.101.refs_1_.refs_2_.refs_4_), custom_call_target="tpu_custom_call" | custom-call | flops 16777216 | bytes 458752 | tf_op jit(solution)/shard_map/output/pallas_call | solution.py:51
  43.1 0.8 %output.4.refs_5_ = f32[1,256,512]{2,1,0:T(8,128)} custom-call(bf16[256,128]{1,0:T(8,128)(2,1)S(1)} %collective-permute-done.21.refs_0_, f32[256,256]{1,0:T(8,128)S(1)} %far_total.1.refs_1_.refs_2_, bf16[256,256]{1,0:T(8,128)(2,1)S(1)} %get-tuple-element.101.refs_1_.refs_2_.refs_4_, f32[1,256,512]{2,1,0:T(8,128)} %output.3.refs_3_), custom_call_target="tpu_custom_call", output_to_operand_aliasing={{}: (3, {})} | custom-call | flops 16777216 | bytes 983040 | tf_op jit(solution)/shard_map/output/pallas_call | solution.py:51
  44.0 0.9 %output.5 = f32[1,256,512]{2,1,0:T(8,128)} custom-call(bf16[256,128]{1,0:T(8,128)(2,1)S(1)} %collective-permute-done.18.refs_0_, bf16[256,128]{1,0:T(8,128)(2,1)S(1)} %collective-permute-done.19.refs_1_, f32[256,256]{1,0:T(8,128)S(1)} %far_total.1.refs_1_.refs_2_, f32[256,256]{1,0:T(8,128)S(1)} %get-tuple-element.104.refs_1_.refs_3_, ...), custom_call_target="tpu_custom_call", output_to_operand_aliasing={{}: (5, {})} | custom-call | flops 33554432 | bytes 1310720 | tf_op jit(solution)/shard_map/output/pallas_call | solution.py:51
  (26 shorter events, 0.1 us)
Async XLA Ops:
  0.0 4.6 %copy-start = (bf16[3,1,4,5,64,64]{5,4,3,2,1,0:T(8,128)(2,1)S(1)}, bf16[3,1,4,5,64,64]{5,4,3,2,1,0:T(8,128)(2,1)}, u32[]{:S(2)}) copy-start(bf16[3,1,4,5,64,64]{5,4,3,2,1,0:T(8,128)(2,1)} %blocks.7) | copy-start | bytes 1474564
  0.0 4.6 %copy-start.3 = (f32[1,256,512]{2,1,0:T(8,128)S(1)}, f32[1,256,512]{2,1,0:T(8,128)}, u32[]{:S(2)}) copy-start(f32[1,256,512]{2,1,0:T(8,128)} %rhs.3) | copy-start | bytes 1572868
  1.5 4.8 %collective-permute-start.1 = (bf16[64,512]{1,0:T(8,128)(2,1)S(1)}, bf16[64,512]{1,0:T(8,128)(2,1)S(1)}, u32[]{:S(2)}, u32[]{:S(2)}) collective-permute-start(bf16[64,512]{1,0:T(8,128)(2,1)S(1)} %get-tuple-element.63), channel_id=1, source_target_pairs={{0,1},{1,0},{2,3},{3,2},{4,5},{5,4},{6,7},{7,6},{8,9},{9,8},{10,11... | collective-permute-start | bytes 196616 | tf_op jit(solution)/shard_map/ppermute | solution.py:337
  2.0 4.3 %collective-permute-start.2 = (bf16[64,256]{1,0:T(8,128)(2,1)S(1)}, bf16[64,256]{1,0:T(8,128)(2,1)S(1)}, u32[]{:S(2)}, u32[]{:S(2)}) collective-permute-start(bf16[64,256]{1,0:T(8,128)(2,1)S(1)} %get-tuple-element.55._), channel_id=1, source_target_pairs={{0,3},{1,2},{2,1},{3,0},{4,7},{5,6},{6,5},{7,4},{8,11},{9,10},{10,... | collective-permute-start | bytes 98312 | tf_op jit(solution)/shard_map/ppermute | solution.py:357
  4.6 3.4 %collective-permute-start = (bf16[64,256]{1,0:T(8,128)(2,1)S(1)}, bf16[64,256]{1,0:T(8,128)(2,1)S(1)}, u32[]{:S(2)}, u32[]{:S(2)}) collective-permute-start(bf16[64,256]{1,0:T(8,128)(2,1)S(1)} %get-tuple-element.62), channel_id=1, source_target_pairs={{0,3},{1,2},{2,1},{3,0},{4,7},{5,6},{6,5},{7,4},{8,11},{9,10},{10,... | collective-permute-start | bytes 98312 | tf_op jit(solution)/shard_map/ppermute | solution.py:357
  6.7 6.7 %copy-start.1 = (bf16[3,1,4,3,64,64]{5,4,3,2,1,0:T(8,128)(2,1)S(1)}, bf16[3,1,4,3,64,64]{5,4,3,2,1,0:T(8,128)(2,1)}, u32[]{:S(2)}) copy-start(bf16[3,1,4,3,64,64]{5,4,3,2,1,0:T(8,128)(2,1)} %rblocks.5) | copy-start | bytes 884740
  8.5 7.1 %collective-permute-start.3 = (bf16[256,256]{1,0:T(8,128)(2,1)S(1)}, bf16[256,256]{1,0:T(8,128)(2,1)S(1)}, u32[]{:S(2)}, u32[]{:S(2)}) collective-permute-start(bf16[256,256]{1,0:T(8,128)(2,1)S(1)} %get-tuple-element.72._), channel_id=1, source_target_pairs={{0,4},{4,0},{8,12},{12,8},{16,20},{20,16},{24,28},{28,24},{1,5},{5... | collective-permute-start | bytes 393224 | tf_op jit(solution)/shard_map/ppermute | solution.py:337
  10.0 4.5 %collective-permute-start.4 = (bf16[64,256]{1,0:T(8,128)(2,1)S(1)}, bf16[64,256]{1,0:T(8,128)(2,1)S(1)}, u32[]{:S(2)}, u32[]{:S(2)}) collective-permute-start(bf16[64,256]{1,0:T(8,128)(2,1)S(1)} %get-tuple-element.76), channel_id=1, source_target_pairs={{0,5},{1,4},{2,7},{3,6},{4,1},{5,0},{6,3},{7,2},{8,13},{9,12},{10,... | collective-permute-start | bytes 98312 | tf_op jit(solution)/shard_map/ppermute | solution.py:345
  10.0 4.5 %collective-permute-start.5 = (bf16[64,256]{1,0:T(8,128)(2,1)S(1)}, bf16[64,256]{1,0:T(8,128)(2,1)S(1)}, u32[]{:S(2)}, u32[]{:S(2)}) collective-permute-start(bf16[64,256]{1,0:T(8,128)(2,1)S(1)} %get-tuple-element.77), channel_id=1, source_target_pairs={{0,7},{1,6},{2,5},{3,4},{4,3},{5,2},{6,1},{7,0},{8,15},{9,14},{10,... | collective-permute-start | bytes 98312 | tf_op jit(solution)/shard_map/ppermute | solution.py:345
  12.0 2.6 %collective-permute-start.6 = (bf16[64,256]{1,0:T(8,128)(2,1)S(1)}, bf16[64,256]{1,0:T(8,128)(2,1)S(1)}, u32[]{:S(2)}, u32[]{:S(2)}) collective-permute-start(bf16[64,256]{1,0:T(8,128)(2,1)S(1)} %get-tuple-element.78), channel_id=1, source_target_pairs={{0,1},{1,0},{2,3},{3,2},{4,5},{5,4},{6,7},{7,6},{8,9},{9,8},{10,11... | collective-permute-start | bytes 98312 | tf_op jit(solution)/shard_map/ppermute | solution.py:345
  12.2 3.3 %collective-permute-start.7 = (bf16[64,256]{1,0:T(8,128)(2,1)S(1)}, bf16[64,256]{1,0:T(8,128)(2,1)S(1)}, u32[]{:S(2)}, u32[]{:S(2)}) collective-permute-start(bf16[64,256]{1,0:T(8,128)(2,1)S(1)} %get-tuple-element.79), channel_id=1, source_target_pairs={{0,3},{1,2},{2,1},{3,0},{4,7},{5,6},{6,5},{7,4},{8,11},{9,10},{10,... | collective-permute-start | bytes 98312 | tf_op jit(solution)/shard_map/ppermute | solution.py:345
  16.1 7.8 %collective-permute-start.8 = (bf16[256,128]{1,0:T(8,128)(2,1)S(1)}, bf16[256,128]{1,0:T(8,128)(2,1)S(1)}, u32[]{:S(2)}, u32[]{:S(2)}) collective-permute-start(bf16[256,128]{1,0:T(8,128)(2,1)S(1)} %get-tuple-element.84._), channel_id=1, source_target_pairs={{0,8},{4,12},{8,0},{12,4},{16,24},{20,28},{24,16},{28,20},{1,9},{5... | collective-permute-start | bytes 196616 | tf_op jit(solution)/shard_map/ppermute | solution.py:337
  17.7 5.0 %collective-permute-start.9 = (bf16[64,128]{1,0:T(8,128)(2,1)S(1)}, bf16[64,128]{1,0:T(8,128)(2,1)S(1)}, u32[]{:S(2)}, u32[]{:S(2)}) collective-permute-start(bf16[64,128]{1,0:T(8,128)(2,1)S(1)} %get-tuple-element.88), channel_id=1, source_target_pairs={{0,9},{1,8},{2,11},{3,10},{4,13},{5,12},{6,15},{7,14},{8,1},{9,0},... | collective-permute-start | bytes 49160 | tf_op jit(solution)/shard_map/ppermute | solution.py:345
  17.7 4.9 %collective-permute-start.10 = (bf16[64,128]{1,0:T(8,128)(2,1)S(1)}, bf16[64,128]{1,0:T(8,128)(2,1)S(1)}, u32[]{:S(2)}, u32[]{:S(2)}) collective-permute-start(bf16[64,128]{1,0:T(8,128)(2,1)S(1)} %get-tuple-element.89), channel_id=1, source_target_pairs={{0,11},{1,10},{2,9},{3,8},{4,15},{5,14},{6,13},{7,12},{8,3},{9,2},... | collective-permute-start | bytes 49160 | tf_op jit(solution)/shard_map/ppermute | solution.py:345
  20.4 2.3 %collective-permute-start.11 = (bf16[64,128]{1,0:T(8,128)(2,1)S(1)}, bf16[64,128]{1,0:T(8,128)(2,1)S(1)}, u32[]{:S(2)}, u32[]{:S(2)}) collective-permute-start(bf16[64,128]{1,0:T(8,128)(2,1)S(1)} %get-tuple-element.90), channel_id=1, source_target_pairs={{0,1},{1,0},{2,3},{3,2},{4,5},{5,4},{6,7},{7,6},{8,9},{9,8},{10,11... | collective-permute-start | bytes 49160 | tf_op jit(solution)/shard_map/ppermute | solution.py:345
  20.7 3.2 %collective-permute-start.12 = (bf16[64,128]{1,0:T(8,128)(2,1)S(1)}, bf16[64,128]{1,0:T(8,128)(2,1)S(1)}, u32[]{:S(2)}, u32[]{:S(2)}) collective-permute-start(bf16[64,128]{1,0:T(8,128)(2,1)S(1)} %get-tuple-element.91), channel_id=1, source_target_pairs={{0,3},{1,2},{2,1},{3,0},{4,7},{5,6},{6,5},{7,4},{8,11},{9,10},{10,... | collective-permute-start | bytes 49160 | tf_op jit(solution)/shard_map/ppermute | solution.py:345
  21.6 7.2 %copy-start.4 = (bf16[256,1024]{1,0:T(8,128)(2,1)S(1)}, bf16[256,1024]{1,0:T(8,128)(2,1)}, u32[]{:S(2)}) copy-start(bf16[256,1024]{1,0:T(8,128)(2,1)} %refs_4_.1) | copy-start | bytes 1572868
  22.7 6.2 %copy-start.2 = (bf16[3,1,4,2,64,64]{5,4,3,2,1,0:T(8,128)(2,1)S(1)}, bf16[3,1,4,2,64,64]{5,4,3,2,1,0:T(8,128)(2,1)}, u32[]{:S(2)}) copy-start(bf16[3,1,4,2,64,64]{5,4,3,2,1,0:T(8,128)(2,1)} %blocks_1.1) | copy-start | bytes 589828
  24.4 4.5 %copy-start.5 = (s32[3,1,4,2]{2,3,1,0:T(2,128)S(1)}, s32[3,1,4,2]{2,3,1,0:T(2,128)}, u32[]{:S(2)}) copy-start(s32[3,1,4,2]{2,3,1,0:T(2,128)} %param.13) | copy-start | bytes 292
  24.4 6.8 %collective-permute-start.13 = (bf16[256,128]{1,0:T(8,128)(2,1)S(1)}, bf16[256,128]{1,0:T(8,128)(2,1)S(1)}, u32[]{:S(2)}, u32[]{:S(2)}) collective-permute-start(bf16[256,128]{1,0:T(8,128)(2,1)S(1)} %get-tuple-element.93.refs_0_._.own), channel_id=1, source_target_pairs={{0,16},{1,17},{2,18},{3,19},{4,20},{5,21},{6,22},{7,23},{8,24},{9,... | collective-permute-start | bytes 196616 | tf_op jit(solution)/shard_map/ppermute | solution.py:345
  27.0 7.1 %collective-permute-start.15 = (bf16[256,128]{1,0:T(8,128)(2,1)S(1)}, bf16[256,128]{1,0:T(8,128)(2,1)S(1)}, u32[]{:S(2)}, u32[]{:S(2)}) collective-permute-start(bf16[256,128]{1,0:T(8,128)(2,1)S(1)} %get-tuple-element.93.refs_0_._.own), channel_id=1, source_target_pairs={{0,18},{1,19},{2,16},{3,17},{4,22},{5,23},{6,20},{7,21},{8,26},{9,... | collective-permute-start | bytes 196616 | tf_op jit(solution)/shard_map/ppermute | solution.py:345
  27.7 6.5 %collective-permute-start.16 = (bf16[256,128]{1,0:T(8,128)(2,1)S(1)}, bf16[256,128]{1,0:T(8,128)(2,1)S(1)}, u32[]{:S(2)}, u32[]{:S(2)}) collective-permute-start(bf16[256,128]{1,0:T(8,128)(2,1)S(1)} %get-tuple-element.93.refs_0_._.own), channel_id=1, source_target_pairs={{0,2},{1,3},{2,0},{3,1},{4,6},{5,7},{6,4},{7,5},{8,10},{9,11},{10,... | collective-permute-start | bytes 196616 | tf_op jit(solution)/shard_map/ppermute | solution.py:337
  31.2 4.3 %collective-permute-start.14 = (bf16[256,128]{1,0:T(8,128)(2,1)S(1)}, bf16[256,128]{1,0:T(8,128)(2,1)S(1)}, u32[]{:S(2)}, u32[]{:S(2)}) collective-permute-start(bf16[256,128]{1,0:T(8,128)(2,1)S(1)} %share_sum.2.refs_0_), channel_id=1, source_target_pairs={{0,1},{1,0},{2,3},{3,2},{4,5},{5,4},{6,7},{7,6},{8,9},{9,8},{10,11... | collective-permute-start | bytes 196616 | tf_op jit(solution)/shard_map/ppermute | solution.py:337
  34.2 1.3 %collective-permute-start.17 = (bf16[256,128]{1,0:T(8,128)(2,1)S(1)}, bf16[256,128]{1,0:T(8,128)(2,1)S(1)}, u32[]{:S(2)}, u32[]{:S(2)}) collective-permute-start(bf16[256,128]{1,0:T(8,128)(2,1)S(1)} %share_sum.3.refs_2_), channel_id=1, source_target_pairs={{0,1},{1,0},{2,3},{3,2},{4,5},{5,4},{6,7},{7,6},{8,9},{9,8},{10,11... | collective-permute-start | bytes 196616 | tf_op jit(solution)/shard_map/ppermute | solution.py:337
  34.3 7.8 %collective-permute-start.20 = (bf16[256,256]{1,0:T(8,128)(2,1)S(1)}, bf16[256,256]{1,0:T(8,128)(2,1)S(1)}, u32[]{:S(2)}, u32[]{:S(2)}) collective-permute-start(bf16[256,256]{1,0:T(8,128)(2,1)S(1)} %get-tuple-element.100.bases), channel_id=1, source_target_pairs={{0,4},{4,0},{8,12},{12,8},{16,20},{20,16},{24,28},{28,24},{1,5},{5... | collective-permute-start | bytes 393224 | tf_op jit(solution)/shard_map/ppermute | solution.py:337
  35.8 7.3 %collective-permute-start.21 = (bf16[256,128]{1,0:T(8,128)(2,1)S(1)}, bf16[256,128]{1,0:T(8,128)(2,1)S(1)}, u32[]{:S(2)}, u32[]{:S(2)}) collective-permute-start(bf16[256,128]{1,0:T(8,128)(2,1)S(1)} %up.1.refs_0_), channel_id=1, source_target_pairs={{0,12},{4,8},{8,4},{12,0},{16,28},{20,24},{24,20},{28,16},{1,13},{... | collective-permute-start | bytes 196616 | tf_op jit(solution)/shard_map/ppermute | solution.py:337
  35.9 8.1 %collective-permute-start.18 = (bf16[256,128]{1,0:T(8,128)(2,1)S(1)}, bf16[256,128]{1,0:T(8,128)(2,1)S(1)}, u32[]{:S(2)}, u32[]{:S(2)}) collective-permute-start(bf16[256,128]{1,0:T(8,128)(2,1)S(1)} %up.1.refs_0_), channel_id=1, source_target_pairs={{0,4},{4,0},{8,12},{12,8},{16,20},{20,16},{24,28},{28,24},{1,5},{5... | collective-permute-start | bytes 196616 | tf_op jit(solution)/shard_map/ppermute | solution.py:337
  37.1 6.8 %collective-permute-start.19 = (bf16[256,128]{1,0:T(8,128)(2,1)S(1)}, bf16[256,128]{1,0:T(8,128)(2,1)S(1)}, u32[]{:S(2)}, u32[]{:S(2)}) collective-permute-start(bf16[256,128]{1,0:T(8,128)(2,1)S(1)} %up.1.refs_0_), channel_id=1, source_target_pairs={{0,8},{4,12},{8,0},{12,4},{16,24},{20,28},{24,16},{28,20},{1,9},{5... | collective-permute-start | bytes 196616 | tf_op jit(solution)/shard_map/ppermute | solution.py:337

commit v12 on v10

--- a/solution.py
+++ b/solution.py
@@ -239,10 +239,16 @@
 
 
 def fine_operators_kernel(
-    _, pcols, blocks_0, blocks_1, scale_0, local_0, scale_1, local_1, lower, upper, held
+    places, _, pcols, blocks_0, blocks_1, scale_0, local_0, scale_1, local_1,
+    base, near, far, lower, upper, both, total, held,
 ):
+    lower[...] = raising(0, pcols, blocks_0, local_0, scale_0, held)
     upper[...] = raising(1, pcols, blocks_1, local_1, scale_1, held)
-    lower[...] = raising(0, pcols, blocks_0, local_0, scale_0, held)
+    both[...] = matmul(lower[...], upper[...]).astype(bf16)
+    width = near.shape[1]
+    for slot, (place, source) in enumerate(zip(places, (near, far))):
+        made = base[:, lanes_of(place, width)] + matmul(lower[...], source[...])
+        total[:, slot * width : (slot + 1) * width] = made
 
 
 def restricted(level_idx, rmat, kept, other):
@@ -270,6 +276,14 @@
 
 def share_sum_kernel(far, own, *refs):
     refs[-1][...] = (far[...].astype(f32) + own[...].astype(f32)).astype(bf16)
+
+
+def coarse_kernel(offsets, inverse, *refs):
+    *parts, value, out = refs
+    value = value[...]
+    for part, offset in zip(parts, offsets):
+        value = value + inverse_part(inverse, part, offset)
+    out[...] = value
 
 
 def up_kernel(offsets, inverse, *refs):
@@ -285,20 +299,19 @@
     raised[...] = (base[...] + matmul(up[...], value)).astype(bf16)
 
 
-def output_kernel(places, raised, *refs):
-    count = len(places)
-    coarse, refs = refs[:count], refs[count:]
-    bases, refs = refs[: sum(raised)], refs[sum(raised) :]
-    base, lower, upper = refs[:3]
+def output_kernel(places, slots, *refs):
+    coarse, (base, lower, total, both) = refs[: len(places)], refs[len(places) : len(places) + 4]
     out, made, sems = refs[-3:]
     copies = []
-    for slot, (place, value) in enumerate(zip(places, coarse)):
-        value = value[...]
-        if raised[slot]:
-            value = (bases[sum(raised[:slot])][...] + matmul(upper[...], value)).astype(bf16)
-        lanes = lanes_of(place, value.shape[1])
-        made[slot] = base[:, lanes] + matmul(lower[...], value)
-        copy = pltpu.make_async_copy(made.at[slot], out.at[0, :, lanes], sems.at[slot])
+    for item, (place, value) in enumerate(zip(places, coarse)):
+        width = value.shape[1]
+        lanes = lanes_of(place, width)
+        if slots[item] is None:
+            made[item] = base[:, lanes] + matmul(lower[...], value[...])
+        else:
+            held = total[:, slots[item] * width : (slots[item] + 1) * width]
+            made[item] = held + matmul(both[...], value[...])
+        copy = pltpu.make_async_copy(made.at[item], out.at[0, :, lanes], sems.at[item])
         copy.start()
         copies.append(copy)
     for copy in copies:
@@ -438,47 +451,50 @@
         + [value for pair in operators[2:] for value in pair],
         flops=flops(rows, 2 * (levels - 2) + pieces), scratch=held,
     )
-    lower, upper = run(
-        fine_operators_kernel, "fine_operators", [square_shape] * 2,
+    places = [place_of(0, 1), place_of(1, 1)]
+    lower, upper, both, total = run(
+        functools.partial(fine_operators_kernel, places), "fine_operators",
+        [square_shape] * 3 + [array((rows, half), f32)],
         [mine, pcols, of_level(prolong_blocks, 0), of_level(prolong_blocks, 1),
-         *operators[0], *operators[1]],
-        flops=flops(rows, 2), scratch=held,
+         *operators[0], *operators[1], base, bases[0], far_base],
+        flops=flops(rows, 4), scratch=held,
     )
     parts = {}
-    for offset in range(0, pieces, 2):
+    for offset in reversed(range(0, pieces, 2)):
         (parts[offset],) = run(
             share_sum_kernel, "share_sum", [chunk_shape],
             [far_parts[offset], own_parts[offset], coarse_mat, upper],
         )
-        parts[offset + 1] = exchange(parts[offset], "narrow", 1)
     offsets = tuple(parts)
-    operands = [coarse_mat] + [parts[o] for o in offsets] + [bases[-1]]
+    (value,) = run(
+        functools.partial(coarse_kernel, offsets), "coarse", [real_shape],
+        [coarse_mat] + [parts[o] for o in offsets] + [bases[-1]], flops=flops(width, len(offsets)),
+    )
+    parts = {o + 1: exchange(parts[o], "narrow", 1) for o in reversed(offsets)}
+    offsets = tuple(parts)
+    operands = [coarse_mat] + [parts[o] for o in offsets] + [value]
     for idx in reversed(range(2, last)):
         operands += [bases[idx], ups[idx - 2]]
-    coarse, near = run(
+    value, near = run(
         functools.partial(up_kernel, offsets), "up", [chunk_shape] * 2,
         operands + [bases[1], upper], flops=flops(width, len(offsets) + levels - 2),
     )
-    diagonal = exchange(coarse, "wide", 3)
+    diagonal, other = (exchange(value, "wide", bits) for bits in (3, 2))
     far = exchange(near, "wide", 1)
-    other = exchange(coarse, "wide", 2)
     result = None
     for group in (
         [(near, place_of(0, 0), None)],
-        [(diagonal, place_of(1, 1), far_base),
-         (far, place_of(1, 0), None),
-         (other, place_of(0, 1), bases[0])],
+        [(diagonal, place_of(1, 1), 1)],
+        [(far, place_of(1, 0), None), (other, place_of(0, 1), 0)],
     ):
-        values, places, raising_bases = zip(*group)
-        raised = tuple(value is not None for value in raising_bases)
-        operands = list(values) + [value for value in raising_bases if value is not None]
-        operands += [base, lower, upper]
+        values, places, slots = zip(*group)
+        operands = [*values, base, lower, total, both]
         aliases = {}
         if result is not None:
             aliases[len(operands)] = 0
             operands.append(in_hbm(result))
         (result,) = run(
-            functools.partial(output_kernel, places, raised),
+            functools.partial(output_kernel, places, slots),
             "output", [array((1, rows, fields), f32)], operands,
             flops=flops(width, len(group)), out_space=pltpu.HBM, aliases=aliases,
             scratch=[

time: 43.5 us -> 43 us (0.989)
  waiting for transfers between devices: 8.8 us -> 6.86 us
  Pallas kernels: 11.3 us -> 12.1 us
  local copies, waits for them, and re-layouts: 0.12 us -> 0.71 us
    ppermute x14, waiting for transfers between devices: 5.45 us -> 3.54 us  [exchange(): return lax.ppermute(value, axis, [(i, i ^ bit) for i in range(count)])]
    ppermute x2, waiting for transfers between devices: 2.67 us -> 1.41 us  [exchange_both(): return lax.ppermute(value, ('wide', 'narrow'), pairs)]
    ppermute x5, waiting for transfers between devices: 0.68 us -> 1.91 us  [swap_outer(): return lax.ppermute(outer, 'narrow', gaps)]
    ppermute x14, starting transfers between devices: 14 us -> 12.9 us  [exchange(): return lax.ppermute(value, axis, [(i, i ^ bit) for i in range(count)])]
    pallas_call x19 -> x21, Pallas kernels: 11.3 us -> 12.1 us  [run(): pl.pallas_call(body, grid=(1,) if windows else (), out_shape=[out_space(o...]
    ppermute x5, starting transfers between devices: 5.14 us -> 6.01 us  [swap_outer(): return lax.ppermute(outer, 'narrow', gaps)]
    unnamed x14, local copies, waits for them, and re-layouts: 0.12 us -> 0.71 us
  transfers between devices with their start and end apart: 21 -> 21, of which waited for: 10 -> 9; matrix products, arithmetic and copies ran while one was open for 0% -> 0% of each run, Pallas kernels for 18% -> 22%
where the time goes in v12:
time: 43 us; the launch traced here: 42.8 us
  starting transfers between devices  22.9 us (53%)
  Pallas kernels  12.1 us (28%)
  waiting for transfers between devices  6.86 us (16%)
  local copies, waits for them, and re-layouts  0.71 us (2%)
    ppermute x14, starting transfers between devices, exchange(): return lax.ppermute(value, axis, [(i, i ^ bit) for i in range(count)])  12.9 us
    pallas_call x21, Pallas kernels, run(): pl.pallas_call(body, grid=(1,) if windows else (), out_shape=[out_space(o...  12.1 us
    ppermute x5, starting transfers between devices, swap_outer(): return lax.ppermute(outer, 'narrow', gaps)  6.01 us
    ppermute x2, starting transfers between devices, exchange_both(): return lax.ppermute(value, ('wide', 'narrow'), pairs)  4.06 us
    ppermute x14, waiting for transfers between devices, exchange(): return lax.ppermute(value, axis, [(i, i ^ bit) for i in range(count)])  3.54 us
    ppermute x5, waiting for transfers between devices, swap_outer(): return lax.ppermute(outer, 'narrow', gaps)  1.91 us
    ppermute x2, waiting for transfers between devices, exchange_both(): return lax.ppermute(value, ('wide', 'narrow'), pairs)  1.41 us
  transfers between devices with their start and end apart: 21, of which 9 were waited for; matrix products, arithmetic and copies ran while one was open for 0% of the time, Pallas kernels for 22%

profile of v12, /device:TPU:0, one launch (start us, length us, event | category | flops | bytes accessed | tf_op | source)
XLA Modules:
  0.0 42.8 jit_solution(3187919298464510480)
XLA Ops:
  0.0 1.3 %start.1 = (s32[3,1,4,5]{3,2,1,0:T(4,128)S(1)}, bf16[64,512]{1,0:T(8,128)(2,1)S(1)}, bf16[64,256]{1,0:T(8,128)(2,1)S(1)}, bf16[64,256]{1,0:T(8,128)(2,1)S(1)}) custom-call(f32[1,256,512]{2,1,0:T(8,128)} %rhs.3, bf16[3,1,4,5,64,64]{5,4,3,2,1,0:T(8,128)(2,1)} %blocks.7, s32[3,1,4,5]{3,2,1,0:T(4,128)} %refs_0_.2), custom_call_target="tpu_custom_call" | custom-call | bytes 1016048 | tf_op jit(solution)/shard_map/start/pallas_call | solution.py:52
  1.3 0.5 %collective-permute-start.1 = (bf16[64,512]{1,0:T(8,128)(2,1)S(1)}, bf16[64,512]{1,0:T(8,128)(2,1)S(1)}, u32[]{:S(2)}, u32[]{:S(2)}) collective-permute-start(bf16[64,512]{1,0:T(8,128)(2,1)S(1)} %get-tuple-element.55), channel_id=1, source_target_pairs={{0,1},{1,0},{2,3},{3,2},{4,5},{5,4},{6,7},{7,6},{8,9},{9,8},{10,11... | collective-permute-start | bytes 196616 | tf_op jit(solution)/shard_map/ppermute | solution.py:323
  1.8 2.6 %collective-permute-start = (bf16[64,256]{1,0:T(8,128)(2,1)S(1)}, bf16[64,256]{1,0:T(8,128)(2,1)S(1)}, u32[]{:S(2)}, u32[]{:S(2)}) collective-permute-start(bf16[64,256]{1,0:T(8,128)(2,1)S(1)} %get-tuple-element.51._), channel_id=1, source_target_pairs={{0,3},{1,2},{2,1},{3,0},{4,7},{5,6},{6,5},{7,4},{8,11},{9,10},{10,... | collective-permute-start | bytes 98312 | tf_op jit(solution)/shard_map/ppermute | solution.py:338
  4.5 1.1 %first_local.1 = (f32[256,512]{1,0:T(8,128)S(1)}, f32[256,512]{1,0:T(8,128)S(1)}, bf16[256,256]{1,0:T(8,128)(2,1)S(1)}, bf16[256,128]{1,0:T(8,128)(2,1)S(1)}, f32[256,1]{1,0:T(8,128)S(1)}) custom-call(f32[1,256,512]{2,1,0:T(8,128)S(1)} %copy-done.3, bf16[64,256]{1,0:T(8,128)(2,1)S(1)} %get-tuple-element.51._, s32[3,1,4,5]{3,2,1,0:T(4,128)S(1)} %get-tuple-element.52.cols, ...), custom_call_target="tpu_custom_call" | custom-call | flops 67108864 | bytes 1048816 | tf_op jit(solution)/shard_map/first_local/pallas_call | solution.py:52
  5.6 0.5 %collective-permute-done.outer = bf16[64,256]{1,0:T(8,128)(2,1)S(1)} collective-permute-done((bf16[64,256]{1,0:T(8,128)(2,1)S(1)}, bf16[64,256]{1,0:T(8,128)(2,1)S(1)}, u32[]{:S(2)}, u32[]{:S(2)}) %collective-permute-start) | collective-permute-done | bytes 32800 | tf_op jit(solution)/shard_map/ppermute | solution.py:338
  6.1 0.2 first_residual.2
  6.3 1.7 %collective-permute-start.2 = (bf16[256,128]{1,0:T(8,128)(2,1)S(1)}, bf16[256,128]{1,0:T(8,128)(2,1)S(1)}, u32[]{:S(2)}, u32[]{:S(2)}) collective-permute-start(bf16[256,128]{1,0:T(8,128)(2,1)S(1)} %get-tuple-element.56._), channel_id=1, source_target_pairs={{0,4},{4,0},{8,12},{12,8},{16,20},{20,16},{24,28},{28,24},{1,5},{5... | collective-permute-start | bytes 196616 | tf_op jit(solution)/shard_map/ppermute | solution.py:323
  8.0 0.2 first_residual.3
  8.2 1.4 %collective-permute-start.6 = (bf16[256,128]{1,0:T(8,128)(2,1)S(1)}, bf16[256,128]{1,0:T(8,128)(2,1)S(1)}, u32[]{:S(2)}, u32[]{:S(2)}) collective-permute-start(bf16[256,128]{1,0:T(8,128)(2,1)S(1)} %get-tuple-element.68), channel_id=1, source_target_pairs={{0,4},{4,0},{8,12},{12,8},{16,20},{20,16},{24,28},{28,24},{1,5},{5... | collective-permute-start | bytes 196616 | tf_op jit(solution)/shard_map/ppermute | solution.py:323
  9.6 1.1 %operators.2 = (bf16[256,512]{1,0:T(8,128)(2,1)S(1)}, bf16[256,256]{1,0:T(8,128)(2,1)S(1)}, bf16[256,128]{1,0:T(8,128)(2,1)S(1)}, f32[256,1]{1,0:T(8,128)S(1)}) custom-call(bf16[256,128]{1,0:T(8,128)(2,1)S(1)} %get-tuple-element.56._, s32[3,3,1,4]{3,2,1,0:T(1,128)S(1)} %bitcast.2, bf16[3,1,4,3,64,64]{5,4,3,2,1,0:T(8,128)(2,1)S(1)} %copy-done.1, ...), custom_call_target="tpu_custom_call" | custom-call | bytes 852352 | tf_op jit(solution)/shard_map/operators/pallas_call | solution.py:52
  10.8 0.2 join.3
  11.0 1.6 %collective-permute-start.3 = (bf16[64,128]{1,0:T(8,128)(2,1)S(1)}, bf16[64,128]{1,0:T(8,128)(2,1)S(1)}, u32[]{:S(2)}, u32[]{:S(2)}) collective-permute-start(bf16[64,128]{1,0:T(8,128)(2,1)S(1)} %get-tuple-element.64), channel_id=1, source_target_pairs={{0,3},{1,2},{2,1},{3,0},{4,7},{5,6},{6,5},{7,4},{8,11},{9,10},{10,... | collective-permute-start | bytes 49160 | tf_op jit(solution)/shard_map/ppermute | solution.py:338
  12.6 0.6 %collective-permute-start.4 = (bf16[64,128]{1,0:T(8,128)(2,1)S(1)}, bf16[64,128]{1,0:T(8,128)(2,1)S(1)}, u32[]{:S(2)}, u32[]{:S(2)}) collective-permute-start(bf16[64,128]{1,0:T(8,128)(2,1)S(1)} %get-tuple-element.65), channel_id=1, source_target_pairs={{0,1},{1,0},{2,3},{3,2},{4,5},{5,4},{6,7},{7,6},{8,9},{9,8},{10,11... | collective-permute-start | bytes 49160 | tf_op jit(solution)/shard_map/ppermute | solution.py:323
  13.2 0.2 join.4
  13.4 0.8 %collective-permute-start.7 = (bf16[64,128]{1,0:T(8,128)(2,1)S(1)}, bf16[64,128]{1,0:T(8,128)(2,1)S(1)}, u32[]{:S(2)}, u32[]{:S(2)}) collective-permute-start(bf16[64,128]{1,0:T(8,128)(2,1)S(1)} %get-tuple-element.73), channel_id=1, source_target_pairs={{0,3},{1,2},{2,1},{3,0},{4,7},{5,6},{6,5},{7,4},{8,11},{9,10},{10,... | collective-permute-start | bytes 49160 | tf_op jit(solution)/shard_map/ppermute | solution.py:338
  14.2 0.6 %collective-permute-start.8 = (bf16[64,128]{1,0:T(8,128)(2,1)S(1)}, bf16[64,128]{1,0:T(8,128)(2,1)S(1)}, u32[]{:S(2)}, u32[]{:S(2)}) collective-permute-start(bf16[64,128]{1,0:T(8,128)(2,1)S(1)} %get-tuple-element.74), channel_id=1, source_target_pairs={{0,1},{1,0},{2,3},{3,2},{4,5},{5,4},{6,7},{7,6},{8,9},{9,8},{10,11... | collective-permute-start | bytes 49160 | tf_op jit(solution)/shard_map/ppermute | solution.py:323
  14.9 0.2 residual.3
  15.1 1.6 %collective-permute-start.9 = (bf16[256,128]{1,0:T(8,128)(2,1)S(1)}, bf16[256,128]{1,0:T(8,128)(2,1)S(1)}, u32[]{:S(2)}, u32[]{:S(2)}) collective-permute-start(bf16[256,128]{1,0:T(8,128)(2,1)S(1)} %get-tuple-element.70._), channel_id=1, source_target_pairs={{0,8},{4,12},{8,0},{12,4},{16,24},{20,28},{24,16},{28,20},{1,9},{5... | collective-permute-start | bytes 196616 | tf_op jit(solution)/shard_map/ppermute | solution.py:323
  16.8 1.4 %collective-permute-start.12 = (bf16[256,128]{1,0:T(8,128)(2,1)S(1)}, bf16[256,128]{1,0:T(8,128)(2,1)S(1)}, u32[]{:S(2)}, u32[]{:S(2)}) collective-permute-start(bf16[256,128]{1,0:T(8,128)(2,1)S(1)} %get-tuple-element.85.near), channel_id=1, source_target_pairs={{0,4},{4,0},{8,12},{12,8},{16,20},{20,16},{24,28},{28,24},{1,5},{5... | collective-permute-start | bytes 196616 | tf_op jit(solution)/shard_map/ppermute | solution.py:323
  18.1 0.2 residual.4
  18.3 1.2 %operators.3 = (bf16[256,512]{1,0:T(8,128)(2,1)S(1)}, bf16[256,256]{1,0:T(8,128)(2,1)S(1)}, bf16[256,128]{1,0:T(8,128)(2,1)S(1)}, f32[256,1]{1,0:T(8,128)S(1)}, bf16[256,256]{1,0:T(8,128)(2,1)S(1)}) custom-call(bf16[256,128]{1,0:T(8,128)(2,1)S(1)} %get-tuple-element.70._, s32[3,3,1,4]{3,2,1,0:T(1,128)S(1)} %bitcast.3, ...), custom_call_target="tpu_custom_call" | custom-call | bytes 1147264 | tf_op jit(solution)/shard_map/operators/pallas_call | solution.py:52
  19.5 0.2 join.5
  19.8 0.9 %collective-permute-start.10 = (bf16[64,128]{1,0:T(8,128)(2,1)S(1)}, bf16[64,128]{1,0:T(8,128)(2,1)S(1)}, u32[]{:S(2)}, u32[]{:S(2)}) collective-permute-start(bf16[64,128]{1,0:T(8,128)(2,1)S(1)} %get-tuple-element.81), channel_id=1, source_target_pairs={{0,3},{1,2},{2,1},{3,0},{4,7},{5,6},{6,5},{7,4},{8,11},{9,10},{10,... | collective-permute-start | bytes 49160 | tf_op jit(solution)/shard_map/ppermute | solution.py:338
  20.7 0.9 %collective-permute-start.11 = (bf16[64,128]{1,0:T(8,128)(2,1)S(1)}, bf16[64,128]{1,0:T(8,128)(2,1)S(1)}, u32[]{:S(2)}, u32[]{:S(2)}) collective-permute-start(bf16[64,128]{1,0:T(8,128)(2,1)S(1)} %get-tuple-element.82), channel_id=1, source_target_pairs={{0,1},{1,0},{2,3},{3,2},{4,5},{5,4},{6,7},{7,6},{8,9},{9,8},{10,11... | collective-permute-start | bytes 49160 | tf_op jit(solution)/shard_map/ppermute | solution.py:323
  21.6 1.4 %collective-permute-done.10.outer = bf16[64,128]{1,0:T(8,128)(2,1)S(1)} collective-permute-done((bf16[64,128]{1,0:T(8,128)(2,1)S(1)}, bf16[64,128]{1,0:T(8,128)(2,1)S(1)}, u32[]{:S(2)}, u32[]{:S(2)}) %collective-permute-start.10) | collective-permute-done | bytes 16416 | tf_op jit(solution)/shard_map/ppermute | solution.py:338
  23.0 0.4 residual.5
  23.4 3.7 %collective-permute-start.15 = (bf16[256,128]{1,0:T(8,128)(2,1)S(1)}, bf16[256,128]{1,0:T(8,128)(2,1)S(1)}, u32[]{:S(2)}, u32[]{:S(2)}) collective-permute-start(bf16[256,128]{1,0:T(8,128)(2,1)S(1)} %get-tuple-element.84.refs_0_._.own), channel_id=1, source_target_pairs={{0,18},{1,19},{2,16},{3,17},{4,22},{5,23},{6,20},{7,21},{8,26},{9,... | collective-permute-start | bytes 196616 | tf_op jit(solution)/shard_map/ppermute | solution.py:332
  27.1 0.4 collective-permute-start.16
  27.5 0.3 collective-permute-start.13
  27.9 0.7 %copy-done.6 = s32[3,1,4,2]{2,3,1,0:T(2,128)S(1)} copy-done((s32[3,1,4,2]{2,3,1,0:T(2,128)S(1)}, s32[3,1,4,2]{2,3,1,0:T(2,128)}, u32[]{:S(2)}) %copy-start.6) | copy-done | bytes 120
  28.6 1.2 %fine_operators.1 = (bf16[256,256]{1,0:T(8,128)(2,1)S(1)}, bf16[256,256]{1,0:T(8,128)(2,1)S(1)}, bf16[256,256]{1,0:T(8,128)(2,1)S(1)}, f32[256,256]{1,0:T(8,128)S(1)}) custom-call(bf16[256,128]{1,0:T(8,128)(2,1)S(1)} %get-tuple-element.84.refs_0_._.own, s32[3,1,2,4]{3,2,1,0:T(2,128)S(1)} %bitcast.4, bf16[3,1,4,2,64,64]{5,4,3,2,1,0:T(8,128)(2,1)S(1)} %copy-done.2, ...), custom_call_target="tpu_custom_call" | custom-call | flops 134217728 | bytes 1378400 | tf_op jit(solution)/shard_map/fine_operators/pallas_call | solution.py:52
  29.8 1.1 %coarse_operators.1.refs_0_.inverse = bf16[256,1024]{1,0:T(8,128)(2,1)S(1)} custom-call(bf16[256,128]{1,0:T(8,128)(2,1)S(1)} %get-tuple-element.84.refs_0_._.own, bf16[256,128]{1,0:T(8,128)(2,1)S(1)} %collective-permute-done.12.refs_1_.far, s32[3,1,2,4]{3,2,1,0:T(2,128)S(1)} %bitcast.5, bf16[256,1024]{1,0:T(8,128)(2,1)S(1)} %copy-done.4, ...), custom_call_target="tpu_custom_call" | custom-call | flops 201326592 | bytes 984160 | tf_op jit(solution)/shard_map/coarse_operators/pallas_call | solution.py:52
  30.9 0.1 collective-permute-done.15.far
  31.0 0.7 %collective-permute-done.16.own = bf16[256,128]{1,0:T(8,128)(2,1)S(1)} collective-permute-done((bf16[256,128]{1,0:T(8,128)(2,1)S(1)}, bf16[256,128]{1,0:T(8,128)(2,1)S(1)}, u32[]{:S(2)}, u32[]{:S(2)}) %collective-permute-start.16) | collective-permute-done | bytes 65568 | tf_op jit(solution)/shard_map/ppermute | solution.py:323
  31.7 0.1 collective-permute-start.17
  31.8 1.3 %collective-permute-done.13.far = bf16[256,128]{1,0:T(8,128)(2,1)S(1)} collective-permute-done((bf16[256,128]{1,0:T(8,128)(2,1)S(1)}, bf16[256,128]{1,0:T(8,128)(2,1)S(1)}, u32[]{:S(2)}, u32[]{:S(2)}) %collective-permute-start.13) | collective-permute-done | bytes 65568 | tf_op jit(solution)/shard_map/ppermute | solution.py:332
  33.2 0.2 coarse.1.refs_2_
  33.4 1.0 %collective-permute-done.14.refs_0_ = bf16[256,128]{1,0:T(8,128)(2,1)S(1)} collective-permute-done((bf16[256,128]{1,0:T(8,128)(2,1)S(1)}, bf16[256,128]{1,0:T(8,128)(2,1)S(1)}, u32[]{:S(2)}, u32[]{:S(2)}) %collective-permute-start.14) | collective-permute-done | bytes 65568 | tf_op jit(solution)/shard_map/ppermute | solution.py:323
  34.4 0.4 up.1
  34.8 2.0 %collective-permute-start.20 = (bf16[256,128]{1,0:T(8,128)(2,1)S(1)}, bf16[256,128]{1,0:T(8,128)(2,1)S(1)}, u32[]{:S(2)}, u32[]{:S(2)}) collective-permute-start(bf16[256,128]{1,0:T(8,128)(2,1)S(1)} %get-tuple-element.93), channel_id=1, source_target_pairs={{0,12},{4,8},{8,4},{12,0},{16,28},{20,24},{24,20},{28,16},{1,13},{... | collective-permute-start | bytes 196616 | tf_op jit(solution)/shard_map/ppermute | solution.py:323
  36.8 0.8 %collective-permute-start.18 = (bf16[256,128]{1,0:T(8,128)(2,1)S(1)}, bf16[256,128]{1,0:T(8,128)(2,1)S(1)}, u32[]{:S(2)}, u32[]{:S(2)}) collective-permute-start(bf16[256,128]{1,0:T(8,128)(2,1)S(1)} %get-tuple-element.92.refs_0_), channel_id=1, source_target_pairs={{0,4},{4,0},{8,12},{12,8},{16,20},{20,16},{24,28},{28,24},{1,5},{5... | collective-permute-start | bytes 196616 | tf_op jit(solution)/shard_map/ppermute | solution.py:323
  37.7 0.7 %collective-permute-start.19 = (bf16[256,128]{1,0:T(8,128)(2,1)S(1)}, bf16[256,128]{1,0:T(8,128)(2,1)S(1)}, u32[]{:S(2)}, u32[]{:S(2)}) collective-permute-start(bf16[256,128]{1,0:T(8,128)(2,1)S(1)} %get-tuple-element.93), channel_id=1, source_target_pairs={{0,8},{4,12},{8,0},{12,4},{16,24},{20,28},{24,16},{28,20},{1,9},{5... | collective-permute-start | bytes 196616 | tf_op jit(solution)/shard_map/ppermute | solution.py:323
  38.4 0.8 %output.3.refs_5_ = f32[1,256,512]{2,1,0:T(8,128)} custom-call(bf16[256,128]{1,0:T(8,128)(2,1)S(1)} %get-tuple-element.92.refs_0_, f32[256,512]{1,0:T(8,128)S(1)} %get-tuple-element.88.base.refs_1_.refs_2_, bf16[256,256]{1,0:T(8,128)(2,1)S(1)} %get-tuple-element.94.refs_2_.refs_3_, f32[256,256]{1,0:T(8,128)S(1)} %get-tuple-element.95.refs_3_.refs_4_, ...), custom_call_target="tpu_custom_call" | custom-call | flops 16777216 | bytes 1114112 | tf_op jit(solution)/shard_map/output/pallas_call | solution.py:52
  39.2 0.9 %collective-permute-done.20.refs_0_ = bf16[256,128]{1,0:T(8,128)(2,1)S(1)} collective-permute-done((bf16[256,128]{1,0:T(8,128)(2,1)S(1)}, bf16[256,128]{1,0:T(8,128)(2,1)S(1)}, u32[]{:S(2)}, u32[]{:S(2)}) %collective-permute-start.20) | collective-permute-done | bytes 65568 | tf_op jit(solution)/shard_map/ppermute | solution.py:323
  40.2 0.8 %output.4.refs_6_ = f32[1,256,512]{2,1,0:T(8,128)} custom-call(bf16[256,128]{1,0:T(8,128)(2,1)S(1)} %collective-permute-done.20.refs_0_, f32[256,512]{1,0:T(8,128)S(1)} %get-tuple-element.88.base.refs_1_.refs_2_, bf16[256,256]{1,0:T(8,128)(2,1)S(1)} %get-tuple-element.94.refs_2_.refs_3_, ...), custom_call_target="tpu_custom_call", output_to_operand_aliasing={{}: (5, {})} | custom-call | flops 16777216 | bytes 1638400 | tf_op jit(solution)/shard_map/output/pallas_call | solution.py:52
  41.0 0.4 collective-permute-done.18.refs_0_
  41.4 0.5 %collective-permute-done.19.refs_1_ = bf16[256,128]{1,0:T(8,128)(2,1)S(1)} collective-permute-done((bf16[256,128]{1,0:T(8,128)(2,1)S(1)}, bf16[256,128]{1,0:T(8,128)(2,1)S(1)}, u32[]{:S(2)}, u32[]{:S(2)}) %collective-permute-start.19) | collective-permute-done | bytes 65568 | tf_op jit(solution)/shard_map/ppermute | solution.py:323
  41.9 0.9 %output.5 = f32[1,256,512]{2,1,0:T(8,128)} custom-call(bf16[256,128]{1,0:T(8,128)(2,1)S(1)} %collective-permute-done.18.refs_0_, bf16[256,128]{1,0:T(8,128)(2,1)S(1)} %collective-permute-done.19.refs_1_, f32[256,512]{1,0:T(8,128)S(1)} %get-tuple-element.88.base.refs_1_.refs_2_, ...), custom_call_target="tpu_custom_call", output_to_operand_aliasing={{}: (6, {})} | custom-call | flops 33554432 | bytes 1703936 | tf_op jit(solution)/shard_map/output/pallas_call | solution.py:52
  (29 shorter events, 0.2 us)
Async XLA Ops:
  0.0 4.4 %copy-start = (bf16[3,1,4,5,64,64]{5,4,3,2,1,0:T(8,128)(2,1)S(1)}, bf16[3,1,4,5,64,64]{5,4,3,2,1,0:T(8,128)(2,1)}, u32[]{:S(2)}) copy-start(bf16[3,1,4,5,64,64]{5,4,3,2,1,0:T(8,128)(2,1)} %blocks.7) | copy-start | bytes 1474564
  0.0 4.4 %copy-start.3 = (f32[1,256,512]{2,1,0:T(8,128)S(1)}, f32[1,256,512]{2,1,0:T(8,128)}, u32[]{:S(2)}) copy-start(f32[1,256,512]{2,1,0:T(8,128)} %rhs.3) | copy-start | bytes 1572868
  1.3 4.8 %collective-permute-start.1 = (bf16[64,512]{1,0:T(8,128)(2,1)S(1)}, bf16[64,512]{1,0:T(8,128)(2,1)S(1)}, u32[]{:S(2)}, u32[]{:S(2)}) collective-permute-start(bf16[64,512]{1,0:T(8,128)(2,1)S(1)} %get-tuple-element.55), channel_id=1, source_target_pairs={{0,1},{1,0},{2,3},{3,2},{4,5},{5,4},{6,7},{7,6},{8,9},{9,8},{10,11... | collective-permute-start | bytes 196616 | tf_op jit(solution)/shard_map/ppermute | solution.py:323
  1.8 4.3 %collective-permute-start = (bf16[64,256]{1,0:T(8,128)(2,1)S(1)}, bf16[64,256]{1,0:T(8,128)(2,1)S(1)}, u32[]{:S(2)}, u32[]{:S(2)}) collective-permute-start(bf16[64,256]{1,0:T(8,128)(2,1)S(1)} %get-tuple-element.51._), channel_id=1, source_target_pairs={{0,3},{1,2},{2,1},{3,0},{4,7},{5,6},{6,5},{7,4},{8,11},{9,10},{10,... | collective-permute-start | bytes 98312 | tf_op jit(solution)/shard_map/ppermute | solution.py:338
  4.4 3.6 %collective-permute-start.5 = (bf16[64,256]{1,0:T(8,128)(2,1)S(1)}, bf16[64,256]{1,0:T(8,128)(2,1)S(1)}, u32[]{:S(2)}, u32[]{:S(2)}) collective-permute-start(bf16[64,256]{1,0:T(8,128)(2,1)S(1)} %get-tuple-element.66), channel_id=1, source_target_pairs={{0,3},{1,2},{2,1},{3,0},{4,7},{5,6},{6,5},{7,4},{8,11},{9,10},{10,... | collective-permute-start | bytes 98312 | tf_op jit(solution)/shard_map/ppermute | solution.py:338
  6.1 3.5 %copy-start.1 = (bf16[3,1,4,3,64,64]{5,4,3,2,1,0:T(8,128)(2,1)S(1)}, bf16[3,1,4,3,64,64]{5,4,3,2,1,0:T(8,128)(2,1)}, u32[]{:S(2)}) copy-start(bf16[3,1,4,3,64,64]{5,4,3,2,1,0:T(8,128)(2,1)} %refs_0_.3) | copy-start | bytes 884740
  6.3 4.5 %collective-permute-start.2 = (bf16[256,128]{1,0:T(8,128)(2,1)S(1)}, bf16[256,128]{1,0:T(8,128)(2,1)S(1)}, u32[]{:S(2)}, u32[]{:S(2)}) collective-permute-start(bf16[256,128]{1,0:T(8,128)(2,1)S(1)} %get-tuple-element.56._), channel_id=1, source_target_pairs={{0,4},{4,0},{8,12},{12,8},{16,20},{20,16},{24,28},{28,24},{1,5},{5... | collective-permute-start | bytes 196616 | tf_op jit(solution)/shard_map/ppermute | solution.py:323
  8.0 1.6 %copy-start.5 = (s32[3,1,4,3]{2,1,3,0:T(1,128)S(1)}, s32[3,1,4,3]{2,1,3,0:T(1,128)}, u32[]{:S(2)}) copy-start(s32[3,1,4,3]{2,1,3,0:T(1,128)} %param.11) | copy-start | bytes 436
  8.2 5.0 %collective-permute-start.6 = (bf16[256,128]{1,0:T(8,128)(2,1)S(1)}, bf16[256,128]{1,0:T(8,128)(2,1)S(1)}, u32[]{:S(2)}, u32[]{:S(2)}) collective-permute-start(bf16[256,128]{1,0:T(8,128)(2,1)S(1)} %get-tuple-element.68), channel_id=1, source_target_pairs={{0,4},{4,0},{8,12},{12,8},{16,20},{20,16},{24,28},{28,24},{1,5},{5... | collective-permute-start | bytes 196616 | tf_op jit(solution)/shard_map/ppermute | solution.py:323
  11.0 3.9 %collective-permute-start.3 = (bf16[64,128]{1,0:T(8,128)(2,1)S(1)}, bf16[64,128]{1,0:T(8,128)(2,1)S(1)}, u32[]{:S(2)}, u32[]{:S(2)}) collective-permute-start(bf16[64,128]{1,0:T(8,128)(2,1)S(1)} %get-tuple-element.64), channel_id=1, source_target_pairs={{0,3},{1,2},{2,1},{3,0},{4,7},{5,6},{6,5},{7,4},{8,11},{9,10},{10,... | collective-permute-start | bytes 49160 | tf_op jit(solution)/shard_map/ppermute | solution.py:338
  12.6 2.3 %collective-permute-start.4 = (bf16[64,128]{1,0:T(8,128)(2,1)S(1)}, bf16[64,128]{1,0:T(8,128)(2,1)S(1)}, u32[]{:S(2)}, u32[]{:S(2)}) collective-permute-start(bf16[64,128]{1,0:T(8,128)(2,1)S(1)} %get-tuple-element.65), channel_id=1, source_target_pairs={{0,1},{1,0},{2,3},{3,2},{4,5},{5,4},{6,7},{7,6},{8,9},{9,8},{10,11... | collective-permute-start | bytes 49160 | tf_op jit(solution)/shard_map/ppermute | solution.py:323
  13.4 4.7 %collective-permute-start.7 = (bf16[64,128]{1,0:T(8,128)(2,1)S(1)}, bf16[64,128]{1,0:T(8,128)(2,1)S(1)}, u32[]{:S(2)}, u32[]{:S(2)}) collective-permute-start(bf16[64,128]{1,0:T(8,128)(2,1)S(1)} %get-tuple-element.73), channel_id=1, source_target_pairs={{0,3},{1,2},{2,1},{3,0},{4,7},{5,6},{6,5},{7,4},{8,11},{9,10},{10,... | collective-permute-start | bytes 49160 | tf_op jit(solution)/shard_map/ppermute | solution.py:338
  14.2 3.9 %collective-permute-start.8 = (bf16[64,128]{1,0:T(8,128)(2,1)S(1)}, bf16[64,128]{1,0:T(8,128)(2,1)S(1)}, u32[]{:S(2)}, u32[]{:S(2)}) collective-permute-start(bf16[64,128]{1,0:T(8,128)(2,1)S(1)} %get-tuple-element.74), channel_id=1, source_target_pairs={{0,1},{1,0},{2,3},{3,2},{4,5},{5,4},{6,7},{7,6},{8,9},{9,8},{10,11... | collective-permute-start | bytes 49160 | tf_op jit(solution)/shard_map/ppermute | solution.py:323
  15.1 4.4 %collective-permute-start.9 = (bf16[256,128]{1,0:T(8,128)(2,1)S(1)}, bf16[256,128]{1,0:T(8,128)(2,1)S(1)}, u32[]{:S(2)}, u32[]{:S(2)}) collective-permute-start(bf16[256,128]{1,0:T(8,128)(2,1)S(1)} %get-tuple-element.70._), channel_id=1, source_target_pairs={{0,8},{4,12},{8,0},{12,4},{16,24},{20,28},{24,16},{28,20},{1,9},{5... | collective-permute-start | bytes 196616 | tf_op jit(solution)/shard_map/ppermute | solution.py:323
  16.8 11.1 %collective-permute-start.12 = (bf16[256,128]{1,0:T(8,128)(2,1)S(1)}, bf16[256,128]{1,0:T(8,128)(2,1)S(1)}, u32[]{:S(2)}, u32[]{:S(2)}) collective-permute-start(bf16[256,128]{1,0:T(8,128)(2,1)S(1)} %get-tuple-element.85.near), channel_id=1, source_target_pairs={{0,4},{4,0},{8,12},{12,8},{16,20},{20,16},{24,28},{28,24},{1,5},{5... | collective-permute-start | bytes 196616 | tf_op jit(solution)/shard_map/ppermute | solution.py:323
  19.8 8.1 %copy-start.2 = (bf16[3,1,4,2,64,64]{5,4,3,2,1,0:T(8,128)(2,1)S(1)}, bf16[3,1,4,2,64,64]{5,4,3,2,1,0:T(8,128)(2,1)}, u32[]{:S(2)}) copy-start(bf16[3,1,4,2,64,64]{5,4,3,2,1,0:T(8,128)(2,1)} %blocks_1.1) | copy-start | bytes 589828
  19.8 3.2 %collective-permute-start.10 = (bf16[64,128]{1,0:T(8,128)(2,1)S(1)}, bf16[64,128]{1,0:T(8,128)(2,1)S(1)}, u32[]{:S(2)}, u32[]{:S(2)}) collective-permute-start(bf16[64,128]{1,0:T(8,128)(2,1)S(1)} %get-tuple-element.81), channel_id=1, source_target_pairs={{0,3},{1,2},{2,1},{3,0},{4,7},{5,6},{6,5},{7,4},{8,11},{9,10},{10,... | collective-permute-start | bytes 49160 | tf_op jit(solution)/shard_map/ppermute | solution.py:338
  20.7 2.3 %collective-permute-start.11 = (bf16[64,128]{1,0:T(8,128)(2,1)S(1)}, bf16[64,128]{1,0:T(8,128)(2,1)S(1)}, u32[]{:S(2)}, u32[]{:S(2)}) collective-permute-start(bf16[64,128]{1,0:T(8,128)(2,1)S(1)} %get-tuple-element.82), channel_id=1, source_target_pairs={{0,1},{1,0},{2,3},{3,2},{4,5},{5,4},{6,7},{7,6},{8,9},{9,8},{10,11... | collective-permute-start | bytes 49160 | tf_op jit(solution)/shard_map/ppermute | solution.py:323
  23.4 7.6 %collective-permute-start.15 = (bf16[256,128]{1,0:T(8,128)(2,1)S(1)}, bf16[256,128]{1,0:T(8,128)(2,1)S(1)}, u32[]{:S(2)}, u32[]{:S(2)}) collective-permute-start(bf16[256,128]{1,0:T(8,128)(2,1)S(1)} %get-tuple-element.84.refs_0_._.own), channel_id=1, source_target_pairs={{0,18},{1,19},{2,16},{3,17},{4,22},{5,23},{6,20},{7,21},{8,26},{9,... | collective-permute-start | bytes 196616 | tf_op jit(solution)/shard_map/ppermute | solution.py:332
  27.1 4.5 %collective-permute-start.16 = (bf16[256,128]{1,0:T(8,128)(2,1)S(1)}, bf16[256,128]{1,0:T(8,128)(2,1)S(1)}, u32[]{:S(2)}, u32[]{:S(2)}) collective-permute-start(bf16[256,128]{1,0:T(8,128)(2,1)S(1)} %get-tuple-element.84.refs_0_._.own), channel_id=1, source_target_pairs={{0,2},{1,3},{2,0},{3,1},{4,6},{5,7},{6,4},{7,5},{8,10},{9,11},{10,... | collective-permute-start | bytes 196616 | tf_op jit(solution)/shard_map/ppermute | solution.py:323
  27.5 5.5 %collective-permute-start.13 = (bf16[256,128]{1,0:T(8,128)(2,1)S(1)}, bf16[256,128]{1,0:T(8,128)(2,1)S(1)}, u32[]{:S(2)}, u32[]{:S(2)}) collective-permute-start(bf16[256,128]{1,0:T(8,128)(2,1)S(1)} %get-tuple-element.84.refs_0_._.own), channel_id=1, source_target_pairs={{0,16},{1,17},{2,18},{3,19},{4,20},{5,21},{6,22},{7,23},{8,24},{9,... | collective-permute-start | bytes 196616 | tf_op jit(solution)/shard_map/ppermute | solution.py:332
  27.9 0.7 %copy-start.6 = (s32[3,1,4,2]{2,3,1,0:T(2,128)S(1)}, s32[3,1,4,2]{2,3,1,0:T(2,128)}, u32[]{:S(2)}) copy-start(s32[3,1,4,2]{2,3,1,0:T(2,128)} %param.13) | copy-start | bytes 292
  28.6 1.2 %copy-start.4 = (bf16[256,1024]{1,0:T(8,128)(2,1)S(1)}, bf16[256,1024]{1,0:T(8,128)(2,1)}, u32[]{:S(2)}) copy-start(bf16[256,1024]{1,0:T(8,128)(2,1)} %refs_3_.1) | copy-start | bytes 1572868
  31.7 1.7 %collective-permute-start.17 = (bf16[256,128]{1,0:T(8,128)(2,1)S(1)}, bf16[256,128]{1,0:T(8,128)(2,1)S(1)}, u32[]{:S(2)}, u32[]{:S(2)}) collective-permute-start(bf16[256,128]{1,0:T(8,128)(2,1)S(1)} %share_sum.3.refs_0_), channel_id=1, source_target_pairs={{0,1},{1,0},{2,3},{3,2},{4,5},{5,4},{6,7},{7,6},{8,9},{9,8},{10,11... | collective-permute-start | bytes 196616 | tf_op jit(solution)/shard_map/ppermute | solution.py:323
  33.1 1.3 %collective-permute-start.14 = (bf16[256,128]{1,0:T(8,128)(2,1)S(1)}, bf16[256,128]{1,0:T(8,128)(2,1)S(1)}, u32[]{:S(2)}, u32[]{:S(2)}) collective-permute-start(bf16[256,128]{1,0:T(8,128)(2,1)S(1)} %share_sum.2.refs_1_), channel_id=1, source_target_pairs={{0,1},{1,0},{2,3},{3,2},{4,5},{5,4},{6,7},{7,6},{8,9},{9,8},{10,11... | collective-permute-start | bytes 196616 | tf_op jit(solution)/shard_map/ppermute | solution.py:323
  34.8 5.3 %collective-permute-start.20 = (bf16[256,128]{1,0:T(8,128)(2,1)S(1)}, bf16[256,128]{1,0:T(8,128)(2,1)S(1)}, u32[]{:S(2)}, u32[]{:S(2)}) collective-permute-start(bf16[256,128]{1,0:T(8,128)(2,1)S(1)} %get-tuple-element.93), channel_id=1, source_target_pairs={{0,12},{4,8},{8,4},{12,0},{16,28},{20,24},{24,20},{28,16},{1,13},{... | collective-permute-start | bytes 196616 | tf_op jit(solution)/shard_map/ppermute | solution.py:323
  36.8 4.6 %collective-permute-start.18 = (bf16[256,128]{1,0:T(8,128)(2,1)S(1)}, bf16[256,128]{1,0:T(8,128)(2,1)S(1)}, u32[]{:S(2)}, u32[]{:S(2)}) collective-permute-start(bf16[256,128]{1,0:T(8,128)(2,1)S(1)} %get-tuple-element.92.refs_0_), channel_id=1, source_target_pairs={{0,4},{4,0},{8,12},{12,8},{16,20},{20,16},{24,28},{28,24},{1,5},{5... | collective-permute-start | bytes 196616 | tf_op jit(solution)/shard_map/ppermute | solution.py:323
  37.7 4.3 %collective-permute-start.19 = (bf16[256,128]{1,0:T(8,128)(2,1)S(1)}, bf16[256,128]{1,0:T(8,128)(2,1)S(1)}, u32[]{:S(2)}, u32[]{:S(2)}) collective-permute-start(bf16[256,128]{1,0:T(8,128)(2,1)S(1)} %get-tuple-element.93), channel_id=1, source_target_pairs={{0,8},{4,12},{8,0},{12,4},{16,24},{20,28},{24,16},{28,20},{1,9},{5... | collective-permute-start | bytes 196616 | tf_op jit(solution)/shard_map/ppermute | solution.py:323

commit v13 on v12

--- a/solution.py
+++ b/solution.py
@@ -208,11 +208,11 @@
     base[...] = rhs[...] * (relax_down * scale[...]) + (relax_up * scale[...]) * left
 
 
-def operators_kernel(level_idx, _, rcols, rblocks, cols, blocks, *refs):
-    if len(refs) > 4:
-        last_blocks, *refs = refs
-        assemble_share(level_idx + 1, rcols, last_blocks, refs.pop())
-    rmat, local, rim, scale = refs
+def share_kernel(level_idx, _, rcols, rblocks, share):
+    assemble_share(level_idx, rcols, rblocks, share)
+
+
+def operators_kernel(level_idx, _, rcols, rblocks, cols, blocks, rmat, local, rim, scale):
     assemble_restrict(level_idx, rcols, rblocks, rmat)
     assemble_galerkin(level_idx + 1, cols, blocks, local, rim, scale)
 
@@ -408,14 +408,11 @@
     pieces = lax.axis_size("narrow")
     for level_idx in range(levels - 1):
         other = [exchange(value, "wide", 1 << level_idx) for value in sent]
-        shapes = [rmat_shape] + operator_shapes
-        operands = [anchor, rcols, of_level(restrict_blocks, level_idx),
-                    gcols, of_level(galerkin_blocks, level_idx + 1)]
-        if level_idx + 1 == last:
-            shapes.append(square_shape)
-            operands.append(of_level(restrict_blocks, last))
-        rmat, local, rim, scale, *share = run(
-            functools.partial(operators_kernel, level_idx), "operators", shapes, operands
+        rmat, local, rim, scale = run(
+            functools.partial(operators_kernel, level_idx), "operators",
+            [rmat_shape] + operator_shapes,
+            [anchor, rcols, of_level(restrict_blocks, level_idx),
+             gcols, of_level(galerkin_blocks, level_idx + 1)],
         )
         operators.append((scale, local))
         joined = []
@@ -427,6 +424,12 @@
             )
             inner, outer = exchange(ends[0], "narrow", 1), swap_outer(ends[1])
             joined.append((rhs, smoothed, scale, local, rim, outer, inner))
+        share = []
+        if level_idx + 1 == last:
+            share = run(
+                functools.partial(share_kernel, last), "share", [square_shape],
+                [joined[0][1], rcols, of_level(restrict_blocks, last)],
+            )
         made = []
         for operands in joined:
             value, made_base = run(

time: 43 us -> 43 us (level)
  Pallas kernels: 12.1 us -> 12.8 us
  waiting for transfers between devices: 6.86 us -> 6.19 us
    ppermute x5, waiting for transfers between devices: 1.91 us -> 1.16 us  [swap_outer(): return lax.ppermute(outer, 'narrow', gaps)]
    pallas_call x21 -> x22, Pallas kernels: 12.1 us -> 12.8 us  [run(): pl.pallas_call(body, grid=(1,) if windows else (), out_shape=[out_space(o...]
  transfers between devices with their start and end apart: 21 -> 21, of which waited for: 9 -> 9; matrix products, arithmetic and copies ran while one was open for 0% -> 0% of each run, Pallas kernels for 22% -> 24%
where the time goes in v13:
time: 43 us; the launch traced here: 42.8 us
  starting transfers between devices  22.9 us (53%)
  Pallas kernels  12.8 us (30%)
  waiting for transfers between devices  6.19 us (14%)
  local copies, waits for them, and re-layouts  0.71 us (2%)
    ppermute x14, starting transfers between devices, exchange(): return lax.ppermute(value, axis, [(i, i ^ bit) for i in range(count)])  12.9 us
    pallas_call x22, Pallas kernels, run(): pl.pallas_call(body, grid=(1,) if windows else (), out_shape=[out_space(o...  12.8 us
    ppermute x5, starting transfers between devices, swap_outer(): return lax.ppermute(outer, 'narrow', gaps)  6.01 us
    ppermute x2, starting transfers between devices, exchange_both(): return lax.ppermute(value, ('wide', 'narrow'), pairs)  4.06 us
    ppermute x14, waiting for transfers between devices, exchange(): return lax.ppermute(value, axis, [(i, i ^ bit) for i in range(count)])  3.45 us
    ppermute x2, waiting for transfers between devices, exchange_both(): return lax.ppermute(value, ('wide', 'narrow'), pairs)  1.57 us
    ppermute x5, waiting for transfers between devices, swap_outer(): return lax.ppermute(outer, 'narrow', gaps)  1.16 us
  transfers between devices with their start and end apart: 21, of which 9 were waited for; matrix products, arithmetic and copies ran while one was open for 0% of the time, Pallas kernels for 24%

profile of v13, /device:TPU:0, one launch (start us, length us, event | category | flops | bytes accessed | tf_op | source)
XLA Modules:
  0.0 42.8 jit_solution(17897865625680692278)
XLA Ops:
  0.0 1.3 %start.1 = (s32[3,1,4,5]{3,2,1,0:T(4,128)S(1)}, bf16[64,512]{1,0:T(8,128)(2,1)S(1)}, bf16[64,256]{1,0:T(8,128)(2,1)S(1)}, bf16[64,256]{1,0:T(8,128)(2,1)S(1)}) custom-call(f32[1,256,512]{2,1,0:T(8,128)} %rhs.3, bf16[3,1,4,5,64,64]{5,4,3,2,1,0:T(8,128)(2,1)} %blocks.7, s32[3,1,4,5]{3,2,1,0:T(4,128)} %refs_0_.1), custom_call_target="tpu_custom_call" | custom-call | bytes 1016048 | tf_op jit(solution)/shard_map/start/pallas_call | solution.py:52
  1.3 0.5 %collective-permute-start.1 = (bf16[64,512]{1,0:T(8,128)(2,1)S(1)}, bf16[64,512]{1,0:T(8,128)(2,1)S(1)}, u32[]{:S(2)}, u32[]{:S(2)}) collective-permute-start(bf16[64,512]{1,0:T(8,128)(2,1)S(1)} %get-tuple-element.54), channel_id=1, source_target_pairs={{0,1},{1,0},{2,3},{3,2},{4,5},{5,4},{6,7},{7,6},{8,9},{9,8},{10,11... | collective-permute-start | bytes 196616 | tf_op jit(solution)/shard_map/ppermute | solution.py:323
  1.8 2.6 %collective-permute-start = (bf16[64,256]{1,0:T(8,128)(2,1)S(1)}, bf16[64,256]{1,0:T(8,128)(2,1)S(1)}, u32[]{:S(2)}, u32[]{:S(2)}) collective-permute-start(bf16[64,256]{1,0:T(8,128)(2,1)S(1)} %get-tuple-element.50._), channel_id=1, source_target_pairs={{0,3},{1,2},{2,1},{3,0},{4,7},{5,6},{6,5},{7,4},{8,11},{9,10},{10,... | collective-permute-start | bytes 98312 | tf_op jit(solution)/shard_map/ppermute | solution.py:338
  4.5 1.1 %first_local.1 = (f32[256,512]{1,0:T(8,128)S(1)}, f32[256,512]{1,0:T(8,128)S(1)}, bf16[256,256]{1,0:T(8,128)(2,1)S(1)}, bf16[256,128]{1,0:T(8,128)(2,1)S(1)}, f32[256,1]{1,0:T(8,128)S(1)}) custom-call(f32[1,256,512]{2,1,0:T(8,128)S(1)} %copy-done.3, bf16[64,256]{1,0:T(8,128)(2,1)S(1)} %get-tuple-element.50._, s32[3,1,4,5]{3,2,1,0:T(4,128)S(1)} %get-tuple-element.51.cols, ...), custom_call_target="tpu_custom_call" | custom-call | flops 67108864 | bytes 1048816 | tf_op jit(solution)/shard_map/first_local/pallas_call | solution.py:52
  5.6 0.5 %collective-permute-done.outer = bf16[64,256]{1,0:T(8,128)(2,1)S(1)} collective-permute-done((bf16[64,256]{1,0:T(8,128)(2,1)S(1)}, bf16[64,256]{1,0:T(8,128)(2,1)S(1)}, u32[]{:S(2)}, u32[]{:S(2)}) %collective-permute-start) | collective-permute-done | bytes 32800 | tf_op jit(solution)/shard_map/ppermute | solution.py:338
  6.1 0.2 first_residual.2
  6.3 1.7 %collective-permute-start.2 = (bf16[256,128]{1,0:T(8,128)(2,1)S(1)}, bf16[256,128]{1,0:T(8,128)(2,1)S(1)}, u32[]{:S(2)}, u32[]{:S(2)}) collective-permute-start(bf16[256,128]{1,0:T(8,128)(2,1)S(1)} %get-tuple-element.55._), channel_id=1, source_target_pairs={{0,4},{4,0},{8,12},{12,8},{16,20},{20,16},{24,28},{28,24},{1,5},{5... | collective-permute-start | bytes 196616 | tf_op jit(solution)/shard_map/ppermute | solution.py:323
  8.0 0.2 first_residual.3
  8.2 1.4 %collective-permute-start.6 = (bf16[256,128]{1,0:T(8,128)(2,1)S(1)}, bf16[256,128]{1,0:T(8,128)(2,1)S(1)}, u32[]{:S(2)}, u32[]{:S(2)}) collective-permute-start(bf16[256,128]{1,0:T(8,128)(2,1)S(1)} %get-tuple-element.67), channel_id=1, source_target_pairs={{0,4},{4,0},{8,12},{12,8},{16,20},{20,16},{24,28},{28,24},{1,5},{5... | collective-permute-start | bytes 196616 | tf_op jit(solution)/shard_map/ppermute | solution.py:323
  9.6 1.1 %operators.2 = (bf16[256,512]{1,0:T(8,128)(2,1)S(1)}, bf16[256,256]{1,0:T(8,128)(2,1)S(1)}, bf16[256,128]{1,0:T(8,128)(2,1)S(1)}, f32[256,1]{1,0:T(8,128)S(1)}) custom-call(bf16[256,128]{1,0:T(8,128)(2,1)S(1)} %get-tuple-element.55._, s32[3,3,1,4]{3,2,1,0:T(1,128)S(1)} %bitcast.2, bf16[3,1,4,3,64,64]{5,4,3,2,1,0:T(8,128)(2,1)S(1)} %copy-done.1, ...), custom_call_target="tpu_custom_call" | custom-call | bytes 852352 | tf_op jit(solution)/shard_map/operators/pallas_call | solution.py:52
  10.8 0.2 join.3
  11.0 1.6 %collective-permute-start.3 = (bf16[64,128]{1,0:T(8,128)(2,1)S(1)}, bf16[64,128]{1,0:T(8,128)(2,1)S(1)}, u32[]{:S(2)}, u32[]{:S(2)}) collective-permute-start(bf16[64,128]{1,0:T(8,128)(2,1)S(1)} %get-tuple-element.63), channel_id=1, source_target_pairs={{0,3},{1,2},{2,1},{3,0},{4,7},{5,6},{6,5},{7,4},{8,11},{9,10},{10,... | collective-permute-start | bytes 49160 | tf_op jit(solution)/shard_map/ppermute | solution.py:338
  12.6 0.6 %collective-permute-start.4 = (bf16[64,128]{1,0:T(8,128)(2,1)S(1)}, bf16[64,128]{1,0:T(8,128)(2,1)S(1)}, u32[]{:S(2)}, u32[]{:S(2)}) collective-permute-start(bf16[64,128]{1,0:T(8,128)(2,1)S(1)} %get-tuple-element.64), channel_id=1, source_target_pairs={{0,1},{1,0},{2,3},{3,2},{4,5},{5,4},{6,7},{7,6},{8,9},{9,8},{10,11... | collective-permute-start | bytes 49160 | tf_op jit(solution)/shard_map/ppermute | solution.py:323
  13.2 0.2 join.4
  13.4 0.8 %collective-permute-start.7 = (bf16[64,128]{1,0:T(8,128)(2,1)S(1)}, bf16[64,128]{1,0:T(8,128)(2,1)S(1)}, u32[]{:S(2)}, u32[]{:S(2)}) collective-permute-start(bf16[64,128]{1,0:T(8,128)(2,1)S(1)} %get-tuple-element.72), channel_id=1, source_target_pairs={{0,3},{1,2},{2,1},{3,0},{4,7},{5,6},{6,5},{7,4},{8,11},{9,10},{10,... | collective-permute-start | bytes 49160 | tf_op jit(solution)/shard_map/ppermute | solution.py:338
  14.2 0.6 %collective-permute-start.8 = (bf16[64,128]{1,0:T(8,128)(2,1)S(1)}, bf16[64,128]{1,0:T(8,128)(2,1)S(1)}, u32[]{:S(2)}, u32[]{:S(2)}) collective-permute-start(bf16[64,128]{1,0:T(8,128)(2,1)S(1)} %get-tuple-element.73), channel_id=1, source_target_pairs={{0,1},{1,0},{2,3},{3,2},{4,5},{5,4},{6,7},{7,6},{8,9},{9,8},{10,11... | collective-permute-start | bytes 49160 | tf_op jit(solution)/shard_map/ppermute | solution.py:323
  14.9 0.2 residual.3
  15.1 1.6 %collective-permute-start.9 = (bf16[256,128]{1,0:T(8,128)(2,1)S(1)}, bf16[256,128]{1,0:T(8,128)(2,1)S(1)}, u32[]{:S(2)}, u32[]{:S(2)}) collective-permute-start(bf16[256,128]{1,0:T(8,128)(2,1)S(1)} %get-tuple-element.69._), channel_id=1, source_target_pairs={{0,8},{4,12},{8,0},{12,4},{16,24},{20,28},{24,16},{28,20},{1,9},{5... | collective-permute-start | bytes 196616 | tf_op jit(solution)/shard_map/ppermute | solution.py:323
  16.8 1.3 %collective-permute-start.12 = (bf16[256,128]{1,0:T(8,128)(2,1)S(1)}, bf16[256,128]{1,0:T(8,128)(2,1)S(1)}, u32[]{:S(2)}, u32[]{:S(2)}) collective-permute-start(bf16[256,128]{1,0:T(8,128)(2,1)S(1)} %get-tuple-element.83.near), channel_id=1, source_target_pairs={{0,4},{4,0},{8,12},{12,8},{16,20},{20,16},{24,28},{28,24},{1,5},{5... | collective-permute-start | bytes 196616 | tf_op jit(solution)/shard_map/ppermute | solution.py:323
  18.1 0.2 residual.4
  18.3 1.1 %operators.3 = (bf16[256,512]{1,0:T(8,128)(2,1)S(1)}, bf16[256,256]{1,0:T(8,128)(2,1)S(1)}, bf16[256,128]{1,0:T(8,128)(2,1)S(1)}, f32[256,1]{1,0:T(8,128)S(1)}) custom-call(bf16[256,128]{1,0:T(8,128)(2,1)S(1)} %get-tuple-element.69._, s32[3,3,1,4]{3,2,1,0:T(1,128)S(1)} %bitcast.3, bf16[3,1,4,3,64,64]{5,4,3,2,1,0:T(8,128)(2,1)S(1)} %copy-done.1, ...), custom_call_target="tpu_custom_call" | custom-call | bytes 852352 | tf_op jit(solution)/shard_map/operators/pallas_call | solution.py:52
  19.4 0.2 join.5
  19.7 0.9 %collective-permute-start.10 = (bf16[64,128]{1,0:T(8,128)(2,1)S(1)}, bf16[64,128]{1,0:T(8,128)(2,1)S(1)}, u32[]{:S(2)}, u32[]{:S(2)}) collective-permute-start(bf16[64,128]{1,0:T(8,128)(2,1)S(1)} %get-tuple-element.80), channel_id=1, source_target_pairs={{0,3},{1,2},{2,1},{3,0},{4,7},{5,6},{6,5},{7,4},{8,11},{9,10},{10,... | collective-permute-start | bytes 49160 | tf_op jit(solution)/shard_map/ppermute | solution.py:338
  20.6 0.9 %collective-permute-start.11 = (bf16[64,128]{1,0:T(8,128)(2,1)S(1)}, bf16[64,128]{1,0:T(8,128)(2,1)S(1)}, u32[]{:S(2)}, u32[]{:S(2)}) collective-permute-start(bf16[64,128]{1,0:T(8,128)(2,1)S(1)} %get-tuple-element.81), channel_id=1, source_target_pairs={{0,1},{1,0},{2,3},{3,2},{4,5},{5,4},{6,7},{7,6},{8,9},{9,8},{10,11... | collective-permute-start | bytes 49160 | tf_op jit(solution)/shard_map/ppermute | solution.py:323
  21.5 0.7 %share.1 = bf16[256,256]{1,0:T(8,128)(2,1)S(1)} custom-call(bf16[256,128]{1,0:T(8,128)(2,1)S(1)} %get-tuple-element.77._.smoothed, s32[3,3,1,4]{3,2,1,0:T(1,128)S(1)} %bitcast.4, bf16[3,1,4,3,64,64]{5,4,3,2,1,0:T(8,128)(2,1)S(1)} %copy-done.1), custom_call_target="tpu_custom_call" | custom-call | bytes 360592 | tf_op jit(solution)/shard_map/share/pallas_call | solution.py:52
  22.2 0.7 %collective-permute-done.10.outer = bf16[64,128]{1,0:T(8,128)(2,1)S(1)} collective-permute-done((bf16[64,128]{1,0:T(8,128)(2,1)S(1)}, bf16[64,128]{1,0:T(8,128)(2,1)S(1)}, u32[]{:S(2)}, u32[]{:S(2)}) %collective-permute-start.10) | collective-permute-done | bytes 16416 | tf_op jit(solution)/shard_map/ppermute | solution.py:338
  22.9 0.4 residual.5
  23.3 3.7 %collective-permute-start.15 = (bf16[256,128]{1,0:T(8,128)(2,1)S(1)}, bf16[256,128]{1,0:T(8,128)(2,1)S(1)}, u32[]{:S(2)}, u32[]{:S(2)}) collective-permute-start(bf16[256,128]{1,0:T(8,128)(2,1)S(1)} %get-tuple-element.82.refs_0_._.own), channel_id=1, source_target_pairs={{0,18},{1,19},{2,16},{3,17},{4,22},{5,23},{6,20},{7,21},{8,26},{9,... | collective-permute-start | bytes 196616 | tf_op jit(solution)/shard_map/ppermute | solution.py:332
  27.1 0.4 collective-permute-start.16
  27.4 0.3 collective-permute-start.13
  27.8 0.7 %copy-done.6 = s32[3,1,4,2]{2,3,1,0:T(2,128)S(1)} copy-done((s32[3,1,4,2]{2,3,1,0:T(2,128)S(1)}, s32[3,1,4,2]{2,3,1,0:T(2,128)}, u32[]{:S(2)}) %copy-start.6) | copy-done | bytes 120
  28.5 1.2 %fine_operators.1 = (bf16[256,256]{1,0:T(8,128)(2,1)S(1)}, bf16[256,256]{1,0:T(8,128)(2,1)S(1)}, bf16[256,256]{1,0:T(8,128)(2,1)S(1)}, f32[256,256]{1,0:T(8,128)S(1)}) custom-call(bf16[256,128]{1,0:T(8,128)(2,1)S(1)} %get-tuple-element.82.refs_0_._.own, s32[3,1,2,4]{3,2,1,0:T(2,128)S(1)} %bitcast.5, bf16[3,1,4,2,64,64]{5,4,3,2,1,0:T(8,128)(2,1)S(1)} %copy-done.2, ...), custom_call_target="tpu_custom_call" | custom-call | flops 134217728 | bytes 1378400 | tf_op jit(solution)/shard_map/fine_operators/pallas_call | solution.py:52
  29.7 1.1 %coarse_operators.1.refs_0_.inverse = bf16[256,1024]{1,0:T(8,128)(2,1)S(1)} custom-call(bf16[256,128]{1,0:T(8,128)(2,1)S(1)} %get-tuple-element.82.refs_0_._.own, bf16[256,128]{1,0:T(8,128)(2,1)S(1)} %collective-permute-done.12.refs_1_.far, s32[3,1,2,4]{3,2,1,0:T(2,128)S(1)} %bitcast.6, bf16[256,1024]{1,0:T(8,128)(2,1)S(1)} %copy-done.4, ...), custom_call_target="tpu_custom_call" | custom-call | flops 201326592 | bytes 984160 | tf_op jit(solution)/shard_map/coarse_operators/pallas_call | solution.py:52
  30.8 0.2 collective-permute-done.15.far
  31.0 0.6 %collective-permute-done.16.own = bf16[256,128]{1,0:T(8,128)(2,1)S(1)} collective-permute-done((bf16[256,128]{1,0:T(8,128)(2,1)S(1)}, bf16[256,128]{1,0:T(8,128)(2,1)S(1)}, u32[]{:S(2)}, u32[]{:S(2)}) %collective-permute-start.16) | collective-permute-done | bytes 65568 | tf_op jit(solution)/shard_map/ppermute | solution.py:323
  31.7 1.4 %collective-permute-done.13.far = bf16[256,128]{1,0:T(8,128)(2,1)S(1)} collective-permute-done((bf16[256,128]{1,0:T(8,128)(2,1)S(1)}, bf16[256,128]{1,0:T(8,128)(2,1)S(1)}, u32[]{:S(2)}, u32[]{:S(2)}) %collective-permute-start.13) | collective-permute-done | bytes 65568 | tf_op jit(solution)/shard_map/ppermute | solution.py:332
  33.2 0.2 coarse.1.refs_2_
  33.4 1.0 %collective-permute-done.14.refs_0_ = bf16[256,128]{1,0:T(8,128)(2,1)S(1)} collective-permute-done((bf16[256,128]{1,0:T(8,128)(2,1)S(1)}, bf16[256,128]{1,0:T(8,128)(2,1)S(1)}, u32[]{:S(2)}, u32[]{:S(2)}) %collective-permute-start.14) | collective-permute-done | bytes 65568 | tf_op jit(solution)/shard_map/ppermute | solution.py:323
  34.4 0.4 up.1
  34.8 2.0 %collective-permute-start.20 = (bf16[256,128]{1,0:T(8,128)(2,1)S(1)}, bf16[256,128]{1,0:T(8,128)(2,1)S(1)}, u32[]{:S(2)}, u32[]{:S(2)}) collective-permute-start(bf16[256,128]{1,0:T(8,128)(2,1)S(1)} %get-tuple-element.91), channel_id=1, source_target_pairs={{0,12},{4,8},{8,4},{12,0},{16,28},{20,24},{24,20},{28,16},{1,13},{... | collective-permute-start | bytes 196616 | tf_op jit(solution)/shard_map/ppermute | solution.py:323
  36.8 0.8 %collective-permute-start.18 = (bf16[256,128]{1,0:T(8,128)(2,1)S(1)}, bf16[256,128]{1,0:T(8,128)(2,1)S(1)}, u32[]{:S(2)}, u32[]{:S(2)}) collective-permute-start(bf16[256,128]{1,0:T(8,128)(2,1)S(1)} %get-tuple-element.90.refs_0_), channel_id=1, source_target_pairs={{0,4},{4,0},{8,12},{12,8},{16,20},{20,16},{24,28},{28,24},{1,5},{5... | collective-permute-start | bytes 196616 | tf_op jit(solution)/shard_map/ppermute | solution.py:323
  37.6 0.7 %collective-permute-start.19 = (bf16[256,128]{1,0:T(8,128)(2,1)S(1)}, bf16[256,128]{1,0:T(8,128)(2,1)S(1)}, u32[]{:S(2)}, u32[]{:S(2)}) collective-permute-start(bf16[256,128]{1,0:T(8,128)(2,1)S(1)} %get-tuple-element.91), channel_id=1, source_target_pairs={{0,8},{4,12},{8,0},{12,4},{16,24},{20,28},{24,16},{28,20},{1,9},{5... | collective-permute-start | bytes 196616 | tf_op jit(solution)/shard_map/ppermute | solution.py:323
  38.4 0.8 %output.3.refs_5_ = f32[1,256,512]{2,1,0:T(8,128)} custom-call(bf16[256,128]{1,0:T(8,128)(2,1)S(1)} %get-tuple-element.90.refs_0_, f32[256,512]{1,0:T(8,128)S(1)} %get-tuple-element.86.base.refs_1_.refs_2_, bf16[256,256]{1,0:T(8,128)(2,1)S(1)} %get-tuple-element.92.refs_2_.refs_3_, f32[256,256]{1,0:T(8,128)S(1)} %get-tuple-element.93.refs_3_.refs_4_, ...), custom_call_target="tpu_custom_call" | custom-call | flops 16777216 | bytes 1114112 | tf_op jit(solution)/shard_map/output/pallas_call | solution.py:52
  39.2 0.9 %collective-permute-done.20.refs_0_ = bf16[256,128]{1,0:T(8,128)(2,1)S(1)} collective-permute-done((bf16[256,128]{1,0:T(8,128)(2,1)S(1)}, bf16[256,128]{1,0:T(8,128)(2,1)S(1)}, u32[]{:S(2)}, u32[]{:S(2)}) %collective-permute-start.20) | collective-permute-done | bytes 65568 | tf_op jit(solution)/shard_map/ppermute | solution.py:323
  40.2 0.8 %output.4.refs_6_ = f32[1,256,512]{2,1,0:T(8,128)} custom-call(bf16[256,128]{1,0:T(8,128)(2,1)S(1)} %collective-permute-done.20.refs_0_, f32[256,512]{1,0:T(8,128)S(1)} %get-tuple-element.86.base.refs_1_.refs_2_, bf16[256,256]{1,0:T(8,128)(2,1)S(1)} %get-tuple-element.92.refs_2_.refs_3_, ...), custom_call_target="tpu_custom_call", output_to_operand_aliasing={{}: (5, {})} | custom-call | flops 16777216 | bytes 1638400 | tf_op jit(solution)/shard_map/output/pallas_call | solution.py:52
  41.0 0.4 collective-permute-done.18.refs_0_
  41.4 0.5 %collective-permute-done.19.refs_1_ = bf16[256,128]{1,0:T(8,128)(2,1)S(1)} collective-permute-done((bf16[256,128]{1,0:T(8,128)(2,1)S(1)}, bf16[256,128]{1,0:T(8,128)(2,1)S(1)}, u32[]{:S(2)}, u32[]{:S(2)}) %collective-permute-start.19) | collective-permute-done | bytes 65568 | tf_op jit(solution)/shard_map/ppermute | solution.py:323
  41.9 0.9 %output.5 = f32[1,256,512]{2,1,0:T(8,128)} custom-call(bf16[256,128]{1,0:T(8,128)(2,1)S(1)} %collective-permute-done.18.refs_0_, bf16[256,128]{1,0:T(8,128)(2,1)S(1)} %collective-permute-done.19.refs_1_, f32[256,512]{1,0:T(8,128)S(1)} %get-tuple-element.86.base.refs_1_.refs_2_, ...), custom_call_target="tpu_custom_call", output_to_operand_aliasing={{}: (6, {})} | custom-call | flops 33554432 | bytes 1703936 | tf_op jit(solution)/shard_map/output/pallas_call | solution.py:52
  (30 shorter events, 0.3 us)
Async XLA Ops:
  0.0 4.4 %copy-start = (bf16[3,1,4,5,64,64]{5,4,3,2,1,0:T(8,128)(2,1)S(1)}, bf16[3,1,4,5,64,64]{5,4,3,2,1,0:T(8,128)(2,1)}, u32[]{:S(2)}) copy-start(bf16[3,1,4,5,64,64]{5,4,3,2,1,0:T(8,128)(2,1)} %blocks.7) | copy-start | bytes 1474564
  0.0 4.4 %copy-start.3 = (f32[1,256,512]{2,1,0:T(8,128)S(1)}, f32[1,256,512]{2,1,0:T(8,128)}, u32[]{:S(2)}) copy-start(f32[1,256,512]{2,1,0:T(8,128)} %rhs.3) | copy-start | bytes 1572868
  1.3 4.8 %collective-permute-start.1 = (bf16[64,512]{1,0:T(8,128)(2,1)S(1)}, bf16[64,512]{1,0:T(8,128)(2,1)S(1)}, u32[]{:S(2)}, u32[]{:S(2)}) collective-permute-start(bf16[64,512]{1,0:T(8,128)(2,1)S(1)} %get-tuple-element.54), channel_id=1, source_target_pairs={{0,1},{1,0},{2,3},{3,2},{4,5},{5,4},{6,7},{7,6},{8,9},{9,8},{10,11... | collective-permute-start | bytes 196616 | tf_op jit(solution)/shard_map/ppermute | solution.py:323
  1.8 4.3 %collective-permute-start = (bf16[64,256]{1,0:T(8,128)(2,1)S(1)}, bf16[64,256]{1,0:T(8,128)(2,1)S(1)}, u32[]{:S(2)}, u32[]{:S(2)}) collective-permute-start(bf16[64,256]{1,0:T(8,128)(2,1)S(1)} %get-tuple-element.50._), channel_id=1, source_target_pairs={{0,3},{1,2},{2,1},{3,0},{4,7},{5,6},{6,5},{7,4},{8,11},{9,10},{10,... | collective-permute-start | bytes 98312 | tf_op jit(solution)/shard_map/ppermute | solution.py:338
  4.4 3.6 %collective-permute-start.5 = (bf16[64,256]{1,0:T(8,128)(2,1)S(1)}, bf16[64,256]{1,0:T(8,128)(2,1)S(1)}, u32[]{:S(2)}, u32[]{:S(2)}) collective-permute-start(bf16[64,256]{1,0:T(8,128)(2,1)S(1)} %get-tuple-element.65), channel_id=1, source_target_pairs={{0,3},{1,2},{2,1},{3,0},{4,7},{5,6},{6,5},{7,4},{8,11},{9,10},{10,... | collective-permute-start | bytes 98312 | tf_op jit(solution)/shard_map/ppermute | solution.py:338
  6.1 3.5 %copy-start.1 = (bf16[3,1,4,3,64,64]{5,4,3,2,1,0:T(8,128)(2,1)S(1)}, bf16[3,1,4,3,64,64]{5,4,3,2,1,0:T(8,128)(2,1)}, u32[]{:S(2)}) copy-start(bf16[3,1,4,3,64,64]{5,4,3,2,1,0:T(8,128)(2,1)} %rblocks.5) | copy-start | bytes 884740
  6.3 4.5 %collective-permute-start.2 = (bf16[256,128]{1,0:T(8,128)(2,1)S(1)}, bf16[256,128]{1,0:T(8,128)(2,1)S(1)}, u32[]{:S(2)}, u32[]{:S(2)}) collective-permute-start(bf16[256,128]{1,0:T(8,128)(2,1)S(1)} %get-tuple-element.55._), channel_id=1, source_target_pairs={{0,4},{4,0},{8,12},{12,8},{16,20},{20,16},{24,28},{28,24},{1,5},{5... | collective-permute-start | bytes 196616 | tf_op jit(solution)/shard_map/ppermute | solution.py:323
  8.0 1.6 %copy-start.5 = (s32[3,1,4,3]{2,1,3,0:T(1,128)S(1)}, s32[3,1,4,3]{2,1,3,0:T(1,128)}, u32[]{:S(2)}) copy-start(s32[3,1,4,3]{2,1,3,0:T(1,128)} %param.11) | copy-start | bytes 436
  8.2 5.0 %collective-permute-start.6 = (bf16[256,128]{1,0:T(8,128)(2,1)S(1)}, bf16[256,128]{1,0:T(8,128)(2,1)S(1)}, u32[]{:S(2)}, u32[]{:S(2)}) collective-permute-start(bf16[256,128]{1,0:T(8,128)(2,1)S(1)} %get-tuple-element.67), channel_id=1, source_target_pairs={{0,4},{4,0},{8,12},{12,8},{16,20},{20,16},{24,28},{28,24},{1,5},{5... | collective-permute-start | bytes 196616 | tf_op jit(solution)/shard_map/ppermute | solution.py:323
  11.0 3.9 %collective-permute-start.3 = (bf16[64,128]{1,0:T(8,128)(2,1)S(1)}, bf16[64,128]{1,0:T(8,128)(2,1)S(1)}, u32[]{:S(2)}, u32[]{:S(2)}) collective-permute-start(bf16[64,128]{1,0:T(8,128)(2,1)S(1)} %get-tuple-element.63), channel_id=1, source_target_pairs={{0,3},{1,2},{2,1},{3,0},{4,7},{5,6},{6,5},{7,4},{8,11},{9,10},{10,... | collective-permute-start | bytes 49160 | tf_op jit(solution)/shard_map/ppermute | solution.py:338
  12.6 2.3 %collective-permute-start.4 = (bf16[64,128]{1,0:T(8,128)(2,1)S(1)}, bf16[64,128]{1,0:T(8,128)(2,1)S(1)}, u32[]{:S(2)}, u32[]{:S(2)}) collective-permute-start(bf16[64,128]{1,0:T(8,128)(2,1)S(1)} %get-tuple-element.64), channel_id=1, source_target_pairs={{0,1},{1,0},{2,3},{3,2},{4,5},{5,4},{6,7},{7,6},{8,9},{9,8},{10,11... | collective-permute-start | bytes 49160 | tf_op jit(solution)/shard_map/ppermute | solution.py:323
  13.4 4.7 %collective-permute-start.7 = (bf16[64,128]{1,0:T(8,128)(2,1)S(1)}, bf16[64,128]{1,0:T(8,128)(2,1)S(1)}, u32[]{:S(2)}, u32[]{:S(2)}) collective-permute-start(bf16[64,128]{1,0:T(8,128)(2,1)S(1)} %get-tuple-element.72), channel_id=1, source_target_pairs={{0,3},{1,2},{2,1},{3,0},{4,7},{5,6},{6,5},{7,4},{8,11},{9,10},{10,... | collective-permute-start | bytes 49160 | tf_op jit(solution)/shard_map/ppermute | solution.py:338
  14.2 3.9 %collective-permute-start.8 = (bf16[64,128]{1,0:T(8,128)(2,1)S(1)}, bf16[64,128]{1,0:T(8,128)(2,1)S(1)}, u32[]{:S(2)}, u32[]{:S(2)}) collective-permute-start(bf16[64,128]{1,0:T(8,128)(2,1)S(1)} %get-tuple-element.73), channel_id=1, source_target_pairs={{0,1},{1,0},{2,3},{3,2},{4,5},{5,4},{6,7},{7,6},{8,9},{9,8},{10,11... | collective-permute-start | bytes 49160 | tf_op jit(solution)/shard_map/ppermute | solution.py:323
  15.1 4.3 %collective-permute-start.9 = (bf16[256,128]{1,0:T(8,128)(2,1)S(1)}, bf16[256,128]{1,0:T(8,128)(2,1)S(1)}, u32[]{:S(2)}, u32[]{:S(2)}) collective-permute-start(bf16[256,128]{1,0:T(8,128)(2,1)S(1)} %get-tuple-element.69._), channel_id=1, source_target_pairs={{0,8},{4,12},{8,0},{12,4},{16,24},{20,28},{24,16},{28,20},{1,9},{5... | collective-permute-start | bytes 196616 | tf_op jit(solution)/shard_map/ppermute | solution.py:323
  16.8 11.0 %collective-permute-start.12 = (bf16[256,128]{1,0:T(8,128)(2,1)S(1)}, bf16[256,128]{1,0:T(8,128)(2,1)S(1)}, u32[]{:S(2)}, u32[]{:S(2)}) collective-permute-start(bf16[256,128]{1,0:T(8,128)(2,1)S(1)} %get-tuple-element.83.near), channel_id=1, source_target_pairs={{0,4},{4,0},{8,12},{12,8},{16,20},{20,16},{24,28},{28,24},{1,5},{5... | collective-permute-start | bytes 196616 | tf_op jit(solution)/shard_map/ppermute | solution.py:323
  19.7 3.2 %collective-permute-start.10 = (bf16[64,128]{1,0:T(8,128)(2,1)S(1)}, bf16[64,128]{1,0:T(8,128)(2,1)S(1)}, u32[]{:S(2)}, u32[]{:S(2)}) collective-permute-start(bf16[64,128]{1,0:T(8,128)(2,1)S(1)} %get-tuple-element.80), channel_id=1, source_target_pairs={{0,3},{1,2},{2,1},{3,0},{4,7},{5,6},{6,5},{7,4},{8,11},{9,10},{10,... | collective-permute-start | bytes 49160 | tf_op jit(solution)/shard_map/ppermute | solution.py:338
  20.6 2.3 %collective-permute-start.11 = (bf16[64,128]{1,0:T(8,128)(2,1)S(1)}, bf16[64,128]{1,0:T(8,128)(2,1)S(1)}, u32[]{:S(2)}, u32[]{:S(2)}) collective-permute-start(bf16[64,128]{1,0:T(8,128)(2,1)S(1)} %get-tuple-element.81), channel_id=1, source_target_pairs={{0,1},{1,0},{2,3},{3,2},{4,5},{5,4},{6,7},{7,6},{8,9},{9,8},{10,11... | collective-permute-start | bytes 49160 | tf_op jit(solution)/shard_map/ppermute | solution.py:323
  22.2 5.6 %copy-start.2 = (bf16[3,1,4,2,64,64]{5,4,3,2,1,0:T(8,128)(2,1)S(1)}, bf16[3,1,4,2,64,64]{5,4,3,2,1,0:T(8,128)(2,1)}, u32[]{:S(2)}) copy-start(bf16[3,1,4,2,64,64]{5,4,3,2,1,0:T(8,128)(2,1)} %blocks_1.1) | copy-start | bytes 589828
  23.3 7.6 %collective-permute-start.15 = (bf16[256,128]{1,0:T(8,128)(2,1)S(1)}, bf16[256,128]{1,0:T(8,128)(2,1)S(1)}, u32[]{:S(2)}, u32[]{:S(2)}) collective-permute-start(bf16[256,128]{1,0:T(8,128)(2,1)S(1)} %get-tuple-element.82.refs_0_._.own), channel_id=1, source_target_pairs={{0,18},{1,19},{2,16},{3,17},{4,22},{5,23},{6,20},{7,21},{8,26},{9,... | collective-permute-start | bytes 196616 | tf_op jit(solution)/shard_map/ppermute | solution.py:332
  27.1 4.5 %collective-permute-start.16 = (bf16[256,128]{1,0:T(8,128)(2,1)S(1)}, bf16[256,128]{1,0:T(8,128)(2,1)S(1)}, u32[]{:S(2)}, u32[]{:S(2)}) collective-permute-start(bf16[256,128]{1,0:T(8,128)(2,1)S(1)} %get-tuple-element.82.refs_0_._.own), channel_id=1, source_target_pairs={{0,2},{1,3},{2,0},{3,1},{4,6},{5,7},{6,4},{7,5},{8,10},{9,11},{10,... | collective-permute-start | bytes 196616 | tf_op jit(solution)/shard_map/ppermute | solution.py:323
  27.4 5.6 %collective-permute-start.13 = (bf16[256,128]{1,0:T(8,128)(2,1)S(1)}, bf16[256,128]{1,0:T(8,128)(2,1)S(1)}, u32[]{:S(2)}, u32[]{:S(2)}) collective-permute-start(bf16[256,128]{1,0:T(8,128)(2,1)S(1)} %get-tuple-element.82.refs_0_._.own), channel_id=1, source_target_pairs={{0,16},{1,17},{2,18},{3,19},{4,20},{5,21},{6,22},{7,23},{8,24},{9,... | collective-permute-start | bytes 196616 | tf_op jit(solution)/shard_map/ppermute | solution.py:332
  27.8 0.7 %copy-start.6 = (s32[3,1,4,2]{2,3,1,0:T(2,128)S(1)}, s32[3,1,4,2]{2,3,1,0:T(2,128)}, u32[]{:S(2)}) copy-start(s32[3,1,4,2]{2,3,1,0:T(2,128)} %param.13) | copy-start | bytes 292
  28.5 1.2 %copy-start.4 = (bf16[256,1024]{1,0:T(8,128)(2,1)S(1)}, bf16[256,1024]{1,0:T(8,128)(2,1)}, u32[]{:S(2)}) copy-start(bf16[256,1024]{1,0:T(8,128)(2,1)} %refs_3_.1) | copy-start | bytes 1572868
  31.6 1.8 %collective-permute-start.17 = (bf16[256,128]{1,0:T(8,128)(2,1)S(1)}, bf16[256,128]{1,0:T(8,128)(2,1)S(1)}, u32[]{:S(2)}, u32[]{:S(2)}) collective-permute-start(bf16[256,128]{1,0:T(8,128)(2,1)S(1)} %share_sum.3.refs_0_), channel_id=1, source_target_pairs={{0,1},{1,0},{2,3},{3,2},{4,5},{5,4},{6,7},{7,6},{8,9},{9,8},{10,11... | collective-permute-start | bytes 196616 | tf_op jit(solution)/shard_map/ppermute | solution.py:323
  33.1 1.3 %collective-permute-start.14 = (bf16[256,128]{1,0:T(8,128)(2,1)S(1)}, bf16[256,128]{1,0:T(8,128)(2,1)S(1)}, u32[]{:S(2)}, u32[]{:S(2)}) collective-permute-start(bf16[256,128]{1,0:T(8,128)(2,1)S(1)} %share_sum.2.refs_1_), channel_id=1, source_target_pairs={{0,1},{1,0},{2,3},{3,2},{4,5},{5,4},{6,7},{7,6},{8,9},{9,8},{10,11... | collective-permute-start | bytes 196616 | tf_op jit(solution)/shard_map/ppermute | solution.py:323
  34.8 5.3 %collective-permute-start.20 = (bf16[256,128]{1,0:T(8,128)(2,1)S(1)}, bf16[256,128]{1,0:T(8,128)(2,1)S(1)}, u32[]{:S(2)}, u32[]{:S(2)}) collective-permute-start(bf16[256,128]{1,0:T(8,128)(2,1)S(1)} %get-tuple-element.91), channel_id=1, source_target_pairs={{0,12},{4,8},{8,4},{12,0},{16,28},{20,24},{24,20},{28,16},{1,13},{... | collective-permute-start | bytes 196616 | tf_op jit(solution)/shard_map/ppermute | solution.py:323
  36.8 4.6 %collective-permute-start.18 = (bf16[256,128]{1,0:T(8,128)(2,1)S(1)}, bf16[256,128]{1,0:T(8,128)(2,1)S(1)}, u32[]{:S(2)}, u32[]{:S(2)}) collective-permute-start(bf16[256,128]{1,0:T(8,128)(2,1)S(1)} %get-tuple-element.90.refs_0_), channel_id=1, source_target_pairs={{0,4},{4,0},{8,12},{12,8},{16,20},{20,16},{24,28},{28,24},{1,5},{5... | collective-permute-start | bytes 196616 | tf_op jit(solution)/shard_map/ppermute | solution.py:323
  37.6 4.3 %collective-permute-start.19 = (bf16[256,128]{1,0:T(8,128)(2,1)S(1)}, bf16[256,128]{1,0:T(8,128)(2,1)S(1)}, u32[]{:S(2)}, u32[]{:S(2)}) collective-permute-start(bf16[256,128]{1,0:T(8,128)(2,1)S(1)} %get-tuple-element.91), channel_id=1, source_target_pairs={{0,8},{4,12},{8,0},{12,4},{16,24},{20,28},{24,16},{28,20},{1,9},{5... | collective-permute-start | bytes 196616 | tf_op jit(solution)/shard_map/ppermute | solution.py:323

commit v14 on v13

--- a/solution.py
+++ b/solution.py
@@ -488,7 +488,7 @@
     for group in (
         [(near, place_of(0, 0), None)],
         [(diagonal, place_of(1, 1), 1)],
-        [(far, place_of(1, 0), None), (other, place_of(0, 1), 0)],
+        [(other, place_of(0, 1), 0), (far, place_of(1, 0), None)],
     ):
         values, places, slots = zip(*group)
         operands = [*values, base, lower, total, both]

time: 43 us -> 42.9 us (level)
  transfers between devices with their start and end apart: 21 -> 21, of which waited for: 9 -> 8; matrix products, arithmetic and copies ran while one was open for 0% -> 0% of each run, Pallas kernels for 24% -> 24%
where the time goes in v14:
time: 42.9 us; the launch traced here: 42.8 us
  starting transfers between devices  22.9 us (53%)
  Pallas kernels  12.8 us (30%)
  waiting for transfers between devices  6.12 us (14%)
  local copies, waits for them, and re-layouts  0.71 us (2%)
    ppermute x14, starting transfers between devices, exchange(): return lax.ppermute(value, axis, [(i, i ^ bit) for i in range(count)])  12.9 us
    pallas_call x22, Pallas kernels, run(): pl.pallas_call(body, grid=(1,) if windows else (), out_shape=[out_space(o...  12.8 us
    ppermute x5, starting transfers between devices, swap_outer(): return lax.ppermute(outer, 'narrow', gaps)  6.01 us
    ppermute x2, starting transfers between devices, exchange_both(): return lax.ppermute(value, ('wide', 'narrow'), pairs)  4.06 us
    ppermute x14, waiting for transfers between devices, exchange(): return lax.ppermute(value, axis, [(i, i ^ bit) for i in range(count)])  3.38 us
    ppermute x2, waiting for transfers between devices, exchange_both(): return lax.ppermute(value, ('wide', 'narrow'), pairs)  1.57 us
    ppermute x5, waiting for transfers between devices, swap_outer(): return lax.ppermute(outer, 'narrow', gaps)  1.16 us
  transfers between devices with their start and end apart: 21, of which 8 were waited for; matrix products, arithmetic and copies ran while one was open for 0% of the time, Pallas kernels for 24%

profile of v14, /device:TPU:0, one launch (start us, length us, event | category | flops | bytes accessed | tf_op | source)
XLA Modules:
  0.0 42.8 jit_solution(14797644054607576935)
XLA Ops:
  0.0 1.3 %start.1 = (s32[3,1,4,5]{3,2,1,0:T(4,128)S(1)}, bf16[64,512]{1,0:T(8,128)(2,1)S(1)}, bf16[64,256]{1,0:T(8,128)(2,1)S(1)}, bf16[64,256]{1,0:T(8,128)(2,1)S(1)}) custom-call(f32[1,256,512]{2,1,0:T(8,128)} %rhs.3, bf16[3,1,4,5,64,64]{5,4,3,2,1,0:T(8,128)(2,1)} %blocks.7, s32[3,1,4,5]{3,2,1,0:T(4,128)} %refs_0_.1), custom_call_target="tpu_custom_call" | custom-call | bytes 1016048 | tf_op jit(solution)/shard_map/start/pallas_call | solution.py:52
  1.3 0.5 %collective-permute-start.1 = (bf16[64,512]{1,0:T(8,128)(2,1)S(1)}, bf16[64,512]{1,0:T(8,128)(2,1)S(1)}, u32[]{:S(2)}, u32[]{:S(2)}) collective-permute-start(bf16[64,512]{1,0:T(8,128)(2,1)S(1)} %get-tuple-element.54), channel_id=1, source_target_pairs={{0,1},{1,0},{2,3},{3,2},{4,5},{5,4},{6,7},{7,6},{8,9},{9,8},{10,11... | collective-permute-start | bytes 196616 | tf_op jit(solution)/shard_map/ppermute | solution.py:323
  1.8 2.6 %collective-permute-start = (bf16[64,256]{1,0:T(8,128)(2,1)S(1)}, bf16[64,256]{1,0:T(8,128)(2,1)S(1)}, u32[]{:S(2)}, u32[]{:S(2)}) collective-permute-start(bf16[64,256]{1,0:T(8,128)(2,1)S(1)} %get-tuple-element.50._), channel_id=1, source_target_pairs={{0,3},{1,2},{2,1},{3,0},{4,7},{5,6},{6,5},{7,4},{8,11},{9,10},{10,... | collective-permute-start | bytes 98312 | tf_op jit(solution)/shard_map/ppermute | solution.py:338
  4.5 1.1 %first_local.1 = (f32[256,512]{1,0:T(8,128)S(1)}, f32[256,512]{1,0:T(8,128)S(1)}, bf16[256,256]{1,0:T(8,128)(2,1)S(1)}, bf16[256,128]{1,0:T(8,128)(2,1)S(1)}, f32[256,1]{1,0:T(8,128)S(1)}) custom-call(f32[1,256,512]{2,1,0:T(8,128)S(1)} %copy-done.3, bf16[64,256]{1,0:T(8,128)(2,1)S(1)} %get-tuple-element.50._, s32[3,1,4,5]{3,2,1,0:T(4,128)S(1)} %get-tuple-element.51.cols, ...), custom_call_target="tpu_custom_call" | custom-call | flops 67108864 | bytes 1048816 | tf_op jit(solution)/shard_map/first_local/pallas_call | solution.py:52
  5.6 0.5 %collective-permute-done.outer = bf16[64,256]{1,0:T(8,128)(2,1)S(1)} collective-permute-done((bf16[64,256]{1,0:T(8,128)(2,1)S(1)}, bf16[64,256]{1,0:T(8,128)(2,1)S(1)}, u32[]{:S(2)}, u32[]{:S(2)}) %collective-permute-start) | collective-permute-done | bytes 32800 | tf_op jit(solution)/shard_map/ppermute | solution.py:338
  6.1 0.2 first_residual.2
  6.3 1.7 %collective-permute-start.2 = (bf16[256,128]{1,0:T(8,128)(2,1)S(1)}, bf16[256,128]{1,0:T(8,128)(2,1)S(1)}, u32[]{:S(2)}, u32[]{:S(2)}) collective-permute-start(bf16[256,128]{1,0:T(8,128)(2,1)S(1)} %get-tuple-element.55._), channel_id=1, source_target_pairs={{0,4},{4,0},{8,12},{12,8},{16,20},{20,16},{24,28},{28,24},{1,5},{5... | collective-permute-start | bytes 196616 | tf_op jit(solution)/shard_map/ppermute | solution.py:323
  8.0 0.2 first_residual.3
  8.2 1.4 %collective-permute-start.6 = (bf16[256,128]{1,0:T(8,128)(2,1)S(1)}, bf16[256,128]{1,0:T(8,128)(2,1)S(1)}, u32[]{:S(2)}, u32[]{:S(2)}) collective-permute-start(bf16[256,128]{1,0:T(8,128)(2,1)S(1)} %get-tuple-element.67), channel_id=1, source_target_pairs={{0,4},{4,0},{8,12},{12,8},{16,20},{20,16},{24,28},{28,24},{1,5},{5... | collective-permute-start | bytes 196616 | tf_op jit(solution)/shard_map/ppermute | solution.py:323
  9.6 1.1 %operators.2 = (bf16[256,512]{1,0:T(8,128)(2,1)S(1)}, bf16[256,256]{1,0:T(8,128)(2,1)S(1)}, bf16[256,128]{1,0:T(8,128)(2,1)S(1)}, f32[256,1]{1,0:T(8,128)S(1)}) custom-call(bf16[256,128]{1,0:T(8,128)(2,1)S(1)} %get-tuple-element.55._, s32[3,3,1,4]{3,2,1,0:T(1,128)S(1)} %bitcast.2, bf16[3,1,4,3,64,64]{5,4,3,2,1,0:T(8,128)(2,1)S(1)} %copy-done.1, ...), custom_call_target="tpu_custom_call" | custom-call | bytes 852352 | tf_op jit(solution)/shard_map/operators/pallas_call | solution.py:52
  10.8 0.2 join.3
  11.0 1.6 %collective-permute-start.3 = (bf16[64,128]{1,0:T(8,128)(2,1)S(1)}, bf16[64,128]{1,0:T(8,128)(2,1)S(1)}, u32[]{:S(2)}, u32[]{:S(2)}) collective-permute-start(bf16[64,128]{1,0:T(8,128)(2,1)S(1)} %get-tuple-element.63), channel_id=1, source_target_pairs={{0,3},{1,2},{2,1},{3,0},{4,7},{5,6},{6,5},{7,4},{8,11},{9,10},{10,... | collective-permute-start | bytes 49160 | tf_op jit(solution)/shard_map/ppermute | solution.py:338
  12.6 0.6 %collective-permute-start.4 = (bf16[64,128]{1,0:T(8,128)(2,1)S(1)}, bf16[64,128]{1,0:T(8,128)(2,1)S(1)}, u32[]{:S(2)}, u32[]{:S(2)}) collective-permute-start(bf16[64,128]{1,0:T(8,128)(2,1)S(1)} %get-tuple-element.64), channel_id=1, source_target_pairs={{0,1},{1,0},{2,3},{3,2},{4,5},{5,4},{6,7},{7,6},{8,9},{9,8},{10,11... | collective-permute-start | bytes 49160 | tf_op jit(solution)/shard_map/ppermute | solution.py:323
  13.2 0.2 join.4
  13.4 0.8 %collective-permute-start.7 = (bf16[64,128]{1,0:T(8,128)(2,1)S(1)}, bf16[64,128]{1,0:T(8,128)(2,1)S(1)}, u32[]{:S(2)}, u32[]{:S(2)}) collective-permute-start(bf16[64,128]{1,0:T(8,128)(2,1)S(1)} %get-tuple-element.72), channel_id=1, source_target_pairs={{0,3},{1,2},{2,1},{3,0},{4,7},{5,6},{6,5},{7,4},{8,11},{9,10},{10,... | collective-permute-start | bytes 49160 | tf_op jit(solution)/shard_map/ppermute | solution.py:338
  14.2 0.6 %collective-permute-start.8 = (bf16[64,128]{1,0:T(8,128)(2,1)S(1)}, bf16[64,128]{1,0:T(8,128)(2,1)S(1)}, u32[]{:S(2)}, u32[]{:S(2)}) collective-permute-start(bf16[64,128]{1,0:T(8,128)(2,1)S(1)} %get-tuple-element.73), channel_id=1, source_target_pairs={{0,1},{1,0},{2,3},{3,2},{4,5},{5,4},{6,7},{7,6},{8,9},{9,8},{10,11... | collective-permute-start | bytes 49160 | tf_op jit(solution)/shard_map/ppermute | solution.py:323
  14.9 0.2 residual.3
  15.1 1.6 %collective-permute-start.9 = (bf16[256,128]{1,0:T(8,128)(2,1)S(1)}, bf16[256,128]{1,0:T(8,128)(2,1)S(1)}, u32[]{:S(2)}, u32[]{:S(2)}) collective-permute-start(bf16[256,128]{1,0:T(8,128)(2,1)S(1)} %get-tuple-element.69._), channel_id=1, source_target_pairs={{0,8},{4,12},{8,0},{12,4},{16,24},{20,28},{24,16},{28,20},{1,9},{5... | collective-permute-start | bytes 196616 | tf_op jit(solution)/shard_map/ppermute | solution.py:323
  16.8 1.3 %collective-permute-start.12 = (bf16[256,128]{1,0:T(8,128)(2,1)S(1)}, bf16[256,128]{1,0:T(8,128)(2,1)S(1)}, u32[]{:S(2)}, u32[]{:S(2)}) collective-permute-start(bf16[256,128]{1,0:T(8,128)(2,1)S(1)} %get-tuple-element.83.near), channel_id=1, source_target_pairs={{0,4},{4,0},{8,12},{12,8},{16,20},{20,16},{24,28},{28,24},{1,5},{5... | collective-permute-start | bytes 196616 | tf_op jit(solution)/shard_map/ppermute | solution.py:323
  18.1 0.2 residual.4
  18.3 1.1 %operators.3 = (bf16[256,512]{1,0:T(8,128)(2,1)S(1)}, bf16[256,256]{1,0:T(8,128)(2,1)S(1)}, bf16[256,128]{1,0:T(8,128)(2,1)S(1)}, f32[256,1]{1,0:T(8,128)S(1)}) custom-call(bf16[256,128]{1,0:T(8,128)(2,1)S(1)} %get-tuple-element.69._, s32[3,3,1,4]{3,2,1,0:T(1,128)S(1)} %bitcast.3, bf16[3,1,4,3,64,64]{5,4,3,2,1,0:T(8,128)(2,1)S(1)} %copy-done.1, ...), custom_call_target="tpu_custom_call" | custom-call | bytes 852352 | tf_op jit(solution)/shard_map/operators/pallas_call | solution.py:52
  19.4 0.2 join.5
  19.7 0.9 %collective-permute-start.10 = (bf16[64,128]{1,0:T(8,128)(2,1)S(1)}, bf16[64,128]{1,0:T(8,128)(2,1)S(1)}, u32[]{:S(2)}, u32[]{:S(2)}) collective-permute-start(bf16[64,128]{1,0:T(8,128)(2,1)S(1)} %get-tuple-element.80), channel_id=1, source_target_pairs={{0,3},{1,2},{2,1},{3,0},{4,7},{5,6},{6,5},{7,4},{8,11},{9,10},{10,... | collective-permute-start | bytes 49160 | tf_op jit(solution)/shard_map/ppermute | solution.py:338
  20.6 0.9 %collective-permute-start.11 = (bf16[64,128]{1,0:T(8,128)(2,1)S(1)}, bf16[64,128]{1,0:T(8,128)(2,1)S(1)}, u32[]{:S(2)}, u32[]{:S(2)}) collective-permute-start(bf16[64,128]{1,0:T(8,128)(2,1)S(1)} %get-tuple-element.81), channel_id=1, source_target_pairs={{0,1},{1,0},{2,3},{3,2},{4,5},{5,4},{6,7},{7,6},{8,9},{9,8},{10,11... | collective-permute-start | bytes 49160 | tf_op jit(solution)/shard_map/ppermute | solution.py:323
  21.5 0.7 %share.1 = bf16[256,256]{1,0:T(8,128)(2,1)S(1)} custom-call(bf16[256,128]{1,0:T(8,128)(2,1)S(1)} %get-tuple-element.77._.smoothed, s32[3,3,1,4]{3,2,1,0:T(1,128)S(1)} %bitcast.4, bf16[3,1,4,3,64,64]{5,4,3,2,1,0:T(8,128)(2,1)S(1)} %copy-done.1), custom_call_target="tpu_custom_call" | custom-call | bytes 360592 | tf_op jit(solution)/shard_map/share/pallas_call | solution.py:52
  22.2 0.7 %collective-permute-done.10.outer = bf16[64,128]{1,0:T(8,128)(2,1)S(1)} collective-permute-done((bf16[64,128]{1,0:T(8,128)(2,1)S(1)}, bf16[64,128]{1,0:T(8,128)(2,1)S(1)}, u32[]{:S(2)}, u32[]{:S(2)}) %collective-permute-start.10) | collective-permute-done | bytes 16416 | tf_op jit(solution)/shard_map/ppermute | solution.py:338
  22.9 0.4 residual.5
  23.3 3.7 %collective-permute-start.15 = (bf16[256,128]{1,0:T(8,128)(2,1)S(1)}, bf16[256,128]{1,0:T(8,128)(2,1)S(1)}, u32[]{:S(2)}, u32[]{:S(2)}) collective-permute-start(bf16[256,128]{1,0:T(8,128)(2,1)S(1)} %get-tuple-element.82.refs_0_._.own), channel_id=1, source_target_pairs={{0,18},{1,19},{2,16},{3,17},{4,22},{5,23},{6,20},{7,21},{8,26},{9,... | collective-permute-start | bytes 196616 | tf_op jit(solution)/shard_map/ppermute | solution.py:332
  27.1 0.4 collective-permute-start.16
  27.4 0.3 collective-permute-start.13
  27.8 0.7 %copy-done.6 = s32[3,1,4,2]{2,3,1,0:T(2,128)S(1)} copy-done((s32[3,1,4,2]{2,3,1,0:T(2,128)S(1)}, s32[3,1,4,2]{2,3,1,0:T(2,128)}, u32[]{:S(2)}) %copy-start.6) | copy-done | bytes 120
  28.5 1.2 %fine_operators.1 = (bf16[256,256]{1,0:T(8,128)(2,1)S(1)}, bf16[256,256]{1,0:T(8,128)(2,1)S(1)}, bf16[256,256]{1,0:T(8,128)(2,1)S(1)}, f32[256,256]{1,0:T(8,128)S(1)}) custom-call(bf16[256,128]{1,0:T(8,128)(2,1)S(1)} %get-tuple-element.82.refs_0_._.own, s32[3,1,2,4]{3,2,1,0:T(2,128)S(1)} %bitcast.5, bf16[3,1,4,2,64,64]{5,4,3,2,1,0:T(8,128)(2,1)S(1)} %copy-done.2, ...), custom_call_target="tpu_custom_call" | custom-call | flops 134217728 | bytes 1378400 | tf_op jit(solution)/shard_map/fine_operators/pallas_call | solution.py:52
  29.7 1.1 %coarse_operators.1.refs_0_.inverse = bf16[256,1024]{1,0:T(8,128)(2,1)S(1)} custom-call(bf16[256,128]{1,0:T(8,128)(2,1)S(1)} %get-tuple-element.82.refs_0_._.own, bf16[256,128]{1,0:T(8,128)(2,1)S(1)} %collective-permute-done.12.refs_1_.far, s32[3,1,2,4]{3,2,1,0:T(2,128)S(1)} %bitcast.6, bf16[256,1024]{1,0:T(8,128)(2,1)S(1)} %copy-done.4, ...), custom_call_target="tpu_custom_call" | custom-call | flops 201326592 | bytes 984160 | tf_op jit(solution)/shard_map/coarse_operators/pallas_call | solution.py:52
  30.8 0.2 collective-permute-done.15.far
  31.0 0.6 %collective-permute-done.16.own = bf16[256,128]{1,0:T(8,128)(2,1)S(1)} collective-permute-done((bf16[256,128]{1,0:T(8,128)(2,1)S(1)}, bf16[256,128]{1,0:T(8,128)(2,1)S(1)}, u32[]{:S(2)}, u32[]{:S(2)}) %collective-permute-start.16) | collective-permute-done | bytes 65568 | tf_op jit(solution)/shard_map/ppermute | solution.py:323
  31.7 1.4 %collective-permute-done.13.far = bf16[256,128]{1,0:T(8,128)(2,1)S(1)} collective-permute-done((bf16[256,128]{1,0:T(8,128)(2,1)S(1)}, bf16[256,128]{1,0:T(8,128)(2,1)S(1)}, u32[]{:S(2)}, u32[]{:S(2)}) %collective-permute-start.13) | collective-permute-done | bytes 65568 | tf_op jit(solution)/shard_map/ppermute | solution.py:332
  33.1 0.1 collective-permute-start.14
  33.2 0.2 coarse.1.refs_2_
  33.4 1.0 %collective-permute-done.14.refs_0_ = bf16[256,128]{1,0:T(8,128)(2,1)S(1)} collective-permute-done((bf16[256,128]{1,0:T(8,128)(2,1)S(1)}, bf16[256,128]{1,0:T(8,128)(2,1)S(1)}, u32[]{:S(2)}, u32[]{:S(2)}) %collective-permute-start.14) | collective-permute-done | bytes 65568 | tf_op jit(solution)/shard_map/ppermute | solution.py:323
  34.4 0.4 up.1
  34.8 2.0 %collective-permute-start.20 = (bf16[256,128]{1,0:T(8,128)(2,1)S(1)}, bf16[256,128]{1,0:T(8,128)(2,1)S(1)}, u32[]{:S(2)}, u32[]{:S(2)}) collective-permute-start(bf16[256,128]{1,0:T(8,128)(2,1)S(1)} %get-tuple-element.90), channel_id=1, source_target_pairs={{0,12},{4,8},{8,4},{12,0},{16,28},{20,24},{24,20},{28,16},{1,13},{... | collective-permute-start | bytes 196616 | tf_op jit(solution)/shard_map/ppermute | solution.py:323
  36.8 0.8 %collective-permute-start.18 = (bf16[256,128]{1,0:T(8,128)(2,1)S(1)}, bf16[256,128]{1,0:T(8,128)(2,1)S(1)}, u32[]{:S(2)}, u32[]{:S(2)}) collective-permute-start(bf16[256,128]{1,0:T(8,128)(2,1)S(1)} %get-tuple-element.90), channel_id=1, source_target_pairs={{0,8},{4,12},{8,0},{12,4},{16,24},{20,28},{24,16},{28,20},{1,9},{5... | collective-permute-start | bytes 196616 | tf_op jit(solution)/shard_map/ppermute | solution.py:323
  37.6 0.8 %collective-permute-start.19 = (bf16[256,128]{1,0:T(8,128)(2,1)S(1)}, bf16[256,128]{1,0:T(8,128)(2,1)S(1)}, u32[]{:S(2)}, u32[]{:S(2)}) collective-permute-start(bf16[256,128]{1,0:T(8,128)(2,1)S(1)} %get-tuple-element.91.refs_0_), channel_id=1, source_target_pairs={{0,4},{4,0},{8,12},{12,8},{16,20},{20,16},{24,28},{28,24},{1,5},{5... | collective-permute-start | bytes 196616 | tf_op jit(solution)/shard_map/ppermute | solution.py:323
  38.4 0.8 %output.3.refs_5_ = f32[1,256,512]{2,1,0:T(8,128)} custom-call(bf16[256,128]{1,0:T(8,128)(2,1)S(1)} %get-tuple-element.91.refs_0_, f32[256,512]{1,0:T(8,128)S(1)} %get-tuple-element.86.base.refs_1_.refs_2_, bf16[256,256]{1,0:T(8,128)(2,1)S(1)} %get-tuple-element.92.refs_2_.refs_3_, f32[256,256]{1,0:T(8,128)S(1)} %get-tuple-element.93.refs_3_.refs_4_, ...), custom_call_target="tpu_custom_call" | custom-call | flops 16777216 | bytes 1114112 | tf_op jit(solution)/shard_map/output/pallas_call | solution.py:52
  39.2 1.3 %collective-permute-done.20.refs_0_ = bf16[256,128]{1,0:T(8,128)(2,1)S(1)} collective-permute-done((bf16[256,128]{1,0:T(8,128)(2,1)S(1)}, bf16[256,128]{1,0:T(8,128)(2,1)S(1)}, u32[]{:S(2)}, u32[]{:S(2)}) %collective-permute-start.20) | collective-permute-done | bytes 65568 | tf_op jit(solution)/shard_map/ppermute | solution.py:323
  40.6 0.8 %output.4.refs_6_ = f32[1,256,512]{2,1,0:T(8,128)} custom-call(bf16[256,128]{1,0:T(8,128)(2,1)S(1)} %collective-permute-done.20.refs_0_, f32[256,512]{1,0:T(8,128)S(1)} %get-tuple-element.86.base.refs_1_.refs_2_, bf16[256,256]{1,0:T(8,128)(2,1)S(1)} %get-tuple-element.92.refs_2_.refs_3_, ...), custom_call_target="tpu_custom_call", output_to_operand_aliasing={{}: (5, {})} | custom-call | flops 16777216 | bytes 1638400 | tf_op jit(solution)/shard_map/output/pallas_call | solution.py:52
  41.4 0.4 collective-permute-done.19.refs_1_
  41.8 0.9 %output.5 = f32[1,256,512]{2,1,0:T(8,128)} custom-call(bf16[256,128]{1,0:T(8,128)(2,1)S(1)} %collective-permute-done.18.refs_0_, bf16[256,128]{1,0:T(8,128)(2,1)S(1)} %collective-permute-done.19.refs_1_, f32[256,512]{1,0:T(8,128)S(1)} %get-tuple-element.86.base.refs_1_.refs_2_, ...), custom_call_target="tpu_custom_call", output_to_operand_aliasing={{}: (6, {})} | custom-call | flops 33554432 | bytes 1703936 | tf_op jit(solution)/shard_map/output/pallas_call | solution.py:52
  (30 shorter events, 0.2 us)
Async XLA Ops:
  0.0 4.4 %copy-start = (bf16[3,1,4,5,64,64]{5,4,3,2,1,0:T(8,128)(2,1)S(1)}, bf16[3,1,4,5,64,64]{5,4,3,2,1,0:T(8,128)(2,1)}, u32[]{:S(2)}) copy-start(bf16[3,1,4,5,64,64]{5,4,3,2,1,0:T(8,128)(2,1)} %blocks.7) | copy-start | bytes 1474564
  0.0 4.4 %copy-start.3 = (f32[1,256,512]{2,1,0:T(8,128)S(1)}, f32[1,256,512]{2,1,0:T(8,128)}, u32[]{:S(2)}) copy-start(f32[1,256,512]{2,1,0:T(8,128)} %rhs.3) | copy-start | bytes 1572868
  1.3 4.8 %collective-permute-start.1 = (bf16[64,512]{1,0:T(8,128)(2,1)S(1)}, bf16[64,512]{1,0:T(8,128)(2,1)S(1)}, u32[]{:S(2)}, u32[]{:S(2)}) collective-permute-start(bf16[64,512]{1,0:T(8,128)(2,1)S(1)} %get-tuple-element.54), channel_id=1, source_target_pairs={{0,1},{1,0},{2,3},{3,2},{4,5},{5,4},{6,7},{7,6},{8,9},{9,8},{10,11... | collective-permute-start | bytes 196616 | tf_op jit(solution)/shard_map/ppermute | solution.py:323
  1.8 4.3 %collective-permute-start = (bf16[64,256]{1,0:T(8,128)(2,1)S(1)}, bf16[64,256]{1,0:T(8,128)(2,1)S(1)}, u32[]{:S(2)}, u32[]{:S(2)}) collective-permute-start(bf16[64,256]{1,0:T(8,128)(2,1)S(1)} %get-tuple-element.50._), channel_id=1, source_target_pairs={{0,3},{1,2},{2,1},{3,0},{4,7},{5,6},{6,5},{7,4},{8,11},{9,10},{10,... | collective-permute-start | bytes 98312 | tf_op jit(solution)/shard_map/ppermute | solution.py:338
  4.4 3.6 %collective-permute-start.5 = (bf16[64,256]{1,0:T(8,128)(2,1)S(1)}, bf16[64,256]{1,0:T(8,128)(2,1)S(1)}, u32[]{:S(2)}, u32[]{:S(2)}) collective-permute-start(bf16[64,256]{1,0:T(8,128)(2,1)S(1)} %get-tuple-element.65), channel_id=1, source_target_pairs={{0,3},{1,2},{2,1},{3,0},{4,7},{5,6},{6,5},{7,4},{8,11},{9,10},{10,... | collective-permute-start | bytes 98312 | tf_op jit(solution)/shard_map/ppermute | solution.py:338
  6.1 3.5 %copy-start.1 = (bf16[3,1,4,3,64,64]{5,4,3,2,1,0:T(8,128)(2,1)S(1)}, bf16[3,1,4,3,64,64]{5,4,3,2,1,0:T(8,128)(2,1)}, u32[]{:S(2)}) copy-start(bf16[3,1,4,3,64,64]{5,4,3,2,1,0:T(8,128)(2,1)} %rblocks.5) | copy-start | bytes 884740
  6.3 4.5 %collective-permute-start.2 = (bf16[256,128]{1,0:T(8,128)(2,1)S(1)}, bf16[256,128]{1,0:T(8,128)(2,1)S(1)}, u32[]{:S(2)}, u32[]{:S(2)}) collective-permute-start(bf16[256,128]{1,0:T(8,128)(2,1)S(1)} %get-tuple-element.55._), channel_id=1, source_target_pairs={{0,4},{4,0},{8,12},{12,8},{16,20},{20,16},{24,28},{28,24},{1,5},{5... | collective-permute-start | bytes 196616 | tf_op jit(solution)/shard_map/ppermute | solution.py:323
  8.0 1.6 %copy-start.5 = (s32[3,1,4,3]{2,1,3,0:T(1,128)S(1)}, s32[3,1,4,3]{2,1,3,0:T(1,128)}, u32[]{:S(2)}) copy-start(s32[3,1,4,3]{2,1,3,0:T(1,128)} %param.11) | copy-start | bytes 436
  8.2 5.0 %collective-permute-start.6 = (bf16[256,128]{1,0:T(8,128)(2,1)S(1)}, bf16[256,128]{1,0:T(8,128)(2,1)S(1)}, u32[]{:S(2)}, u32[]{:S(2)}) collective-permute-start(bf16[256,128]{1,0:T(8,128)(2,1)S(1)} %get-tuple-element.67), channel_id=1, source_target_pairs={{0,4},{4,0},{8,12},{12,8},{16,20},{20,16},{24,28},{28,24},{1,5},{5... | collective-permute-start | bytes 196616 | tf_op jit(solution)/shard_map/ppermute | solution.py:323
  11.0 3.9 %collective-permute-start.3 = (bf16[64,128]{1,0:T(8,128)(2,1)S(1)}, bf16[64,128]{1,0:T(8,128)(2,1)S(1)}, u32[]{:S(2)}, u32[]{:S(2)}) collective-permute-start(bf16[64,128]{1,0:T(8,128)(2,1)S(1)} %get-tuple-element.63), channel_id=1, source_target_pairs={{0,3},{1,2},{2,1},{3,0},{4,7},{5,6},{6,5},{7,4},{8,11},{9,10},{10,... | collective-permute-start | bytes 49160 | tf_op jit(solution)/shard_map/ppermute | solution.py:338
  12.6 2.3 %collective-permute-start.4 = (bf16[64,128]{1,0:T(8,128)(2,1)S(1)}, bf16[64,128]{1,0:T(8,128)(2,1)S(1)}, u32[]{:S(2)}, u32[]{:S(2)}) collective-permute-start(bf16[64,128]{1,0:T(8,128)(2,1)S(1)} %get-tuple-element.64), channel_id=1, source_target_pairs={{0,1},{1,0},{2,3},{3,2},{4,5},{5,4},{6,7},{7,6},{8,9},{9,8},{10,11... | collective-permute-start | bytes 49160 | tf_op jit(solution)/shard_map/ppermute | solution.py:323
  13.4 4.7 %collective-permute-start.7 = (bf16[64,128]{1,0:T(8,128)(2,1)S(1)}, bf16[64,128]{1,0:T(8,128)(2,1)S(1)}, u32[]{:S(2)}, u32[]{:S(2)}) collective-permute-start(bf16[64,128]{1,0:T(8,128)(2,1)S(1)} %get-tuple-element.72), channel_id=1, source_target_pairs={{0,3},{1,2},{2,1},{3,0},{4,7},{5,6},{6,5},{7,4},{8,11},{9,10},{10,... | collective-permute-start | bytes 49160 | tf_op jit(solution)/shard_map/ppermute | solution.py:338
  14.2 3.9 %collective-permute-start.8 = (bf16[64,128]{1,0:T(8,128)(2,1)S(1)}, bf16[64,128]{1,0:T(8,128)(2,1)S(1)}, u32[]{:S(2)}, u32[]{:S(2)}) collective-permute-start(bf16[64,128]{1,0:T(8,128)(2,1)S(1)} %get-tuple-element.73), channel_id=1, source_target_pairs={{0,1},{1,0},{2,3},{3,2},{4,5},{5,4},{6,7},{7,6},{8,9},{9,8},{10,11... | collective-permute-start | bytes 49160 | tf_op jit(solution)/shard_map/ppermute | solution.py:323
  15.1 4.3 %collective-permute-start.9 = (bf16[256,128]{1,0:T(8,128)(2,1)S(1)}, bf16[256,128]{1,0:T(8,128)(2,1)S(1)}, u32[]{:S(2)}, u32[]{:S(2)}) collective-permute-start(bf16[256,128]{1,0:T(8,128)(2,1)S(1)} %get-tuple-element.69._), channel_id=1, source_target_pairs={{0,8},{4,12},{8,0},{12,4},{16,24},{20,28},{24,16},{28,20},{1,9},{5... | collective-permute-start | bytes 196616 | tf_op jit(solution)/shard_map/ppermute | solution.py:323
  16.8 11.0 %collective-permute-start.12 = (bf16[256,128]{1,0:T(8,128)(2,1)S(1)}, bf16[256,128]{1,0:T(8,128)(2,1)S(1)}, u32[]{:S(2)}, u32[]{:S(2)}) collective-permute-start(bf16[256,128]{1,0:T(8,128)(2,1)S(1)} %get-tuple-element.83.near), channel_id=1, source_target_pairs={{0,4},{4,0},{8,12},{12,8},{16,20},{20,16},{24,28},{28,24},{1,5},{5... | collective-permute-start | bytes 196616 | tf_op jit(solution)/shard_map/ppermute | solution.py:323
  19.7 3.2 %collective-permute-start.10 = (bf16[64,128]{1,0:T(8,128)(2,1)S(1)}, bf16[64,128]{1,0:T(8,128)(2,1)S(1)}, u32[]{:S(2)}, u32[]{:S(2)}) collective-permute-start(bf16[64,128]{1,0:T(8,128)(2,1)S(1)} %get-tuple-element.80), channel_id=1, source_target_pairs={{0,3},{1,2},{2,1},{3,0},{4,7},{5,6},{6,5},{7,4},{8,11},{9,10},{10,... | collective-permute-start | bytes 49160 | tf_op jit(solution)/shard_map/ppermute | solution.py:338
  20.6 2.3 %collective-permute-start.11 = (bf16[64,128]{1,0:T(8,128)(2,1)S(1)}, bf16[64,128]{1,0:T(8,128)(2,1)S(1)}, u32[]{:S(2)}, u32[]{:S(2)}) collective-permute-start(bf16[64,128]{1,0:T(8,128)(2,1)S(1)} %get-tuple-element.81), channel_id=1, source_target_pairs={{0,1},{1,0},{2,3},{3,2},{4,5},{5,4},{6,7},{7,6},{8,9},{9,8},{10,11... | collective-permute-start | bytes 49160 | tf_op jit(solution)/shard_map/ppermute | solution.py:323
  22.2 5.6 %copy-start.2 = (bf16[3,1,4,2,64,64]{5,4,3,2,1,0:T(8,128)(2,1)S(1)}, bf16[3,1,4,2,64,64]{5,4,3,2,1,0:T(8,128)(2,1)}, u32[]{:S(2)}) copy-start(bf16[3,1,4,2,64,64]{5,4,3,2,1,0:T(8,128)(2,1)} %blocks_1.1) | copy-start | bytes 589828
  23.3 7.6 %collective-permute-start.15 = (bf16[256,128]{1,0:T(8,128)(2,1)S(1)}, bf16[256,128]{1,0:T(8,128)(2,1)S(1)}, u32[]{:S(2)}, u32[]{:S(2)}) collective-permute-start(bf16[256,128]{1,0:T(8,128)(2,1)S(1)} %get-tuple-element.82.refs_0_._.own), channel_id=1, source_target_pairs={{0,18},{1,19},{2,16},{3,17},{4,22},{5,23},{6,20},{7,21},{8,26},{9,... | collective-permute-start | bytes 196616 | tf_op jit(solution)/shard_map/ppermute | solution.py:332
  27.1 4.5 %collective-permute-start.16 = (bf16[256,128]{1,0:T(8,128)(2,1)S(1)}, bf16[256,128]{1,0:T(8,128)(2,1)S(1)}, u32[]{:S(2)}, u32[]{:S(2)}) collective-permute-start(bf16[256,128]{1,0:T(8,128)(2,1)S(1)} %get-tuple-element.82.refs_0_._.own), channel_id=1, source_target_pairs={{0,2},{1,3},{2,0},{3,1},{4,6},{5,7},{6,4},{7,5},{8,10},{9,11},{10,... | collective-permute-start | bytes 196616 | tf_op jit(solution)/shard_map/ppermute | solution.py:323
  27.4 5.6 %collective-permute-start.13 = (bf16[256,128]{1,0:T(8,128)(2,1)S(1)}, bf16[256,128]{1,0:T(8,128)(2,1)S(1)}, u32[]{:S(2)}, u32[]{:S(2)}) collective-permute-start(bf16[256,128]{1,0:T(8,128)(2,1)S(1)} %get-tuple-element.82.refs_0_._.own), channel_id=1, source_target_pairs={{0,16},{1,17},{2,18},{3,19},{4,20},{5,21},{6,22},{7,23},{8,24},{9,... | collective-permute-start | bytes 196616 | tf_op jit(solution)/shard_map/ppermute | solution.py:332
  27.8 0.7 %copy-start.6 = (s32[3,1,4,2]{2,3,1,0:T(2,128)S(1)}, s32[3,1,4,2]{2,3,1,0:T(2,128)}, u32[]{:S(2)}) copy-start(s32[3,1,4,2]{2,3,1,0:T(2,128)} %param.13) | copy-start | bytes 292
  28.5 1.2 %copy-start.4 = (bf16[256,1024]{1,0:T(8,128)(2,1)S(1)}, bf16[256,1024]{1,0:T(8,128)(2,1)}, u32[]{:S(2)}) copy-start(bf16[256,1024]{1,0:T(8,128)(2,1)} %refs_3_.1) | copy-start | bytes 1572868
  31.6 1.8 %collective-permute-start.17 = (bf16[256,128]{1,0:T(8,128)(2,1)S(1)}, bf16[256,128]{1,0:T(8,128)(2,1)S(1)}, u32[]{:S(2)}, u32[]{:S(2)}) collective-permute-start(bf16[256,128]{1,0:T(8,128)(2,1)S(1)} %share_sum.3.refs_0_), channel_id=1, source_target_pairs={{0,1},{1,0},{2,3},{3,2},{4,5},{5,4},{6,7},{7,6},{8,9},{9,8},{10,11... | collective-permute-start | bytes 196616 | tf_op jit(solution)/shard_map/ppermute | solution.py:323
  33.1 1.3 %collective-permute-start.14 = (bf16[256,128]{1,0:T(8,128)(2,1)S(1)}, bf16[256,128]{1,0:T(8,128)(2,1)S(1)}, u32[]{:S(2)}, u32[]{:S(2)}) collective-permute-start(bf16[256,128]{1,0:T(8,128)(2,1)S(1)} %share_sum.2.refs_1_), channel_id=1, source_target_pairs={{0,1},{1,0},{2,3},{3,2},{4,5},{5,4},{6,7},{7,6},{8,9},{9,8},{10,11... | collective-permute-start | bytes 196616 | tf_op jit(solution)/shard_map/ppermute | solution.py:323
  34.8 5.7 %collective-permute-start.20 = (bf16[256,128]{1,0:T(8,128)(2,1)S(1)}, bf16[256,128]{1,0:T(8,128)(2,1)S(1)}, u32[]{:S(2)}, u32[]{:S(2)}) collective-permute-start(bf16[256,128]{1,0:T(8,128)(2,1)S(1)} %get-tuple-element.90), channel_id=1, source_target_pairs={{0,12},{4,8},{8,4},{12,0},{16,28},{20,24},{24,20},{28,16},{1,13},{... | collective-permute-start | bytes 196616 | tf_op jit(solution)/shard_map/ppermute | solution.py:323
  36.8 4.6 %collective-permute-start.18 = (bf16[256,128]{1,0:T(8,128)(2,1)S(1)}, bf16[256,128]{1,0:T(8,128)(2,1)S(1)}, u32[]{:S(2)}, u32[]{:S(2)}) collective-permute-start(bf16[256,128]{1,0:T(8,128)(2,1)S(1)} %get-tuple-element.90), channel_id=1, source_target_pairs={{0,8},{4,12},{8,0},{12,4},{16,24},{20,28},{24,16},{28,20},{1,9},{5... | collective-permute-start | bytes 196616 | tf_op jit(solution)/shard_map/ppermute | solution.py:323
  37.6 4.3 %collective-permute-start.19 = (bf16[256,128]{1,0:T(8,128)(2,1)S(1)}, bf16[256,128]{1,0:T(8,128)(2,1)S(1)}, u32[]{:S(2)}, u32[]{:S(2)}) collective-permute-start(bf16[256,128]{1,0:T(8,128)(2,1)S(1)} %get-tuple-element.91.refs_0_), channel_id=1, source_target_pairs={{0,4},{4,0},{8,12},{12,8},{16,20},{20,16},{24,28},{28,24},{1,5},{5... | collective-permute-start | bytes 196616 | tf_op jit(solution)/shard_map/ppermute | solution.py:323

commit v15 on v14

--- a/solution.py
+++ b/solution.py
@@ -200,11 +200,15 @@
     base[...] = made.astype(base.dtype)
 
 
-def last_residual_kernel(rhs, smoothed, scale, local, rim, outer, inner, share, out, base):
+def last_residual_kernel(
+    rhs, smoothed, scale, local, rim, outer, inner, share, out, base, lower_rows
+):
     rims = jnp.concatenate([inner[...], outer[...]], axis=0)
     left = rhs[...] - matmul(local[...], smoothed[...])
     residual = (left - matmul(rim[...], rims)).astype(bf16)
-    out[...] = matmul(share[...], residual).astype(bf16)
+    made = matmul(share[...], residual).astype(bf16)
+    out[...] = made
+    lower_rows[...] = made[lower_rows.shape[0] :]
     base[...] = rhs[...] * (relax_down * scale[...]) + (relax_up * scale[...]) * left
 
 
@@ -274,8 +278,16 @@
     return matmul(inverse[:, pl.ds(pl.multiple_of(piece * depth, depth), depth)], part[...])
 
 
-def share_sum_kernel(far, own, *refs):
-    refs[-1][...] = (far[...].astype(f32) + own[...].astype(f32)).astype(bf16)
+def share_sum_kernel(far, own, _, out, upper_rows):
+    made = (far[...].astype(f32) + own[...].astype(f32)).astype(bf16)
+    out[...] = made
+    upper_rows[...] = made[: upper_rows.shape[0]]
+
+
+def share_join_kernel(upper_rows, far, own, _, out):
+    rows = upper_rows.shape[0]
+    out[:rows, :] = upper_rows[...]
+    out[rows:, :] = (far[...].astype(f32) + own[...].astype(f32)).astype(bf16)
 
 
 def coarse_kernel(offsets, inverse, *refs):
@@ -432,9 +444,10 @@
             )
         made = []
         for operands in joined:
-            value, made_base = run(
+            value, made_base, *lower_rows = run(
                 last_residual_kernel if share else residual_kernel, "residual",
-                [chunk_shape, real_shape if made or level_idx else chunk_shape],
+                [chunk_shape, real_shape if made or level_idx else chunk_shape]
+                + [array((rows // 2, width), bf16)] * len(share),
                 [*operands, *(share or [joined[-1][1]])],
                 flops=flops(width, 2) if not made else late_cost,
             )
@@ -443,9 +456,13 @@
         sent, kept = made[:1], made[-1:]
         anchor = made[0]
     (mine,) = kept
-    far_parts = {o: exchange_both(mine, 1 << last, o) for o in range(0, pieces, 2)}
+    (lower_rows,) = lower_rows
+    far_part = exchange_both(mine, 1 << last, 0)
+    across = {
+        o: (exchange_both(lower_rows, 1 << last, o), exchange(lower_rows, "narrow", o))
+        for o in range(2, pieces, 2)
+    }
     far_base = exchange(bases[0], "wide", 1)
-    own_parts = {o: exchange(mine, "narrow", o) if o else mine for o in range(0, pieces, 2)}
     coarse_mat, *ups = run(
         functools.partial(coarse_operators_kernel, 2, levels), "coarse_operators",
         [array((rows, pieces * rows), bf16)] + [square_shape] * (levels - 3),
@@ -462,11 +479,15 @@
          *operators[0], *operators[1], base, bases[0], far_base],
         flops=flops(rows, 4), scratch=held,
     )
-    parts = {}
-    for offset in reversed(range(0, pieces, 2)):
+    total_share, upper_rows = run(
+        share_sum_kernel, "share_sum", [chunk_shape, array((rows // 2, width), bf16)],
+        [far_part, mine, coarse_mat],
+    )
+    parts = {0: total_share}
+    for offset, (far_rows, own_rows) in across.items():
         (parts[offset],) = run(
-            share_sum_kernel, "share_sum", [chunk_shape],
-            [far_parts[offset], own_parts[offset], coarse_mat, upper],
+            share_join_kernel, "share_join", [chunk_shape],
+            [exchange(upper_rows, "narrow", offset), far_rows, own_rows, upper],
         )
     offsets = tuple(parts)
     (value,) = run(

time: 42.9 us -> 44.5 us (1.037)
  waiting for transfers between devices: 6.12 us -> 8.31 us
  local copies, waits for them, and re-layouts: 0.71 us -> 0.03 us
    ppermute x14 -> x15, waiting for transfers between devices: 3.38 us -> 6.41 us  [exchange(): return lax.ppermute(value, axis, [(i, i ^ bit) for i in range(count)])]
    ppermute x14 -> x15, starting transfers between devices: 12.9 us -> 14.7 us  [exchange(): return lax.ppermute(value, axis, [(i, i ^ bit) for i in range(count)])]
    ppermute x2, starting transfers between devices: 4.06 us -> 3.11 us  [exchange_both(): return lax.ppermute(value, ('wide', 'narrow'), pairs)]
    ppermute x5, starting transfers between devices: 6.01 us -> 5.14 us  [swap_outer(): return lax.ppermute(outer, 'narrow', gaps)]
    unnamed x14, local copies, waits for them, and re-layouts: 0.71 us -> 0.03 us
    ppermute x5, waiting for transfers between devices: 1.16 us -> 0.51 us  [swap_outer(): return lax.ppermute(outer, 'narrow', gaps)]
  transfers between devices with their start and end apart: 21 -> 22, of which waited for: 8 -> 6; matrix products, arithmetic and copies ran while one was open for 0% -> 0% of each run, Pallas kernels for 24% -> 22%
where the time goes in v15:
time: 44.5 us; the launch traced here: 44.4 us
  starting transfers between devices  23 us (52%)
  Pallas kernels  12.8 us (29%)
  waiting for transfers between devices  8.31 us (19%)
    ppermute x15, starting transfers between devices, exchange(): return lax.ppermute(value, axis, [(i, i ^ bit) for i in range(count)])  14.7 us
    pallas_call x22, Pallas kernels, run(): pl.pallas_call(body, grid=(1,) if windows else (), out_shape=[out_space(o...  12.8 us
    ppermute x15, waiting for transfers between devices, exchange(): return lax.ppermute(value, axis, [(i, i ^ bit) for i in range(count)])  6.41 us
    ppermute x5, starting transfers between devices, swap_outer(): return lax.ppermute(outer, 'narrow', gaps)  5.14 us
    ppermute x2, starting transfers between devices, exchange_both(): return lax.ppermute(value, ('wide', 'narrow'), pairs)  3.11 us
    ppermute x2, waiting for transfers between devices, exchange_both(): return lax.ppermute(value, ('wide', 'narrow'), pairs)  1.4 us
  transfers between devices with their start and end apart: 22, of which 6 were waited for; matrix products, arithmetic and copies ran while one was open for 0% of the time, Pallas kernels for 22%

profile of v15, /device:TPU:0, one launch (start us, length us, event | category | flops | bytes accessed | tf_op | source)
XLA Modules:
  0.0 44.4 jit_solution(2431604590399993088)
XLA Ops:
  0.0 1.3 %start.1 = (s32[3,1,4,5]{3,2,1,0:T(4,128)S(1)}, bf16[64,512]{1,0:T(8,128)(2,1)S(1)}, bf16[64,256]{1,0:T(8,128)(2,1)S(1)}, bf16[64,256]{1,0:T(8,128)(2,1)S(1)}) custom-call(f32[1,256,512]{2,1,0:T(8,128)} %rhs.3, bf16[3,1,4,5,64,64]{5,4,3,2,1,0:T(8,128)(2,1)} %blocks.7, s32[3,1,4,5]{3,2,1,0:T(4,128)} %refs_0_.1), custom_call_target="tpu_custom_call" | custom-call | bytes 1016048 | tf_op jit(solution)/shard_map/start/pallas_call | solution.py:52
  1.3 0.5 %collective-permute-start.1 = (bf16[64,512]{1,0:T(8,128)(2,1)S(1)}, bf16[64,512]{1,0:T(8,128)(2,1)S(1)}, u32[]{:S(2)}, u32[]{:S(2)}) collective-permute-start(bf16[64,512]{1,0:T(8,128)(2,1)S(1)} %get-tuple-element.57), channel_id=1, source_target_pairs={{0,1},{1,0},{2,3},{3,2},{4,5},{5,4},{6,7},{7,6},{8,9},{9,8},{10,11... | collective-permute-start | bytes 196616 | tf_op jit(solution)/shard_map/ppermute | solution.py:335
  1.8 2.6 %collective-permute-start = (bf16[64,256]{1,0:T(8,128)(2,1)S(1)}, bf16[64,256]{1,0:T(8,128)(2,1)S(1)}, u32[]{:S(2)}, u32[]{:S(2)}) collective-permute-start(bf16[64,256]{1,0:T(8,128)(2,1)S(1)} %get-tuple-element.53._), channel_id=1, source_target_pairs={{0,3},{1,2},{2,1},{3,0},{4,7},{5,6},{6,5},{7,4},{8,11},{9,10},{10,... | collective-permute-start | bytes 98312 | tf_op jit(solution)/shard_map/ppermute | solution.py:350
  4.5 1.1 %first_local.1 = (f32[256,512]{1,0:T(8,128)S(1)}, f32[256,512]{1,0:T(8,128)S(1)}, bf16[256,256]{1,0:T(8,128)(2,1)S(1)}, bf16[256,128]{1,0:T(8,128)(2,1)S(1)}, f32[256,1]{1,0:T(8,128)S(1)}) custom-call(f32[1,256,512]{2,1,0:T(8,128)S(1)} %copy-done.3, bf16[64,256]{1,0:T(8,128)(2,1)S(1)} %get-tuple-element.53._, s32[3,1,4,5]{3,2,1,0:T(4,128)S(1)} %get-tuple-element.54.cols, ...), custom_call_target="tpu_custom_call" | custom-call | flops 67108864 | bytes 1048816 | tf_op jit(solution)/shard_map/first_local/pallas_call | solution.py:52
  5.6 0.5 %collective-permute-done.outer = bf16[64,256]{1,0:T(8,128)(2,1)S(1)} collective-permute-done((bf16[64,256]{1,0:T(8,128)(2,1)S(1)}, bf16[64,256]{1,0:T(8,128)(2,1)S(1)}, u32[]{:S(2)}, u32[]{:S(2)}) %collective-permute-start) | collective-permute-done | bytes 32800 | tf_op jit(solution)/shard_map/ppermute | solution.py:350
  6.1 0.2 first_residual.2
  6.3 1.7 %collective-permute-start.2 = (bf16[256,128]{1,0:T(8,128)(2,1)S(1)}, bf16[256,128]{1,0:T(8,128)(2,1)S(1)}, u32[]{:S(2)}, u32[]{:S(2)}) collective-permute-start(bf16[256,128]{1,0:T(8,128)(2,1)S(1)} %get-tuple-element.58._), channel_id=1, source_target_pairs={{0,4},{4,0},{8,12},{12,8},{16,20},{20,16},{24,28},{28,24},{1,5},{5... | collective-permute-start | bytes 196616 | tf_op jit(solution)/shard_map/ppermute | solution.py:335
  8.0 0.2 first_residual.3
  8.2 1.4 %collective-permute-start.6 = (bf16[256,128]{1,0:T(8,128)(2,1)S(1)}, bf16[256,128]{1,0:T(8,128)(2,1)S(1)}, u32[]{:S(2)}, u32[]{:S(2)}) collective-permute-start(bf16[256,128]{1,0:T(8,128)(2,1)S(1)} %get-tuple-element.70), channel_id=1, source_target_pairs={{0,4},{4,0},{8,12},{12,8},{16,20},{20,16},{24,28},{28,24},{1,5},{5... | collective-permute-start | bytes 196616 | tf_op jit(solution)/shard_map/ppermute | solution.py:335
  9.6 1.1 %operators.2 = (bf16[256,512]{1,0:T(8,128)(2,1)S(1)}, bf16[256,256]{1,0:T(8,128)(2,1)S(1)}, bf16[256,128]{1,0:T(8,128)(2,1)S(1)}, f32[256,1]{1,0:T(8,128)S(1)}) custom-call(bf16[256,128]{1,0:T(8,128)(2,1)S(1)} %get-tuple-element.58._, s32[3,3,1,4]{3,2,1,0:T(1,128)S(1)} %bitcast.2, bf16[3,1,4,3,64,64]{5,4,3,2,1,0:T(8,128)(2,1)S(1)} %copy-done.1, ...), custom_call_target="tpu_custom_call" | custom-call | bytes 852352 | tf_op jit(solution)/shard_map/operators/pallas_call | solution.py:52
  10.8 0.2 join.3
  11.0 1.6 %collective-permute-start.3 = (bf16[64,128]{1,0:T(8,128)(2,1)S(1)}, bf16[64,128]{1,0:T(8,128)(2,1)S(1)}, u32[]{:S(2)}, u32[]{:S(2)}) collective-permute-start(bf16[64,128]{1,0:T(8,128)(2,1)S(1)} %get-tuple-element.66), channel_id=1, source_target_pairs={{0,3},{1,2},{2,1},{3,0},{4,7},{5,6},{6,5},{7,4},{8,11},{9,10},{10,... | collective-permute-start | bytes 49160 | tf_op jit(solution)/shard_map/ppermute | solution.py:350
  12.6 0.6 %collective-permute-start.4 = (bf16[64,128]{1,0:T(8,128)(2,1)S(1)}, bf16[64,128]{1,0:T(8,128)(2,1)S(1)}, u32[]{:S(2)}, u32[]{:S(2)}) collective-permute-start(bf16[64,128]{1,0:T(8,128)(2,1)S(1)} %get-tuple-element.67), channel_id=1, source_target_pairs={{0,1},{1,0},{2,3},{3,2},{4,5},{5,4},{6,7},{7,6},{8,9},{9,8},{10,11... | collective-permute-start | bytes 49160 | tf_op jit(solution)/shard_map/ppermute | solution.py:335
  13.2 0.2 join.4
  13.4 0.8 %collective-permute-start.7 = (bf16[64,128]{1,0:T(8,128)(2,1)S(1)}, bf16[64,128]{1,0:T(8,128)(2,1)S(1)}, u32[]{:S(2)}, u32[]{:S(2)}) collective-permute-start(bf16[64,128]{1,0:T(8,128)(2,1)S(1)} %get-tuple-element.75), channel_id=1, source_target_pairs={{0,3},{1,2},{2,1},{3,0},{4,7},{5,6},{6,5},{7,4},{8,11},{9,10},{10,... | collective-permute-start | bytes 49160 | tf_op jit(solution)/shard_map/ppermute | solution.py:350
  14.2 0.6 %collective-permute-start.8 = (bf16[64,128]{1,0:T(8,128)(2,1)S(1)}, bf16[64,128]{1,0:T(8,128)(2,1)S(1)}, u32[]{:S(2)}, u32[]{:S(2)}) collective-permute-start(bf16[64,128]{1,0:T(8,128)(2,1)S(1)} %get-tuple-element.76), channel_id=1, source_target_pairs={{0,1},{1,0},{2,3},{3,2},{4,5},{5,4},{6,7},{7,6},{8,9},{9,8},{10,11... | collective-permute-start | bytes 49160 | tf_op jit(solution)/shard_map/ppermute | solution.py:335
  14.9 0.2 residual.3
  15.1 1.6 %collective-permute-start.9 = (bf16[256,128]{1,0:T(8,128)(2,1)S(1)}, bf16[256,128]{1,0:T(8,128)(2,1)S(1)}, u32[]{:S(2)}, u32[]{:S(2)}) collective-permute-start(bf16[256,128]{1,0:T(8,128)(2,1)S(1)} %get-tuple-element.72._), channel_id=1, source_target_pairs={{0,8},{4,12},{8,0},{12,4},{16,24},{20,28},{24,16},{28,20},{1,9},{5... | collective-permute-start | bytes 196616 | tf_op jit(solution)/shard_map/ppermute | solution.py:335
  16.8 0.2 residual.4
  17.0 1.1 %operators.3 = (bf16[256,512]{1,0:T(8,128)(2,1)S(1)}, bf16[256,256]{1,0:T(8,128)(2,1)S(1)}, bf16[256,128]{1,0:T(8,128)(2,1)S(1)}, f32[256,1]{1,0:T(8,128)S(1)}) custom-call(bf16[256,128]{1,0:T(8,128)(2,1)S(1)} %get-tuple-element.72._, s32[3,3,1,4]{3,2,1,0:T(1,128)S(1)} %bitcast.3, bf16[3,1,4,3,64,64]{5,4,3,2,1,0:T(8,128)(2,1)S(1)} %copy-done.1, ...), custom_call_target="tpu_custom_call" | custom-call | bytes 852352 | tf_op jit(solution)/shard_map/operators/pallas_call | solution.py:52
  18.1 1.4 %collective-permute-done.9.other = bf16[256,128]{1,0:T(8,128)(2,1)S(1)} collective-permute-done((bf16[256,128]{1,0:T(8,128)(2,1)S(1)}, bf16[256,128]{1,0:T(8,128)(2,1)S(1)}, u32[]{:S(2)}, u32[]{:S(2)}) %collective-permute-start.9) | collective-permute-done | bytes 65568 | tf_op jit(solution)/shard_map/ppermute | solution.py:335
  19.4 0.2 join.5
  19.7 0.1 collective-permute-start.10
  19.8 1.5 %collective-permute-start.11 = (bf16[64,128]{1,0:T(8,128)(2,1)S(1)}, bf16[64,128]{1,0:T(8,128)(2,1)S(1)}, u32[]{:S(2)}, u32[]{:S(2)}) collective-permute-start(bf16[64,128]{1,0:T(8,128)(2,1)S(1)} %get-tuple-element.84), channel_id=1, source_target_pairs={{0,1},{1,0},{2,3},{3,2},{4,5},{5,4},{6,7},{7,6},{8,9},{9,8},{10,11... | collective-permute-start | bytes 49160 | tf_op jit(solution)/shard_map/ppermute | solution.py:335
  21.2 1.6 %collective-permute-start.12 = (bf16[256,128]{1,0:T(8,128)(2,1)S(1)}, bf16[256,128]{1,0:T(8,128)(2,1)S(1)}, u32[]{:S(2)}, u32[]{:S(2)}) collective-permute-start(bf16[256,128]{1,0:T(8,128)(2,1)S(1)} %get-tuple-element.86.near), channel_id=1, source_target_pairs={{0,4},{4,0},{8,12},{12,8},{16,20},{20,16},{24,28},{28,24},{1,5},{5... | collective-permute-start | bytes 196616 | tf_op jit(solution)/shard_map/ppermute | solution.py:335
  22.8 0.7 %share.1 = bf16[256,256]{1,0:T(8,128)(2,1)S(1)} custom-call(bf16[256,128]{1,0:T(8,128)(2,1)S(1)} %get-tuple-element.80._.smoothed, s32[3,3,1,4]{3,2,1,0:T(1,128)S(1)} %bitcast.4, bf16[3,1,4,3,64,64]{5,4,3,2,1,0:T(8,128)(2,1)S(1)} %copy-done.1), custom_call_target="tpu_custom_call" | custom-call | bytes 360592 | tf_op jit(solution)/shard_map/share/pallas_call | solution.py:52
  23.6 0.4 residual.5
  24.0 2.7 %collective-permute-start.13 = (bf16[256,128]{1,0:T(8,128)(2,1)S(1)}, bf16[256,128]{1,0:T(8,128)(2,1)S(1)}, u32[]{:S(2)}, u32[]{:S(2)}) collective-permute-start(bf16[256,128]{1,0:T(8,128)(2,1)S(1)} %get-tuple-element.85.refs_0_.own._), channel_id=1, source_target_pairs={{0,16},{1,17},{2,18},{3,19},{4,20},{5,21},{6,22},{7,23},{8,24},{9,... | collective-permute-start | bytes 196616 | tf_op jit(solution)/shard_map/ppermute | solution.py:344
  26.7 0.5 %collective-permute-start.15 = (bf16[128,128]{1,0:T(8,128)(2,1)S(1)}, bf16[128,128]{1,0:T(8,128)(2,1)S(1)}, u32[]{:S(2)}, u32[]{:S(2)}) collective-permute-start(bf16[128,128]{1,0:T(8,128)(2,1)S(1)} %get-tuple-element.88), channel_id=1, source_target_pairs={{0,18},{1,19},{2,16},{3,17},{4,22},{5,23},{6,20},{7,21},{8,26},{9,... | collective-permute-start | bytes 98312 | tf_op jit(solution)/shard_map/ppermute | solution.py:344
  27.2 1.3 %collective-permute-start.16 = (bf16[128,128]{1,0:T(8,128)(2,1)S(1)}, bf16[128,128]{1,0:T(8,128)(2,1)S(1)}, u32[]{:S(2)}, u32[]{:S(2)}) collective-permute-start(bf16[128,128]{1,0:T(8,128)(2,1)S(1)} %get-tuple-element.88), channel_id=1, source_target_pairs={{0,2},{1,3},{2,0},{3,1},{4,6},{5,7},{6,4},{7,5},{8,10},{9,11},{10,... | collective-permute-start | bytes 98312 | tf_op jit(solution)/shard_map/ppermute | solution.py:335
  28.5 1.1 %coarse_operators.1._.inverse = bf16[256,1024]{1,0:T(8,128)(2,1)S(1)} custom-call(bf16[256,128]{1,0:T(8,128)(2,1)S(1)} %get-tuple-element.85.refs_0_.own._, bf16[256,128]{1,0:T(8,128)(2,1)S(1)} %collective-permute-done.12.refs_1_.far, s32[3,1,2,4]{3,2,1,0:T(2,128)S(1)} %bitcast.5, bf16[256,1024]{1,0:T(8,128)(2,1)S(1)} %copy-done.4, ...), custom_call_target="tpu_custom_call" | custom-call | flops 201326592 | bytes 984160 | tf_op jit(solution)/shard_map/coarse_operators/pallas_call | solution.py:52
  29.6 1.4 %collective-permute-done.13.far = bf16[256,128]{1,0:T(8,128)(2,1)S(1)} collective-permute-done((bf16[256,128]{1,0:T(8,128)(2,1)S(1)}, bf16[256,128]{1,0:T(8,128)(2,1)S(1)}, u32[]{:S(2)}, u32[]{:S(2)}) %collective-permute-start.13) | collective-permute-done | bytes 65568 | tf_op jit(solution)/shard_map/ppermute | solution.py:344
  31.0 0.1 collective-permute-start.14
  31.1 1.2 %fine_operators.1 = (bf16[256,256]{1,0:T(8,128)(2,1)S(1)}, bf16[256,256]{1,0:T(8,128)(2,1)S(1)}, bf16[256,256]{1,0:T(8,128)(2,1)S(1)}, f32[256,256]{1,0:T(8,128)S(1)}) custom-call(bf16[256,128]{1,0:T(8,128)(2,1)S(1)} %get-tuple-element.85.refs_0_.own._, s32[3,1,2,4]{3,2,1,0:T(2,128)S(1)} %bitcast.6, bf16[3,1,4,2,64,64]{5,4,3,2,1,0:T(8,128)(2,1)S(1)} %copy-done.2, ...), custom_call_target="tpu_custom_call" | custom-call | flops 134217728 | bytes 1378400 | tf_op jit(solution)/shard_map/fine_operators/pallas_call | solution.py:52
  32.3 0.1 collective-permute-start.18
  32.4 0.0 collective-permute-done.15.far
  32.4 2.6 %collective-permute-done.14.upper_rows = bf16[128,128]{1,0:T(8,128)(2,1)S(1)} collective-permute-done((bf16[128,128]{1,0:T(8,128)(2,1)S(1)}, bf16[128,128]{1,0:T(8,128)(2,1)S(1)}, u32[]{:S(2)}, u32[]{:S(2)}) %collective-permute-start.14) | collective-permute-done | bytes 32800 | tf_op jit(solution)/shard_map/ppermute | solution.py:335
  35.0 0.1 collective-permute-start.17
  35.1 0.2 coarse.1.refs_2_
  35.3 1.0 %collective-permute-done.17.refs_0_ = bf16[256,128]{1,0:T(8,128)(2,1)S(1)} collective-permute-done((bf16[256,128]{1,0:T(8,128)(2,1)S(1)}, bf16[256,128]{1,0:T(8,128)(2,1)S(1)}, u32[]{:S(2)}, u32[]{:S(2)}) %collective-permute-start.17) | collective-permute-done | bytes 65568 | tf_op jit(solution)/shard_map/ppermute | solution.py:335
  36.3 0.4 up.1
  36.8 1.1 %collective-permute-start.21 = (bf16[256,128]{1,0:T(8,128)(2,1)S(1)}, bf16[256,128]{1,0:T(8,128)(2,1)S(1)}, u32[]{:S(2)}, u32[]{:S(2)}) collective-permute-start(bf16[256,128]{1,0:T(8,128)(2,1)S(1)} %get-tuple-element.96), channel_id=1, source_target_pairs={{0,12},{4,8},{8,4},{12,0},{16,28},{20,24},{24,20},{28,16},{1,13},{... | collective-permute-start | bytes 196616 | tf_op jit(solution)/shard_map/ppermute | solution.py:335
  37.9 1.1 %collective-permute-start.19 = (bf16[256,128]{1,0:T(8,128)(2,1)S(1)}, bf16[256,128]{1,0:T(8,128)(2,1)S(1)}, u32[]{:S(2)}, u32[]{:S(2)}) collective-permute-start(bf16[256,128]{1,0:T(8,128)(2,1)S(1)} %get-tuple-element.96), channel_id=1, source_target_pairs={{0,8},{4,12},{8,0},{12,4},{16,24},{20,28},{24,16},{28,20},{1,9},{5... | collective-permute-start | bytes 196616 | tf_op jit(solution)/shard_map/ppermute | solution.py:335
  39.0 1.4 %collective-permute-start.20 = (bf16[256,128]{1,0:T(8,128)(2,1)S(1)}, bf16[256,128]{1,0:T(8,128)(2,1)S(1)}, u32[]{:S(2)}, u32[]{:S(2)}) collective-permute-start(bf16[256,128]{1,0:T(8,128)(2,1)S(1)} %get-tuple-element.97.refs_0_), channel_id=1, source_target_pairs={{0,4},{4,0},{8,12},{12,8},{16,20},{20,16},{24,28},{28,24},{1,5},{5... | collective-permute-start | bytes 196616 | tf_op jit(solution)/shard_map/ppermute | solution.py:335
  40.3 0.8 %output.3.refs_5_ = f32[1,256,512]{2,1,0:T(8,128)} custom-call(bf16[256,128]{1,0:T(8,128)(2,1)S(1)} %get-tuple-element.97.refs_0_, f32[256,512]{1,0:T(8,128)S(1)} %get-tuple-element.91.base.refs_1_.refs_2_, bf16[256,256]{1,0:T(8,128)(2,1)S(1)} %get-tuple-element.98.refs_2_.refs_3_, f32[256,256]{1,0:T(8,128)S(1)} %get-tuple-element.99.refs_3_.refs_4_, ...), custom_call_target="tpu_custom_call" | custom-call | flops 16777216 | bytes 1114112 | tf_op jit(solution)/shard_map/output/pallas_call | solution.py:52
  41.2 1.4 %collective-permute-done.21.refs_0_ = bf16[256,128]{1,0:T(8,128)(2,1)S(1)} collective-permute-done((bf16[256,128]{1,0:T(8,128)(2,1)S(1)}, bf16[256,128]{1,0:T(8,128)(2,1)S(1)}, u32[]{:S(2)}, u32[]{:S(2)}) %collective-permute-start.21) | collective-permute-done | bytes 65568 | tf_op jit(solution)/shard_map/ppermute | solution.py:335
  42.6 0.8 %output.4.refs_6_ = f32[1,256,512]{2,1,0:T(8,128)} custom-call(bf16[256,128]{1,0:T(8,128)(2,1)S(1)} %collective-permute-done.21.refs_0_, f32[256,512]{1,0:T(8,128)S(1)} %get-tuple-element.91.base.refs_1_.refs_2_, bf16[256,256]{1,0:T(8,128)(2,1)S(1)} %get-tuple-element.98.refs_2_.refs_3_, ...), custom_call_target="tpu_custom_call", output_to_operand_aliasing={{}: (5, {})} | custom-call | flops 16777216 | bytes 1638400 | tf_op jit(solution)/shard_map/output/pallas_call | solution.py:52
  43.5 0.9 %output.5 = f32[1,256,512]{2,1,0:T(8,128)} custom-call(bf16[256,128]{1,0:T(8,128)(2,1)S(1)} %collective-permute-done.19.refs_0_, bf16[256,128]{1,0:T(8,128)(2,1)S(1)} %collective-permute-done.20.refs_1_, f32[256,512]{1,0:T(8,128)S(1)} %get-tuple-element.91.base.refs_1_.refs_2_, ...), custom_call_target="tpu_custom_call", output_to_operand_aliasing={{}: (6, {})} | custom-call | flops 33554432 | bytes 1703936 | tf_op jit(solution)/shard_map/output/pallas_call | solution.py:52
  (32 shorter events, 0.1 us)
Async XLA Ops:
  0.0 4.4 %copy-start = (bf16[3,1,4,5,64,64]{5,4,3,2,1,0:T(8,128)(2,1)S(1)}, bf16[3,1,4,5,64,64]{5,4,3,2,1,0:T(8,128)(2,1)}, u32[]{:S(2)}) copy-start(bf16[3,1,4,5,64,64]{5,4,3,2,1,0:T(8,128)(2,1)} %blocks.7) | copy-start | bytes 1474564
  0.0 4.4 %copy-start.3 = (f32[1,256,512]{2,1,0:T(8,128)S(1)}, f32[1,256,512]{2,1,0:T(8,128)}, u32[]{:S(2)}) copy-start(f32[1,256,512]{2,1,0:T(8,128)} %rhs.3) | copy-start | bytes 1572868
  1.3 4.8 %collective-permute-start.1 = (bf16[64,512]{1,0:T(8,128)(2,1)S(1)}, bf16[64,512]{1,0:T(8,128)(2,1)S(1)}, u32[]{:S(2)}, u32[]{:S(2)}) collective-permute-start(bf16[64,512]{1,0:T(8,128)(2,1)S(1)} %get-tuple-element.57), channel_id=1, source_target_pairs={{0,1},{1,0},{2,3},{3,2},{4,5},{5,4},{6,7},{7,6},{8,9},{9,8},{10,11... | collective-permute-start | bytes 196616 | tf_op jit(solution)/shard_map/ppermute | solution.py:335
  1.8 4.3 %collective-permute-start = (bf16[64,256]{1,0:T(8,128)(2,1)S(1)}, bf16[64,256]{1,0:T(8,128)(2,1)S(1)}, u32[]{:S(2)}, u32[]{:S(2)}) collective-permute-start(bf16[64,256]{1,0:T(8,128)(2,1)S(1)} %get-tuple-element.53._), channel_id=1, source_target_pairs={{0,3},{1,2},{2,1},{3,0},{4,7},{5,6},{6,5},{7,4},{8,11},{9,10},{10,... | collective-permute-start | bytes 98312 | tf_op jit(solution)/shard_map/ppermute | solution.py:350
  4.4 3.6 %collective-permute-start.5 = (bf16[64,256]{1,0:T(8,128)(2,1)S(1)}, bf16[64,256]{1,0:T(8,128)(2,1)S(1)}, u32[]{:S(2)}, u32[]{:S(2)}) collective-permute-start(bf16[64,256]{1,0:T(8,128)(2,1)S(1)} %get-tuple-element.68), channel_id=1, source_target_pairs={{0,3},{1,2},{2,1},{3,0},{4,7},{5,6},{6,5},{7,4},{8,11},{9,10},{10,... | collective-permute-start | bytes 98312 | tf_op jit(solution)/shard_map/ppermute | solution.py:350
  6.1 3.5 %copy-start.1 = (bf16[3,1,4,3,64,64]{5,4,3,2,1,0:T(8,128)(2,1)S(1)}, bf16[3,1,4,3,64,64]{5,4,3,2,1,0:T(8,128)(2,1)}, u32[]{:S(2)}) copy-start(bf16[3,1,4,3,64,64]{5,4,3,2,1,0:T(8,128)(2,1)} %rblocks.5) | copy-start | bytes 884740
  6.3 4.5 %collective-permute-start.2 = (bf16[256,128]{1,0:T(8,128)(2,1)S(1)}, bf16[256,128]{1,0:T(8,128)(2,1)S(1)}, u32[]{:S(2)}, u32[]{:S(2)}) collective-permute-start(bf16[256,128]{1,0:T(8,128)(2,1)S(1)} %get-tuple-element.58._), channel_id=1, source_target_pairs={{0,4},{4,0},{8,12},{12,8},{16,20},{20,16},{24,28},{28,24},{1,5},{5... | collective-permute-start | bytes 196616 | tf_op jit(solution)/shard_map/ppermute | solution.py:335
  8.0 1.6 %copy-start.5 = (s32[3,1,4,3]{2,1,3,0:T(1,128)S(1)}, s32[3,1,4,3]{2,1,3,0:T(1,128)}, u32[]{:S(2)}) copy-start(s32[3,1,4,3]{2,1,3,0:T(1,128)} %param.11) | copy-start | bytes 436
  8.2 5.0 %collective-permute-start.6 = (bf16[256,128]{1,0:T(8,128)(2,1)S(1)}, bf16[256,128]{1,0:T(8,128)(2,1)S(1)}, u32[]{:S(2)}, u32[]{:S(2)}) collective-permute-start(bf16[256,128]{1,0:T(8,128)(2,1)S(1)} %get-tuple-element.70), channel_id=1, source_target_pairs={{0,4},{4,0},{8,12},{12,8},{16,20},{20,16},{24,28},{28,24},{1,5},{5... | collective-permute-start | bytes 196616 | tf_op jit(solution)/shard_map/ppermute | solution.py:335
  11.0 3.9 %collective-permute-start.3 = (bf16[64,128]{1,0:T(8,128)(2,1)S(1)}, bf16[64,128]{1,0:T(8,128)(2,1)S(1)}, u32[]{:S(2)}, u32[]{:S(2)}) collective-permute-start(bf16[64,128]{1,0:T(8,128)(2,1)S(1)} %get-tuple-element.66), channel_id=1, source_target_pairs={{0,3},{1,2},{2,1},{3,0},{4,7},{5,6},{6,5},{7,4},{8,11},{9,10},{10,... | collective-permute-start | bytes 49160 | tf_op jit(solution)/shard_map/ppermute | solution.py:350
  12.6 2.3 %collective-permute-start.4 = (bf16[64,128]{1,0:T(8,128)(2,1)S(1)}, bf16[64,128]{1,0:T(8,128)(2,1)S(1)}, u32[]{:S(2)}, u32[]{:S(2)}) collective-permute-start(bf16[64,128]{1,0:T(8,128)(2,1)S(1)} %get-tuple-element.67), channel_id=1, source_target_pairs={{0,1},{1,0},{2,3},{3,2},{4,5},{5,4},{6,7},{7,6},{8,9},{9,8},{10,11... | collective-permute-start | bytes 49160 | tf_op jit(solution)/shard_map/ppermute | solution.py:335
  13.4 3.4 %collective-permute-start.7 = (bf16[64,128]{1,0:T(8,128)(2,1)S(1)}, bf16[64,128]{1,0:T(8,128)(2,1)S(1)}, u32[]{:S(2)}, u32[]{:S(2)}) collective-permute-start(bf16[64,128]{1,0:T(8,128)(2,1)S(1)} %get-tuple-element.75), channel_id=1, source_target_pairs={{0,3},{1,2},{2,1},{3,0},{4,7},{5,6},{6,5},{7,4},{8,11},{9,10},{10,... | collective-permute-start | bytes 49160 | tf_op jit(solution)/shard_map/ppermute | solution.py:350
  14.2 2.5 %collective-permute-start.8 = (bf16[64,128]{1,0:T(8,128)(2,1)S(1)}, bf16[64,128]{1,0:T(8,128)(2,1)S(1)}, u32[]{:S(2)}, u32[]{:S(2)}) collective-permute-start(bf16[64,128]{1,0:T(8,128)(2,1)S(1)} %get-tuple-element.76), channel_id=1, source_target_pairs={{0,1},{1,0},{2,3},{3,2},{4,5},{5,4},{6,7},{7,6},{8,9},{9,8},{10,11... | collective-permute-start | bytes 49160 | tf_op jit(solution)/shard_map/ppermute | solution.py:335
  15.1 4.3 %collective-permute-start.9 = (bf16[256,128]{1,0:T(8,128)(2,1)S(1)}, bf16[256,128]{1,0:T(8,128)(2,1)S(1)}, u32[]{:S(2)}, u32[]{:S(2)}) collective-permute-start(bf16[256,128]{1,0:T(8,128)(2,1)S(1)} %get-tuple-element.72._), channel_id=1, source_target_pairs={{0,8},{4,12},{8,0},{12,4},{16,24},{20,28},{24,16},{28,20},{1,9},{5... | collective-permute-start | bytes 196616 | tf_op jit(solution)/shard_map/ppermute | solution.py:335
  19.7 3.9 %collective-permute-start.10 = (bf16[64,128]{1,0:T(8,128)(2,1)S(1)}, bf16[64,128]{1,0:T(8,128)(2,1)S(1)}, u32[]{:S(2)}, u32[]{:S(2)}) collective-permute-start(bf16[64,128]{1,0:T(8,128)(2,1)S(1)} %get-tuple-element.83), channel_id=1, source_target_pairs={{0,3},{1,2},{2,1},{3,0},{4,7},{5,6},{6,5},{7,4},{8,11},{9,10},{10,... | collective-permute-start | bytes 49160 | tf_op jit(solution)/shard_map/ppermute | solution.py:350
  19.8 3.8 %collective-permute-start.11 = (bf16[64,128]{1,0:T(8,128)(2,1)S(1)}, bf16[64,128]{1,0:T(8,128)(2,1)S(1)}, u32[]{:S(2)}, u32[]{:S(2)}) collective-permute-start(bf16[64,128]{1,0:T(8,128)(2,1)S(1)} %get-tuple-element.84), channel_id=1, source_target_pairs={{0,1},{1,0},{2,3},{3,2},{4,5},{5,4},{6,7},{7,6},{8,9},{9,8},{10,11... | collective-permute-start | bytes 49160 | tf_op jit(solution)/shard_map/ppermute | solution.py:335
  21.2 7.3 %collective-permute-start.12 = (bf16[256,128]{1,0:T(8,128)(2,1)S(1)}, bf16[256,128]{1,0:T(8,128)(2,1)S(1)}, u32[]{:S(2)}, u32[]{:S(2)}) collective-permute-start(bf16[256,128]{1,0:T(8,128)(2,1)S(1)} %get-tuple-element.86.near), channel_id=1, source_target_pairs={{0,4},{4,0},{8,12},{12,8},{16,20},{20,16},{24,28},{28,24},{1,5},{5... | collective-permute-start | bytes 196616 | tf_op jit(solution)/shard_map/ppermute | solution.py:335
  22.8 5.7 %copy-start.4 = (bf16[256,1024]{1,0:T(8,128)(2,1)S(1)}, bf16[256,1024]{1,0:T(8,128)(2,1)}, u32[]{:S(2)}) copy-start(bf16[256,1024]{1,0:T(8,128)(2,1)} %refs_3_.1) | copy-start | bytes 1572868
  23.6 4.9 %copy-start.2 = (bf16[3,1,4,2,64,64]{5,4,3,2,1,0:T(8,128)(2,1)S(1)}, bf16[3,1,4,2,64,64]{5,4,3,2,1,0:T(8,128)(2,1)}, u32[]{:S(2)}) copy-start(bf16[3,1,4,2,64,64]{5,4,3,2,1,0:T(8,128)(2,1)} %blocks_1.1) | copy-start | bytes 589828
  24.0 4.5 %copy-start.6 = (s32[3,1,4,2]{2,3,1,0:T(2,128)S(1)}, s32[3,1,4,2]{2,3,1,0:T(2,128)}, u32[]{:S(2)}) copy-start(s32[3,1,4,2]{2,3,1,0:T(2,128)} %param.13) | copy-start | bytes 292
  24.0 7.0 %collective-permute-start.13 = (bf16[256,128]{1,0:T(8,128)(2,1)S(1)}, bf16[256,128]{1,0:T(8,128)(2,1)S(1)}, u32[]{:S(2)}, u32[]{:S(2)}) collective-permute-start(bf16[256,128]{1,0:T(8,128)(2,1)S(1)} %get-tuple-element.85.refs_0_.own._), channel_id=1, source_target_pairs={{0,16},{1,17},{2,18},{3,19},{4,20},{5,21},{6,22},{7,23},{8,24},{9,... | collective-permute-start | bytes 196616 | tf_op jit(solution)/shard_map/ppermute | solution.py:344
  26.7 5.7 %collective-permute-start.15 = (bf16[128,128]{1,0:T(8,128)(2,1)S(1)}, bf16[128,128]{1,0:T(8,128)(2,1)S(1)}, u32[]{:S(2)}, u32[]{:S(2)}) collective-permute-start(bf16[128,128]{1,0:T(8,128)(2,1)S(1)} %get-tuple-element.88), channel_id=1, source_target_pairs={{0,18},{1,19},{2,16},{3,17},{4,22},{5,23},{6,20},{7,21},{8,26},{9,... | collective-permute-start | bytes 98312 | tf_op jit(solution)/shard_map/ppermute | solution.py:344
  27.2 5.3 %collective-permute-start.16 = (bf16[128,128]{1,0:T(8,128)(2,1)S(1)}, bf16[128,128]{1,0:T(8,128)(2,1)S(1)}, u32[]{:S(2)}, u32[]{:S(2)}) collective-permute-start(bf16[128,128]{1,0:T(8,128)(2,1)S(1)} %get-tuple-element.88), channel_id=1, source_target_pairs={{0,2},{1,3},{2,0},{3,1},{4,6},{5,7},{6,4},{7,5},{8,10},{9,11},{10,... | collective-permute-start | bytes 98312 | tf_op jit(solution)/shard_map/ppermute | solution.py:335
  31.0 4.0 %collective-permute-start.14 = (bf16[128,128]{1,0:T(8,128)(2,1)S(1)}, bf16[128,128]{1,0:T(8,128)(2,1)S(1)}, u32[]{:S(2)}, u32[]{:S(2)}) collective-permute-start(bf16[128,128]{1,0:T(8,128)(2,1)S(1)} %get-tuple-element.87), channel_id=1, source_target_pairs={{0,2},{1,3},{2,0},{3,1},{4,6},{5,7},{6,4},{7,5},{8,10},{9,11},{10,... | collective-permute-start | bytes 98312 | tf_op jit(solution)/shard_map/ppermute | solution.py:335
  32.3 3.0 %collective-permute-start.18 = (bf16[256,128]{1,0:T(8,128)(2,1)S(1)}, bf16[256,128]{1,0:T(8,128)(2,1)S(1)}, u32[]{:S(2)}, u32[]{:S(2)}) collective-permute-start(bf16[256,128]{1,0:T(8,128)(2,1)S(1)} %get-tuple-element.93.refs_0_), channel_id=1, source_target_pairs={{0,1},{1,0},{2,3},{3,2},{4,5},{5,4},{6,7},{7,6},{8,9},{9,8},{10,11... | collective-permute-start | bytes 196616 | tf_op jit(solution)/shard_map/ppermute | solution.py:335
  35.0 1.3 %collective-permute-start.17 = (bf16[256,128]{1,0:T(8,128)(2,1)S(1)}, bf16[256,128]{1,0:T(8,128)(2,1)S(1)}, u32[]{:S(2)}, u32[]{:S(2)}) collective-permute-start(bf16[256,128]{1,0:T(8,128)(2,1)S(1)} %share_join.1.refs_1_), channel_id=1, source_target_pairs={{0,1},{1,0},{2,3},{3,2},{4,5},{5,4},{6,7},{7,6},{8,9},{9,8},{10,11... | collective-permute-start | bytes 196616 | tf_op jit(solution)/shard_map/ppermute | solution.py:335
  36.8 5.8 %collective-permute-start.21 = (bf16[256,128]{1,0:T(8,128)(2,1)S(1)}, bf16[256,128]{1,0:T(8,128)(2,1)S(1)}, u32[]{:S(2)}, u32[]{:S(2)}) collective-permute-start(bf16[256,128]{1,0:T(8,128)(2,1)S(1)} %get-tuple-element.96), channel_id=1, source_target_pairs={{0,12},{4,8},{8,4},{12,0},{16,28},{20,24},{24,20},{28,16},{1,13},{... | collective-permute-start | bytes 196616 | tf_op jit(solution)/shard_map/ppermute | solution.py:335
  37.9 5.6 %collective-permute-start.19 = (bf16[256,128]{1,0:T(8,128)(2,1)S(1)}, bf16[256,128]{1,0:T(8,128)(2,1)S(1)}, u32[]{:S(2)}, u32[]{:S(2)}) collective-permute-start(bf16[256,128]{1,0:T(8,128)(2,1)S(1)} %get-tuple-element.96), channel_id=1, source_target_pairs={{0,8},{4,12},{8,0},{12,4},{16,24},{20,28},{24,16},{28,20},{1,9},{5... | collective-permute-start | bytes 196616 | tf_op jit(solution)/shard_map/ppermute | solution.py:335
  39.0 4.5 %collective-permute-start.20 = (bf16[256,128]{1,0:T(8,128)(2,1)S(1)}, bf16[256,128]{1,0:T(8,128)(2,1)S(1)}, u32[]{:S(2)}, u32[]{:S(2)}) collective-permute-start(bf16[256,128]{1,0:T(8,128)(2,1)S(1)} %get-tuple-element.97.refs_0_), channel_id=1, source_target_pairs={{0,4},{4,0},{8,12},{12,8},{16,20},{20,16},{24,28},{28,24},{1,5},{5... | collective-permute-start | bytes 196616 | tf_op jit(solution)/shard_map/ppermute | solution.py:335

commit v16 on v14

--- a/solution.py
+++ b/solution.py
@@ -192,20 +192,22 @@
         ref[...] = (rest[:, lanes] - matmul(rim[...], rims)).astype(bf16)
 
 
-def residual_kernel(rhs, smoothed, scale, local, rim, outer, inner, _, out, base):
+def local_kernel(rhs, smoothed, local, *refs):
+    refs[-1][...] = rhs[...] - matmul(local[...], smoothed[...])
+
+
+def residual_kernel(rhs, left, scale, rim, outer, inner, _, out, base):
     rims = jnp.concatenate([inner[...], outer[...]], axis=0)
-    left = rhs[...] - matmul(local[...], smoothed[...])
-    out[...] = (left - matmul(rim[...], rims)).astype(bf16)
-    made = rhs[...] * (relax_down * scale[...]) + (relax_up * scale[...]) * left
+    out[...] = (left[...] - matmul(rim[...], rims)).astype(bf16)
+    made = rhs[...] * (relax_down * scale[...]) + (relax_up * scale[...]) * left[...]
     base[...] = made.astype(base.dtype)
 
 
-def last_residual_kernel(rhs, smoothed, scale, local, rim, outer, inner, share, out, base):
+def last_residual_kernel(rhs, left, scale, rim, outer, inner, share, out, base):
     rims = jnp.concatenate([inner[...], outer[...]], axis=0)
-    left = rhs[...] - matmul(local[...], smoothed[...])
-    residual = (left - matmul(rim[...], rims)).astype(bf16)
+    residual = (left[...] - matmul(rim[...], rims)).astype(bf16)
     out[...] = matmul(share[...], residual).astype(bf16)
-    base[...] = rhs[...] * (relax_down * scale[...]) + (relax_up * scale[...]) * left
+    base[...] = rhs[...] * (relax_down * scale[...]) + (relax_up * scale[...]) * left[...]
 
 
 def share_kernel(level_idx, _, rcols, rblocks, share):
@@ -423,19 +425,23 @@
                 [rmat, near, far, scale], flops=flops(width, 2),
             )
             inner, outer = exchange(ends[0], "narrow", 1), swap_outer(ends[1])
-            joined.append((rhs, smoothed, scale, local, rim, outer, inner))
+            joined.append((smoothed, rhs, scale, rim, outer, inner))
+            anchor = smoothed
         share = []
         if level_idx + 1 == last:
             share = run(
                 functools.partial(share_kernel, last), "share", [square_shape],
-                [joined[0][1], rcols, of_level(restrict_blocks, last)],
+                [anchor, rcols, of_level(restrict_blocks, last)],
             )
         made = []
-        for operands in joined:
+        for smoothed, rhs, *operands in joined:
+            (left,) = run(
+                local_kernel, "local", [real_shape], [rhs, smoothed, local, *made], flops=flops(width)
+            )
             value, made_base = run(
                 last_residual_kernel if share else residual_kernel, "residual",
                 [chunk_shape, real_shape if made or level_idx else chunk_shape],
-                [*operands, *(share or [joined[-1][1]])],
+                [rhs, left, *operands, *(share or [anchor])],
                 flops=flops(width, 2) if not made else late_cost,
             )
             made.append(value)

time: 42.9 us -> 43.2 us (level)
    ppermute x2, waiting for transfers between devices: 1.57 us -> 1.12 us  [exchange_both(): return lax.ppermute(value, ('wide', 'narrow'), pairs)]
    pallas_call x22 -> x25, Pallas kernels: 12.8 us -> 13.1 us  [run(): pl.pallas_call(body, grid=(1,) if windows else (), out_shape=[out_space(o...]
where the time goes in v16:
time: 43.2 us; the launch traced here: 43 us
  starting transfers between devices  22.7 us (53%)
  Pallas kernels  13.1 us (30%)
  waiting for transfers between devices  6.16 us (14%)
  local copies, waits for them, and re-layouts  0.71 us (2%)
    ppermute x14, starting transfers between devices, exchange(): return lax.ppermute(value, axis, [(i, i ^ bit) for i in range(count)])  13.2 us
    pallas_call x25, Pallas kernels, run(): pl.pallas_call(body, grid=(1,) if windows else (), out_shape=[out_space(o...  13.1 us
    ppermute x5, starting transfers between devices, swap_outer(): return lax.ppermute(outer, 'narrow', gaps)  5.82 us
    ppermute x2, starting transfers between devices, exchange_both(): return lax.ppermute(value, ('wide', 'narrow'), pairs)  3.71 us
    ppermute x14, waiting for transfers between devices, exchange(): return lax.ppermute(value, axis, [(i, i ^ bit) for i in range(count)])  3.69 us
    ppermute x5, waiting for transfers between devices, swap_outer(): return lax.ppermute(outer, 'narrow', gaps)  1.35 us
    ppermute x2, waiting for transfers between devices, exchange_both(): return lax.ppermute(value, ('wide', 'narrow'), pairs)  1.12 us
  transfers between devices with their start and end apart: 21, of which 8 were waited for; matrix products, arithmetic and copies ran while one was open for 0% of the time, Pallas kernels for 24%

profile of v16, /device:TPU:0, one launch (start us, length us, event | category | flops | bytes accessed | tf_op | source)
XLA Modules:
  0.0 43.0 jit_solution(6407638025585073740)
XLA Ops:
  0.0 1.3 %start.1 = (s32[3,1,4,5]{3,2,1,0:T(4,128)S(1)}, bf16[64,512]{1,0:T(8,128)(2,1)S(1)}, bf16[64,256]{1,0:T(8,128)(2,1)S(1)}, bf16[64,256]{1,0:T(8,128)(2,1)S(1)}) custom-call(f32[1,256,512]{2,1,0:T(8,128)} %rhs.3, bf16[3,1,4,5,64,64]{5,4,3,2,1,0:T(8,128)(2,1)} %blocks.7, s32[3,1,4,5]{3,2,1,0:T(4,128)} %refs_0_.1), custom_call_target="tpu_custom_call" | custom-call | bytes 1016048 | tf_op jit(solution)/shard_map/start/pallas_call | solution.py:52
  1.3 0.5 %collective-permute-start.1 = (bf16[64,512]{1,0:T(8,128)(2,1)S(1)}, bf16[64,512]{1,0:T(8,128)(2,1)S(1)}, u32[]{:S(2)}, u32[]{:S(2)}) collective-permute-start(bf16[64,512]{1,0:T(8,128)(2,1)S(1)} %get-tuple-element.54), channel_id=1, source_target_pairs={{0,1},{1,0},{2,3},{3,2},{4,5},{5,4},{6,7},{7,6},{8,9},{9,8},{10,11... | collective-permute-start | bytes 196616 | tf_op jit(solution)/shard_map/ppermute | solution.py:325
  1.8 2.6 %collective-permute-start = (bf16[64,256]{1,0:T(8,128)(2,1)S(1)}, bf16[64,256]{1,0:T(8,128)(2,1)S(1)}, u32[]{:S(2)}, u32[]{:S(2)}) collective-permute-start(bf16[64,256]{1,0:T(8,128)(2,1)S(1)} %get-tuple-element.50._), channel_id=1, source_target_pairs={{0,3},{1,2},{2,1},{3,0},{4,7},{5,6},{6,5},{7,4},{8,11},{9,10},{10,... | collective-permute-start | bytes 98312 | tf_op jit(solution)/shard_map/ppermute | solution.py:340
  4.5 1.1 %first_local.1 = (f32[256,512]{1,0:T(8,128)S(1)}, f32[256,512]{1,0:T(8,128)S(1)}, bf16[256,256]{1,0:T(8,128)(2,1)S(1)}, bf16[256,128]{1,0:T(8,128)(2,1)S(1)}, f32[256,1]{1,0:T(8,128)S(1)}) custom-call(f32[1,256,512]{2,1,0:T(8,128)S(1)} %copy-done.3, bf16[64,256]{1,0:T(8,128)(2,1)S(1)} %get-tuple-element.50._, s32[3,1,4,5]{3,2,1,0:T(4,128)S(1)} %get-tuple-element.51.cols, ...), custom_call_target="tpu_custom_call" | custom-call | flops 67108864 | bytes 1048816 | tf_op jit(solution)/shard_map/first_local/pallas_call | solution.py:52
  5.6 0.5 %collective-permute-done.outer = bf16[64,256]{1,0:T(8,128)(2,1)S(1)} collective-permute-done((bf16[64,256]{1,0:T(8,128)(2,1)S(1)}, bf16[64,256]{1,0:T(8,128)(2,1)S(1)}, u32[]{:S(2)}, u32[]{:S(2)}) %collective-permute-start) | collective-permute-done | bytes 32800 | tf_op jit(solution)/shard_map/ppermute | solution.py:340
  6.1 0.2 first_residual.2
  6.3 1.7 %collective-permute-start.2 = (bf16[256,128]{1,0:T(8,128)(2,1)S(1)}, bf16[256,128]{1,0:T(8,128)(2,1)S(1)}, u32[]{:S(2)}, u32[]{:S(2)}) collective-permute-start(bf16[256,128]{1,0:T(8,128)(2,1)S(1)} %get-tuple-element.55._), channel_id=1, source_target_pairs={{0,4},{4,0},{8,12},{12,8},{16,20},{20,16},{24,28},{28,24},{1,5},{5... | collective-permute-start | bytes 196616 | tf_op jit(solution)/shard_map/ppermute | solution.py:325
  8.0 0.2 first_residual.3
  8.2 1.4 %collective-permute-start.6 = (bf16[256,128]{1,0:T(8,128)(2,1)S(1)}, bf16[256,128]{1,0:T(8,128)(2,1)S(1)}, u32[]{:S(2)}, u32[]{:S(2)}) collective-permute-start(bf16[256,128]{1,0:T(8,128)(2,1)S(1)} %get-tuple-element.67), channel_id=1, source_target_pairs={{0,4},{4,0},{8,12},{12,8},{16,20},{20,16},{24,28},{28,24},{1,5},{5... | collective-permute-start | bytes 196616 | tf_op jit(solution)/shard_map/ppermute | solution.py:325
  9.6 1.1 %operators.2 = (bf16[256,512]{1,0:T(8,128)(2,1)S(1)}, bf16[256,256]{1,0:T(8,128)(2,1)S(1)}, bf16[256,128]{1,0:T(8,128)(2,1)S(1)}, f32[256,1]{1,0:T(8,128)S(1)}) custom-call(bf16[256,128]{1,0:T(8,128)(2,1)S(1)} %get-tuple-element.55._, s32[3,3,1,4]{3,2,1,0:T(1,128)S(1)} %bitcast.2, bf16[3,1,4,3,64,64]{5,4,3,2,1,0:T(8,128)(2,1)S(1)} %copy-done.1, ...), custom_call_target="tpu_custom_call" | custom-call | bytes 852352 | tf_op jit(solution)/shard_map/operators/pallas_call | solution.py:52
  10.8 0.2 join.3
  11.0 1.6 %collective-permute-start.3 = (bf16[64,128]{1,0:T(8,128)(2,1)S(1)}, bf16[64,128]{1,0:T(8,128)(2,1)S(1)}, u32[]{:S(2)}, u32[]{:S(2)}) collective-permute-start(bf16[64,128]{1,0:T(8,128)(2,1)S(1)} %get-tuple-element.63), channel_id=1, source_target_pairs={{0,3},{1,2},{2,1},{3,0},{4,7},{5,6},{6,5},{7,4},{8,11},{9,10},{10,... | collective-permute-start | bytes 49160 | tf_op jit(solution)/shard_map/ppermute | solution.py:340
  12.6 0.6 %collective-permute-start.4 = (bf16[64,128]{1,0:T(8,128)(2,1)S(1)}, bf16[64,128]{1,0:T(8,128)(2,1)S(1)}, u32[]{:S(2)}, u32[]{:S(2)}) collective-permute-start(bf16[64,128]{1,0:T(8,128)(2,1)S(1)} %get-tuple-element.64), channel_id=1, source_target_pairs={{0,1},{1,0},{2,3},{3,2},{4,5},{5,4},{6,7},{7,6},{8,9},{9,8},{10,11... | collective-permute-start | bytes 49160 | tf_op jit(solution)/shard_map/ppermute | solution.py:325
  13.2 0.2 join.4
  13.4 0.8 %collective-permute-start.7 = (bf16[64,128]{1,0:T(8,128)(2,1)S(1)}, bf16[64,128]{1,0:T(8,128)(2,1)S(1)}, u32[]{:S(2)}, u32[]{:S(2)}) collective-permute-start(bf16[64,128]{1,0:T(8,128)(2,1)S(1)} %get-tuple-element.72), channel_id=1, source_target_pairs={{0,3},{1,2},{2,1},{3,0},{4,7},{5,6},{6,5},{7,4},{8,11},{9,10},{10,... | collective-permute-start | bytes 49160 | tf_op jit(solution)/shard_map/ppermute | solution.py:340
  14.2 0.6 %collective-permute-start.8 = (bf16[64,128]{1,0:T(8,128)(2,1)S(1)}, bf16[64,128]{1,0:T(8,128)(2,1)S(1)}, u32[]{:S(2)}, u32[]{:S(2)}) collective-permute-start(bf16[64,128]{1,0:T(8,128)(2,1)S(1)} %get-tuple-element.73), channel_id=1, source_target_pairs={{0,1},{1,0},{2,3},{3,2},{4,5},{5,4},{6,7},{7,6},{8,9},{9,8},{10,11... | collective-permute-start | bytes 49160 | tf_op jit(solution)/shard_map/ppermute | solution.py:325
  14.9 0.2 local.3.left
  15.1 0.2 residual.3
  15.3 1.6 %collective-permute-start.9 = (bf16[256,128]{1,0:T(8,128)(2,1)S(1)}, bf16[256,128]{1,0:T(8,128)(2,1)S(1)}, u32[]{:S(2)}, u32[]{:S(2)}) collective-permute-start(bf16[256,128]{1,0:T(8,128)(2,1)S(1)} %get-tuple-element.69._.refs_0_), channel_id=1, source_target_pairs={{0,8},{4,12},{8,0},{12,4},{16,24},{20,28},{24,16},{28,20},{1,9},{5... | collective-permute-start | bytes 196616 | tf_op jit(solution)/shard_map/ppermute | solution.py:325
  16.9 1.3 %collective-permute-start.12 = (bf16[256,128]{1,0:T(8,128)(2,1)S(1)}, bf16[256,128]{1,0:T(8,128)(2,1)S(1)}, u32[]{:S(2)}, u32[]{:S(2)}) collective-permute-start(bf16[256,128]{1,0:T(8,128)(2,1)S(1)} %get-tuple-element.83.near), channel_id=1, source_target_pairs={{0,4},{4,0},{8,12},{12,8},{16,20},{20,16},{24,28},{28,24},{1,5},{5... | collective-permute-start | bytes 196616 | tf_op jit(solution)/shard_map/ppermute | solution.py:325
  18.2 0.2 local.4.left
  18.6 1.1 %operators.3 = (bf16[256,512]{1,0:T(8,128)(2,1)S(1)}, bf16[256,256]{1,0:T(8,128)(2,1)S(1)}, bf16[256,128]{1,0:T(8,128)(2,1)S(1)}, f32[256,1]{1,0:T(8,128)S(1)}) custom-call(bf16[256,128]{1,0:T(8,128)(2,1)S(1)} %get-tuple-element.69._.refs_0_, s32[3,3,1,4]{3,2,1,0:T(1,128)S(1)} %bitcast.3, bf16[3,1,4,3,64,64]{5,4,3,2,1,0:T(8,128)(2,1)S(1)} %copy-done.1, ...), custom_call_target="tpu_custom_call" | custom-call | bytes 852352 | tf_op jit(solution)/shard_map/operators/pallas_call | solution.py:52
  19.7 0.2 join.5
  20.0 0.8 %collective-permute-start.10 = (bf16[64,128]{1,0:T(8,128)(2,1)S(1)}, bf16[64,128]{1,0:T(8,128)(2,1)S(1)}, u32[]{:S(2)}, u32[]{:S(2)}) collective-permute-start(bf16[64,128]{1,0:T(8,128)(2,1)S(1)} %get-tuple-element.80), channel_id=1, source_target_pairs={{0,3},{1,2},{2,1},{3,0},{4,7},{5,6},{6,5},{7,4},{8,11},{9,10},{10,... | collective-permute-start | bytes 49160 | tf_op jit(solution)/shard_map/ppermute | solution.py:340
  20.7 0.9 %collective-permute-start.11 = (bf16[64,128]{1,0:T(8,128)(2,1)S(1)}, bf16[64,128]{1,0:T(8,128)(2,1)S(1)}, u32[]{:S(2)}, u32[]{:S(2)}) collective-permute-start(bf16[64,128]{1,0:T(8,128)(2,1)S(1)} %get-tuple-element.81), channel_id=1, source_target_pairs={{0,1},{1,0},{2,3},{3,2},{4,5},{5,4},{6,7},{7,6},{8,9},{9,8},{10,11... | collective-permute-start | bytes 49160 | tf_op jit(solution)/shard_map/ppermute | solution.py:325
  21.6 0.7 %share.1 = bf16[256,256]{1,0:T(8,128)(2,1)S(1)} custom-call(bf16[256,128]{1,0:T(8,128)(2,1)S(1)} %get-tuple-element.77.smoothed._, s32[3,3,1,4]{3,2,1,0:T(1,128)S(1)} %bitcast.4, bf16[3,1,4,3,64,64]{5,4,3,2,1,0:T(8,128)(2,1)S(1)} %copy-done.1), custom_call_target="tpu_custom_call" | custom-call | bytes 360592 | tf_op jit(solution)/shard_map/share/pallas_call | solution.py:52
  22.3 0.2 local.5.left
  22.5 0.8 %collective-permute-done.10.outer = bf16[64,128]{1,0:T(8,128)(2,1)S(1)} collective-permute-done((bf16[64,128]{1,0:T(8,128)(2,1)S(1)}, bf16[64,128]{1,0:T(8,128)(2,1)S(1)}, u32[]{:S(2)}, u32[]{:S(2)}) %collective-permute-start.10) | collective-permute-done | bytes 16416 | tf_op jit(solution)/shard_map/ppermute | solution.py:340
  23.4 0.3 residual.5
  23.7 3.4 %collective-permute-start.15 = (bf16[256,128]{1,0:T(8,128)(2,1)S(1)}, bf16[256,128]{1,0:T(8,128)(2,1)S(1)}, u32[]{:S(2)}, u32[]{:S(2)}) collective-permute-start(bf16[256,128]{1,0:T(8,128)(2,1)S(1)} %get-tuple-element.82.refs_0_._.own), channel_id=1, source_target_pairs={{0,18},{1,19},{2,16},{3,17},{4,22},{5,23},{6,20},{7,21},{8,26},{9,... | collective-permute-start | bytes 196616 | tf_op jit(solution)/shard_map/ppermute | solution.py:334
  27.1 0.7 %collective-permute-start.16 = (bf16[256,128]{1,0:T(8,128)(2,1)S(1)}, bf16[256,128]{1,0:T(8,128)(2,1)S(1)}, u32[]{:S(2)}, u32[]{:S(2)}) collective-permute-start(bf16[256,128]{1,0:T(8,128)(2,1)S(1)} %get-tuple-element.82.refs_0_._.own), channel_id=1, source_target_pairs={{0,2},{1,3},{2,0},{3,1},{4,6},{5,7},{6,4},{7,5},{8,10},{9,11},{10,... | collective-permute-start | bytes 196616 | tf_op jit(solution)/shard_map/ppermute | solution.py:325
  27.8 0.3 collective-permute-start.13
  28.2 0.7 %copy-done.6 = s32[3,1,4,2]{2,3,1,0:T(2,128)S(1)} copy-done((s32[3,1,4,2]{2,3,1,0:T(2,128)S(1)}, s32[3,1,4,2]{2,3,1,0:T(2,128)}, u32[]{:S(2)}) %copy-start.6) | copy-done | bytes 120
  28.9 1.2 %fine_operators.1 = (bf16[256,256]{1,0:T(8,128)(2,1)S(1)}, bf16[256,256]{1,0:T(8,128)(2,1)S(1)}, bf16[256,256]{1,0:T(8,128)(2,1)S(1)}, f32[256,256]{1,0:T(8,128)S(1)}) custom-call(bf16[256,128]{1,0:T(8,128)(2,1)S(1)} %get-tuple-element.82.refs_0_._.own, s32[3,1,2,4]{3,2,1,0:T(2,128)S(1)} %bitcast.5, bf16[3,1,4,2,64,64]{5,4,3,2,1,0:T(8,128)(2,1)S(1)} %copy-done.2, ...), custom_call_target="tpu_custom_call" | custom-call | flops 134217728 | bytes 1378400 | tf_op jit(solution)/shard_map/fine_operators/pallas_call | solution.py:52
  30.1 1.1 %coarse_operators.1.refs_0_.inverse = bf16[256,1024]{1,0:T(8,128)(2,1)S(1)} custom-call(bf16[256,128]{1,0:T(8,128)(2,1)S(1)} %get-tuple-element.82.refs_0_._.own, bf16[256,128]{1,0:T(8,128)(2,1)S(1)} %collective-permute-done.12.refs_1_.far, s32[3,1,2,4]{3,2,1,0:T(2,128)S(1)} %bitcast.6, bf16[256,1024]{1,0:T(8,128)(2,1)S(1)} %copy-done.4, ...), custom_call_target="tpu_custom_call" | custom-call | flops 201326592 | bytes 984160 | tf_op jit(solution)/shard_map/coarse_operators/pallas_call | solution.py:52
  31.2 0.6 %collective-permute-done.16.own = bf16[256,128]{1,0:T(8,128)(2,1)S(1)} collective-permute-done((bf16[256,128]{1,0:T(8,128)(2,1)S(1)}, bf16[256,128]{1,0:T(8,128)(2,1)S(1)}, u32[]{:S(2)}, u32[]{:S(2)}) %collective-permute-start.16) | collective-permute-done | bytes 65568 | tf_op jit(solution)/shard_map/ppermute | solution.py:325
  31.9 1.1 %collective-permute-done.13.far = bf16[256,128]{1,0:T(8,128)(2,1)S(1)} collective-permute-done((bf16[256,128]{1,0:T(8,128)(2,1)S(1)}, bf16[256,128]{1,0:T(8,128)(2,1)S(1)}, u32[]{:S(2)}, u32[]{:S(2)}) %collective-permute-start.13) | collective-permute-done | bytes 65568 | tf_op jit(solution)/shard_map/ppermute | solution.py:334
  33.1 0.2 coarse.1.refs_2_
  33.3 1.0 %collective-permute-done.14.refs_0_ = bf16[256,128]{1,0:T(8,128)(2,1)S(1)} collective-permute-done((bf16[256,128]{1,0:T(8,128)(2,1)S(1)}, bf16[256,128]{1,0:T(8,128)(2,1)S(1)}, u32[]{:S(2)}, u32[]{:S(2)}) %collective-permute-start.14) | collective-permute-done | bytes 65568 | tf_op jit(solution)/shard_map/ppermute | solution.py:325
  34.3 0.4 up.1
  34.8 2.3 %collective-permute-start.20 = (bf16[256,128]{1,0:T(8,128)(2,1)S(1)}, bf16[256,128]{1,0:T(8,128)(2,1)S(1)}, u32[]{:S(2)}, u32[]{:S(2)}) collective-permute-start(bf16[256,128]{1,0:T(8,128)(2,1)S(1)} %get-tuple-element.90), channel_id=1, source_target_pairs={{0,12},{4,8},{8,4},{12,0},{16,28},{20,24},{24,20},{28,16},{1,13},{... | collective-permute-start | bytes 196616 | tf_op jit(solution)/shard_map/ppermute | solution.py:325
  37.0 0.8 %collective-permute-start.18 = (bf16[256,128]{1,0:T(8,128)(2,1)S(1)}, bf16[256,128]{1,0:T(8,128)(2,1)S(1)}, u32[]{:S(2)}, u32[]{:S(2)}) collective-permute-start(bf16[256,128]{1,0:T(8,128)(2,1)S(1)} %get-tuple-element.90), channel_id=1, source_target_pairs={{0,8},{4,12},{8,0},{12,4},{16,24},{20,28},{24,16},{28,20},{1,9},{5... | collective-permute-start | bytes 196616 | tf_op jit(solution)/shard_map/ppermute | solution.py:325
  37.8 0.5 %collective-permute-start.19 = (bf16[256,128]{1,0:T(8,128)(2,1)S(1)}, bf16[256,128]{1,0:T(8,128)(2,1)S(1)}, u32[]{:S(2)}, u32[]{:S(2)}) collective-permute-start(bf16[256,128]{1,0:T(8,128)(2,1)S(1)} %get-tuple-element.91.refs_0_), channel_id=1, source_target_pairs={{0,4},{4,0},{8,12},{12,8},{16,20},{20,16},{24,28},{28,24},{1,5},{5... | collective-permute-start | bytes 196616 | tf_op jit(solution)/shard_map/ppermute | solution.py:325
  38.3 0.8 %output.3.refs_5_ = f32[1,256,512]{2,1,0:T(8,128)} custom-call(bf16[256,128]{1,0:T(8,128)(2,1)S(1)} %get-tuple-element.91.refs_0_, f32[256,512]{1,0:T(8,128)S(1)} %get-tuple-element.86.base.refs_1_.refs_2_, bf16[256,256]{1,0:T(8,128)(2,1)S(1)} %get-tuple-element.92.refs_2_.refs_3_, f32[256,256]{1,0:T(8,128)S(1)} %get-tuple-element.93.refs_3_.refs_4_, ...), custom_call_target="tpu_custom_call" | custom-call | flops 16777216 | bytes 1114112 | tf_op jit(solution)/shard_map/output/pallas_call | solution.py:52
  39.2 1.3 %collective-permute-done.20.refs_0_ = bf16[256,128]{1,0:T(8,128)(2,1)S(1)} collective-permute-done((bf16[256,128]{1,0:T(8,128)(2,1)S(1)}, bf16[256,128]{1,0:T(8,128)(2,1)S(1)}, u32[]{:S(2)}, u32[]{:S(2)}) %collective-permute-start.20) | collective-permute-done | bytes 65568 | tf_op jit(solution)/shard_map/ppermute | solution.py:325
  40.5 0.8 %output.4.refs_6_ = f32[1,256,512]{2,1,0:T(8,128)} custom-call(bf16[256,128]{1,0:T(8,128)(2,1)S(1)} %collective-permute-done.20.refs_0_, f32[256,512]{1,0:T(8,128)S(1)} %get-tuple-element.86.base.refs_1_.refs_2_, bf16[256,256]{1,0:T(8,128)(2,1)S(1)} %get-tuple-element.92.refs_2_.refs_3_, ...), custom_call_target="tpu_custom_call", output_to_operand_aliasing={{}: (5, {})} | custom-call | flops 16777216 | bytes 1638400 | tf_op jit(solution)/shard_map/output/pallas_call | solution.py:52
  41.4 0.6 %collective-permute-done.19.refs_1_ = bf16[256,128]{1,0:T(8,128)(2,1)S(1)} collective-permute-done((bf16[256,128]{1,0:T(8,128)(2,1)S(1)}, bf16[256,128]{1,0:T(8,128)(2,1)S(1)}, u32[]{:S(2)}, u32[]{:S(2)}) %collective-permute-start.19) | collective-permute-done | bytes 65568 | tf_op jit(solution)/shard_map/ppermute | solution.py:325
  42.1 0.9 %output.5 = f32[1,256,512]{2,1,0:T(8,128)} custom-call(bf16[256,128]{1,0:T(8,128)(2,1)S(1)} %collective-permute-done.18.refs_0_, bf16[256,128]{1,0:T(8,128)(2,1)S(1)} %collective-permute-done.19.refs_1_, f32[256,512]{1,0:T(8,128)S(1)} %get-tuple-element.86.base.refs_1_.refs_2_, ...), custom_call_target="tpu_custom_call", output_to_operand_aliasing={{}: (6, {})} | custom-call | flops 33554432 | bytes 1703936 | tf_op jit(solution)/shard_map/output/pallas_call | solution.py:52
  (33 shorter events, 0.5 us)
Async XLA Ops:
  0.0 4.4 %copy-start = (bf16[3,1,4,5,64,64]{5,4,3,2,1,0:T(8,128)(2,1)S(1)}, bf16[3,1,4,5,64,64]{5,4,3,2,1,0:T(8,128)(2,1)}, u32[]{:S(2)}) copy-start(bf16[3,1,4,5,64,64]{5,4,3,2,1,0:T(8,128)(2,1)} %blocks.7) | copy-start | bytes 1474564
  0.0 4.4 %copy-start.3 = (f32[1,256,512]{2,1,0:T(8,128)S(1)}, f32[1,256,512]{2,1,0:T(8,128)}, u32[]{:S(2)}) copy-start(f32[1,256,512]{2,1,0:T(8,128)} %rhs.3) | copy-start | bytes 1572868
  1.3 4.8 %collective-permute-start.1 = (bf16[64,512]{1,0:T(8,128)(2,1)S(1)}, bf16[64,512]{1,0:T(8,128)(2,1)S(1)}, u32[]{:S(2)}, u32[]{:S(2)}) collective-permute-start(bf16[64,512]{1,0:T(8,128)(2,1)S(1)} %get-tuple-element.54), channel_id=1, source_target_pairs={{0,1},{1,0},{2,3},{3,2},{4,5},{5,4},{6,7},{7,6},{8,9},{9,8},{10,11... | collective-permute-start | bytes 196616 | tf_op jit(solution)/shard_map/ppermute | solution.py:325
  1.8 4.3 %collective-permute-start = (bf16[64,256]{1,0:T(8,128)(2,1)S(1)}, bf16[64,256]{1,0:T(8,128)(2,1)S(1)}, u32[]{:S(2)}, u32[]{:S(2)}) collective-permute-start(bf16[64,256]{1,0:T(8,128)(2,1)S(1)} %get-tuple-element.50._), channel_id=1, source_target_pairs={{0,3},{1,2},{2,1},{3,0},{4,7},{5,6},{6,5},{7,4},{8,11},{9,10},{10,... | collective-permute-start | bytes 98312 | tf_op jit(solution)/shard_map/ppermute | solution.py:340
  4.4 3.6 %collective-permute-start.5 = (bf16[64,256]{1,0:T(8,128)(2,1)S(1)}, bf16[64,256]{1,0:T(8,128)(2,1)S(1)}, u32[]{:S(2)}, u32[]{:S(2)}) collective-permute-start(bf16[64,256]{1,0:T(8,128)(2,1)S(1)} %get-tuple-element.65), channel_id=1, source_target_pairs={{0,3},{1,2},{2,1},{3,0},{4,7},{5,6},{6,5},{7,4},{8,11},{9,10},{10,... | collective-permute-start | bytes 98312 | tf_op jit(solution)/shard_map/ppermute | solution.py:340
  6.1 3.5 %copy-start.1 = (bf16[3,1,4,3,64,64]{5,4,3,2,1,0:T(8,128)(2,1)S(1)}, bf16[3,1,4,3,64,64]{5,4,3,2,1,0:T(8,128)(2,1)}, u32[]{:S(2)}) copy-start(bf16[3,1,4,3,64,64]{5,4,3,2,1,0:T(8,128)(2,1)} %rblocks.5) | copy-start | bytes 884740
  6.3 4.5 %collective-permute-start.2 = (bf16[256,128]{1,0:T(8,128)(2,1)S(1)}, bf16[256,128]{1,0:T(8,128)(2,1)S(1)}, u32[]{:S(2)}, u32[]{:S(2)}) collective-permute-start(bf16[256,128]{1,0:T(8,128)(2,1)S(1)} %get-tuple-element.55._), channel_id=1, source_target_pairs={{0,4},{4,0},{8,12},{12,8},{16,20},{20,16},{24,28},{28,24},{1,5},{5... | collective-permute-start | bytes 196616 | tf_op jit(solution)/shard_map/ppermute | solution.py:325
  8.0 1.6 %copy-start.5 = (s32[3,1,4,3]{2,1,3,0:T(1,128)S(1)}, s32[3,1,4,3]{2,1,3,0:T(1,128)}, u32[]{:S(2)}) copy-start(s32[3,1,4,3]{2,1,3,0:T(1,128)} %param.11) | copy-start | bytes 436
  8.2 5.0 %collective-permute-start.6 = (bf16[256,128]{1,0:T(8,128)(2,1)S(1)}, bf16[256,128]{1,0:T(8,128)(2,1)S(1)}, u32[]{:S(2)}, u32[]{:S(2)}) collective-permute-start(bf16[256,128]{1,0:T(8,128)(2,1)S(1)} %get-tuple-element.67), channel_id=1, source_target_pairs={{0,4},{4,0},{8,12},{12,8},{16,20},{20,16},{24,28},{28,24},{1,5},{5... | collective-permute-start | bytes 196616 | tf_op jit(solution)/shard_map/ppermute | solution.py:325
  11.0 4.1 %collective-permute-start.3 = (bf16[64,128]{1,0:T(8,128)(2,1)S(1)}, bf16[64,128]{1,0:T(8,128)(2,1)S(1)}, u32[]{:S(2)}, u32[]{:S(2)}) collective-permute-start(bf16[64,128]{1,0:T(8,128)(2,1)S(1)} %get-tuple-element.63), channel_id=1, source_target_pairs={{0,3},{1,2},{2,1},{3,0},{4,7},{5,6},{6,5},{7,4},{8,11},{9,10},{10,... | collective-permute-start | bytes 49160 | tf_op jit(solution)/shard_map/ppermute | solution.py:340
  12.6 2.5 %collective-permute-start.4 = (bf16[64,128]{1,0:T(8,128)(2,1)S(1)}, bf16[64,128]{1,0:T(8,128)(2,1)S(1)}, u32[]{:S(2)}, u32[]{:S(2)}) collective-permute-start(bf16[64,128]{1,0:T(8,128)(2,1)S(1)} %get-tuple-element.64), channel_id=1, source_target_pairs={{0,1},{1,0},{2,3},{3,2},{4,5},{5,4},{6,7},{7,6},{8,9},{9,8},{10,11... | collective-permute-start | bytes 49160 | tf_op jit(solution)/shard_map/ppermute | solution.py:325
  13.4 5.0 %collective-permute-start.7 = (bf16[64,128]{1,0:T(8,128)(2,1)S(1)}, bf16[64,128]{1,0:T(8,128)(2,1)S(1)}, u32[]{:S(2)}, u32[]{:S(2)}) collective-permute-start(bf16[64,128]{1,0:T(8,128)(2,1)S(1)} %get-tuple-element.72), channel_id=1, source_target_pairs={{0,3},{1,2},{2,1},{3,0},{4,7},{5,6},{6,5},{7,4},{8,11},{9,10},{10,... | collective-permute-start | bytes 49160 | tf_op jit(solution)/shard_map/ppermute | solution.py:340
  14.2 4.2 %collective-permute-start.8 = (bf16[64,128]{1,0:T(8,128)(2,1)S(1)}, bf16[64,128]{1,0:T(8,128)(2,1)S(1)}, u32[]{:S(2)}, u32[]{:S(2)}) collective-permute-start(bf16[64,128]{1,0:T(8,128)(2,1)S(1)} %get-tuple-element.73), channel_id=1, source_target_pairs={{0,1},{1,0},{2,3},{3,2},{4,5},{5,4},{6,7},{7,6},{8,9},{9,8},{10,11... | collective-permute-start | bytes 49160 | tf_op jit(solution)/shard_map/ppermute | solution.py:325
  15.3 4.5 %collective-permute-start.9 = (bf16[256,128]{1,0:T(8,128)(2,1)S(1)}, bf16[256,128]{1,0:T(8,128)(2,1)S(1)}, u32[]{:S(2)}, u32[]{:S(2)}) collective-permute-start(bf16[256,128]{1,0:T(8,128)(2,1)S(1)} %get-tuple-element.69._.refs_0_), channel_id=1, source_target_pairs={{0,8},{4,12},{8,0},{12,4},{16,24},{20,28},{24,16},{28,20},{1,9},{5... | collective-permute-start | bytes 196616 | tf_op jit(solution)/shard_map/ppermute | solution.py:325
  16.9 11.3 %collective-permute-start.12 = (bf16[256,128]{1,0:T(8,128)(2,1)S(1)}, bf16[256,128]{1,0:T(8,128)(2,1)S(1)}, u32[]{:S(2)}, u32[]{:S(2)}) collective-permute-start(bf16[256,128]{1,0:T(8,128)(2,1)S(1)} %get-tuple-element.83.near), channel_id=1, source_target_pairs={{0,4},{4,0},{8,12},{12,8},{16,20},{20,16},{24,28},{28,24},{1,5},{5... | collective-permute-start | bytes 196616 | tf_op jit(solution)/shard_map/ppermute | solution.py:325
  20.0 3.4 %collective-permute-start.10 = (bf16[64,128]{1,0:T(8,128)(2,1)S(1)}, bf16[64,128]{1,0:T(8,128)(2,1)S(1)}, u32[]{:S(2)}, u32[]{:S(2)}) collective-permute-start(bf16[64,128]{1,0:T(8,128)(2,1)S(1)} %get-tuple-element.80), channel_id=1, source_target_pairs={{0,3},{1,2},{2,1},{3,0},{4,7},{5,6},{6,5},{7,4},{8,11},{9,10},{10,... | collective-permute-start | bytes 49160 | tf_op jit(solution)/shard_map/ppermute | solution.py:340
  20.7 2.7 %collective-permute-start.11 = (bf16[64,128]{1,0:T(8,128)(2,1)S(1)}, bf16[64,128]{1,0:T(8,128)(2,1)S(1)}, u32[]{:S(2)}, u32[]{:S(2)}) collective-permute-start(bf16[64,128]{1,0:T(8,128)(2,1)S(1)} %get-tuple-element.81), channel_id=1, source_target_pairs={{0,1},{1,0},{2,3},{3,2},{4,5},{5,4},{6,7},{7,6},{8,9},{9,8},{10,11... | collective-permute-start | bytes 49160 | tf_op jit(solution)/shard_map/ppermute | solution.py:325
  22.5 5.7 %copy-start.2 = (bf16[3,1,4,2,64,64]{5,4,3,2,1,0:T(8,128)(2,1)S(1)}, bf16[3,1,4,2,64,64]{5,4,3,2,1,0:T(8,128)(2,1)}, u32[]{:S(2)}) copy-start(bf16[3,1,4,2,64,64]{5,4,3,2,1,0:T(8,128)(2,1)} %blocks_1.1) | copy-start | bytes 589828
  23.7 7.5 %collective-permute-start.15 = (bf16[256,128]{1,0:T(8,128)(2,1)S(1)}, bf16[256,128]{1,0:T(8,128)(2,1)S(1)}, u32[]{:S(2)}, u32[]{:S(2)}) collective-permute-start(bf16[256,128]{1,0:T(8,128)(2,1)S(1)} %get-tuple-element.82.refs_0_._.own), channel_id=1, source_target_pairs={{0,18},{1,19},{2,16},{3,17},{4,22},{5,23},{6,20},{7,21},{8,26},{9,... | collective-permute-start | bytes 196616 | tf_op jit(solution)/shard_map/ppermute | solution.py:334
  27.1 4.7 %collective-permute-start.16 = (bf16[256,128]{1,0:T(8,128)(2,1)S(1)}, bf16[256,128]{1,0:T(8,128)(2,1)S(1)}, u32[]{:S(2)}, u32[]{:S(2)}) collective-permute-start(bf16[256,128]{1,0:T(8,128)(2,1)S(1)} %get-tuple-element.82.refs_0_._.own), channel_id=1, source_target_pairs={{0,2},{1,3},{2,0},{3,1},{4,6},{5,7},{6,4},{7,5},{8,10},{9,11},{10,... | collective-permute-start | bytes 196616 | tf_op jit(solution)/shard_map/ppermute | solution.py:325
  27.8 5.2 %collective-permute-start.13 = (bf16[256,128]{1,0:T(8,128)(2,1)S(1)}, bf16[256,128]{1,0:T(8,128)(2,1)S(1)}, u32[]{:S(2)}, u32[]{:S(2)}) collective-permute-start(bf16[256,128]{1,0:T(8,128)(2,1)S(1)} %get-tuple-element.82.refs_0_._.own), channel_id=1, source_target_pairs={{0,16},{1,17},{2,18},{3,19},{4,20},{5,21},{6,22},{7,23},{8,24},{9,... | collective-permute-start | bytes 196616 | tf_op jit(solution)/shard_map/ppermute | solution.py:334
  28.2 0.7 %copy-start.6 = (s32[3,1,4,2]{2,3,1,0:T(2,128)S(1)}, s32[3,1,4,2]{2,3,1,0:T(2,128)}, u32[]{:S(2)}) copy-start(s32[3,1,4,2]{2,3,1,0:T(2,128)} %param.13) | copy-start | bytes 292
  28.9 1.2 %copy-start.4 = (bf16[256,1024]{1,0:T(8,128)(2,1)S(1)}, bf16[256,1024]{1,0:T(8,128)(2,1)}, u32[]{:S(2)}) copy-start(bf16[256,1024]{1,0:T(8,128)(2,1)} %refs_3_.1) | copy-start | bytes 1572868
  31.8 1.5 %collective-permute-start.17 = (bf16[256,128]{1,0:T(8,128)(2,1)S(1)}, bf16[256,128]{1,0:T(8,128)(2,1)S(1)}, u32[]{:S(2)}, u32[]{:S(2)}) collective-permute-start(bf16[256,128]{1,0:T(8,128)(2,1)S(1)} %share_sum.3.refs_0_), channel_id=1, source_target_pairs={{0,1},{1,0},{2,3},{3,2},{4,5},{5,4},{6,7},{7,6},{8,9},{9,8},{10,11... | collective-permute-start | bytes 196616 | tf_op jit(solution)/shard_map/ppermute | solution.py:325
  33.0 1.3 %collective-permute-start.14 = (bf16[256,128]{1,0:T(8,128)(2,1)S(1)}, bf16[256,128]{1,0:T(8,128)(2,1)S(1)}, u32[]{:S(2)}, u32[]{:S(2)}) collective-permute-start(bf16[256,128]{1,0:T(8,128)(2,1)S(1)} %share_sum.2.refs_1_), channel_id=1, source_target_pairs={{0,1},{1,0},{2,3},{3,2},{4,5},{5,4},{6,7},{7,6},{8,9},{9,8},{10,11... | collective-permute-start | bytes 196616 | tf_op jit(solution)/shard_map/ppermute | solution.py:325
  34.8 5.7 %collective-permute-start.20 = (bf16[256,128]{1,0:T(8,128)(2,1)S(1)}, bf16[256,128]{1,0:T(8,128)(2,1)S(1)}, u32[]{:S(2)}, u32[]{:S(2)}) collective-permute-start(bf16[256,128]{1,0:T(8,128)(2,1)S(1)} %get-tuple-element.90), channel_id=1, source_target_pairs={{0,12},{4,8},{8,4},{12,0},{16,28},{20,24},{24,20},{28,16},{1,13},{... | collective-permute-start | bytes 196616 | tf_op jit(solution)/shard_map/ppermute | solution.py:325
  37.0 4.4 %collective-permute-start.18 = (bf16[256,128]{1,0:T(8,128)(2,1)S(1)}, bf16[256,128]{1,0:T(8,128)(2,1)S(1)}, u32[]{:S(2)}, u32[]{:S(2)}) collective-permute-start(bf16[256,128]{1,0:T(8,128)(2,1)S(1)} %get-tuple-element.90), channel_id=1, source_target_pairs={{0,8},{4,12},{8,0},{12,4},{16,24},{20,28},{24,16},{28,20},{1,9},{5... | collective-permute-start | bytes 196616 | tf_op jit(solution)/shard_map/ppermute | solution.py:325
  37.8 4.3 %collective-permute-start.19 = (bf16[256,128]{1,0:T(8,128)(2,1)S(1)}, bf16[256,128]{1,0:T(8,128)(2,1)S(1)}, u32[]{:S(2)}, u32[]{:S(2)}) collective-permute-start(bf16[256,128]{1,0:T(8,128)(2,1)S(1)} %get-tuple-element.91.refs_0_), channel_id=1, source_target_pairs={{0,4},{4,0},{8,12},{12,8},{16,20},{20,16},{24,28},{28,24},{1,5},{5... | collective-permute-start | bytes 196616 | tf_op jit(solution)/shard_map/ppermute | solution.py:325

commit v17 on v14

--- a/solution.py
+++ b/solution.py
@@ -184,8 +184,8 @@
 
 
 def first_residual_kernel(places, rest, rim, outer, inner, *refs):
-    width = refs[0].shape[1]
-    for slot, (ref, place) in enumerate(zip(refs, places)):
+    width = refs[-1].shape[1]
+    for slot, (ref, place) in enumerate(zip(refs[-2:], places)):
         lanes = lanes_of(place, width)
         columns = pl.ds(slot * width, width)
         rims = jnp.concatenate([inner[:, lanes], outer[:, columns]], axis=0)
@@ -394,14 +394,16 @@
         [level_rhs, first, gcols, of_level(galerkin_blocks, 0)], flops=flops(fields),
     )
     operators = [(scale, local)]
-    sent, kept = [], []
-    for places, outer in zip(pairs, outers):
-        far, near = run(
-            functools.partial(first_residual_kernel, places), "first_residual", [chunk_shape] * 2,
-            [rest, rim, outer, inner],
+    first_operands = [rest, rim, inner]
+
+    def first_chunk(slot, after):
+        rest, rim, inner = first_operands
+        return run(
+            functools.partial(first_residual_kernel, pairs[slot]), "first_residual",
+            [chunk_shape] * 2, [rest, rim, outers[slot], inner, *after],
         )
-        sent.append(far)
-        kept.append(near)
+
+    sent, kept = zip(first_chunk(0, ()))
     last = levels - 1
     bases = []
     anchor = sent[0]
@@ -415,6 +417,10 @@
              gcols, of_level(galerkin_blocks, level_idx + 1)],
         )
         operators.append((scale, local))
+        if level_idx == 0:
+            far, near = first_chunk(1, [scale])
+            other.append(exchange(far, "wide", 1))
+            kept = [kept[0], near]
         joined = []
         for near, far in zip(kept, other):
             rhs, smoothed, *ends = run(

time: 42.9 us -> 43.2 us (level)
  waiting for transfers between devices: 6.12 us -> 8.26 us
  starting transfers between devices: 22.9 us -> 21 us
    ppermute x5, waiting for transfers between devices: 1.16 us -> 2.27 us  [swap_outer(): return lax.ppermute(outer, 'narrow', gaps)]
    ppermute x2, starting transfers between devices: 4.06 us -> 3.05 us  [exchange_both(): return lax.ppermute(value, ('wide', 'narrow'), pairs)]
    ppermute x14, waiting for transfers between devices: 3.38 us -> 4.29 us  [exchange(): return lax.ppermute(value, axis, [(i, i ^ bit) for i in range(count)])]
    ppermute x14, starting transfers between devices: 12.9 us -> 12.1 us  [exchange(): return lax.ppermute(value, axis, [(i, i ^ bit) for i in range(count)])]
  transfers between devices with their start and end apart: 21 -> 21, of which waited for: 8 -> 9; matrix products, arithmetic and copies ran while one was open for 0% -> 0% of each run, Pallas kernels for 24% -> 24%
where the time goes in v17:
time: 43.2 us; the launch traced here: 43 us
  starting transfers between devices  21 us (49%)
  Pallas kernels  12.8 us (30%)
  waiting for transfers between devices  8.26 us (19%)
  local copies, waits for them, and re-layouts  0.71 us (2%)
    pallas_call x22, Pallas kernels, run(): pl.pallas_call(body, grid=(1,) if windows else (), out_shape=[out_space(o...  12.8 us
    ppermute x14, starting transfers between devices, exchange(): return lax.ppermute(value, axis, [(i, i ^ bit) for i in range(count)])  12.1 us
    ppermute x5, starting transfers between devices, swap_outer(): return lax.ppermute(outer, 'narrow', gaps)  5.85 us
    ppermute x14, waiting for transfers between devices, exchange(): return lax.ppermute(value, axis, [(i, i ^ bit) for i in range(count)])  4.29 us
    ppermute x2, starting transfers between devices, exchange_both(): return lax.ppermute(value, ('wide', 'narrow'), pairs)  3.05 us
    ppermute x5, waiting for transfers between devices, swap_outer(): return lax.ppermute(outer, 'narrow', gaps)  2.27 us
    ppermute x2, waiting for transfers between devices, exchange_both(): return lax.ppermute(value, ('wide', 'narrow'), pairs)  1.7 us
  transfers between devices with their start and end apart: 21, of which 9 were waited for; matrix products, arithmetic and copies ran while one was open for 0% of the time, Pallas kernels for 24%

profile of v17, /device:TPU:0, one launch (start us, length us, event | category | flops | bytes accessed | tf_op | source)
XLA Modules:
  0.0 43.0 jit_solution(91187531583279661)
XLA Ops:
  0.0 1.3 %start.1 = (s32[3,1,4,5]{3,2,1,0:T(4,128)S(1)}, bf16[64,512]{1,0:T(8,128)(2,1)S(1)}, bf16[64,256]{1,0:T(8,128)(2,1)S(1)}, bf16[64,256]{1,0:T(8,128)(2,1)S(1)}) custom-call(f32[1,256,512]{2,1,0:T(8,128)} %rhs.3, bf16[3,1,4,5,64,64]{5,4,3,2,1,0:T(8,128)(2,1)} %blocks.7, s32[3,1,4,5]{3,2,1,0:T(4,128)} %refs_0_.1), custom_call_target="tpu_custom_call" | custom-call | bytes 1016048 | tf_op jit(solution)/shard_map/start/pallas_call | solution.py:52
  1.3 0.5 %collective-permute-start.1 = (bf16[64,512]{1,0:T(8,128)(2,1)S(1)}, bf16[64,512]{1,0:T(8,128)(2,1)S(1)}, u32[]{:S(2)}, u32[]{:S(2)}) collective-permute-start(bf16[64,512]{1,0:T(8,128)(2,1)S(1)} %get-tuple-element.54), channel_id=1, source_target_pairs={{0,1},{1,0},{2,3},{3,2},{4,5},{5,4},{6,7},{7,6},{8,9},{9,8},{10,11... | collective-permute-start | bytes 196616 | tf_op jit(solution)/shard_map/ppermute | solution.py:323
  1.8 2.6 %collective-permute-start = (bf16[64,256]{1,0:T(8,128)(2,1)S(1)}, bf16[64,256]{1,0:T(8,128)(2,1)S(1)}, u32[]{:S(2)}, u32[]{:S(2)}) collective-permute-start(bf16[64,256]{1,0:T(8,128)(2,1)S(1)} %get-tuple-element.50._), channel_id=1, source_target_pairs={{0,3},{1,2},{2,1},{3,0},{4,7},{5,6},{6,5},{7,4},{8,11},{9,10},{10,... | collective-permute-start | bytes 98312 | tf_op jit(solution)/shard_map/ppermute | solution.py:338
  4.5 1.1 %first_local.1 = (f32[256,512]{1,0:T(8,128)S(1)}, f32[256,512]{1,0:T(8,128)S(1)}, bf16[256,256]{1,0:T(8,128)(2,1)S(1)}, bf16[256,128]{1,0:T(8,128)(2,1)S(1)}, f32[256,1]{1,0:T(8,128)S(1)}) custom-call(f32[1,256,512]{2,1,0:T(8,128)S(1)} %copy-done.3, bf16[64,256]{1,0:T(8,128)(2,1)S(1)} %get-tuple-element.50._, s32[3,1,4,5]{3,2,1,0:T(4,128)S(1)} %get-tuple-element.51.cols, ...), custom_call_target="tpu_custom_call" | custom-call | flops 67108864 | bytes 1048816 | tf_op jit(solution)/shard_map/first_local/pallas_call | solution.py:52
  5.6 0.5 %collective-permute-done.outer = bf16[64,256]{1,0:T(8,128)(2,1)S(1)} collective-permute-done((bf16[64,256]{1,0:T(8,128)(2,1)S(1)}, bf16[64,256]{1,0:T(8,128)(2,1)S(1)}, u32[]{:S(2)}, u32[]{:S(2)}) %collective-permute-start) | collective-permute-done | bytes 32800 | tf_op jit(solution)/shard_map/ppermute | solution.py:338
  6.1 0.2 first_residual.2
  6.3 1.7 %collective-permute-start.2 = (bf16[256,128]{1,0:T(8,128)(2,1)S(1)}, bf16[256,128]{1,0:T(8,128)(2,1)S(1)}, u32[]{:S(2)}, u32[]{:S(2)}) collective-permute-start(bf16[256,128]{1,0:T(8,128)(2,1)S(1)} %get-tuple-element.55._), channel_id=1, source_target_pairs={{0,4},{4,0},{8,12},{12,8},{16,20},{20,16},{24,28},{28,24},{1,5},{5... | collective-permute-start | bytes 196616 | tf_op jit(solution)/shard_map/ppermute | solution.py:323
  8.0 1.1 %operators.2 = (bf16[256,512]{1,0:T(8,128)(2,1)S(1)}, bf16[256,256]{1,0:T(8,128)(2,1)S(1)}, bf16[256,128]{1,0:T(8,128)(2,1)S(1)}, f32[256,1]{1,0:T(8,128)S(1)}) custom-call(bf16[256,128]{1,0:T(8,128)(2,1)S(1)} %get-tuple-element.55._, s32[3,3,1,4]{3,2,1,0:T(1,128)S(1)} %bitcast.2, bf16[3,1,4,3,64,64]{5,4,3,2,1,0:T(8,128)(2,1)S(1)} %copy-done.1, ...), custom_call_target="tpu_custom_call" | custom-call | bytes 852352 | tf_op jit(solution)/shard_map/operators/pallas_call | solution.py:52
  9.1 0.2 first_residual.3
  9.3 0.5 %collective-permute-start.6 = (bf16[256,128]{1,0:T(8,128)(2,1)S(1)}, bf16[256,128]{1,0:T(8,128)(2,1)S(1)}, u32[]{:S(2)}, u32[]{:S(2)}) collective-permute-start(bf16[256,128]{1,0:T(8,128)(2,1)S(1)} %get-tuple-element.67), channel_id=1, source_target_pairs={{0,4},{4,0},{8,12},{12,8},{16,20},{20,16},{24,28},{28,24},{1,5},{5... | collective-permute-start | bytes 196616 | tf_op jit(solution)/shard_map/ppermute | solution.py:323
  9.9 0.8 %collective-permute-done.2.other = bf16[256,128]{1,0:T(8,128)(2,1)S(1)} collective-permute-done((bf16[256,128]{1,0:T(8,128)(2,1)S(1)}, bf16[256,128]{1,0:T(8,128)(2,1)S(1)}, u32[]{:S(2)}, u32[]{:S(2)}) %collective-permute-start.2) | collective-permute-done | bytes 65568 | tf_op jit(solution)/shard_map/ppermute | solution.py:323
  10.7 0.2 join.3
  10.9 1.7 %collective-permute-start.3 = (bf16[64,128]{1,0:T(8,128)(2,1)S(1)}, bf16[64,128]{1,0:T(8,128)(2,1)S(1)}, u32[]{:S(2)}, u32[]{:S(2)}) collective-permute-start(bf16[64,128]{1,0:T(8,128)(2,1)S(1)} %get-tuple-element.63), channel_id=1, source_target_pairs={{0,3},{1,2},{2,1},{3,0},{4,7},{5,6},{6,5},{7,4},{8,11},{9,10},{10,... | collective-permute-start | bytes 49160 | tf_op jit(solution)/shard_map/ppermute | solution.py:338
  12.6 0.6 %collective-permute-start.4 = (bf16[64,128]{1,0:T(8,128)(2,1)S(1)}, bf16[64,128]{1,0:T(8,128)(2,1)S(1)}, u32[]{:S(2)}, u32[]{:S(2)}) collective-permute-start(bf16[64,128]{1,0:T(8,128)(2,1)S(1)} %get-tuple-element.64), channel_id=1, source_target_pairs={{0,1},{1,0},{2,3},{3,2},{4,5},{5,4},{6,7},{7,6},{8,9},{9,8},{10,11... | collective-permute-start | bytes 49160 | tf_op jit(solution)/shard_map/ppermute | solution.py:323
  13.2 0.5 %collective-permute-done.6.other = bf16[256,128]{1,0:T(8,128)(2,1)S(1)} collective-permute-done((bf16[256,128]{1,0:T(8,128)(2,1)S(1)}, bf16[256,128]{1,0:T(8,128)(2,1)S(1)}, u32[]{:S(2)}, u32[]{:S(2)}) %collective-permute-start.6) | collective-permute-done | bytes 65568 | tf_op jit(solution)/shard_map/ppermute | solution.py:323
  13.7 0.2 join.4
  13.9 1.5 %collective-permute-start.7 = (bf16[64,128]{1,0:T(8,128)(2,1)S(1)}, bf16[64,128]{1,0:T(8,128)(2,1)S(1)}, u32[]{:S(2)}, u32[]{:S(2)}) collective-permute-start(bf16[64,128]{1,0:T(8,128)(2,1)S(1)} %get-tuple-element.72), channel_id=1, source_target_pairs={{0,3},{1,2},{2,1},{3,0},{4,7},{5,6},{6,5},{7,4},{8,11},{9,10},{10,... | collective-permute-start | bytes 49160 | tf_op jit(solution)/shard_map/ppermute | solution.py:338
  15.4 0.6 %collective-permute-start.8 = (bf16[64,128]{1,0:T(8,128)(2,1)S(1)}, bf16[64,128]{1,0:T(8,128)(2,1)S(1)}, u32[]{:S(2)}, u32[]{:S(2)}) collective-permute-start(bf16[64,128]{1,0:T(8,128)(2,1)S(1)} %get-tuple-element.73), channel_id=1, source_target_pairs={{0,1},{1,0},{2,3},{3,2},{4,5},{5,4},{6,7},{7,6},{8,9},{9,8},{10,11... | collective-permute-start | bytes 49160 | tf_op jit(solution)/shard_map/ppermute | solution.py:323
  16.0 0.2 residual.3
  16.2 1.6 %collective-permute-start.9 = (bf16[256,128]{1,0:T(8,128)(2,1)S(1)}, bf16[256,128]{1,0:T(8,128)(2,1)S(1)}, u32[]{:S(2)}, u32[]{:S(2)}) collective-permute-start(bf16[256,128]{1,0:T(8,128)(2,1)S(1)} %get-tuple-element.69._), channel_id=1, source_target_pairs={{0,8},{4,12},{8,0},{12,4},{16,24},{20,28},{24,16},{28,20},{1,9},{5... | collective-permute-start | bytes 196616 | tf_op jit(solution)/shard_map/ppermute | solution.py:323
  17.9 0.7 %collective-permute-start.12 = (bf16[256,128]{1,0:T(8,128)(2,1)S(1)}, bf16[256,128]{1,0:T(8,128)(2,1)S(1)}, u32[]{:S(2)}, u32[]{:S(2)}) collective-permute-start(bf16[256,128]{1,0:T(8,128)(2,1)S(1)} %get-tuple-element.83.near), channel_id=1, source_target_pairs={{0,4},{4,0},{8,12},{12,8},{16,20},{20,16},{24,28},{28,24},{1,5},{5... | collective-permute-start | bytes 196616 | tf_op jit(solution)/shard_map/ppermute | solution.py:323
  18.6 0.2 residual.4
  18.8 1.1 %operators.3 = (bf16[256,512]{1,0:T(8,128)(2,1)S(1)}, bf16[256,256]{1,0:T(8,128)(2,1)S(1)}, bf16[256,128]{1,0:T(8,128)(2,1)S(1)}, f32[256,1]{1,0:T(8,128)S(1)}) custom-call(bf16[256,128]{1,0:T(8,128)(2,1)S(1)} %get-tuple-element.69._, s32[3,3,1,4]{3,2,1,0:T(1,128)S(1)} %bitcast.3, bf16[3,1,4,3,64,64]{5,4,3,2,1,0:T(8,128)(2,1)S(1)} %copy-done.1, ...), custom_call_target="tpu_custom_call" | custom-call | bytes 852352 | tf_op jit(solution)/shard_map/operators/pallas_call | solution.py:52
  19.9 0.6 %collective-permute-done.9.other = bf16[256,128]{1,0:T(8,128)(2,1)S(1)} collective-permute-done((bf16[256,128]{1,0:T(8,128)(2,1)S(1)}, bf16[256,128]{1,0:T(8,128)(2,1)S(1)}, u32[]{:S(2)}, u32[]{:S(2)}) %collective-permute-start.9) | collective-permute-done | bytes 65568 | tf_op jit(solution)/shard_map/ppermute | solution.py:323
  20.6 0.2 join.5
  20.8 0.1 collective-permute-start.10
  20.9 0.6 %collective-permute-start.11 = (bf16[64,128]{1,0:T(8,128)(2,1)S(1)}, bf16[64,128]{1,0:T(8,128)(2,1)S(1)}, u32[]{:S(2)}, u32[]{:S(2)}) collective-permute-start(bf16[64,128]{1,0:T(8,128)(2,1)S(1)} %get-tuple-element.81), channel_id=1, source_target_pairs={{0,1},{1,0},{2,3},{3,2},{4,5},{5,4},{6,7},{7,6},{8,9},{9,8},{10,11... | collective-permute-start | bytes 49160 | tf_op jit(solution)/shard_map/ppermute | solution.py:323
  21.5 0.7 %share.1 = bf16[256,256]{1,0:T(8,128)(2,1)S(1)} custom-call(bf16[256,128]{1,0:T(8,128)(2,1)S(1)} %get-tuple-element.77._.smoothed, s32[3,3,1,4]{3,2,1,0:T(1,128)S(1)} %bitcast.4, bf16[3,1,4,3,64,64]{5,4,3,2,1,0:T(8,128)(2,1)S(1)} %copy-done.1), custom_call_target="tpu_custom_call" | custom-call | bytes 360592 | tf_op jit(solution)/shard_map/share/pallas_call | solution.py:52
  22.2 1.8 %collective-permute-done.10.outer = bf16[64,128]{1,0:T(8,128)(2,1)S(1)} collective-permute-done((bf16[64,128]{1,0:T(8,128)(2,1)S(1)}, bf16[64,128]{1,0:T(8,128)(2,1)S(1)}, u32[]{:S(2)}, u32[]{:S(2)}) %collective-permute-start.10) | collective-permute-done | bytes 16416 | tf_op jit(solution)/shard_map/ppermute | solution.py:338
  24.0 0.4 residual.5
  24.4 2.7 %collective-permute-start.15 = (bf16[256,128]{1,0:T(8,128)(2,1)S(1)}, bf16[256,128]{1,0:T(8,128)(2,1)S(1)}, u32[]{:S(2)}, u32[]{:S(2)}) collective-permute-start(bf16[256,128]{1,0:T(8,128)(2,1)S(1)} %get-tuple-element.82.refs_0_._.own), channel_id=1, source_target_pairs={{0,18},{1,19},{2,16},{3,17},{4,22},{5,23},{6,20},{7,21},{8,26},{9,... | collective-permute-start | bytes 196616 | tf_op jit(solution)/shard_map/ppermute | solution.py:332
  27.2 1.4 %collective-permute-start.16 = (bf16[256,128]{1,0:T(8,128)(2,1)S(1)}, bf16[256,128]{1,0:T(8,128)(2,1)S(1)}, u32[]{:S(2)}, u32[]{:S(2)}) collective-permute-start(bf16[256,128]{1,0:T(8,128)(2,1)S(1)} %get-tuple-element.82.refs_0_._.own), channel_id=1, source_target_pairs={{0,2},{1,3},{2,0},{3,1},{4,6},{5,7},{6,4},{7,5},{8,10},{9,11},{10,... | collective-permute-start | bytes 196616 | tf_op jit(solution)/shard_map/ppermute | solution.py:323
  28.6 0.3 collective-permute-start.13
  28.9 0.7 %copy-done.6 = s32[3,1,4,2]{2,3,1,0:T(2,128)S(1)} copy-done((s32[3,1,4,2]{2,3,1,0:T(2,128)S(1)}, s32[3,1,4,2]{2,3,1,0:T(2,128)}, u32[]{:S(2)}) %copy-start.6) | copy-done | bytes 120
  29.6 1.2 %fine_operators.1 = (bf16[256,256]{1,0:T(8,128)(2,1)S(1)}, bf16[256,256]{1,0:T(8,128)(2,1)S(1)}, bf16[256,256]{1,0:T(8,128)(2,1)S(1)}, f32[256,256]{1,0:T(8,128)S(1)}) custom-call(bf16[256,128]{1,0:T(8,128)(2,1)S(1)} %get-tuple-element.82.refs_0_._.own, s32[3,1,2,4]{3,2,1,0:T(2,128)S(1)} %bitcast.5, bf16[3,1,4,2,64,64]{5,4,3,2,1,0:T(8,128)(2,1)S(1)} %copy-done.2, ...), custom_call_target="tpu_custom_call" | custom-call | flops 134217728 | bytes 1378400 | tf_op jit(solution)/shard_map/fine_operators/pallas_call | solution.py:52
  30.8 1.1 %coarse_operators.1.refs_0_.inverse = bf16[256,1024]{1,0:T(8,128)(2,1)S(1)} custom-call(bf16[256,128]{1,0:T(8,128)(2,1)S(1)} %get-tuple-element.82.refs_0_._.own, bf16[256,128]{1,0:T(8,128)(2,1)S(1)} %collective-permute-done.12.refs_1_.far, s32[3,1,2,4]{3,2,1,0:T(2,128)S(1)} %bitcast.6, bf16[256,1024]{1,0:T(8,128)(2,1)S(1)} %copy-done.4, ...), custom_call_target="tpu_custom_call" | custom-call | flops 201326592 | bytes 984160 | tf_op jit(solution)/shard_map/coarse_operators/pallas_call | solution.py:52
  32.0 1.7 %collective-permute-done.13.far = bf16[256,128]{1,0:T(8,128)(2,1)S(1)} collective-permute-done((bf16[256,128]{1,0:T(8,128)(2,1)S(1)}, bf16[256,128]{1,0:T(8,128)(2,1)S(1)}, u32[]{:S(2)}, u32[]{:S(2)}) %collective-permute-start.13) | collective-permute-done | bytes 65568 | tf_op jit(solution)/shard_map/ppermute | solution.py:332
  33.8 0.2 coarse.1.refs_2_
  34.1 1.0 %collective-permute-done.14.refs_0_ = bf16[256,128]{1,0:T(8,128)(2,1)S(1)} collective-permute-done((bf16[256,128]{1,0:T(8,128)(2,1)S(1)}, bf16[256,128]{1,0:T(8,128)(2,1)S(1)}, u32[]{:S(2)}, u32[]{:S(2)}) %collective-permute-start.14) | collective-permute-done | bytes 65568 | tf_op jit(solution)/shard_map/ppermute | solution.py:323
  35.1 0.4 up.1
  35.5 1.8 %collective-permute-start.20 = (bf16[256,128]{1,0:T(8,128)(2,1)S(1)}, bf16[256,128]{1,0:T(8,128)(2,1)S(1)}, u32[]{:S(2)}, u32[]{:S(2)}) collective-permute-start(bf16[256,128]{1,0:T(8,128)(2,1)S(1)} %get-tuple-element.90), channel_id=1, source_target_pairs={{0,12},{4,8},{8,4},{12,0},{16,28},{20,24},{24,20},{28,16},{1,13},{... | collective-permute-start | bytes 196616 | tf_op jit(solution)/shard_map/ppermute | solution.py:323
  37.3 0.4 %collective-permute-start.18 = (bf16[256,128]{1,0:T(8,128)(2,1)S(1)}, bf16[256,128]{1,0:T(8,128)(2,1)S(1)}, u32[]{:S(2)}, u32[]{:S(2)}) collective-permute-start(bf16[256,128]{1,0:T(8,128)(2,1)S(1)} %get-tuple-element.90), channel_id=1, source_target_pairs={{0,8},{4,12},{8,0},{12,4},{16,24},{20,28},{24,16},{28,20},{1,9},{5... | collective-permute-start | bytes 196616 | tf_op jit(solution)/shard_map/ppermute | solution.py:323
  37.8 1.3 %collective-permute-start.19 = (bf16[256,128]{1,0:T(8,128)(2,1)S(1)}, bf16[256,128]{1,0:T(8,128)(2,1)S(1)}, u32[]{:S(2)}, u32[]{:S(2)}) collective-permute-start(bf16[256,128]{1,0:T(8,128)(2,1)S(1)} %get-tuple-element.91.refs_0_), channel_id=1, source_target_pairs={{0,4},{4,0},{8,12},{12,8},{16,20},{20,16},{24,28},{28,24},{1,5},{5... | collective-permute-start | bytes 196616 | tf_op jit(solution)/shard_map/ppermute | solution.py:323
  39.1 0.8 %output.3.refs_5_ = f32[1,256,512]{2,1,0:T(8,128)} custom-call(bf16[256,128]{1,0:T(8,128)(2,1)S(1)} %get-tuple-element.91.refs_0_, f32[256,512]{1,0:T(8,128)S(1)} %get-tuple-element.86.base.refs_1_.refs_2_, bf16[256,256]{1,0:T(8,128)(2,1)S(1)} %get-tuple-element.92.refs_2_.refs_3_, f32[256,256]{1,0:T(8,128)S(1)} %get-tuple-element.93.refs_3_.refs_4_, ...), custom_call_target="tpu_custom_call" | custom-call | flops 16777216 | bytes 1114112 | tf_op jit(solution)/shard_map/output/pallas_call | solution.py:52
  39.9 1.1 %collective-permute-done.20.refs_0_ = bf16[256,128]{1,0:T(8,128)(2,1)S(1)} collective-permute-done((bf16[256,128]{1,0:T(8,128)(2,1)S(1)}, bf16[256,128]{1,0:T(8,128)(2,1)S(1)}, u32[]{:S(2)}, u32[]{:S(2)}) %collective-permute-start.20) | collective-permute-done | bytes 65568 | tf_op jit(solution)/shard_map/ppermute | solution.py:323
  41.0 0.8 %output.4.refs_6_ = f32[1,256,512]{2,1,0:T(8,128)} custom-call(bf16[256,128]{1,0:T(8,128)(2,1)S(1)} %collective-permute-done.20.refs_0_, f32[256,512]{1,0:T(8,128)S(1)} %get-tuple-element.86.base.refs_1_.refs_2_, bf16[256,256]{1,0:T(8,128)(2,1)S(1)} %get-tuple-element.92.refs_2_.refs_3_, ...), custom_call_target="tpu_custom_call", output_to_operand_aliasing={{}: (5, {})} | custom-call | flops 16777216 | bytes 1638400 | tf_op jit(solution)/shard_map/output/pallas_call | solution.py:52
  41.9 0.2 collective-permute-done.19.refs_1_
  42.1 0.9 %output.5 = f32[1,256,512]{2,1,0:T(8,128)} custom-call(bf16[256,128]{1,0:T(8,128)(2,1)S(1)} %collective-permute-done.18.refs_0_, bf16[256,128]{1,0:T(8,128)(2,1)S(1)} %collective-permute-done.19.refs_1_, f32[256,512]{1,0:T(8,128)S(1)} %get-tuple-element.86.base.refs_1_.refs_2_, ...), custom_call_target="tpu_custom_call", output_to_operand_aliasing={{}: (6, {})} | custom-call | flops 33554432 | bytes 1703936 | tf_op jit(solution)/shard_map/output/pallas_call | solution.py:52
  (30 shorter events, 0.3 us)
Async XLA Ops:
  0.0 4.4 %copy-start = (bf16[3,1,4,5,64,64]{5,4,3,2,1,0:T(8,128)(2,1)S(1)}, bf16[3,1,4,5,64,64]{5,4,3,2,1,0:T(8,128)(2,1)}, u32[]{:S(2)}) copy-start(bf16[3,1,4,5,64,64]{5,4,3,2,1,0:T(8,128)(2,1)} %blocks.7) | copy-start | bytes 1474564
  0.0 4.4 %copy-start.3 = (f32[1,256,512]{2,1,0:T(8,128)S(1)}, f32[1,256,512]{2,1,0:T(8,128)}, u32[]{:S(2)}) copy-start(f32[1,256,512]{2,1,0:T(8,128)} %rhs.3) | copy-start | bytes 1572868
  1.3 4.8 %collective-permute-start.1 = (bf16[64,512]{1,0:T(8,128)(2,1)S(1)}, bf16[64,512]{1,0:T(8,128)(2,1)S(1)}, u32[]{:S(2)}, u32[]{:S(2)}) collective-permute-start(bf16[64,512]{1,0:T(8,128)(2,1)S(1)} %get-tuple-element.54), channel_id=1, source_target_pairs={{0,1},{1,0},{2,3},{3,2},{4,5},{5,4},{6,7},{7,6},{8,9},{9,8},{10,11... | collective-permute-start | bytes 196616 | tf_op jit(solution)/shard_map/ppermute | solution.py:323
  1.8 4.3 %collective-permute-start = (bf16[64,256]{1,0:T(8,128)(2,1)S(1)}, bf16[64,256]{1,0:T(8,128)(2,1)S(1)}, u32[]{:S(2)}, u32[]{:S(2)}) collective-permute-start(bf16[64,256]{1,0:T(8,128)(2,1)S(1)} %get-tuple-element.50._), channel_id=1, source_target_pairs={{0,3},{1,2},{2,1},{3,0},{4,7},{5,6},{6,5},{7,4},{8,11},{9,10},{10,... | collective-permute-start | bytes 98312 | tf_op jit(solution)/shard_map/ppermute | solution.py:338
  4.4 4.7 %collective-permute-start.5 = (bf16[64,256]{1,0:T(8,128)(2,1)S(1)}, bf16[64,256]{1,0:T(8,128)(2,1)S(1)}, u32[]{:S(2)}, u32[]{:S(2)}) collective-permute-start(bf16[64,256]{1,0:T(8,128)(2,1)S(1)} %get-tuple-element.65), channel_id=1, source_target_pairs={{0,3},{1,2},{2,1},{3,0},{4,7},{5,6},{6,5},{7,4},{8,11},{9,10},{10,... | collective-permute-start | bytes 98312 | tf_op jit(solution)/shard_map/ppermute | solution.py:338
  5.6 2.4 %copy-start.1 = (bf16[3,1,4,3,64,64]{5,4,3,2,1,0:T(8,128)(2,1)S(1)}, bf16[3,1,4,3,64,64]{5,4,3,2,1,0:T(8,128)(2,1)}, u32[]{:S(2)}) copy-start(bf16[3,1,4,3,64,64]{5,4,3,2,1,0:T(8,128)(2,1)} %rblocks.5) | copy-start | bytes 884740
  6.1 1.9 %copy-start.5 = (s32[3,1,4,3]{2,1,3,0:T(1,128)S(1)}, s32[3,1,4,3]{2,1,3,0:T(1,128)}, u32[]{:S(2)}) copy-start(s32[3,1,4,3]{2,1,3,0:T(1,128)} %param.11) | copy-start | bytes 436
  6.3 4.4 %collective-permute-start.2 = (bf16[256,128]{1,0:T(8,128)(2,1)S(1)}, bf16[256,128]{1,0:T(8,128)(2,1)S(1)}, u32[]{:S(2)}, u32[]{:S(2)}) collective-permute-start(bf16[256,128]{1,0:T(8,128)(2,1)S(1)} %get-tuple-element.55._), channel_id=1, source_target_pairs={{0,4},{4,0},{8,12},{12,8},{16,20},{20,16},{24,28},{28,24},{1,5},{5... | collective-permute-start | bytes 196616 | tf_op jit(solution)/shard_map/ppermute | solution.py:323
  9.3 4.3 %collective-permute-start.6 = (bf16[256,128]{1,0:T(8,128)(2,1)S(1)}, bf16[256,128]{1,0:T(8,128)(2,1)S(1)}, u32[]{:S(2)}, u32[]{:S(2)}) collective-permute-start(bf16[256,128]{1,0:T(8,128)(2,1)S(1)} %get-tuple-element.67), channel_id=1, source_target_pairs={{0,4},{4,0},{8,12},{12,8},{16,20},{20,16},{24,28},{28,24},{1,5},{5... | collective-permute-start | bytes 196616 | tf_op jit(solution)/shard_map/ppermute | solution.py:323
  10.9 5.1 %collective-permute-start.3 = (bf16[64,128]{1,0:T(8,128)(2,1)S(1)}, bf16[64,128]{1,0:T(8,128)(2,1)S(1)}, u32[]{:S(2)}, u32[]{:S(2)}) collective-permute-start(bf16[64,128]{1,0:T(8,128)(2,1)S(1)} %get-tuple-element.63), channel_id=1, source_target_pairs={{0,3},{1,2},{2,1},{3,0},{4,7},{5,6},{6,5},{7,4},{8,11},{9,10},{10,... | collective-permute-start | bytes 49160 | tf_op jit(solution)/shard_map/ppermute | solution.py:338
  12.6 3.4 %collective-permute-start.4 = (bf16[64,128]{1,0:T(8,128)(2,1)S(1)}, bf16[64,128]{1,0:T(8,128)(2,1)S(1)}, u32[]{:S(2)}, u32[]{:S(2)}) collective-permute-start(bf16[64,128]{1,0:T(8,128)(2,1)S(1)} %get-tuple-element.64), channel_id=1, source_target_pairs={{0,1},{1,0},{2,3},{3,2},{4,5},{5,4},{6,7},{7,6},{8,9},{9,8},{10,11... | collective-permute-start | bytes 49160 | tf_op jit(solution)/shard_map/ppermute | solution.py:323
  13.9 4.7 %collective-permute-start.7 = (bf16[64,128]{1,0:T(8,128)(2,1)S(1)}, bf16[64,128]{1,0:T(8,128)(2,1)S(1)}, u32[]{:S(2)}, u32[]{:S(2)}) collective-permute-start(bf16[64,128]{1,0:T(8,128)(2,1)S(1)} %get-tuple-element.72), channel_id=1, source_target_pairs={{0,3},{1,2},{2,1},{3,0},{4,7},{5,6},{6,5},{7,4},{8,11},{9,10},{10,... | collective-permute-start | bytes 49160 | tf_op jit(solution)/shard_map/ppermute | solution.py:338
  15.4 3.2 %collective-permute-start.8 = (bf16[64,128]{1,0:T(8,128)(2,1)S(1)}, bf16[64,128]{1,0:T(8,128)(2,1)S(1)}, u32[]{:S(2)}, u32[]{:S(2)}) collective-permute-start(bf16[64,128]{1,0:T(8,128)(2,1)S(1)} %get-tuple-element.73), channel_id=1, source_target_pairs={{0,1},{1,0},{2,3},{3,2},{4,5},{5,4},{6,7},{7,6},{8,9},{9,8},{10,11... | collective-permute-start | bytes 49160 | tf_op jit(solution)/shard_map/ppermute | solution.py:323
  16.2 4.3 %collective-permute-start.9 = (bf16[256,128]{1,0:T(8,128)(2,1)S(1)}, bf16[256,128]{1,0:T(8,128)(2,1)S(1)}, u32[]{:S(2)}, u32[]{:S(2)}) collective-permute-start(bf16[256,128]{1,0:T(8,128)(2,1)S(1)} %get-tuple-element.69._), channel_id=1, source_target_pairs={{0,8},{4,12},{8,0},{12,4},{16,24},{20,28},{24,16},{28,20},{1,9},{5... | collective-permute-start | bytes 196616 | tf_op jit(solution)/shard_map/ppermute | solution.py:323
  17.9 11.0 %collective-permute-start.12 = (bf16[256,128]{1,0:T(8,128)(2,1)S(1)}, bf16[256,128]{1,0:T(8,128)(2,1)S(1)}, u32[]{:S(2)}, u32[]{:S(2)}) collective-permute-start(bf16[256,128]{1,0:T(8,128)(2,1)S(1)} %get-tuple-element.83.near), channel_id=1, source_target_pairs={{0,4},{4,0},{8,12},{12,8},{16,20},{20,16},{24,28},{28,24},{1,5},{5... | collective-permute-start | bytes 196616 | tf_op jit(solution)/shard_map/ppermute | solution.py:323
  20.8 3.2 %collective-permute-start.10 = (bf16[64,128]{1,0:T(8,128)(2,1)S(1)}, bf16[64,128]{1,0:T(8,128)(2,1)S(1)}, u32[]{:S(2)}, u32[]{:S(2)}) collective-permute-start(bf16[64,128]{1,0:T(8,128)(2,1)S(1)} %get-tuple-element.80), channel_id=1, source_target_pairs={{0,3},{1,2},{2,1},{3,0},{4,7},{5,6},{6,5},{7,4},{8,11},{9,10},{10,... | collective-permute-start | bytes 49160 | tf_op jit(solution)/shard_map/ppermute | solution.py:338
  20.9 3.2 %collective-permute-start.11 = (bf16[64,128]{1,0:T(8,128)(2,1)S(1)}, bf16[64,128]{1,0:T(8,128)(2,1)S(1)}, u32[]{:S(2)}, u32[]{:S(2)}) collective-permute-start(bf16[64,128]{1,0:T(8,128)(2,1)S(1)} %get-tuple-element.81), channel_id=1, source_target_pairs={{0,1},{1,0},{2,3},{3,2},{4,5},{5,4},{6,7},{7,6},{8,9},{9,8},{10,11... | collective-permute-start | bytes 49160 | tf_op jit(solution)/shard_map/ppermute | solution.py:323
  22.2 6.7 %copy-start.2 = (bf16[3,1,4,2,64,64]{5,4,3,2,1,0:T(8,128)(2,1)S(1)}, bf16[3,1,4,2,64,64]{5,4,3,2,1,0:T(8,128)(2,1)}, u32[]{:S(2)}) copy-start(bf16[3,1,4,2,64,64]{5,4,3,2,1,0:T(8,128)(2,1)} %blocks_1.1) | copy-start | bytes 589828
  24.4 7.5 %collective-permute-start.15 = (bf16[256,128]{1,0:T(8,128)(2,1)S(1)}, bf16[256,128]{1,0:T(8,128)(2,1)S(1)}, u32[]{:S(2)}, u32[]{:S(2)}) collective-permute-start(bf16[256,128]{1,0:T(8,128)(2,1)S(1)} %get-tuple-element.82.refs_0_._.own), channel_id=1, source_target_pairs={{0,18},{1,19},{2,16},{3,17},{4,22},{5,23},{6,20},{7,21},{8,26},{9,... | collective-permute-start | bytes 196616 | tf_op jit(solution)/shard_map/ppermute | solution.py:332
  27.2 4.8 %collective-permute-start.16 = (bf16[256,128]{1,0:T(8,128)(2,1)S(1)}, bf16[256,128]{1,0:T(8,128)(2,1)S(1)}, u32[]{:S(2)}, u32[]{:S(2)}) collective-permute-start(bf16[256,128]{1,0:T(8,128)(2,1)S(1)} %get-tuple-element.82.refs_0_._.own), channel_id=1, source_target_pairs={{0,2},{1,3},{2,0},{3,1},{4,6},{5,7},{6,4},{7,5},{8,10},{9,11},{10,... | collective-permute-start | bytes 196616 | tf_op jit(solution)/shard_map/ppermute | solution.py:323
  28.6 5.2 %collective-permute-start.13 = (bf16[256,128]{1,0:T(8,128)(2,1)S(1)}, bf16[256,128]{1,0:T(8,128)(2,1)S(1)}, u32[]{:S(2)}, u32[]{:S(2)}) collective-permute-start(bf16[256,128]{1,0:T(8,128)(2,1)S(1)} %get-tuple-element.82.refs_0_._.own), channel_id=1, source_target_pairs={{0,16},{1,17},{2,18},{3,19},{4,20},{5,21},{6,22},{7,23},{8,24},{9,... | collective-permute-start | bytes 196616 | tf_op jit(solution)/shard_map/ppermute | solution.py:332
  28.9 0.7 %copy-start.6 = (s32[3,1,4,2]{2,3,1,0:T(2,128)S(1)}, s32[3,1,4,2]{2,3,1,0:T(2,128)}, u32[]{:S(2)}) copy-start(s32[3,1,4,2]{2,3,1,0:T(2,128)} %param.13) | copy-start | bytes 292
  29.6 1.2 %copy-start.4 = (bf16[256,1024]{1,0:T(8,128)(2,1)S(1)}, bf16[256,1024]{1,0:T(8,128)(2,1)}, u32[]{:S(2)}) copy-start(bf16[256,1024]{1,0:T(8,128)(2,1)} %refs_3_.1) | copy-start | bytes 1572868
  32.0 2.1 %collective-permute-start.17 = (bf16[256,128]{1,0:T(8,128)(2,1)S(1)}, bf16[256,128]{1,0:T(8,128)(2,1)S(1)}, u32[]{:S(2)}, u32[]{:S(2)}) collective-permute-start(bf16[256,128]{1,0:T(8,128)(2,1)S(1)} %share_sum.3.refs_0_), channel_id=1, source_target_pairs={{0,1},{1,0},{2,3},{3,2},{4,5},{5,4},{6,7},{7,6},{8,9},{9,8},{10,11... | collective-permute-start | bytes 196616 | tf_op jit(solution)/shard_map/ppermute | solution.py:323
  33.8 1.3 %collective-permute-start.14 = (bf16[256,128]{1,0:T(8,128)(2,1)S(1)}, bf16[256,128]{1,0:T(8,128)(2,1)S(1)}, u32[]{:S(2)}, u32[]{:S(2)}) collective-permute-start(bf16[256,128]{1,0:T(8,128)(2,1)S(1)} %share_sum.2.refs_1_), channel_id=1, source_target_pairs={{0,1},{1,0},{2,3},{3,2},{4,5},{5,4},{6,7},{7,6},{8,9},{9,8},{10,11... | collective-permute-start | bytes 196616 | tf_op jit(solution)/shard_map/ppermute | solution.py:323
  35.5 5.5 %collective-permute-start.20 = (bf16[256,128]{1,0:T(8,128)(2,1)S(1)}, bf16[256,128]{1,0:T(8,128)(2,1)S(1)}, u32[]{:S(2)}, u32[]{:S(2)}) collective-permute-start(bf16[256,128]{1,0:T(8,128)(2,1)S(1)} %get-tuple-element.90), channel_id=1, source_target_pairs={{0,12},{4,8},{8,4},{12,0},{16,28},{20,24},{24,20},{28,16},{1,13},{... | collective-permute-start | bytes 196616 | tf_op jit(solution)/shard_map/ppermute | solution.py:323
  37.3 4.6 %collective-permute-start.18 = (bf16[256,128]{1,0:T(8,128)(2,1)S(1)}, bf16[256,128]{1,0:T(8,128)(2,1)S(1)}, u32[]{:S(2)}, u32[]{:S(2)}) collective-permute-start(bf16[256,128]{1,0:T(8,128)(2,1)S(1)} %get-tuple-element.90), channel_id=1, source_target_pairs={{0,8},{4,12},{8,0},{12,4},{16,24},{20,28},{24,16},{28,20},{1,9},{5... | collective-permute-start | bytes 196616 | tf_op jit(solution)/shard_map/ppermute | solution.py:323
  37.8 4.3 %collective-permute-start.19 = (bf16[256,128]{1,0:T(8,128)(2,1)S(1)}, bf16[256,128]{1,0:T(8,128)(2,1)S(1)}, u32[]{:S(2)}, u32[]{:S(2)}) collective-permute-start(bf16[256,128]{1,0:T(8,128)(2,1)S(1)} %get-tuple-element.91.refs_0_), channel_id=1, source_target_pairs={{0,4},{4,0},{8,12},{12,8},{16,20},{20,16},{24,28},{28,24},{1,5},{5... | collective-permute-start | bytes 196616 | tf_op jit(solution)/shard_map/ppermute | solution.py:323

commit v18 on v14

--- a/solution.py
+++ b/solution.py
@@ -473,7 +473,7 @@
         functools.partial(coarse_kernel, offsets), "coarse", [real_shape],
         [coarse_mat] + [parts[o] for o in offsets] + [bases[-1]], flops=flops(width, len(offsets)),
     )
-    parts = {o + 1: exchange(parts[o], "narrow", 1) for o in reversed(offsets)}
+    parts = {o + 1: exchange(parts[o], "narrow", 1) for o in offsets}
     offsets = tuple(parts)
     operands = [coarse_mat] + [parts[o] for o in offsets] + [value]
     for idx in reversed(range(2, last)):

time: 42.9 us -> 43.5 us (1.014)
  waiting for transfers between devices: 6.12 us -> 6.64 us
    ppermute x2, waiting for transfers between devices: 1.57 us -> 2.55 us  [exchange_both(): return lax.ppermute(value, ('wide', 'narrow'), pairs)]
    ppermute x14, waiting for transfers between devices: 3.38 us -> 2.93 us  [exchange(): return lax.ppermute(value, axis, [(i, i ^ bit) for i in range(count)])]
  transfers between devices with their start and end apart: 21 -> 21, of which waited for: 8 -> 6; matrix products, arithmetic and copies ran while one was open for 0% -> 0% of each run, Pallas kernels for 24% -> 23%
where the time goes in v18:
time: 43.5 us; the launch traced here: 43.3 us
  starting transfers between devices  22.9 us (53%)
  Pallas kernels  12.8 us (29%)
  waiting for transfers between devices  6.64 us (15%)
  local copies, waits for them, and re-layouts  0.71 us (2%)
    ppermute x14, starting transfers between devices, exchange(): return lax.ppermute(value, axis, [(i, i ^ bit) for i in range(count)])  12.9 us
    pallas_call x22, Pallas kernels, run(): pl.pallas_call(body, grid=(1,) if windows else (), out_shape=[out_space(o...  12.8 us
    ppermute x5, starting transfers between devices, swap_outer(): return lax.ppermute(outer, 'narrow', gaps)  6.01 us
    ppermute x2, starting transfers between devices, exchange_both(): return lax.ppermute(value, ('wide', 'narrow'), pairs)  4.07 us
    ppermute x14, waiting for transfers between devices, exchange(): return lax.ppermute(value, axis, [(i, i ^ bit) for i in range(count)])  2.93 us
    ppermute x2, waiting for transfers between devices, exchange_both(): return lax.ppermute(value, ('wide', 'narrow'), pairs)  2.55 us
    ppermute x5, waiting for transfers between devices, swap_outer(): return lax.ppermute(outer, 'narrow', gaps)  1.16 us
  transfers between devices with their start and end apart: 21, of which 6 were waited for; matrix products, arithmetic and copies ran while one was open for 0% of the time, Pallas kernels for 23%

profile of v18, /device:TPU:0, one launch (start us, length us, event | category | flops | bytes accessed | tf_op | source)
XLA Modules:
  0.0 43.3 jit_solution(16107926687209508655)
XLA Ops:
  0.0 1.3 %start.1 = (s32[3,1,4,5]{3,2,1,0:T(4,128)S(1)}, bf16[64,512]{1,0:T(8,128)(2,1)S(1)}, bf16[64,256]{1,0:T(8,128)(2,1)S(1)}, bf16[64,256]{1,0:T(8,128)(2,1)S(1)}) custom-call(f32[1,256,512]{2,1,0:T(8,128)} %rhs.3, bf16[3,1,4,5,64,64]{5,4,3,2,1,0:T(8,128)(2,1)} %blocks.7, s32[3,1,4,5]{3,2,1,0:T(4,128)} %refs_0_.1), custom_call_target="tpu_custom_call" | custom-call | bytes 1016048 | tf_op jit(solution)/shard_map/start/pallas_call | solution.py:52
  1.3 0.5 %collective-permute-start.1 = (bf16[64,512]{1,0:T(8,128)(2,1)S(1)}, bf16[64,512]{1,0:T(8,128)(2,1)S(1)}, u32[]{:S(2)}, u32[]{:S(2)}) collective-permute-start(bf16[64,512]{1,0:T(8,128)(2,1)S(1)} %get-tuple-element.54), channel_id=1, source_target_pairs={{0,1},{1,0},{2,3},{3,2},{4,5},{5,4},{6,7},{7,6},{8,9},{9,8},{10,11... | collective-permute-start | bytes 196616 | tf_op jit(solution)/shard_map/ppermute | solution.py:323
  1.8 2.6 %collective-permute-start = (bf16[64,256]{1,0:T(8,128)(2,1)S(1)}, bf16[64,256]{1,0:T(8,128)(2,1)S(1)}, u32[]{:S(2)}, u32[]{:S(2)}) collective-permute-start(bf16[64,256]{1,0:T(8,128)(2,1)S(1)} %get-tuple-element.50._), channel_id=1, source_target_pairs={{0,3},{1,2},{2,1},{3,0},{4,7},{5,6},{6,5},{7,4},{8,11},{9,10},{10,... | collective-permute-start | bytes 98312 | tf_op jit(solution)/shard_map/ppermute | solution.py:338
  4.4 0.0 collective-permute-start.5
  4.5 1.1 %first_local.1 = (f32[256,512]{1,0:T(8,128)S(1)}, f32[256,512]{1,0:T(8,128)S(1)}, bf16[256,256]{1,0:T(8,128)(2,1)S(1)}, bf16[256,128]{1,0:T(8,128)(2,1)S(1)}, f32[256,1]{1,0:T(8,128)S(1)}) custom-call(f32[1,256,512]{2,1,0:T(8,128)S(1)} %copy-done.3, bf16[64,256]{1,0:T(8,128)(2,1)S(1)} %get-tuple-element.50._, s32[3,1,4,5]{3,2,1,0:T(4,128)S(1)} %get-tuple-element.51.cols, ...), custom_call_target="tpu_custom_call" | custom-call | flops 67108864 | bytes 1048816 | tf_op jit(solution)/shard_map/first_local/pallas_call | solution.py:52
  5.6 0.5 %collective-permute-done.outer = bf16[64,256]{1,0:T(8,128)(2,1)S(1)} collective-permute-done((bf16[64,256]{1,0:T(8,128)(2,1)S(1)}, bf16[64,256]{1,0:T(8,128)(2,1)S(1)}, u32[]{:S(2)}, u32[]{:S(2)}) %collective-permute-start) | collective-permute-done | bytes 32800 | tf_op jit(solution)/shard_map/ppermute | solution.py:338
  6.1 0.2 first_residual.2
  6.3 1.7 %collective-permute-start.2 = (bf16[256,128]{1,0:T(8,128)(2,1)S(1)}, bf16[256,128]{1,0:T(8,128)(2,1)S(1)}, u32[]{:S(2)}, u32[]{:S(2)}) collective-permute-start(bf16[256,128]{1,0:T(8,128)(2,1)S(1)} %get-tuple-element.55._), channel_id=1, source_target_pairs={{0,4},{4,0},{8,12},{12,8},{16,20},{20,16},{24,28},{28,24},{1,5},{5... | collective-permute-start | bytes 196616 | tf_op jit(solution)/shard_map/ppermute | solution.py:323
  8.0 0.2 first_residual.3
  8.2 1.4 %collective-permute-start.6 = (bf16[256,128]{1,0:T(8,128)(2,1)S(1)}, bf16[256,128]{1,0:T(8,128)(2,1)S(1)}, u32[]{:S(2)}, u32[]{:S(2)}) collective-permute-start(bf16[256,128]{1,0:T(8,128)(2,1)S(1)} %get-tuple-element.67), channel_id=1, source_target_pairs={{0,4},{4,0},{8,12},{12,8},{16,20},{20,16},{24,28},{28,24},{1,5},{5... | collective-permute-start | bytes 196616 | tf_op jit(solution)/shard_map/ppermute | solution.py:323
  9.6 1.1 %operators.2 = (bf16[256,512]{1,0:T(8,128)(2,1)S(1)}, bf16[256,256]{1,0:T(8,128)(2,1)S(1)}, bf16[256,128]{1,0:T(8,128)(2,1)S(1)}, f32[256,1]{1,0:T(8,128)S(1)}) custom-call(bf16[256,128]{1,0:T(8,128)(2,1)S(1)} %get-tuple-element.55._, s32[3,3,1,4]{3,2,1,0:T(1,128)S(1)} %bitcast.2, bf16[3,1,4,3,64,64]{5,4,3,2,1,0:T(8,128)(2,1)S(1)} %copy-done.1, ...), custom_call_target="tpu_custom_call" | custom-call | bytes 852352 | tf_op jit(solution)/shard_map/operators/pallas_call | solution.py:52
  10.8 0.2 join.3
  11.0 1.6 %collective-permute-start.3 = (bf16[64,128]{1,0:T(8,128)(2,1)S(1)}, bf16[64,128]{1,0:T(8,128)(2,1)S(1)}, u32[]{:S(2)}, u32[]{:S(2)}) collective-permute-start(bf16[64,128]{1,0:T(8,128)(2,1)S(1)} %get-tuple-element.63), channel_id=1, source_target_pairs={{0,3},{1,2},{2,1},{3,0},{4,7},{5,6},{6,5},{7,4},{8,11},{9,10},{10,... | collective-permute-start | bytes 49160 | tf_op jit(solution)/shard_map/ppermute | solution.py:338
  12.6 0.6 %collective-permute-start.4 = (bf16[64,128]{1,0:T(8,128)(2,1)S(1)}, bf16[64,128]{1,0:T(8,128)(2,1)S(1)}, u32[]{:S(2)}, u32[]{:S(2)}) collective-permute-start(bf16[64,128]{1,0:T(8,128)(2,1)S(1)} %get-tuple-element.64), channel_id=1, source_target_pairs={{0,1},{1,0},{2,3},{3,2},{4,5},{5,4},{6,7},{7,6},{8,9},{9,8},{10,11... | collective-permute-start | bytes 49160 | tf_op jit(solution)/shard_map/ppermute | solution.py:323
  13.2 0.2 join.4
  13.4 0.8 %collective-permute-start.7 = (bf16[64,128]{1,0:T(8,128)(2,1)S(1)}, bf16[64,128]{1,0:T(8,128)(2,1)S(1)}, u32[]{:S(2)}, u32[]{:S(2)}) collective-permute-start(bf16[64,128]{1,0:T(8,128)(2,1)S(1)} %get-tuple-element.72), channel_id=1, source_target_pairs={{0,3},{1,2},{2,1},{3,0},{4,7},{5,6},{6,5},{7,4},{8,11},{9,10},{10,... | collective-permute-start | bytes 49160 | tf_op jit(solution)/shard_map/ppermute | solution.py:338
  14.2 0.6 %collective-permute-start.8 = (bf16[64,128]{1,0:T(8,128)(2,1)S(1)}, bf16[64,128]{1,0:T(8,128)(2,1)S(1)}, u32[]{:S(2)}, u32[]{:S(2)}) collective-permute-start(bf16[64,128]{1,0:T(8,128)(2,1)S(1)} %get-tuple-element.73), channel_id=1, source_target_pairs={{0,1},{1,0},{2,3},{3,2},{4,5},{5,4},{6,7},{7,6},{8,9},{9,8},{10,11... | collective-permute-start | bytes 49160 | tf_op jit(solution)/shard_map/ppermute | solution.py:323
  14.9 0.2 residual.3
  15.1 1.6 %collective-permute-start.9 = (bf16[256,128]{1,0:T(8,128)(2,1)S(1)}, bf16[256,128]{1,0:T(8,128)(2,1)S(1)}, u32[]{:S(2)}, u32[]{:S(2)}) collective-permute-start(bf16[256,128]{1,0:T(8,128)(2,1)S(1)} %get-tuple-element.69._), channel_id=1, source_target_pairs={{0,8},{4,12},{8,0},{12,4},{16,24},{20,28},{24,16},{28,20},{1,9},{5... | collective-permute-start | bytes 196616 | tf_op jit(solution)/shard_map/ppermute | solution.py:323
  16.8 1.3 %collective-permute-start.12 = (bf16[256,128]{1,0:T(8,128)(2,1)S(1)}, bf16[256,128]{1,0:T(8,128)(2,1)S(1)}, u32[]{:S(2)}, u32[]{:S(2)}) collective-permute-start(bf16[256,128]{1,0:T(8,128)(2,1)S(1)} %get-tuple-element.83.near), channel_id=1, source_target_pairs={{0,4},{4,0},{8,12},{12,8},{16,20},{20,16},{24,28},{28,24},{1,5},{5... | collective-permute-start | bytes 196616 | tf_op jit(solution)/shard_map/ppermute | solution.py:323
  18.1 0.2 residual.4
  18.3 1.1 %operators.3 = (bf16[256,512]{1,0:T(8,128)(2,1)S(1)}, bf16[256,256]{1,0:T(8,128)(2,1)S(1)}, bf16[256,128]{1,0:T(8,128)(2,1)S(1)}, f32[256,1]{1,0:T(8,128)S(1)}) custom-call(bf16[256,128]{1,0:T(8,128)(2,1)S(1)} %get-tuple-element.69._, s32[3,3,1,4]{3,2,1,0:T(1,128)S(1)} %bitcast.3, bf16[3,1,4,3,64,64]{5,4,3,2,1,0:T(8,128)(2,1)S(1)} %copy-done.1, ...), custom_call_target="tpu_custom_call" | custom-call | bytes 852352 | tf_op jit(solution)/shard_map/operators/pallas_call | solution.py:52
  19.4 0.2 join.5
  19.7 0.9 %collective-permute-start.10 = (bf16[64,128]{1,0:T(8,128)(2,1)S(1)}, bf16[64,128]{1,0:T(8,128)(2,1)S(1)}, u32[]{:S(2)}, u32[]{:S(2)}) collective-permute-start(bf16[64,128]{1,0:T(8,128)(2,1)S(1)} %get-tuple-element.80), channel_id=1, source_target_pairs={{0,3},{1,2},{2,1},{3,0},{4,7},{5,6},{6,5},{7,4},{8,11},{9,10},{10,... | collective-permute-start | bytes 49160 | tf_op jit(solution)/shard_map/ppermute | solution.py:338
  20.6 0.9 %collective-permute-start.11 = (bf16[64,128]{1,0:T(8,128)(2,1)S(1)}, bf16[64,128]{1,0:T(8,128)(2,1)S(1)}, u32[]{:S(2)}, u32[]{:S(2)}) collective-permute-start(bf16[64,128]{1,0:T(8,128)(2,1)S(1)} %get-tuple-element.81), channel_id=1, source_target_pairs={{0,1},{1,0},{2,3},{3,2},{4,5},{5,4},{6,7},{7,6},{8,9},{9,8},{10,11... | collective-permute-start | bytes 49160 | tf_op jit(solution)/shard_map/ppermute | solution.py:323
  21.5 0.7 %share.1 = bf16[256,256]{1,0:T(8,128)(2,1)S(1)} custom-call(bf16[256,128]{1,0:T(8,128)(2,1)S(1)} %get-tuple-element.77._.smoothed, s32[3,3,1,4]{3,2,1,0:T(1,128)S(1)} %bitcast.4, bf16[3,1,4,3,64,64]{5,4,3,2,1,0:T(8,128)(2,1)S(1)} %copy-done.1), custom_call_target="tpu_custom_call" | custom-call | bytes 360592 | tf_op jit(solution)/shard_map/share/pallas_call | solution.py:52
  22.2 0.7 %collective-permute-done.10.outer = bf16[64,128]{1,0:T(8,128)(2,1)S(1)} collective-permute-done((bf16[64,128]{1,0:T(8,128)(2,1)S(1)}, bf16[64,128]{1,0:T(8,128)(2,1)S(1)}, u32[]{:S(2)}, u32[]{:S(2)}) %collective-permute-start.10) | collective-permute-done | bytes 16416 | tf_op jit(solution)/shard_map/ppermute | solution.py:338
  22.9 0.4 residual.5
  23.3 2.7 %collective-permute-start.16 = (bf16[256,128]{1,0:T(8,128)(2,1)S(1)}, bf16[256,128]{1,0:T(8,128)(2,1)S(1)}, u32[]{:S(2)}, u32[]{:S(2)}) collective-permute-start(bf16[256,128]{1,0:T(8,128)(2,1)S(1)} %get-tuple-element.82.refs_0_._.own), channel_id=1, source_target_pairs={{0,16},{1,17},{2,18},{3,19},{4,20},{5,21},{6,22},{7,23},{8,24},{9,... | collective-permute-start | bytes 196616 | tf_op jit(solution)/shard_map/ppermute | solution.py:332
  26.0 1.4 %collective-permute-start.13 = (bf16[256,128]{1,0:T(8,128)(2,1)S(1)}, bf16[256,128]{1,0:T(8,128)(2,1)S(1)}, u32[]{:S(2)}, u32[]{:S(2)}) collective-permute-start(bf16[256,128]{1,0:T(8,128)(2,1)S(1)} %get-tuple-element.82.refs_0_._.own), channel_id=1, source_target_pairs={{0,18},{1,19},{2,16},{3,17},{4,22},{5,23},{6,20},{7,21},{8,26},{9,... | collective-permute-start | bytes 196616 | tf_op jit(solution)/shard_map/ppermute | solution.py:332
  27.4 0.4 collective-permute-start.14
  27.8 0.7 %copy-done.6 = s32[3,1,4,2]{2,3,1,0:T(2,128)S(1)} copy-done((s32[3,1,4,2]{2,3,1,0:T(2,128)S(1)}, s32[3,1,4,2]{2,3,1,0:T(2,128)}, u32[]{:S(2)}) %copy-start.6) | copy-done | bytes 120
  28.5 1.2 %fine_operators.1 = (bf16[256,256]{1,0:T(8,128)(2,1)S(1)}, bf16[256,256]{1,0:T(8,128)(2,1)S(1)}, bf16[256,256]{1,0:T(8,128)(2,1)S(1)}, f32[256,256]{1,0:T(8,128)S(1)}) custom-call(bf16[256,128]{1,0:T(8,128)(2,1)S(1)} %get-tuple-element.82.refs_0_._.own, s32[3,1,2,4]{3,2,1,0:T(2,128)S(1)} %bitcast.5, bf16[3,1,4,2,64,64]{5,4,3,2,1,0:T(8,128)(2,1)S(1)} %copy-done.2, ...), custom_call_target="tpu_custom_call" | custom-call | flops 134217728 | bytes 1378400 | tf_op jit(solution)/shard_map/fine_operators/pallas_call | solution.py:52
  29.7 1.1 %coarse_operators.1.refs_0_.inverse = bf16[256,1024]{1,0:T(8,128)(2,1)S(1)} custom-call(bf16[256,128]{1,0:T(8,128)(2,1)S(1)} %get-tuple-element.82.refs_0_._.own, bf16[256,128]{1,0:T(8,128)(2,1)S(1)} %collective-permute-done.12.refs_1_.far, s32[3,1,2,4]{3,2,1,0:T(2,128)S(1)} %bitcast.6, bf16[256,1024]{1,0:T(8,128)(2,1)S(1)} %copy-done.4, ...), custom_call_target="tpu_custom_call" | custom-call | flops 201326592 | bytes 984160 | tf_op jit(solution)/shard_map/coarse_operators/pallas_call | solution.py:52
  30.8 0.1 collective-permute-start.17
  30.9 2.5 %collective-permute-done.13.far = bf16[256,128]{1,0:T(8,128)(2,1)S(1)} collective-permute-done((bf16[256,128]{1,0:T(8,128)(2,1)S(1)}, bf16[256,128]{1,0:T(8,128)(2,1)S(1)}, u32[]{:S(2)}, u32[]{:S(2)}) %collective-permute-start.13) | collective-permute-done | bytes 65568 | tf_op jit(solution)/shard_map/ppermute | solution.py:332
  33.5 0.1 collective-permute-start.15
  33.6 0.2 coarse.1.refs_2_
  33.8 1.0 %collective-permute-done.15.refs_0_ = bf16[256,128]{1,0:T(8,128)(2,1)S(1)} collective-permute-done((bf16[256,128]{1,0:T(8,128)(2,1)S(1)}, bf16[256,128]{1,0:T(8,128)(2,1)S(1)}, u32[]{:S(2)}, u32[]{:S(2)}) %collective-permute-start.15) | collective-permute-done | bytes 65568 | tf_op jit(solution)/shard_map/ppermute | solution.py:323
  34.8 0.4 up.1
  35.2 1.4 %collective-permute-start.20 = (bf16[256,128]{1,0:T(8,128)(2,1)S(1)}, bf16[256,128]{1,0:T(8,128)(2,1)S(1)}, u32[]{:S(2)}, u32[]{:S(2)}) collective-permute-start(bf16[256,128]{1,0:T(8,128)(2,1)S(1)} %get-tuple-element.90), channel_id=1, source_target_pairs={{0,12},{4,8},{8,4},{12,0},{16,28},{20,24},{24,20},{28,16},{1,13},{... | collective-permute-start | bytes 196616 | tf_op jit(solution)/shard_map/ppermute | solution.py:323
  36.6 1.5 %collective-permute-start.18 = (bf16[256,128]{1,0:T(8,128)(2,1)S(1)}, bf16[256,128]{1,0:T(8,128)(2,1)S(1)}, u32[]{:S(2)}, u32[]{:S(2)}) collective-permute-start(bf16[256,128]{1,0:T(8,128)(2,1)S(1)} %get-tuple-element.90), channel_id=1, source_target_pairs={{0,8},{4,12},{8,0},{12,4},{16,24},{20,28},{24,16},{28,20},{1,9},{5... | collective-permute-start | bytes 196616 | tf_op jit(solution)/shard_map/ppermute | solution.py:323
  38.1 0.7 %collective-permute-start.19 = (bf16[256,128]{1,0:T(8,128)(2,1)S(1)}, bf16[256,128]{1,0:T(8,128)(2,1)S(1)}, u32[]{:S(2)}, u32[]{:S(2)}) collective-permute-start(bf16[256,128]{1,0:T(8,128)(2,1)S(1)} %get-tuple-element.91.refs_0_), channel_id=1, source_target_pairs={{0,4},{4,0},{8,12},{12,8},{16,20},{20,16},{24,28},{28,24},{1,5},{5... | collective-permute-start | bytes 196616 | tf_op jit(solution)/shard_map/ppermute | solution.py:323
  38.8 0.8 %output.3.refs_5_ = f32[1,256,512]{2,1,0:T(8,128)} custom-call(bf16[256,128]{1,0:T(8,128)(2,1)S(1)} %get-tuple-element.91.refs_0_, f32[256,512]{1,0:T(8,128)S(1)} %get-tuple-element.86.base.refs_1_.refs_2_, bf16[256,256]{1,0:T(8,128)(2,1)S(1)} %get-tuple-element.92.refs_2_.refs_3_, f32[256,256]{1,0:T(8,128)S(1)} %get-tuple-element.93.refs_3_.refs_4_, ...), custom_call_target="tpu_custom_call" | custom-call | flops 16777216 | bytes 1114112 | tf_op jit(solution)/shard_map/output/pallas_call | solution.py:52
  39.6 1.5 %collective-permute-done.20.refs_0_ = bf16[256,128]{1,0:T(8,128)(2,1)S(1)} collective-permute-done((bf16[256,128]{1,0:T(8,128)(2,1)S(1)}, bf16[256,128]{1,0:T(8,128)(2,1)S(1)}, u32[]{:S(2)}, u32[]{:S(2)}) %collective-permute-start.20) | collective-permute-done | bytes 65568 | tf_op jit(solution)/shard_map/ppermute | solution.py:323
  41.2 0.8 %output.4.refs_6_ = f32[1,256,512]{2,1,0:T(8,128)} custom-call(bf16[256,128]{1,0:T(8,128)(2,1)S(1)} %collective-permute-done.20.refs_0_, f32[256,512]{1,0:T(8,128)S(1)} %get-tuple-element.86.base.refs_1_.refs_2_, bf16[256,256]{1,0:T(8,128)(2,1)S(1)} %get-tuple-element.92.refs_2_.refs_3_, ...), custom_call_target="tpu_custom_call", output_to_operand_aliasing={{}: (5, {})} | custom-call | flops 16777216 | bytes 1638400 | tf_op jit(solution)/shard_map/output/pallas_call | solution.py:52
  42.0 0.4 collective-permute-done.19.refs_1_
  42.4 0.9 %output.5 = f32[1,256,512]{2,1,0:T(8,128)} custom-call(bf16[256,128]{1,0:T(8,128)(2,1)S(1)} %collective-permute-done.18.refs_0_, bf16[256,128]{1,0:T(8,128)(2,1)S(1)} %collective-permute-done.19.refs_1_, f32[256,512]{1,0:T(8,128)S(1)} %get-tuple-element.86.base.refs_1_.refs_2_, ...), custom_call_target="tpu_custom_call", output_to_operand_aliasing={{}: (6, {})} | custom-call | flops 33554432 | bytes 1703936 | tf_op jit(solution)/shard_map/output/pallas_call | solution.py:52
  (30 shorter events, 0.1 us)
Async XLA Ops:
  0.0 4.4 %copy-start = (bf16[3,1,4,5,64,64]{5,4,3,2,1,0:T(8,128)(2,1)S(1)}, bf16[3,1,4,5,64,64]{5,4,3,2,1,0:T(8,128)(2,1)}, u32[]{:S(2)}) copy-start(bf16[3,1,4,5,64,64]{5,4,3,2,1,0:T(8,128)(2,1)} %blocks.7) | copy-start | bytes 1474564
  0.0 4.4 %copy-start.3 = (f32[1,256,512]{2,1,0:T(8,128)S(1)}, f32[1,256,512]{2,1,0:T(8,128)}, u32[]{:S(2)}) copy-start(f32[1,256,512]{2,1,0:T(8,128)} %rhs.3) | copy-start | bytes 1572868
  1.3 4.8 %collective-permute-start.1 = (bf16[64,512]{1,0:T(8,128)(2,1)S(1)}, bf16[64,512]{1,0:T(8,128)(2,1)S(1)}, u32[]{:S(2)}, u32[]{:S(2)}) collective-permute-start(bf16[64,512]{1,0:T(8,128)(2,1)S(1)} %get-tuple-element.54), channel_id=1, source_target_pairs={{0,1},{1,0},{2,3},{3,2},{4,5},{5,4},{6,7},{7,6},{8,9},{9,8},{10,11... | collective-permute-start | bytes 196616 | tf_op jit(solution)/shard_map/ppermute | solution.py:323
  1.8 4.3 %collective-permute-start = (bf16[64,256]{1,0:T(8,128)(2,1)S(1)}, bf16[64,256]{1,0:T(8,128)(2,1)S(1)}, u32[]{:S(2)}, u32[]{:S(2)}) collective-permute-start(bf16[64,256]{1,0:T(8,128)(2,1)S(1)} %get-tuple-element.50._), channel_id=1, source_target_pairs={{0,3},{1,2},{2,1},{3,0},{4,7},{5,6},{6,5},{7,4},{8,11},{9,10},{10,... | collective-permute-start | bytes 98312 | tf_op jit(solution)/shard_map/ppermute | solution.py:338
  4.4 3.6 %collective-permute-start.5 = (bf16[64,256]{1,0:T(8,128)(2,1)S(1)}, bf16[64,256]{1,0:T(8,128)(2,1)S(1)}, u32[]{:S(2)}, u32[]{:S(2)}) collective-permute-start(bf16[64,256]{1,0:T(8,128)(2,1)S(1)} %get-tuple-element.65), channel_id=1, source_target_pairs={{0,3},{1,2},{2,1},{3,0},{4,7},{5,6},{6,5},{7,4},{8,11},{9,10},{10,... | collective-permute-start | bytes 98312 | tf_op jit(solution)/shard_map/ppermute | solution.py:338
  6.1 3.5 %copy-start.1 = (bf16[3,1,4,3,64,64]{5,4,3,2,1,0:T(8,128)(2,1)S(1)}, bf16[3,1,4,3,64,64]{5,4,3,2,1,0:T(8,128)(2,1)}, u32[]{:S(2)}) copy-start(bf16[3,1,4,3,64,64]{5,4,3,2,1,0:T(8,128)(2,1)} %rblocks.5) | copy-start | bytes 884740
  6.3 4.5 %collective-permute-start.2 = (bf16[256,128]{1,0:T(8,128)(2,1)S(1)}, bf16[256,128]{1,0:T(8,128)(2,1)S(1)}, u32[]{:S(2)}, u32[]{:S(2)}) collective-permute-start(bf16[256,128]{1,0:T(8,128)(2,1)S(1)} %get-tuple-element.55._), channel_id=1, source_target_pairs={{0,4},{4,0},{8,12},{12,8},{16,20},{20,16},{24,28},{28,24},{1,5},{5... | collective-permute-start | bytes 196616 | tf_op jit(solution)/shard_map/ppermute | solution.py:323
  8.0 1.6 %copy-start.5 = (s32[3,1,4,3]{2,1,3,0:T(1,128)S(1)}, s32[3,1,4,3]{2,1,3,0:T(1,128)}, u32[]{:S(2)}) copy-start(s32[3,1,4,3]{2,1,3,0:T(1,128)} %param.11) | copy-start | bytes 436
  8.2 5.0 %collective-permute-start.6 = (bf16[256,128]{1,0:T(8,128)(2,1)S(1)}, bf16[256,128]{1,0:T(8,128)(2,1)S(1)}, u32[]{:S(2)}, u32[]{:S(2)}) collective-permute-start(bf16[256,128]{1,0:T(8,128)(2,1)S(1)} %get-tuple-element.67), channel_id=1, source_target_pairs={{0,4},{4,0},{8,12},{12,8},{16,20},{20,16},{24,28},{28,24},{1,5},{5... | collective-permute-start | bytes 196616 | tf_op jit(solution)/shard_map/ppermute | solution.py:323
  11.0 3.9 %collective-permute-start.3 = (bf16[64,128]{1,0:T(8,128)(2,1)S(1)}, bf16[64,128]{1,0:T(8,128)(2,1)S(1)}, u32[]{:S(2)}, u32[]{:S(2)}) collective-permute-start(bf16[64,128]{1,0:T(8,128)(2,1)S(1)} %get-tuple-element.63), channel_id=1, source_target_pairs={{0,3},{1,2},{2,1},{3,0},{4,7},{5,6},{6,5},{7,4},{8,11},{9,10},{10,... | collective-permute-start | bytes 49160 | tf_op jit(solution)/shard_map/ppermute | solution.py:338
  12.6 2.3 %collective-permute-start.4 = (bf16[64,128]{1,0:T(8,128)(2,1)S(1)}, bf16[64,128]{1,0:T(8,128)(2,1)S(1)}, u32[]{:S(2)}, u32[]{:S(2)}) collective-permute-start(bf16[64,128]{1,0:T(8,128)(2,1)S(1)} %get-tuple-element.64), channel_id=1, source_target_pairs={{0,1},{1,0},{2,3},{3,2},{4,5},{5,4},{6,7},{7,6},{8,9},{9,8},{10,11... | collective-permute-start | bytes 49160 | tf_op jit(solution)/shard_map/ppermute | solution.py:323
  13.4 4.7 %collective-permute-start.7 = (bf16[64,128]{1,0:T(8,128)(2,1)S(1)}, bf16[64,128]{1,0:T(8,128)(2,1)S(1)}, u32[]{:S(2)}, u32[]{:S(2)}) collective-permute-start(bf16[64,128]{1,0:T(8,128)(2,1)S(1)} %get-tuple-element.72), channel_id=1, source_target_pairs={{0,3},{1,2},{2,1},{3,0},{4,7},{5,6},{6,5},{7,4},{8,11},{9,10},{10,... | collective-permute-start | bytes 49160 | tf_op jit(solution)/shard_map/ppermute | solution.py:338
  14.2 3.9 %collective-permute-start.8 = (bf16[64,128]{1,0:T(8,128)(2,1)S(1)}, bf16[64,128]{1,0:T(8,128)(2,1)S(1)}, u32[]{:S(2)}, u32[]{:S(2)}) collective-permute-start(bf16[64,128]{1,0:T(8,128)(2,1)S(1)} %get-tuple-element.73), channel_id=1, source_target_pairs={{0,1},{1,0},{2,3},{3,2},{4,5},{5,4},{6,7},{7,6},{8,9},{9,8},{10,11... | collective-permute-start | bytes 49160 | tf_op jit(solution)/shard_map/ppermute | solution.py:323
  15.1 4.3 %collective-permute-start.9 = (bf16[256,128]{1,0:T(8,128)(2,1)S(1)}, bf16[256,128]{1,0:T(8,128)(2,1)S(1)}, u32[]{:S(2)}, u32[]{:S(2)}) collective-permute-start(bf16[256,128]{1,0:T(8,128)(2,1)S(1)} %get-tuple-element.69._), channel_id=1, source_target_pairs={{0,8},{4,12},{8,0},{12,4},{16,24},{20,28},{24,16},{28,20},{1,9},{5... | collective-permute-start | bytes 196616 | tf_op jit(solution)/shard_map/ppermute | solution.py:323
  16.8 11.0 %collective-permute-start.12 = (bf16[256,128]{1,0:T(8,128)(2,1)S(1)}, bf16[256,128]{1,0:T(8,128)(2,1)S(1)}, u32[]{:S(2)}, u32[]{:S(2)}) collective-permute-start(bf16[256,128]{1,0:T(8,128)(2,1)S(1)} %get-tuple-element.83.near), channel_id=1, source_target_pairs={{0,4},{4,0},{8,12},{12,8},{16,20},{20,16},{24,28},{28,24},{1,5},{5... | collective-permute-start | bytes 196616 | tf_op jit(solution)/shard_map/ppermute | solution.py:323
  19.7 3.2 %collective-permute-start.10 = (bf16[64,128]{1,0:T(8,128)(2,1)S(1)}, bf16[64,128]{1,0:T(8,128)(2,1)S(1)}, u32[]{:S(2)}, u32[]{:S(2)}) collective-permute-start(bf16[64,128]{1,0:T(8,128)(2,1)S(1)} %get-tuple-element.80), channel_id=1, source_target_pairs={{0,3},{1,2},{2,1},{3,0},{4,7},{5,6},{6,5},{7,4},{8,11},{9,10},{10,... | collective-permute-start | bytes 49160 | tf_op jit(solution)/shard_map/ppermute | solution.py:338
  20.6 2.3 %collective-permute-start.11 = (bf16[64,128]{1,0:T(8,128)(2,1)S(1)}, bf16[64,128]{1,0:T(8,128)(2,1)S(1)}, u32[]{:S(2)}, u32[]{:S(2)}) collective-permute-start(bf16[64,128]{1,0:T(8,128)(2,1)S(1)} %get-tuple-element.81), channel_id=1, source_target_pairs={{0,1},{1,0},{2,3},{3,2},{4,5},{5,4},{6,7},{7,6},{8,9},{9,8},{10,11... | collective-permute-start | bytes 49160 | tf_op jit(solution)/shard_map/ppermute | solution.py:323
  22.2 5.6 %copy-start.2 = (bf16[3,1,4,2,64,64]{5,4,3,2,1,0:T(8,128)(2,1)S(1)}, bf16[3,1,4,2,64,64]{5,4,3,2,1,0:T(8,128)(2,1)}, u32[]{:S(2)}) copy-start(bf16[3,1,4,2,64,64]{5,4,3,2,1,0:T(8,128)(2,1)} %blocks_1.1) | copy-start | bytes 589828
  23.3 7.5 %collective-permute-start.16 = (bf16[256,128]{1,0:T(8,128)(2,1)S(1)}, bf16[256,128]{1,0:T(8,128)(2,1)S(1)}, u32[]{:S(2)}, u32[]{:S(2)}) collective-permute-start(bf16[256,128]{1,0:T(8,128)(2,1)S(1)} %get-tuple-element.82.refs_0_._.own), channel_id=1, source_target_pairs={{0,16},{1,17},{2,18},{3,19},{4,20},{5,21},{6,22},{7,23},{8,24},{9,... | collective-permute-start | bytes 196616 | tf_op jit(solution)/shard_map/ppermute | solution.py:332
  26.0 7.5 %collective-permute-start.13 = (bf16[256,128]{1,0:T(8,128)(2,1)S(1)}, bf16[256,128]{1,0:T(8,128)(2,1)S(1)}, u32[]{:S(2)}, u32[]{:S(2)}) collective-permute-start(bf16[256,128]{1,0:T(8,128)(2,1)S(1)} %get-tuple-element.82.refs_0_._.own), channel_id=1, source_target_pairs={{0,18},{1,19},{2,16},{3,17},{4,22},{5,23},{6,20},{7,21},{8,26},{9,... | collective-permute-start | bytes 196616 | tf_op jit(solution)/shard_map/ppermute | solution.py:332
  27.4 6.1 %collective-permute-start.14 = (bf16[256,128]{1,0:T(8,128)(2,1)S(1)}, bf16[256,128]{1,0:T(8,128)(2,1)S(1)}, u32[]{:S(2)}, u32[]{:S(2)}) collective-permute-start(bf16[256,128]{1,0:T(8,128)(2,1)S(1)} %get-tuple-element.82.refs_0_._.own), channel_id=1, source_target_pairs={{0,2},{1,3},{2,0},{3,1},{4,6},{5,7},{6,4},{7,5},{8,10},{9,11},{10,... | collective-permute-start | bytes 196616 | tf_op jit(solution)/shard_map/ppermute | solution.py:323
  27.8 0.7 %copy-start.6 = (s32[3,1,4,2]{2,3,1,0:T(2,128)S(1)}, s32[3,1,4,2]{2,3,1,0:T(2,128)}, u32[]{:S(2)}) copy-start(s32[3,1,4,2]{2,3,1,0:T(2,128)} %param.13) | copy-start | bytes 292
  28.5 1.2 %copy-start.4 = (bf16[256,1024]{1,0:T(8,128)(2,1)S(1)}, bf16[256,1024]{1,0:T(8,128)(2,1)}, u32[]{:S(2)}) copy-start(bf16[256,1024]{1,0:T(8,128)(2,1)} %refs_3_.1) | copy-start | bytes 1572868
  30.8 3.0 %collective-permute-start.17 = (bf16[256,128]{1,0:T(8,128)(2,1)S(1)}, bf16[256,128]{1,0:T(8,128)(2,1)S(1)}, u32[]{:S(2)}, u32[]{:S(2)}) collective-permute-start(bf16[256,128]{1,0:T(8,128)(2,1)S(1)} %share_sum.3.refs_1_), channel_id=1, source_target_pairs={{0,1},{1,0},{2,3},{3,2},{4,5},{5,4},{6,7},{7,6},{8,9},{9,8},{10,11... | collective-permute-start | bytes 196616 | tf_op jit(solution)/shard_map/ppermute | solution.py:323
  33.5 1.3 %collective-permute-start.15 = (bf16[256,128]{1,0:T(8,128)(2,1)S(1)}, bf16[256,128]{1,0:T(8,128)(2,1)S(1)}, u32[]{:S(2)}, u32[]{:S(2)}) collective-permute-start(bf16[256,128]{1,0:T(8,128)(2,1)S(1)} %share_sum.2.refs_0_), channel_id=1, source_target_pairs={{0,1},{1,0},{2,3},{3,2},{4,5},{5,4},{6,7},{7,6},{8,9},{9,8},{10,11... | collective-permute-start | bytes 196616 | tf_op jit(solution)/shard_map/ppermute | solution.py:323
  35.2 5.9 %collective-permute-start.20 = (bf16[256,128]{1,0:T(8,128)(2,1)S(1)}, bf16[256,128]{1,0:T(8,128)(2,1)S(1)}, u32[]{:S(2)}, u32[]{:S(2)}) collective-permute-start(bf16[256,128]{1,0:T(8,128)(2,1)S(1)} %get-tuple-element.90), channel_id=1, source_target_pairs={{0,12},{4,8},{8,4},{12,0},{16,28},{20,24},{24,20},{28,16},{1,13},{... | collective-permute-start | bytes 196616 | tf_op jit(solution)/shard_map/ppermute | solution.py:323
  36.6 5.4 %collective-permute-start.18 = (bf16[256,128]{1,0:T(8,128)(2,1)S(1)}, bf16[256,128]{1,0:T(8,128)(2,1)S(1)}, u32[]{:S(2)}, u32[]{:S(2)}) collective-permute-start(bf16[256,128]{1,0:T(8,128)(2,1)S(1)} %get-tuple-element.90), channel_id=1, source_target_pairs={{0,8},{4,12},{8,0},{12,4},{16,24},{20,28},{24,16},{28,20},{1,9},{5... | collective-permute-start | bytes 196616 | tf_op jit(solution)/shard_map/ppermute | solution.py:323
  38.1 4.3 %collective-permute-start.19 = (bf16[256,128]{1,0:T(8,128)(2,1)S(1)}, bf16[256,128]{1,0:T(8,128)(2,1)S(1)}, u32[]{:S(2)}, u32[]{:S(2)}) collective-permute-start(bf16[256,128]{1,0:T(8,128)(2,1)S(1)} %get-tuple-element.91.refs_0_), channel_id=1, source_target_pairs={{0,4},{4,0},{8,12},{12,8},{16,20},{20,16},{24,28},{28,24},{1,5},{5... | collective-permute-start | bytes 196616 | tf_op jit(solution)/shard_map/ppermute | solution.py:323

commit v19 on v14

--- a/solution.py
+++ b/solution.py
@@ -140,7 +140,7 @@
 
 
 def start_kernel(places, rhs, blocks, *refs):
-    table, held, inner_ref, *outers, rows, outer, pivots, sems = refs
+    table, held, *ends, rows, inner, outer, pivots, sems = refs
     count, size = blocks.shape[2], blocks.shape[4]
     copies = []
     for slot, which in enumerate((0, count - 1)):
@@ -157,11 +157,12 @@
         (rows[slot] * (relax_down / diagonal_of(pivots[slot].astype(f32)))).astype(bf16)
         for slot in range(2)
     )
-    put_ends(first, last, inner_ref, outer)
-    for ref, pair in zip(outers, places):
-        width = ref.shape[1] // 2
-        for slot, place in enumerate(pair):
-            ref[:, slot * width : (slot + 1) * width] = outer[:, lanes_of(place, width)]
+    put_ends(first, last, inner, outer)
+    for source, made in ((inner, ends[: len(places)]), (outer, ends[len(places) :])):
+        for ref, pair in zip(made, places):
+            width = ref.shape[1] // 2
+            for slot, place in enumerate(pair):
+                ref[:, slot * width : (slot + 1) * width] = source[:, lanes_of(place, width)]
 
 
 def first_local_kernel(rhs, _, cols, blocks, rest, base, local, rim, scale):
@@ -188,7 +189,7 @@
     for slot, (ref, place) in enumerate(zip(refs, places)):
         lanes = lanes_of(place, width)
         columns = pl.ds(slot * width, width)
-        rims = jnp.concatenate([inner[:, lanes], outer[:, columns]], axis=0)
+        rims = jnp.concatenate([inner[:, columns], outer[:, columns]], axis=0)
         ref[...] = (rest[:, lanes] - matmul(rim[...], rims)).astype(bf16)
 
 
@@ -376,26 +377,27 @@
         return (0, far, half), (1, given, width)
 
     pairs = [(place_of(1, given), place_of(0, given)) for given in (1, 0)]
-    gcols, inner, *outers = run(
+    gcols, *ends = run(
         functools.partial(start_kernel, pairs), "start",
-        [array(galerkin_cols.shape, jnp.int32), ends_shape(fields)] + [ends_shape(half)] * 2,
+        [array(galerkin_cols.shape, jnp.int32)] + [ends_shape(half)] * 4,
         [in_hbm(level_rhs), in_hbm(galerkin_blocks), in_hbm(galerkin_cols)],
         scratch=[
-            pltpu.VMEM((2, size, fields), f32), pltpu.VMEM((size, fields), bf16),
+            pltpu.VMEM((2, size, fields), f32),
+            pltpu.VMEM((size, fields), bf16), pltpu.VMEM((size, fields), bf16),
             pltpu.VMEM((2, size, size), bf16), pltpu.SemaphoreType.DMA((5,)),
         ],
     )
     gcols = in_vmem(gcols), scalars()
-    first = outers[0]
-    outers = [swap_outer(outer) for outer in outers]
-    inner = exchange(inner, "narrow", 1)
+    first = ends[0]
+    outers = [swap_outer(outer) for outer in ends[2:]]
+    inners = [exchange(inner, "narrow", 1) for inner in ends[:2]]
     rest, base, local, rim, scale = run(
         first_local_kernel, "first_local", [array((rows, fields), f32)] * 2 + operator_shapes,
         [level_rhs, first, gcols, of_level(galerkin_blocks, 0)], flops=flops(fields),
     )
     operators = [(scale, local)]
     sent, kept = [], []
-    for places, outer in zip(pairs, outers):
+    for places, inner, outer in zip(pairs, inners, outers):
         far, near = run(
             functools.partial(first_residual_kernel, places), "first_residual", [chunk_shape] * 2,
             [rest, rim, outer, inner],

time: 42.9 us -> 43 us (level)
    ppermute x14 -> x15, starting transfers between devices: 12.9 us -> 13.2 us  [exchange(): return lax.ppermute(value, axis, [(i, i ^ bit) for i in range(count)])]
    ppermute x14 -> x15, waiting for transfers between devices: 3.38 us -> 3.62 us  [exchange(): return lax.ppermute(value, axis, [(i, i ^ bit) for i in range(count)])]
  transfers between devices with their start and end apart: 21 -> 22, of which waited for: 8 -> 8; matrix products, arithmetic and copies ran while one was open for 0% -> 0% of each run, Pallas kernels for 24% -> 24%
where the time goes in v19:
time: 43 us; the launch traced here: 42.8 us
  starting transfers between devices  23.1 us (54%)
  Pallas kernels  12.8 us (30%)
  waiting for transfers between devices  5.95 us (14%)
  local copies, waits for them, and re-layouts  0.71 us (2%)
    ppermute x15, starting transfers between devices, exchange(): return lax.ppermute(value, axis, [(i, i ^ bit) for i in range(count)])  13.2 us
    pallas_call x22, Pallas kernels, run(): pl.pallas_call(body, grid=(1,) if windows else (), out_shape=[out_space(o...  12.8 us
    ppermute x5, starting transfers between devices, swap_outer(): return lax.ppermute(outer, 'narrow', gaps)  5.85 us
    ppermute x2, starting transfers between devices, exchange_both(): return lax.ppermute(value, ('wide', 'narrow'), pairs)  4.07 us
    ppermute x15, waiting for transfers between devices, exchange(): return lax.ppermute(value, axis, [(i, i ^ bit) for i in range(count)])  3.62 us
    ppermute x2, waiting for transfers between devices, exchange_both(): return lax.ppermute(value, ('wide', 'narrow'), pairs)  1.32 us
    ppermute x5, waiting for transfers between devices, swap_outer(): return lax.ppermute(outer, 'narrow', gaps)  1.01 us
  transfers between devices with their start and end apart: 22, of which 8 were waited for; matrix products, arithmetic and copies ran while one was open for 0% of the time, Pallas kernels for 24%

profile of v19, /device:TPU:0, one launch (start us, length us, event | category | flops | bytes accessed | tf_op | source)
XLA Modules:
  0.0 42.8 jit_solution(5707959450978790307)
XLA Ops:
  0.0 1.3 %start.1 = (s32[3,1,4,5]{3,2,1,0:T(4,128)S(1)}, bf16[64,256]{1,0:T(8,128)(2,1)S(1)}, bf16[64,256]{1,0:T(8,128)(2,1)S(1)}, bf16[64,256]{1,0:T(8,128)(2,1)S(1)}, bf16[64,256]{1,0:T(8,128)(2,1)S(1)}) custom-call(f32[1,256,512]{2,1,0:T(8,128)} %rhs.3, bf16[3,1,4,5,64,64]{5,4,3,2,1,0:T(8,128)(2,1)} %blocks.7, s32[3,1,4,5]{3,2,1,0:T(4,128)} %refs_0_.1), custom_call_target="tpu_custom_call" | custom-call | bytes 1016048 | tf_op jit(solution)/shard_map/start/pallas_call | solution.py:52
  1.3 0.5 %collective-permute-start.1 = (bf16[64,256]{1,0:T(8,128)(2,1)S(1)}, bf16[64,256]{1,0:T(8,128)(2,1)S(1)}, u32[]{:S(2)}, u32[]{:S(2)}) collective-permute-start(bf16[64,256]{1,0:T(8,128)(2,1)S(1)} %get-tuple-element.51._), channel_id=1, source_target_pairs={{0,1},{1,0},{2,3},{3,2},{4,5},{5,4},{6,7},{7,6},{8,9},{9,8},{10,11... | collective-permute-start | bytes 98312 | tf_op jit(solution)/shard_map/ppermute | solution.py:324
  1.8 2.6 %collective-permute-start = (bf16[64,256]{1,0:T(8,128)(2,1)S(1)}, bf16[64,256]{1,0:T(8,128)(2,1)S(1)}, u32[]{:S(2)}, u32[]{:S(2)}) collective-permute-start(bf16[64,256]{1,0:T(8,128)(2,1)S(1)} %get-tuple-element.55), channel_id=1, source_target_pairs={{0,3},{1,2},{2,1},{3,0},{4,7},{5,6},{6,5},{7,4},{8,11},{9,10},{10,... | collective-permute-start | bytes 98312 | tf_op jit(solution)/shard_map/ppermute | solution.py:339
  4.5 0.1 collective-permute-start.6
  4.6 1.1 %first_local.1 = (f32[256,512]{1,0:T(8,128)S(1)}, f32[256,512]{1,0:T(8,128)S(1)}, bf16[256,256]{1,0:T(8,128)(2,1)S(1)}, bf16[256,128]{1,0:T(8,128)(2,1)S(1)}, f32[256,1]{1,0:T(8,128)S(1)}) custom-call(f32[1,256,512]{2,1,0:T(8,128)S(1)} %copy-done.3, bf16[64,256]{1,0:T(8,128)(2,1)S(1)} %get-tuple-element.51._, s32[3,1,4,5]{3,2,1,0:T(4,128)S(1)} %get-tuple-element.52.cols, ...), custom_call_target="tpu_custom_call" | custom-call | flops 67108864 | bytes 1048816 | tf_op jit(solution)/shard_map/first_local/pallas_call | solution.py:52
  5.8 0.3 collective-permute-done.outer
  6.1 0.2 first_residual.2
  6.3 1.8 %collective-permute-start.2 = (bf16[256,128]{1,0:T(8,128)(2,1)S(1)}, bf16[256,128]{1,0:T(8,128)(2,1)S(1)}, u32[]{:S(2)}, u32[]{:S(2)}) collective-permute-start(bf16[256,128]{1,0:T(8,128)(2,1)S(1)} %get-tuple-element.56._), channel_id=1, source_target_pairs={{0,4},{4,0},{8,12},{12,8},{16,20},{20,16},{24,28},{28,24},{1,5},{5... | collective-permute-start | bytes 196616 | tf_op jit(solution)/shard_map/ppermute | solution.py:324
  8.1 0.2 first_residual.3
  8.2 1.4 %collective-permute-start.7 = (bf16[256,128]{1,0:T(8,128)(2,1)S(1)}, bf16[256,128]{1,0:T(8,128)(2,1)S(1)}, u32[]{:S(2)}, u32[]{:S(2)}) collective-permute-start(bf16[256,128]{1,0:T(8,128)(2,1)S(1)} %get-tuple-element.69), channel_id=1, source_target_pairs={{0,4},{4,0},{8,12},{12,8},{16,20},{20,16},{24,28},{28,24},{1,5},{5... | collective-permute-start | bytes 196616 | tf_op jit(solution)/shard_map/ppermute | solution.py:324
  9.7 1.1 %operators.2 = (bf16[256,512]{1,0:T(8,128)(2,1)S(1)}, bf16[256,256]{1,0:T(8,128)(2,1)S(1)}, bf16[256,128]{1,0:T(8,128)(2,1)S(1)}, f32[256,1]{1,0:T(8,128)S(1)}) custom-call(bf16[256,128]{1,0:T(8,128)(2,1)S(1)} %get-tuple-element.56._, s32[3,3,1,4]{3,2,1,0:T(1,128)S(1)} %bitcast.2, bf16[3,1,4,3,64,64]{5,4,3,2,1,0:T(8,128)(2,1)S(1)} %copy-done.1, ...), custom_call_target="tpu_custom_call" | custom-call | bytes 852352 | tf_op jit(solution)/shard_map/operators/pallas_call | solution.py:52
  10.8 0.2 join.3
  11.0 1.5 %collective-permute-start.3 = (bf16[64,128]{1,0:T(8,128)(2,1)S(1)}, bf16[64,128]{1,0:T(8,128)(2,1)S(1)}, u32[]{:S(2)}, u32[]{:S(2)}) collective-permute-start(bf16[64,128]{1,0:T(8,128)(2,1)S(1)} %get-tuple-element.64), channel_id=1, source_target_pairs={{0,3},{1,2},{2,1},{3,0},{4,7},{5,6},{6,5},{7,4},{8,11},{9,10},{10,... | collective-permute-start | bytes 49160 | tf_op jit(solution)/shard_map/ppermute | solution.py:339
  12.5 0.6 %collective-permute-start.4 = (bf16[64,128]{1,0:T(8,128)(2,1)S(1)}, bf16[64,128]{1,0:T(8,128)(2,1)S(1)}, u32[]{:S(2)}, u32[]{:S(2)}) collective-permute-start(bf16[64,128]{1,0:T(8,128)(2,1)S(1)} %get-tuple-element.65), channel_id=1, source_target_pairs={{0,1},{1,0},{2,3},{3,2},{4,5},{5,4},{6,7},{7,6},{8,9},{9,8},{10,11... | collective-permute-start | bytes 49160 | tf_op jit(solution)/shard_map/ppermute | solution.py:324
  13.2 0.2 join.4
  13.4 0.8 %collective-permute-start.8 = (bf16[64,128]{1,0:T(8,128)(2,1)S(1)}, bf16[64,128]{1,0:T(8,128)(2,1)S(1)}, u32[]{:S(2)}, u32[]{:S(2)}) collective-permute-start(bf16[64,128]{1,0:T(8,128)(2,1)S(1)} %get-tuple-element.74), channel_id=1, source_target_pairs={{0,3},{1,2},{2,1},{3,0},{4,7},{5,6},{6,5},{7,4},{8,11},{9,10},{10,... | collective-permute-start | bytes 49160 | tf_op jit(solution)/shard_map/ppermute | solution.py:339
  14.2 0.7 %collective-permute-start.9 = (bf16[64,128]{1,0:T(8,128)(2,1)S(1)}, bf16[64,128]{1,0:T(8,128)(2,1)S(1)}, u32[]{:S(2)}, u32[]{:S(2)}) collective-permute-start(bf16[64,128]{1,0:T(8,128)(2,1)S(1)} %get-tuple-element.75), channel_id=1, source_target_pairs={{0,1},{1,0},{2,3},{3,2},{4,5},{5,4},{6,7},{7,6},{8,9},{9,8},{10,11... | collective-permute-start | bytes 49160 | tf_op jit(solution)/shard_map/ppermute | solution.py:324
  14.9 0.2 residual.3
  15.1 1.6 %collective-permute-start.10 = (bf16[256,128]{1,0:T(8,128)(2,1)S(1)}, bf16[256,128]{1,0:T(8,128)(2,1)S(1)}, u32[]{:S(2)}, u32[]{:S(2)}) collective-permute-start(bf16[256,128]{1,0:T(8,128)(2,1)S(1)} %get-tuple-element.71._), channel_id=1, source_target_pairs={{0,8},{4,12},{8,0},{12,4},{16,24},{20,28},{24,16},{28,20},{1,9},{5... | collective-permute-start | bytes 196616 | tf_op jit(solution)/shard_map/ppermute | solution.py:324
  16.7 1.4 %collective-permute-start.13 = (bf16[256,128]{1,0:T(8,128)(2,1)S(1)}, bf16[256,128]{1,0:T(8,128)(2,1)S(1)}, u32[]{:S(2)}, u32[]{:S(2)}) collective-permute-start(bf16[256,128]{1,0:T(8,128)(2,1)S(1)} %get-tuple-element.85.near), channel_id=1, source_target_pairs={{0,4},{4,0},{8,12},{12,8},{16,20},{20,16},{24,28},{28,24},{1,5},{5... | collective-permute-start | bytes 196616 | tf_op jit(solution)/shard_map/ppermute | solution.py:324
  18.2 0.2 residual.4
  18.4 1.1 %operators.3 = (bf16[256,512]{1,0:T(8,128)(2,1)S(1)}, bf16[256,256]{1,0:T(8,128)(2,1)S(1)}, bf16[256,128]{1,0:T(8,128)(2,1)S(1)}, f32[256,1]{1,0:T(8,128)S(1)}) custom-call(bf16[256,128]{1,0:T(8,128)(2,1)S(1)} %get-tuple-element.71._, s32[3,3,1,4]{3,2,1,0:T(1,128)S(1)} %bitcast.3, bf16[3,1,4,3,64,64]{5,4,3,2,1,0:T(8,128)(2,1)S(1)} %copy-done.1, ...), custom_call_target="tpu_custom_call" | custom-call | bytes 852352 | tf_op jit(solution)/shard_map/operators/pallas_call | solution.py:52
  19.5 0.2 join.5
  19.7 0.9 %collective-permute-start.11 = (bf16[64,128]{1,0:T(8,128)(2,1)S(1)}, bf16[64,128]{1,0:T(8,128)(2,1)S(1)}, u32[]{:S(2)}, u32[]{:S(2)}) collective-permute-start(bf16[64,128]{1,0:T(8,128)(2,1)S(1)} %get-tuple-element.82), channel_id=1, source_target_pairs={{0,3},{1,2},{2,1},{3,0},{4,7},{5,6},{6,5},{7,4},{8,11},{9,10},{10,... | collective-permute-start | bytes 49160 | tf_op jit(solution)/shard_map/ppermute | solution.py:339
  20.6 1.0 %collective-permute-start.12 = (bf16[64,128]{1,0:T(8,128)(2,1)S(1)}, bf16[64,128]{1,0:T(8,128)(2,1)S(1)}, u32[]{:S(2)}, u32[]{:S(2)}) collective-permute-start(bf16[64,128]{1,0:T(8,128)(2,1)S(1)} %get-tuple-element.83), channel_id=1, source_target_pairs={{0,1},{1,0},{2,3},{3,2},{4,5},{5,4},{6,7},{7,6},{8,9},{9,8},{10,11... | collective-permute-start | bytes 49160 | tf_op jit(solution)/shard_map/ppermute | solution.py:324
  21.6 0.7 %share.1 = bf16[256,256]{1,0:T(8,128)(2,1)S(1)} custom-call(bf16[256,128]{1,0:T(8,128)(2,1)S(1)} %get-tuple-element.79._.smoothed, s32[3,3,1,4]{3,2,1,0:T(1,128)S(1)} %bitcast.4, bf16[3,1,4,3,64,64]{5,4,3,2,1,0:T(8,128)(2,1)S(1)} %copy-done.1), custom_call_target="tpu_custom_call" | custom-call | bytes 360592 | tf_op jit(solution)/shard_map/share/pallas_call | solution.py:52
  22.3 0.7 %collective-permute-done.11.outer = bf16[64,128]{1,0:T(8,128)(2,1)S(1)} collective-permute-done((bf16[64,128]{1,0:T(8,128)(2,1)S(1)}, bf16[64,128]{1,0:T(8,128)(2,1)S(1)}, u32[]{:S(2)}, u32[]{:S(2)}) %collective-permute-start.11) | collective-permute-done | bytes 16416 | tf_op jit(solution)/shard_map/ppermute | solution.py:339
  23.0 0.4 residual.5
  23.4 3.7 %collective-permute-start.16 = (bf16[256,128]{1,0:T(8,128)(2,1)S(1)}, bf16[256,128]{1,0:T(8,128)(2,1)S(1)}, u32[]{:S(2)}, u32[]{:S(2)}) collective-permute-start(bf16[256,128]{1,0:T(8,128)(2,1)S(1)} %get-tuple-element.84.refs_0_._.own), channel_id=1, source_target_pairs={{0,18},{1,19},{2,16},{3,17},{4,22},{5,23},{6,20},{7,21},{8,26},{9,... | collective-permute-start | bytes 196616 | tf_op jit(solution)/shard_map/ppermute | solution.py:333
  27.1 0.4 collective-permute-start.17
  27.5 0.3 collective-permute-start.14
  27.9 0.7 %copy-done.6 = s32[3,1,4,2]{2,3,1,0:T(2,128)S(1)} copy-done((s32[3,1,4,2]{2,3,1,0:T(2,128)S(1)}, s32[3,1,4,2]{2,3,1,0:T(2,128)}, u32[]{:S(2)}) %copy-start.6) | copy-done | bytes 120
  28.5 1.2 %fine_operators.1 = (bf16[256,256]{1,0:T(8,128)(2,1)S(1)}, bf16[256,256]{1,0:T(8,128)(2,1)S(1)}, bf16[256,256]{1,0:T(8,128)(2,1)S(1)}, f32[256,256]{1,0:T(8,128)S(1)}) custom-call(bf16[256,128]{1,0:T(8,128)(2,1)S(1)} %get-tuple-element.84.refs_0_._.own, s32[3,1,2,4]{3,2,1,0:T(2,128)S(1)} %bitcast.5, bf16[3,1,4,2,64,64]{5,4,3,2,1,0:T(8,128)(2,1)S(1)} %copy-done.2, ...), custom_call_target="tpu_custom_call" | custom-call | flops 134217728 | bytes 1378400 | tf_op jit(solution)/shard_map/fine_operators/pallas_call | solution.py:52
  29.7 1.1 %coarse_operators.1.refs_0_.inverse = bf16[256,1024]{1,0:T(8,128)(2,1)S(1)} custom-call(bf16[256,128]{1,0:T(8,128)(2,1)S(1)} %get-tuple-element.84.refs_0_._.own, bf16[256,128]{1,0:T(8,128)(2,1)S(1)} %collective-permute-done.13.refs_1_.far, s32[3,1,2,4]{3,2,1,0:T(2,128)S(1)} %bitcast.6, bf16[256,1024]{1,0:T(8,128)(2,1)S(1)} %copy-done.4, ...), custom_call_target="tpu_custom_call" | custom-call | flops 201326592 | bytes 984160 | tf_op jit(solution)/shard_map/coarse_operators/pallas_call | solution.py:52
  30.9 0.1 collective-permute-done.16.far
  31.0 0.7 %collective-permute-done.17.own = bf16[256,128]{1,0:T(8,128)(2,1)S(1)} collective-permute-done((bf16[256,128]{1,0:T(8,128)(2,1)S(1)}, bf16[256,128]{1,0:T(8,128)(2,1)S(1)}, u32[]{:S(2)}, u32[]{:S(2)}) %collective-permute-start.17) | collective-permute-done | bytes 65568 | tf_op jit(solution)/shard_map/ppermute | solution.py:324
  31.7 1.2 %collective-permute-done.14.far = bf16[256,128]{1,0:T(8,128)(2,1)S(1)} collective-permute-done((bf16[256,128]{1,0:T(8,128)(2,1)S(1)}, bf16[256,128]{1,0:T(8,128)(2,1)S(1)}, u32[]{:S(2)}, u32[]{:S(2)}) %collective-permute-start.14) | collective-permute-done | bytes 65568 | tf_op jit(solution)/shard_map/ppermute | solution.py:333
  33.1 0.2 coarse.1.refs_2_
  33.3 1.0 %collective-permute-done.15.refs_0_ = bf16[256,128]{1,0:T(8,128)(2,1)S(1)} collective-permute-done((bf16[256,128]{1,0:T(8,128)(2,1)S(1)}, bf16[256,128]{1,0:T(8,128)(2,1)S(1)}, u32[]{:S(2)}, u32[]{:S(2)}) %collective-permute-start.15) | collective-permute-done | bytes 65568 | tf_op jit(solution)/shard_map/ppermute | solution.py:324
  34.3 0.4 %up.1 = (bf16[256,128]{1,0:T(8,128)(2,1)S(1)}, bf16[256,128]{1,0:T(8,128)(2,1)S(1)}) custom-call(bf16[256,1024]{1,0:T(8,128)(2,1)S(1)} %coarse_operators.1.refs_0_.inverse, bf16[256,128]{1,0:T(8,128)(2,1)S(1)} %collective-permute-done.15.refs_0_, bf16[256,128]{1,0:T(8,128)(2,1)S(1)} %collective-permute-done.18.refs_1_, f32[256,128]{1,0:T(8,128)S(1)} %coarse.1.refs_2_, ...), custom_call_target="tpu_custom_call" | custom-call | flops 50331648 | bytes 1048576 | tf_op jit(solution)/shard_map/up/pallas_call | solution.py:52
  34.7 2.1 %collective-permute-start.21 = (bf16[256,128]{1,0:T(8,128)(2,1)S(1)}, bf16[256,128]{1,0:T(8,128)(2,1)S(1)}, u32[]{:S(2)}, u32[]{:S(2)}) collective-permute-start(bf16[256,128]{1,0:T(8,128)(2,1)S(1)} %get-tuple-element.92), channel_id=1, source_target_pairs={{0,12},{4,8},{8,4},{12,0},{16,28},{20,24},{24,20},{28,16},{1,13},{... | collective-permute-start | bytes 196616 | tf_op jit(solution)/shard_map/ppermute | solution.py:324
  36.9 0.8 %collective-permute-start.19 = (bf16[256,128]{1,0:T(8,128)(2,1)S(1)}, bf16[256,128]{1,0:T(8,128)(2,1)S(1)}, u32[]{:S(2)}, u32[]{:S(2)}) collective-permute-start(bf16[256,128]{1,0:T(8,128)(2,1)S(1)} %get-tuple-element.92), channel_id=1, source_target_pairs={{0,8},{4,12},{8,0},{12,4},{16,24},{20,28},{24,16},{28,20},{1,9},{5... | collective-permute-start | bytes 196616 | tf_op jit(solution)/shard_map/ppermute | solution.py:324
  37.6 0.7 %collective-permute-start.20 = (bf16[256,128]{1,0:T(8,128)(2,1)S(1)}, bf16[256,128]{1,0:T(8,128)(2,1)S(1)}, u32[]{:S(2)}, u32[]{:S(2)}) collective-permute-start(bf16[256,128]{1,0:T(8,128)(2,1)S(1)} %get-tuple-element.93.refs_0_), channel_id=1, source_target_pairs={{0,4},{4,0},{8,12},{12,8},{16,20},{20,16},{24,28},{28,24},{1,5},{5... | collective-permute-start | bytes 196616 | tf_op jit(solution)/shard_map/ppermute | solution.py:324
  38.3 0.8 %output.3.refs_5_ = f32[1,256,512]{2,1,0:T(8,128)} custom-call(bf16[256,128]{1,0:T(8,128)(2,1)S(1)} %get-tuple-element.93.refs_0_, f32[256,512]{1,0:T(8,128)S(1)} %get-tuple-element.88.base.refs_1_.refs_2_, bf16[256,256]{1,0:T(8,128)(2,1)S(1)} %get-tuple-element.94.refs_2_.refs_3_, f32[256,256]{1,0:T(8,128)S(1)} %get-tuple-element.95.refs_3_.refs_4_, ...), custom_call_target="tpu_custom_call" | custom-call | flops 16777216 | bytes 1114112 | tf_op jit(solution)/shard_map/output/pallas_call | solution.py:52
  39.1 1.3 %collective-permute-done.21.refs_0_ = bf16[256,128]{1,0:T(8,128)(2,1)S(1)} collective-permute-done((bf16[256,128]{1,0:T(8,128)(2,1)S(1)}, bf16[256,128]{1,0:T(8,128)(2,1)S(1)}, u32[]{:S(2)}, u32[]{:S(2)}) %collective-permute-start.21) | collective-permute-done | bytes 65568 | tf_op jit(solution)/shard_map/ppermute | solution.py:324
  40.5 0.8 %output.4.refs_6_ = f32[1,256,512]{2,1,0:T(8,128)} custom-call(bf16[256,128]{1,0:T(8,128)(2,1)S(1)} %collective-permute-done.21.refs_0_, f32[256,512]{1,0:T(8,128)S(1)} %get-tuple-element.88.base.refs_1_.refs_2_, bf16[256,256]{1,0:T(8,128)(2,1)S(1)} %get-tuple-element.94.refs_2_.refs_3_, ...), custom_call_target="tpu_custom_call", output_to_operand_aliasing={{}: (5, {})} | custom-call | flops 16777216 | bytes 1638400 | tf_op jit(solution)/shard_map/output/pallas_call | solution.py:52
  41.3 0.6 %collective-permute-done.20.refs_1_ = bf16[256,128]{1,0:T(8,128)(2,1)S(1)} collective-permute-done((bf16[256,128]{1,0:T(8,128)(2,1)S(1)}, bf16[256,128]{1,0:T(8,128)(2,1)S(1)}, u32[]{:S(2)}, u32[]{:S(2)}) %collective-permute-start.20) | collective-permute-done | bytes 65568 | tf_op jit(solution)/shard_map/ppermute | solution.py:324
  41.9 0.9 %output.5 = f32[1,256,512]{2,1,0:T(8,128)} custom-call(bf16[256,128]{1,0:T(8,128)(2,1)S(1)} %collective-permute-done.19.refs_0_, bf16[256,128]{1,0:T(8,128)(2,1)S(1)} %collective-permute-done.20.refs_1_, f32[256,512]{1,0:T(8,128)S(1)} %get-tuple-element.88.base.refs_1_.refs_2_, ...), custom_call_target="tpu_custom_call", output_to_operand_aliasing={{}: (6, {})} | custom-call | flops 33554432 | bytes 1703936 | tf_op jit(solution)/shard_map/output/pallas_call | solution.py:52
  (32 shorter events, 0.3 us)
Async XLA Ops:
  0.0 4.6 %copy-start = (bf16[3,1,4,5,64,64]{5,4,3,2,1,0:T(8,128)(2,1)S(1)}, bf16[3,1,4,5,64,64]{5,4,3,2,1,0:T(8,128)(2,1)}, u32[]{:S(2)}) copy-start(bf16[3,1,4,5,64,64]{5,4,3,2,1,0:T(8,128)(2,1)} %blocks.7) | copy-start | bytes 1474564
  0.0 4.6 %copy-start.3 = (f32[1,256,512]{2,1,0:T(8,128)S(1)}, f32[1,256,512]{2,1,0:T(8,128)}, u32[]{:S(2)}) copy-start(f32[1,256,512]{2,1,0:T(8,128)} %rhs.3) | copy-start | bytes 1572868
  1.3 4.4 %collective-permute-start.1 = (bf16[64,256]{1,0:T(8,128)(2,1)S(1)}, bf16[64,256]{1,0:T(8,128)(2,1)S(1)}, u32[]{:S(2)}, u32[]{:S(2)}) collective-permute-start(bf16[64,256]{1,0:T(8,128)(2,1)S(1)} %get-tuple-element.51._), channel_id=1, source_target_pairs={{0,1},{1,0},{2,3},{3,2},{4,5},{5,4},{6,7},{7,6},{8,9},{9,8},{10,11... | collective-permute-start | bytes 98312 | tf_op jit(solution)/shard_map/ppermute | solution.py:324
  1.8 4.3 %collective-permute-start = (bf16[64,256]{1,0:T(8,128)(2,1)S(1)}, bf16[64,256]{1,0:T(8,128)(2,1)S(1)}, u32[]{:S(2)}, u32[]{:S(2)}) collective-permute-start(bf16[64,256]{1,0:T(8,128)(2,1)S(1)} %get-tuple-element.55), channel_id=1, source_target_pairs={{0,3},{1,2},{2,1},{3,0},{4,7},{5,6},{6,5},{7,4},{8,11},{9,10},{10,... | collective-permute-start | bytes 98312 | tf_op jit(solution)/shard_map/ppermute | solution.py:339
  4.4 3.6 %collective-permute-start.5 = (bf16[64,256]{1,0:T(8,128)(2,1)S(1)}, bf16[64,256]{1,0:T(8,128)(2,1)S(1)}, u32[]{:S(2)}, u32[]{:S(2)}) collective-permute-start(bf16[64,256]{1,0:T(8,128)(2,1)S(1)} %get-tuple-element.66), channel_id=1, source_target_pairs={{0,3},{1,2},{2,1},{3,0},{4,7},{5,6},{6,5},{7,4},{8,11},{9,10},{10,... | collective-permute-start | bytes 98312 | tf_op jit(solution)/shard_map/ppermute | solution.py:339
  4.5 3.6 %collective-permute-start.6 = (bf16[64,256]{1,0:T(8,128)(2,1)S(1)}, bf16[64,256]{1,0:T(8,128)(2,1)S(1)}, u32[]{:S(2)}, u32[]{:S(2)}) collective-permute-start(bf16[64,256]{1,0:T(8,128)(2,1)S(1)} %get-tuple-element.67), channel_id=1, source_target_pairs={{0,1},{1,0},{2,3},{3,2},{4,5},{5,4},{6,7},{7,6},{8,9},{9,8},{10,11... | collective-permute-start | bytes 98312 | tf_op jit(solution)/shard_map/ppermute | solution.py:324
  6.1 3.5 %copy-start.1 = (bf16[3,1,4,3,64,64]{5,4,3,2,1,0:T(8,128)(2,1)S(1)}, bf16[3,1,4,3,64,64]{5,4,3,2,1,0:T(8,128)(2,1)}, u32[]{:S(2)}) copy-start(bf16[3,1,4,3,64,64]{5,4,3,2,1,0:T(8,128)(2,1)} %rblocks.5) | copy-start | bytes 884740
  6.3 4.5 %collective-permute-start.2 = (bf16[256,128]{1,0:T(8,128)(2,1)S(1)}, bf16[256,128]{1,0:T(8,128)(2,1)S(1)}, u32[]{:S(2)}, u32[]{:S(2)}) collective-permute-start(bf16[256,128]{1,0:T(8,128)(2,1)S(1)} %get-tuple-element.56._), channel_id=1, source_target_pairs={{0,4},{4,0},{8,12},{12,8},{16,20},{20,16},{24,28},{28,24},{1,5},{5... | collective-permute-start | bytes 196616 | tf_op jit(solution)/shard_map/ppermute | solution.py:324
  8.0 1.6 %copy-start.5 = (s32[3,1,4,3]{2,1,3,0:T(1,128)S(1)}, s32[3,1,4,3]{2,1,3,0:T(1,128)}, u32[]{:S(2)}) copy-start(s32[3,1,4,3]{2,1,3,0:T(1,128)} %param.11) | copy-start | bytes 436
  8.2 4.9 %collective-permute-start.7 = (bf16[256,128]{1,0:T(8,128)(2,1)S(1)}, bf16[256,128]{1,0:T(8,128)(2,1)S(1)}, u32[]{:S(2)}, u32[]{:S(2)}) collective-permute-start(bf16[256,128]{1,0:T(8,128)(2,1)S(1)} %get-tuple-element.69), channel_id=1, source_target_pairs={{0,4},{4,0},{8,12},{12,8},{16,20},{20,16},{24,28},{28,24},{1,5},{5... | collective-permute-start | bytes 196616 | tf_op jit(solution)/shard_map/ppermute | solution.py:324
  11.0 3.9 %collective-permute-start.3 = (bf16[64,128]{1,0:T(8,128)(2,1)S(1)}, bf16[64,128]{1,0:T(8,128)(2,1)S(1)}, u32[]{:S(2)}, u32[]{:S(2)}) collective-permute-start(bf16[64,128]{1,0:T(8,128)(2,1)S(1)} %get-tuple-element.64), channel_id=1, source_target_pairs={{0,3},{1,2},{2,1},{3,0},{4,7},{5,6},{6,5},{7,4},{8,11},{9,10},{10,... | collective-permute-start | bytes 49160 | tf_op jit(solution)/shard_map/ppermute | solution.py:339
  12.5 2.3 %collective-permute-start.4 = (bf16[64,128]{1,0:T(8,128)(2,1)S(1)}, bf16[64,128]{1,0:T(8,128)(2,1)S(1)}, u32[]{:S(2)}, u32[]{:S(2)}) collective-permute-start(bf16[64,128]{1,0:T(8,128)(2,1)S(1)} %get-tuple-element.65), channel_id=1, source_target_pairs={{0,1},{1,0},{2,3},{3,2},{4,5},{5,4},{6,7},{7,6},{8,9},{9,8},{10,11... | collective-permute-start | bytes 49160 | tf_op jit(solution)/shard_map/ppermute | solution.py:324
  13.4 4.8 %collective-permute-start.8 = (bf16[64,128]{1,0:T(8,128)(2,1)S(1)}, bf16[64,128]{1,0:T(8,128)(2,1)S(1)}, u32[]{:S(2)}, u32[]{:S(2)}) collective-permute-start(bf16[64,128]{1,0:T(8,128)(2,1)S(1)} %get-tuple-element.74), channel_id=1, source_target_pairs={{0,3},{1,2},{2,1},{3,0},{4,7},{5,6},{6,5},{7,4},{8,11},{9,10},{10,... | collective-permute-start | bytes 49160 | tf_op jit(solution)/shard_map/ppermute | solution.py:339
  14.2 4.0 %collective-permute-start.9 = (bf16[64,128]{1,0:T(8,128)(2,1)S(1)}, bf16[64,128]{1,0:T(8,128)(2,1)S(1)}, u32[]{:S(2)}, u32[]{:S(2)}) collective-permute-start(bf16[64,128]{1,0:T(8,128)(2,1)S(1)} %get-tuple-element.75), channel_id=1, source_target_pairs={{0,1},{1,0},{2,3},{3,2},{4,5},{5,4},{6,7},{7,6},{8,9},{9,8},{10,11... | collective-permute-start | bytes 49160 | tf_op jit(solution)/shard_map/ppermute | solution.py:324
  15.1 4.4 %collective-permute-start.10 = (bf16[256,128]{1,0:T(8,128)(2,1)S(1)}, bf16[256,128]{1,0:T(8,128)(2,1)S(1)}, u32[]{:S(2)}, u32[]{:S(2)}) collective-permute-start(bf16[256,128]{1,0:T(8,128)(2,1)S(1)} %get-tuple-element.71._), channel_id=1, source_target_pairs={{0,8},{4,12},{8,0},{12,4},{16,24},{20,28},{24,16},{28,20},{1,9},{5... | collective-permute-start | bytes 196616 | tf_op jit(solution)/shard_map/ppermute | solution.py:324
  16.7 11.1 %collective-permute-start.13 = (bf16[256,128]{1,0:T(8,128)(2,1)S(1)}, bf16[256,128]{1,0:T(8,128)(2,1)S(1)}, u32[]{:S(2)}, u32[]{:S(2)}) collective-permute-start(bf16[256,128]{1,0:T(8,128)(2,1)S(1)} %get-tuple-element.85.near), channel_id=1, source_target_pairs={{0,4},{4,0},{8,12},{12,8},{16,20},{20,16},{24,28},{28,24},{1,5},{5... | collective-permute-start | bytes 196616 | tf_op jit(solution)/shard_map/ppermute | solution.py:324
  19.7 3.2 %collective-permute-start.11 = (bf16[64,128]{1,0:T(8,128)(2,1)S(1)}, bf16[64,128]{1,0:T(8,128)(2,1)S(1)}, u32[]{:S(2)}, u32[]{:S(2)}) collective-permute-start(bf16[64,128]{1,0:T(8,128)(2,1)S(1)} %get-tuple-element.82), channel_id=1, source_target_pairs={{0,3},{1,2},{2,1},{3,0},{4,7},{5,6},{6,5},{7,4},{8,11},{9,10},{10,... | collective-permute-start | bytes 49160 | tf_op jit(solution)/shard_map/ppermute | solution.py:339
  20.6 2.4 %collective-permute-start.12 = (bf16[64,128]{1,0:T(8,128)(2,1)S(1)}, bf16[64,128]{1,0:T(8,128)(2,1)S(1)}, u32[]{:S(2)}, u32[]{:S(2)}) collective-permute-start(bf16[64,128]{1,0:T(8,128)(2,1)S(1)} %get-tuple-element.83), channel_id=1, source_target_pairs={{0,1},{1,0},{2,3},{3,2},{4,5},{5,4},{6,7},{7,6},{8,9},{9,8},{10,11... | collective-permute-start | bytes 49160 | tf_op jit(solution)/shard_map/ppermute | solution.py:324
  22.3 5.6 %copy-start.2 = (bf16[3,1,4,2,64,64]{5,4,3,2,1,0:T(8,128)(2,1)S(1)}, bf16[3,1,4,2,64,64]{5,4,3,2,1,0:T(8,128)(2,1)}, u32[]{:S(2)}) copy-start(bf16[3,1,4,2,64,64]{5,4,3,2,1,0:T(8,128)(2,1)} %blocks_1.1) | copy-start | bytes 589828
  23.4 7.6 %collective-permute-start.16 = (bf16[256,128]{1,0:T(8,128)(2,1)S(1)}, bf16[256,128]{1,0:T(8,128)(2,1)S(1)}, u32[]{:S(2)}, u32[]{:S(2)}) collective-permute-start(bf16[256,128]{1,0:T(8,128)(2,1)S(1)} %get-tuple-element.84.refs_0_._.own), channel_id=1, source_target_pairs={{0,18},{1,19},{2,16},{3,17},{4,22},{5,23},{6,20},{7,21},{8,26},{9,... | collective-permute-start | bytes 196616 | tf_op jit(solution)/shard_map/ppermute | solution.py:333
  27.1 4.5 %collective-permute-start.17 = (bf16[256,128]{1,0:T(8,128)(2,1)S(1)}, bf16[256,128]{1,0:T(8,128)(2,1)S(1)}, u32[]{:S(2)}, u32[]{:S(2)}) collective-permute-start(bf16[256,128]{1,0:T(8,128)(2,1)S(1)} %get-tuple-element.84.refs_0_._.own), channel_id=1, source_target_pairs={{0,2},{1,3},{2,0},{3,1},{4,6},{5,7},{6,4},{7,5},{8,10},{9,11},{10,... | collective-permute-start | bytes 196616 | tf_op jit(solution)/shard_map/ppermute | solution.py:324
  27.5 5.4 %collective-permute-start.14 = (bf16[256,128]{1,0:T(8,128)(2,1)S(1)}, bf16[256,128]{1,0:T(8,128)(2,1)S(1)}, u32[]{:S(2)}, u32[]{:S(2)}) collective-permute-start(bf16[256,128]{1,0:T(8,128)(2,1)S(1)} %get-tuple-element.84.refs_0_._.own), channel_id=1, source_target_pairs={{0,16},{1,17},{2,18},{3,19},{4,20},{5,21},{6,22},{7,23},{8,24},{9,... | collective-permute-start | bytes 196616 | tf_op jit(solution)/shard_map/ppermute | solution.py:333
  27.9 0.7 %copy-start.6 = (s32[3,1,4,2]{2,3,1,0:T(2,128)S(1)}, s32[3,1,4,2]{2,3,1,0:T(2,128)}, u32[]{:S(2)}) copy-start(s32[3,1,4,2]{2,3,1,0:T(2,128)} %param.13) | copy-start | bytes 292
  28.5 1.2 %copy-start.4 = (bf16[256,1024]{1,0:T(8,128)(2,1)S(1)}, bf16[256,1024]{1,0:T(8,128)(2,1)}, u32[]{:S(2)}) copy-start(bf16[256,1024]{1,0:T(8,128)(2,1)} %refs_3_.1) | copy-start | bytes 1572868
  31.7 1.6 %collective-permute-start.18 = (bf16[256,128]{1,0:T(8,128)(2,1)S(1)}, bf16[256,128]{1,0:T(8,128)(2,1)S(1)}, u32[]{:S(2)}, u32[]{:S(2)}) collective-permute-start(bf16[256,128]{1,0:T(8,128)(2,1)S(1)} %share_sum.3.refs_0_), channel_id=1, source_target_pairs={{0,1},{1,0},{2,3},{3,2},{4,5},{5,4},{6,7},{7,6},{8,9},{9,8},{10,11... | collective-permute-start | bytes 196616 | tf_op jit(solution)/shard_map/ppermute | solution.py:324
  33.0 1.3 %collective-permute-start.15 = (bf16[256,128]{1,0:T(8,128)(2,1)S(1)}, bf16[256,128]{1,0:T(8,128)(2,1)S(1)}, u32[]{:S(2)}, u32[]{:S(2)}) collective-permute-start(bf16[256,128]{1,0:T(8,128)(2,1)S(1)} %share_sum.2.refs_1_), channel_id=1, source_target_pairs={{0,1},{1,0},{2,3},{3,2},{4,5},{5,4},{6,7},{7,6},{8,9},{9,8},{10,11... | collective-permute-start | bytes 196616 | tf_op jit(solution)/shard_map/ppermute | solution.py:324
  34.7 5.7 %collective-permute-start.21 = (bf16[256,128]{1,0:T(8,128)(2,1)S(1)}, bf16[256,128]{1,0:T(8,128)(2,1)S(1)}, u32[]{:S(2)}, u32[]{:S(2)}) collective-permute-start(bf16[256,128]{1,0:T(8,128)(2,1)S(1)} %get-tuple-element.92), channel_id=1, source_target_pairs={{0,12},{4,8},{8,4},{12,0},{16,28},{20,24},{24,20},{28,16},{1,13},{... | collective-permute-start | bytes 196616 | tf_op jit(solution)/shard_map/ppermute | solution.py:324
  36.9 4.5 %collective-permute-start.19 = (bf16[256,128]{1,0:T(8,128)(2,1)S(1)}, bf16[256,128]{1,0:T(8,128)(2,1)S(1)}, u32[]{:S(2)}, u32[]{:S(2)}) collective-permute-start(bf16[256,128]{1,0:T(8,128)(2,1)S(1)} %get-tuple-element.92), channel_id=1, source_target_pairs={{0,8},{4,12},{8,0},{12,4},{16,24},{20,28},{24,16},{28,20},{1,9},{5... | collective-permute-start | bytes 196616 | tf_op jit(solution)/shard_map/ppermute | solution.py:324
  37.6 4.3 %collective-permute-start.20 = (bf16[256,128]{1,0:T(8,128)(2,1)S(1)}, bf16[256,128]{1,0:T(8,128)(2,1)S(1)}, u32[]{:S(2)}, u32[]{:S(2)}) collective-permute-start(bf16[256,128]{1,0:T(8,128)(2,1)S(1)} %get-tuple-element.93.refs_0_), channel_id=1, source_target_pairs={{0,4},{4,0},{8,12},{12,8},{16,20},{20,16},{24,28},{28,24},{1,5},{5... | collective-permute-start | bytes 196616 | tf_op jit(solution)/shard_map/ppermute | solution.py:324
